TPU v7x, 32 devices: a whole 2x2x4 slice. The times are simulated.
32 devices in a mesh: groups: 2 (over x), expert: 4 (over y, core), mp: 4 (over z).
Axes of the slice: x: 2, y: 2, z: 4, core: 2. Of those that a mesh axis runs over, the one named last changes fastest.
Arguments:
- tokens: bfloat16 [256, 4096], P(('groups', 'expert', 'mp')), parts along dimension 0, may hold values from -6 to 6
- routes: int32 [256, 8], P(('groups', 'expert', 'mp')), parts along dimension 0, may hold values from 0 to 15, all different within a row; in each aligned block of 8 rows (0 to 7, 8 to 15, ...) at most 5 rows name the same one
- probs: float32 [256, 8], P(('groups', 'expert', 'mp')), parts along dimension 0, may hold values from 0.1 to 1
- w_gate: bfloat16 [16, 4096, 768], P('expert', None, 'mp'), may hold values from -0.09375 to 0.09375
- w_up: bfloat16 [16, 4096, 768], P('expert', None, 'mp'), may hold values from -0.09375 to 0.09375
- w_down: bfloat16 [16, 768, 4096], P('expert', 'mp'), may hold values from -0.21875 to 0.21875
- gate_left: bfloat16 [16, 32, 4096], P('expert', None, 'mp'), may hold values from -0.046875 to 0.046875
- gate_right: bfloat16 [16, 32, 768], P('expert', 'mp'), may hold values from -1 to 1
- up_left: bfloat16 [16, 32, 4096], P('expert', None, 'mp'), may hold values from -0.046875 to 0.046875
- up_right: bfloat16 [16, 32, 768], P('expert', 'mp'), may hold values from -1 to 1
- down_left: bfloat16 [16, 32, 768], P('expert', 'mp'), may hold values from -0.109375 to 0.109375
- down_right: bfloat16 [16, 32, 4096], P('expert', None, 'mp'), may hold values from -1 to 1
Outputs:
- mixed: bfloat16 [256, 4096], P(('groups', 'expert', 'mp')), parts along dimension 0
There are 2 independent parts, one for each index of `groups`. A program takes and returns all parts, laid end to end along the dimension named above; an argument that names none is the same for every part. Nothing has to cross between parts.
Inputs may be any that keep to these rules, and one draw needn't show every extreme that they name: `routes`: each row names 8 different experts; within the rows of one device no expert is named by more than 5 rows, a bound that some block reaches.
All inputs are finite; a program needn't handle non-finite values.
Results may differ from a plain program's by a relative error of at most 0.014.
Values may be sent and summed in bfloat16 or wider, within the bound.
No kernel may reach another device: no remote copies, remote signals or barrier semaphores. Data moves between devices by JAX's collectives and lax.ppermute only.
A program may use at most 128 MiB of HBM per device.

v0:
```python
import jax
import jax.numpy as jnp
from jax import lax
from jax.sharding import PartitionSpec as P


def merge_input(base, left, right):
    product = jnp.einsum("erd,erf->edf", left, right, preferred_element_type=jnp.float32)
    return (base.astype(jnp.float32) + product).astype(jnp.bfloat16)


def local(
    tokens,
    routes,
    probs,
    w_gate,
    w_up,
    w_down,
    gate_left,
    gate_right,
    up_left,
    up_right,
    down_left,
    down_right,
):
    highest = lax.Precision.HIGHEST
    rows_dev, width = tokens.shape
    top_count = routes.shape[1]
    exp_dev = w_gate.shape[0]
    expert_groups = lax.axis_size("expert")
    model_groups = lax.axis_size("mp")
    experts = exp_dev * expert_groups
    capacity = (rows_dev * top_count + experts - 1) // experts + 1
    entries = rows_dev * top_count
    full_left = (
        lax.all_gather(gate_left, "mp", axis=2, tiled=True),
        lax.all_gather(up_left, "mp", axis=2, tiled=True),
        lax.all_gather(down_right, "mp", axis=2, tiled=True),
    )
    local_right = (
        lax.all_to_all(gate_right, "mp", split_axis=2, concat_axis=1, tiled=True),
        lax.all_to_all(up_right, "mp", split_axis=2, concat_axis=1, tiled=True),
        lax.all_to_all(down_left, "mp", split_axis=2, concat_axis=1, tiled=True),
    )
    gate_merged = merge_input(w_gate, full_left[0], local_right[0])
    up_merged = merge_input(w_up, full_left[1], local_right[1])
    down_extra = jnp.einsum(
        "erf,erd->efd", local_right[2], full_left[2], preferred_element_type=jnp.float32
    )
    down_merged = (w_down.astype(jnp.float32) + down_extra).astype(jnp.bfloat16)
    flat_routes = routes.reshape(entries)
    expert_hits = (flat_routes[:, None] == jnp.arange(experts, dtype=jnp.int32)[None, :]).astype(
        jnp.int32
    )
    order_all = jnp.cumsum(expert_hits, axis=0) - 1
    slot_rank = jnp.sum(expert_hits * order_all, axis=1)
    target = flat_routes * capacity + slot_rank
    placed = target[:, None] == jnp.arange(experts * capacity, dtype=jnp.int32)[None, :]
    owner_token = (jnp.arange(entries, dtype=jnp.int32) // top_count)[:, None] == jnp.arange(
        rows_dev, dtype=jnp.int32
    )[None, :]
    picks = jnp.einsum(
        "js,jt->st",
        placed.astype(jnp.bfloat16),
        owner_token.astype(jnp.bfloat16),
        preferred_element_type=jnp.float32,
    ).astype(jnp.bfloat16)
    outgoing = jnp.dot(picks, tokens, preferred_element_type=jnp.float32).astype(jnp.bfloat16)
    weighted_owner = owner_token.astype(jnp.float32) * probs.reshape(entries)[:, None]
    weigh = jnp.einsum("jt,js->ts", weighted_owner, placed.astype(jnp.float32), precision=highest)
    outgoing = outgoing.reshape(expert_groups, exp_dev, capacity, width)
    spread = jnp.broadcast_to(
        outgoing[:, None], (expert_groups, model_groups, exp_dev, capacity, width)
    )
    spread = spread.reshape(expert_groups * model_groups, exp_dev, capacity, width)
    routed = lax.all_to_all(spread, ("expert", "mp"), split_axis=0, concat_axis=0, tiled=True)
    gate_act = jnp.einsum("secd,edf->secf", routed, gate_merged, preferred_element_type=jnp.float32)
    up_act = jnp.einsum("secd,edf->secf", routed, up_merged, preferred_element_type=jnp.float32)
    hidden = (jax.nn.silu(gate_act) * up_act).astype(jnp.bfloat16)
    result = jnp.einsum("secf,efd->secd", hidden, down_merged, preferred_element_type=jnp.float32)
    partials = result.astype(jnp.bfloat16)
    partials = partials.reshape(expert_groups, model_groups, exp_dev, capacity, width)
    sending = partials.reshape(expert_groups * model_groups, exp_dev, capacity, width)
    pieces = lax.all_to_all(sending, ("expert", "mp"), split_axis=0, concat_axis=0, tiled=True)
    pieces = pieces.reshape(expert_groups, model_groups, exp_dev, capacity, width)
    expert_out = jnp.sum(pieces.astype(jnp.float32), axis=1).astype(jnp.bfloat16)
    expert_out = expert_out.reshape(experts * capacity, width)
    mixed = jnp.dot(
        weigh, expert_out.astype(jnp.float32), precision=highest, preferred_element_type=jnp.float32
    )
    return mixed.astype(jnp.bfloat16)


def solution(mesh):
    return jax.shard_map(
        local,
        mesh=mesh,
        in_specs=(
            P(("groups", "expert", "mp"), None),
            P(("groups", "expert", "mp"), None),
            P(("groups", "expert", "mp"), None),
            P("expert", None, "mp"),
            P("expert", None, "mp"),
            P("expert", "mp", None),
            P("expert", None, "mp"),
            P("expert", "mp", None),
            P("expert", None, "mp"),
            P("expert", "mp", None),
            P("expert", "mp", None),
            P("expert", None, "mp"),
        ),
        out_specs=P(("groups", "expert", "mp"), None),
        check_vma=False,
    )
```

profile of v0, /device:TPU:0, one launch (start us, length us, event | category | flops | bytes accessed | tf_op | source)
XLA Modules:
  0.0 252.7 jit_solution(12432521440216509149)
XLA Ops:
  6.5 1.3 copy.36
  7.8 1.4 reshape.43
  9.2 6.3 %all-to-all-start.1 = ((bf16[4,2,3072]{2,1,0:T(2,128)(2,1)}), bf16[4,2,3072]{2,1,0:T(2,128)(2,1)S(1)}, u32[]{:S(2)}, u32[]{:S(2)}) async-start(bf16[4,2,3072]{2,1,0:T(2,128)(2,1)} %reshape.43), calls=%async_computation.1 | async-start | bytes 98304 | tf_op jit(solution)/shard_map/all_to_all | solution.py:41
  16.4 1.3 copy.41
  17.7 1.4 reshape.45
  19.3 1.9 all-to-all-done.1
  21.3 3.3 %all-to-all-start.3 = ((bf16[4,2,3072]{2,1,0:T(2,128)(2,1)}), bf16[4,2,3072]{2,1,0:T(2,128)(2,1)S(1)}, u32[]{:S(2)}, u32[]{:S(2)}) async-start(bf16[4,2,3072]{2,1,0:T(2,128)(2,1)} %reshape.45), calls=%async_computation.3 | async-start | bytes 98304 | tf_op jit(solution)/shard_map/all_to_all | solution.py:42
  24.5 1.3 copy.33
  25.8 1.4 reshape.47
  27.2 3.0 %all-to-all-done.3 = bf16[4,2,3072]{2,1,0:T(2,128)(2,1)S(1)} async-done(((bf16[4,2,3072]{2,1,0:T(2,128)(2,1)}), bf16[4,2,3072]{2,1,0:T(2,128)(2,1)S(1)}, u32[]{:S(2)}, u32[]{:S(2)}) %all-to-all-start.3) | async-done | bytes 49184 | tf_op jit(solution)/shard_map/all_to_all | solution.py:42
  30.2 3.3 %all-to-all-start = ((bf16[4,2,3072]{2,1,0:T(2,128)(2,1)}), bf16[4,2,3072]{2,1,0:T(2,128)(2,1)S(1)}, u32[]{:S(2)}, u32[]{:S(2)}) async-start(bf16[4,2,3072]{2,1,0:T(2,128)(2,1)} %reshape.47), calls=%async_computation | async-start | bytes 98304 | tf_op jit(solution)/shard_map/all_to_all | solution.py:43
  35.0 4.2 %all-to-all-done = bf16[4,2,3072]{2,1,0:T(2,128)(2,1)S(1)} async-done(((bf16[4,2,3072]{2,1,0:T(2,128)(2,1)}), bf16[4,2,3072]{2,1,0:T(2,128)(2,1)S(1)}, u32[]{:S(2)}, u32[]{:S(2)}) %all-to-all-start) | async-done | bytes 49184 | tf_op jit(solution)/shard_map/all_to_all | solution.py:43
  39.2 2.8 %broadcast_in_dim.5 = bf16[4,4,4,5,4096]{4,2,3,1,0:T(4,128)(2,1)} broadcast(bf16[4,4,5,4096]{3,1,2,0:T(4,128)(2,1)S(1)} %copy.39), dimensions={0,2,3,4} | broadcast | bytes 3276800 | tf_op jit(solution)/shard_map/broadcast_in_dim | solution.py:72
  41.9 3.7 %all-to-all-start.2 = ((bf16[16,4,5,4096]{3,1,2,0:T(4,128)(2,1)}), bf16[16,4,5,4096]{3,1,2,0:T(4,128)(2,1)S(1)}, u32[]{:S(2)}, u32[]{:S(2)}) async-start(bf16[16,4,5,4096]{3,1,2,0:T(4,128)(2,1)} %bitcast.12), calls=%async_computation.2 | async-start | bytes 5242880 | tf_op jit(solution)/shard_map/all_to_all | solution.py:76
  47.9 0.9 reshape.44
  48.8 1.1 copy.38
  50.0 1.7 reshape.46
  51.7 1.1 copy.43
  52.8 1.7 reshape.48
  54.5 1.1 copy.35
  55.7 52.5 %all-gather.6.cloned.1.call-done = bf16[4,32,4096]{2,1,0:T(8,128)(2,1)} async-done(((bf16[4,32,1024]{2,1,0:T(8,128)(2,1)}), bf16[4,32,4096]{2,1,0:T(8,128)(2,1)}) %all-gather.6.cloned.1.call-update) | async-done | bytes 1048592 | tf_op jit(solution)/shard_map/all_gather | solution.py:36
  108.1 17.6 %all-to-all-done.2 = bf16[16,4,5,4096]{3,1,2,0:T(4,128)(2,1)S(1)} async-done(((bf16[16,4,5,4096]{3,1,2,0:T(4,128)(2,1)}), bf16[16,4,5,4096]{3,1,2,0:T(4,128)(2,1)S(1)}, u32[]{:S(2)}, u32[]{:S(2)}) %all-to-all-start.2) | async-done | bytes 2621472 | tf_op jit(solution)/shard_map/all_to_all | solution.py:76
  125.7 7.3 %fusion.14 = f32[16,4,5,192]{3,0,2,1:T(8,128)S(1)} fusion(bf16[16,4,5,4096]{3,1,2,0:T(4,128)(2,1)S(1)} %all-to-all-done.2, bf16[4,32,4096]{2,1,0:T(8,128)(2,1)} %all-gather.6.cloned.1.call-done, bf16[4,4096,192]{1,2,0:T(8,128)(2,1)} %param.15, bf16[4,4,8,192]{3,2,1,0:T(8,128)(2,1)} %copy.38), kind=kOutput, calls=%fused_computation.16 | convolution fusion | flops 714080256 | bytes 10256384 | tf_op jit(solution)/shard_map/secd,edf->secf/dot_general | solution.py:77
  133.0 6.9 %all-gather.8.cloned.1.call-done = bf16[4,32,4096]{2,1,0:T(8,128)(2,1)} async-done(((bf16[4,32,1024]{2,1,0:T(8,128)(2,1)}), bf16[4,32,4096]{2,1,0:T(8,128)(2,1)}) %all-gather.8.cloned.1.call-update) | async-done | bytes 1048592 | tf_op jit(solution)/shard_map/all_gather | solution.py:37
  139.9 7.3 %fusion.29 = bf16[16,4,5,192]{3,0,2,1:T(8,128)(2,1)S(1)} fusion(bf16[16,4,5,4096]{3,1,2,0:T(4,128)(2,1)S(1)} %all-to-all-done.2, bf16[4,32,4096]{2,1,0:T(8,128)(2,1)} %all-gather.8.cloned.1.call-done, bf16[4,4096,192]{1,2,0:T(8,128)(2,1)} %param.16, f32[16,4,5,192]{3,0,2,1:T(8,128)S(1)} %fusion.14, bf16[4,4,8,192]{3,2,1,0:T(8,128)(2,1)S(1)} %copy-done.4), kind=kOutput, calls=%fused_computation.19 | convolution fusion | flops 714448896 | bytes 10379264 | tf_op jit(solution)/shard_map/secd,edf->secf/dot_general | solution.py:78
  147.2 21.3 %all-gather.4.cloned.1.call-done = bf16[4,32,4096]{2,1,0:T(8,128)(2,1)} async-done(((bf16[4,32,1024]{2,1,0:T(8,128)(2,1)}), bf16[4,32,4096]{2,1,0:T(8,128)(2,1)}) %all-gather.4.cloned.1.call-update) | async-done | bytes 1048592 | tf_op jit(solution)/shard_map/all_gather | solution.py:38
  168.5 5.8 %fusion.9 = bf16[16,4,5,4096]{3,0,2,1:T(8,128)(2,1)S(1)} fusion(bf16[16,4,5,192]{3,0,2,1:T(8,128)(2,1)S(1)} %fusion.29, bf16[4,192,4096]{2,1,0:T(8,128)(2,1)} %param.17, bf16[4,32,4096]{2,1,0:T(8,128)(2,1)} %all-gather.4.cloned.1.call-done, bf16[4,4,8,192]{3,2,1,0:T(8,128)(2,1)S(1)} %copy-done.3), kind=kOutput, calls=%fused_computation.10 | convolution fusion | flops 715390976 | bytes 10133504 | tf_op jit(solution)/shard_map/secf,efd->secd/dot_general | solution.py:80
  174.3 3.7 %copy.45 = bf16[16,4,5,4096]{3,1,2,0:T(4,128)(2,1)} copy(bf16[16,4,5,4096]{3,0,2,1:T(8,128)(2,1)S(1)} %fusion.9) | data formatting | bytes 5242880 | tf_op jit(solution)/shard_map/convert_element_type | solution.py:81
  178.0 4.2 %all-to-all-start.4 = ((bf16[16,4,5,4096]{3,1,2,0:T(4,128)(2,1)}), bf16[16,4,5,4096]{3,1,2,0:T(4,128)(2,1)S(1)}, u32[]{:S(2)}, u32[]{:S(2)}) async-start(bf16[16,4,5,4096]{3,1,2,0:T(4,128)(2,1)} %copy.45), calls=%async_computation.4 | async-start | bytes 5242880 | tf_op jit(solution)/shard_map/all_to_all | solution.py:84
  182.6 60.3 %all-to-all-done.4 = bf16[16,4,5,4096]{3,1,2,0:T(4,128)(2,1)S(1)} async-done(((bf16[16,4,5,4096]{3,1,2,0:T(4,128)(2,1)}), bf16[16,4,5,4096]{3,1,2,0:T(4,128)(2,1)S(1)}, u32[]{:S(2)}, u32[]{:S(2)}) %all-to-all-start.4) | async-done | bytes 2621472 | tf_op jit(solution)/shard_map/all_to_all | solution.py:84
  242.9 1.5 bitcast_reduce_fusion
  245.1 1.0 convolution_convert_fusion.1
  (30 shorter events, 5.8 us)
Async XLA Ops:
  6.5 27.0 %copy-start = (bf16[8,4096]{1,0:T(8,128)(2,1)S(1)}, bf16[8,4096]{1,0:T(8,128)(2,1)}, u32[]{:S(2)}) copy-start(bf16[8,4096]{1,0:T(8,128)(2,1)} %param.12) | copy-start | bytes 196612
  9.2 12.0 %all-to-all-start.1 = ((bf16[4,2,3072]{2,1,0:T(2,128)(2,1)}), bf16[4,2,3072]{2,1,0:T(2,128)(2,1)S(1)}, u32[]{:S(2)}, u32[]{:S(2)}) async-start(bf16[4,2,3072]{2,1,0:T(2,128)(2,1)} %reshape.43), calls=%async_computation.1 | async-start | bytes 98304 | tf_op jit(solution)/shard_map/all_to_all | solution.py:41
  21.3 8.9 %all-to-all-start.3 = ((bf16[4,2,3072]{2,1,0:T(2,128)(2,1)}), bf16[4,2,3072]{2,1,0:T(2,128)(2,1)S(1)}, u32[]{:S(2)}, u32[]{:S(2)}) async-start(bf16[4,2,3072]{2,1,0:T(2,128)(2,1)} %reshape.45), calls=%async_computation.3 | async-start | bytes 98304 | tf_op jit(solution)/shard_map/all_to_all | solution.py:42
  30.2 3.3 %copy-start.1 = (bf16[4,2,3072]{2,1,0:T(2,128)(2,1)}, bf16[4,2,3072]{2,1,0:T(2,128)(2,1)S(1)}, u32[]{:S(2)}) copy-start(bf16[4,2,3072]{2,1,0:T(2,128)(2,1)S(1)} %all-to-all-done.3) | copy-start | bytes 147460
  30.2 8.9 %all-to-all-start = ((bf16[4,2,3072]{2,1,0:T(2,128)(2,1)}), bf16[4,2,3072]{2,1,0:T(2,128)(2,1)S(1)}, u32[]{:S(2)}, u32[]{:S(2)}) async-start(bf16[4,2,3072]{2,1,0:T(2,128)(2,1)} %reshape.47), calls=%async_computation | async-start | bytes 98304 | tf_op jit(solution)/shard_map/all_to_all | solution.py:43
  39.2 2.8 %copy-start.2 = (bf16[4,2,3072]{2,1,0:T(2,128)(2,1)}, bf16[4,2,3072]{2,1,0:T(2,128)(2,1)S(1)}, u32[]{:S(2)}) copy-start(bf16[4,2,3072]{2,1,0:T(2,128)(2,1)S(1)} %all-to-all-done) | copy-start | bytes 147460
  41.9 83.8 %all-to-all-start.2 = ((bf16[16,4,5,4096]{3,1,2,0:T(4,128)(2,1)}), bf16[16,4,5,4096]{3,1,2,0:T(4,128)(2,1)S(1)}, u32[]{:S(2)}, u32[]{:S(2)}) async-start(bf16[16,4,5,4096]{3,1,2,0:T(4,128)(2,1)} %bitcast.12), calls=%async_computation.2 | async-start | bytes 5242880 | tf_op jit(solution)/shard_map/all_to_all | solution.py:76
  45.7 62.4 %all-gather.6.cloned.1.call-start = ((), (), s32[]{:S(2)}) async-start(), calls=%async_computation.6 | async-start | bytes 1310720 | tf_op jit(solution)/shard_map/all_gather | solution.py:36
  46.4 93.5 %all-gather.8.cloned.1.call-start = ((), (), s32[]{:S(2)}) async-start(), calls=%async_computation.7 | async-start | bytes 1310720 | tf_op jit(solution)/shard_map/all_gather | solution.py:37
  47.2 121.4 %all-gather.4.cloned.1.call-start = ((), (), s32[]{:S(2)}) async-start(), calls=%async_computation.5 | async-start | bytes 1310720 | tf_op jit(solution)/shard_map/all_gather | solution.py:38
  55.7 84.2 %copy-start.4 = (bf16[4,4,8,192]{3,2,1,0:T(8,128)(2,1)S(1)}, bf16[4,4,8,192]{3,2,1,0:T(8,128)(2,1)}, u32[]{:S(2)}) copy-start(bf16[4,4,8,192]{3,2,1,0:T(8,128)(2,1)} %copy.43) | copy-start | bytes 147460
  133.0 35.5 %copy-start.3 = (bf16[4,4,8,192]{3,2,1,0:T(8,128)(2,1)S(1)}, bf16[4,4,8,192]{3,2,1,0:T(8,128)(2,1)}, u32[]{:S(2)}) copy-start(bf16[4,4,8,192]{3,2,1,0:T(8,128)(2,1)} %copy.35) | copy-start | bytes 147460
  174.3 8.0 %copy-start.5 = (f32[8,8]{1,0:T(8,128)S(1)}, f32[8,8]{1,0:T(8,128)}, u32[]{:S(2)}) copy-start(f32[8,8]{1,0:T(8,128)} %param.14) | copy-start | bytes 772
  178.0 64.9 %all-to-all-start.4 = ((bf16[16,4,5,4096]{3,1,2,0:T(4,128)(2,1)}), bf16[16,4,5,4096]{3,1,2,0:T(4,128)(2,1)S(1)}, u32[]{:S(2)}, u32[]{:S(2)}) async-start(bf16[16,4,5,4096]{3,1,2,0:T(4,128)(2,1)} %copy.45), calls=%async_computation.4 | async-start | bytes 5242880 | tf_op jit(solution)/shard_map/all_to_all | solution.py:84
Sparse Core Ops, SparseCore 0:
  48.1 59.9 all-gather.5
  109.7 30.1 all-gather.7
  141.5 27.0 all-gather.3
where the time goes:
time: 254 us; the launch traced here: 253 us
  waiting for transfers between devices  170 us (67%)
  local copies, waits for them, and re-layouts  24.6 us (10%)
  matrix products  22.3 us (9%)
  starting transfers between devices  20.9 us (8%)
  between operations  13.3 us (5%)
    all_to_all x1, waiting for transfers between devices, local(): lax.all_to_all(sending, ('expert', 'mp'), split_axis=0, concat_axis=0, ti...  60.3 us
    all_gather x1, waiting for transfers between devices, local(): lax.all_gather(gate_left, 'mp', axis=2, tiled=True)  52.5 us
    all_gather x1, waiting for transfers between devices, local(): lax.all_gather(down_right, 'mp', axis=2, tiled=True)  21.3 us
    all_to_all x1, waiting for transfers between devices, local(): lax.all_to_all(spread, ('expert', 'mp'), split_axis=0, concat_axis=0, til...  17.6 us
    unnamed x21, local copies, waits for them, and re-layouts  12.4 us
    dot_general x1, matrix products, local(): jnp.einsum('secd,edf->secf', routed, gate_merged, preferred_element_type=...  7.33 us
    dot_general x1, matrix products, local(): jnp.einsum('secd,edf->secf', routed, up_merged, preferred_element_type=jn...  7.29 us
    all_gather x1, waiting for transfers between devices, local(): lax.all_gather(up_left, 'mp', axis=2, tiled=True)  6.85 us
  transfers between devices with their start and end apart: 8, of which 8 were waited for; matrix products, arithmetic and copies ran while one was open for 12% of the time, Pallas kernels for 0%

commit v1 on v0

v1 whole, which is shorter than its diff:
```python
import jax
import jax.numpy as jnp
from jax import lax
from jax.sharding import PartitionSpec as P

BF = jnp.bfloat16
F32 = jnp.float32


def dot_nt(a, b):
    return lax.dot_general(a, b, (((1,), (1,)), ((), ())), preferred_element_type=F32)


def dot_nn(a, b):
    return lax.dot_general(a, b, (((1,), (0,)), ((), ())), preferred_element_type=F32)


def local(
    tokens,
    routes,
    probs,
    w_gate,
    w_up,
    w_down,
    gate_left,
    gate_right,
    up_left,
    up_right,
    down_left,
    down_right,
):
    rows, width = tokens.shape
    exp_dev, _, cols = w_gate.shape
    rank = gate_left.shape[1]
    piece = gate_right.shape[1]
    block = gate_left.shape[2]
    groups = lax.axis_size("expert")
    parts = lax.axis_size("mp")
    experts = exp_dev * groups
    me_g = lax.axis_index("expert")
    me_m = lax.axis_index("mp")
    ranks = exp_dev * rank
    hid = exp_dev * cols

    chosen = routes[:, :, None] == jnp.arange(experts, dtype=jnp.int32)
    weight = jnp.sum(jnp.where(chosen, probs[:, :, None], 0.0), axis=1)
    high = lax.reduce_precision(weight, 8, 7)
    low = (weight - high).astype(BF)
    side = jnp.concatenate([high.astype(BF), low], axis=1)
    pad = -(2 * experts) % 128
    sent = jnp.concatenate([tokens, jnp.pad(side, ((0, 0), (0, pad)))], axis=1)
    every = lax.all_gather(sent, ("expert", "mp"), axis=0, tiled=True)
    total = every.shape[0]
    x = every[:, :width]
    side = every[:, width : width + 2 * experts].astype(F32)
    weight = side[:, :experts] + side[:, experts:]
    weight = lax.dynamic_slice(weight, (0, me_g * exp_dev), (total, exp_dev))

    small = jnp.stack([gate_right, up_right, down_left])
    small = small.reshape(3, exp_dev, piece, parts, cols)
    small = lax.all_to_all(small, "mp", split_axis=3, concat_axis=2, tiled=True)
    small = small.reshape(3, ranks, cols)
    same = (jnp.arange(ranks) // rank)[:, None] == (jnp.arange(hid) // cols)[None, :]
    diag = jnp.where(same, jnp.tile(small, (1, 1, exp_dev)), jnp.zeros((), BF))

    mine = lax.dynamic_slice(x, (0, me_m * block), (total, block))
    left = jnp.concatenate([gate_left.reshape(ranks, block), up_left.reshape(ranks, block)])
    inner = lax.psum(dot_nt(mine, left), "mp").astype(BF)

    gate_w = jnp.swapaxes(w_gate, 1, 2).reshape(hid, width)
    up_w = jnp.swapaxes(w_up, 1, 2).reshape(hid, width)
    gate_act = dot_nt(x, gate_w) + dot_nn(inner[:, :ranks], diag[0])
    up_act = dot_nt(x, up_w) + dot_nn(inner[:, ranks:], diag[1])
    scale = jnp.repeat(weight, cols, axis=1)
    hidden = (jax.nn.silu(gate_act) * up_act * scale).astype(BF)
    bottom = lax.psum(dot_nt(hidden, diag[2]), "mp").astype(BF)
    out = dot_nn(hidden, w_down.reshape(hid, width))
    extra = dot_nn(bottom, down_right.reshape(ranks, block))
    out = lax.dynamic_update_slice(
        out, extra + lax.dynamic_slice(out, (0, me_m * block), (total, block)), (0, me_m * block)
    )
    return lax.psum_scatter(out.astype(BF), ("expert", "mp"), scatter_dimension=0, tiled=True)


def solution(mesh):
    return jax.shard_map(
        local,
        mesh=mesh,
        in_specs=(
            P(("groups", "expert", "mp"), None),
            P(("groups", "expert", "mp"), None),
            P(("groups", "expert", "mp"), None),
            P("expert", None, "mp"),
            P("expert", None, "mp"),
            P("expert", "mp", None),
            P("expert", None, "mp"),
            P("expert", "mp", None),
            P("expert", None, "mp"),
            P("expert", "mp", None),
            P("expert", "mp", None),
            P("expert", None, "mp"),
        ),
        out_specs=P(("groups", "expert", "mp"), None),
        check_vma=False,
    )
```

time: 254 us -> 170 us (0.67)
  waiting for transfers between devices: 170 us -> 88 us
  blocking collectives: 0 us -> 36.4 us
  local copies, waits for them, and re-layouts: 24.6 us -> 5.37 us
  starting transfers between devices: 20.9 us -> 6.32 us
  matrix products: 22.3 us -> 15.3 us
  other arithmetic: 1.87 us -> 4.8 us
    all_to_all x5 -> x1, waiting for transfers between devices: 87 us -> 8.07 us  [local(): small = lax.all_to_all(small, 'mp', split_axis=3, concat_axis=2, tiled=True)]
    all_gather x3 -> x1, waiting for transfers between devices: 80.7 us -> 23.9 us  [local(): every = lax.all_gather(sent, ('expert', 'mp'), axis=0, tiled=True)]
    reduce_scatter x0 -> x1, waiting for transfers between devices: none -> 56 us  [local(): lax.psum_scatter(out.astype(BF), ('expert', 'mp'), scatter_dimension=0, t...]
    psum x0 -> x2, blocking collectives: none -> 36.4 us  [the longest x1 19.9 us: local(): inner = lax.psum(dot_nt(mine, left), 'mp').astype(BF)]
    all_to_all x5 -> x1, starting transfers between devices: 20.8 us -> 6.32 us  [local(): small = lax.all_to_all(small, 'mp', split_axis=3, concat_axis=2, tiled=True)]
    unnamed x21 -> x8, local copies, waits for them, and re-layouts: 12.4 us -> 0.02 us
    dot_general x6 -> x8, matrix products: 22.3 us -> 15.3 us  [the longest x4 10.8 us: dot_nt(): lax.dot_general(a, b, (((1,), (1,)), ((), ())), preferred_element_type=F32)]
    convert_element_type x1 -> x0, local copies, waits for them, and re-layouts: 3.74 us -> none  [local(): partials = result.astype(jnp.bfloat16)]
  transfers between devices with their start and end apart: 8 -> 3, of which waited for: 8 -> 3; matrix products, arithmetic and copies ran while one was open for 12% -> 2% of each run, Pallas kernels for 0% -> 0%
where the time goes in v1:
time: 170 us
  waiting for transfers between devices  88 us (52%)
  blocking collectives  36.4 us (21%)
  matrix products  15.3 us (9%)
  between operations  13.6 us (8%)
  starting transfers between devices  6.32 us (4%)
  local copies, waits for them, and re-layouts  5.37 us (3%)
  other arithmetic  4.8 us (3%)
    reduce_scatter x1, waiting for transfers between devices, local(): lax.psum_scatter(out.astype(BF), ('expert', 'mp'), scatter_dimension=0, t...  56 us
    all_gather x1, waiting for transfers between devices, local(): every = lax.all_gather(sent, ('expert', 'mp'), axis=0, tiled=True)  23.9 us
    psum x1, blocking collectives, local(): inner = lax.psum(dot_nt(mine, left), 'mp').astype(BF)  19.9 us
    psum x1, blocking collectives, local(): bottom = lax.psum(dot_nt(hidden, diag[2]), 'mp').astype(BF)  16.5 us
    dot_general x4, matrix products, dot_nt(): lax.dot_general(a, b, (((1,), (1,)), ((), ())), preferred_element_type=F32)  10.8 us
    all_to_all x1, waiting for transfers between devices, local(): small = lax.all_to_all(small, 'mp', split_axis=3, concat_axis=2, tiled=True)  8.07 us
    all_to_all x1, starting transfers between devices, local(): small = lax.all_to_all(small, 'mp', split_axis=3, concat_axis=2, tiled=True)  6.32 us
    dot_general x4, matrix products, dot_nn(): lax.dot_general(a, b, (((1,), (0,)), ((), ())), preferred_element_type=F32)  4.46 us
  transfers between devices with their start and end apart: 3, of which 3 were waited for; matrix products, arithmetic and copies ran while one was open for 2% of the time, Pallas kernels for 0%

profile of v1, /device:TPU:0, one launch (start us, length us, event | category | flops | bytes accessed | tf_op | source)
XLA Modules:
  0.0 169.8 jit_solution(17399230442323517228)
XLA Ops:
  6.5 0.9 select_reduce_fusion
  7.4 0.1 fusion.19
  7.5 1.5 pad_maximum_fusion.1
  9.0 0.9 stack.12
  9.9 0.9 stack.13
  10.8 0.9 stack.14
  11.8 0.2 pad_maximum_fusion
  11.9 0.7 copy.28
  12.7 6.3 %all-to-all-start = ((bf16[3,4,8,4,192]{4,2,1,0,3:T(8,128)(2,1)}), bf16[3,4,8,4,192]{4,2,1,0,3:T(8,128)(2,1)S(1)}, u32[]{:S(2)}, u32[]{:S(2)}) async-start(bf16[3,4,8,4,192]{4,2,1,0,3:T(8,128)(2,1)} %copy.28), calls=%async_computation | async-start | bytes 393216 | tf_op jit(solution)/shard_map/all_to_all | solution.py:61
  19.0 0.2 broadcast_compare_fusion
  19.2 8.1 %all-to-all-done = bf16[3,4,8,4,192]{4,2,1,0,3:T(8,128)(2,1)S(1)} async-done(((bf16[3,4,8,4,192]{4,2,1,0,3:T(8,128)(2,1)}), bf16[3,4,8,4,192]{4,2,1,0,3:T(8,128)(2,1)S(1)}, u32[]{:S(2)}, u32[]{:S(2)}) %all-to-all-start) | async-done | bytes 147488 | tf_op jit(solution)/shard_map/all_to_all | solution.py:61
  27.3 0.2 copy.30
  27.4 0.1 bitcast_select_fusion
  27.5 23.9 %all-gather.2.cloned.1.call-done = bf16[128,4224]{1,0:T(8,128)(2,1)} async-done(((bf16[8,4224]{1,0:T(8,128)(2,1)}), bf16[128,4224]{1,0:T(8,128)(2,1)}) %all-gather.2.cloned.1.call-update) | async-done | bytes 1081360 | tf_op jit(solution)/shard_map/all_gather | solution.py:52
  51.4 0.8 slice_convert_fusion
  52.2 0.1 fusion.26
  52.3 0.1 dynamic-slice_add_fusion
  52.4 0.1 copy.31
  52.5 0.2 copy.32
  52.7 1.4 slice.36
  54.1 0.3 fusion.4
  54.4 19.9 %all-reduce.2 = bf16[128,256]{1,0:T(8,128)(2,1)S(1)} all-reduce(f32[128,256]{1,0:T(8,128)S(1)} %fusion.4), channel_id=1, replica_groups=mesh['groups'=2,'expert'=4,'mp'=4] {'mp'}, use_global_device_ids=true, to_apply=%region_1.2 | all-reduce | flops 32768 | bytes 196608 | tf_op jit(solution)/shard_map/psum | solution.py:68
  74.3 5.3 %fusion.24 = f32[128,768]{1,0:T(8,128)S(1)} fusion(bf16[768,4096]{1,0:T(8,128)(2,1)} %bitcast.35, bf16[128,4224]{1,0:T(8,128)(2,1)} %all-gather.2.cloned.1.call-done), kind=kOutput, calls=%fused_computation.49 | convolution fusion | flops 805306368 | bytes 7733248 | tf_op jit(solution)/shard_map/dot_general | solution.py:11
  79.7 0.2 convolution_add_fusion.2
  79.9 5.0 %fusion.22 = f32[128,768]{1,0:T(8,128)S(1)} fusion(bf16[768,4096]{1,0:T(8,128)(2,1)} %bitcast.36, bf16[128,4224]{1,0:T(8,128)(2,1)S(1)} %copy-done.1), kind=kOutput, calls=%fused_computation.47 | convolution fusion | flops 805306368 | bytes 7733248 | tf_op jit(solution)/shard_map/dot_general | solution.py:11
  84.9 0.3 fusion.3
  85.1 0.2 fusion.9
  85.3 16.5 %psum.15 = bf16[128,128]{1,0:T(8,128)(2,1)S(1)} all-reduce(f32[128,128]{1,0:T(8,128)S(1)} %fusion.9), channel_id=1, replica_groups=mesh['groups'=2,'expert'=4,'mp'=4] {'mp'}, use_global_device_ids=true, to_apply=%region_2.3 | all-reduce | flops 16384 | bytes 98304 | tf_op jit(solution)/shard_map/psum | solution.py:76
  101.9 3.8 %fusion.27 = f32[128,4096]{1,0:T(8,128)S(1)} fusion(bf16[128,768]{1,0:T(8,128)(2,1)S(1)} %fusion.3, bf16[768,4096]{1,0:T(8,128)(2,1)} %bitcast.34), kind=kOutput, calls=%fused_computation.52 | convolution fusion | flops 805306368 | bytes 8585216 | tf_op jit(solution)/shard_map/dot_general | solution.py:15
  105.7 0.2 fusion
  105.9 1.1 convert_element_type.29
  107.0 56.0 %reduce-scatter.2.cloned.1.call-done = bf16[8,4096]{1,0:T(8,128)(2,1)} async-done(((bf16[128,4096]{1,0:T(8,128)(2,1)}), bf16[8,4096]{1,0:T(8,128)(2,1)}) %reduce-scatter.2.cloned.1.call-update) | async-done | bytes 65552 | tf_op jit(solution)/shard_map/reduce_scatter | solution.py:82
  (17 shorter events, 0.1 us)
Async XLA Ops:
  6.5 99.1 %copy-start = (bf16[4,32,1024]{2,1,0:T(8,128)(2,1)S(1)}, bf16[4,32,1024]{2,1,0:T(8,128)(2,1)}, u32[]{:S(2)}) copy-start(bf16[4,32,1024]{2,1,0:T(8,128)(2,1)} %param.23) | copy-start | bytes 786436
  6.5 47.5 %copy-start.2 = (bf16[4,32,1024]{2,1,0:T(8,128)(2,1)S(1)}, bf16[4,32,1024]{2,1,0:T(8,128)(2,1)}, u32[]{:S(2)}) copy-start(bf16[4,32,1024]{2,1,0:T(8,128)(2,1)} %param.20) | copy-start | bytes 786436
  6.5 47.5 %copy-start.3 = (bf16[4,32,1024]{2,1,0:T(8,128)(2,1)S(1)}, bf16[4,32,1024]{2,1,0:T(8,128)(2,1)}, u32[]{:S(2)}) copy-start(bf16[4,32,1024]{2,1,0:T(8,128)(2,1)} %param.18) | copy-start | bytes 786436
  6.5 44.9 %all-gather.2.cloned.1.call-start = ((), (), s32[]{:S(2)}) async-start(), calls=%async_computation.2 | async-start | bytes 1148928 | tf_op jit(solution)/shard_map/all_gather | solution.py:52
  12.7 14.6 %all-to-all-start = ((bf16[3,4,8,4,192]{4,2,1,0,3:T(8,128)(2,1)}), bf16[3,4,8,4,192]{4,2,1,0,3:T(8,128)(2,1)S(1)}, u32[]{:S(2)}, u32[]{:S(2)}) async-start(bf16[3,4,8,4,192]{4,2,1,0,3:T(8,128)(2,1)} %copy.28), calls=%async_computation | async-start | bytes 393216 | tf_op jit(solution)/shard_map/all_to_all | solution.py:61
  19.0 144.0 %reduce-scatter.2.cloned.1.call-start = ((), (), s32[]{:S(2)}) async-start(), calls=%async_computation.3 | async-start | bytes 1114112 | tf_op jit(solution)/shard_map/reduce_scatter | solution.py:82
  52.7 27.2 %copy-start.1 = (bf16[128,4224]{1,0:T(8,128)(2,1)S(1)}, bf16[128,4224]{1,0:T(8,128)(2,1)}, u32[]{:S(2)}) copy-start(bf16[128,4224]{1,0:T(8,128)(2,1)} %all-gather.2.cloned.1.call-done) | copy-start | bytes 3244036
Sparse Core Ops, SparseCore 0:
  9.6 41.8 all-gather.1
  107.1 55.8 reduce-scatter.1

commit v2 on v1

--- a/solution.py
+++ b/solution.py
@@ -36,11 +36,22 @@
     block = gate_left.shape[2]
     groups = lax.axis_size("expert")
     parts = lax.axis_size("mp")
+    chips = groups // 2
     experts = exp_dev * groups
     me_g = lax.axis_index("expert")
     me_m = lax.axis_index("mp")
     ranks = exp_dev * rank
     hid = exp_dev * cols
+
+    def along_z(value, step):
+        return lax.ppermute(value, "mp", [(i, (i + step) % parts) for i in range(parts)])
+
+    def along_y(value, step):
+        pairs = [(i, (i // 2 + step) % chips * 2 + i % 2) for i in range(groups)]
+        return lax.ppermute(value, "expert", pairs)
+
+    def other_core(value):
+        return lax.ppermute(value, "expert", [(i, i ^ 1) for i in range(groups)])
 
     chosen = routes[:, :, None] == jnp.arange(experts, dtype=jnp.int32)
     weight = jnp.sum(jnp.where(chosen, probs[:, :, None], 0.0), axis=1)
@@ -49,7 +60,11 @@
     side = jnp.concatenate([high.astype(BF), low], axis=1)
     pad = -(2 * experts) % 128
     sent = jnp.concatenate([tokens, jnp.pad(side, ((0, 0), (0, pad)))], axis=1)
-    every = lax.all_gather(sent, ("expert", "mp"), axis=0, tiled=True)
+
+    own = [sent] + [along_z(sent, k) for k in range(1, parts)]
+    near = [own] + [[along_y(p, s) for p in own] for s in range(1, chips)]
+    far = [[other_core(p) for p in line] for line in near]
+    every = jnp.concatenate([p for half in (near, far) for line in half for p in line])
     total = every.shape[0]
     x = every[:, :width]
     side = every[:, width : width + 2 * experts].astype(F32)
@@ -57,15 +72,30 @@
     weight = lax.dynamic_slice(weight, (0, me_g * exp_dev), (total, exp_dev))
 
     small = jnp.stack([gate_right, up_right, down_left])
-    small = small.reshape(3, exp_dev, piece, parts, cols)
-    small = lax.all_to_all(small, "mp", split_axis=3, concat_axis=2, tiled=True)
+    small = small.reshape(3 * exp_dev * piece, parts, cols).swapaxes(0, 1)
+    small = jnp.concatenate([small, small])
+    small = [
+        lax.dynamic_index_in_dim(small, me_m + k, 0, keepdims=False) for k in range(parts)
+    ]
+    small = [small[0]] + [along_z(small[k], k) for k in range(1, parts)]
+    small = jnp.stack([small[-k % parts] for k in range(parts)] * 2)
+    small = lax.dynamic_slice_in_dim(small, parts - me_m, parts, 0)
+    small = small.reshape(parts, 3, exp_dev, piece, cols).transpose(1, 2, 0, 3, 4)
     small = small.reshape(3, ranks, cols)
     same = (jnp.arange(ranks) // rank)[:, None] == (jnp.arange(hid) // cols)[None, :]
     diag = jnp.where(same, jnp.tile(small, (1, 1, exp_dev)), jnp.zeros((), BF))
 
+    def sum_parts(value):
+        value = value.astype(BF)
+        result = value.astype(F32)
+        lines = value.reshape(-1, parts, rows, value.shape[1])
+        for k in range(1, parts):
+            result += along_z(jnp.roll(lines, k, axis=1).reshape(value.shape), k).astype(F32)
+        return result.astype(BF)
+
     mine = lax.dynamic_slice(x, (0, me_m * block), (total, block))
     left = jnp.concatenate([gate_left.reshape(ranks, block), up_left.reshape(ranks, block)])
-    inner = lax.psum(dot_nt(mine, left), "mp").astype(BF)
+    inner = sum_parts(dot_nt(mine, left))
 
     gate_w = jnp.swapaxes(w_gate, 1, 2).reshape(hid, width)
     up_w = jnp.swapaxes(w_up, 1, 2).reshape(hid, width)
@@ -73,13 +103,26 @@
     up_act = dot_nt(x, up_w) + dot_nn(inner[:, ranks:], diag[1])
     scale = jnp.repeat(weight, cols, axis=1)
     hidden = (jax.nn.silu(gate_act) * up_act * scale).astype(BF)
-    bottom = lax.psum(dot_nt(hidden, diag[2]), "mp").astype(BF)
+    bottom = sum_parts(dot_nt(hidden, diag[2]))
     out = dot_nn(hidden, w_down.reshape(hid, width))
     extra = dot_nn(bottom, down_right.reshape(ranks, block))
     out = lax.dynamic_update_slice(
         out, extra + lax.dynamic_slice(out, (0, me_m * block), (total, block)), (0, me_m * block)
-    )
-    return lax.psum_scatter(out.astype(BF), ("expert", "mp"), scatter_dimension=0, tiled=True)
+    ).astype(BF)
+
+    out = out.reshape(2, chips, parts, rows, width)
+    out = out[0].astype(F32) + other_core(out[1]).astype(F32)
+    out = out.astype(BF)
+    lines = []
+    for k in range(parts):
+        line = out[0, k].astype(F32)
+        for s in range(1, chips):
+            line += along_y(out[s, k], -s).astype(F32)
+        lines.append(line)
+    result = lines[0]
+    for k in range(1, parts):
+        result += along_z(lines[k].astype(BF), -k).astype(F32)
+    return result.astype(BF)
 
 
 def solution(mesh):

time: 170 us -> 85.2 us (0.50)
  waiting for transfers between devices: 88 us -> 32.3 us
  blocking collectives: 36.4 us -> 0 us
  starting transfers between devices: 6.32 us -> 30 us
  between operations: 13.6 us -> 0.51 us
  matrix products: 15.3 us -> 12.4 us
  local copies, waits for them, and re-layouts: 5.37 us -> 3.64 us
    reduce_scatter x1 -> x0, waiting for transfers between devices: 56 us -> none  [local(): lax.psum_scatter(out.astype(BF), ('expert', 'mp'), scatter_dimension=0, t...]
    psum x2 -> x0, blocking collectives: 36.4 us -> none  [the longest x1 19.9 us: local(): inner = lax.psum(dot_nt(mine, left), 'mp').astype(BF)]
    ppermute x0 -> x32, waiting for transfers between devices: none -> 32.3 us  [the longest x15 19.4 us: along_z(): lax.ppermute(value, 'mp', [(i, (i + step) % parts) for i in range(parts)])]
    ppermute x0 -> x32, starting transfers between devices: none -> 30 us  [the longest x15 17 us: along_z(): lax.ppermute(value, 'mp', [(i, (i + step) % parts) for i in range(parts)])]
    all_gather x1 -> x0, waiting for transfers between devices: 23.9 us -> none  [local(): every = lax.all_gather(sent, ('expert', 'mp'), axis=0, tiled=True)]
    all_to_all x1 -> x0, waiting for transfers between devices: 8.07 us -> none  [local(): small = lax.all_to_all(small, 'mp', split_axis=3, concat_axis=2, tiled=True)]
    all_to_all x1 -> x0, starting transfers between devices: 6.32 us -> none  [local(): small = lax.all_to_all(small, 'mp', split_axis=3, concat_axis=2, tiled=True)]
    dot_general x4, matrix products: 4.46 us -> 1.63 us  [dot_nn(): lax.dot_general(a, b, (((1,), (0,)), ((), ())), preferred_element_type=F32)]
  transfers between devices with their start and end apart: 3 -> 32, of which waited for: 3 -> 18; matrix products, arithmetic and copies ran while one was open for 2% -> 8% of each run, Pallas kernels for 0% -> 0%
where the time goes in v2:
time: 85.2 us; the launch traced here: 85 us
  waiting for transfers between devices  32.3 us (38%)
  starting transfers between devices  30 us (35%)
  matrix products  12.4 us (15%)
  other arithmetic  6.13 us (7%)
  local copies, waits for them, and re-layouts  3.64 us (4%)
    ppermute x15, waiting for transfers between devices, along_z(): lax.ppermute(value, 'mp', [(i, (i + step) % parts) for i in range(parts)])  19.4 us
    ppermute x15, starting transfers between devices, along_z(): lax.ppermute(value, 'mp', [(i, (i + step) % parts) for i in range(parts)])  17 us
    ppermute x8, starting transfers between devices, along_y(): return lax.ppermute(value, 'expert', pairs)  11.1 us
    dot_general x4, matrix products, dot_nt(): lax.dot_general(a, b, (((1,), (1,)), ((), ())), preferred_element_type=F32)  10.8 us
    ppermute x8, waiting for transfers between devices, along_y(): return lax.ppermute(value, 'expert', pairs)  9.09 us
    ppermute x9, waiting for transfers between devices, other_core(): return lax.ppermute(value, 'expert', [(i, i ^ 1) for i in range(groups)])  3.74 us
    concatenate x1, other arithmetic, local(): small = jnp.concatenate([small, small])  2.09 us
    ppermute x9, starting transfers between devices, other_core(): return lax.ppermute(value, 'expert', [(i, i ^ 1) for i in range(groups)])  1.93 us
  transfers between devices with their start and end apart: 32, of which 18 were waited for; matrix products, arithmetic and copies ran while one was open for 8% of the time, Pallas kernels for 0%

profile of v2, /device:TPU:0, one launch (start us, length us, event | category | flops | bytes accessed | tf_op | source)
XLA Modules:
  0.0 85.0 jit_solution(8505302630486437003)
XLA Ops:
  1.8 3.0 %collective-permute-start.3 = (bf16[8,4224]{1,0:T(8,128)(2,1)S(1)}, bf16[8,4224]{1,0:T(8,128)(2,1)S(1)}, u32[]{:S(2)}, u32[]{:S(2)}) collective-permute-start(bf16[8,4224]{1,0:T(8,128)(2,1)S(1)} %get-tuple-element.18), channel_id=1, source_target_pairs={{0,8},{4,12},{8,0},{12,4},{1,9},{5,13},{9,1},{13,5},{2,10},{6,14},... | collective-permute-start | bytes 202760 | tf_op jit(solution)/shard_map/ppermute | solution.py:51
  4.8 3.6 %collective-permute-start.2 = (bf16[8,4224]{1,0:T(8,128)(2,1)S(1)}, bf16[8,4224]{1,0:T(8,128)(2,1)S(1)}, u32[]{:S(2)}, u32[]{:S(2)}) collective-permute-start(bf16[8,4224]{1,0:T(8,128)(2,1)S(1)} %get-tuple-element.18), channel_id=1, source_target_pairs={{0,3},{1,0},{2,1},{3,2},{4,7},{5,4},{6,5},{7,6},{8,11},{9,8},{10,9... | collective-permute-start | bytes 202760 | tf_op jit(solution)/shard_map/ppermute | solution.py:47
  9.5 2.1 %fusion.15 = (bf16[1,96,192]{2,0,1:T(2,128)(2,1)S(1)}, bf16[1,96,192]{2,0,1:T(2,128)(2,1)S(1)}, bf16[1,96,192]{2,0,1:T(2,128)(2,1)S(1)}, bf16[1,96,192]{2,0,1:T(2,128)(2,1)S(1)}) fusion(s32[]{:T(128)S(6)} %select_n.57, bf16[4,96,192]{2,0,1:T(4,128)(2,1)S(1)} %bitcast.104, s32[]{:T(128)S(6)} %select_n.56, s32[]{:T(128)S(6)} %select_n.55, s32[]{:T(128)S(6)} %select_n.54), kind=kLoop, calls=%fused_computation.41 | loop fusion | flops 294912 | bytes 294928 | tf_op jit(solution)/shard_map/concatenate | solution.py:76
  12.2 1.6 %collective-permute-start.20 = (bf16[96,192]{1,0:T(8,128)(2,1)S(1)}, bf16[96,192]{1,0:T(8,128)(2,1)S(1)}, u32[]{:S(2)}, u32[]{:S(2)}) collective-permute-start(bf16[96,192]{1,0:T(8,128)(2,1)S(1)} %bitcast.114), channel_id=1, source_target_pairs={{0,1},{1,2},{2,3},{3,0},{4,5},{5,6},{6,7},{7,4},{8,9},{9,10},{10,1... | collective-permute-start | bytes 110600 | tf_op jit(solution)/shard_map/ppermute | solution.py:47
  14.0 1.7 %collective-permute-done.18 = bf16[96,192]{1,0:T(8,128)(2,1)S(1)} collective-permute-done((bf16[96,192]{1,0:T(8,128)(2,1)S(1)}, bf16[96,192]{1,0:T(8,128)(2,1)S(1)}, u32[]{:S(2)}, u32[]{:S(2)}) %collective-permute-start.18) | collective-permute-done | bytes 36896 | tf_op jit(solution)/shard_map/ppermute | solution.py:47
  15.8 1.3 %collective-permute-start.1 = (bf16[8,4224]{1,0:T(8,128)(2,1)S(1)}, bf16[8,4224]{1,0:T(8,128)(2,1)S(1)}, u32[]{:S(2)}, u32[]{:S(2)}) collective-permute-start(bf16[8,4224]{1,0:T(8,128)(2,1)S(1)} %get-tuple-element.18), channel_id=1, source_target_pairs={{0,2},{1,3},{2,0},{3,1},{4,6},{5,7},{6,4},{7,5},{8,10},{9,11},{10,... | collective-permute-start | bytes 202760 | tf_op jit(solution)/shard_map/ppermute | solution.py:47
  17.3 2.0 %collective-permute-start = (bf16[8,4224]{1,0:T(8,128)(2,1)S(1)}, bf16[8,4224]{1,0:T(8,128)(2,1)S(1)}, u32[]{:S(2)}, u32[]{:S(2)}) collective-permute-start(bf16[8,4224]{1,0:T(8,128)(2,1)S(1)} %get-tuple-element.18), channel_id=1, source_target_pairs={{0,1},{1,2},{2,3},{3,0},{4,5},{5,6},{6,7},{7,4},{8,9},{9,10},{10,1... | collective-permute-start | bytes 202760 | tf_op jit(solution)/shard_map/ppermute | solution.py:47
  19.5 1.2 %stack.36 = bf16[8,96,192]{2,0,1:T(8,128)(2,1)S(1)} concatenate(bf16[1,96,192]{2,0,1:T(2,128)(2,1)S(1)} %get-tuple-element.17, bf16[1,96,192]{2,0,1:T(2,128)(2,1)S(1)} %copy.27, bf16[1,96,192]{2,0,1:T(2,128)(2,1)S(1)} %copy.28, bf16[1,96,192]{2,0,1:T(2,128)(2,1)S(1)} %copy.29, bf16[1,96,192]{2,0,1:T(2,128)(2,1)S(1)} %get-tuple-element.17, bf16[1,96,192]{2,0,1:T(2,128)(2,1)S(1)} %copy.27, ...), dimensions={0} | concatenate | bytes 589824 | tf_op jit(solution)/shard_map/stack | solution.py:81
  21.7 1.6 %collective-permute-done = bf16[8,4224]{1,0:T(8,128)(2,1)S(1)} collective-permute-done((bf16[8,4224]{1,0:T(8,128)(2,1)S(1)}, bf16[8,4224]{1,0:T(8,128)(2,1)S(1)}, u32[]{:S(2)}, u32[]{:S(2)}) %collective-permute-start) | collective-permute-done | bytes 67616 | tf_op jit(solution)/shard_map/ppermute | solution.py:47
  23.9 1.6 %collective-permute-start.4 = (bf16[8,4224]{1,0:T(8,128)(2,1)S(1)}, bf16[8,4224]{1,0:T(8,128)(2,1)S(1)}, u32[]{:S(2)}, u32[]{:S(2)}) collective-permute-start(bf16[8,4224]{1,0:T(8,128)(2,1)S(1)} %collective-permute-done), channel_id=1, source_target_pairs={{0,8},{4,12},{8,0},{12,4},{1,9},{5,13},{9,1},{13,5},{2,10},{6,14},... | collective-permute-start | bytes 202760 | tf_op jit(solution)/shard_map/ppermute | solution.py:51
  25.5 2.9 %collective-permute-done.4 = bf16[8,4224]{1,0:T(8,128)(2,1)S(1)} collective-permute-done((bf16[8,4224]{1,0:T(8,128)(2,1)S(1)}, bf16[8,4224]{1,0:T(8,128)(2,1)S(1)}, u32[]{:S(2)}, u32[]{:S(2)}) %collective-permute-start.4) | collective-permute-done | bytes 67616 | tf_op jit(solution)/shard_map/ppermute | solution.py:51
  28.4 1.8 %collective-permute-start.5 = (bf16[8,4224]{1,0:T(8,128)(2,1)S(1)}, bf16[8,4224]{1,0:T(8,128)(2,1)S(1)}, u32[]{:S(2)}, u32[]{:S(2)}) collective-permute-start(bf16[8,4224]{1,0:T(8,128)(2,1)S(1)} %collective-permute-done.1), channel_id=1, source_target_pairs={{0,8},{4,12},{8,0},{12,4},{1,9},{5,13},{9,1},{13,5},{2,10},{6,14},... | collective-permute-start | bytes 202760 | tf_op jit(solution)/shard_map/ppermute | solution.py:51
  30.2 2.4 %collective-permute-done.5 = bf16[8,4224]{1,0:T(8,128)(2,1)S(1)} collective-permute-done((bf16[8,4224]{1,0:T(8,128)(2,1)S(1)}, bf16[8,4224]{1,0:T(8,128)(2,1)S(1)}, u32[]{:S(2)}, u32[]{:S(2)}) %collective-permute-start.5) | collective-permute-done | bytes 67616 | tf_op jit(solution)/shard_map/ppermute | solution.py:51
  34.8 1.0 %collective-permute-done.12 = bf16[8,4224]{1,0:T(8,128)(2,1)S(1)} collective-permute-done((bf16[8,4224]{1,0:T(8,128)(2,1)S(1)}, bf16[8,4224]{1,0:T(8,128)(2,1)S(1)}, u32[]{:S(2)}, u32[]{:S(2)}) %collective-permute-start.12) | collective-permute-done | bytes 67616 | tf_op jit(solution)/shard_map/ppermute | solution.py:54
  37.8 2.3 %collective-permute-start.17 = (bf16[128,256]{1,0:T(8,128)(2,1)S(1)}, bf16[128,256]{1,0:T(8,128)(2,1)S(1)}, u32[]{:S(2)}, u32[]{:S(2)}) collective-permute-start(bf16[128,256]{1,0:T(8,128)(2,1)S(1)} %bitcast.107), channel_id=1, source_target_pairs={{0,3},{1,0},{2,1},{3,2},{4,7},{5,4},{6,5},{7,6},{8,11},{9,8},{10,9... | collective-permute-start | bytes 196616 | tf_op jit(solution)/shard_map/ppermute | solution.py:47
  40.6 3.1 %collective-permute-done.16 = bf16[128,256]{1,0:T(8,128)(2,1)S(1)} collective-permute-done((bf16[128,256]{1,0:T(8,128)(2,1)S(1)}, bf16[128,256]{1,0:T(8,128)(2,1)S(1)}, u32[]{:S(2)}, u32[]{:S(2)}) %collective-permute-start.16) | collective-permute-done | bytes 65568 | tf_op jit(solution)/shard_map/ppermute | solution.py:47
  43.7 2.7 %collective-permute-done.15 = bf16[128,256]{1,0:T(8,128)(2,1)S(1)} collective-permute-done((bf16[128,256]{1,0:T(8,128)(2,1)S(1)}, bf16[128,256]{1,0:T(8,128)(2,1)S(1)}, u32[]{:S(2)}, u32[]{:S(2)}) %collective-permute-start.15) | collective-permute-done | bytes 65568 | tf_op jit(solution)/shard_map/ppermute | solution.py:47
  46.8 5.1 %convolution_add_fusion.2 = f32[128,768]{1,0:T(8,128)S(1)} fusion(f32[128,768]{1,0:T(8,128)S(1)} %fusion.7, bf16[768,4096]{1,0:T(8,128)(2,1)} %bitcast.93, bf16[128,4224]{1,0:T(8,128)(2,1)S(1)} %constant_dynamic-update-slice_fusion), kind=kOutput, calls=%fused_computation.3 | convolution fusion | flops 805404672 | bytes 8126464 | tf_op jit(solution)/shard_map/dot_general | solution.py:11
  52.0 5.1 %multiply_convert_fusion = bf16[128,768]{1,0:T(8,128)(2,1)S(1)} fusion(f32[128,768]{1,0:T(8,128)S(1)} %copy.37, f32[128,768]{1,0:T(8,128)S(1)} %convolution_add_fusion.2, f32[128,768]{1,0:T(8,128)S(1)} %fusion.6, bf16[768,4096]{1,0:T(8,128)(2,1)} %bitcast.121, bf16[128,4224]{1,0:T(8,128)(2,1)S(1)} %constant_dynamic-update-slice_fusion), kind=kOutput, calls=%fused_computation.20 | convolution fusion | flops 806092800 | bytes 8716288 | tf_op jit(solution)/shard_map/dot_general | solution.py:11
  58.1 2.4 %collective-permute-start.23 = (bf16[128,128]{1,0:T(8,128)(2,1)S(1)}, bf16[128,128]{1,0:T(8,128)(2,1)S(1)}, u32[]{:S(2)}, u32[]{:S(2)}) collective-permute-start(bf16[128,128]{1,0:T(8,128)(2,1)S(1)} %bitcast.119), channel_id=1, source_target_pairs={{0,3},{1,0},{2,1},{3,2},{4,7},{5,4},{6,5},{7,6},{8,11},{9,8},{10,9... | collective-permute-start | bytes 98312 | tf_op jit(solution)/shard_map/ppermute | solution.py:47
  60.5 1.0 %fusion.42 = f32[128,4096]{1,0:T(8,128)S(1)} fusion(bf16[128,768]{1,0:T(8,128)(2,1)S(1)} %multiply_convert_fusion, bf16[768,4096]{1,0:T(8,128)(2,1)S(1)} %bitcast.92), kind=kOutput, calls=%fused_computation.117 | convolution fusion | flops 805306368 | bytes 8585216 | tf_op jit(solution)/shard_map/dot_general | solution.py:15
  61.5 1.1 %collective-permute-done.22 = bf16[128,128]{1,0:T(8,128)(2,1)S(1)} collective-permute-done((bf16[128,128]{1,0:T(8,128)(2,1)S(1)}, bf16[128,128]{1,0:T(8,128)(2,1)S(1)}, u32[]{:S(2)}, u32[]{:S(2)}) %collective-permute-start.22) | collective-permute-done | bytes 32800 | tf_op jit(solution)/shard_map/ppermute | solution.py:47
  62.6 3.5 %collective-permute-done.21 = bf16[128,128]{1,0:T(8,128)(2,1)S(1)} collective-permute-done((bf16[128,128]{1,0:T(8,128)(2,1)S(1)}, bf16[128,128]{1,0:T(8,128)(2,1)S(1)}, u32[]{:S(2)}, u32[]{:S(2)}) %collective-permute-start.21) | collective-permute-done | bytes 32800 | tf_op jit(solution)/shard_map/ppermute | solution.py:47
  66.7 1.9 %collective-permute-done.24 = bf16[2,4,8,4096]{3,2,1,0:T(8,128)(2,1)S(1)} collective-permute-done((bf16[2,4,8,4096]{3,2,1,0:T(8,128)(2,1)S(1)}, bf16[2,4,8,4096]{3,2,1,0:T(8,128)(2,1)S(1)}, u32[]{:S(2)}, u32[]{:S(2)}) %collective-permute-start.24) | collective-permute-done | bytes 524320 | tf_op jit(solution)/shard_map/ppermute | solution.py:54
  68.7 1.9 %collective-permute-start.30 = (bf16[8,4096]{1,0:T(8,128)(2,1)S(1)}, bf16[8,4096]{1,0:T(8,128)(2,1)S(1)}, u32[]{:S(2)}, u32[]{:S(2)}) collective-permute-start(bf16[8,4096]{1,0:T(8,128)(2,1)S(1)} %get-tuple-element.8), channel_id=1, source_target_pairs={{0,8},{4,12},{8,0},{12,4},{1,9},{5,13},{9,1},{13,5},{2,10},{6,14},... | collective-permute-start | bytes 196616 | tf_op jit(solution)/shard_map/ppermute | solution.py:51
  70.8 1.9 %collective-permute-start.26 = (bf16[8,4096]{1,0:T(8,128)(2,1)S(1)}, bf16[8,4096]{1,0:T(8,128)(2,1)S(1)}, u32[]{:S(2)}, u32[]{:S(2)}) collective-permute-start(bf16[8,4096]{1,0:T(8,128)(2,1)S(1)} %get-tuple-element.10), channel_id=1, source_target_pairs={{0,8},{4,12},{8,0},{12,4},{1,9},{5,13},{9,1},{13,5},{2,10},{6,14},... | collective-permute-start | bytes 196616 | tf_op jit(solution)/shard_map/ppermute | solution.py:51
  73.1 2.5 %collective-permute-done.28 = bf16[8,4096]{1,0:T(8,128)(2,1)S(1)} collective-permute-done((bf16[8,4096]{1,0:T(8,128)(2,1)S(1)}, bf16[8,4096]{1,0:T(8,128)(2,1)S(1)}, u32[]{:S(2)}, u32[]{:S(2)}) %collective-permute-start.28) | collective-permute-done | bytes 65568 | tf_op jit(solution)/shard_map/ppermute | solution.py:51
  75.7 1.0 %collective-permute-done.26 = bf16[8,4096]{1,0:T(8,128)(2,1)S(1)} collective-permute-done((bf16[8,4096]{1,0:T(8,128)(2,1)S(1)}, bf16[8,4096]{1,0:T(8,128)(2,1)S(1)}, u32[]{:S(2)}, u32[]{:S(2)}) %collective-permute-start.26) | collective-permute-done | bytes 65568 | tf_op jit(solution)/shard_map/ppermute | solution.py:51
  76.8 2.0 %collective-permute-start.31 = (bf16[8,4096]{1,0:T(8,128)(2,1)S(1)}, bf16[8,4096]{1,0:T(8,128)(2,1)S(1)}, u32[]{:S(2)}, u32[]{:S(2)}) collective-permute-start(bf16[8,4096]{1,0:T(8,128)(2,1)S(1)} %get-tuple-element.12), channel_id=1, source_target_pairs={{0,1},{1,2},{2,3},{3,0},{4,5},{5,6},{6,7},{7,4},{8,9},{9,10},{10,1... | collective-permute-start | bytes 196616 | tf_op jit(solution)/shard_map/ppermute | solution.py:47
  78.8 2.3 %collective-permute-done.27 = bf16[8,4096]{1,0:T(8,128)(2,1)S(1)} collective-permute-done((bf16[8,4096]{1,0:T(8,128)(2,1)S(1)}, bf16[8,4096]{1,0:T(8,128)(2,1)S(1)}, u32[]{:S(2)}, u32[]{:S(2)}) %collective-permute-start.27) | collective-permute-done | bytes 65568 | tf_op jit(solution)/shard_map/ppermute | solution.py:47
  81.1 1.8 %collective-permute-done.31 = bf16[8,4096]{1,0:T(8,128)(2,1)S(1)} collective-permute-done((bf16[8,4096]{1,0:T(8,128)(2,1)S(1)}, bf16[8,4096]{1,0:T(8,128)(2,1)S(1)}, u32[]{:S(2)}, u32[]{:S(2)}) %collective-permute-start.31) | collective-permute-done | bytes 65568 | tf_op jit(solution)/shard_map/ppermute | solution.py:47
  82.9 1.4 %collective-permute-done.29 = bf16[8,4096]{1,0:T(8,128)(2,1)S(1)} collective-permute-done((bf16[8,4096]{1,0:T(8,128)(2,1)S(1)}, bf16[8,4096]{1,0:T(8,128)(2,1)S(1)}, u32[]{:S(2)}, u32[]{:S(2)}) %collective-permute-start.29) | collective-permute-done | bytes 65568 | tf_op jit(solution)/shard_map/ppermute | solution.py:47
  (114 shorter events, 13.4 us)
Async XLA Ops:
  1.8 22.1 %collective-permute-start.3 = (bf16[8,4224]{1,0:T(8,128)(2,1)S(1)}, bf16[8,4224]{1,0:T(8,128)(2,1)S(1)}, u32[]{:S(2)}, u32[]{:S(2)}) collective-permute-start(bf16[8,4224]{1,0:T(8,128)(2,1)S(1)} %get-tuple-element.18), channel_id=1, source_target_pairs={{0,8},{4,12},{8,0},{12,4},{1,9},{5,13},{9,1},{13,5},{2,10},{6,14},... | collective-permute-start | bytes 202760 | tf_op jit(solution)/shard_map/ppermute | solution.py:51
  4.8 16.3 %collective-permute-start.2 = (bf16[8,4224]{1,0:T(8,128)(2,1)S(1)}, bf16[8,4224]{1,0:T(8,128)(2,1)S(1)}, u32[]{:S(2)}, u32[]{:S(2)}) collective-permute-start(bf16[8,4224]{1,0:T(8,128)(2,1)S(1)} %get-tuple-element.18), channel_id=1, source_target_pairs={{0,3},{1,0},{2,1},{3,2},{4,7},{5,4},{6,5},{7,6},{8,11},{9,8},{10,9... | collective-permute-start | bytes 202760 | tf_op jit(solution)/shard_map/ppermute | solution.py:47
  11.6 4.1 %collective-permute-start.18 = (bf16[96,192]{1,0:T(8,128)(2,1)S(1)}, bf16[96,192]{1,0:T(8,128)(2,1)S(1)}, u32[]{:S(2)}, u32[]{:S(2)}) collective-permute-start(bf16[96,192]{1,0:T(8,128)(2,1)S(1)} %bitcast.117), channel_id=1, source_target_pairs={{0,3},{1,0},{2,1},{3,2},{4,7},{5,4},{6,5},{7,6},{8,11},{9,8},{10,9... | collective-permute-start | bytes 110600 | tf_op jit(solution)/shard_map/ppermute | solution.py:47
  12.1 5.1 %collective-permute-start.19 = (bf16[96,192]{1,0:T(8,128)(2,1)S(1)}, bf16[96,192]{1,0:T(8,128)(2,1)S(1)}, u32[]{:S(2)}, u32[]{:S(2)}) collective-permute-start(bf16[96,192]{1,0:T(8,128)(2,1)S(1)} %bitcast.116), channel_id=1, source_target_pairs={{0,2},{1,3},{2,0},{3,1},{4,6},{5,7},{6,4},{7,5},{8,10},{9,11},{10,... | collective-permute-start | bytes 110600 | tf_op jit(solution)/shard_map/ppermute | solution.py:47
  12.2 7.2 %collective-permute-start.20 = (bf16[96,192]{1,0:T(8,128)(2,1)S(1)}, bf16[96,192]{1,0:T(8,128)(2,1)S(1)}, u32[]{:S(2)}, u32[]{:S(2)}) collective-permute-start(bf16[96,192]{1,0:T(8,128)(2,1)S(1)} %bitcast.114), channel_id=1, source_target_pairs={{0,1},{1,2},{2,3},{3,0},{4,5},{5,6},{6,7},{7,4},{8,9},{9,10},{10,1... | collective-permute-start | bytes 110600 | tf_op jit(solution)/shard_map/ppermute | solution.py:47
  15.8 9.7 %collective-permute-start.1 = (bf16[8,4224]{1,0:T(8,128)(2,1)S(1)}, bf16[8,4224]{1,0:T(8,128)(2,1)S(1)}, u32[]{:S(2)}, u32[]{:S(2)}) collective-permute-start(bf16[8,4224]{1,0:T(8,128)(2,1)S(1)} %get-tuple-element.18), channel_id=1, source_target_pairs={{0,2},{1,3},{2,0},{3,1},{4,6},{5,7},{6,4},{7,5},{8,10},{9,11},{10,... | collective-permute-start | bytes 202760 | tf_op jit(solution)/shard_map/ppermute | solution.py:47
  17.3 6.1 %collective-permute-start = (bf16[8,4224]{1,0:T(8,128)(2,1)S(1)}, bf16[8,4224]{1,0:T(8,128)(2,1)S(1)}, u32[]{:S(2)}, u32[]{:S(2)}) collective-permute-start(bf16[8,4224]{1,0:T(8,128)(2,1)S(1)} %get-tuple-element.18), channel_id=1, source_target_pairs={{0,1},{1,2},{2,3},{3,0},{4,5},{5,6},{6,7},{7,4},{8,9},{9,10},{10,1... | collective-permute-start | bytes 202760 | tf_op jit(solution)/shard_map/ppermute | solution.py:47
  19.4 13.9 %collective-permute-start.7 = (bf16[8,4224]{1,0:T(8,128)(2,1)S(1)}, bf16[8,4224]{1,0:T(8,128)(2,1)S(1)}, u32[]{:S(2)}, u32[]{:S(2)}) collective-permute-start(bf16[8,4224]{1,0:T(8,128)(2,1)S(1)} %get-tuple-element.18), channel_id=1, source_target_pairs={{0,4},{4,0},{8,12},{12,8},{1,5},{5,1},{9,13},{13,9},{2,6},{6,2},{1... | collective-permute-start | bytes 202760 | tf_op jit(solution)/shard_map/ppermute | solution.py:54
  21.2 13.6 %collective-permute-start.10 = (bf16[8,4224]{1,0:T(8,128)(2,1)S(1)}, bf16[8,4224]{1,0:T(8,128)(2,1)S(1)}, u32[]{:S(2)}, u32[]{:S(2)}) collective-permute-start(bf16[8,4224]{1,0:T(8,128)(2,1)S(1)} %collective-permute-done.2), channel_id=1, source_target_pairs={{0,4},{4,0},{8,12},{12,8},{1,5},{5,1},{9,13},{13,9},{2,6},{6,2},{1... | collective-permute-start | bytes 202760 | tf_op jit(solution)/shard_map/ppermute | solution.py:54
  23.4 9.3 %collective-permute-start.6 = (bf16[8,4224]{1,0:T(8,128)(2,1)S(1)}, bf16[8,4224]{1,0:T(8,128)(2,1)S(1)}, u32[]{:S(2)}, u32[]{:S(2)}) collective-permute-start(bf16[8,4224]{1,0:T(8,128)(2,1)S(1)} %collective-permute-done.2), channel_id=1, source_target_pairs={{0,8},{4,12},{8,0},{12,4},{1,9},{5,13},{9,1},{13,5},{2,10},{6,14},... | collective-permute-start | bytes 202760 | tf_op jit(solution)/shard_map/ppermute | solution.py:51
  23.9 4.5 %collective-permute-start.4 = (bf16[8,4224]{1,0:T(8,128)(2,1)S(1)}, bf16[8,4224]{1,0:T(8,128)(2,1)S(1)}, u32[]{:S(2)}, u32[]{:S(2)}) collective-permute-start(bf16[8,4224]{1,0:T(8,128)(2,1)S(1)} %collective-permute-done), channel_id=1, source_target_pairs={{0,8},{4,12},{8,0},{12,4},{1,9},{5,13},{9,1},{13,5},{2,10},{6,14},... | collective-permute-start | bytes 202760 | tf_op jit(solution)/shard_map/ppermute | solution.py:51
  25.5 9.3 %collective-permute-start.11 = (bf16[8,4224]{1,0:T(8,128)(2,1)S(1)}, bf16[8,4224]{1,0:T(8,128)(2,1)S(1)}, u32[]{:S(2)}, u32[]{:S(2)}) collective-permute-start(bf16[8,4224]{1,0:T(8,128)(2,1)S(1)} %collective-permute-done.3), channel_id=1, source_target_pairs={{0,4},{4,0},{8,12},{12,8},{1,5},{5,1},{9,13},{13,9},{2,6},{6,2},{1... | collective-permute-start | bytes 202760 | tf_op jit(solution)/shard_map/ppermute | solution.py:54
  28.4 4.3 %collective-permute-start.5 = (bf16[8,4224]{1,0:T(8,128)(2,1)S(1)}, bf16[8,4224]{1,0:T(8,128)(2,1)S(1)}, u32[]{:S(2)}, u32[]{:S(2)}) collective-permute-start(bf16[8,4224]{1,0:T(8,128)(2,1)S(1)} %collective-permute-done.1), channel_id=1, source_target_pairs={{0,8},{4,12},{8,0},{12,4},{1,9},{5,13},{9,1},{13,5},{2,10},{6,14},... | collective-permute-start | bytes 202760 | tf_op jit(solution)/shard_map/ppermute | solution.py:51
  32.7 1.9 %collective-permute-start.9 = (bf16[8,4224]{1,0:T(8,128)(2,1)S(1)}, bf16[8,4224]{1,0:T(8,128)(2,1)S(1)}, u32[]{:S(2)}, u32[]{:S(2)}) collective-permute-start(bf16[8,4224]{1,0:T(8,128)(2,1)S(1)} %collective-permute-done.1), channel_id=1, source_target_pairs={{0,4},{4,0},{8,12},{12,8},{1,5},{5,1},{9,13},{13,9},{2,6},{6,2},{1... | collective-permute-start | bytes 202760 | tf_op jit(solution)/shard_map/ppermute | solution.py:54
  32.7 1.5 %collective-permute-start.8 = (bf16[8,4224]{1,0:T(8,128)(2,1)S(1)}, bf16[8,4224]{1,0:T(8,128)(2,1)S(1)}, u32[]{:S(2)}, u32[]{:S(2)}) collective-permute-start(bf16[8,4224]{1,0:T(8,128)(2,1)S(1)} %collective-permute-done), channel_id=1, source_target_pairs={{0,4},{4,0},{8,12},{12,8},{1,5},{5,1},{9,13},{13,9},{2,6},{6,2},{1... | collective-permute-start | bytes 202760 | tf_op jit(solution)/shard_map/ppermute | solution.py:54
  33.3 2.6 %collective-permute-start.14 = (bf16[8,4224]{1,0:T(8,128)(2,1)S(1)}, bf16[8,4224]{1,0:T(8,128)(2,1)S(1)}, u32[]{:S(2)}, u32[]{:S(2)}) collective-permute-start(bf16[8,4224]{1,0:T(8,128)(2,1)S(1)} %collective-permute-done.6), channel_id=1, source_target_pairs={{0,4},{4,0},{8,12},{12,8},{1,5},{5,1},{9,13},{13,9},{2,6},{6,2},{1... | collective-permute-start | bytes 202760 | tf_op jit(solution)/shard_map/ppermute | solution.py:54
  34.1 1.7 %collective-permute-start.13 = (bf16[8,4224]{1,0:T(8,128)(2,1)S(1)}, bf16[8,4224]{1,0:T(8,128)(2,1)S(1)}, u32[]{:S(2)}, u32[]{:S(2)}) collective-permute-start(bf16[8,4224]{1,0:T(8,128)(2,1)S(1)} %collective-permute-done.5), channel_id=1, source_target_pairs={{0,4},{4,0},{8,12},{12,8},{1,5},{5,1},{9,13},{13,9},{2,6},{6,2},{1... | collective-permute-start | bytes 202760 | tf_op jit(solution)/shard_map/ppermute | solution.py:54
  34.5 1.3 %collective-permute-start.12 = (bf16[8,4224]{1,0:T(8,128)(2,1)S(1)}, bf16[8,4224]{1,0:T(8,128)(2,1)S(1)}, u32[]{:S(2)}, u32[]{:S(2)}) collective-permute-start(bf16[8,4224]{1,0:T(8,128)(2,1)S(1)} %collective-permute-done.4), channel_id=1, source_target_pairs={{0,4},{4,0},{8,12},{12,8},{1,5},{5,1},{9,13},{13,9},{2,6},{6,2},{1... | collective-permute-start | bytes 202760 | tf_op jit(solution)/shard_map/ppermute | solution.py:54
  37.4 6.3 %collective-permute-start.16 = (bf16[128,256]{1,0:T(8,128)(2,1)S(1)}, bf16[128,256]{1,0:T(8,128)(2,1)S(1)}, u32[]{:S(2)}, u32[]{:S(2)}) collective-permute-start(bf16[128,256]{1,0:T(8,128)(2,1)S(1)} %bitcast.106), channel_id=1, source_target_pairs={{0,2},{1,3},{2,0},{3,1},{4,6},{5,7},{6,4},{7,5},{8,10},{9,11},{10,... | collective-permute-start | bytes 196616 | tf_op jit(solution)/shard_map/ppermute | solution.py:47
  37.8 5.9 %collective-permute-start.17 = (bf16[128,256]{1,0:T(8,128)(2,1)S(1)}, bf16[128,256]{1,0:T(8,128)(2,1)S(1)}, u32[]{:S(2)}, u32[]{:S(2)}) collective-permute-start(bf16[128,256]{1,0:T(8,128)(2,1)S(1)} %bitcast.107), channel_id=1, source_target_pairs={{0,3},{1,0},{2,1},{3,2},{4,7},{5,4},{6,5},{7,6},{8,11},{9,8},{10,9... | collective-permute-start | bytes 196616 | tf_op jit(solution)/shard_map/ppermute | solution.py:47
  40.1 6.2 %collective-permute-start.15 = (bf16[128,256]{1,0:T(8,128)(2,1)S(1)}, bf16[128,256]{1,0:T(8,128)(2,1)S(1)}, u32[]{:S(2)}, u32[]{:S(2)}) collective-permute-start(bf16[128,256]{1,0:T(8,128)(2,1)S(1)} %bitcast.108), channel_id=1, source_target_pairs={{0,1},{1,2},{2,3},{3,0},{4,5},{5,6},{6,7},{7,4},{8,9},{9,10},{10,1... | collective-permute-start | bytes 196616 | tf_op jit(solution)/shard_map/ppermute | solution.py:47
  57.4 5.2 %collective-permute-start.22 = (bf16[128,128]{1,0:T(8,128)(2,1)S(1)}, bf16[128,128]{1,0:T(8,128)(2,1)S(1)}, u32[]{:S(2)}, u32[]{:S(2)}) collective-permute-start(bf16[128,128]{1,0:T(8,128)(2,1)S(1)} %bitcast.118), channel_id=1, source_target_pairs={{0,2},{1,3},{2,0},{3,1},{4,6},{5,7},{6,4},{7,5},{8,10},{9,11},{10,... | collective-permute-start | bytes 98312 | tf_op jit(solution)/shard_map/ppermute | solution.py:47
  58.1 4.5 %collective-permute-start.23 = (bf16[128,128]{1,0:T(8,128)(2,1)S(1)}, bf16[128,128]{1,0:T(8,128)(2,1)S(1)}, u32[]{:S(2)}, u32[]{:S(2)}) collective-permute-start(bf16[128,128]{1,0:T(8,128)(2,1)S(1)} %bitcast.119), channel_id=1, source_target_pairs={{0,3},{1,0},{2,1},{3,2},{4,7},{5,4},{6,5},{7,6},{8,11},{9,8},{10,9... | collective-permute-start | bytes 98312 | tf_op jit(solution)/shard_map/ppermute | solution.py:47
  60.5 5.7 %collective-permute-start.21 = (bf16[128,128]{1,0:T(8,128)(2,1)S(1)}, bf16[128,128]{1,0:T(8,128)(2,1)S(1)}, u32[]{:S(2)}, u32[]{:S(2)}) collective-permute-start(bf16[128,128]{1,0:T(8,128)(2,1)S(1)} %bitcast.120), channel_id=1, source_target_pairs={{0,1},{1,2},{2,3},{3,0},{4,5},{5,6},{6,7},{7,4},{8,9},{9,10},{10,1... | collective-permute-start | bytes 98312 | tf_op jit(solution)/shard_map/ppermute | solution.py:47
  66.6 2.0 %collective-permute-start.24 = (bf16[2,4,8,4096]{3,2,1,0:T(8,128)(2,1)S(1)}, bf16[2,4,8,4096]{3,2,1,0:T(8,128)(2,1)S(1)}, u32[]{:S(2)}, u32[]{:S(2)}) collective-permute-start(bf16[2,4,8,4096]{3,2,1,0:T(8,128)(2,1)S(1)} %bitcast.105), channel_id=1, source_target_pairs={{0,4},{4,0},{8,12},{12,8},{1,5},{5,1},{9,13},{13,9},{2,6},{6,2},{1... | collective-permute-start | bytes 1572872 | tf_op jit(solution)/shard_map/ppermute | solution.py:54
  68.7 4.4 %collective-permute-start.30 = (bf16[8,4096]{1,0:T(8,128)(2,1)S(1)}, bf16[8,4096]{1,0:T(8,128)(2,1)S(1)}, u32[]{:S(2)}, u32[]{:S(2)}) collective-permute-start(bf16[8,4096]{1,0:T(8,128)(2,1)S(1)} %get-tuple-element.8), channel_id=1, source_target_pairs={{0,8},{4,12},{8,0},{12,4},{1,9},{5,13},{9,1},{13,5},{2,10},{6,14},... | collective-permute-start | bytes 196616 | tf_op jit(solution)/shard_map/ppermute | solution.py:51
  70.7 5.0 %collective-permute-start.28 = (bf16[8,4096]{1,0:T(8,128)(2,1)S(1)}, bf16[8,4096]{1,0:T(8,128)(2,1)S(1)}, u32[]{:S(2)}, u32[]{:S(2)}) collective-permute-start(bf16[8,4096]{1,0:T(8,128)(2,1)S(1)} %get-tuple-element.9), channel_id=1, source_target_pairs={{0,8},{4,12},{8,0},{12,4},{1,9},{5,13},{9,1},{13,5},{2,10},{6,14},... | collective-permute-start | bytes 196616 | tf_op jit(solution)/shard_map/ppermute | solution.py:51
  70.8 5.8 %collective-permute-start.26 = (bf16[8,4096]{1,0:T(8,128)(2,1)S(1)}, bf16[8,4096]{1,0:T(8,128)(2,1)S(1)}, u32[]{:S(2)}, u32[]{:S(2)}) collective-permute-start(bf16[8,4096]{1,0:T(8,128)(2,1)S(1)} %get-tuple-element.10), channel_id=1, source_target_pairs={{0,8},{4,12},{8,0},{12,4},{1,9},{5,13},{9,1},{13,5},{2,10},{6,14},... | collective-permute-start | bytes 196616 | tf_op jit(solution)/shard_map/ppermute | solution.py:51
  72.7 6.1 %collective-permute-start.25 = (bf16[8,4096]{1,0:T(8,128)(2,1)S(1)}, bf16[8,4096]{1,0:T(8,128)(2,1)S(1)}, u32[]{:S(2)}, u32[]{:S(2)}) collective-permute-start(bf16[8,4096]{1,0:T(8,128)(2,1)S(1)} %get-tuple-element.7), channel_id=1, source_target_pairs={{0,8},{4,12},{8,0},{12,4},{1,9},{5,13},{9,1},{13,5},{2,10},{6,14},... | collective-permute-start | bytes 196616 | tf_op jit(solution)/shard_map/ppermute | solution.py:51
  76.7 4.4 %collective-permute-start.27 = (bf16[8,4096]{1,0:T(8,128)(2,1)S(1)}, bf16[8,4096]{1,0:T(8,128)(2,1)S(1)}, u32[]{:S(2)}, u32[]{:S(2)}) collective-permute-start(bf16[8,4096]{1,0:T(8,128)(2,1)S(1)} %get-tuple-element.11), channel_id=1, source_target_pairs={{0,3},{1,0},{2,1},{3,2},{4,7},{5,4},{6,5},{7,6},{8,11},{9,8},{10,9... | collective-permute-start | bytes 196616 | tf_op jit(solution)/shard_map/ppermute | solution.py:47
  76.8 6.1 %collective-permute-start.31 = (bf16[8,4096]{1,0:T(8,128)(2,1)S(1)}, bf16[8,4096]{1,0:T(8,128)(2,1)S(1)}, u32[]{:S(2)}, u32[]{:S(2)}) collective-permute-start(bf16[8,4096]{1,0:T(8,128)(2,1)S(1)} %get-tuple-element.12), channel_id=1, source_target_pairs={{0,1},{1,2},{2,3},{3,0},{4,5},{5,6},{6,7},{7,4},{8,9},{9,10},{10,1... | collective-permute-start | bytes 196616 | tf_op jit(solution)/shard_map/ppermute | solution.py:47
  78.8 5.5 %collective-permute-start.29 = (bf16[8,4096]{1,0:T(8,128)(2,1)S(1)}, bf16[8,4096]{1,0:T(8,128)(2,1)S(1)}, u32[]{:S(2)}, u32[]{:S(2)}) collective-permute-start(bf16[8,4096]{1,0:T(8,128)(2,1)S(1)} %get-tuple-element.13), channel_id=1, source_target_pairs={{0,2},{1,3},{2,0},{3,1},{4,6},{5,7},{6,4},{7,5},{8,10},{9,11},{10,... | collective-permute-start | bytes 196616 | tf_op jit(solution)/shard_map/ppermute | solution.py:47
  (5 other events, 90.3 us)

commit v3 on v2

v3 whole, which is shorter than its diff:
```python
import jax
import jax.numpy as jnp
from jax import lax
from jax.sharding import PartitionSpec as P

BF = jnp.bfloat16
F32 = jnp.float32


def dot_nt(a, b):
    return lax.dot_general(a, b, (((1,), (1,)), ((), ())), preferred_element_type=F32)


def dot_nn(a, b):
    return lax.dot_general(a, b, (((1,), (0,)), ((), ())), preferred_element_type=F32)


def local(
    tokens,
    routes,
    probs,
    w_gate,
    w_up,
    w_down,
    gate_left,
    gate_right,
    up_left,
    up_right,
    down_left,
    down_right,
):
    rows, width = tokens.shape
    exp_dev, _, cols = w_gate.shape
    rank = gate_left.shape[1]
    piece = gate_right.shape[1]
    block = gate_left.shape[2]
    parts = lax.axis_size("mp")
    chips = lax.axis_size("y")
    groups = chips * 2
    experts = exp_dev * groups
    me_g = lax.axis_index("y") * 2 + lax.axis_index("core")
    me_m = lax.axis_index("mp")
    ranks = exp_dev * rank
    hid = exp_dev * cols

    def along_z(value, step):
        return lax.ppermute(value, "mp", [(i, (i + step) % parts) for i in range(parts)])

    def other_core(value):
        return lax.ppermute(value, "core", [(0, 1), (1, 0)])

    def swap(value):
        return lax.all_to_all(value, ("y", "mp"), split_axis=0, concat_axis=0, tiled=True)

    chosen = routes[:, :, None] == jnp.arange(experts, dtype=jnp.int32)
    weight = jnp.sum(jnp.where(chosen, probs[:, :, None], 0.0), axis=1)
    high = lax.reduce_precision(weight, 8, 7)
    low = (weight - high).astype(BF)
    side = jnp.concatenate([high.astype(BF), low], axis=1)
    pad = -(2 * experts) % 128
    sent = jnp.concatenate([tokens, jnp.pad(side, ((0, 0), (0, pad)))], axis=1)

    near = swap(jnp.broadcast_to(sent, (chips * parts,) + sent.shape)).reshape(-1, sent.shape[1])
    every = jnp.concatenate([near, other_core(near)])
    total = every.shape[0]
    x = every[:, :width]
    side = every[:, width : width + 2 * experts].astype(F32)
    weight = side[:, :experts] + side[:, experts:]
    weight = lax.dynamic_slice(weight, (0, me_g * exp_dev), (total, exp_dev))

    small = jnp.stack([gate_right, up_right, down_left])
    small = small.reshape(3 * exp_dev * piece, parts, cols).swapaxes(0, 1)
    small = jnp.concatenate([small, small])
    small = [
        lax.dynamic_index_in_dim(small, me_m + k, 0, keepdims=False) for k in range(parts)
    ]
    small = [small[0]] + [along_z(small[k], k) for k in range(1, parts)]
    small = jnp.stack([small[-k % parts] for k in range(parts)] * 2)
    small = lax.dynamic_slice_in_dim(small, parts - me_m, parts, 0)
    small = small.reshape(parts, 3, exp_dev, piece, cols).transpose(1, 2, 0, 3, 4)
    small = small.reshape(3, ranks, cols)
    same = (jnp.arange(ranks) // rank)[:, None] == (jnp.arange(hid) // cols)[None, :]
    diag = jnp.where(same, jnp.tile(small, (1, 1, exp_dev)), jnp.zeros((), BF))

    def sum_parts(value):
        value = value.astype(BF)
        result = value.astype(F32)
        for k in range(1, parts):
            result += along_z(value, k).astype(F32)
        return result.astype(BF)

    mine = lax.dynamic_slice(x, (0, me_m * block), (total, block))
    left = jnp.concatenate([gate_left.reshape(ranks, block), up_left.reshape(ranks, block)])
    inner = sum_parts(dot_nt(mine, left))

    gate_w = jnp.swapaxes(w_gate, 1, 2).reshape(hid, width)
    up_w = jnp.swapaxes(w_up, 1, 2).reshape(hid, width)
    gate_act, up_act = lax.optimization_barrier((dot_nt(x, gate_w), dot_nt(x, up_w)))
    gate_act += dot_nn(inner[:, :ranks], diag[0])
    up_act += dot_nn(inner[:, ranks:], diag[1])
    scale = jnp.repeat(weight, cols, axis=1)
    hidden = (jax.nn.silu(gate_act) * up_act * scale).astype(BF)
    bottom = sum_parts(dot_nt(hidden, diag[2]))
    out = dot_nn(hidden, w_down.reshape(hid, width))
    extra = dot_nn(bottom, down_right.reshape(ranks, block))
    out = lax.dynamic_update_slice(
        out, extra + lax.dynamic_slice(out, (0, me_m * block), (total, block)), (0, me_m * block)
    ).astype(BF)

    out = out.reshape(2, chips * parts, rows, width)
    out = out[0].astype(F32) + other_core(out[1]).astype(F32)
    return jnp.sum(swap(out.astype(BF)).astype(F32), axis=0).astype(BF)


def solution(mesh):
    count = mesh.shape
    fine = jax.sharding.Mesh(
        mesh.devices.reshape(count["groups"], count["expert"] // 2, 2, count["mp"]),
        ("groups", "y", "core", "mp"),
    )
    expert = ("y", "core")
    return jax.shard_map(
        local,
        mesh=fine,
        in_specs=(
            P(("groups", "y", "core", "mp"), None),
            P(("groups", "y", "core", "mp"), None),
            P(("groups", "y", "core", "mp"), None),
            P(expert, None, "mp"),
            P(expert, None, "mp"),
            P(expert, "mp", None),
            P(expert, None, "mp"),
            P(expert, "mp", None),
            P(expert, None, "mp"),
            P(expert, "mp", None),
            P(expert, "mp", None),
            P(expert, None, "mp"),
        ),
        out_specs=P(("groups", "y", "core", "mp"), None),
        check_vma=False,
    )
```

time: 85.2 us -> 74.5 us (0.87)
  blocking collectives: 0 us -> 19.7 us
  waiting for transfers between devices: 32.3 us -> 12.6 us
  starting transfers between devices: 30 us -> 19.5 us
    all_to_all x0 -> x1, blocking collectives: none -> 19.7 us  [swap(): lax.all_to_all(value, ('y', 'mp'), split_axis=0, concat_axis=0, tiled=True)]
    ppermute x15 -> x9, waiting for transfers between devices: 19.4 us -> 0.14 us  [along_z(): lax.ppermute(value, 'mp', [(i, (i + step) % parts) for i in range(parts)])]
    ppermute x17 -> x2, starting transfers between devices: 13 us -> 0.07 us  [other_core(): return lax.ppermute(value, 'core', [(0, 1), (1, 0)])]
    ppermute x17 -> x2, waiting for transfers between devices: 12.8 us -> 1.9 us  [other_core(): return lax.ppermute(value, 'core', [(0, 1), (1, 0)])]
    all_to_all x0 -> x1, waiting for transfers between devices: none -> 10.6 us  [swap(): lax.all_to_all(value, ('y', 'mp'), split_axis=0, concat_axis=0, tiled=True)]
    all_to_all x0 -> x1, starting transfers between devices: none -> 7.28 us  [swap(): lax.all_to_all(value, ('y', 'mp'), split_axis=0, concat_axis=0, tiled=True)]
    ppermute x15 -> x9, starting transfers between devices: 17 us -> 12.2 us  [along_z(): lax.ppermute(value, 'mp', [(i, (i + step) % parts) for i in range(parts)])]
    dot_general x4, matrix products: 10.8 us -> 7.88 us  [dot_nt(): lax.dot_general(a, b, (((1,), (1,)), ((), ())), preferred_element_type=F32)]
  transfers between devices with their start and end apart: 32 -> 12, of which waited for: 18 -> 3; matrix products, arithmetic and copies ran while one was open for 8% -> 23% of each run, Pallas kernels for 0% -> 0%
where the time goes in v3:
time: 74.5 us; the launch traced here: 74.1 us
  blocking collectives  19.7 us (26%)
  starting transfers between devices  19.5 us (26%)
  waiting for transfers between devices  12.6 us (17%)
  matrix products  12.4 us (17%)
  other arithmetic  6.21 us (8%)
  local copies, waits for them, and re-layouts  3.22 us (4%)
    all_to_all x1, blocking collectives, swap(): lax.all_to_all(value, ('y', 'mp'), split_axis=0, concat_axis=0, tiled=True)  19.7 us
    ppermute x9, starting transfers between devices, along_z(): lax.ppermute(value, 'mp', [(i, (i + step) % parts) for i in range(parts)])  12.2 us
    all_to_all x1, waiting for transfers between devices, swap(): lax.all_to_all(value, ('y', 'mp'), split_axis=0, concat_axis=0, tiled=True)  10.6 us
    dot_general x4, matrix products, dot_nt(): lax.dot_general(a, b, (((1,), (1,)), ((), ())), preferred_element_type=F32)  7.88 us
    all_to_all x1, starting transfers between devices, swap(): lax.all_to_all(value, ('y', 'mp'), split_axis=0, concat_axis=0, tiled=True)  7.28 us
    dot_general x4, matrix products, dot_nn(): lax.dot_general(a, b, (((1,), (0,)), ((), ())), preferred_element_type=F32)  4.52 us
    concatenate x1, other arithmetic, local(): small = jnp.concatenate([small, small])  2.09 us
    ppermute x2, waiting for transfers between devices, other_core(): return lax.ppermute(value, 'core', [(0, 1), (1, 0)])  1.9 us
  transfers between devices with their start and end apart: 12, of which 3 were waited for; matrix products, arithmetic and copies ran while one was open for 23% of the time, Pallas kernels for 0%

profile of v3, /device:TPU:0, one launch (start us, length us, event | category | flops | bytes accessed | tf_op | source)
XLA Modules:
  0.0 74.1 jit_solution(2785750004330484124)
XLA Ops:
  0.0 0.9 %select_reduce_fusion = f32[8,16]{1,0:T(8,128)S(1)} fusion(f32[8,8]{1,0:T(8,128)} %param.14, s32[8,8]{1,0:T(8,128)} %param.13), kind=kLoop, calls=%fused_computation.49 | loop fusion | flops 2944 | bytes 1024 | tf_op jit(solution)/shard_map/reduce_sum | solution.py:56
  1.0 0.8 %pad_maximum_fusion.1 = bf16[8,4224]{1,0:T(8,128)(2,1)S(1)} fusion(bf16[8,128]{1,0:T(8,128)(2,1)S(1)} %fusion.24, bf16[8,4096]{1,0:T(8,128)(2,1)} %param.12), kind=kLoop, calls=%fused_computation.39 | loop fusion | flops 135168 | bytes 135168 | tf_op jit(solution)/shard_map/concatenate | solution.py:61
  1.8 0.8 %broadcast_in_dim.33 = bf16[8,8,4224]{2,1,0:T(8,128)(2,1)} broadcast(bf16[8,4224]{1,0:T(8,128)(2,1)S(1)} %pad_maximum_fusion.1), dimensions={1,2} | broadcast | bytes 608256 | tf_op jit(solution)/shard_map/broadcast_in_dim | solution.py:63
  2.7 7.3 %all-to-all-start = ((bf16[8,8,4224]{2,1,0:T(8,128)(2,1)}), bf16[8,8,4224]{2,1,0:T(8,128)(2,1)S(1)}, u32[]{:S(2)}, u32[]{:S(2)}) async-start(bf16[8,8,4224]{2,1,0:T(8,128)(2,1)} %broadcast_in_dim.33), calls=%async_computation | async-start | bytes 1081344 | tf_op jit(solution)/shard_map/all_to_all | solution.py:53
  9.9 0.9 %pad_maximum_fusion = bf16[3,4,8,768]{3,2,1,0:T(8,128)(2,1)S(1)} fusion(bf16[1,4,8,768]{3,2,1,0:T(8,128)(2,1)} %bitcast.73, bf16[1,4,8,768]{3,2,1,0:T(8,128)(2,1)} %bitcast.74, bf16[1,4,8,768]{3,2,1,0:T(8,128)(2,1)} %bitcast.75), kind=kLoop, calls=%fused_computation.33 | loop fusion | flops 147456 | bytes 294912 | tf_op jit(solution)/shard_map/stack | solution.py:71
  10.8 0.2 reshape.74
  11.0 2.1 %fusion.10 = (bf16[1,96,192]{2,0,1:T(2,128)(2,1)S(1)}, bf16[1,96,192]{2,0,1:T(2,128)(2,1)S(1)}, bf16[1,96,192]{2,0,1:T(2,128)(2,1)S(1)}, bf16[1,96,192]{2,0,1:T(2,128)(2,1)S(1)}) fusion(s32[]{:T(128)S(6)} %select_n.57, bf16[4,96,192]{2,0,1:T(4,128)(2,1)S(1)} %bitcast.72, s32[]{:T(128)S(6)} %select_n.56, s32[]{:T(128)S(6)} %select_n.55, s32[]{:T(128)S(6)} %select_n.54), kind=kLoop, calls=%fused_computation.35 | loop fusion | flops 294912 | bytes 294928 | tf_op jit(solution)/shard_map/concatenate | solution.py:73
  13.1 3.9 %collective-permute-start.4 = (bf16[96,192]{1,0:T(8,128)(2,1)S(1)}, bf16[96,192]{1,0:T(8,128)(2,1)S(1)}, u32[]{:S(2)}, u32[]{:S(2)}) collective-permute-start(bf16[96,192]{1,0:T(8,128)(2,1)S(1)} %bitcast.76), channel_id=1, source_target_pairs={{0,3},{1,0},{2,1},{3,2},{4,7},{5,4},{6,5},{7,6},{8,11},{9,8},{10,9... | collective-permute-start | bytes 110600 | tf_op jit(solution)/shard_map/ppermute | solution.py:47
  17.1 1.2 %collective-permute-start.6 = (bf16[96,192]{1,0:T(8,128)(2,1)S(1)}, bf16[96,192]{1,0:T(8,128)(2,1)S(1)}, u32[]{:S(2)}, u32[]{:S(2)}) collective-permute-start(bf16[96,192]{1,0:T(8,128)(2,1)S(1)} %bitcast.80), channel_id=1, source_target_pairs={{0,1},{1,2},{2,3},{3,0},{4,5},{5,6},{6,7},{7,4},{8,9},{9,10},{10,1... | collective-permute-start | bytes 110600 | tf_op jit(solution)/shard_map/ppermute | solution.py:47
  18.3 10.6 %all-to-all-done = bf16[8,8,4224]{2,1,0:T(8,128)(2,1)S(1)} async-done(((bf16[8,8,4224]{2,1,0:T(8,128)(2,1)}), bf16[8,8,4224]{2,1,0:T(8,128)(2,1)S(1)}, u32[]{:S(2)}, u32[]{:S(2)}) %all-to-all-start) | async-done | bytes 540704 | tf_op jit(solution)/shard_map/all_to_all | solution.py:53
  28.9 0.2 broadcast_compare_fusion
  29.3 1.2 %stack.36 = bf16[8,96,192]{2,0,1:T(8,128)(2,1)S(1)} concatenate(bf16[1,96,192]{2,0,1:T(2,128)(2,1)S(1)} %get-tuple-element.12, bf16[1,96,192]{2,0,1:T(2,128)(2,1)S(1)} %copy.27, bf16[1,96,192]{2,0,1:T(2,128)(2,1)S(1)} %copy.28, bf16[1,96,192]{2,0,1:T(2,128)(2,1)S(1)} %copy.29, bf16[1,96,192]{2,0,1:T(2,128)(2,1)S(1)} %get-tuple-element.12, bf16[1,96,192]{2,0,1:T(2,128)(2,1)S(1)} %copy.27, ...), dimensions={0} | concatenate | bytes 589824 | tf_op jit(solution)/shard_map/stack | solution.py:78
  30.7 0.2 copy.35
  31.1 0.3 convolution_convert_fusion
  31.4 0.2 collective-permute-start.3
  31.6 1.3 %collective-permute-start.2 = (bf16[128,256]{1,0:T(8,128)(2,1)S(1)}, bf16[128,256]{1,0:T(8,128)(2,1)S(1)}, u32[]{:S(2)}, u32[]{:S(2)}) collective-permute-start(bf16[128,256]{1,0:T(8,128)(2,1)S(1)} %convolution_convert_fusion), channel_id=1, source_target_pairs={{0,2},{1,3},{2,0},{3,1},{4,6},{5,7},{6,4},{7,5},{8,10},{9,11},{10,... | collective-permute-start | bytes 196616 | tf_op jit(solution)/shard_map/ppermute | solution.py:47
  32.9 0.7 collective-permute-start.1
  33.7 5.1 %fusion.28 = f32[128,768]{1,0:T(8,128)S(1)} fusion(bf16[128,4096]{1,0:T(8,128)(2,1)S(1)} %fusion.4, bf16[768,4096]{1,0:T(8,128)(2,1)} %bitcast.62), kind=kOutput, calls=%fused_computation.74 | convolution fusion | flops 805306368 | bytes 7733248 | tf_op jit(solution)/shard_map/dot_general | solution.py:11
  38.9 2.2 %fusion.27 = f32[128,768]{1,0:T(8,128)S(1)} fusion(bf16[128,4096]{1,0:T(8,128)(2,1)S(1)} %fusion.4, bf16[768,4096]{1,0:T(8,128)(2,1)S(1)} %bitcast.65), kind=kOutput, calls=%fused_computation.73 | convolution fusion | flops 805306368 | bytes 7733248 | tf_op jit(solution)/shard_map/dot_general | solution.py:11
  41.3 0.2 copy.37
  41.6 0.2 convolution_add_fusion.2
  41.8 0.2 fusion.3
  42.0 0.2 convolution_convert_fusion.1
  42.2 3.2 %collective-permute-start.9 = (bf16[128,128]{1,0:T(8,128)(2,1)S(1)}, bf16[128,128]{1,0:T(8,128)(2,1)S(1)}, u32[]{:S(2)}, u32[]{:S(2)}) collective-permute-start(bf16[128,128]{1,0:T(8,128)(2,1)S(1)} %convolution_convert_fusion.1), channel_id=1, source_target_pairs={{0,3},{1,0},{2,1},{3,2},{4,7},{5,4},{6,5},{7,6},{8,11},{9,8},{10,9... | collective-permute-start | bytes 98312 | tf_op jit(solution)/shard_map/ppermute | solution.py:47
  45.4 1.7 %collective-permute-start.7 = (bf16[128,128]{1,0:T(8,128)(2,1)S(1)}, bf16[128,128]{1,0:T(8,128)(2,1)S(1)}, u32[]{:S(2)}, u32[]{:S(2)}) collective-permute-start(bf16[128,128]{1,0:T(8,128)(2,1)S(1)} %convolution_convert_fusion.1), channel_id=1, source_target_pairs={{0,1},{1,2},{2,3},{3,0},{4,5},{5,6},{6,7},{7,4},{8,9},{9,10},{10,1... | collective-permute-start | bytes 98312 | tf_op jit(solution)/shard_map/ppermute | solution.py:47
  47.2 3.8 %fusion.29 = f32[128,4096]{1,0:T(8,128)S(1)} fusion(bf16[128,768]{1,0:T(8,128)(2,1)S(1)} %fusion.3, bf16[768,4096]{1,0:T(8,128)(2,1)} %bitcast.61), kind=kOutput, calls=%fused_computation.75 | convolution fusion | flops 805306368 | bytes 8585216 | tf_op jit(solution)/shard_map/dot_general | solution.py:15
  51.2 0.2 fusion
  51.4 0.1 convert_element_type.83
  51.6 1.9 %collective-permute-done.10 = bf16[8,8,4096]{2,1,0:T(8,128)(2,1)S(1)} collective-permute-done((bf16[8,8,4096]{2,1,0:T(8,128)(2,1)S(1)}, bf16[8,8,4096]{2,1,0:T(8,128)(2,1)S(1)}, u32[]{:S(2)}, u32[]{:S(2)}) %collective-permute-start.10) | collective-permute-done | bytes 524320 | tf_op jit(solution)/shard_map/ppermute | solution.py:50
  53.5 0.1 fusion.5
  53.7 19.7 %all_to_all.10 = bf16[8,8,4096]{2,1,0:T(8,128)(2,1)S(1)} all-to-all(bf16[8,8,4096]{2,1,0:T(8,128)(2,1)S(1)} %fusion.5), channel_id=1, replica_groups=mesh['groups'=2,'y'=2,'core'=2,'mp'=4] {'y','mp'}, dimensions={0} | all-to-all | bytes 1048576 | tf_op jit(solution)/shard_map/all_to_all | solution.py:53
  73.4 0.7 reduce_sum.22
  (47 shorter events, 1.4 us)
Async XLA Ops:
  0.0 51.2 %copy-start = (bf16[4,32,1024]{2,1,0:T(8,128)(2,1)S(1)}, bf16[4,32,1024]{2,1,0:T(8,128)(2,1)}, u32[]{:S(2)}) copy-start(bf16[4,32,1024]{2,1,0:T(8,128)(2,1)} %param.23) | copy-start | bytes 786436
  0.0 31.1 %copy-start.1 = (bf16[4,32,1024]{2,1,0:T(8,128)(2,1)S(1)}, bf16[4,32,1024]{2,1,0:T(8,128)(2,1)}, u32[]{:S(2)}) copy-start(bf16[4,32,1024]{2,1,0:T(8,128)(2,1)} %param.20) | copy-start | bytes 786436
  0.0 31.1 %copy-start.2 = (bf16[4,32,1024]{2,1,0:T(8,128)(2,1)S(1)}, bf16[4,32,1024]{2,1,0:T(8,128)(2,1)}, u32[]{:S(2)}) copy-start(bf16[4,32,1024]{2,1,0:T(8,128)(2,1)} %param.18) | copy-start | bytes 786436
  2.7 26.2 %all-to-all-start = ((bf16[8,8,4224]{2,1,0:T(8,128)(2,1)}), bf16[8,8,4224]{2,1,0:T(8,128)(2,1)S(1)}, u32[]{:S(2)}, u32[]{:S(2)}) async-start(bf16[8,8,4224]{2,1,0:T(8,128)(2,1)} %broadcast_in_dim.33), calls=%async_computation | async-start | bytes 1081344 | tf_op jit(solution)/shard_map/all_to_all | solution.py:53
  13.1 15.9 %collective-permute-start.4 = (bf16[96,192]{1,0:T(8,128)(2,1)S(1)}, bf16[96,192]{1,0:T(8,128)(2,1)S(1)}, u32[]{:S(2)}, u32[]{:S(2)}) collective-permute-start(bf16[96,192]{1,0:T(8,128)(2,1)S(1)} %bitcast.76), channel_id=1, source_target_pairs={{0,3},{1,0},{2,1},{3,2},{4,7},{5,4},{6,5},{7,6},{8,11},{9,8},{10,9... | collective-permute-start | bytes 110600 | tf_op jit(solution)/shard_map/ppermute | solution.py:47
  17.0 12.1 %collective-permute-start.5 = (bf16[96,192]{1,0:T(8,128)(2,1)S(1)}, bf16[96,192]{1,0:T(8,128)(2,1)S(1)}, u32[]{:S(2)}, u32[]{:S(2)}) collective-permute-start(bf16[96,192]{1,0:T(8,128)(2,1)S(1)} %bitcast.78), channel_id=1, source_target_pairs={{0,2},{1,3},{2,0},{3,1},{4,6},{5,7},{6,4},{7,5},{8,10},{9,11},{10,... | collective-permute-start | bytes 110600 | tf_op jit(solution)/shard_map/ppermute | solution.py:47
  17.1 12.1 %collective-permute-start.6 = (bf16[96,192]{1,0:T(8,128)(2,1)S(1)}, bf16[96,192]{1,0:T(8,128)(2,1)S(1)}, u32[]{:S(2)}, u32[]{:S(2)}) collective-permute-start(bf16[96,192]{1,0:T(8,128)(2,1)S(1)} %bitcast.80), channel_id=1, source_target_pairs={{0,1},{1,2},{2,3},{3,0},{4,5},{5,6},{6,7},{7,4},{8,9},{9,10},{10,1... | collective-permute-start | bytes 110600 | tf_op jit(solution)/shard_map/ppermute | solution.py:47
  28.8 2.1 %collective-permute-start = (bf16[64,4224]{1,0:T(8,128)(2,1)S(1)}, bf16[64,4224]{1,0:T(8,128)(2,1)S(1)}, u32[]{:S(2)}, u32[]{:S(2)}) collective-permute-start(bf16[64,4224]{1,0:T(8,128)(2,1)S(1)} %bitcast.66), channel_id=1, source_target_pairs={{0,4},{4,0},{1,5},{5,1},{2,6},{6,2},{3,7},{7,3},{8,12},{12,8},{9,1... | collective-permute-start | bytes 1622024 | tf_op jit(solution)/shard_map/ppermute | solution.py:50
  31.0 7.9 %slice-start = ((s8[6291456]{0:T(1024)(128)(4,1)}), s8[4194304]{0:T(1024)(128)(4,1)S(1)}, s32[]{:S(2)}) async-start(s8[6291456]{0:T(1024)(128)(4,1)} %bitcast.63), calls=%async_computation.2 | async-start | bytes 8388608
  31.4 10.1 %collective-permute-start.3 = (bf16[128,256]{1,0:T(8,128)(2,1)S(1)}, bf16[128,256]{1,0:T(8,128)(2,1)S(1)}, u32[]{:S(2)}, u32[]{:S(2)}) collective-permute-start(bf16[128,256]{1,0:T(8,128)(2,1)S(1)} %convolution_convert_fusion), channel_id=1, source_target_pairs={{0,3},{1,0},{2,1},{3,2},{4,7},{5,4},{6,5},{7,6},{8,11},{9,8},{10,9... | collective-permute-start | bytes 196616 | tf_op jit(solution)/shard_map/ppermute | solution.py:47
  31.6 9.9 %collective-permute-start.2 = (bf16[128,256]{1,0:T(8,128)(2,1)S(1)}, bf16[128,256]{1,0:T(8,128)(2,1)S(1)}, u32[]{:S(2)}, u32[]{:S(2)}) collective-permute-start(bf16[128,256]{1,0:T(8,128)(2,1)S(1)} %convolution_convert_fusion), channel_id=1, source_target_pairs={{0,2},{1,3},{2,0},{3,1},{4,6},{5,7},{6,4},{7,5},{8,10},{9,11},{10,... | collective-permute-start | bytes 196616 | tf_op jit(solution)/shard_map/ppermute | solution.py:47
  32.9 8.6 %collective-permute-start.1 = (bf16[128,256]{1,0:T(8,128)(2,1)S(1)}, bf16[128,256]{1,0:T(8,128)(2,1)S(1)}, u32[]{:S(2)}, u32[]{:S(2)}) collective-permute-start(bf16[128,256]{1,0:T(8,128)(2,1)S(1)} %convolution_convert_fusion), channel_id=1, source_target_pairs={{0,1},{1,2},{2,3},{3,0},{4,5},{5,6},{6,7},{7,4},{8,9},{9,10},{10,1... | collective-permute-start | bytes 196616 | tf_op jit(solution)/shard_map/ppermute | solution.py:47
  33.7 5.2 %slice-start.1 = ((s8[6291456]{0:T(1024)(128)(4,1)}), s8[2097152]{0:T(1024)(128)(4,1)S(1)}, s32[]{:S(2)}) async-start(s8[6291456]{0:T(1024)(128)(4,1)} %bitcast.63), calls=%async_computation.3 | async-start | bytes 4194304
  42.2 8.8 %collective-permute-start.9 = (bf16[128,128]{1,0:T(8,128)(2,1)S(1)}, bf16[128,128]{1,0:T(8,128)(2,1)S(1)}, u32[]{:S(2)}, u32[]{:S(2)}) collective-permute-start(bf16[128,128]{1,0:T(8,128)(2,1)S(1)} %convolution_convert_fusion.1), channel_id=1, source_target_pairs={{0,3},{1,0},{2,1},{3,2},{4,7},{5,4},{6,5},{7,6},{8,11},{9,8},{10,9... | collective-permute-start | bytes 98312 | tf_op jit(solution)/shard_map/ppermute | solution.py:47
  45.4 5.6 %collective-permute-start.8 = (bf16[128,128]{1,0:T(8,128)(2,1)S(1)}, bf16[128,128]{1,0:T(8,128)(2,1)S(1)}, u32[]{:S(2)}, u32[]{:S(2)}) collective-permute-start(bf16[128,128]{1,0:T(8,128)(2,1)S(1)} %convolution_convert_fusion.1), channel_id=1, source_target_pairs={{0,2},{1,3},{2,0},{3,1},{4,6},{5,7},{6,4},{7,5},{8,10},{9,11},{10,... | collective-permute-start | bytes 98312 | tf_op jit(solution)/shard_map/ppermute | solution.py:47
  45.4 5.7 %collective-permute-start.7 = (bf16[128,128]{1,0:T(8,128)(2,1)S(1)}, bf16[128,128]{1,0:T(8,128)(2,1)S(1)}, u32[]{:S(2)}, u32[]{:S(2)}) collective-permute-start(bf16[128,128]{1,0:T(8,128)(2,1)S(1)} %convolution_convert_fusion.1), channel_id=1, source_target_pairs={{0,1},{1,2},{2,3},{3,0},{4,5},{5,6},{6,7},{7,4},{8,9},{9,10},{10,1... | collective-permute-start | bytes 98312 | tf_op jit(solution)/shard_map/ppermute | solution.py:47
  51.6 2.0 %collective-permute-start.10 = (bf16[8,8,4096]{2,1,0:T(8,128)(2,1)S(1)}, bf16[8,8,4096]{2,1,0:T(8,128)(2,1)S(1)}, u32[]{:S(2)}, u32[]{:S(2)}) collective-permute-start(bf16[8,8,4096]{2,1,0:T(8,128)(2,1)S(1)} %slice_bitcast_fusion), channel_id=1, source_target_pairs={{0,4},{4,0},{1,5},{5,1},{2,6},{6,2},{3,7},{7,3},{8,12},{12,8},{9,1... | collective-permute-start | bytes 1572872 | tf_op jit(solution)/shard_map/ppermute | solution.py:50

commit v4 on v3

--- a/solution.py
+++ b/solution.py
@@ -1,6 +1,10 @@
+import functools
+
 import jax
 import jax.numpy as jnp
 from jax import lax
+from jax.experimental import pallas as pl
+from jax.experimental.pallas import tpu as pltpu
 from jax.sharding import PartitionSpec as P
 
 BF = jnp.bfloat16
@@ -13,6 +17,36 @@
 
 def dot_nn(a, b):
     return lax.dot_general(a, b, (((1,), (0,)), ((), ())), preferred_element_type=F32)
+
+
+def attach_kernel(experts, tokens_ref, routes_ref, probs_ref, out_ref):
+    rows, width = tokens_ref.shape
+    half = (out_ref.shape[1] - width) // 2
+    out_ref[:, :width] = tokens_ref[...]
+    routes = routes_ref[...]
+    probs = probs_ref[...]
+    ids = lax.broadcasted_iota(jnp.int32, (rows, half), 1)
+    weight = jnp.zeros((rows, half), F32)
+    for k in range(routes.shape[1]):
+        weight += jnp.where(ids == routes[:, k : k + 1], probs[:, k : k + 1], 0.0)
+    high = weight.astype(BF)
+    low = (weight - high.astype(F32)).astype(BF)
+    out_ref[:, width : width + half] = high
+    out_ref[:, width + half :] = low
+
+
+def attach(tokens, routes, probs, experts):
+    rows, width = tokens.shape
+    half = -(-experts // 128) * 128
+    return pl.pallas_call(
+        functools.partial(attach_kernel, experts),
+        out_shape=jax.ShapeDtypeStruct((rows, width + 2 * half), BF),
+        name="attach",
+    )(tokens, routes, probs)
+
+
+def after(value, earlier):
+    return lax.optimization_barrier((value, earlier))[0]
 
 
 def local(
@@ -49,23 +83,22 @@
     def other_core(value):
         return lax.ppermute(value, "core", [(0, 1), (1, 0)])
 
-    def swap(value):
-        return lax.all_to_all(value, ("y", "mp"), split_axis=0, concat_axis=0, tiled=True)
+    def along_y(value, step):
+        return lax.ppermute(value, "y", [(i, (i + step) % chips) for i in range(chips)])
 
-    chosen = routes[:, :, None] == jnp.arange(experts, dtype=jnp.int32)
-    weight = jnp.sum(jnp.where(chosen, probs[:, :, None], 0.0), axis=1)
-    high = lax.reduce_precision(weight, 8, 7)
-    low = (weight - high).astype(BF)
-    side = jnp.concatenate([high.astype(BF), low], axis=1)
-    pad = -(2 * experts) % 128
-    sent = jnp.concatenate([tokens, jnp.pad(side, ((0, 0), (0, pad)))], axis=1)
-
-    near = swap(jnp.broadcast_to(sent, (chips * parts,) + sent.shape)).reshape(-1, sent.shape[1])
-    every = jnp.concatenate([near, other_core(near)])
+    sent = attach(tokens, routes, probs, experts)
+    rest = jnp.concatenate([along_z(sent, k) for k in range(1, parts)])
+    first = [sent] + [along_y(sent, s) for s in range(1, chips)]
+    lines = [jnp.concatenate([sent, rest])]
+    partner = [other_core(lines[0])]
+    for s in range(1, chips):
+        lines.append(jnp.concatenate([first[s], along_y(rest, s)]))
+        partner.append(other_core(lines[s]))
+    every = jnp.concatenate(lines + partner)
     total = every.shape[0]
     x = every[:, :width]
-    side = every[:, width : width + 2 * experts].astype(F32)
-    weight = side[:, :experts] + side[:, experts:]
+    half = (every.shape[1] - width) // 2
+    weight = every[:, width : width + half].astype(F32) + every[:, width + half :].astype(F32)
     weight = lax.dynamic_slice(weight, (0, me_g * exp_dev), (total, exp_dev))
 
     small = jnp.stack([gate_right, up_right, down_left])
@@ -74,6 +107,7 @@
     small = [
         lax.dynamic_index_in_dim(small, me_m + k, 0, keepdims=False) for k in range(parts)
     ]
+    small = after(small, partner[0])
     small = [small[0]] + [along_z(small[k], k) for k in range(1, parts)]
     small = jnp.stack([small[-k % parts] for k in range(parts)] * 2)
     small = lax.dynamic_slice_in_dim(small, parts - me_m, parts, 0)
@@ -85,8 +119,9 @@
     def sum_parts(value):
         value = value.astype(BF)
         result = value.astype(F32)
+        lines = value.reshape(-1, parts, rows, value.shape[1])
         for k in range(1, parts):
-            result += along_z(value, k).astype(F32)
+            result += along_z(jnp.roll(lines, k, axis=1).reshape(value.shape), k).astype(F32)
         return result.astype(BF)
 
     mine = lax.dynamic_slice(x, (0, me_m * block), (total, block))
@@ -107,9 +142,19 @@
         out, extra + lax.dynamic_slice(out, (0, me_m * block), (total, block)), (0, me_m * block)
     ).astype(BF)
 
-    out = out.reshape(2, chips * parts, rows, width)
-    out = out[0].astype(F32) + other_core(out[1]).astype(F32)
-    return jnp.sum(swap(out.astype(BF)).astype(F32), axis=0).astype(BF)
+    out = out.reshape(2, chips, parts, rows, width)
+    out = (out[0].astype(F32) + other_core(out[1]).astype(F32)).astype(BF)
+    rest = out[0, 1:].astype(F32)
+    back = [along_y(out[s, 1:], -s) for s in range(1, chips)]
+    for piece in back:
+        rest += piece.astype(F32)
+    rest = rest.astype(BF)
+    result = out[0, 0].astype(F32)
+    for s in range(1, chips):
+        result += along_y(after(out[s, 0], back[s - 1]), -s).astype(F32)
+    for k in range(1, parts):
+        result += along_z(rest[k - 1], -k).astype(F32)
+    return result.astype(BF)
 
 
 def solution(mesh):

time: 74.5 us -> 75.3 us (1.011)
  blocking collectives: 19.7 us -> 0 us
  waiting for transfers between devices: 12.6 us -> 30.6 us
  starting transfers between devices: 19.5 us -> 22.6 us
  other arithmetic: 6.21 us -> 4.4 us
  Pallas kernels: 0 us -> 1.62 us
    all_to_all x1 -> x0, blocking collectives: 19.7 us -> none  [swap(): lax.all_to_all(value, ('y', 'mp'), split_axis=0, concat_axis=0, tiled=True)]
    ppermute x9 -> x15, waiting for transfers between devices: 0.14 us -> 15.4 us  [along_z(): lax.ppermute(value, 'mp', [(i, (i + step) % parts) for i in range(parts)])]
    ppermute x0 -> x4, waiting for transfers between devices: none -> 13.3 us  [along_y(): lax.ppermute(value, 'y', [(i, (i + step) % chips) for i in range(chips)])]
    all_to_all x1 -> x0, waiting for transfers between devices: 10.6 us -> none  [swap(): lax.all_to_all(value, ('y', 'mp'), split_axis=0, concat_axis=0, tiled=True)]
    all_to_all x1 -> x0, starting transfers between devices: 7.28 us -> none  [swap(): lax.all_to_all(value, ('y', 'mp'), split_axis=0, concat_axis=0, tiled=True)]
    ppermute x9 -> x15, starting transfers between devices: 12.2 us -> 17.8 us  [along_z(): lax.ppermute(value, 'mp', [(i, (i + step) % parts) for i in range(parts)])]
    ppermute x0 -> x4, starting transfers between devices: none -> 4.6 us  [along_y(): lax.ppermute(value, 'y', [(i, (i + step) % chips) for i in range(chips)])]
    unnamed x13 -> x28, local copies, waits for them, and re-layouts: 0.05 us -> 1.95 us
  transfers between devices with their start and end apart: 12 -> 22, of which waited for: 3 -> 13; matrix products, arithmetic and copies ran while one was open for 23% -> 12% of each run, Pallas kernels for 0% -> 0%
where the time goes in v4:
time: 75.3 us; the launch traced here: 75.1 us
  waiting for transfers between devices  30.6 us (41%)
  starting transfers between devices  22.6 us (30%)
  matrix products  12.4 us (16%)
  other arithmetic  4.4 us (6%)
  local copies, waits for them, and re-layouts  2.9 us (4%)
  Pallas kernels  1.62 us (2%)
    ppermute x15, starting transfers between devices, along_z(): lax.ppermute(value, 'mp', [(i, (i + step) % parts) for i in range(parts)])  17.8 us
    ppermute x15, waiting for transfers between devices, along_z(): lax.ppermute(value, 'mp', [(i, (i + step) % parts) for i in range(parts)])  15.4 us
    ppermute x4, waiting for transfers between devices, along_y(): lax.ppermute(value, 'y', [(i, (i + step) % chips) for i in range(chips)])  13.3 us
    dot_general x4, matrix products, dot_nt(): lax.dot_general(a, b, (((1,), (1,)), ((), ())), preferred_element_type=F32)  7.85 us
    ppermute x4, starting transfers between devices, along_y(): lax.ppermute(value, 'y', [(i, (i + step) % chips) for i in range(chips)])  4.6 us
    dot_general x4, matrix products, dot_nn(): lax.dot_general(a, b, (((1,), (0,)), ((), ())), preferred_element_type=F32)  4.52 us
    concatenate x1, other arithmetic, local(): small = jnp.concatenate([small, small])  2.09 us
    unnamed x28, local copies, waits for them, and re-layouts  1.95 us
  transfers between devices with their start and end apart: 22, of which 13 were waited for; matrix products, arithmetic and copies ran while one was open for 12% of the time, Pallas kernels for 0%

profile of v4, /device:TPU:0, one launch (start us, length us, event | category | flops | bytes accessed | tf_op | source)
XLA Modules:
  0.0 75.1 jit_solution(3607417495766955062)
XLA Ops:
  0.0 1.6 %attach.1 = bf16[8,4352]{1,0:T(8,128)(2,1)} custom-call(bf16[8,4096]{1,0:T(8,128)(2,1)} %tokens_ref.1, s32[8,8]{1,0:T(8,128)} %routes_ref.1, f32[8,8]{1,0:T(8,128)} %probs_ref.1), custom_call_target="tpu_custom_call" | custom-call | tf_op jit(solution)/shard_map/attach/pallas_call | solution.py:41
  1.6 3.0 %collective-permute-start.3 = (bf16[8,4352]{1,0:T(8,128)(2,1)}, bf16[8,4352]{1,0:T(8,128)(2,1)S(1)}, u32[]{:S(2)}, u32[]{:S(2)}) collective-permute-start(bf16[8,4352]{1,0:T(8,128)(2,1)} %attach.1), channel_id=1, source_target_pairs={{0,8},{8,0},{1,9},{9,1},{2,10},{10,2},{3,11},{11,3},{4,12},{12,4},... | collective-permute-start | bytes 208904 | tf_op jit(solution)/shard_map/ppermute | solution.py:87
  4.6 3.6 %collective-permute-start.2 = (bf16[8,4352]{1,0:T(8,128)(2,1)}, bf16[8,4352]{1,0:T(8,128)(2,1)S(1)}, u32[]{:S(2)}, u32[]{:S(2)}) collective-permute-start(bf16[8,4352]{1,0:T(8,128)(2,1)} %attach.1), channel_id=1, source_target_pairs={{0,3},{1,0},{2,1},{3,2},{4,7},{5,4},{6,5},{7,6},{8,11},{9,8},{10,9... | collective-permute-start | bytes 208904 | tf_op jit(solution)/shard_map/ppermute | solution.py:81
  8.2 1.0 %collective-permute-start = (bf16[8,4352]{1,0:T(8,128)(2,1)}, bf16[8,4352]{1,0:T(8,128)(2,1)S(1)}, u32[]{:S(2)}, u32[]{:S(2)}) collective-permute-start(bf16[8,4352]{1,0:T(8,128)(2,1)} %attach.1), channel_id=1, source_target_pairs={{0,1},{1,2},{2,3},{3,0},{4,5},{5,6},{6,7},{7,4},{8,9},{9,10},{10,1... | collective-permute-start | bytes 208904 | tf_op jit(solution)/shard_map/ppermute | solution.py:81
  9.2 0.9 %constant_dynamic-update-slice_fusion.7 = bf16[128,4352]{1,0:T(8,128)(2,1)S(1)} fusion(bf16[8,4352]{1,0:T(8,128)(2,1)} %attach.1), kind=kLoop, calls=%fused_computation.75 | loop fusion | bytes 139264
  10.1 0.9 %pad_maximum_fusion.3 = bf16[3,4,8,768]{3,2,1,0:T(8,128)(2,1)S(1)} fusion(bf16[1,4,8,768]{3,2,1,0:T(8,128)(2,1)} %bitcast.110, bf16[1,4,8,768]{3,2,1,0:T(8,128)(2,1)} %bitcast.111, bf16[1,4,8,768]{3,2,1,0:T(8,128)(2,1)} %bitcast.112), kind=kLoop, calls=%fused_computation.35 | loop fusion | flops 147456 | bytes 294912 | tf_op jit(solution)/shard_map/stack | solution.py:104
  11.2 2.1 %fusion.14 = (bf16[1,96,192]{2,0,1:T(2,128)(2,1)S(1)}, bf16[1,96,192]{2,0,1:T(2,128)(2,1)S(1)}, bf16[1,96,192]{2,0,1:T(2,128)(2,1)S(1)}, bf16[1,96,192]{2,0,1:T(2,128)(2,1)S(1)}) fusion(s32[]{:T(128)S(6)} %select_n.52, bf16[4,96,192]{2,0,1:T(4,128)(2,1)S(1)} %bitcast.105, s32[]{:T(128)S(6)} %select_n.51, s32[]{:T(128)S(6)} %select_n.50, s32[]{:T(128)S(6)} %select_n.49), kind=kLoop, calls=%fused_computation.42 | loop fusion | flops 294912 | bytes 294928 | tf_op jit(solution)/shard_map/concatenate | solution.py:106
  13.5 1.4 %collective-permute-done.1 = bf16[8,4352]{1,0:T(8,128)(2,1)S(1)} collective-permute-done((bf16[8,4352]{1,0:T(8,128)(2,1)}, bf16[8,4352]{1,0:T(8,128)(2,1)S(1)}, u32[]{:S(2)}, u32[]{:S(2)}) %collective-permute-start.1) | collective-permute-done | bytes 69664 | tf_op jit(solution)/shard_map/ppermute | solution.py:81
  15.7 6.3 %collective-permute-done.4 = bf16[24,4352]{1,0:T(8,128)(2,1)S(1)} collective-permute-done((bf16[24,4352]{1,0:T(8,128)(2,1)S(1)}, bf16[24,4352]{1,0:T(8,128)(2,1)S(1)}, u32[]{:S(2)}, u32[]{:S(2)}) %collective-permute-start.4) | collective-permute-done | bytes 208928 | tf_op jit(solution)/shard_map/ppermute | solution.py:87
  22.1 0.8 %collective-permute-start.10 = (bf16[96,192]{1,0:T(8,128)(2,1)S(1)}, bf16[96,192]{1,0:T(8,128)(2,1)S(1)}, u32[]{:S(2)}, u32[]{:S(2)}) collective-permute-start(bf16[96,192]{1,0:T(8,128)(2,1)S(1)} %get-tuple-element.14), channel_id=1, source_target_pairs={{0,3},{1,0},{2,1},{3,2},{4,7},{5,4},{6,5},{7,6},{8,11},{9,8},{10,9... | collective-permute-start | bytes 110600 | tf_op jit(solution)/shard_map/ppermute | solution.py:81
  22.9 0.7 collective-permute-start.11
  23.6 1.9 %collective-permute-start.12 = (bf16[96,192]{1,0:T(8,128)(2,1)S(1)}, bf16[96,192]{1,0:T(8,128)(2,1)S(1)}, u32[]{:S(2)}, u32[]{:S(2)}) collective-permute-start(bf16[96,192]{1,0:T(8,128)(2,1)S(1)} %get-tuple-element.16), channel_id=1, source_target_pairs={{0,1},{1,2},{2,3},{3,0},{4,5},{5,6},{6,7},{7,4},{8,9},{9,10},{10,1... | collective-permute-start | bytes 110600 | tf_op jit(solution)/shard_map/ppermute | solution.py:81
  25.5 0.8 %collective-permute-done.10 = bf16[96,192]{1,0:T(8,128)(2,1)S(1)} collective-permute-done((bf16[96,192]{1,0:T(8,128)(2,1)S(1)}, bf16[96,192]{1,0:T(8,128)(2,1)S(1)}, u32[]{:S(2)}, u32[]{:S(2)}) %collective-permute-start.10) | collective-permute-done | bytes 36896 | tf_op jit(solution)/shard_map/ppermute | solution.py:81
  26.3 3.7 %collective-permute-done.11 = bf16[96,192]{1,0:T(8,128)(2,1)S(1)} collective-permute-done((bf16[96,192]{1,0:T(8,128)(2,1)S(1)}, bf16[96,192]{1,0:T(8,128)(2,1)S(1)}, u32[]{:S(2)}, u32[]{:S(2)}) %collective-permute-start.11) | collective-permute-done | bytes 36896 | tf_op jit(solution)/shard_map/ppermute | solution.py:81
  30.5 0.8 %copy-done.2 = bf16[4,32,1024]{2,1,0:T(8,128)(2,1)S(1)} copy-done((bf16[4,32,1024]{2,1,0:T(8,128)(2,1)S(1)}, bf16[4,32,1024]{2,1,0:T(8,128)(2,1)}, u32[]{:S(2)}) %copy-start.2) | copy-done | bytes 262168
  31.8 5.1 %fusion.25 = f32[128,768]{1,0:T(8,128)S(1)} fusion(bf16[768,4096]{1,0:T(8,128)(2,1)} %bitcast.91, bf16[128,4352]{1,0:T(8,128)(2,1)S(1)} %constant_dynamic-update-slice_fusion), kind=kOutput, calls=%fused_computation.95 | convolution fusion | flops 805306368 | bytes 7733248 | tf_op jit(solution)/shard_map/dot_general | solution.py:15
  36.9 2.2 %fusion.27 = f32[128,768]{1,0:T(8,128)S(1)} fusion(bf16[768,4096]{1,0:T(8,128)(2,1)S(1)} %bitcast.94, bf16[128,4352]{1,0:T(8,128)(2,1)S(1)} %constant_dynamic-update-slice_fusion), kind=kOutput, calls=%fused_computation.97 | convolution fusion | flops 805306368 | bytes 7733248 | tf_op jit(solution)/shard_map/dot_general | solution.py:15
  39.2 1.2 %collective-permute-start.8 = (bf16[128,256]{1,0:T(8,128)(2,1)S(1)}, bf16[128,256]{1,0:T(8,128)(2,1)S(1)}, u32[]{:S(2)}, u32[]{:S(2)}) collective-permute-start(bf16[128,256]{1,0:T(8,128)(2,1)S(1)} %bitcast.107), channel_id=1, source_target_pairs={{0,2},{1,3},{2,0},{3,1},{4,6},{5,7},{6,4},{7,5},{8,10},{9,11},{10,... | collective-permute-start | bytes 196616 | tf_op jit(solution)/shard_map/ppermute | solution.py:81
  40.3 1.0 %collective-permute-start.9 = (bf16[128,256]{1,0:T(8,128)(2,1)S(1)}, bf16[128,256]{1,0:T(8,128)(2,1)S(1)}, u32[]{:S(2)}, u32[]{:S(2)}) collective-permute-start(bf16[128,256]{1,0:T(8,128)(2,1)S(1)} %bitcast.108), channel_id=1, source_target_pairs={{0,3},{1,0},{2,1},{3,2},{4,7},{5,4},{6,5},{7,6},{8,11},{9,8},{10,9... | collective-permute-start | bytes 196616 | tf_op jit(solution)/shard_map/ppermute | solution.py:81
  41.4 1.1 %collective-permute-start.7 = (bf16[128,256]{1,0:T(8,128)(2,1)S(1)}, bf16[128,256]{1,0:T(8,128)(2,1)S(1)}, u32[]{:S(2)}, u32[]{:S(2)}) collective-permute-start(bf16[128,256]{1,0:T(8,128)(2,1)S(1)} %bitcast.109), channel_id=1, source_target_pairs={{0,1},{1,2},{2,3},{3,0},{4,5},{5,6},{6,7},{7,4},{8,9},{9,10},{10,1... | collective-permute-start | bytes 196616 | tf_op jit(solution)/shard_map/ppermute | solution.py:81
  42.9 2.6 %collective-permute-done.8 = bf16[128,256]{1,0:T(8,128)(2,1)S(1)} collective-permute-done((bf16[128,256]{1,0:T(8,128)(2,1)S(1)}, bf16[128,256]{1,0:T(8,128)(2,1)S(1)}, u32[]{:S(2)}, u32[]{:S(2)}) %collective-permute-start.8) | collective-permute-done | bytes 65568 | tf_op jit(solution)/shard_map/ppermute | solution.py:81
  46.0 1.5 %collective-permute-done.7 = bf16[128,256]{1,0:T(8,128)(2,1)S(1)} collective-permute-done((bf16[128,256]{1,0:T(8,128)(2,1)S(1)}, bf16[128,256]{1,0:T(8,128)(2,1)S(1)}, u32[]{:S(2)}, u32[]{:S(2)}) %collective-permute-start.7) | collective-permute-done | bytes 65568 | tf_op jit(solution)/shard_map/ppermute | solution.py:81
  48.2 1.4 %collective-permute-start.14 = (bf16[128,128]{1,0:T(8,128)(2,1)S(1)}, bf16[128,128]{1,0:T(8,128)(2,1)S(1)}, u32[]{:S(2)}, u32[]{:S(2)}) collective-permute-start(bf16[128,128]{1,0:T(8,128)(2,1)S(1)} %bitcast.113), channel_id=1, source_target_pairs={{0,2},{1,3},{2,0},{3,1},{4,6},{5,7},{6,4},{7,5},{8,10},{9,11},{10,... | collective-permute-start | bytes 98312 | tf_op jit(solution)/shard_map/ppermute | solution.py:81
  49.6 0.8 %collective-permute-start.15 = (bf16[128,128]{1,0:T(8,128)(2,1)S(1)}, bf16[128,128]{1,0:T(8,128)(2,1)S(1)}, u32[]{:S(2)}, u32[]{:S(2)}) collective-permute-start(bf16[128,128]{1,0:T(8,128)(2,1)S(1)} %bitcast.114), channel_id=1, source_target_pairs={{0,3},{1,0},{2,1},{3,2},{4,7},{5,4},{6,5},{7,6},{8,11},{9,8},{10,9... | collective-permute-start | bytes 98312 | tf_op jit(solution)/shard_map/ppermute | solution.py:81
  50.4 1.3 %collective-permute-start.13 = (bf16[128,128]{1,0:T(8,128)(2,1)S(1)}, bf16[128,128]{1,0:T(8,128)(2,1)S(1)}, u32[]{:S(2)}, u32[]{:S(2)}) collective-permute-start(bf16[128,128]{1,0:T(8,128)(2,1)S(1)} %bitcast.115), channel_id=1, source_target_pairs={{0,1},{1,2},{2,3},{3,0},{4,5},{5,6},{6,7},{7,4},{8,9},{9,10},{10,1... | collective-permute-start | bytes 98312 | tf_op jit(solution)/shard_map/ppermute | solution.py:81
  51.7 3.8 %fusion.37 = f32[128,4096]{1,0:T(8,128)S(1)} fusion(bf16[128,768]{1,0:T(8,128)(2,1)S(1)} %fusion.3, bf16[768,4096]{1,0:T(8,128)(2,1)} %bitcast.90), kind=kOutput, calls=%fused_computation.107 | convolution fusion | flops 805306368 | bytes 8585216 | tf_op jit(solution)/shard_map/dot_general | solution.py:19
  56.6 1.9 %collective-permute-done.16 = bf16[2,4,8,4096]{3,2,1,0:T(8,128)(2,1)S(1)} collective-permute-done((bf16[2,4,8,4096]{3,2,1,0:T(8,128)(2,1)S(1)}, bf16[2,4,8,4096]{3,2,1,0:T(8,128)(2,1)S(1)}, u32[]{:S(2)}, u32[]{:S(2)}) %collective-permute-start.16) | collective-permute-done | bytes 524320 | tf_op jit(solution)/shard_map/ppermute | solution.py:84
  59.3 6.4 %collective-permute-done.17 = bf16[3,8,4096]{2,1,0:T(8,128)(2,1)S(1)} collective-permute-done((bf16[3,8,4096]{2,1,0:T(8,128)(2,1)S(1)}, bf16[3,8,4096]{2,1,0:T(8,128)(2,1)S(1)}, u32[]{:S(2)}, u32[]{:S(2)}) %collective-permute-start.17) | collective-permute-done | bytes 196640 | tf_op jit(solution)/shard_map/ppermute | solution.py:87
  66.3 2.1 %collective-permute-start.19 = (bf16[8,4096]{1,0:T(8,128)(2,1)S(1)}, bf16[8,4096]{1,0:T(8,128)(2,1)S(1)}, u32[]{:S(2)}, u32[]{:S(2)}) collective-permute-start(bf16[8,4096]{1,0:T(8,128)(2,1)S(1)} %get-tuple-element.23), channel_id=1, source_target_pairs={{0,3},{1,0},{2,1},{3,2},{4,7},{5,4},{6,5},{7,6},{8,11},{9,8},{10,9... | collective-permute-start | bytes 196616 | tf_op jit(solution)/shard_map/ppermute | solution.py:81
  68.4 1.1 %collective-permute-start.20 = (bf16[8,4096]{1,0:T(8,128)(2,1)S(1)}, bf16[8,4096]{1,0:T(8,128)(2,1)S(1)}, u32[]{:S(2)}, u32[]{:S(2)}) collective-permute-start(bf16[8,4096]{1,0:T(8,128)(2,1)S(1)} %get-tuple-element.25), channel_id=1, source_target_pairs={{0,2},{1,3},{2,0},{3,1},{4,6},{5,7},{6,4},{7,5},{8,10},{9,11},{10,... | collective-permute-start | bytes 196616 | tf_op jit(solution)/shard_map/ppermute | solution.py:81
  70.6 3.8 %collective-permute-done.21 = bf16[8,4096]{1,0:T(8,128)(2,1)S(1)} collective-permute-done((bf16[8,4096]{1,0:T(8,128)(2,1)S(1)}, bf16[8,4096]{1,0:T(8,128)(2,1)S(1)}, u32[]{:S(2)}, u32[]{:S(2)}) %collective-permute-start.21) | collective-permute-done | bytes 65568 | tf_op jit(solution)/shard_map/ppermute | solution.py:81
  74.4 0.7 fusion.13
  (92 shorter events, 7.3 us)
Async XLA Ops:
  0.0 56.1 %copy-start = (bf16[4,32,1024]{2,1,0:T(8,128)(2,1)S(1)}, bf16[4,32,1024]{2,1,0:T(8,128)(2,1)}, u32[]{:S(2)}) copy-start(bf16[4,32,1024]{2,1,0:T(8,128)(2,1)} %param.23) | copy-start | bytes 786436
  1.6 14.0 %collective-permute-start.3 = (bf16[8,4352]{1,0:T(8,128)(2,1)}, bf16[8,4352]{1,0:T(8,128)(2,1)S(1)}, u32[]{:S(2)}, u32[]{:S(2)}) collective-permute-start(bf16[8,4352]{1,0:T(8,128)(2,1)} %attach.1), channel_id=1, source_target_pairs={{0,8},{8,0},{1,9},{9,1},{2,10},{10,2},{3,11},{11,3},{4,12},{12,4},... | collective-permute-start | bytes 208904 | tf_op jit(solution)/shard_map/ppermute | solution.py:87
  4.6 8.9 %collective-permute-start.2 = (bf16[8,4352]{1,0:T(8,128)(2,1)}, bf16[8,4352]{1,0:T(8,128)(2,1)S(1)}, u32[]{:S(2)}, u32[]{:S(2)}) collective-permute-start(bf16[8,4352]{1,0:T(8,128)(2,1)} %attach.1), channel_id=1, source_target_pairs={{0,3},{1,0},{2,1},{3,2},{4,7},{5,4},{6,5},{7,6},{8,11},{9,8},{10,9... | collective-permute-start | bytes 208904 | tf_op jit(solution)/shard_map/ppermute | solution.py:81
  8.2 6.7 %collective-permute-start.1 = (bf16[8,4352]{1,0:T(8,128)(2,1)}, bf16[8,4352]{1,0:T(8,128)(2,1)S(1)}, u32[]{:S(2)}, u32[]{:S(2)}) collective-permute-start(bf16[8,4352]{1,0:T(8,128)(2,1)} %attach.1), channel_id=1, source_target_pairs={{0,2},{1,3},{2,0},{3,1},{4,6},{5,7},{6,4},{7,5},{8,10},{9,11},{10,... | collective-permute-start | bytes 208904 | tf_op jit(solution)/shard_map/ppermute | solution.py:81
  8.2 6.7 %collective-permute-start = (bf16[8,4352]{1,0:T(8,128)(2,1)}, bf16[8,4352]{1,0:T(8,128)(2,1)S(1)}, u32[]{:S(2)}, u32[]{:S(2)}) collective-permute-start(bf16[8,4352]{1,0:T(8,128)(2,1)} %attach.1), channel_id=1, source_target_pairs={{0,1},{1,2},{2,3},{3,0},{4,5},{5,6},{6,7},{7,4},{8,9},{9,10},{10,1... | collective-permute-start | bytes 208904 | tf_op jit(solution)/shard_map/ppermute | solution.py:81
  11.0 4.5 %copy-start.1 = (bf16[8,4352]{1,0:T(8,128)(2,1)S(1)}, bf16[8,4352]{1,0:T(8,128)(2,1)}, u32[]{:S(2)}) copy-start(bf16[8,4352]{1,0:T(8,128)(2,1)} %attach.1) | copy-start | bytes 208900
  14.9 7.0 %collective-permute-start.4 = (bf16[24,4352]{1,0:T(8,128)(2,1)S(1)}, bf16[24,4352]{1,0:T(8,128)(2,1)S(1)}, u32[]{:S(2)}, u32[]{:S(2)}) collective-permute-start(bf16[24,4352]{1,0:T(8,128)(2,1)S(1)} %pad_maximum_fusion.2), channel_id=1, source_target_pairs={{0,8},{8,0},{1,9},{9,1},{2,10},{10,2},{3,11},{11,3},{4,12},{12,4},... | collective-permute-start | bytes 626696 | tf_op jit(solution)/shard_map/ppermute | solution.py:87
  15.5 6.6 %collective-permute-start.5 = (bf16[32,4352]{1,0:T(8,128)(2,1)S(1)}, bf16[32,4352]{1,0:T(8,128)(2,1)S(1)}, u32[]{:S(2)}, u32[]{:S(2)}) collective-permute-start(bf16[32,4352]{1,0:T(8,128)(2,1)S(1)} %pad_maximum_fusion), channel_id=1, source_target_pairs={{0,4},{4,0},{1,5},{5,1},{2,6},{6,2},{3,7},{7,3},{8,12},{12,8},{9,1... | collective-permute-start | bytes 835592 | tf_op jit(solution)/shard_map/ppermute | solution.py:84
  22.0 8.3 %collective-permute-start.6 = (bf16[32,4352]{1,0:T(8,128)(2,1)S(1)}, bf16[32,4352]{1,0:T(8,128)(2,1)S(1)}, u32[]{:S(2)}, u32[]{:S(2)}) collective-permute-start(bf16[32,4352]{1,0:T(8,128)(2,1)S(1)} %pad_maximum_fusion.1), channel_id=1, source_target_pairs={{0,4},{4,0},{1,5},{5,1},{2,6},{6,2},{3,7},{7,3},{8,12},{12,8},{9,1... | collective-permute-start | bytes 835592 | tf_op jit(solution)/shard_map/ppermute | solution.py:84
  22.1 4.2 %collective-permute-start.10 = (bf16[96,192]{1,0:T(8,128)(2,1)S(1)}, bf16[96,192]{1,0:T(8,128)(2,1)S(1)}, u32[]{:S(2)}, u32[]{:S(2)}) collective-permute-start(bf16[96,192]{1,0:T(8,128)(2,1)S(1)} %get-tuple-element.14), channel_id=1, source_target_pairs={{0,3},{1,0},{2,1},{3,2},{4,7},{5,4},{6,5},{7,6},{8,11},{9,8},{10,9... | collective-permute-start | bytes 110600 | tf_op jit(solution)/shard_map/ppermute | solution.py:81
  22.9 7.1 %collective-permute-start.11 = (bf16[96,192]{1,0:T(8,128)(2,1)S(1)}, bf16[96,192]{1,0:T(8,128)(2,1)S(1)}, u32[]{:S(2)}, u32[]{:S(2)}) collective-permute-start(bf16[96,192]{1,0:T(8,128)(2,1)S(1)} %get-tuple-element.15), channel_id=1, source_target_pairs={{0,2},{1,3},{2,0},{3,1},{4,6},{5,7},{6,4},{7,5},{8,10},{9,11},{10,... | collective-permute-start | bytes 110600 | tf_op jit(solution)/shard_map/ppermute | solution.py:81
  23.6 6.4 %collective-permute-start.12 = (bf16[96,192]{1,0:T(8,128)(2,1)S(1)}, bf16[96,192]{1,0:T(8,128)(2,1)S(1)}, u32[]{:S(2)}, u32[]{:S(2)}) collective-permute-start(bf16[96,192]{1,0:T(8,128)(2,1)S(1)} %get-tuple-element.16), channel_id=1, source_target_pairs={{0,1},{1,2},{2,3},{3,0},{4,5},{5,6},{6,7},{7,4},{8,9},{9,10},{10,1... | collective-permute-start | bytes 110600 | tf_op jit(solution)/shard_map/ppermute | solution.py:81
  30.4 1.0 %copy-start.2 = (bf16[4,32,1024]{2,1,0:T(8,128)(2,1)S(1)}, bf16[4,32,1024]{2,1,0:T(8,128)(2,1)}, u32[]{:S(2)}) copy-start(bf16[4,32,1024]{2,1,0:T(8,128)(2,1)} %param.20) | copy-start | bytes 786436
  30.4 1.0 %copy-start.3 = (bf16[4,32,1024]{2,1,0:T(8,128)(2,1)S(1)}, bf16[4,32,1024]{2,1,0:T(8,128)(2,1)}, u32[]{:S(2)}) copy-start(bf16[4,32,1024]{2,1,0:T(8,128)(2,1)} %param.18) | copy-start | bytes 786436
  30.4 6.5 %slice-start = ((s8[6291456]{0:T(1024)(128)(4,1)}), s8[4194304]{0:T(1024)(128)(4,1)S(1)}, s32[]{:S(2)}) async-start(s8[6291456]{0:T(1024)(128)(4,1)} %bitcast.92), calls=%async_computation | async-start | bytes 8388608
  31.8 5.2 %slice-start.1 = ((s8[6291456]{0:T(1024)(128)(4,1)}), s8[2097152]{0:T(1024)(128)(4,1)S(1)}, s32[]{:S(2)}) async-start(s8[6291456]{0:T(1024)(128)(4,1)} %bitcast.92), calls=%async_computation.1 | async-start | bytes 4194304
  39.2 6.3 %collective-permute-start.8 = (bf16[128,256]{1,0:T(8,128)(2,1)S(1)}, bf16[128,256]{1,0:T(8,128)(2,1)S(1)}, u32[]{:S(2)}, u32[]{:S(2)}) collective-permute-start(bf16[128,256]{1,0:T(8,128)(2,1)S(1)} %bitcast.107), channel_id=1, source_target_pairs={{0,2},{1,3},{2,0},{3,1},{4,6},{5,7},{6,4},{7,5},{8,10},{9,11},{10,... | collective-permute-start | bytes 196616 | tf_op jit(solution)/shard_map/ppermute | solution.py:81
  40.3 5.7 %collective-permute-start.9 = (bf16[128,256]{1,0:T(8,128)(2,1)S(1)}, bf16[128,256]{1,0:T(8,128)(2,1)S(1)}, u32[]{:S(2)}, u32[]{:S(2)}) collective-permute-start(bf16[128,256]{1,0:T(8,128)(2,1)S(1)} %bitcast.108), channel_id=1, source_target_pairs={{0,3},{1,0},{2,1},{3,2},{4,7},{5,4},{6,5},{7,6},{8,11},{9,8},{10,9... | collective-permute-start | bytes 196616 | tf_op jit(solution)/shard_map/ppermute | solution.py:81
  41.4 6.1 %collective-permute-start.7 = (bf16[128,256]{1,0:T(8,128)(2,1)S(1)}, bf16[128,256]{1,0:T(8,128)(2,1)S(1)}, u32[]{:S(2)}, u32[]{:S(2)}) collective-permute-start(bf16[128,256]{1,0:T(8,128)(2,1)S(1)} %bitcast.109), channel_id=1, source_target_pairs={{0,1},{1,2},{2,3},{3,0},{4,5},{5,6},{6,7},{7,4},{8,9},{9,10},{10,1... | collective-permute-start | bytes 196616 | tf_op jit(solution)/shard_map/ppermute | solution.py:81
  48.2 7.3 %collective-permute-start.14 = (bf16[128,128]{1,0:T(8,128)(2,1)S(1)}, bf16[128,128]{1,0:T(8,128)(2,1)S(1)}, u32[]{:S(2)}, u32[]{:S(2)}) collective-permute-start(bf16[128,128]{1,0:T(8,128)(2,1)S(1)} %bitcast.113), channel_id=1, source_target_pairs={{0,2},{1,3},{2,0},{3,1},{4,6},{5,7},{6,4},{7,5},{8,10},{9,11},{10,... | collective-permute-start | bytes 98312 | tf_op jit(solution)/shard_map/ppermute | solution.py:81
  49.6 5.9 %collective-permute-start.15 = (bf16[128,128]{1,0:T(8,128)(2,1)S(1)}, bf16[128,128]{1,0:T(8,128)(2,1)S(1)}, u32[]{:S(2)}, u32[]{:S(2)}) collective-permute-start(bf16[128,128]{1,0:T(8,128)(2,1)S(1)} %bitcast.114), channel_id=1, source_target_pairs={{0,3},{1,0},{2,1},{3,2},{4,7},{5,4},{6,5},{7,6},{8,11},{9,8},{10,9... | collective-permute-start | bytes 98312 | tf_op jit(solution)/shard_map/ppermute | solution.py:81
  50.4 5.7 %collective-permute-start.13 = (bf16[128,128]{1,0:T(8,128)(2,1)S(1)}, bf16[128,128]{1,0:T(8,128)(2,1)S(1)}, u32[]{:S(2)}, u32[]{:S(2)}) collective-permute-start(bf16[128,128]{1,0:T(8,128)(2,1)S(1)} %bitcast.115), channel_id=1, source_target_pairs={{0,1},{1,2},{2,3},{3,0},{4,5},{5,6},{6,7},{7,4},{8,9},{9,10},{10,1... | collective-permute-start | bytes 98312 | tf_op jit(solution)/shard_map/ppermute | solution.py:81
  56.6 2.0 %collective-permute-start.16 = (bf16[2,4,8,4096]{3,2,1,0:T(8,128)(2,1)S(1)}, bf16[2,4,8,4096]{3,2,1,0:T(8,128)(2,1)S(1)}, u32[]{:S(2)}, u32[]{:S(2)}) collective-permute-start(bf16[2,4,8,4096]{3,2,1,0:T(8,128)(2,1)S(1)} %bitcast.106), channel_id=1, source_target_pairs={{0,4},{4,0},{1,5},{5,1},{2,6},{6,2},{3,7},{7,3},{8,12},{12,8},{9,1... | collective-permute-start | bytes 1572872 | tf_op jit(solution)/shard_map/ppermute | solution.py:84
  58.7 7.0 %collective-permute-start.17 = (bf16[3,8,4096]{2,1,0:T(8,128)(2,1)S(1)}, bf16[3,8,4096]{2,1,0:T(8,128)(2,1)S(1)}, u32[]{:S(2)}, u32[]{:S(2)}) collective-permute-start(bf16[3,8,4096]{2,1,0:T(8,128)(2,1)S(1)} %slice_bitcast_fusion.1), channel_id=1, source_target_pairs={{0,8},{8,0},{1,9},{9,1},{2,10},{10,2},{3,11},{11,3},{4,12},{12,4},... | collective-permute-start | bytes 589832 | tf_op jit(solution)/shard_map/ppermute | solution.py:87
  65.7 4.3 %collective-permute-start.18 = (bf16[8,4096]{1,0:T(8,128)(2,1)S(1)}, bf16[8,4096]{1,0:T(8,128)(2,1)S(1)}, u32[]{:S(2)}, u32[]{:S(2)}) collective-permute-start(bf16[8,4096]{1,0:T(8,128)(2,1)S(1)} %slice_bitcast_fusion.11), channel_id=1, source_target_pairs={{0,8},{8,0},{1,9},{9,1},{2,10},{10,2},{3,11},{11,3},{4,12},{12,4},... | collective-permute-start | bytes 196616 | tf_op jit(solution)/shard_map/ppermute | solution.py:87
  66.3 4.3 %collective-permute-start.19 = (bf16[8,4096]{1,0:T(8,128)(2,1)S(1)}, bf16[8,4096]{1,0:T(8,128)(2,1)S(1)}, u32[]{:S(2)}, u32[]{:S(2)}) collective-permute-start(bf16[8,4096]{1,0:T(8,128)(2,1)S(1)} %get-tuple-element.23), channel_id=1, source_target_pairs={{0,3},{1,0},{2,1},{3,2},{4,7},{5,4},{6,5},{7,6},{8,11},{9,8},{10,9... | collective-permute-start | bytes 196616 | tf_op jit(solution)/shard_map/ppermute | solution.py:81
  68.3 6.1 %collective-permute-start.21 = (bf16[8,4096]{1,0:T(8,128)(2,1)S(1)}, bf16[8,4096]{1,0:T(8,128)(2,1)S(1)}, u32[]{:S(2)}, u32[]{:S(2)}) collective-permute-start(bf16[8,4096]{1,0:T(8,128)(2,1)S(1)} %get-tuple-element.24), channel_id=1, source_target_pairs={{0,1},{1,2},{2,3},{3,0},{4,5},{5,6},{6,7},{7,4},{8,9},{9,10},{10,1... | collective-permute-start | bytes 196616 | tf_op jit(solution)/shard_map/ppermute | solution.py:81
  68.4 6.0 %collective-permute-start.20 = (bf16[8,4096]{1,0:T(8,128)(2,1)S(1)}, bf16[8,4096]{1,0:T(8,128)(2,1)S(1)}, u32[]{:S(2)}, u32[]{:S(2)}) collective-permute-start(bf16[8,4096]{1,0:T(8,128)(2,1)S(1)} %get-tuple-element.25), channel_id=1, source_target_pairs={{0,2},{1,3},{2,0},{3,1},{4,6},{5,7},{6,4},{7,5},{8,10},{9,11},{10,... | collective-permute-start | bytes 196616 | tf_op jit(solution)/shard_map/ppermute | solution.py:81

commit v5 on v3

v5 whole, which is shorter than its diff:
```python
import functools

import jax
import jax.numpy as jnp
from jax import lax
from jax.experimental import pallas as pl
from jax.experimental.pallas import tpu as pltpu
from jax.sharding import PartitionSpec as P

BF = jnp.bfloat16
F32 = jnp.float32
VMEM_LIMIT = 40 * 1024 * 1024


def dot_nt(a, b):
    return lax.dot_general(a, b, (((1,), (1,)), ((), ())), preferred_element_type=F32)


def dot_nn(a, b):
    return lax.dot_general(a, b, (((1,), (0,)), ((), ())), preferred_element_type=F32)


def after(value, earlier):
    return lax.optimization_barrier((value, earlier))[0]


def half_of(part, parts):
    return lax.rem(part, parts) // (parts // 2)


def rotated(value, rows, parts, step):
    if step == 0:
        return value
    span = rows * parts
    lines = []
    for start in range(0, value.shape[0], span):
        cut = start + span - step * rows
        lines += [value[cut : start + span], value[start:cut]]
    return jnp.concatenate(lines)


def attach_kernel(parts, tokens_ref, routes_ref, probs_ref, *out_refs):
    rows, width = tokens_ref.shape
    wide = width // 2
    pair = out_refs[-1].shape[1] - wide
    me = lax.axis_index("mp")
    routes = routes_ref[...]
    probs = probs_ref[...]
    lane = lax.broadcasted_iota(jnp.int32, (rows, pair), 1)
    ids = jnp.where(lane < pair // 2, lane, lane - pair // 2)
    weight = jnp.zeros((rows, pair), F32)
    for k in range(routes.shape[1]):
        weight += jnp.where(ids == routes[:, k : k + 1], probs[:, k : k + 1], 0.0)
    high = weight.astype(BF).astype(F32)
    side = jnp.where(lane < pair // 2, high, weight - high).astype(BF)
    for k in range(parts):
        half = half_of(me + k, parts)
        one = pl.multiple_of(half * wide, 128)
        two = pl.multiple_of((1 - half) * wide, 128)
        out_refs[k][...] = tokens_ref[:, pl.ds(one, wide)]
        out_refs[parts + k][:, :wide] = tokens_ref[:, pl.ds(two, wide)]
        out_refs[parts + k][:, wide:] = side


def attach(tokens, routes, probs, experts, parts):
    rows, width = tokens.shape
    pair = 2 * (-(-experts // 64) * 64)
    outs = pl.pallas_call(
        functools.partial(attach_kernel, parts),
        out_shape=[jax.ShapeDtypeStruct((rows, width // 2), BF)] * parts
        + [jax.ShapeDtypeStruct((rows, width // 2 + pair), BF)] * parts,
        name="attach",
    )(tokens, routes, probs)
    return outs[:parts], outs[parts:]


def inner_kernel(parts, rows, count, *refs):
    lines, (gate_ref, up_ref), outs = refs[:count], refs[count : count + 2], refs[count + 2 :]
    exp_dev, rank, block = gate_ref.shape
    offset = pl.multiple_of(lax.rem(lax.axis_index("mp"), parts // 2) * block, 128)
    x = jnp.concatenate([line[:, pl.ds(offset, block)] for line in lines])
    left = jnp.concatenate(
        [ref[...].reshape(exp_dev * rank, block) for ref in (gate_ref, up_ref)]
    )
    value = dot_nt(x, left)
    for k in range(parts):
        outs[k][...] = rotated(value, rows, parts, k).astype(BF)


def inner_products(lines, gate_left, up_left, parts, rows):
    total = sum(line.shape[0] for line in lines)
    ranks = 2 * gate_left.shape[0] * gate_left.shape[1]
    return pl.pallas_call(
        functools.partial(inner_kernel, parts, rows, len(lines)),
        out_shape=[jax.ShapeDtypeStruct((total, ranks), BF)] * parts,
        compiler_params=pltpu.CompilerParams(vmem_limit_bytes=VMEM_LIMIT),
        name="inner",
    )(*lines, gate_left, up_left)


def raw_kernel(count, wide, half_ref, *refs):
    lines, (gate_ref, up_ref), rest = refs[:count], refs[count : count + 2], refs[count + 2 :]
    x = jnp.concatenate([line[:, :wide] for line in lines])
    gate, up = dot_nt(x, gate_ref[...]), dot_nt(x, up_ref[...])
    if len(rest) == 4:
        gate += rest[0][...]
        up += rest[1][...]
    rest[-2][...] = gate
    rest[-1][...] = up


def raw_products(half, lines, gate_w, up_w, earlier):
    hid, width = gate_w.shape
    wide = width // 2
    total = sum(line.shape[0] for line in lines)
    tile = hid // 3 if hid % 384 == 0 else hid
    weights = pl.BlockSpec((tile, wide), lambda i, half: (i, half[0]))
    result = pl.BlockSpec((total, tile), lambda i, half: (0, i))
    return pl.pallas_call(
        functools.partial(raw_kernel, len(lines), wide),
        grid_spec=pltpu.PrefetchScalarGridSpec(
            num_scalar_prefetch=1,
            grid=(hid // tile,),
            in_specs=[pl.BlockSpec(line.shape, lambda i, half: (0, 0)) for line in lines]
            + [weights] * 2
            + [result] * len(earlier),
            out_specs=[result] * 2,
        ),
        out_shape=[jax.ShapeDtypeStruct((total, hid), F32)] * 2,
        compiler_params=pltpu.CompilerParams(vmem_limit_bytes=VMEM_LIMIT),
        name="raw",
    )(half, *lines, gate_w, up_w, *earlier)


def hidden_kernel(parts, rows, count, exp_dev, pair, place_ref, *refs):
    lines, inner, rest = refs[:count], refs[count : count + parts], refs[count + parts :]
    gate_ref, up_ref, diag_ref, hidden_ref = rest[:4]
    outs = rest[4:]
    hid = gate_ref.shape[1]
    ranks = diag_ref.shape[1]
    wide = lines[0].shape[1] - pair
    total = sum(ref[...].astype(F32) for ref in inner).astype(BF)
    gate = gate_ref[...] + dot_nn(total[:, :ranks], diag_ref[0])
    up = up_ref[...] + dot_nn(total[:, ranks:], diag_ref[1])
    lane = lax.broadcasted_iota(jnp.int32, (pair, hid), 0)
    lane = jnp.where(lane < pair // 2, lane, lane - pair // 2)
    owner = lax.broadcasted_iota(jnp.int32, (pair, hid), 1) // (hid // exp_dev)
    pick = (lane == owner + place_ref[0]).astype(F32).astype(BF)
    scale = dot_nn(jnp.concatenate([line[:, wide:] for line in lines]), pick)
    hidden = (gate / (1.0 + jnp.exp(-gate)) * up * scale).astype(BF)
    hidden_ref[...] = hidden
    value = dot_nt(hidden, diag_ref[2])
    for k in range(parts):
        outs[k][...] = rotated(value, rows, parts, k).astype(BF)


def hidden_units(place, lines, inner, raw, diag, parts, rows, exp_dev, pair):
    total, hid = raw[0].shape
    ranks = diag.shape[1]
    vmem = pl.BlockSpec(memory_space=pltpu.VMEM)
    return pl.pallas_call(
        functools.partial(hidden_kernel, parts, rows, len(lines), exp_dev, pair),
        in_specs=[pl.BlockSpec(memory_space=pltpu.SMEM)]
        + [vmem] * (len(lines) + len(inner) + 3),
        out_shape=[jax.ShapeDtypeStruct((total, hid), BF)]
        + [jax.ShapeDtypeStruct((total, ranks), BF)] * parts,
        compiler_params=pltpu.CompilerParams(vmem_limit_bytes=VMEM_LIMIT),
        name="hidden",
    )(place, *lines, *inner, *raw, diag)


def down_kernel(place_ref, hidden_ref, down_ref, *refs):
    near_ref, far_ref = refs[-2:]
    near = near_ref.shape[0]
    value = dot_nn(hidden_ref[...], down_ref[...])
    near_ref[...] = value[:near]
    far_ref[...] = value[near:].astype(BF)
    if len(refs) > 2:
        right_ref, bottom = refs[0], refs[1:-2]
        step = pl.program_id(0) - place_ref[1]

        @pl.when((step >= 0) & (step < place_ref[2]))
        def _():
            low = sum(ref[...].astype(F32) for ref in bottom).astype(BF)
            extra = value + dot_nn(low, right_ref[...])
            near_ref[...] = extra[:near]
            far_ref[...] = extra[near:].astype(BF)


def down_products(place, hidden, down_w, right, bottom):
    total, hid = hidden.shape
    wide = down_w.shape[1] // 2
    tile = min(512, right.shape[1])
    steps = wide // tile
    last = right.shape[1] // tile - 1
    specs = [
        pl.BlockSpec((total, hid), lambda i, place: (0, 0)),
        pl.BlockSpec((hid, tile), lambda i, place: (0, place[0] * steps + i)),
    ]
    args = [hidden, down_w]
    if bottom:
        specs.append(
            pl.BlockSpec(
                (right.shape[0], tile),
                lambda i, place: (0, jnp.minimum(jnp.maximum(i - place[1], 0), last)),
            )
        )
        specs += [pl.BlockSpec(b.shape, lambda i, place: (0, 0)) for b in bottom]
        args += [right, *bottom]
    return pl.pallas_call(
        down_kernel,
        grid_spec=pltpu.PrefetchScalarGridSpec(
            num_scalar_prefetch=1,
            grid=(steps,),
            in_specs=specs,
            out_specs=[pl.BlockSpec((total // 2, tile), lambda i, place: (0, i))] * 2,
        ),
        out_shape=[
            jax.ShapeDtypeStruct((total // 2, wide), F32),
            jax.ShapeDtypeStruct((total // 2, wide), BF),
        ],
        compiler_params=pltpu.CompilerParams(vmem_limit_bytes=VMEM_LIMIT),
        name="down",
    )(place, *args)


def local(
    tokens,
    routes,
    probs,
    w_gate,
    w_up,
    w_down,
    gate_left,
    gate_right,
    up_left,
    up_right,
    down_left,
    down_right,
):
    rows, width = tokens.shape
    exp_dev, _, cols = w_gate.shape
    rank = gate_left.shape[1]
    piece = gate_right.shape[1]
    block = gate_left.shape[2]
    parts = lax.axis_size("mp")
    chips = lax.axis_size("y")
    experts = exp_dev * chips * 2
    me_g = lax.axis_index("y") * 2 + lax.axis_index("core")
    me_m = lax.axis_index("mp")
    ranks = exp_dev * rank
    hid = exp_dev * cols
    wide = width // 2

    def along_z(value, step):
        return lax.ppermute(value, "mp", [(i, (i + step) % parts) for i in range(parts)])

    def along_y(value, step):
        return lax.ppermute(value, "y", [(i, (i + step) % chips) for i in range(chips)])

    def other_core(value):
        return lax.ppermute(value, "core", [(0, 1), (1, 0)])

    def gather(own, pieces):
        line = jnp.concatenate([own] + pieces)
        lines = [line] + [along_y(line, s) for s in range(1, chips)]
        return lines + [other_core(line) for line in lines]

    one, two = attach(tokens, routes, probs, experts, parts)
    pieces = [along_z(one[k], k) for k in range(1, parts)]
    two = [two[0]] + list(after(tuple(two[1:]), pieces[0]))
    lines = gather(one[0], pieces)
    pieces = [along_z(two[k], k) for k in range(1, parts)]
    lines_two = gather(two[0], pieces)

    small = jnp.stack([gate_right, up_right, down_left])
    small = small.reshape(3 * exp_dev * piece, parts, cols).swapaxes(0, 1)
    small = jnp.concatenate([small, small])
    small = [
        lax.dynamic_index_in_dim(small, me_m + k, 0, keepdims=False) for k in range(parts)
    ]
    small = after(tuple(small), pieces[-1])
    small = [small[0]] + [along_z(small[k], k) for k in range(1, parts)]
    small = jnp.stack([small[-k % parts] for k in range(parts)] * 2)
    small = lax.dynamic_slice_in_dim(small, parts - me_m, parts, 0)
    small = small.reshape(parts, 3, exp_dev, piece, cols).transpose(1, 2, 0, 3, 4)
    small = small.reshape(3, ranks, cols)
    same = (jnp.arange(ranks) // rank)[:, None] == (jnp.arange(hid) // cols)[None, :]
    diag = jnp.where(same, jnp.tile(small, (1, 1, exp_dev)), jnp.zeros((), BF))

    half = half_of(me_m, parts)
    inner = inner_products(lines, gate_left, up_left, parts, rows)
    inner = [inner[0]] + [along_z(inner[k], k) for k in range(1, parts)]
    gate_w = jnp.swapaxes(w_gate, 1, 2).reshape(hid, width)
    up_w = jnp.swapaxes(w_up, 1, 2).reshape(hid, width)
    raw = raw_products(half[None], lines, gate_w, up_w, ())
    raw = raw_products(1 - half[None], lines_two, gate_w, up_w, raw)
    first_expert = (me_g * exp_dev)[None]
    hidden, *bottom = hidden_units(
        first_expert, lines_two, inner, raw, diag, parts, rows, exp_dev, two[0].shape[1] - wide
    )
    bottom = [bottom[0]] + [along_z(bottom[k], k) for k in range(1, parts)]

    down_w = w_down.reshape(hid, width)
    right = down_right.reshape(ranks, block)
    tile = min(512, block)
    tiles = block // tile
    start = lax.rem(me_m, parts // 2) * tiles

    def combine(near, far):
        out = (near + other_core(far).astype(F32)).reshape(chips, parts, rows, wide)
        line = out[0]
        for s in range(1, chips):
            line += along_y(out[s].astype(BF), -s).astype(F32)
        return [line[0]] + [along_z(line[k].astype(BF), -k).astype(F32) for k in range(1, parts)]

    tiles = jnp.int32(tiles)
    got_one = combine(*down_products(jnp.stack([1 - half, start, tiles]), hidden, down_w, right, ()))
    got_two = combine(*down_products(jnp.stack([half, start, tiles]), hidden, down_w, right, bottom))
    result = []
    for side in range(2):
        total = jnp.zeros((rows, wide), F32)
        for k in range(parts):
            total += jnp.where(half_of(me_m + k, parts) == side, got_two[k], got_one[k])
        result.append(total)
    return jnp.concatenate(result, axis=1).astype(BF)


def solution(mesh):
    count = mesh.shape
    fine = jax.sharding.Mesh(
        mesh.devices.reshape(count["groups"], count["expert"] // 2, 2, count["mp"]),
        ("groups", "y", "core", "mp"),
    )
    expert = ("y", "core")
    return jax.shard_map(
        local,
        mesh=fine,
        in_specs=(
            P(("groups", "y", "core", "mp"), None),
            P(("groups", "y", "core", "mp"), None),
            P(("groups", "y", "core", "mp"), None),
            P(expert, None, "mp"),
            P(expert, None, "mp"),
            P(expert, "mp", None),
            P(expert, None, "mp"),
            P(expert, "mp", None),
            P(expert, None, "mp"),
            P(expert, "mp", None),
            P(expert, "mp", None),
            P(expert, None, "mp"),
        ),
        out_specs=P(("groups", "y", "core", "mp"), None),
        check_vma=False,
    )
```

time: 74.5 us -> 96.7 us (1.30)
  starting transfers between devices: 19.5 us -> 40.2 us
  blocking collectives: 19.7 us -> 0 us
  Pallas kernels: 0 us -> 14.6 us
  matrix products: 12.4 us -> 0 us
  waiting for transfers between devices: 12.6 us -> 24.1 us
  local copies, waits for them, and re-layouts: 3.22 us -> 11.7 us
    ppermute x9 -> x21, starting transfers between devices: 12.2 us -> 34 us  [along_z(): lax.ppermute(value, 'mp', [(i, (i + step) % parts) for i in range(parts)])]
    ppermute x9 -> x21, waiting for transfers between devices: 0.14 us -> 20.8 us  [along_z(): lax.ppermute(value, 'mp', [(i, (i + step) % parts) for i in range(parts)])]
    all_to_all x1 -> x0, blocking collectives: 19.7 us -> none  [swap(): lax.all_to_all(value, ('y', 'mp'), split_axis=0, concat_axis=0, tiled=True)]
    pallas_call x0 -> x7, Pallas kernels: none -> 14.6 us  [the longest x2 7.6 us: raw_products(): pl.pallas_call(functools.partial(raw_kernel, len(lines), wide), grid_spec...]
    dot_general x8 -> x0, matrix products: 12.4 us -> none  [the longest x4 7.88 us: dot_nt(): lax.dot_general(a, b, (((1,), (1,)), ((), ())), preferred_element_type=F32)]
    all_to_all x1 -> x0, waiting for transfers between devices: 10.6 us -> none  [swap(): lax.all_to_all(value, ('y', 'mp'), split_axis=0, concat_axis=0, tiled=True)]
    unnamed x13 -> x33, local copies, waits for them, and re-layouts: 0.05 us -> 8.16 us
    all_to_all x1 -> x0, starting transfers between devices: 7.28 us -> none  [swap(): lax.all_to_all(value, ('y', 'mp'), split_axis=0, concat_axis=0, tiled=True)]
  transfers between devices with their start and end apart: 12 -> 31, of which waited for: 3 -> 13; matrix products, arithmetic and copies ran while one was open for 23% -> 10% of each run, Pallas kernels for 0% -> 11%
where the time goes in v5:
time: 96.7 us; the launch traced here: 96.2 us
  starting transfers between devices  40.2 us (42%)
  waiting for transfers between devices  24.1 us (25%)
  Pallas kernels  14.6 us (15%)
  local copies, waits for them, and re-layouts  11.7 us (12%)
  other arithmetic  5.25 us (5%)
    ppermute x21, starting transfers between devices, along_z(): lax.ppermute(value, 'mp', [(i, (i + step) % parts) for i in range(parts)])  34 us
    ppermute x21, waiting for transfers between devices, along_z(): lax.ppermute(value, 'mp', [(i, (i + step) % parts) for i in range(parts)])  20.8 us
    unnamed x33, local copies, waits for them, and re-layouts  8.16 us
    pallas_call x2, Pallas kernels, raw_products(): pl.pallas_call(functools.partial(raw_kernel, len(lines), wide), grid_spec...  7.6 us
    ppermute x4, starting transfers between devices, along_y(): lax.ppermute(value, 'y', [(i, (i + step) % chips) for i in range(chips)])  5.44 us
    pallas_call x2, Pallas kernels, down_products(): pl.pallas_call(down_kernel, grid_spec=pltpu.PrefetchScalarGridSpec(num_sc...  4.47 us
    ppermute x4, waiting for transfers between devices, along_y(): lax.ppermute(value, 'y', [(i, (i + step) % chips) for i in range(chips)])  3.27 us
    another operation x3, local copies, waits for them, and re-layouts, local(): diag = jnp.where(same, jnp.tile(small, (1, 1, exp_dev)), jnp.zeros((), BF))  3.22 us
  transfers between devices with their start and end apart: 31, of which 13 were waited for; matrix products, arithmetic and copies ran while one was open for 10% of the time, Pallas kernels for 11%

profile of v5, /device:TPU:0, one launch (start us, length us, event | category | flops | bytes accessed | tf_op | source)
XLA Modules:
  0.0 96.2 jit_solution(14846404592045913389)
XLA Ops:
  0.0 1.6 %attach.1 = (bf16[8,2048]{1,0:T(8,128)(2,1)}, bf16[8,2048]{1,0:T(8,128)(2,1)}, bf16[8,2048]{1,0:T(8,128)(2,1)}, bf16[8,2048]{1,0:T(8,128)(2,1)}, bf16[8,2176]{1,...) custom-call(bf16[8,4096]{1,0:T(8,128)(2,1)} %tokens_ref.1, ...), custom_call_target="tpu_custom_call" | custom-call | tf_op jit(solution)/shard_map/attach/pallas_call | solution.py:68
  1.7 3.0 %collective-permute-start = (bf16[8,2048]{1,0:T(8,128)(2,1)}, bf16[8,2048]{1,0:T(8,128)(2,1)S(1)}, u32[]{:S(2)}, u32[]{:S(2)}) collective-permute-start(bf16[8,2048]{1,0:T(8,128)(2,1)} %get-tuple-element.41), channel_id=1, source_target_pairs={{0,1},{1,2},{2,3},{3,0},{4,5},{5,6},{6,7},{7,4},{8,9},{9,10},{10,1... | collective-permute-start | bytes 98312 | tf_op jit(solution)/shard_map/ppermute | solution.py:256
  4.7 2.6 %collective-permute-start.7 = (bf16[8,2048]{1,0:T(8,128)(2,1)}, bf16[8,2048]{1,0:T(8,128)(2,1)S(1)}, u32[]{:S(2)}, u32[]{:S(2)}) collective-permute-start(bf16[8,2048]{1,0:T(8,128)(2,1)} %get-tuple-element.46), channel_id=1, source_target_pairs={{0,2},{1,3},{2,0},{3,1},{4,6},{5,7},{6,4},{7,5},{8,10},{9,11},{10,... | collective-permute-start | bytes 98312 | tf_op jit(solution)/shard_map/ppermute | solution.py:256
  7.3 1.3 %collective-permute-start.8 = (bf16[8,2048]{1,0:T(8,128)(2,1)}, bf16[8,2048]{1,0:T(8,128)(2,1)S(1)}, u32[]{:S(2)}, u32[]{:S(2)}) collective-permute-start(bf16[8,2048]{1,0:T(8,128)(2,1)} %get-tuple-element.47), channel_id=1, source_target_pairs={{0,3},{1,0},{2,1},{3,2},{4,7},{5,4},{6,5},{7,6},{8,11},{9,8},{10,9... | collective-permute-start | bytes 98312 | tf_op jit(solution)/shard_map/ppermute | solution.py:256
  11.3 2.1 %fusion.4 = (bf16[1,96,192]{2,0,1:T(2,128)(2,1)S(1)}, bf16[1,96,192]{2,0,1:T(2,128)(2,1)S(1)}, bf16[1,96,192]{2,0,1:T(2,128)(2,1)S(1)}, bf16[1,96,192]{2,0,1:T(2,128)(2,1)S(1)}) fusion(s32[]{:T(128)S(6)} %select_n.120, bf16[4,96,192]{2,0,1:T(4,128)(2,1)S(1)} %bitcast.87, s32[]{:T(128)S(6)} %select_n.119, s32[]{:T(128)S(6)} %select_n.118, s32[]{:T(128)S(6)} %select_n.117), kind=kLoop, calls=%fused_computation.21 | loop fusion | flops 294912 | bytes 294928 | tf_op jit(solution)/shard_map/concatenate | solution.py:278
  14.3 1.6 %collective-permute-start.9 = (bf16[32,2048]{1,0:T(8,128)(2,1)S(1)}, bf16[32,2048]{1,0:T(8,128)(2,1)S(1)}, u32[]{:S(2)}, u32[]{:S(2)}) collective-permute-start(bf16[32,2048]{1,0:T(8,128)(2,1)S(1)} %constant_dynamic-update-slice_fusion.4.refs_0_), channel_id=1, source_target_pairs={{0,8},{8,0},{1,9},{9,1},{2,10},{10,2},{3,11},{11,3},{4,12},{12,4},... | collective-permute-start | bytes 393224 | tf_op jit(solution)/shard_map/ppermute | solution.py:259
  16.3 2.8 %collective-permute-start.3 = (bf16[8,2176]{1,0:T(8,128)(2,1)}, bf16[8,2176]{1,0:T(8,128)(2,1)S(1)}, u32[]{:S(2)}, u32[]{:S(2)}) collective-permute-start(bf16[8,2176]{1,0:T(8,128)(2,1)} %get-tuple-element.44), channel_id=1, source_target_pairs={{0,3},{1,0},{2,1},{3,2},{4,7},{5,4},{6,5},{7,6},{8,11},{9,8},{10,9... | collective-permute-start | bytes 104456 | tf_op jit(solution)/shard_map/ppermute | solution.py:256
  19.6 2.2 %collective-permute-done.2 = bf16[8,2176]{1,0:T(8,128)(2,1)S(1)} collective-permute-done((bf16[8,2176]{1,0:T(8,128)(2,1)}, bf16[8,2176]{1,0:T(8,128)(2,1)S(1)}, u32[]{:S(2)}, u32[]{:S(2)}) %collective-permute-start.2) | collective-permute-done | bytes 34848 | tf_op jit(solution)/shard_map/ppermute | solution.py:256
  22.8 2.7 %collective-permute-start.15 = (bf16[96,192]{1,0:T(8,128)(2,1)S(1)}, bf16[96,192]{1,0:T(8,128)(2,1)S(1)}, u32[]{:S(2)}, u32[]{:S(2)}) collective-permute-start(bf16[96,192]{1,0:T(8,128)(2,1)S(1)} %get-tuple-element.57), channel_id=1, source_target_pairs={{0,3},{1,0},{2,1},{3,2},{4,7},{5,4},{6,5},{7,6},{8,11},{9,8},{10,9... | collective-permute-start | bytes 110600 | tf_op jit(solution)/shard_map/ppermute | solution.py:256
  25.5 1.7 %collective-permute-done.15 = bf16[96,192]{1,0:T(8,128)(2,1)S(1)} collective-permute-done((bf16[96,192]{1,0:T(8,128)(2,1)S(1)}, bf16[96,192]{1,0:T(8,128)(2,1)S(1)}, u32[]{:S(2)}, u32[]{:S(2)}) %collective-permute-start.15) | collective-permute-done | bytes 36896 | tf_op jit(solution)/shard_map/ppermute | solution.py:256
  27.3 1.2 %collective-permute-start.16 = (bf16[96,192]{1,0:T(8,128)(2,1)S(1)}, bf16[96,192]{1,0:T(8,128)(2,1)S(1)}, u32[]{:S(2)}, u32[]{:S(2)}) collective-permute-start(bf16[96,192]{1,0:T(8,128)(2,1)S(1)} %get-tuple-element.58), channel_id=1, source_target_pairs={{0,2},{1,3},{2,0},{3,1},{4,6},{5,7},{6,4},{7,5},{8,10},{9,11},{10,... | collective-permute-start | bytes 110600 | tf_op jit(solution)/shard_map/ppermute | solution.py:256
  28.5 4.3 %collective-permute-done.16 = bf16[96,192]{1,0:T(8,128)(2,1)S(1)} collective-permute-done((bf16[96,192]{1,0:T(8,128)(2,1)S(1)}, bf16[96,192]{1,0:T(8,128)(2,1)S(1)}, u32[]{:S(2)}, u32[]{:S(2)}) %collective-permute-start.16) | collective-permute-done | bytes 36896 | tf_op jit(solution)/shard_map/ppermute | solution.py:256
  32.8 1.3 %collective-permute-start.17 = (bf16[96,192]{1,0:T(8,128)(2,1)S(1)}, bf16[96,192]{1,0:T(8,128)(2,1)S(1)}, u32[]{:S(2)}, u32[]{:S(2)}) collective-permute-start(bf16[96,192]{1,0:T(8,128)(2,1)S(1)} %get-tuple-element.59), channel_id=1, source_target_pairs={{0,1},{1,2},{2,3},{3,0},{4,5},{5,6},{6,7},{7,4},{8,9},{9,10},{10,1... | collective-permute-start | bytes 110600 | tf_op jit(solution)/shard_map/ppermute | solution.py:256
  34.1 4.6 %collective-permute-done.17 = bf16[96,192]{1,0:T(8,128)(2,1)S(1)} collective-permute-done((bf16[96,192]{1,0:T(8,128)(2,1)S(1)}, bf16[96,192]{1,0:T(8,128)(2,1)S(1)}, u32[]{:S(2)}, u32[]{:S(2)}) %collective-permute-start.17) | collective-permute-done | bytes 36896 | tf_op jit(solution)/shard_map/ppermute | solution.py:256
  40.0 2.1 %copy.16 = bf16[3,128,768]{2,1,0:T(8,128)(2,1)} copy(bf16[3,128,768]{1,2,0:T(8,128)(2,1)} %bitcast.84) | data formatting | bytes 1179648 | tf_op jit(solution)/shard_map/tile | solution.py:289
  44.0 2.6 %collective-permute-start.13 = (bf16[128,256]{1,0:T(8,128)(2,1)S(1)}, bf16[128,256]{1,0:T(8,128)(2,1)S(1)}, u32[]{:S(2)}, u32[]{:S(2)}) collective-permute-start(bf16[128,256]{1,0:T(8,128)(2,1)S(1)} %get-tuple-element.50), channel_id=1, source_target_pairs={{0,2},{1,3},{2,0},{3,1},{4,6},{5,7},{6,4},{7,5},{8,10},{9,11},{10,... | collective-permute-start | bytes 196616 | tf_op jit(solution)/shard_map/ppermute | solution.py:256
  46.6 1.2 %collective-permute-start.14 = (bf16[128,256]{1,0:T(8,128)(2,1)S(1)}, bf16[128,256]{1,0:T(8,128)(2,1)S(1)}, u32[]{:S(2)}, u32[]{:S(2)}) collective-permute-start(bf16[128,256]{1,0:T(8,128)(2,1)S(1)} %get-tuple-element.51), channel_id=1, source_target_pairs={{0,3},{1,0},{2,1},{3,2},{4,7},{5,4},{6,5},{7,6},{8,11},{9,8},{10,9... | collective-permute-start | bytes 196616 | tf_op jit(solution)/shard_map/ppermute | solution.py:256
  48.9 2.8 %copy-done = bf16[4,4096,192]{1,2,0:T(8,128)(2,1)S(1)} copy-done((bf16[4,4096,192]{1,2,0:T(8,128)(2,1)S(1)}, bf16[4,4096,192]{1,2,0:T(8,128)(2,1)}, u32[]{:S(2)}) %copy-start) | copy-done | bytes 6291480
  51.7 2.8 %copy-done.1 = bf16[4,4096,192]{1,2,0:T(8,128)(2,1)S(1)} copy-done((bf16[4,4096,192]{1,2,0:T(8,128)(2,1)S(1)}, bf16[4,4096,192]{1,2,0:T(8,128)(2,1)}, u32[]{:S(2)}) %copy-start.1) | copy-done | bytes 6291480
  54.5 3.1 %raw.2 = (f32[128,768]{1,0:T(8,128)S(1)}, f32[128,768]{1,0:T(8,128)S(1)}) custom-call(s32[1]{0:T(128)} %bitcast.half_ref, bf16[32,2048]{1,0:T(8,128)(2,1)S(1)} %constant_dynamic-update-slice_fusion.4.refs_0_, bf16[32,2048]{1,0:T(8,128)(2,1)S(1)} %collective-permute-done.9.refs_1_, bf16[32,2048]{1,0:T(8,128)(2,1)S(1)} %collective-permute-done.10.refs_2_, ...), custom_call_target="tpu_custom_call" | custom-call | tf_op jit(solution)/shard_map/raw/pallas_call | solution.py:119
  57.6 4.5 %raw.3 = (f32[128,768]{1,0:T(8,128)S(1)}, f32[128,768]{1,0:T(8,128)S(1)}) custom-call(s32[1]{0:T(128)S(6)} %sub.40.half_ref, bf16[32,2176]{1,0:T(8,128)(2,1)S(1)} %constant_dynamic-update-slice_fusion.refs_0_, bf16[32,2176]{1,0:T(8,128)(2,1)S(1)} %collective-permute-done.4.refs_1_, bf16[32,2176]{1,0:T(8,128)(2,1)S(1)} %collective-permute-done.5.refs_2_, ...), custom_call_target="tpu_custom_call" | custom-call | tf_op jit(solution)/shard_map/raw/pallas_call | solution.py:119
  62.8 2.0 %down.3 = (f32[64,2048]{1,0:T(8,128)S(1)}, bf16[64,2048]{1,0:T(8,128)(2,1)S(1)}) custom-call(s32[3]{0:T(128)S(1)} %pad_add_fusion.place_ref, bf16[128,768]{1,0:T(8,128)(2,1)S(1)} %get-tuple-element.60.hidden_ref, bf16[768,4096]{1,0:T(8,128)(2,1)S(1)} %bitcast.81), custom_call_target="tpu_custom_call" | custom-call | tf_op jit(solution)/shard_map/down/pallas_call | solution.py:210
  65.7 1.3 %collective-permute-start.19 = (bf16[128,128]{1,0:T(8,128)(2,1)S(1)}, bf16[128,128]{1,0:T(8,128)(2,1)S(1)}, u32[]{:S(2)}, u32[]{:S(2)}) collective-permute-start(bf16[128,128]{1,0:T(8,128)(2,1)S(1)} %get-tuple-element.63), channel_id=1, source_target_pairs={{0,2},{1,3},{2,0},{3,1},{4,6},{5,7},{6,4},{7,5},{8,10},{9,11},{10,... | collective-permute-start | bytes 98312 | tf_op jit(solution)/shard_map/ppermute | solution.py:256
  67.1 2.8 %collective-permute-start.20 = (bf16[128,128]{1,0:T(8,128)(2,1)S(1)}, bf16[128,128]{1,0:T(8,128)(2,1)S(1)}, u32[]{:S(2)}, u32[]{:S(2)}) collective-permute-start(bf16[128,128]{1,0:T(8,128)(2,1)S(1)} %get-tuple-element.64), channel_id=1, source_target_pairs={{0,3},{1,0},{2,1},{3,2},{4,7},{5,4},{6,5},{7,6},{8,11},{9,8},{10,9... | collective-permute-start | bytes 98312 | tf_op jit(solution)/shard_map/ppermute | solution.py:256
  71.6 2.5 %down.2 = (f32[64,2048]{1,0:T(8,128)S(1)}, bf16[64,2048]{1,0:T(8,128)(2,1)S(1)}) custom-call(s32[3]{0:T(128)S(1)} %pad_add_fusion.1.place_ref, bf16[128,768]{1,0:T(8,128)(2,1)S(1)} %get-tuple-element.60.hidden_ref, bf16[768,4096]{1,0:T(8,128)(2,1)S(1)} %bitcast.82, bf16[128,1024]{1,0:T(8,128)(2,1)S(1)} %bitcast.83, ...), custom_call_target="tpu_custom_call" | custom-call | tf_op jit(solution)/shard_map/down/pallas_call | solution.py:210
  74.2 1.6 %collective-permute-start.24 = (bf16[4,8,2048]{2,1,0:T(8,128)(2,1)S(1)}, bf16[4,8,2048]{2,1,0:T(8,128)(2,1)S(1)}, u32[]{:S(2)}, u32[]{:S(2)}) collective-permute-start(bf16[4,8,2048]{2,1,0:T(8,128)(2,1)S(1)} %fusion.3), channel_id=1, source_target_pairs={{0,8},{8,0},{1,9},{9,1},{2,10},{10,2},{3,11},{11,3},{4,12},{12,4},... | collective-permute-start | bytes 393224 | tf_op jit(solution)/shard_map/ppermute | solution.py:259
  75.9 1.4 %collective-permute-start.22 = (bf16[4,8,2048]{2,1,0:T(8,128)(2,1)S(1)}, bf16[4,8,2048]{2,1,0:T(8,128)(2,1)S(1)}, u32[]{:S(2)}, u32[]{:S(2)}) collective-permute-start(bf16[4,8,2048]{2,1,0:T(8,128)(2,1)S(1)} %fusion.2), channel_id=1, source_target_pairs={{0,8},{8,0},{1,9},{9,1},{2,10},{10,2},{3,11},{11,3},{4,12},{12,4},... | collective-permute-start | bytes 393224 | tf_op jit(solution)/shard_map/ppermute | solution.py:259
  77.3 3.3 %collective-permute-done.24 = bf16[4,8,2048]{2,1,0:T(8,128)(2,1)S(1)} collective-permute-done((bf16[4,8,2048]{2,1,0:T(8,128)(2,1)S(1)}, bf16[4,8,2048]{2,1,0:T(8,128)(2,1)S(1)}, u32[]{:S(2)}, u32[]{:S(2)}) %collective-permute-start.24) | collective-permute-done | bytes 131104 | tf_op jit(solution)/shard_map/ppermute | solution.py:259
  80.6 4.1 %collective-permute-start.26 = (bf16[8,2048]{1,0:T(8,128)(2,1)S(1)}, bf16[8,2048]{1,0:T(8,128)(2,1)S(1)}, u32[]{:S(2)}, u32[]{:S(2)}) collective-permute-start(bf16[8,2048]{1,0:T(8,128)(2,1)S(1)} %get-tuple-element.84), channel_id=1, source_target_pairs={{0,3},{1,0},{2,1},{3,2},{4,7},{5,4},{6,5},{7,6},{8,11},{9,8},{10,9... | collective-permute-start | bytes 98312 | tf_op jit(solution)/shard_map/ppermute | solution.py:256
  85.4 3.2 %collective-permute-start.25 = (bf16[8,2048]{1,0:T(8,128)(2,1)S(1)}, bf16[8,2048]{1,0:T(8,128)(2,1)S(1)}, u32[]{:S(2)}, u32[]{:S(2)}) collective-permute-start(bf16[8,2048]{1,0:T(8,128)(2,1)S(1)} %get-tuple-element.81), channel_id=1, source_target_pairs={{0,3},{1,0},{2,1},{3,2},{4,7},{5,4},{6,5},{7,6},{8,11},{9,8},{10,9... | collective-permute-start | bytes 98312 | tf_op jit(solution)/shard_map/ppermute | solution.py:256
  90.6 2.9 %collective-permute-done.27 = bf16[8,2048]{1,0:T(8,128)(2,1)S(1)} collective-permute-done((bf16[8,2048]{1,0:T(8,128)(2,1)S(1)}, bf16[8,2048]{1,0:T(8,128)(2,1)S(1)}, u32[]{:S(2)}, u32[]{:S(2)}) %collective-permute-start.27) | collective-permute-done | bytes 32800 | tf_op jit(solution)/shard_map/ppermute | solution.py:256
  93.5 2.0 %collective-permute-done.29 = bf16[8,2048]{1,0:T(8,128)(2,1)S(1)} collective-permute-done((bf16[8,2048]{1,0:T(8,128)(2,1)S(1)}, bf16[8,2048]{1,0:T(8,128)(2,1)S(1)}, u32[]{:S(2)}, u32[]{:S(2)}) %collective-permute-start.29) | collective-permute-done | bytes 32800 | tf_op jit(solution)/shard_map/ppermute | solution.py:256
  (99 shorter events, 16.3 us)
Async XLA Ops:
  0.0 42.6 %copy-start.3 = (bf16[4,32,1024]{2,1,0:T(8,128)(2,1)S(1)}, bf16[4,32,1024]{2,1,0:T(8,128)(2,1)}, u32[]{:S(2)}) copy-start(bf16[4,32,1024]{2,1,0:T(8,128)(2,1)} %refs_4_.1) | copy-start | bytes 786436
  1.7 12.0 %collective-permute-start = (bf16[8,2048]{1,0:T(8,128)(2,1)}, bf16[8,2048]{1,0:T(8,128)(2,1)S(1)}, u32[]{:S(2)}, u32[]{:S(2)}) collective-permute-start(bf16[8,2048]{1,0:T(8,128)(2,1)} %get-tuple-element.41), channel_id=1, source_target_pairs={{0,1},{1,2},{2,3},{3,0},{4,5},{5,6},{6,7},{7,4},{8,9},{9,10},{10,1... | collective-permute-start | bytes 98312 | tf_op jit(solution)/shard_map/ppermute | solution.py:256
  4.7 9.6 %collective-permute-start.7 = (bf16[8,2048]{1,0:T(8,128)(2,1)}, bf16[8,2048]{1,0:T(8,128)(2,1)S(1)}, u32[]{:S(2)}, u32[]{:S(2)}) collective-permute-start(bf16[8,2048]{1,0:T(8,128)(2,1)} %get-tuple-element.46), channel_id=1, source_target_pairs={{0,2},{1,3},{2,0},{3,1},{4,6},{5,7},{6,4},{7,5},{8,10},{9,11},{10,... | collective-permute-start | bytes 98312 | tf_op jit(solution)/shard_map/ppermute | solution.py:256
  7.3 7.0 %collective-permute-start.8 = (bf16[8,2048]{1,0:T(8,128)(2,1)}, bf16[8,2048]{1,0:T(8,128)(2,1)S(1)}, u32[]{:S(2)}, u32[]{:S(2)}) collective-permute-start(bf16[8,2048]{1,0:T(8,128)(2,1)} %get-tuple-element.47), channel_id=1, source_target_pairs={{0,3},{1,0},{2,1},{3,2},{4,7},{5,4},{6,5},{7,6},{8,11},{9,8},{10,9... | collective-permute-start | bytes 98312 | tf_op jit(solution)/shard_map/ppermute | solution.py:256
  13.6 6.0 %collective-permute-start.1 = (bf16[8,2176]{1,0:T(8,128)(2,1)}, bf16[8,2176]{1,0:T(8,128)(2,1)S(1)}, u32[]{:S(2)}, u32[]{:S(2)}) collective-permute-start(bf16[8,2176]{1,0:T(8,128)(2,1)} %get-tuple-element.42), channel_id=1, source_target_pairs={{0,1},{1,2},{2,3},{3,0},{4,5},{5,6},{6,7},{7,4},{8,9},{9,10},{10,1... | collective-permute-start | bytes 104456 | tf_op jit(solution)/shard_map/ppermute | solution.py:256
  14.3 24.4 %collective-permute-start.9 = (bf16[32,2048]{1,0:T(8,128)(2,1)S(1)}, bf16[32,2048]{1,0:T(8,128)(2,1)S(1)}, u32[]{:S(2)}, u32[]{:S(2)}) collective-permute-start(bf16[32,2048]{1,0:T(8,128)(2,1)S(1)} %constant_dynamic-update-slice_fusion.4.refs_0_), channel_id=1, source_target_pairs={{0,8},{8,0},{1,9},{9,1},{2,10},{10,2},{3,11},{11,3},{4,12},{12,4},... | collective-permute-start | bytes 393224 | tf_op jit(solution)/shard_map/ppermute | solution.py:259
  15.9 26.7 %collective-permute-start.10 = (bf16[32,2048]{1,0:T(8,128)(2,1)S(1)}, bf16[32,2048]{1,0:T(8,128)(2,1)S(1)}, u32[]{:S(2)}, u32[]{:S(2)}) collective-permute-start(bf16[32,2048]{1,0:T(8,128)(2,1)S(1)} %constant_dynamic-update-slice_fusion.4.refs_0_), channel_id=1, source_target_pairs={{0,4},{4,0},{1,5},{5,1},{2,6},{6,2},{3,7},{7,3},{8,12},{12,8},{9,1... | collective-permute-start | bytes 393224 | tf_op jit(solution)/shard_map/ppermute | solution.py:262
  15.9 5.9 %collective-permute-start.2 = (bf16[8,2176]{1,0:T(8,128)(2,1)}, bf16[8,2176]{1,0:T(8,128)(2,1)S(1)}, u32[]{:S(2)}, u32[]{:S(2)}) collective-permute-start(bf16[8,2176]{1,0:T(8,128)(2,1)} %get-tuple-element.43), channel_id=1, source_target_pairs={{0,2},{1,3},{2,0},{3,1},{4,6},{5,7},{6,4},{7,5},{8,10},{9,11},{10,... | collective-permute-start | bytes 104456 | tf_op jit(solution)/shard_map/ppermute | solution.py:256
  16.3 5.7 %collective-permute-start.3 = (bf16[8,2176]{1,0:T(8,128)(2,1)}, bf16[8,2176]{1,0:T(8,128)(2,1)S(1)}, u32[]{:S(2)}, u32[]{:S(2)}) collective-permute-start(bf16[8,2176]{1,0:T(8,128)(2,1)} %get-tuple-element.44), channel_id=1, source_target_pairs={{0,3},{1,0},{2,1},{3,2},{4,7},{5,4},{6,5},{7,6},{8,11},{9,8},{10,9... | collective-permute-start | bytes 104456 | tf_op jit(solution)/shard_map/ppermute | solution.py:256
  22.0 20.2 %collective-permute-start.4 = (bf16[32,2176]{1,0:T(8,128)(2,1)S(1)}, bf16[32,2176]{1,0:T(8,128)(2,1)S(1)}, u32[]{:S(2)}, u32[]{:S(2)}) collective-permute-start(bf16[32,2176]{1,0:T(8,128)(2,1)S(1)} %constant_dynamic-update-slice_fusion.refs_0_), channel_id=1, source_target_pairs={{0,8},{8,0},{1,9},{9,1},{2,10},{10,2},{3,11},{11,3},{4,12},{12,4},... | collective-permute-start | bytes 417800 | tf_op jit(solution)/shard_map/ppermute | solution.py:259
  22.8 34.7 %collective-permute-start.5 = (bf16[32,2176]{1,0:T(8,128)(2,1)S(1)}, bf16[32,2176]{1,0:T(8,128)(2,1)S(1)}, u32[]{:S(2)}, u32[]{:S(2)}) collective-permute-start(bf16[32,2176]{1,0:T(8,128)(2,1)S(1)} %constant_dynamic-update-slice_fusion.refs_0_), channel_id=1, source_target_pairs={{0,4},{4,0},{1,5},{5,1},{2,6},{6,2},{3,7},{7,3},{8,12},{12,8},{9,1... | collective-permute-start | bytes 417800 | tf_op jit(solution)/shard_map/ppermute | solution.py:262
  22.8 4.4 %collective-permute-start.15 = (bf16[96,192]{1,0:T(8,128)(2,1)S(1)}, bf16[96,192]{1,0:T(8,128)(2,1)S(1)}, u32[]{:S(2)}, u32[]{:S(2)}) collective-permute-start(bf16[96,192]{1,0:T(8,128)(2,1)S(1)} %get-tuple-element.57), channel_id=1, source_target_pairs={{0,3},{1,0},{2,1},{3,2},{4,7},{5,4},{6,5},{7,6},{8,11},{9,8},{10,9... | collective-permute-start | bytes 110600 | tf_op jit(solution)/shard_map/ppermute | solution.py:256
  27.3 5.5 %collective-permute-start.16 = (bf16[96,192]{1,0:T(8,128)(2,1)S(1)}, bf16[96,192]{1,0:T(8,128)(2,1)S(1)}, u32[]{:S(2)}, u32[]{:S(2)}) collective-permute-start(bf16[96,192]{1,0:T(8,128)(2,1)S(1)} %get-tuple-element.58), channel_id=1, source_target_pairs={{0,2},{1,3},{2,0},{3,1},{4,6},{5,7},{6,4},{7,5},{8,10},{9,11},{10,... | collective-permute-start | bytes 110600 | tf_op jit(solution)/shard_map/ppermute | solution.py:256
  32.8 5.9 %collective-permute-start.17 = (bf16[96,192]{1,0:T(8,128)(2,1)S(1)}, bf16[96,192]{1,0:T(8,128)(2,1)S(1)}, u32[]{:S(2)}, u32[]{:S(2)}) collective-permute-start(bf16[96,192]{1,0:T(8,128)(2,1)S(1)} %get-tuple-element.59), channel_id=1, source_target_pairs={{0,1},{1,2},{2,3},{3,0},{4,5},{5,6},{6,7},{7,4},{8,9},{9,10},{10,1... | collective-permute-start | bytes 110600 | tf_op jit(solution)/shard_map/ppermute | solution.py:256
  38.8 3.9 %collective-permute-start.11 = (bf16[32,2048]{1,0:T(8,128)(2,1)S(1)}, bf16[32,2048]{1,0:T(8,128)(2,1)S(1)}, u32[]{:S(2)}, u32[]{:S(2)}) collective-permute-start(bf16[32,2048]{1,0:T(8,128)(2,1)S(1)} %collective-permute-done.9.refs_1_), channel_id=1, source_target_pairs={{0,4},{4,0},{1,5},{5,1},{2,6},{6,2},{3,7},{7,3},{8,12},{12,8},{9,1... | collective-permute-start | bytes 393224 | tf_op jit(solution)/shard_map/ppermute | solution.py:262
  42.2 15.4 %collective-permute-start.6 = (bf16[32,2176]{1,0:T(8,128)(2,1)S(1)}, bf16[32,2176]{1,0:T(8,128)(2,1)S(1)}, u32[]{:S(2)}, u32[]{:S(2)}) collective-permute-start(bf16[32,2176]{1,0:T(8,128)(2,1)S(1)} %collective-permute-done.4.refs_1_), channel_id=1, source_target_pairs={{0,4},{4,0},{1,5},{5,1},{2,6},{6,2},{3,7},{7,3},{8,12},{12,8},{9,1... | collective-permute-start | bytes 417800 | tf_op jit(solution)/shard_map/ppermute | solution.py:262
  43.9 18.3 %collective-permute-start.12 = (bf16[128,256]{1,0:T(8,128)(2,1)S(1)}, bf16[128,256]{1,0:T(8,128)(2,1)S(1)}, u32[]{:S(2)}, u32[]{:S(2)}) collective-permute-start(bf16[128,256]{1,0:T(8,128)(2,1)S(1)} %get-tuple-element.49), channel_id=1, source_target_pairs={{0,1},{1,2},{2,3},{3,0},{4,5},{5,6},{6,7},{7,4},{8,9},{9,10},{10,1... | collective-permute-start | bytes 196616 | tf_op jit(solution)/shard_map/ppermute | solution.py:256
  44.0 18.2 %collective-permute-start.13 = (bf16[128,256]{1,0:T(8,128)(2,1)S(1)}, bf16[128,256]{1,0:T(8,128)(2,1)S(1)}, u32[]{:S(2)}, u32[]{:S(2)}) collective-permute-start(bf16[128,256]{1,0:T(8,128)(2,1)S(1)} %get-tuple-element.50), channel_id=1, source_target_pairs={{0,2},{1,3},{2,0},{3,1},{4,6},{5,7},{6,4},{7,5},{8,10},{9,11},{10,... | collective-permute-start | bytes 196616 | tf_op jit(solution)/shard_map/ppermute | solution.py:256
  46.6 15.7 %collective-permute-start.14 = (bf16[128,256]{1,0:T(8,128)(2,1)S(1)}, bf16[128,256]{1,0:T(8,128)(2,1)S(1)}, u32[]{:S(2)}, u32[]{:S(2)}) collective-permute-start(bf16[128,256]{1,0:T(8,128)(2,1)S(1)} %get-tuple-element.51), channel_id=1, source_target_pairs={{0,3},{1,0},{2,1},{3,2},{4,7},{5,4},{6,5},{7,6},{8,11},{9,8},{10,9... | collective-permute-start | bytes 196616 | tf_op jit(solution)/shard_map/ppermute | solution.py:256
  64.8 9.3 %collective-permute-start.23 = (bf16[64,2048]{1,0:T(8,128)(2,1)S(1)}, bf16[64,2048]{1,0:T(8,128)(2,1)S(1)}, u32[]{:S(2)}, u32[]{:S(2)}) collective-permute-start(bf16[64,2048]{1,0:T(8,128)(2,1)S(1)} %get-tuple-element.68), channel_id=1, source_target_pairs={{0,4},{4,0},{1,5},{5,1},{2,6},{6,2},{3,7},{7,3},{8,12},{12,8},{9,1... | collective-permute-start | bytes 786440 | tf_op jit(solution)/shard_map/ppermute | solution.py:262
  64.9 5.9 %collective-permute-start.18 = (bf16[128,128]{1,0:T(8,128)(2,1)S(1)}, bf16[128,128]{1,0:T(8,128)(2,1)S(1)}, u32[]{:S(2)}, u32[]{:S(2)}) collective-permute-start(bf16[128,128]{1,0:T(8,128)(2,1)S(1)} %get-tuple-element.62), channel_id=1, source_target_pairs={{0,1},{1,2},{2,3},{3,0},{4,5},{5,6},{6,7},{7,4},{8,9},{9,10},{10,1... | collective-permute-start | bytes 98312 | tf_op jit(solution)/shard_map/ppermute | solution.py:256
  65.7 5.5 %collective-permute-start.19 = (bf16[128,128]{1,0:T(8,128)(2,1)S(1)}, bf16[128,128]{1,0:T(8,128)(2,1)S(1)}, u32[]{:S(2)}, u32[]{:S(2)}) collective-permute-start(bf16[128,128]{1,0:T(8,128)(2,1)S(1)} %get-tuple-element.63), channel_id=1, source_target_pairs={{0,2},{1,3},{2,0},{3,1},{4,6},{5,7},{6,4},{7,5},{8,10},{9,11},{10,... | collective-permute-start | bytes 98312 | tf_op jit(solution)/shard_map/ppermute | solution.py:256
  67.1 4.5 %collective-permute-start.20 = (bf16[128,128]{1,0:T(8,128)(2,1)S(1)}, bf16[128,128]{1,0:T(8,128)(2,1)S(1)}, u32[]{:S(2)}, u32[]{:S(2)}) collective-permute-start(bf16[128,128]{1,0:T(8,128)(2,1)S(1)} %get-tuple-element.64), channel_id=1, source_target_pairs={{0,3},{1,0},{2,1},{3,2},{4,7},{5,4},{6,5},{7,6},{8,11},{9,8},{10,9... | collective-permute-start | bytes 98312 | tf_op jit(solution)/shard_map/ppermute | solution.py:256
  74.0 1.8 %collective-permute-start.21 = (bf16[64,2048]{1,0:T(8,128)(2,1)S(1)}, bf16[64,2048]{1,0:T(8,128)(2,1)S(1)}, u32[]{:S(2)}, u32[]{:S(2)}) collective-permute-start(bf16[64,2048]{1,0:T(8,128)(2,1)S(1)} %get-tuple-element.66), channel_id=1, source_target_pairs={{0,4},{4,0},{1,5},{5,1},{2,6},{6,2},{3,7},{7,3},{8,12},{12,8},{9,1... | collective-permute-start | bytes 786440 | tf_op jit(solution)/shard_map/ppermute | solution.py:262
  74.2 6.4 %collective-permute-start.24 = (bf16[4,8,2048]{2,1,0:T(8,128)(2,1)S(1)}, bf16[4,8,2048]{2,1,0:T(8,128)(2,1)S(1)}, u32[]{:S(2)}, u32[]{:S(2)}) collective-permute-start(bf16[4,8,2048]{2,1,0:T(8,128)(2,1)S(1)} %fusion.3), channel_id=1, source_target_pairs={{0,8},{8,0},{1,9},{9,1},{2,10},{10,2},{3,11},{11,3},{4,12},{12,4},... | collective-permute-start | bytes 393224 | tf_op jit(solution)/shard_map/ppermute | solution.py:259
  75.9 9.5 %collective-permute-start.22 = (bf16[4,8,2048]{2,1,0:T(8,128)(2,1)S(1)}, bf16[4,8,2048]{2,1,0:T(8,128)(2,1)S(1)}, u32[]{:S(2)}, u32[]{:S(2)}) collective-permute-start(bf16[4,8,2048]{2,1,0:T(8,128)(2,1)S(1)} %fusion.2), channel_id=1, source_target_pairs={{0,8},{8,0},{1,9},{9,1},{2,10},{10,2},{3,11},{11,3},{4,12},{12,4},... | collective-permute-start | bytes 393224 | tf_op jit(solution)/shard_map/ppermute | solution.py:259
  80.6 9.2 %collective-permute-start.26 = (bf16[8,2048]{1,0:T(8,128)(2,1)S(1)}, bf16[8,2048]{1,0:T(8,128)(2,1)S(1)}, u32[]{:S(2)}, u32[]{:S(2)}) collective-permute-start(bf16[8,2048]{1,0:T(8,128)(2,1)S(1)} %get-tuple-element.84), channel_id=1, source_target_pairs={{0,3},{1,0},{2,1},{3,2},{4,7},{5,4},{6,5},{7,6},{8,11},{9,8},{10,9... | collective-permute-start | bytes 98312 | tf_op jit(solution)/shard_map/ppermute | solution.py:256
  84.8 5.1 %collective-permute-start.28 = (bf16[8,2048]{1,0:T(8,128)(2,1)S(1)}, bf16[8,2048]{1,0:T(8,128)(2,1)S(1)}, u32[]{:S(2)}, u32[]{:S(2)}) collective-permute-start(bf16[8,2048]{1,0:T(8,128)(2,1)S(1)} %get-tuple-element.83), channel_id=1, source_target_pairs={{0,2},{1,3},{2,0},{3,1},{4,6},{5,7},{6,4},{7,5},{8,10},{9,11},{10,... | collective-permute-start | bytes 98312 | tf_op jit(solution)/shard_map/ppermute | solution.py:256
  84.8 5.8 %collective-permute-start.30 = (bf16[8,2048]{1,0:T(8,128)(2,1)S(1)}, bf16[8,2048]{1,0:T(8,128)(2,1)S(1)}, u32[]{:S(2)}, u32[]{:S(2)}) collective-permute-start(bf16[8,2048]{1,0:T(8,128)(2,1)S(1)} %get-tuple-element.82), channel_id=1, source_target_pairs={{0,1},{1,2},{2,3},{3,0},{4,5},{5,6},{6,7},{7,4},{8,9},{9,10},{10,1... | collective-permute-start | bytes 98312 | tf_op jit(solution)/shard_map/ppermute | solution.py:256
  85.4 5.1 %collective-permute-start.25 = (bf16[8,2048]{1,0:T(8,128)(2,1)S(1)}, bf16[8,2048]{1,0:T(8,128)(2,1)S(1)}, u32[]{:S(2)}, u32[]{:S(2)}) collective-permute-start(bf16[8,2048]{1,0:T(8,128)(2,1)S(1)} %get-tuple-element.81), channel_id=1, source_target_pairs={{0,3},{1,0},{2,1},{3,2},{4,7},{5,4},{6,5},{7,6},{8,11},{9,8},{10,9... | collective-permute-start | bytes 98312 | tf_op jit(solution)/shard_map/ppermute | solution.py:256
  88.7 4.8 %collective-permute-start.27 = (bf16[8,2048]{1,0:T(8,128)(2,1)S(1)}, bf16[8,2048]{1,0:T(8,128)(2,1)S(1)}, u32[]{:S(2)}, u32[]{:S(2)}) collective-permute-start(bf16[8,2048]{1,0:T(8,128)(2,1)S(1)} %get-tuple-element.80), channel_id=1, source_target_pairs={{0,2},{1,3},{2,0},{3,1},{4,6},{5,7},{6,4},{7,5},{8,10},{9,11},{10,... | collective-permute-start | bytes 98312 | tf_op jit(solution)/shard_map/ppermute | solution.py:256
  89.8 5.7 %collective-permute-start.29 = (bf16[8,2048]{1,0:T(8,128)(2,1)S(1)}, bf16[8,2048]{1,0:T(8,128)(2,1)S(1)}, u32[]{:S(2)}, u32[]{:S(2)}) collective-permute-start(bf16[8,2048]{1,0:T(8,128)(2,1)S(1)} %get-tuple-element.79), channel_id=1, source_target_pairs={{0,1},{1,2},{2,3},{3,0},{4,5},{5,6},{6,7},{7,4},{8,9},{9,10},{10,1... | collective-permute-start | bytes 98312 | tf_op jit(solution)/shard_map/ppermute | solution.py:256
  (8 other events, 47.9 us)

commit v6 on v5

v6 whole, which is shorter than its diff:
```python
import functools

import jax
import jax.numpy as jnp
from jax import lax
from jax.experimental import pallas as pl
from jax.experimental.pallas import tpu as pltpu
from jax.sharding import PartitionSpec as P

BF = jnp.bfloat16
F32 = jnp.float32
VMEM_LIMIT = 24 * 1024 * 1024
STREAM_LIMIT = 56 * 1024 * 1024


def dot_nt(a, b):
    return lax.dot_general(a, b, (((1,), (1,)), ((), ())), preferred_element_type=F32)


def dot_nn(a, b):
    return lax.dot_general(a, b, (((1,), (0,)), ((), ())), preferred_element_type=F32)


def after(value, earlier):
    return lax.optimization_barrier((value, earlier))[0]


def rotated(value, rows, parts, step):
    if step == 0:
        return value
    span = rows * parts
    lines = []
    for start in range(0, value.shape[0], span):
        cut = start + span - step * rows
        lines += [value[cut : start + span], value[start:cut]]
    return jnp.concatenate(lines)


def attach_kernel(tokens_ref, routes_ref, probs_ref, out_ref):
    rows, width = tokens_ref.shape
    pair = out_ref.shape[1] - width
    out_ref[:, :width] = tokens_ref[...]
    routes = routes_ref[...]
    probs = probs_ref[...]
    lane = lax.broadcasted_iota(jnp.int32, (rows, pair), 1)
    ids = jnp.where(lane < pair // 2, lane, lane - pair // 2)
    weight = jnp.zeros((rows, pair), F32)
    for k in range(routes.shape[1]):
        weight += jnp.where(ids == routes[:, k : k + 1], probs[:, k : k + 1], 0.0)
    high = weight.astype(BF).astype(F32)
    out_ref[:, width:] = jnp.where(lane < pair // 2, high, weight - high).astype(BF)


def attach(tokens, routes, probs, pair):
    rows, width = tokens.shape
    return pl.pallas_call(
        attach_kernel,
        out_shape=jax.ShapeDtypeStruct((rows, width + pair), BF),
        name="attach",
    )(tokens, routes, probs)


def cut_kernel(parts, *refs):
    ins, outs = refs[:3], refs[3:]
    exp_dev, piece, hid = ins[0].shape
    cols = hid // parts
    me = lax.axis_index("mp")
    for n, ref in enumerate(ins):
        value = ref[...].reshape(exp_dev * piece, hid).astype(F32)
        blocks = [value[:, j * cols : (j + 1) * cols] for j in range(parts)]
        for k in range(parts):
            target = lax.rem(me + k, parts)
            block = blocks[0]
            for j in range(1, parts):
                block = jnp.where(target == j, blocks[j], block)
            outs[k][n] = block.astype(BF)


def cut(factors, parts):
    exp_dev, piece, hid = factors[0].shape
    return pl.pallas_call(
        functools.partial(cut_kernel, parts),
        out_shape=[jax.ShapeDtypeStruct((3, exp_dev * piece, hid // parts), BF)] * parts,
        name="cut",
    )(*factors)


def spread_kernel(parts, exp_dev, *refs):
    pieces, out_ref = refs[:-1], refs[-1]
    _, ranks, hid = out_ref.shape
    rank = ranks // exp_dev
    piece = rank // parts
    me = lax.axis_index("mp")
    row = lax.broadcasted_iota(jnp.int32, (ranks, ranks), 0)
    col = lax.broadcasted_iota(jnp.int32, (ranks, ranks), 1)
    step = lax.rem(me - row % rank // piece + parts, parts)
    source = (step * exp_dev + row // rank) * piece + row % piece
    order = (col == source).astype(F32).astype(BF)
    own = (
        lax.broadcasted_iota(jnp.int32, (ranks, hid), 0) // rank
        == lax.broadcasted_iota(jnp.int32, (ranks, hid), 1) // (hid // exp_dev)
    )
    for n in range(3):
        value = dot_nn(order, jnp.concatenate([p[n].astype(F32) for p in pieces]).astype(BF))
        value = jnp.concatenate([value] * exp_dev, axis=1)
        out_ref[n] = jnp.where(own, value, 0.0).astype(BF)


def spread(pieces, parts, exp_dev):
    _, span, cols = pieces[0].shape
    return pl.pallas_call(
        functools.partial(spread_kernel, parts, exp_dev),
        out_shape=jax.ShapeDtypeStruct((3, span * parts, cols * exp_dev), BF),
        name="spread",
    )(*pieces)


def inner_kernel(parts, rows, count, *refs):
    lines, (gate_ref, up_ref), outs = refs[:count], refs[count : count + 2], refs[count + 2 :]
    exp_dev, rank, block = gate_ref.shape
    offset = pl.multiple_of(lax.axis_index("mp") * block, 128)
    x = jnp.concatenate([line[:, pl.ds(offset, block)] for line in lines])
    left = jnp.concatenate(
        [ref[...].reshape(exp_dev * rank, block) for ref in (gate_ref, up_ref)]
    )
    value = dot_nt(x, left)
    for k in range(parts):
        outs[k][...] = rotated(value, rows, parts, k).astype(BF)


def inner_products(lines, gate_left, up_left, parts, rows):
    total = sum(line.shape[0] for line in lines)
    ranks = 2 * gate_left.shape[0] * gate_left.shape[1]
    return pl.pallas_call(
        functools.partial(inner_kernel, parts, rows, len(lines)),
        out_shape=[jax.ShapeDtypeStruct((total, ranks), BF)] * parts,
        compiler_params=pltpu.CompilerParams(vmem_limit_bytes=VMEM_LIMIT),
        name="inner",
    )(*lines, gate_left, up_left)


def raw_kernel(count, *refs):
    lines, (gate_w, up_w, gate_ref, up_ref) = refs[:count], refs[count:]
    x = jnp.concatenate([line[:, : gate_w.shape[1]] for line in lines])
    gate_ref[...] = dot_nt(x, gate_w[...])
    up_ref[...] = dot_nt(x, up_w[...])


def raw_products(lines, gate_w, up_w):
    hid, width = gate_w.shape
    total = sum(line.shape[0] for line in lines)
    tile = hid // 3 if hid % 384 == 0 else hid
    weights = pl.BlockSpec((tile, width), lambda i: (i, 0))
    result = pl.BlockSpec((total, tile), lambda i: (0, i))
    return pl.pallas_call(
        functools.partial(raw_kernel, len(lines)),
        grid=(hid // tile,),
        in_specs=[pl.BlockSpec(line.shape, lambda i: (0, 0)) for line in lines] + [weights] * 2,
        out_specs=[result] * 2,
        out_shape=[jax.ShapeDtypeStruct((total, hid), F32)] * 2,
        compiler_params=pltpu.CompilerParams(vmem_limit_bytes=STREAM_LIMIT),
        name="raw",
    )(*lines, gate_w, up_w)


def hidden_kernel(parts, rows, count, exp_dev, pair, place_ref, *refs):
    lines, inner, rest = refs[:count], refs[count : count + parts], refs[count + parts :]
    gate_ref, up_ref, diag_ref, hidden_ref = rest[:4]
    outs = rest[4:]
    hid = gate_ref.shape[1]
    ranks = diag_ref.shape[1]
    wide = lines[0].shape[1] - pair
    total = sum(ref[...].astype(F32) for ref in inner).astype(BF)
    gate = gate_ref[...] + dot_nn(total[:, :ranks], diag_ref[0])
    up = up_ref[...] + dot_nn(total[:, ranks:], diag_ref[1])
    lane = lax.broadcasted_iota(jnp.int32, (pair, hid), 0)
    lane = jnp.where(lane < pair // 2, lane, lane - pair // 2)
    owner = lax.broadcasted_iota(jnp.int32, (pair, hid), 1) // (hid // exp_dev)
    pick = (lane == owner + place_ref[0]).astype(F32).astype(BF)
    scale = dot_nn(jnp.concatenate([line[:, wide:] for line in lines]), pick)
    hidden = (gate / (1.0 + jnp.exp(-gate)) * up * scale).astype(BF)
    hidden_ref[...] = hidden
    value = dot_nt(hidden, diag_ref[2])
    for k in range(parts):
        outs[k][...] = rotated(value, rows, parts, k).astype(BF)


def hidden_units(place, lines, inner, raw, diag, parts, rows, exp_dev, pair):
    total, hid = raw[0].shape
    ranks = diag.shape[1]
    vmem = pl.BlockSpec(memory_space=pltpu.VMEM)
    return pl.pallas_call(
        functools.partial(hidden_kernel, parts, rows, len(lines), exp_dev, pair),
        in_specs=[pl.BlockSpec(memory_space=pltpu.SMEM)]
        + [vmem] * (len(lines) + len(inner) + 3),
        out_shape=[jax.ShapeDtypeStruct((total, hid), BF)]
        + [jax.ShapeDtypeStruct((total, ranks), BF)] * parts,
        compiler_params=pltpu.CompilerParams(vmem_limit_bytes=VMEM_LIMIT),
        name="hidden",
    )(place, *lines, *inner, *raw, diag)


def down_kernel(hidden_ref, down_ref, near_ref, far_ref):
    near = near_ref.shape[0]
    value = dot_nn(hidden_ref[...], down_ref[...])
    near_ref[...] = value[:near]
    far_ref[...] = value[near:].astype(BF)


def down_products(hidden, down_w):
    total, hid = hidden.shape
    width = down_w.shape[1]
    tile = 1024
    return pl.pallas_call(
        down_kernel,
        grid=(width // tile,),
        in_specs=[
            pl.BlockSpec((total, hid), lambda i: (0, 0)),
            pl.BlockSpec((hid, tile), lambda i: (0, i)),
        ],
        out_specs=[pl.BlockSpec((total // 2, tile), lambda i: (0, i))] * 2,
        out_shape=[
            jax.ShapeDtypeStruct((total // 2, width), F32),
            jax.ShapeDtypeStruct((total // 2, width), BF),
        ],
        compiler_params=pltpu.CompilerParams(vmem_limit_bytes=STREAM_LIMIT),
        name="down",
    )(hidden, down_w)


def extra_kernel(right_ref, *refs):
    bottom, (near_ref, far_ref) = refs[:-2], refs[-2:]
    near = near_ref.shape[0]
    low = sum(ref[...].astype(F32) for ref in bottom).astype(BF)
    value = dot_nn(low, right_ref[...])
    near_ref[...] = value[:near]
    far_ref[...] = value[near:].astype(BF)


def extra_products(right, bottom):
    total = bottom[0].shape[0]
    block = right.shape[1]
    return pl.pallas_call(
        extra_kernel,
        out_shape=[
            jax.ShapeDtypeStruct((total // 2, block), F32),
            jax.ShapeDtypeStruct((total // 2, block), BF),
        ],
        compiler_params=pltpu.CompilerParams(vmem_limit_bytes=VMEM_LIMIT),
        name="extra",
    )(right, *bottom)


def merge_kernel(own_ref, back_ref, extra_ref, *out_refs):
    block = extra_ref.shape[2]
    offset = pl.multiple_of(lax.axis_index("mp") * block, 128)
    for k, out_ref in enumerate(out_refs):
        total = own_ref[k]
        if k > 0:
            total += back_ref[k - 1]
        out_ref[...] = total.astype(out_ref.dtype)
        low = own_ref[k, :, pl.ds(offset, block)] + extra_ref[k]
        if k > 0:
            low += back_ref[k - 1, :, pl.ds(offset, block)]
        out_ref[:, pl.ds(offset, block)] = low.astype(out_ref.dtype)


def merge(own, back, extra):
    parts, rows, width = own.shape
    return pl.pallas_call(
        merge_kernel,
        out_shape=[jax.ShapeDtypeStruct((rows, width), F32)]
        + [jax.ShapeDtypeStruct((rows, width), BF)] * (parts - 1),
        compiler_params=pltpu.CompilerParams(vmem_limit_bytes=VMEM_LIMIT),
        name="merge",
    )(own, back, extra)


def local(
    tokens,
    routes,
    probs,
    w_gate,
    w_up,
    w_down,
    gate_left,
    gate_right,
    up_left,
    up_right,
    down_left,
    down_right,
):
    rows, width = tokens.shape
    exp_dev, _, cols = w_gate.shape
    rank = gate_left.shape[1]
    block = gate_left.shape[2]
    parts = lax.axis_size("mp")
    chips = lax.axis_size("y")
    experts = exp_dev * chips * 2
    me_g = lax.axis_index("y") * 2 + lax.axis_index("core")
    ranks = exp_dev * rank
    hid = exp_dev * cols

    def along_z(value, step):
        return lax.ppermute(value, "mp", [(i, (i + step) % parts) for i in range(parts)])

    def along_y(value, step):
        return lax.ppermute(value, "y", [(i, (i + step) % chips) for i in range(chips)])

    def other_core(value):
        return lax.ppermute(value, "core", [(0, 1), (1, 0)])

    pair = 2 * (-(-experts // 64) * 64)
    sent = attach(tokens, routes, probs, pair)
    arrived = [along_z(sent, k) for k in range(1, parts)]
    first = [along_y(sent, s) for s in range(1, chips)]
    rest = jnp.concatenate(arrived)
    lines = [jnp.concatenate([sent, rest])]
    partner = [other_core(lines[0])]
    for s in range(1, chips):
        lines.append(jnp.concatenate([first[s - 1], along_y(rest, s)]))
        partner.append(other_core(lines[s]))
    lines += partner

    small = cut((gate_right, up_right, down_left), parts)
    small = after(tuple(small), arrived[-1])
    small = [small[0]] + [along_z(small[k], k) for k in range(1, parts)]

    inner = inner_products(lines, gate_left, up_left, parts, rows)
    inner = [inner[0]] + [along_z(inner[k], k) for k in range(1, parts)]
    gate_w = jnp.swapaxes(w_gate, 1, 2).reshape(hid, width)
    up_w = jnp.swapaxes(w_up, 1, 2).reshape(hid, width)
    raw = raw_products(lines, gate_w, up_w)
    diag = spread(after(tuple(small), raw[0]), parts, exp_dev)
    first_expert = (me_g * exp_dev)[None]
    hidden, *bottom = hidden_units(
        first_expert, lines, inner, raw, diag, parts, rows, exp_dev, pair
    )
    bottom = [bottom[0]] + [along_z(bottom[k], k) for k in range(1, parts)]

    near, far = down_products(hidden, w_down.reshape(hid, width))
    out = (near + other_core(far).astype(F32)).reshape(chips, parts, rows, width)
    back = [along_y(out[s, 1:].astype(BF), -s) for s in range(1, chips)]

    bottom = after(tuple(bottom), out)
    near, far = extra_products(down_right.reshape(ranks, block), bottom)
    extra = (near + other_core(far).astype(F32)).reshape(chips, parts, rows, block)
    total = extra[0]
    for s in range(1, chips):
        total += along_y(extra[s].astype(BF), -s).astype(F32)

    own = [along_y(after(out[s, 0].astype(BF), back[s - 1]), -s) for s in range(1, chips)]
    back = sum(piece.astype(F32) for piece in back)
    result, *pieces = merge(out[0], back, total)
    for piece in own:
        result += piece.astype(F32)
    for k in range(1, parts):
        result += along_z(pieces[k - 1], -k).astype(F32)
    return result.astype(BF)


def solution(mesh):
    count = mesh.shape
    fine = jax.sharding.Mesh(
        mesh.devices.reshape(count["groups"], count["expert"] // 2, 2, count["mp"]),
        ("groups", "y", "core", "mp"),
    )
    expert = ("y", "core")
    return jax.shard_map(
        local,
        mesh=fine,
        in_specs=(
            P(("groups", "y", "core", "mp"), None),
            P(("groups", "y", "core", "mp"), None),
            P(("groups", "y", "core", "mp"), None),
            P(expert, None, "mp"),
            P(expert, None, "mp"),
            P(expert, "mp", None),
            P(expert, None, "mp"),
            P(expert, "mp", None),
            P(expert, None, "mp"),
            P(expert, "mp", None),
            P(expert, "mp", None),
            P(expert, None, "mp"),
        ),
        out_specs=P(("groups", "y", "core", "mp"), None),
        check_vma=False,
    )
```

time: 96.7 us -> 85.1 us (0.88)
  starting transfers between devices: 40.2 us -> 30.3 us
  Pallas kernels: 14.6 us -> 20.3 us
  waiting for transfers between devices: 24.1 us -> 20.2 us
  other arithmetic: 5.25 us -> 3.04 us
  local copies, waits for them, and re-layouts: 11.7 us -> 10.2 us
    ppermute x21 -> x15, starting transfers between devices: 34 us -> 22.6 us  [along_z(): lax.ppermute(value, 'mp', [(i, (i + step) % parts) for i in range(parts)])]
    ppermute x21 -> x15, waiting for transfers between devices: 20.8 us -> 11 us  [along_z(): lax.ppermute(value, 'mp', [(i, (i + step) % parts) for i in range(parts)])]
    ppermute x4 -> x5, waiting for transfers between devices: 3.27 us -> 9.14 us  [along_y(): lax.ppermute(value, 'y', [(i, (i + step) % chips) for i in range(chips)])]
    pallas_call x5 -> x7, Pallas kernels: 13.7 us -> 19.5 us  [the longest x1 8.52 us: raw_products(): pl.pallas_call(functools.partial(raw_kernel, len(lines)), grid=(hid // ti...]
    another operation x4 -> x0, local copies, waits for them, and re-layouts: 3.22 us -> none  [the longest x3 3.22 us: local(): diag = jnp.where(same, jnp.tile(small, (1, 1, exp_dev)), jnp.zeros((), BF))]
    ppermute x4 -> x5, starting transfers between devices: 5.44 us -> 7.5 us  [along_y(): lax.ppermute(value, 'y', [(i, (i + step) % chips) for i in range(chips)])]
    unnamed x33 -> x37, local copies, waits for them, and re-layouts: 8.16 us -> 10.1 us
    concatenate x2, other arithmetic: 2.73 us -> 0.92 us  [the longest x1 0.9 us: local(): lines = [jnp.concatenate([sent, rest])]]
  transfers between devices with their start and end apart: 31 -> 24, of which waited for: 13 -> 9; matrix products, arithmetic and copies ran while one was open for 10% -> 3% of each run, Pallas kernels for 11% -> 15%
where the time goes in v6:
time: 85.1 us; the launch traced here: 84.4 us
  starting transfers between devices  30.3 us (36%)
  Pallas kernels  20.3 us (24%)
  waiting for transfers between devices  20.2 us (24%)
  local copies, waits for them, and re-layouts  10.2 us (12%)
  other arithmetic  3.04 us (4%)
    ppermute x15, starting transfers between devices, along_z(): lax.ppermute(value, 'mp', [(i, (i + step) % parts) for i in range(parts)])  22.6 us
    ppermute x15, waiting for transfers between devices, along_z(): lax.ppermute(value, 'mp', [(i, (i + step) % parts) for i in range(parts)])  11 us
    unnamed x37, local copies, waits for them, and re-layouts  10.1 us
    ppermute x5, waiting for transfers between devices, along_y(): lax.ppermute(value, 'y', [(i, (i + step) % chips) for i in range(chips)])  9.14 us
    pallas_call x1, Pallas kernels, raw_products(): pl.pallas_call(functools.partial(raw_kernel, len(lines)), grid=(hid // ti...  8.52 us
    ppermute x5, starting transfers between devices, along_y(): lax.ppermute(value, 'y', [(i, (i + step) % chips) for i in range(chips)])  7.5 us
    pallas_call x1, Pallas kernels, down_products(): pl.pallas_call(down_kernel, grid=(width // tile,), in_specs=[pl.BlockSpec...  5.28 us
    pallas_call x1, Pallas kernels, spread(): pl.pallas_call(functools.partial(spread_kernel, parts, exp_dev), out_shap...  2.01 us
  transfers between devices with their start and end apart: 24, of which 9 were waited for; matrix products, arithmetic and copies ran while one was open for 3% of the time, Pallas kernels for 15%

profile of v6, /device:TPU:0, one launch (start us, length us, event | category | flops | bytes accessed | tf_op | source)
XLA Modules:
  0.0 84.4 jit_solution(5030450470268458827)
XLA Ops:
  0.0 1.6 %attach.1 = bf16[8,4224]{1,0:T(8,128)(2,1)} custom-call(bf16[8,4096]{1,0:T(8,128)(2,1)} %tokens_ref.1, s32[8,8]{1,0:T(8,128)} %routes_ref.1, f32[8,8]{1,0:T(8,128)} %probs_ref.1), custom_call_target="tpu_custom_call" | custom-call | tf_op jit(solution)/shard_map/attach/pallas_call | solution.py:56
  1.6 5.0 %collective-permute-start.2 = (bf16[8,4224]{1,0:T(8,128)(2,1)}, bf16[8,4224]{1,0:T(8,128)(2,1)S(1)}, u32[]{:S(2)}, u32[]{:S(2)}) collective-permute-start(bf16[8,4224]{1,0:T(8,128)(2,1)} %attach.1), channel_id=1, source_target_pairs={{0,3},{1,0},{2,1},{3,2},{4,7},{5,4},{6,5},{7,6},{8,11},{9,8},{10,9... | collective-permute-start | bytes 202760 | tf_op jit(solution)/shard_map/ppermute | solution.py:305
  6.6 1.0 %collective-permute-start = (bf16[8,4224]{1,0:T(8,128)(2,1)}, bf16[8,4224]{1,0:T(8,128)(2,1)S(1)}, u32[]{:S(2)}, u32[]{:S(2)}) collective-permute-start(bf16[8,4224]{1,0:T(8,128)(2,1)} %attach.1), channel_id=1, source_target_pairs={{0,1},{1,2},{2,3},{3,0},{4,5},{5,6},{6,7},{7,4},{8,9},{9,10},{10,1... | collective-permute-start | bytes 202760 | tf_op jit(solution)/shard_map/ppermute | solution.py:305
  7.6 1.5 %collective-permute-start.3 = (bf16[8,4224]{1,0:T(8,128)(2,1)}, bf16[8,4224]{1,0:T(8,128)(2,1)S(1)}, u32[]{:S(2)}, u32[]{:S(2)}) collective-permute-start(bf16[8,4224]{1,0:T(8,128)(2,1)} %attach.1), channel_id=1, source_target_pairs={{0,8},{8,0},{1,9},{9,1},{2,10},{10,2},{3,11},{11,3},{4,12},{12,4},... | collective-permute-start | bytes 202760 | tf_op jit(solution)/shard_map/ppermute | solution.py:308
  9.5 4.0 %collective-permute-done.1 = bf16[8,4224]{1,0:T(8,128)(2,1)S(1)} collective-permute-done((bf16[8,4224]{1,0:T(8,128)(2,1)}, bf16[8,4224]{1,0:T(8,128)(2,1)S(1)}, u32[]{:S(2)}, u32[]{:S(2)}) %collective-permute-start.1) | collective-permute-done | bytes 67616 | tf_op jit(solution)/shard_map/ppermute | solution.py:305
  13.5 1.6 %collective-permute-start.4 = (bf16[24,4224]{1,0:T(8,128)(2,1)S(1)}, bf16[24,4224]{1,0:T(8,128)(2,1)S(1)}, u32[]{:S(2)}, u32[]{:S(2)}) collective-permute-start(bf16[24,4224]{1,0:T(8,128)(2,1)S(1)} %pad_maximum_fusion.1), channel_id=1, source_target_pairs={{0,8},{8,0},{1,9},{9,1},{2,10},{10,2},{3,11},{11,3},{4,12},{12,4},... | collective-permute-start | bytes 608264 | tf_op jit(solution)/shard_map/ppermute | solution.py:308
  16.1 4.3 %collective-permute-done.4 = bf16[24,4224]{1,0:T(8,128)(2,1)S(1)} collective-permute-done((bf16[24,4224]{1,0:T(8,128)(2,1)S(1)}, bf16[24,4224]{1,0:T(8,128)(2,1)S(1)}, u32[]{:S(2)}, u32[]{:S(2)}) %collective-permute-start.4) | collective-permute-done | bytes 202784 | tf_op jit(solution)/shard_map/ppermute | solution.py:308
  20.5 1.8 %cut.1 = (bf16[3,32,192]{2,1,0:T(8,128)(2,1)}, bf16[3,32,192]{2,1,0:T(8,128)(2,1)}, bf16[3,32,192]{2,1,0:T(8,128)(2,1)}, bf16[3,32,192]{2,1,0:T(8,128)(2,1)}) custom-call(bf16[4,8,768]{2,1,0:T(8,128)(2,1)} %refs_0_.1, bf16[4,8,768]{2,1,0:T(8,128)(2,1)} %refs_1_.1, bf16[4,8,768]{2,1,0:T(8,128)(2,1)} %refs_2_.1), custom_call_target="tpu_custom_call" | custom-call | tf_op jit(solution)/shard_map/cut/pallas_call | solution.py:81
  22.4 1.0 %copy-done.11 = bf16[4,32,1024]{2,1,0:T(8,128)(2,1)S(1)} copy-done((bf16[4,32,1024]{2,1,0:T(8,128)(2,1)S(1)}, bf16[4,32,1024]{2,1,0:T(8,128)(2,1)}, u32[]{:S(2)}) %copy-start.11) | copy-done | bytes 262168
  24.7 1.9 %collective-permute-start.7 = (bf16[128,256]{1,0:T(8,128)(2,1)S(1)}, bf16[128,256]{1,0:T(8,128)(2,1)S(1)}, u32[]{:S(2)}, u32[]{:S(2)}) collective-permute-start(bf16[128,256]{1,0:T(8,128)(2,1)S(1)} %get-tuple-element.42), channel_id=1, source_target_pairs={{0,1},{1,2},{2,3},{3,0},{4,5},{5,6},{6,7},{7,4},{8,9},{9,10},{10,1... | collective-permute-start | bytes 196616 | tf_op jit(solution)/shard_map/ppermute | solution.py:305
  26.6 2.5 %collective-permute-start.8 = (bf16[128,256]{1,0:T(8,128)(2,1)S(1)}, bf16[128,256]{1,0:T(8,128)(2,1)S(1)}, u32[]{:S(2)}, u32[]{:S(2)}) collective-permute-start(bf16[128,256]{1,0:T(8,128)(2,1)S(1)} %get-tuple-element.43), channel_id=1, source_target_pairs={{0,2},{1,3},{2,0},{3,1},{4,6},{5,7},{6,4},{7,5},{8,10},{9,11},{10,... | collective-permute-start | bytes 196616 | tf_op jit(solution)/shard_map/ppermute | solution.py:305
  29.2 1.5 %collective-permute-start.11 = (bf16[3,32,192]{2,1,0:T(8,128)(2,1)}, bf16[3,32,192]{2,1,0:T(8,128)(2,1)S(1)}, u32[]{:S(2)}, u32[]{:S(2)}) collective-permute-start(bf16[3,32,192]{2,1,0:T(8,128)(2,1)} %get-tuple-element.53), channel_id=1, source_target_pairs={{0,2},{1,3},{2,0},{3,1},{4,6},{5,7},{6,4},{7,5},{8,10},{9,11},{10,... | collective-permute-start | bytes 110600 | tf_op jit(solution)/shard_map/ppermute | solution.py:305
  30.7 2.8 %collective-permute-start.12 = (bf16[3,32,192]{2,1,0:T(8,128)(2,1)}, bf16[3,32,192]{2,1,0:T(8,128)(2,1)S(1)}, u32[]{:S(2)}, u32[]{:S(2)}) collective-permute-start(bf16[3,32,192]{2,1,0:T(8,128)(2,1)} %get-tuple-element.54), channel_id=1, source_target_pairs={{0,3},{1,0},{2,1},{3,2},{4,7},{5,4},{6,5},{7,6},{8,11},{9,8},{10,9... | collective-permute-start | bytes 110600 | tf_op jit(solution)/shard_map/ppermute | solution.py:305
  33.6 8.5 %raw.1 = (f32[128,768]{1,0:T(8,128)}, f32[128,768]{1,0:T(8,128)}) custom-call(bf16[32,4224]{1,0:T(8,128)(2,1)} %copy-done, bf16[32,4224]{1,0:T(8,128)(2,1)} %copy-done.2, bf16[32,4224]{1,0:T(8,128)(2,1)} %copy-done.4, bf16[32,4224]{1,0:T(8,128)(2,1)} %copy-done.6, bf16[768,4096]{1,0:T(8,128)(2,1)} %bitcast.25, bf16[768,4096]{1,0:T(8,128)(2,1)} %bitcast.26), custom_call_target="tpu_custom_call" | custom-call | tf_op jit(solution)/shard_map/raw/pallas_call | solution.py:155
  42.7 2.0 %spread.1.refs_10_ = bf16[3,128,768]{2,1,0:T(8,128)(2,1)} custom-call(bf16[3,32,192]{2,1,0:T(8,128)(2,1)} %get-tuple-element.55.refs_0_, bf16[3,32,192]{2,1,0:T(8,128)(2,1)} %copy-done.15, bf16[3,32,192]{2,1,0:T(8,128)(2,1)} %copy-done.16, bf16[3,32,192]{2,1,0:T(8,128)(2,1)} %copy-done.17), custom_call_target="tpu_custom_call" | custom-call | tf_op jit(solution)/shard_map/spread/pallas_call | solution.py:111
  45.7 1.0 %copy-done.3 = bf16[32,4224]{1,0:T(8,128)(2,1)S(1)} copy-done((bf16[32,4224]{1,0:T(8,128)(2,1)S(1)}, bf16[32,4224]{1,0:T(8,128)(2,1)}, u32[]{:S(2)}) %copy-start.3) | copy-done | bytes 270360
  46.7 1.0 %copy-done.5 = bf16[32,4224]{1,0:T(8,128)(2,1)S(1)} copy-done((bf16[32,4224]{1,0:T(8,128)(2,1)S(1)}, bf16[32,4224]{1,0:T(8,128)(2,1)}, u32[]{:S(2)}) %copy-start.5) | copy-done | bytes 270360
  47.6 1.0 %copy-done.7 = bf16[32,4224]{1,0:T(8,128)(2,1)S(1)} copy-done((bf16[32,4224]{1,0:T(8,128)(2,1)S(1)}, bf16[32,4224]{1,0:T(8,128)(2,1)}, u32[]{:S(2)}) %copy-start.7) | copy-done | bytes 270360
  48.6 1.1 %copy-done.8 = bf16[3,128,768]{2,1,0:T(8,128)(2,1)S(1)} copy-done((bf16[3,128,768]{2,1,0:T(8,128)(2,1)S(1)}, bf16[3,128,768]{2,1,0:T(8,128)(2,1)}, u32[]{:S(2)}) %copy-start.8) | copy-done | bytes 589848
  49.6 1.0 %copy-done.9 = f32[128,768]{1,0:T(8,128)S(1)} copy-done((f32[128,768]{1,0:T(8,128)S(1)}, f32[128,768]{1,0:T(8,128)}, u32[]{:S(2)}) %copy-start.9) | copy-done | bytes 393240
  50.6 1.0 %copy-done.10 = f32[128,768]{1,0:T(8,128)S(1)} copy-done((f32[128,768]{1,0:T(8,128)S(1)}, f32[128,768]{1,0:T(8,128)}, u32[]{:S(2)}) %copy-start.10) | copy-done | bytes 393240
  52.8 5.3 %down.1 = (f32[64,4096]{1,0:T(8,128)}, bf16[64,4096]{1,0:T(8,128)(2,1)}) custom-call(bf16[128,768]{1,0:T(8,128)(2,1)} %copy-done.14, bf16[768,4096]{1,0:T(8,128)(2,1)} %bitcast.24), custom_call_target="tpu_custom_call" | custom-call | tf_op jit(solution)/shard_map/down/pallas_call | solution.py:214
  58.7 3.2 %collective-permute-start.17 = (bf16[128,128]{1,0:T(8,128)(2,1)S(1)}, bf16[128,128]{1,0:T(8,128)(2,1)S(1)}, u32[]{:S(2)}, u32[]{:S(2)}) collective-permute-start(bf16[128,128]{1,0:T(8,128)(2,1)S(1)} %get-tuple-element.65), channel_id=1, source_target_pairs={{0,3},{1,0},{2,1},{3,2},{4,7},{5,4},{6,5},{7,6},{8,11},{9,8},{10,9... | collective-permute-start | bytes 98312 | tf_op jit(solution)/shard_map/ppermute | solution.py:305
  61.9 1.3 %convert_add_fusion = f32[64,4096]{1,0:T(8,128)S(1)} fusion(f32[64,4096]{1,0:T(8,128)} %get-tuple-element.60, bf16[64,4096]{1,0:T(8,128)(2,1)S(1)} %collective-permute-done.13), kind=kLoop, calls=%fused_computation | loop fusion | flops 524288 | bytes 2621440 | tf_op jit(solution)/shard_map/add | solution.py:342
  64.7 1.6 %collective-permute-start.14 = (bf16[3,8,4096]{2,1,0:T(8,128)(2,1)S(1)}, bf16[3,8,4096]{2,1,0:T(8,128)(2,1)S(1)}, u32[]{:S(2)}, u32[]{:S(2)}) collective-permute-start(bf16[3,8,4096]{2,1,0:T(8,128)(2,1)S(1)} %slice_bitcast_fusion.1), channel_id=1, source_target_pairs={{0,8},{8,0},{1,9},{9,1},{2,10},{10,2},{3,11},{11,3},{4,12},{12,4},... | collective-permute-start | bytes 589832 | tf_op jit(solution)/shard_map/ppermute | solution.py:308
  66.4 1.3 %collective-permute-start.19 = (bf16[4,8,1024]{2,1,0:T(8,128)(2,1)S(1)}, bf16[4,8,1024]{2,1,0:T(8,128)(2,1)S(1)}, u32[]{:S(2)}, u32[]{:S(2)}) collective-permute-start(bf16[4,8,1024]{2,1,0:T(8,128)(2,1)S(1)} %fusion.1), channel_id=1, source_target_pairs={{0,8},{8,0},{1,9},{9,1},{2,10},{10,2},{3,11},{11,3},{4,12},{12,4},... | collective-permute-start | bytes 196616 | tf_op jit(solution)/shard_map/ppermute | solution.py:308
  67.7 4.8 %collective-permute-done.14 = bf16[3,8,4096]{2,1,0:T(8,128)(2,1)S(1)} collective-permute-done((bf16[3,8,4096]{2,1,0:T(8,128)(2,1)S(1)}, bf16[3,8,4096]{2,1,0:T(8,128)(2,1)S(1)}, u32[]{:S(2)}, u32[]{:S(2)}) %collective-permute-start.14) | collective-permute-done | bytes 196640 | tf_op jit(solution)/shard_map/ppermute | solution.py:308
  72.5 1.5 %collective-permute-start.20 = (bf16[8,4096]{1,0:T(8,128)(2,1)S(1)}, bf16[8,4096]{1,0:T(8,128)(2,1)S(1)}, u32[]{:S(2)}, u32[]{:S(2)}) collective-permute-start(bf16[8,4096]{1,0:T(8,128)(2,1)S(1)} %slice_bitcast_fusion.3), channel_id=1, source_target_pairs={{0,8},{8,0},{1,9},{9,1},{2,10},{10,2},{3,11},{11,3},{4,12},{12,4},... | collective-permute-start | bytes 196616 | tf_op jit(solution)/shard_map/ppermute | solution.py:308
  74.1 3.3 %collective-permute-start.21 = (bf16[8,4096]{1,0:T(8,128)(2,1)S(1)}, bf16[8,4096]{1,0:T(8,128)(2,1)S(1)}, u32[]{:S(2)}, u32[]{:S(2)}) collective-permute-start(bf16[8,4096]{1,0:T(8,128)(2,1)S(1)} %get-tuple-element.74), channel_id=1, source_target_pairs={{0,3},{1,0},{2,1},{3,2},{4,7},{5,4},{6,5},{7,6},{8,11},{9,8},{10,9... | collective-permute-start | bytes 196616 | tf_op jit(solution)/shard_map/ppermute | solution.py:305
  78.1 1.4 %collective-permute-done.21 = bf16[8,4096]{1,0:T(8,128)(2,1)S(1)} collective-permute-done((bf16[8,4096]{1,0:T(8,128)(2,1)S(1)}, bf16[8,4096]{1,0:T(8,128)(2,1)S(1)}, u32[]{:S(2)}, u32[]{:S(2)}) %collective-permute-start.21) | collective-permute-done | bytes 65568 | tf_op jit(solution)/shard_map/ppermute | solution.py:305
  79.5 3.2 %collective-permute-done.22 = bf16[8,4096]{1,0:T(8,128)(2,1)S(1)} collective-permute-done((bf16[8,4096]{1,0:T(8,128)(2,1)S(1)}, bf16[8,4096]{1,0:T(8,128)(2,1)S(1)}, u32[]{:S(2)}, u32[]{:S(2)}) %collective-permute-start.22) | collective-permute-done | bytes 65568 | tf_op jit(solution)/shard_map/ppermute | solution.py:305
  82.7 1.0 %collective-permute-done.23 = bf16[8,4096]{1,0:T(8,128)(2,1)S(1)} collective-permute-done((bf16[8,4096]{1,0:T(8,128)(2,1)S(1)}, bf16[8,4096]{1,0:T(8,128)(2,1)S(1)}, u32[]{:S(2)}, u32[]{:S(2)}) %collective-permute-start.23) | collective-permute-done | bytes 65568 | tf_op jit(solution)/shard_map/ppermute | solution.py:305
  (75 shorter events, 9.0 us)
Async XLA Ops:
  1.6 7.9 %collective-permute-start.2 = (bf16[8,4224]{1,0:T(8,128)(2,1)}, bf16[8,4224]{1,0:T(8,128)(2,1)S(1)}, u32[]{:S(2)}, u32[]{:S(2)}) collective-permute-start(bf16[8,4224]{1,0:T(8,128)(2,1)} %attach.1), channel_id=1, source_target_pairs={{0,3},{1,0},{2,1},{3,2},{4,7},{5,4},{6,5},{7,6},{8,11},{9,8},{10,9... | collective-permute-start | bytes 202760 | tf_op jit(solution)/shard_map/ppermute | solution.py:305
  6.6 6.9 %collective-permute-start.1 = (bf16[8,4224]{1,0:T(8,128)(2,1)}, bf16[8,4224]{1,0:T(8,128)(2,1)S(1)}, u32[]{:S(2)}, u32[]{:S(2)}) collective-permute-start(bf16[8,4224]{1,0:T(8,128)(2,1)} %attach.1), channel_id=1, source_target_pairs={{0,2},{1,3},{2,0},{3,1},{4,6},{5,7},{6,4},{7,5},{8,10},{9,11},{10,... | collective-permute-start | bytes 202760 | tf_op jit(solution)/shard_map/ppermute | solution.py:305
  6.6 6.9 %collective-permute-start = (bf16[8,4224]{1,0:T(8,128)(2,1)}, bf16[8,4224]{1,0:T(8,128)(2,1)S(1)}, u32[]{:S(2)}, u32[]{:S(2)}) collective-permute-start(bf16[8,4224]{1,0:T(8,128)(2,1)} %attach.1), channel_id=1, source_target_pairs={{0,1},{1,2},{2,3},{3,0},{4,5},{5,6},{6,7},{7,4},{8,9},{9,10},{10,1... | collective-permute-start | bytes 202760 | tf_op jit(solution)/shard_map/ppermute | solution.py:305
  7.6 8.4 %collective-permute-start.3 = (bf16[8,4224]{1,0:T(8,128)(2,1)}, bf16[8,4224]{1,0:T(8,128)(2,1)S(1)}, u32[]{:S(2)}, u32[]{:S(2)}) collective-permute-start(bf16[8,4224]{1,0:T(8,128)(2,1)} %attach.1), channel_id=1, source_target_pairs={{0,8},{8,0},{1,9},{9,1},{2,10},{10,2},{3,11},{11,3},{4,12},{12,4},... | collective-permute-start | bytes 202760 | tf_op jit(solution)/shard_map/ppermute | solution.py:308
  13.5 6.9 %collective-permute-start.4 = (bf16[24,4224]{1,0:T(8,128)(2,1)S(1)}, bf16[24,4224]{1,0:T(8,128)(2,1)S(1)}, u32[]{:S(2)}, u32[]{:S(2)}) collective-permute-start(bf16[24,4224]{1,0:T(8,128)(2,1)S(1)} %pad_maximum_fusion.1), channel_id=1, source_target_pairs={{0,8},{8,0},{1,9},{9,1},{2,10},{10,2},{3,11},{11,3},{4,12},{12,4},... | collective-permute-start | bytes 608264 | tf_op jit(solution)/shard_map/ppermute | solution.py:308
  16.0 17.5 %copy-start = (bf16[32,4224]{1,0:T(8,128)(2,1)}, bf16[32,4224]{1,0:T(8,128)(2,1)S(1)}, u32[]{:S(2)}) copy-start(bf16[32,4224]{1,0:T(8,128)(2,1)S(1)} %pad_maximum_fusion.refs_0_) | copy-start | bytes 811012
  16.0 6.4 %collective-permute-start.5 = (bf16[32,4224]{1,0:T(8,128)(2,1)S(1)}, bf16[32,4224]{1,0:T(8,128)(2,1)S(1)}, u32[]{:S(2)}, u32[]{:S(2)}) collective-permute-start(bf16[32,4224]{1,0:T(8,128)(2,1)S(1)} %pad_maximum_fusion.refs_0_), channel_id=1, source_target_pairs={{0,4},{4,0},{1,5},{5,1},{2,6},{6,2},{3,7},{7,3},{8,12},{12,8},{9,1... | collective-permute-start | bytes 811016 | tf_op jit(solution)/shard_map/ppermute | solution.py:311
  20.4 13.1 %copy-start.2 = (bf16[32,4224]{1,0:T(8,128)(2,1)}, bf16[32,4224]{1,0:T(8,128)(2,1)S(1)}, u32[]{:S(2)}) copy-start(bf16[32,4224]{1,0:T(8,128)(2,1)S(1)} %constant_dynamic-update-slice_fusion.refs_1_) | copy-start | bytes 811012
  20.5 1.9 %collective-permute-start.6 = (bf16[32,4224]{1,0:T(8,128)(2,1)S(1)}, bf16[32,4224]{1,0:T(8,128)(2,1)S(1)}, u32[]{:S(2)}, u32[]{:S(2)}) collective-permute-start(bf16[32,4224]{1,0:T(8,128)(2,1)S(1)} %constant_dynamic-update-slice_fusion.refs_1_), channel_id=1, source_target_pairs={{0,4},{4,0},{1,5},{5,1},{2,6},{6,2},{3,7},{7,3},{8,12},{12,8},{9,1... | collective-permute-start | bytes 811016 | tf_op jit(solution)/shard_map/ppermute | solution.py:311
  22.4 8.3 %collective-permute-start.10 = (bf16[3,32,192]{2,1,0:T(8,128)(2,1)}, bf16[3,32,192]{2,1,0:T(8,128)(2,1)S(1)}, u32[]{:S(2)}, u32[]{:S(2)}) collective-permute-start(bf16[3,32,192]{2,1,0:T(8,128)(2,1)} %get-tuple-element.52), channel_id=1, source_target_pairs={{0,1},{1,2},{2,3},{3,0},{4,5},{5,6},{6,7},{7,4},{8,9},{9,10},{10,1... | collective-permute-start | bytes 110600 | tf_op jit(solution)/shard_map/ppermute | solution.py:305
  22.4 11.2 %copy-start.4 = (bf16[32,4224]{1,0:T(8,128)(2,1)}, bf16[32,4224]{1,0:T(8,128)(2,1)S(1)}, u32[]{:S(2)}) copy-start(bf16[32,4224]{1,0:T(8,128)(2,1)S(1)} %collective-permute-done.5.refs_2_) | copy-start | bytes 811012
  22.4 1.1 %copy-start.11 = (bf16[4,32,1024]{2,1,0:T(8,128)(2,1)S(1)}, bf16[4,32,1024]{2,1,0:T(8,128)(2,1)}, u32[]{:S(2)}) copy-start(bf16[4,32,1024]{2,1,0:T(8,128)(2,1)} %refs_4_.1) | copy-start | bytes 786436
  24.4 9.1 %copy-start.6 = (bf16[32,4224]{1,0:T(8,128)(2,1)}, bf16[32,4224]{1,0:T(8,128)(2,1)S(1)}, u32[]{:S(2)}) copy-start(bf16[32,4224]{1,0:T(8,128)(2,1)S(1)} %collective-permute-done.6.refs_3_) | copy-start | bytes 811012
  24.7 20.0 %collective-permute-start.7 = (bf16[128,256]{1,0:T(8,128)(2,1)S(1)}, bf16[128,256]{1,0:T(8,128)(2,1)S(1)}, u32[]{:S(2)}, u32[]{:S(2)}) collective-permute-start(bf16[128,256]{1,0:T(8,128)(2,1)S(1)} %get-tuple-element.42), channel_id=1, source_target_pairs={{0,1},{1,2},{2,3},{3,0},{4,5},{5,6},{6,7},{7,4},{8,9},{9,10},{10,1... | collective-permute-start | bytes 196616 | tf_op jit(solution)/shard_map/ppermute | solution.py:305
  26.6 18.1 %collective-permute-start.8 = (bf16[128,256]{1,0:T(8,128)(2,1)S(1)}, bf16[128,256]{1,0:T(8,128)(2,1)S(1)}, u32[]{:S(2)}, u32[]{:S(2)}) collective-permute-start(bf16[128,256]{1,0:T(8,128)(2,1)S(1)} %get-tuple-element.43), channel_id=1, source_target_pairs={{0,2},{1,3},{2,0},{3,1},{4,6},{5,7},{6,4},{7,5},{8,10},{9,11},{10,... | collective-permute-start | bytes 196616 | tf_op jit(solution)/shard_map/ppermute | solution.py:305
  29.2 15.6 %collective-permute-start.9 = (bf16[128,256]{1,0:T(8,128)(2,1)S(1)}, bf16[128,256]{1,0:T(8,128)(2,1)S(1)}, u32[]{:S(2)}, u32[]{:S(2)}) collective-permute-start(bf16[128,256]{1,0:T(8,128)(2,1)S(1)} %get-tuple-element.44), channel_id=1, source_target_pairs={{0,3},{1,0},{2,1},{3,2},{4,7},{5,4},{6,5},{7,6},{8,11},{9,8},{10,9... | collective-permute-start | bytes 196616 | tf_op jit(solution)/shard_map/ppermute | solution.py:305
  29.2 12.9 %collective-permute-start.11 = (bf16[3,32,192]{2,1,0:T(8,128)(2,1)}, bf16[3,32,192]{2,1,0:T(8,128)(2,1)S(1)}, u32[]{:S(2)}, u32[]{:S(2)}) collective-permute-start(bf16[3,32,192]{2,1,0:T(8,128)(2,1)} %get-tuple-element.53), channel_id=1, source_target_pairs={{0,2},{1,3},{2,0},{3,1},{4,6},{5,7},{6,4},{7,5},{8,10},{9,11},{10,... | collective-permute-start | bytes 110600 | tf_op jit(solution)/shard_map/ppermute | solution.py:305
  30.7 11.4 %copy-start.15 = (bf16[3,32,192]{2,1,0:T(8,128)(2,1)}, bf16[3,32,192]{2,1,0:T(8,128)(2,1)S(1)}, u32[]{:S(2)}) copy-start(bf16[3,32,192]{2,1,0:T(8,128)(2,1)S(1)} %collective-permute-done.10.refs_1_) | copy-start | bytes 110596
  30.7 11.4 %collective-permute-start.12 = (bf16[3,32,192]{2,1,0:T(8,128)(2,1)}, bf16[3,32,192]{2,1,0:T(8,128)(2,1)S(1)}, u32[]{:S(2)}, u32[]{:S(2)}) collective-permute-start(bf16[3,32,192]{2,1,0:T(8,128)(2,1)} %get-tuple-element.54), channel_id=1, source_target_pairs={{0,3},{1,0},{2,1},{3,2},{4,7},{5,4},{6,5},{7,6},{8,11},{9,8},{10,9... | collective-permute-start | bytes 110600 | tf_op jit(solution)/shard_map/ppermute | solution.py:305
  48.6 1.1 %copy-start.8 = (bf16[3,128,768]{2,1,0:T(8,128)(2,1)S(1)}, bf16[3,128,768]{2,1,0:T(8,128)(2,1)}, u32[]{:S(2)}) copy-start(bf16[3,128,768]{2,1,0:T(8,128)(2,1)} %spread.1.refs_10_) | copy-start | bytes 1769476
  52.8 11.6 %copy-start.13 = (bf16[4,32,1024]{2,1,0:T(8,128)(2,1)S(1)}, bf16[4,32,1024]{2,1,0:T(8,128)(2,1)}, u32[]{:S(2)}) copy-start(bf16[4,32,1024]{2,1,0:T(8,128)(2,1)} %param.23) | copy-start | bytes 786436
  58.1 3.8 %collective-permute-start.13 = (bf16[64,4096]{1,0:T(8,128)(2,1)}, bf16[64,4096]{1,0:T(8,128)(2,1)S(1)}, u32[]{:S(2)}, u32[]{:S(2)}) collective-permute-start(bf16[64,4096]{1,0:T(8,128)(2,1)} %get-tuple-element.61), channel_id=1, source_target_pairs={{0,4},{4,0},{1,5},{5,1},{2,6},{6,2},{3,7},{7,3},{8,12},{12,8},{9,1... | collective-permute-start | bytes 1572872 | tf_op jit(solution)/shard_map/ppermute | solution.py:311
  58.1 6.0 %collective-permute-start.15 = (bf16[128,128]{1,0:T(8,128)(2,1)S(1)}, bf16[128,128]{1,0:T(8,128)(2,1)S(1)}, u32[]{:S(2)}, u32[]{:S(2)}) collective-permute-start(bf16[128,128]{1,0:T(8,128)(2,1)S(1)} %get-tuple-element.63), channel_id=1, source_target_pairs={{0,1},{1,2},{2,3},{3,0},{4,5},{5,6},{6,7},{7,4},{8,9},{9,10},{10,1... | collective-permute-start | bytes 98312 | tf_op jit(solution)/shard_map/ppermute | solution.py:305
  58.1 6.0 %collective-permute-start.16 = (bf16[128,128]{1,0:T(8,128)(2,1)S(1)}, bf16[128,128]{1,0:T(8,128)(2,1)S(1)}, u32[]{:S(2)}, u32[]{:S(2)}) collective-permute-start(bf16[128,128]{1,0:T(8,128)(2,1)S(1)} %get-tuple-element.64), channel_id=1, source_target_pairs={{0,2},{1,3},{2,0},{3,1},{4,6},{5,7},{6,4},{7,5},{8,10},{9,11},{10,... | collective-permute-start | bytes 98312 | tf_op jit(solution)/shard_map/ppermute | solution.py:305
  58.7 5.7 %collective-permute-start.17 = (bf16[128,128]{1,0:T(8,128)(2,1)S(1)}, bf16[128,128]{1,0:T(8,128)(2,1)S(1)}, u32[]{:S(2)}, u32[]{:S(2)}) collective-permute-start(bf16[128,128]{1,0:T(8,128)(2,1)S(1)} %get-tuple-element.65), channel_id=1, source_target_pairs={{0,3},{1,0},{2,1},{3,2},{4,7},{5,4},{6,5},{7,6},{8,11},{9,8},{10,9... | collective-permute-start | bytes 98312 | tf_op jit(solution)/shard_map/ppermute | solution.py:305
  64.6 1.7 %collective-permute-start.18 = (bf16[64,1024]{1,0:T(8,128)(2,1)S(1)}, bf16[64,1024]{1,0:T(8,128)(2,1)S(1)}, u32[]{:S(2)}, u32[]{:S(2)}) collective-permute-start(bf16[64,1024]{1,0:T(8,128)(2,1)S(1)} %get-tuple-element.71), channel_id=1, source_target_pairs={{0,4},{4,0},{1,5},{5,1},{2,6},{6,2},{3,7},{7,3},{8,12},{12,8},{9,1... | collective-permute-start | bytes 393224 | tf_op jit(solution)/shard_map/ppermute | solution.py:311
  64.7 7.8 %collective-permute-start.14 = (bf16[3,8,4096]{2,1,0:T(8,128)(2,1)S(1)}, bf16[3,8,4096]{2,1,0:T(8,128)(2,1)S(1)}, u32[]{:S(2)}, u32[]{:S(2)}) collective-permute-start(bf16[3,8,4096]{2,1,0:T(8,128)(2,1)S(1)} %slice_bitcast_fusion.1), channel_id=1, source_target_pairs={{0,8},{8,0},{1,9},{9,1},{2,10},{10,2},{3,11},{11,3},{4,12},{12,4},... | collective-permute-start | bytes 589832 | tf_op jit(solution)/shard_map/ppermute | solution.py:308
  66.4 7.7 %collective-permute-start.19 = (bf16[4,8,1024]{2,1,0:T(8,128)(2,1)S(1)}, bf16[4,8,1024]{2,1,0:T(8,128)(2,1)S(1)}, u32[]{:S(2)}, u32[]{:S(2)}) collective-permute-start(bf16[4,8,1024]{2,1,0:T(8,128)(2,1)S(1)} %fusion.1), channel_id=1, source_target_pairs={{0,8},{8,0},{1,9},{9,1},{2,10},{10,2},{3,11},{11,3},{4,12},{12,4},... | collective-permute-start | bytes 196616 | tf_op jit(solution)/shard_map/ppermute | solution.py:308
  72.5 5.6 %collective-permute-start.20 = (bf16[8,4096]{1,0:T(8,128)(2,1)S(1)}, bf16[8,4096]{1,0:T(8,128)(2,1)S(1)}, u32[]{:S(2)}, u32[]{:S(2)}) collective-permute-start(bf16[8,4096]{1,0:T(8,128)(2,1)S(1)} %slice_bitcast_fusion.3), channel_id=1, source_target_pairs={{0,8},{8,0},{1,9},{9,1},{2,10},{10,2},{3,11},{11,3},{4,12},{12,4},... | collective-permute-start | bytes 196616 | tf_op jit(solution)/shard_map/ppermute | solution.py:308
  74.1 5.4 %collective-permute-start.21 = (bf16[8,4096]{1,0:T(8,128)(2,1)S(1)}, bf16[8,4096]{1,0:T(8,128)(2,1)S(1)}, u32[]{:S(2)}, u32[]{:S(2)}) collective-permute-start(bf16[8,4096]{1,0:T(8,128)(2,1)S(1)} %get-tuple-element.74), channel_id=1, source_target_pairs={{0,3},{1,0},{2,1},{3,2},{4,7},{5,4},{6,5},{7,6},{8,11},{9,8},{10,9... | collective-permute-start | bytes 196616 | tf_op jit(solution)/shard_map/ppermute | solution.py:305
  77.4 5.3 %collective-permute-start.22 = (bf16[8,4096]{1,0:T(8,128)(2,1)S(1)}, bf16[8,4096]{1,0:T(8,128)(2,1)S(1)}, u32[]{:S(2)}, u32[]{:S(2)}) collective-permute-start(bf16[8,4096]{1,0:T(8,128)(2,1)S(1)} %get-tuple-element.75), channel_id=1, source_target_pairs={{0,2},{1,3},{2,0},{3,1},{4,6},{5,7},{6,4},{7,5},{8,10},{9,11},{10,... | collective-permute-start | bytes 196616 | tf_op jit(solution)/shard_map/ppermute | solution.py:305
  77.6 6.1 %collective-permute-start.23 = (bf16[8,4096]{1,0:T(8,128)(2,1)S(1)}, bf16[8,4096]{1,0:T(8,128)(2,1)S(1)}, u32[]{:S(2)}, u32[]{:S(2)}) collective-permute-start(bf16[8,4096]{1,0:T(8,128)(2,1)S(1)} %get-tuple-element.76), channel_id=1, source_target_pairs={{0,1},{1,2},{2,3},{3,0},{4,5},{5,6},{6,7},{7,4},{8,9},{9,10},{10,1... | collective-permute-start | bytes 196616 | tf_op jit(solution)/shard_map/ppermute | solution.py:305
  (10 other events, 8.6 us)

commit v7 on v6

--- a/solution.py
+++ b/solution.py
@@ -9,8 +9,9 @@
 
 BF = jnp.bfloat16
 F32 = jnp.float32
-VMEM_LIMIT = 24 * 1024 * 1024
-STREAM_LIMIT = 56 * 1024 * 1024
+PIECES = 4
+VMEM_LIMIT = 16 * 1024 * 1024
+BRIEF = pl.CostEstimate(flops=1, bytes_accessed=1, transcendentals=0)
 
 
 def dot_nt(a, b):
@@ -19,6 +20,10 @@
 
 def dot_nn(a, b):
     return lax.dot_general(a, b, (((1,), (0,)), ((), ())), preferred_element_type=F32)
+
+
+def in_hbm(*values):
+    return [pltpu.with_memory_space_constraint(v, pltpu.HBM) for v in values]
 
 
 def after(value, earlier):
@@ -56,8 +61,9 @@
     return pl.pallas_call(
         attach_kernel,
         out_shape=jax.ShapeDtypeStruct((rows, width + pair), BF),
+        cost_estimate=BRIEF,
         name="attach",
-    )(tokens, routes, probs)
+    )(*in_hbm(tokens, routes, probs))
 
 
 def cut_kernel(parts, *refs):
@@ -81,8 +87,9 @@
     return pl.pallas_call(
         functools.partial(cut_kernel, parts),
         out_shape=[jax.ShapeDtypeStruct((3, exp_dev * piece, hid // parts), BF)] * parts,
+        cost_estimate=BRIEF,
         name="cut",
-    )(*factors)
+    )(*in_hbm(*factors))
 
 
 def spread_kernel(parts, exp_dev, *refs):
@@ -111,6 +118,7 @@
     return pl.pallas_call(
         functools.partial(spread_kernel, parts, exp_dev),
         out_shape=jax.ShapeDtypeStruct((3, span * parts, cols * exp_dev), BF),
+        cost_estimate=BRIEF,
         name="spread",
     )(*pieces)
 
@@ -135,30 +143,62 @@
         functools.partial(inner_kernel, parts, rows, len(lines)),
         out_shape=[jax.ShapeDtypeStruct((total, ranks), BF)] * parts,
         compiler_params=pltpu.CompilerParams(vmem_limit_bytes=VMEM_LIMIT),
+        cost_estimate=BRIEF,
         name="inner",
     )(*lines, gate_left, up_left)
 
 
+def load_kernel(count, *refs):
+    sources, targets, sems = refs[:count], refs[count:-1], refs[-1]
+    copies = []
+    for n in range(count):
+        step = sources[n].shape[0] // PIECES
+        for i in range(PIECES):
+            span = pl.ds(i * step, step)
+            copies.append(
+                pltpu.make_async_copy(
+                    sources[n].at[span], targets[n].at[span], sems.at[n * PIECES + i]
+                )
+            )
+    for copy in copies:
+        copy.start()
+    for copy in copies:
+        copy.wait()
+
+
+def load(*weights):
+    count = len(weights)
+    return pl.pallas_call(
+        functools.partial(load_kernel, count),
+        in_specs=[pl.BlockSpec(memory_space=pltpu.HBM)] * count,
+        out_specs=[pl.BlockSpec(memory_space=pltpu.VMEM)] * count,
+        out_shape=[pltpu.VMEM(w.shape, w.dtype) for w in weights],
+        scratch_shapes=[pltpu.SemaphoreType.DMA((count * PIECES,))],
+        compiler_params=pltpu.CompilerParams(vmem_limit_bytes=VMEM_LIMIT),
+        cost_estimate=BRIEF,
+        name="load",
+    )(*in_hbm(*weights))
+
+
 def raw_kernel(count, *refs):
     lines, (gate_w, up_w, gate_ref, up_ref) = refs[:count], refs[count:]
-    x = jnp.concatenate([line[:, : gate_w.shape[1]] for line in lines])
-    gate_ref[...] = dot_nt(x, gate_w[...])
-    up_ref[...] = dot_nt(x, up_w[...])
+    hid, width = gate_w.shape
+    x = jnp.concatenate([line[:, :width] for line in lines])
+    tile = hid // 3 if hid % 384 == 0 else hid
+    for i in range(hid // tile):
+        span = slice(i * tile, (i + 1) * tile)
+        gate_ref[:, span] = dot_nt(x, gate_w[span])
+        up_ref[:, span] = dot_nt(x, up_w[span])
 
 
 def raw_products(lines, gate_w, up_w):
-    hid, width = gate_w.shape
+    hid = gate_w.shape[0]
     total = sum(line.shape[0] for line in lines)
-    tile = hid // 3 if hid % 384 == 0 else hid
-    weights = pl.BlockSpec((tile, width), lambda i: (i, 0))
-    result = pl.BlockSpec((total, tile), lambda i: (0, i))
     return pl.pallas_call(
         functools.partial(raw_kernel, len(lines)),
-        grid=(hid // tile,),
-        in_specs=[pl.BlockSpec(line.shape, lambda i: (0, 0)) for line in lines] + [weights] * 2,
-        out_specs=[result] * 2,
         out_shape=[jax.ShapeDtypeStruct((total, hid), F32)] * 2,
-        compiler_params=pltpu.CompilerParams(vmem_limit_bytes=STREAM_LIMIT),
+        compiler_params=pltpu.CompilerParams(vmem_limit_bytes=VMEM_LIMIT),
+        cost_estimate=BRIEF,
         name="raw",
     )(*lines, gate_w, up_w)
 
@@ -196,34 +236,32 @@
         out_shape=[jax.ShapeDtypeStruct((total, hid), BF)]
         + [jax.ShapeDtypeStruct((total, ranks), BF)] * parts,
         compiler_params=pltpu.CompilerParams(vmem_limit_bytes=VMEM_LIMIT),
+        cost_estimate=BRIEF,
         name="hidden",
     )(place, *lines, *inner, *raw, diag)
 
 
 def down_kernel(hidden_ref, down_ref, near_ref, far_ref):
-    near = near_ref.shape[0]
-    value = dot_nn(hidden_ref[...], down_ref[...])
-    near_ref[...] = value[:near]
-    far_ref[...] = value[near:].astype(BF)
+    near, width = near_ref.shape
+    hidden = hidden_ref[...]
+    tile = min(1024, width)
+    for i in range(width // tile):
+        span = slice(i * tile, (i + 1) * tile)
+        value = dot_nn(hidden, down_ref[:, span])
+        near_ref[:, span] = value[:near]
+        far_ref[:, span] = value[near:].astype(BF)
 
 
 def down_products(hidden, down_w):
-    total, hid = hidden.shape
-    width = down_w.shape[1]
-    tile = 1024
+    total, width = hidden.shape[0], down_w.shape[1]
     return pl.pallas_call(
         down_kernel,
-        grid=(width // tile,),
-        in_specs=[
-            pl.BlockSpec((total, hid), lambda i: (0, 0)),
-            pl.BlockSpec((hid, tile), lambda i: (0, i)),
-        ],
-        out_specs=[pl.BlockSpec((total // 2, tile), lambda i: (0, i))] * 2,
         out_shape=[
             jax.ShapeDtypeStruct((total // 2, width), F32),
             jax.ShapeDtypeStruct((total // 2, width), BF),
         ],
-        compiler_params=pltpu.CompilerParams(vmem_limit_bytes=STREAM_LIMIT),
+        compiler_params=pltpu.CompilerParams(vmem_limit_bytes=VMEM_LIMIT),
+        cost_estimate=BRIEF,
         name="down",
     )(hidden, down_w)
 
@@ -247,33 +285,71 @@
             jax.ShapeDtypeStruct((total // 2, block), BF),
         ],
         compiler_params=pltpu.CompilerParams(vmem_limit_bytes=VMEM_LIMIT),
+        cost_estimate=BRIEF,
         name="extra",
     )(right, *bottom)
 
 
-def merge_kernel(own_ref, back_ref, extra_ref, *out_refs):
-    block = extra_ref.shape[2]
+def fold_kernel(head, near_ref, far_ref, own_ref, *out_refs):
+    span = own_ref.shape[0]
+    total = near_ref[...] + far_ref[...].astype(F32)
+    own_ref[...] = total[:span]
+    per = 2 if head else 1
+    for n in range(len(out_refs) // per):
+        line = total[(n + 1) * span : (n + 2) * span]
+        if head:
+            out_refs[2 * n][...] = line[:head].astype(BF)
+            out_refs[2 * n + 1][...] = line[head:].astype(BF)
+        else:
+            out_refs[n][...] = line.astype(BF)
+
+
+def fold(near, far, chips, head):
+    total, width = near.shape
+    span = total // chips
+    cuts = [head, span - head] if head else [span]
+    return pl.pallas_call(
+        functools.partial(fold_kernel, head),
+        out_shape=[jax.ShapeDtypeStruct((span, width), F32)]
+        + [jax.ShapeDtypeStruct((rows, width), BF) for rows in cuts] * (chips - 1),
+        compiler_params=pltpu.CompilerParams(vmem_limit_bytes=VMEM_LIMIT),
+        cost_estimate=BRIEF,
+        name="fold",
+    )(near, far)
+
+
+def merge_kernel(count, own_ref, low_ref, *refs):
+    backs, lows, outs = refs[:count], refs[count : 2 * count], refs[2 * count :]
+    rows = outs[0].shape[0]
+    block = low_ref.shape[1]
     offset = pl.multiple_of(lax.axis_index("mp") * block, 128)
-    for k, out_ref in enumerate(out_refs):
-        total = own_ref[k]
-        if k > 0:
-            total += back_ref[k - 1]
-        out_ref[...] = total.astype(out_ref.dtype)
-        low = own_ref[k, :, pl.ds(offset, block)] + extra_ref[k]
-        if k > 0:
-            low += back_ref[k - 1, :, pl.ds(offset, block)]
-        out_ref[:, pl.ds(offset, block)] = low.astype(out_ref.dtype)
-
-
-def merge(own, back, extra):
-    parts, rows, width = own.shape
-    return pl.pallas_call(
-        merge_kernel,
+    low = low_ref[...]
+    for ref in lows:
+        low += ref[...].astype(F32)
+    total = own_ref[rows:]
+    part = own_ref[:, pl.ds(offset, block)] + low
+    after_own = part[rows:]
+    for ref in backs:
+        total += ref[...].astype(F32)
+        after_own += ref[:, pl.ds(offset, block)].astype(F32)
+    outs[0][...] = own_ref[:rows]
+    outs[0][:, pl.ds(offset, block)] = part[:rows]
+    for k in range(1, len(outs)):
+        span = slice((k - 1) * rows, k * rows)
+        outs[k][...] = total[span].astype(BF)
+        outs[k][:, pl.ds(offset, block)] = after_own[span].astype(BF)
+
+
+def merge(own, low, backs, lows, rows):
+    total, width = own.shape
+    return pl.pallas_call(
+        functools.partial(merge_kernel, len(backs)),
         out_shape=[jax.ShapeDtypeStruct((rows, width), F32)]
-        + [jax.ShapeDtypeStruct((rows, width), BF)] * (parts - 1),
-        compiler_params=pltpu.CompilerParams(vmem_limit_bytes=VMEM_LIMIT),
+        + [jax.ShapeDtypeStruct((rows, width), BF)] * (total // rows - 1),
+        compiler_params=pltpu.CompilerParams(vmem_limit_bytes=VMEM_LIMIT),
+        cost_estimate=BRIEF,
         name="merge",
-    )(own, back, extra)
+    )(own, low, *backs, *lows)
 
 
 def local(
@@ -314,45 +390,47 @@
     sent = attach(tokens, routes, probs, pair)
     arrived = [along_z(sent, k) for k in range(1, parts)]
     first = [along_y(sent, s) for s in range(1, chips)]
-    rest = jnp.concatenate(arrived)
+    gate_w = jnp.swapaxes(w_gate, 1, 2).reshape(hid, width)
+    up_w = jnp.swapaxes(w_up, 1, 2).reshape(hid, width)
+    gate_w, up_w, gate_left, up_left = load(
+        *after((gate_w, up_w, gate_left, up_left), first)
+    )
+    small = cut((gate_right, up_right, down_left), parts)
+    rest = after(jnp.concatenate(arrived), (gate_w, up_w, small))
     lines = [jnp.concatenate([sent, rest])]
     partner = [other_core(lines[0])]
+    down_w, right = load(*after((w_down.reshape(hid, width), down_right), rest))
+    small = after(tuple(small), rest)
+    small = [small[0]] + [along_z(small[k], k) for k in range(1, parts)]
     for s in range(1, chips):
-        lines.append(jnp.concatenate([first[s - 1], along_y(rest, s)]))
-        partner.append(other_core(lines[s]))
+        line = jnp.concatenate([first[s - 1], along_y(rest, s)])
+        line = after(line, (down_w, tuple(small)))
+        lines.append(line)
+        partner.append(other_core(line))
     lines += partner
-
-    small = cut((gate_right, up_right, down_left), parts)
-    small = after(tuple(small), arrived[-1])
-    small = [small[0]] + [along_z(small[k], k) for k in range(1, parts)]
+    diag = spread(small, parts, exp_dev)
 
     inner = inner_products(lines, gate_left, up_left, parts, rows)
     inner = [inner[0]] + [along_z(inner[k], k) for k in range(1, parts)]
-    gate_w = jnp.swapaxes(w_gate, 1, 2).reshape(hid, width)
-    up_w = jnp.swapaxes(w_up, 1, 2).reshape(hid, width)
     raw = raw_products(lines, gate_w, up_w)
-    diag = spread(after(tuple(small), raw[0]), parts, exp_dev)
     first_expert = (me_g * exp_dev)[None]
     hidden, *bottom = hidden_units(
         first_expert, lines, inner, raw, diag, parts, rows, exp_dev, pair
     )
     bottom = [bottom[0]] + [along_z(bottom[k], k) for k in range(1, parts)]
 
-    near, far = down_products(hidden, w_down.reshape(hid, width))
-    out = (near + other_core(far).astype(F32)).reshape(chips, parts, rows, width)
-    back = [along_y(out[s, 1:].astype(BF), -s) for s in range(1, chips)]
+    near, far = down_products(hidden, down_w)
+    out, *others = fold(near, other_core(far), chips, rows)
+    backs = [along_y(others[2 * s - 1], -s) for s in range(1, chips)]
 
     bottom = after(tuple(bottom), out)
-    near, far = extra_products(down_right.reshape(ranks, block), bottom)
-    extra = (near + other_core(far).astype(F32)).reshape(chips, parts, rows, block)
-    total = extra[0]
-    for s in range(1, chips):
-        total += along_y(extra[s].astype(BF), -s).astype(F32)
-
-    own = [along_y(after(out[s, 0].astype(BF), back[s - 1]), -s) for s in range(1, chips)]
-    back = sum(piece.astype(F32) for piece in back)
-    result, *pieces = merge(out[0], back, total)
-    for piece in own:
+    near, far = extra_products(right.reshape(ranks, block), bottom)
+    low, *lows = fold(near, other_core(far), chips, 0)
+    lows = [along_y(lows[s - 1], -s) for s in range(1, chips)]
+
+    heads = [along_y(after(others[2 * s - 2], backs[s - 1]), -s) for s in range(1, chips)]
+    result, *pieces = merge(out, low, backs, lows, rows)
+    for piece in heads:
         result += piece.astype(F32)
     for k in range(1, parts):
         result += along_z(pieces[k - 1], -k).astype(F32)

time: 85.1 us -> 80.4 us (0.945)
  waiting for transfers between devices: 20.2 us -> 11.9 us
  local copies, waits for them, and re-layouts: 10.2 us -> 14.1 us
  other arithmetic: 3.04 us -> 0.73 us
  starting transfers between devices: 30.3 us -> 31.7 us
  Pallas kernels: 20.3 us -> 21.3 us
    ppermute x15, waiting for transfers between devices: 11 us -> 4.94 us  [along_z(): lax.ppermute(value, 'mp', [(i, (i + step) % parts) for i in range(parts)])]
    unnamed x37 -> x30, local copies, waits for them, and re-layouts: 10.1 us -> 14.1 us
    ppermute x5, waiting for transfers between devices: 9.14 us -> 5.78 us  [along_y(): lax.ppermute(value, 'y', [(i, (i + step) % chips) for i in range(chips)])]
    add x3 -> x0, other arithmetic: 1.37 us -> none  [the longest x2 1.35 us: local(): near + other_core(far).astype(F32)]
    ppermute x4, waiting for transfers between devices: 0.01 us -> 1.18 us  [other_core(): return lax.ppermute(value, 'core', [(0, 1), (1, 0)])]
    pallas_call x1, Pallas kernels: 0.51 us -> 1.42 us  [hidden_units(): pl.pallas_call(functools.partial(hidden_kernel, parts, rows, len(lines),...]
    concatenate x1, other arithmetic: 0.9 us -> 0.02 us  [local(): lines = [jnp.concatenate([sent, rest])]]
    pallas_call x3 -> x7, Pallas kernels: 13.9 us -> 13.1 us  [the longest x2 7.74 us: load(): pl.pallas_call(functools.partial(load_kernel, count), in_specs=[pl.BlockS...]
  transfers between devices with their start and end apart: 24 -> 24, of which waited for: 9 -> 9; matrix products, arithmetic and copies ran while one was open for 3% -> 0% of each run, Pallas kernels for 15% -> 20%
where the time goes in v7:
time: 80.4 us; the launch traced here: 80 us
  starting transfers between devices  31.7 us (39%)
  Pallas kernels  21.3 us (26%)
  local copies, waits for them, and re-layouts  14.1 us (18%)
  waiting for transfers between devices  11.9 us (15%)
    ppermute x15, starting transfers between devices, along_z(): lax.ppermute(value, 'mp', [(i, (i + step) % parts) for i in range(parts)])  23.1 us
    unnamed x30, local copies, waits for them, and re-layouts  14.1 us
    ppermute x5, starting transfers between devices, along_y(): lax.ppermute(value, 'y', [(i, (i + step) % chips) for i in range(chips)])  7.97 us
    pallas_call x2, Pallas kernels, load(): pl.pallas_call(functools.partial(load_kernel, count), in_specs=[pl.BlockS...  7.74 us
    ppermute x5, waiting for transfers between devices, along_y(): lax.ppermute(value, 'y', [(i, (i + step) % chips) for i in range(chips)])  5.78 us
    ppermute x15, waiting for transfers between devices, along_z(): lax.ppermute(value, 'mp', [(i, (i + step) % parts) for i in range(parts)])  4.94 us
    pallas_call x1, Pallas kernels, raw_products(): pl.pallas_call(functools.partial(raw_kernel, len(lines)), out_shape=[jax....  4.18 us
    pallas_call x1, Pallas kernels, spread(): pl.pallas_call(functools.partial(spread_kernel, parts, exp_dev), out_shap...  2.16 us
  transfers between devices with their start and end apart: 24, of which 9 were waited for; matrix products, arithmetic and copies ran while one was open for 0% of the time, Pallas kernels for 20%

profile of v7, /device:TPU:0, one launch (start us, length us, event | category | flops | bytes accessed | tf_op | source)
XLA Modules:
  0.0 80.0 jit_solution(4664495525689395910)
XLA Ops:
  0.0 1.6 %attach.1 = bf16[8,4224]{1,0:T(8,128)(2,1)} custom-call(bf16[8,4096]{1,0:T(8,128)(2,1)} %tokens_ref.1, s32[8,8]{1,0:T(8,128)} %routes_ref.1, f32[8,8]{1,0:T(8,128)} %probs_ref.1), custom_call_target="tpu_custom_call" | custom-call | flops 1 | bytes 1 | tf_op jit(solution)/shard_map/attach/pallas_call | solution.py:61
  1.6 3.0 %collective-permute-start.3 = (bf16[8,4224]{1,0:T(8,128)(2,1)}, bf16[8,4224]{1,0:T(8,128)(2,1)S(1)}, u32[]{:S(2)}, u32[]{:S(2)}) collective-permute-start(bf16[8,4224]{1,0:T(8,128)(2,1)} %attach.1), channel_id=1, source_target_pairs={{0,8},{8,0},{1,9},{9,1},{2,10},{10,2},{3,11},{11,3},{4,12},{12,4},... | collective-permute-start | bytes 202760 | tf_op jit(solution)/shard_map/ppermute | solution.py:384
  4.5 3.6 %collective-permute-start.2 = (bf16[8,4224]{1,0:T(8,128)(2,1)}, bf16[8,4224]{1,0:T(8,128)(2,1)S(1)}, u32[]{:S(2)}, u32[]{:S(2)}) collective-permute-start(bf16[8,4224]{1,0:T(8,128)(2,1)} %attach.1), channel_id=1, source_target_pairs={{0,3},{1,0},{2,1},{3,2},{4,7},{5,4},{6,5},{7,6},{8,11},{9,8},{10,9... | collective-permute-start | bytes 202760 | tf_op jit(solution)/shard_map/ppermute | solution.py:381
  8.2 1.0 %collective-permute-start = (bf16[8,4224]{1,0:T(8,128)(2,1)}, bf16[8,4224]{1,0:T(8,128)(2,1)S(1)}, u32[]{:S(2)}, u32[]{:S(2)}) collective-permute-start(bf16[8,4224]{1,0:T(8,128)(2,1)} %attach.1), channel_id=1, source_target_pairs={{0,1},{1,2},{2,3},{3,0},{4,5},{5,6},{6,7},{7,4},{8,9},{9,10},{10,1... | collective-permute-start | bytes 202760 | tf_op jit(solution)/shard_map/ppermute | solution.py:381
  9.2 1.8 %cut.1 = (bf16[3,32,192]{2,1,0:T(8,128)(2,1)}, bf16[3,32,192]{2,1,0:T(8,128)(2,1)}, bf16[3,32,192]{2,1,0:T(8,128)(2,1)}, bf16[3,32,192]{2,1,0:T(8,128)(2,1)}) custom-call(bf16[4,8,768]{2,1,0:T(8,128)(2,1)} %refs_0_.1, bf16[4,8,768]{2,1,0:T(8,128)(2,1)} %refs_1_.1, bf16[4,8,768]{2,1,0:T(8,128)(2,1)} %refs_2_.2), custom_call_target="tpu_custom_call" | custom-call | flops 1 | bytes 1 | tf_op jit(solution)/shard_map/cut/pallas_call | solution.py:87
  11.0 4.8 %load.2 = (bf16[768,4096]{1,0:T(8,128)(2,1)S(1)}, bf16[768,4096]{1,0:T(8,128)(2,1)S(1)}, bf16[4,32,1024]{2,1,0:T(8,128)(2,1)S(1)}, bf16[4,32,1024]{2,1,0:T(8,128)(2,1)S(1)}) custom-call(bf16[768,4096]{1,0:T(8,128)(2,1)} %bitcast.12, bf16[768,4096]{1,0:T(8,128)(2,1)} %bitcast.13, bf16[4,32,1024]{2,1,0:T(8,128)(2,1)} %refs_2_.1, bf16[4,32,1024]{2,1,0:T(8,128)(2,1)} %refs_3_), custom_call_target="tpu_custom_call" | custom-call | flops 1 | bytes 1 | tf_op jit(solution)/shard_map/load/pallas_call | solution.py:171
  15.9 2.7 %copy-done.1 = bf16[768,4096]{1,0:T(8,128)(2,1)} copy-done((bf16[768,4096]{1,0:T(8,128)(2,1)}, bf16[768,4096]{1,0:T(8,128)(2,1)S(1)}, u32[]{:S(2)}) %copy-start.1) | copy-done | bytes 6291480
  18.5 2.6 %copy-done.3 = bf16[768,4096]{1,0:T(8,128)(2,1)} copy-done((bf16[768,4096]{1,0:T(8,128)(2,1)}, bf16[768,4096]{1,0:T(8,128)(2,1)S(1)}, u32[]{:S(2)}) %copy-start.3) | copy-done | bytes 6291480
  21.8 2.5 %collective-permute-start.5 = (bf16[3,32,192]{2,1,0:T(8,128)(2,1)S(1)}, bf16[3,32,192]{2,1,0:T(8,128)(2,1)S(1)}, u32[]{:S(2)}, u32[]{:S(2)}) collective-permute-start(bf16[3,32,192]{2,1,0:T(8,128)(2,1)S(1)} %copy-done.12), channel_id=1, source_target_pairs={{0,1},{1,2},{2,3},{3,0},{4,5},{5,6},{6,7},{7,4},{8,9},{9,10},{10,1... | collective-permute-start | bytes 110600 | tf_op jit(solution)/shard_map/ppermute | solution.py:381
  25.2 1.5 %collective-permute-start.7 = (bf16[3,32,192]{2,1,0:T(8,128)(2,1)S(1)}, bf16[3,32,192]{2,1,0:T(8,128)(2,1)S(1)}, u32[]{:S(2)}, u32[]{:S(2)}) collective-permute-start(bf16[3,32,192]{2,1,0:T(8,128)(2,1)S(1)} %copy-done.10), channel_id=1, source_target_pairs={{0,3},{1,0},{2,1},{3,2},{4,7},{5,4},{6,5},{7,6},{8,11},{9,8},{10,9... | collective-permute-start | bytes 110600 | tf_op jit(solution)/shard_map/ppermute | solution.py:381
  26.8 2.9 %load.3 = (bf16[768,4096]{1,0:T(8,128)(2,1)S(1)}, bf16[4,32,1024]{2,1,0:T(8,128)(2,1)S(1)}) custom-call(bf16[768,4096]{1,0:T(8,128)(2,1)} %bitcast.14, bf16[4,32,1024]{2,1,0:T(8,128)(2,1)} %refs_1_.2), custom_call_target="tpu_custom_call" | custom-call | flops 1 | bytes 1 | tf_op jit(solution)/shard_map/load/pallas_call | solution.py:171
  29.7 2.7 %copy-done = bf16[768,4096]{1,0:T(8,128)(2,1)} copy-done((bf16[768,4096]{1,0:T(8,128)(2,1)}, bf16[768,4096]{1,0:T(8,128)(2,1)S(1)}, u32[]{:S(2)}) %copy-start) | copy-done | bytes 6291480
  33.6 1.2 %collective-permute-done.9.refs_3_ = bf16[32,4224]{1,0:T(8,128)(2,1)S(1)} collective-permute-done((bf16[32,4224]{1,0:T(8,128)(2,1)S(1)}, bf16[32,4224]{1,0:T(8,128)(2,1)S(1)}, u32[]{:S(2)}, u32[]{:S(2)}) %collective-permute-start.9) | collective-permute-done | bytes 270368 | tf_op jit(solution)/shard_map/ppermute | solution.py:387
  34.7 1.0 %inner.1 = (bf16[128,256]{1,0:T(8,128)(2,1)S(1)}, bf16[128,256]{1,0:T(8,128)(2,1)}, bf16[128,256]{1,0:T(8,128)(2,1)}, bf16[128,256]{1,0:T(8,128)(2,1)}) custom-call(bf16[32,4224]{1,0:T(8,128)(2,1)S(1)} %pad_maximum_fusion.refs_0_, bf16[32,4224]{1,0:T(8,128)(2,1)S(1)} %pad_maximum_fusion.1.refs_1_, bf16[32,4224]{1,0:T(8,128)(2,1)S(1)} %collective-permute-done.8.refs_2_, ...), custom_call_target="tpu_custom_call" | custom-call | flops 1 | bytes 1 | tf_op jit(solution)/shard_map/inner/pallas_call | solution.py:142
  36.2 2.0 %collective-permute-start.11 = (bf16[128,256]{1,0:T(8,128)(2,1)}, bf16[128,256]{1,0:T(8,128)(2,1)}, u32[]{:S(2)}, u32[]{:S(2)}) collective-permute-start(bf16[128,256]{1,0:T(8,128)(2,1)} %get-tuple-element.79), channel_id=1, source_target_pairs={{0,2},{1,3},{2,0},{3,1},{4,6},{5,7},{6,4},{7,5},{8,10},{9,11},{10,... | collective-permute-start | bytes 196616 | tf_op jit(solution)/shard_map/ppermute | solution.py:381
  38.2 1.3 %collective-permute-start.12 = (bf16[128,256]{1,0:T(8,128)(2,1)}, bf16[128,256]{1,0:T(8,128)(2,1)}, u32[]{:S(2)}, u32[]{:S(2)}) collective-permute-start(bf16[128,256]{1,0:T(8,128)(2,1)} %get-tuple-element.80), channel_id=1, source_target_pairs={{0,3},{1,0},{2,1},{3,2},{4,7},{5,4},{6,5},{7,6},{8,11},{9,8},{10,9... | collective-permute-start | bytes 196616 | tf_op jit(solution)/shard_map/ppermute | solution.py:381
  39.6 2.2 %spread.1.refs_10_ = bf16[3,128,768]{2,1,0:T(8,128)(2,1)} custom-call(bf16[3,32,192]{2,1,0:T(8,128)(2,1)} %get-tuple-element.70.refs_0_, bf16[3,32,192]{2,1,0:T(8,128)(2,1)} %copy-done.7, bf16[3,32,192]{2,1,0:T(8,128)(2,1)} %copy-done.8, bf16[3,32,192]{2,1,0:T(8,128)(2,1)} %copy-done.9), custom_call_target="tpu_custom_call" | custom-call | flops 1 | bytes 1 | tf_op jit(solution)/shard_map/spread/pallas_call | solution.py:118
  41.7 2.8 %copy-done.2 = bf16[768,4096]{1,0:T(8,128)(2,1)S(1)} copy-done((bf16[768,4096]{1,0:T(8,128)(2,1)S(1)}, bf16[768,4096]{1,0:T(8,128)(2,1)}, u32[]{:S(2)}) %copy-start.2) | copy-done | bytes 6291480
  44.5 2.8 %copy-done.4 = bf16[768,4096]{1,0:T(8,128)(2,1)S(1)} copy-done((bf16[768,4096]{1,0:T(8,128)(2,1)S(1)}, bf16[768,4096]{1,0:T(8,128)(2,1)}, u32[]{:S(2)}) %copy-start.4) | copy-done | bytes 6291480
  47.3 4.2 %raw.1 = (f32[128,768]{1,0:T(8,128)S(1)}, f32[128,768]{1,0:T(8,128)S(1)}) custom-call(bf16[32,4224]{1,0:T(8,128)(2,1)S(1)} %pad_maximum_fusion.refs_0_, bf16[32,4224]{1,0:T(8,128)(2,1)S(1)} %pad_maximum_fusion.1.refs_1_, bf16[32,4224]{1,0:T(8,128)(2,1)S(1)} %collective-permute-done.8.refs_2_, bf16[32,4224]{1,0:T(8,128)(2,1)S(1)} %collective-permute-done.9.refs_3_, ...), custom_call_target="tpu_custom_call" | custom-call | flops 1 | bytes 1 | tf_op jit(solution)/shard_map/raw/pallas_call | solution.py:197
  51.5 1.4 %hidden.1 = (bf16[128,768]{1,0:T(8,128)(2,1)S(1)}, bf16[128,128]{1,0:T(8,128)(2,1)S(1)}, bf16[128,128]{1,0:T(8,128)(2,1)S(1)}, bf16[128,128]{1,0:T(8,128)(2,1)S(1)}, bf16[128,128]{1,0:T(8,128)(2,1)S(1)}) custom-call(s32[1]{0:T(128)} %bitcast.place_ref, bf16[32,4224]{1,0:T(8,128)(2,1)S(1)} %pad_maximum_fusion.refs_0_, ...), custom_call_target="tpu_custom_call" | custom-call | flops 1 | bytes 1 | tf_op jit(solution)/shard_map/hidden/pallas_call | solution.py:232
  53.0 1.0 %down.1 = (f32[64,4096]{1,0:T(8,128)S(1)}, bf16[64,4096]{1,0:T(8,128)(2,1)S(1)}) custom-call(bf16[128,768]{1,0:T(8,128)(2,1)S(1)} %get-tuple-element.83.hidden_ref, bf16[768,4096]{1,0:T(8,128)(2,1)S(1)} %bitcast.10), custom_call_target="tpu_custom_call" | custom-call | flops 1 | bytes 1 | tf_op jit(solution)/shard_map/down/pallas_call | solution.py:257
  54.8 1.4 %collective-permute-start.15 = (bf16[128,128]{1,0:T(8,128)(2,1)S(1)}, bf16[128,128]{1,0:T(8,128)(2,1)S(1)}, u32[]{:S(2)}, u32[]{:S(2)}) collective-permute-start(bf16[128,128]{1,0:T(8,128)(2,1)S(1)} %get-tuple-element.90), channel_id=1, source_target_pairs={{0,2},{1,3},{2,0},{3,1},{4,6},{5,7},{6,4},{7,5},{8,10},{9,11},{10,... | collective-permute-start | bytes 98312 | tf_op jit(solution)/shard_map/ppermute | solution.py:381
  56.2 2.8 %collective-permute-start.16 = (bf16[128,128]{1,0:T(8,128)(2,1)S(1)}, bf16[128,128]{1,0:T(8,128)(2,1)S(1)}, u32[]{:S(2)}, u32[]{:S(2)}) collective-permute-start(bf16[128,128]{1,0:T(8,128)(2,1)S(1)} %get-tuple-element.91), channel_id=1, source_target_pairs={{0,3},{1,0},{2,1},{3,2},{4,7},{5,4},{6,5},{7,6},{8,11},{9,8},{10,9... | collective-permute-start | bytes 98312 | tf_op jit(solution)/shard_map/ppermute | solution.py:381
  61.0 1.6 %collective-permute-start.18 = (bf16[24,4096]{1,0:T(8,128)(2,1)S(1)}, bf16[24,4096]{1,0:T(8,128)(2,1)S(1)}, u32[]{:S(2)}, u32[]{:S(2)}) collective-permute-start(bf16[24,4096]{1,0:T(8,128)(2,1)S(1)} %get-tuple-element.99), channel_id=1, source_target_pairs={{0,8},{8,0},{1,9},{9,1},{2,10},{10,2},{3,11},{11,3},{4,12},{12,4},... | collective-permute-start | bytes 589832 | tf_op jit(solution)/shard_map/ppermute | solution.py:384
  62.6 1.3 %collective-permute-start.19 = (bf16[32,1024]{1,0:T(8,128)(2,1)S(1)}, bf16[32,1024]{1,0:T(8,128)(2,1)S(1)}, u32[]{:S(2)}, u32[]{:S(2)}) collective-permute-start(bf16[32,1024]{1,0:T(8,128)(2,1)S(1)} %get-tuple-element.100), channel_id=1, source_target_pairs={{0,8},{8,0},{1,9},{9,1},{2,10},{10,2},{3,11},{11,3},{4,12},{12,4},... | collective-permute-start | bytes 196616 | tf_op jit(solution)/shard_map/ppermute | solution.py:384
  64.0 4.8 %collective-permute-done.18.refs_0_ = bf16[24,4096]{1,0:T(8,128)(2,1)S(1)} collective-permute-done((bf16[24,4096]{1,0:T(8,128)(2,1)S(1)}, bf16[24,4096]{1,0:T(8,128)(2,1)S(1)}, u32[]{:S(2)}, u32[]{:S(2)}) %collective-permute-start.18) | collective-permute-done | bytes 196640 | tf_op jit(solution)/shard_map/ppermute | solution.py:384
  69.8 1.8 %collective-permute-start.23 = (bf16[8,4096]{1,0:T(8,128)(2,1)S(1)}, bf16[8,4096]{1,0:T(8,128)(2,1)S(1)}, u32[]{:S(2)}, u32[]{:S(2)}) collective-permute-start(bf16[8,4096]{1,0:T(8,128)(2,1)S(1)} %get-tuple-element.106), channel_id=1, source_target_pairs={{0,1},{1,2},{2,3},{3,0},{4,5},{5,6},{6,7},{7,4},{8,9},{9,10},{10,1... | collective-permute-start | bytes 196616 | tf_op jit(solution)/shard_map/ppermute | solution.py:381
  71.6 2.9 %collective-permute-start.22 = (bf16[8,4096]{1,0:T(8,128)(2,1)S(1)}, bf16[8,4096]{1,0:T(8,128)(2,1)S(1)}, u32[]{:S(2)}, u32[]{:S(2)}) collective-permute-start(bf16[8,4096]{1,0:T(8,128)(2,1)S(1)} %get-tuple-element.105), channel_id=1, source_target_pairs={{0,2},{1,3},{2,0},{3,1},{4,6},{5,7},{6,4},{7,5},{8,10},{9,11},{10,... | collective-permute-start | bytes 196616 | tf_op jit(solution)/shard_map/ppermute | solution.py:381
  74.5 1.5 %collective-permute-start.20 = (bf16[8,4096]{1,0:T(8,128)(2,1)S(1)}, bf16[8,4096]{1,0:T(8,128)(2,1)S(1)}, u32[]{:S(2)}, u32[]{:S(2)}) collective-permute-start(bf16[8,4096]{1,0:T(8,128)(2,1)S(1)} %get-tuple-element.103), channel_id=1, source_target_pairs={{0,8},{8,0},{1,9},{9,1},{2,10},{10,2},{3,11},{11,3},{4,12},{12,4},... | collective-permute-start | bytes 196616 | tf_op jit(solution)/shard_map/ppermute | solution.py:384
  76.0 1.0 %collective-permute-done.23 = bf16[8,4096]{1,0:T(8,128)(2,1)S(1)} collective-permute-done((bf16[8,4096]{1,0:T(8,128)(2,1)S(1)}, bf16[8,4096]{1,0:T(8,128)(2,1)S(1)}, u32[]{:S(2)}, u32[]{:S(2)}) %collective-permute-start.23) | collective-permute-done | bytes 65568 | tf_op jit(solution)/shard_map/ppermute | solution.py:381
  77.0 1.8 %collective-permute-done.22 = bf16[8,4096]{1,0:T(8,128)(2,1)S(1)} collective-permute-done((bf16[8,4096]{1,0:T(8,128)(2,1)S(1)}, bf16[8,4096]{1,0:T(8,128)(2,1)S(1)}, u32[]{:S(2)}, u32[]{:S(2)}) %collective-permute-start.22) | collective-permute-done | bytes 65568 | tf_op jit(solution)/shard_map/ppermute | solution.py:381
  (64 shorter events, 8.3 us)
Async XLA Ops:
  1.6 9.4 %collective-permute-start.3 = (bf16[8,4224]{1,0:T(8,128)(2,1)}, bf16[8,4224]{1,0:T(8,128)(2,1)S(1)}, u32[]{:S(2)}, u32[]{:S(2)}) collective-permute-start(bf16[8,4224]{1,0:T(8,128)(2,1)} %attach.1), channel_id=1, source_target_pairs={{0,8},{8,0},{1,9},{9,1},{2,10},{10,2},{3,11},{11,3},{4,12},{12,4},... | collective-permute-start | bytes 202760 | tf_op jit(solution)/shard_map/ppermute | solution.py:384
  4.5 16.6 %collective-permute-start.2 = (bf16[8,4224]{1,0:T(8,128)(2,1)}, bf16[8,4224]{1,0:T(8,128)(2,1)S(1)}, u32[]{:S(2)}, u32[]{:S(2)}) collective-permute-start(bf16[8,4224]{1,0:T(8,128)(2,1)} %attach.1), channel_id=1, source_target_pairs={{0,3},{1,0},{2,1},{3,2},{4,7},{5,4},{6,5},{7,6},{8,11},{9,8},{10,9... | collective-permute-start | bytes 202760 | tf_op jit(solution)/shard_map/ppermute | solution.py:381
  8.2 13.0 %collective-permute-start.1 = (bf16[8,4224]{1,0:T(8,128)(2,1)}, bf16[8,4224]{1,0:T(8,128)(2,1)S(1)}, u32[]{:S(2)}, u32[]{:S(2)}) collective-permute-start(bf16[8,4224]{1,0:T(8,128)(2,1)} %attach.1), channel_id=1, source_target_pairs={{0,2},{1,3},{2,0},{3,1},{4,6},{5,7},{6,4},{7,5},{8,10},{9,11},{10,... | collective-permute-start | bytes 202760 | tf_op jit(solution)/shard_map/ppermute | solution.py:381
  8.2 13.0 %collective-permute-start = (bf16[8,4224]{1,0:T(8,128)(2,1)}, bf16[8,4224]{1,0:T(8,128)(2,1)S(1)}, u32[]{:S(2)}, u32[]{:S(2)}) collective-permute-start(bf16[8,4224]{1,0:T(8,128)(2,1)} %attach.1), channel_id=1, source_target_pairs={{0,1},{1,2},{2,3},{3,0},{4,5},{5,6},{6,7},{7,4},{8,9},{9,10},{10,1... | collective-permute-start | bytes 202760 | tf_op jit(solution)/shard_map/ppermute | solution.py:381
  11.0 10.8 %copy-start.6 = (bf16[8,4224]{1,0:T(8,128)(2,1)S(1)}, bf16[8,4224]{1,0:T(8,128)(2,1)}, u32[]{:S(2)}) copy-start(bf16[8,4224]{1,0:T(8,128)(2,1)} %attach.1) | copy-start | bytes 202756
  11.0 10.8 %copy-start.12 = (bf16[3,32,192]{2,1,0:T(8,128)(2,1)S(1)}, bf16[3,32,192]{2,1,0:T(8,128)(2,1)}, u32[]{:S(2)}) copy-start(bf16[3,32,192]{2,1,0:T(8,128)(2,1)} %get-tuple-element.71) | copy-start | bytes 110596
  11.0 13.3 %copy-start.11 = (bf16[3,32,192]{2,1,0:T(8,128)(2,1)S(1)}, bf16[3,32,192]{2,1,0:T(8,128)(2,1)}, u32[]{:S(2)}) copy-start(bf16[3,32,192]{2,1,0:T(8,128)(2,1)} %get-tuple-element.72) | copy-start | bytes 110596
  11.0 14.2 %copy-start.10 = (bf16[3,32,192]{2,1,0:T(8,128)(2,1)S(1)}, bf16[3,32,192]{2,1,0:T(8,128)(2,1)}, u32[]{:S(2)}) copy-start(bf16[3,32,192]{2,1,0:T(8,128)(2,1)} %get-tuple-element.73) | copy-start | bytes 110596
  21.2 11.2 %collective-permute-start.4 = (bf16[24,4224]{1,0:T(8,128)(2,1)S(1)}, bf16[24,4224]{1,0:T(8,128)(2,1)S(1)}, u32[]{:S(2)}, u32[]{:S(2)}) collective-permute-start(bf16[24,4224]{1,0:T(8,128)(2,1)S(1)} %pad_maximum_fusion.2), channel_id=1, source_target_pairs={{0,8},{8,0},{1,9},{9,1},{2,10},{10,2},{3,11},{11,3},{4,12},{12,4},... | collective-permute-start | bytes 608264 | tf_op jit(solution)/shard_map/ppermute | solution.py:384
  21.8 10.6 %collective-permute-start.5 = (bf16[3,32,192]{2,1,0:T(8,128)(2,1)S(1)}, bf16[3,32,192]{2,1,0:T(8,128)(2,1)S(1)}, u32[]{:S(2)}, u32[]{:S(2)}) collective-permute-start(bf16[3,32,192]{2,1,0:T(8,128)(2,1)S(1)} %copy-done.12), channel_id=1, source_target_pairs={{0,1},{1,2},{2,3},{3,0},{4,5},{5,6},{6,7},{7,4},{8,9},{9,10},{10,1... | collective-permute-start | bytes 110600 | tf_op jit(solution)/shard_map/ppermute | solution.py:381
  24.3 8.1 %collective-permute-start.6 = (bf16[3,32,192]{2,1,0:T(8,128)(2,1)S(1)}, bf16[3,32,192]{2,1,0:T(8,128)(2,1)S(1)}, u32[]{:S(2)}, u32[]{:S(2)}) collective-permute-start(bf16[3,32,192]{2,1,0:T(8,128)(2,1)S(1)} %copy-done.11), channel_id=1, source_target_pairs={{0,2},{1,3},{2,0},{3,1},{4,6},{5,7},{6,4},{7,5},{8,10},{9,11},{10,... | collective-permute-start | bytes 110600 | tf_op jit(solution)/shard_map/ppermute | solution.py:381
  25.2 7.2 %collective-permute-start.7 = (bf16[3,32,192]{2,1,0:T(8,128)(2,1)S(1)}, bf16[3,32,192]{2,1,0:T(8,128)(2,1)S(1)}, u32[]{:S(2)}, u32[]{:S(2)}) collective-permute-start(bf16[3,32,192]{2,1,0:T(8,128)(2,1)S(1)} %copy-done.10), channel_id=1, source_target_pairs={{0,3},{1,0},{2,1},{3,2},{4,7},{5,4},{6,5},{7,6},{8,11},{9,8},{10,9... | collective-permute-start | bytes 110600 | tf_op jit(solution)/shard_map/ppermute | solution.py:381
  26.8 6.8 %collective-permute-start.8 = (bf16[32,4224]{1,0:T(8,128)(2,1)S(1)}, bf16[32,4224]{1,0:T(8,128)(2,1)S(1)}, u32[]{:S(2)}, u32[]{:S(2)}) collective-permute-start(bf16[32,4224]{1,0:T(8,128)(2,1)S(1)} %pad_maximum_fusion.refs_0_), channel_id=1, source_target_pairs={{0,4},{4,0},{1,5},{5,1},{2,6},{6,2},{3,7},{7,3},{8,12},{12,8},{9,1... | collective-permute-start | bytes 811016 | tf_op jit(solution)/shard_map/ppermute | solution.py:387
  32.4 7.2 %copy-start.7 = (bf16[3,32,192]{2,1,0:T(8,128)(2,1)}, bf16[3,32,192]{2,1,0:T(8,128)(2,1)S(1)}, u32[]{:S(2)}) copy-start(bf16[3,32,192]{2,1,0:T(8,128)(2,1)S(1)} %collective-permute-done.5.refs_1_) | copy-start | bytes 110596
  33.0 1.7 %collective-permute-start.9 = (bf16[32,4224]{1,0:T(8,128)(2,1)S(1)}, bf16[32,4224]{1,0:T(8,128)(2,1)S(1)}, u32[]{:S(2)}, u32[]{:S(2)}) collective-permute-start(bf16[32,4224]{1,0:T(8,128)(2,1)S(1)} %pad_maximum_fusion.1.refs_1_), channel_id=1, source_target_pairs={{0,4},{4,0},{1,5},{5,1},{2,6},{6,2},{3,7},{7,3},{8,12},{12,8},{9,1... | collective-permute-start | bytes 811016 | tf_op jit(solution)/shard_map/ppermute | solution.py:387
  35.7 15.8 %collective-permute-start.10 = (bf16[128,256]{1,0:T(8,128)(2,1)}, bf16[128,256]{1,0:T(8,128)(2,1)}, u32[]{:S(2)}, u32[]{:S(2)}) collective-permute-start(bf16[128,256]{1,0:T(8,128)(2,1)} %get-tuple-element.78), channel_id=1, source_target_pairs={{0,1},{1,2},{2,3},{3,0},{4,5},{5,6},{6,7},{7,4},{8,9},{9,10},{10,1... | collective-permute-start | bytes 196616 | tf_op jit(solution)/shard_map/ppermute | solution.py:381
  36.2 15.3 %collective-permute-start.11 = (bf16[128,256]{1,0:T(8,128)(2,1)}, bf16[128,256]{1,0:T(8,128)(2,1)}, u32[]{:S(2)}, u32[]{:S(2)}) collective-permute-start(bf16[128,256]{1,0:T(8,128)(2,1)} %get-tuple-element.79), channel_id=1, source_target_pairs={{0,2},{1,3},{2,0},{3,1},{4,6},{5,7},{6,4},{7,5},{8,10},{9,11},{10,... | collective-permute-start | bytes 196616 | tf_op jit(solution)/shard_map/ppermute | solution.py:381
  38.2 13.3 %collective-permute-start.12 = (bf16[128,256]{1,0:T(8,128)(2,1)}, bf16[128,256]{1,0:T(8,128)(2,1)}, u32[]{:S(2)}, u32[]{:S(2)}) collective-permute-start(bf16[128,256]{1,0:T(8,128)(2,1)} %get-tuple-element.80), channel_id=1, source_target_pairs={{0,3},{1,0},{2,1},{3,2},{4,7},{5,4},{6,5},{7,6},{8,11},{9,8},{10,9... | collective-permute-start | bytes 196616 | tf_op jit(solution)/shard_map/ppermute | solution.py:381
  39.6 13.4 %slice-start = ((s8[6291456]{0:T(1024)(128)(4,1)}), s8[2097152]{0:T(1024)(128)(4,1)S(1)}, s32[]{:S(2)}) async-start(s8[6291456]{0:T(1024)(128)(4,1)} %bitcast.9), calls=%async_computation | async-start | bytes 4194304
  47.3 4.2 %copy-start.5 = (bf16[3,128,768]{2,1,0:T(8,128)(2,1)S(1)}, bf16[3,128,768]{2,1,0:T(8,128)(2,1)}, u32[]{:S(2)}) copy-start(bf16[3,128,768]{2,1,0:T(8,128)(2,1)} %spread.1.refs_10_) | copy-start | bytes 1769476
  47.3 5.7 %slice-start.1 = ((s8[6291456]{0:T(1024)(128)(4,1)}), s8[4194304]{0:T(1024)(128)(4,1)S(1)}, s32[]{:S(2)}) async-start(s8[6291456]{0:T(1024)(128)(4,1)} %bitcast.9), calls=%async_computation.1 | async-start | bytes 8388608
  54.0 5.1 %collective-permute-start.13 = (bf16[64,4096]{1,0:T(8,128)(2,1)S(1)}, bf16[64,4096]{1,0:T(8,128)(2,1)S(1)}, u32[]{:S(2)}, u32[]{:S(2)}) collective-permute-start(bf16[64,4096]{1,0:T(8,128)(2,1)S(1)} %get-tuple-element.85), channel_id=1, source_target_pairs={{0,4},{4,0},{1,5},{5,1},{2,6},{6,2},{3,7},{7,3},{8,12},{12,8},{9,1... | collective-permute-start | bytes 1572872 | tf_op jit(solution)/shard_map/ppermute | solution.py:387
  54.1 5.8 %collective-permute-start.14 = (bf16[128,128]{1,0:T(8,128)(2,1)S(1)}, bf16[128,128]{1,0:T(8,128)(2,1)S(1)}, u32[]{:S(2)}, u32[]{:S(2)}) collective-permute-start(bf16[128,128]{1,0:T(8,128)(2,1)S(1)} %get-tuple-element.89), channel_id=1, source_target_pairs={{0,1},{1,2},{2,3},{3,0},{4,5},{5,6},{6,7},{7,4},{8,9},{9,10},{10,1... | collective-permute-start | bytes 98312 | tf_op jit(solution)/shard_map/ppermute | solution.py:381
  54.8 5.6 %collective-permute-start.15 = (bf16[128,128]{1,0:T(8,128)(2,1)S(1)}, bf16[128,128]{1,0:T(8,128)(2,1)S(1)}, u32[]{:S(2)}, u32[]{:S(2)}) collective-permute-start(bf16[128,128]{1,0:T(8,128)(2,1)S(1)} %get-tuple-element.90), channel_id=1, source_target_pairs={{0,2},{1,3},{2,0},{3,1},{4,6},{5,7},{6,4},{7,5},{8,10},{9,11},{10,... | collective-permute-start | bytes 98312 | tf_op jit(solution)/shard_map/ppermute | solution.py:381
  56.2 4.5 %collective-permute-start.16 = (bf16[128,128]{1,0:T(8,128)(2,1)S(1)}, bf16[128,128]{1,0:T(8,128)(2,1)S(1)}, u32[]{:S(2)}, u32[]{:S(2)}) collective-permute-start(bf16[128,128]{1,0:T(8,128)(2,1)S(1)} %get-tuple-element.91), channel_id=1, source_target_pairs={{0,3},{1,0},{2,1},{3,2},{4,7},{5,4},{6,5},{7,6},{8,11},{9,8},{10,9... | collective-permute-start | bytes 98312 | tf_op jit(solution)/shard_map/ppermute | solution.py:381
  60.9 1.7 %collective-permute-start.17 = (bf16[64,1024]{1,0:T(8,128)(2,1)S(1)}, bf16[64,1024]{1,0:T(8,128)(2,1)S(1)}, u32[]{:S(2)}, u32[]{:S(2)}) collective-permute-start(bf16[64,1024]{1,0:T(8,128)(2,1)S(1)} %get-tuple-element.97), channel_id=1, source_target_pairs={{0,4},{4,0},{1,5},{5,1},{2,6},{6,2},{3,7},{7,3},{8,12},{12,8},{9,1... | collective-permute-start | bytes 393224 | tf_op jit(solution)/shard_map/ppermute | solution.py:387
  61.0 7.8 %collective-permute-start.18 = (bf16[24,4096]{1,0:T(8,128)(2,1)S(1)}, bf16[24,4096]{1,0:T(8,128)(2,1)S(1)}, u32[]{:S(2)}, u32[]{:S(2)}) collective-permute-start(bf16[24,4096]{1,0:T(8,128)(2,1)S(1)} %get-tuple-element.99), channel_id=1, source_target_pairs={{0,8},{8,0},{1,9},{9,1},{2,10},{10,2},{3,11},{11,3},{4,12},{12,4},... | collective-permute-start | bytes 589832 | tf_op jit(solution)/shard_map/ppermute | solution.py:384
  62.6 7.1 %collective-permute-start.19 = (bf16[32,1024]{1,0:T(8,128)(2,1)S(1)}, bf16[32,1024]{1,0:T(8,128)(2,1)S(1)}, u32[]{:S(2)}, u32[]{:S(2)}) collective-permute-start(bf16[32,1024]{1,0:T(8,128)(2,1)S(1)} %get-tuple-element.100), channel_id=1, source_target_pairs={{0,8},{8,0},{1,9},{9,1},{2,10},{10,2},{3,11},{11,3},{4,12},{12,4},... | collective-permute-start | bytes 196616 | tf_op jit(solution)/shard_map/ppermute | solution.py:384
  69.8 7.1 %collective-permute-start.23 = (bf16[8,4096]{1,0:T(8,128)(2,1)S(1)}, bf16[8,4096]{1,0:T(8,128)(2,1)S(1)}, u32[]{:S(2)}, u32[]{:S(2)}) collective-permute-start(bf16[8,4096]{1,0:T(8,128)(2,1)S(1)} %get-tuple-element.106), channel_id=1, source_target_pairs={{0,1},{1,2},{2,3},{3,0},{4,5},{5,6},{6,7},{7,4},{8,9},{9,10},{10,1... | collective-permute-start | bytes 196616 | tf_op jit(solution)/shard_map/ppermute | solution.py:381
  71.6 7.1 %collective-permute-start.22 = (bf16[8,4096]{1,0:T(8,128)(2,1)S(1)}, bf16[8,4096]{1,0:T(8,128)(2,1)S(1)}, u32[]{:S(2)}, u32[]{:S(2)}) collective-permute-start(bf16[8,4096]{1,0:T(8,128)(2,1)S(1)} %get-tuple-element.105), channel_id=1, source_target_pairs={{0,2},{1,3},{2,0},{3,1},{4,6},{5,7},{6,4},{7,5},{8,10},{9,11},{10,... | collective-permute-start | bytes 196616 | tf_op jit(solution)/shard_map/ppermute | solution.py:381
  74.5 4.9 %collective-permute-start.21 = (bf16[8,4096]{1,0:T(8,128)(2,1)S(1)}, bf16[8,4096]{1,0:T(8,128)(2,1)S(1)}, u32[]{:S(2)}, u32[]{:S(2)}) collective-permute-start(bf16[8,4096]{1,0:T(8,128)(2,1)S(1)} %get-tuple-element.104), channel_id=1, source_target_pairs={{0,3},{1,0},{2,1},{3,2},{4,7},{5,4},{6,5},{7,6},{8,11},{9,8},{10,9... | collective-permute-start | bytes 196616 | tf_op jit(solution)/shard_map/ppermute | solution.py:381
  74.5 4.9 %collective-permute-start.20 = (bf16[8,4096]{1,0:T(8,128)(2,1)S(1)}, bf16[8,4096]{1,0:T(8,128)(2,1)S(1)}, u32[]{:S(2)}, u32[]{:S(2)}) collective-permute-start(bf16[8,4096]{1,0:T(8,128)(2,1)S(1)} %get-tuple-element.103), channel_id=1, source_target_pairs={{0,8},{8,0},{1,9},{9,1},{2,10},{10,2},{3,11},{11,3},{4,12},{12,4},... | collective-permute-start | bytes 196616 | tf_op jit(solution)/shard_map/ppermute | solution.py:384
  (7 other events, 15.8 us)

commit v8 on v7

--- a/solution.py
+++ b/solution.py
@@ -9,8 +9,8 @@
 
 BF = jnp.bfloat16
 F32 = jnp.float32
-PIECES = 4
 VMEM_LIMIT = 16 * 1024 * 1024
+STREAM_LIMIT = 24 * 1024 * 1024
 BRIEF = pl.CostEstimate(flops=1, bytes_accessed=1, transcendentals=0)
 
 
@@ -67,8 +67,11 @@
 
 
 def cut_kernel(parts, *refs):
-    ins, outs = refs[:3], refs[3:]
+    ins, lefts, left_ref, outs = refs[:3], refs[3:5], refs[5], refs[6:]
     exp_dev, piece, hid = ins[0].shape
+    half = left_ref.shape[0] // 2
+    for n, ref in enumerate(lefts):
+        left_ref[n * half : (n + 1) * half] = ref[...].reshape(half, left_ref.shape[1])
     cols = hid // parts
     me = lax.axis_index("mp")
     for n, ref in enumerate(ins):
@@ -82,14 +85,16 @@
             outs[k][n] = block.astype(BF)
 
 
-def cut(factors, parts):
+def cut(factors, lefts, parts):
     exp_dev, piece, hid = factors[0].shape
+    _, rank, block = lefts[0].shape
     return pl.pallas_call(
         functools.partial(cut_kernel, parts),
-        out_shape=[jax.ShapeDtypeStruct((3, exp_dev * piece, hid // parts), BF)] * parts,
+        out_shape=[jax.ShapeDtypeStruct((2 * exp_dev * rank, block), BF)]
+        + [jax.ShapeDtypeStruct((3, exp_dev * piece, hid // parts), BF)] * parts,
         cost_estimate=BRIEF,
         name="cut",
-    )(*in_hbm(*factors))
+    )(*in_hbm(*factors, *lefts))
 
 
 def spread_kernel(parts, exp_dev, *refs):
@@ -103,10 +108,10 @@
     step = lax.rem(me - row % rank // piece + parts, parts)
     source = (step * exp_dev + row // rank) * piece + row % piece
     order = (col == source).astype(F32).astype(BF)
-    own = (
-        lax.broadcasted_iota(jnp.int32, (ranks, hid), 0) // rank
-        == lax.broadcasted_iota(jnp.int32, (ranks, hid), 1) // (hid // exp_dev)
-    )
+    cols = hid // exp_dev
+    place = lax.broadcasted_iota(jnp.int32, (ranks, hid), 1)
+    place -= lax.broadcasted_iota(jnp.int32, (ranks, hid), 0) // rank * cols
+    own = (place >= 0) & (place < cols)
     for n in range(3):
         value = dot_nn(order, jnp.concatenate([p[n].astype(F32) for p in pieces]).astype(BF))
         value = jnp.concatenate([value] * exp_dev, axis=1)
@@ -124,89 +129,70 @@
 
 
 def inner_kernel(parts, rows, count, *refs):
-    lines, (gate_ref, up_ref), outs = refs[:count], refs[count : count + 2], refs[count + 2 :]
-    exp_dev, rank, block = gate_ref.shape
+    lines, left_ref, outs = refs[:count], refs[count], refs[count + 1 :]
+    block = left_ref.shape[1]
     offset = pl.multiple_of(lax.axis_index("mp") * block, 128)
     x = jnp.concatenate([line[:, pl.ds(offset, block)] for line in lines])
-    left = jnp.concatenate(
-        [ref[...].reshape(exp_dev * rank, block) for ref in (gate_ref, up_ref)]
-    )
-    value = dot_nt(x, left)
+    value = dot_nt(x, left_ref[...])
     for k in range(parts):
         outs[k][...] = rotated(value, rows, parts, k).astype(BF)
 
 
-def inner_products(lines, gate_left, up_left, parts, rows):
+def inner_products(lines, left, parts, rows):
     total = sum(line.shape[0] for line in lines)
-    ranks = 2 * gate_left.shape[0] * gate_left.shape[1]
+    ranks = left.shape[0]
     return pl.pallas_call(
         functools.partial(inner_kernel, parts, rows, len(lines)),
         out_shape=[jax.ShapeDtypeStruct((total, ranks), BF)] * parts,
         compiler_params=pltpu.CompilerParams(vmem_limit_bytes=VMEM_LIMIT),
         cost_estimate=BRIEF,
         name="inner",
-    )(*lines, gate_left, up_left)
-
-
-def load_kernel(count, *refs):
-    sources, targets, sems = refs[:count], refs[count:-1], refs[-1]
+    )(*lines, left)
+
+
+def raw_kernel(count, tiles, *refs):
+    lines, weights, outs = refs[:count], refs[count : count + 2], refs[count + 2 : count + 4]
+    scratch, sems = refs[count + 4 : count + 6], refs[count + 6]
+    hid, width = weights[0].shape
+    tile = hid // tiles
     copies = []
-    for n in range(count):
-        step = sources[n].shape[0] // PIECES
-        for i in range(PIECES):
-            span = pl.ds(i * step, step)
-            copies.append(
-                pltpu.make_async_copy(
-                    sources[n].at[span], targets[n].at[span], sems.at[n * PIECES + i]
-                )
+    for i in range(tiles):
+        for n in range(2):
+            span = pl.ds(i * tile, tile)
+            copy = pltpu.make_async_copy(
+                weights[n].at[span], scratch[n].at[span], sems.at[2 * i + n]
             )
-    for copy in copies:
-        copy.start()
-    for copy in copies:
-        copy.wait()
-
-
-def load(*weights):
-    count = len(weights)
-    return pl.pallas_call(
-        functools.partial(load_kernel, count),
-        in_specs=[pl.BlockSpec(memory_space=pltpu.HBM)] * count,
-        out_specs=[pl.BlockSpec(memory_space=pltpu.VMEM)] * count,
-        out_shape=[pltpu.VMEM(w.shape, w.dtype) for w in weights],
-        scratch_shapes=[pltpu.SemaphoreType.DMA((count * PIECES,))],
-        compiler_params=pltpu.CompilerParams(vmem_limit_bytes=VMEM_LIMIT),
-        cost_estimate=BRIEF,
-        name="load",
-    )(*in_hbm(*weights))
-
-
-def raw_kernel(count, *refs):
-    lines, (gate_w, up_w, gate_ref, up_ref) = refs[:count], refs[count:]
-    hid, width = gate_w.shape
+            copy.start()
+            copies.append(copy)
     x = jnp.concatenate([line[:, :width] for line in lines])
-    tile = hid // 3 if hid % 384 == 0 else hid
-    for i in range(hid // tile):
+    for i in range(tiles):
         span = slice(i * tile, (i + 1) * tile)
-        gate_ref[:, span] = dot_nt(x, gate_w[span])
-        up_ref[:, span] = dot_nt(x, up_w[span])
+        for n in range(2):
+            copies[2 * i + n].wait()
+            outs[n][:, span] = dot_nt(x, scratch[n][span])
 
 
 def raw_products(lines, gate_w, up_w):
     hid = gate_w.shape[0]
     total = sum(line.shape[0] for line in lines)
-    return pl.pallas_call(
-        functools.partial(raw_kernel, len(lines)),
+    tiles = hid // 128
+    vmem = pl.BlockSpec(memory_space=pltpu.VMEM)
+    return pl.pallas_call(
+        functools.partial(raw_kernel, len(lines), tiles),
+        in_specs=[vmem] * len(lines) + [pl.BlockSpec(memory_space=pltpu.HBM)] * 2,
+        out_specs=[vmem] * 2,
         out_shape=[jax.ShapeDtypeStruct((total, hid), F32)] * 2,
-        compiler_params=pltpu.CompilerParams(vmem_limit_bytes=VMEM_LIMIT),
+        scratch_shapes=[pltpu.VMEM(gate_w.shape, BF)] * 2
+        + [pltpu.SemaphoreType.DMA((2 * tiles,))],
+        compiler_params=pltpu.CompilerParams(vmem_limit_bytes=STREAM_LIMIT),
         cost_estimate=BRIEF,
         name="raw",
-    )(*lines, gate_w, up_w)
-
-
-def hidden_kernel(parts, rows, count, exp_dev, pair, place_ref, *refs):
+    )(*lines, *in_hbm(gate_w, up_w))
+
+
+def hidden_kernel(parts, count, exp_dev, pair, place_ref, *refs):
     lines, inner, rest = refs[:count], refs[count : count + parts], refs[count + parts :]
-    gate_ref, up_ref, diag_ref, hidden_ref = rest[:4]
-    outs = rest[4:]
+    gate_ref, up_ref, diag_ref, hidden_ref, near_ref, far_ref = rest
     hid = gate_ref.shape[1]
     ranks = diag_ref.shape[1]
     wide = lines[0].shape[1] - pair
@@ -215,26 +201,28 @@
     up = up_ref[...] + dot_nn(total[:, ranks:], diag_ref[1])
     lane = lax.broadcasted_iota(jnp.int32, (pair, hid), 0)
     lane = jnp.where(lane < pair // 2, lane, lane - pair // 2)
-    owner = lax.broadcasted_iota(jnp.int32, (pair, hid), 1) // (hid // exp_dev)
-    pick = (lane == owner + place_ref[0]).astype(F32).astype(BF)
+    cols = hid // exp_dev
+    place = lax.broadcasted_iota(jnp.int32, (pair, hid), 1) - (lane - place_ref[0]) * cols
+    pick = ((place >= 0) & (place < cols)).astype(F32).astype(BF)
     scale = dot_nn(jnp.concatenate([line[:, wide:] for line in lines]), pick)
     hidden = (gate / (1.0 + jnp.exp(-gate)) * up * scale).astype(BF)
     hidden_ref[...] = hidden
     value = dot_nt(hidden, diag_ref[2])
-    for k in range(parts):
-        outs[k][...] = rotated(value, rows, parts, k).astype(BF)
-
-
-def hidden_units(place, lines, inner, raw, diag, parts, rows, exp_dev, pair):
+    near = near_ref.shape[0]
+    near_ref[...] = value[:near].astype(BF)
+    far_ref[...] = value[near:].astype(BF)
+
+
+def hidden_units(place, lines, inner, raw, diag, parts, exp_dev, pair):
     total, hid = raw[0].shape
     ranks = diag.shape[1]
     vmem = pl.BlockSpec(memory_space=pltpu.VMEM)
     return pl.pallas_call(
-        functools.partial(hidden_kernel, parts, rows, len(lines), exp_dev, pair),
+        functools.partial(hidden_kernel, parts, len(lines), exp_dev, pair),
         in_specs=[pl.BlockSpec(memory_space=pltpu.SMEM)]
         + [vmem] * (len(lines) + len(inner) + 3),
         out_shape=[jax.ShapeDtypeStruct((total, hid), BF)]
-        + [jax.ShapeDtypeStruct((total, ranks), BF)] * parts,
+        + [jax.ShapeDtypeStruct((total // 2, ranks), BF)] * 2,
         compiler_params=pltpu.CompilerParams(vmem_limit_bytes=VMEM_LIMIT),
         cost_estimate=BRIEF,
         name="hidden",
@@ -266,48 +254,59 @@
     )(hidden, down_w)
 
 
-def extra_kernel(right_ref, *refs):
-    bottom, (near_ref, far_ref) = refs[:-2], refs[-2:]
-    near = near_ref.shape[0]
+def turn_kernel(rows, near_ref, far_ref, *out_refs):
+    value = jnp.concatenate([near_ref[...].astype(F32), far_ref[...].astype(F32)], axis=1)
+    for k, out_ref in enumerate(out_refs):
+        out_ref[...] = rotated(value, rows, len(out_refs), k).astype(BF)
+
+
+def turn(near, far, parts, rows):
+    total, ranks = near.shape
+    return pl.pallas_call(
+        functools.partial(turn_kernel, rows),
+        out_shape=[jax.ShapeDtypeStruct((total, 2 * ranks), BF)] * parts,
+        cost_estimate=BRIEF,
+        name="turn",
+    )(near, far)
+
+
+def extra_kernel(chips, near_ref, far_ref, *refs):
+    bottom, own_ref, outs = refs[: -chips], refs[-chips], refs[len(refs) - chips + 1 :]
+    ranks, span = near_ref.shape[0], own_ref.shape[0]
     low = sum(ref[...].astype(F32) for ref in bottom).astype(BF)
-    value = dot_nn(low, right_ref[...])
-    near_ref[...] = value[:near]
-    far_ref[...] = value[near:].astype(BF)
-
-
-def extra_products(right, bottom):
-    total = bottom[0].shape[0]
-    block = right.shape[1]
-    return pl.pallas_call(
-        extra_kernel,
-        out_shape=[
-            jax.ShapeDtypeStruct((total // 2, block), F32),
-            jax.ShapeDtypeStruct((total // 2, block), BF),
-        ],
+    value = dot_nn(low[:, :ranks], near_ref[...]) + dot_nn(low[:, ranks:], far_ref[...])
+    own_ref[...] = value[:span]
+    for n, out_ref in enumerate(outs):
+        out_ref[...] = value[(n + 1) * span : (n + 2) * span].astype(BF)
+
+
+def extra_products(near, far, bottom, chips):
+    span = bottom[0].shape[0] // chips
+    block = near.shape[1]
+    return pl.pallas_call(
+        functools.partial(extra_kernel, chips),
+        out_shape=[jax.ShapeDtypeStruct((span, block), F32)]
+        + [jax.ShapeDtypeStruct((span, block), BF)] * (chips - 1),
         compiler_params=pltpu.CompilerParams(vmem_limit_bytes=VMEM_LIMIT),
         cost_estimate=BRIEF,
         name="extra",
-    )(right, *bottom)
+    )(near, far, *bottom)
 
 
 def fold_kernel(head, near_ref, far_ref, own_ref, *out_refs):
     span = own_ref.shape[0]
     total = near_ref[...] + far_ref[...].astype(F32)
     own_ref[...] = total[:span]
-    per = 2 if head else 1
-    for n in range(len(out_refs) // per):
+    for n in range(len(out_refs) // 2):
         line = total[(n + 1) * span : (n + 2) * span]
-        if head:
-            out_refs[2 * n][...] = line[:head].astype(BF)
-            out_refs[2 * n + 1][...] = line[head:].astype(BF)
-        else:
-            out_refs[n][...] = line.astype(BF)
+        out_refs[2 * n][...] = line[:head].astype(BF)
+        out_refs[2 * n + 1][...] = line[head:].astype(BF)
 
 
 def fold(near, far, chips, head):
     total, width = near.shape
     span = total // chips
-    cuts = [head, span - head] if head else [span]
+    cuts = [head, span - head]
     return pl.pallas_call(
         functools.partial(fold_kernel, head),
         out_shape=[jax.ShapeDtypeStruct((span, width), F32)]
@@ -390,42 +389,40 @@
     sent = attach(tokens, routes, probs, pair)
     arrived = [along_z(sent, k) for k in range(1, parts)]
     first = [along_y(sent, s) for s in range(1, chips)]
-    gate_w = jnp.swapaxes(w_gate, 1, 2).reshape(hid, width)
-    up_w = jnp.swapaxes(w_up, 1, 2).reshape(hid, width)
-    gate_w, up_w, gate_left, up_left = load(
-        *after((gate_w, up_w, gate_left, up_left), first)
-    )
-    small = cut((gate_right, up_right, down_left), parts)
-    rest = after(jnp.concatenate(arrived), (gate_w, up_w, small))
+    left, *small = cut((gate_right, up_right, down_left), (gate_left, up_left), parts)
+    rest = after(jnp.concatenate(arrived), (left, small))
     lines = [jnp.concatenate([sent, rest])]
     partner = [other_core(lines[0])]
-    down_w, right = load(*after((w_down.reshape(hid, width), down_right), rest))
     small = after(tuple(small), rest)
     small = [small[0]] + [along_z(small[k], k) for k in range(1, parts)]
+    right = after(down_right.reshape(ranks, block), rest)
+    partner_right = other_core(right)
     for s in range(1, chips):
         line = jnp.concatenate([first[s - 1], along_y(rest, s)])
-        line = after(line, (down_w, tuple(small)))
+        line = after(line, (tuple(small), partner_right))
         lines.append(line)
         partner.append(other_core(line))
     lines += partner
     diag = spread(small, parts, exp_dev)
 
-    inner = inner_products(lines, gate_left, up_left, parts, rows)
+    inner = inner_products(lines, left, parts, rows)
     inner = [inner[0]] + [along_z(inner[k], k) for k in range(1, parts)]
+    gate_w = jnp.swapaxes(w_gate, 1, 2).reshape(hid, width)
+    up_w = jnp.swapaxes(w_up, 1, 2).reshape(hid, width)
     raw = raw_products(lines, gate_w, up_w)
     first_expert = (me_g * exp_dev)[None]
-    hidden, *bottom = hidden_units(
-        first_expert, lines, inner, raw, diag, parts, rows, exp_dev, pair
+    hidden, near, far = hidden_units(
+        first_expert, lines, inner, raw, diag, parts, exp_dev, pair
     )
+    swapped = other_core(far)
+    bottom = turn(near, swapped, parts, rows)
     bottom = [bottom[0]] + [along_z(bottom[k], k) for k in range(1, parts)]
 
-    near, far = down_products(hidden, down_w)
-    out, *others = fold(near, other_core(far), chips, rows)
+    near, far = down_products(hidden, w_down.reshape(hid, width))
+    out, *others = fold(near, other_core(after(far, swapped)), chips, rows)
     backs = [along_y(others[2 * s - 1], -s) for s in range(1, chips)]
 
-    bottom = after(tuple(bottom), out)
-    near, far = extra_products(right.reshape(ranks, block), bottom)
-    low, *lows = fold(near, other_core(far), chips, 0)
+    low, *lows = extra_products(right, partner_right, bottom, chips)
     lows = [along_y(lows[s - 1], -s) for s in range(1, chips)]
 
     heads = [along_y(after(others[2 * s - 2], backs[s - 1]), -s) for s in range(1, chips)]

time: 80.4 us -> 71.2 us (0.89)
  local copies, waits for them, and re-layouts: 14.1 us -> 1.83 us
  waiting for transfers between devices: 11.9 us -> 17.5 us
  Pallas kernels: 21.3 us -> 19.2 us
  starting transfers between devices: 31.7 us -> 30.3 us
  other arithmetic: 0.73 us -> 1.62 us
    unnamed x30 -> x22, local copies, waits for them, and re-layouts: 14.1 us -> 1.83 us
    ppermute x15, waiting for transfers between devices: 4.94 us -> 12.1 us  [along_z(): lax.ppermute(value, 'mp', [(i, (i + step) % parts) for i in range(parts)])]
    ppermute x5, waiting for transfers between devices: 5.78 us -> 2.25 us  [along_y(): lax.ppermute(value, 'y', [(i, (i + step) % chips) for i in range(chips)])]
    ppermute x5, starting transfers between devices: 7.97 us -> 5.78 us  [along_y(): lax.ppermute(value, 'y', [(i, (i + step) % chips) for i in range(chips)])]
    ppermute x4 -> x5, waiting for transfers between devices: 1.18 us -> 3.2 us  [other_core(): return lax.ppermute(value, 'core', [(0, 1), (1, 0)])]
    pallas_call x5 -> x4, Pallas kernels: 13.5 us -> 11.9 us  [the longest x1 9.76 us: raw_products(): pl.pallas_call(functools.partial(raw_kernel, len(lines), tiles), in_specs...]
    concatenate x1, other arithmetic: 0.02 us -> 0.9 us  [local(): lines = [jnp.concatenate([sent, rest])]]
  transfers between devices with their start and end apart: 24 -> 25, of which waited for: 9 -> 12; matrix products, arithmetic and copies ran while one was open for 0% -> 1% of each run, Pallas kernels for 20% -> 24%
where the time goes in v8:
time: 71.2 us; the launch traced here: 70.7 us
  starting transfers between devices  30.3 us (43%)
  Pallas kernels  19.2 us (27%)
  waiting for transfers between devices  17.5 us (25%)
  local copies, waits for them, and re-layouts  1.83 us (3%)
  other arithmetic  1.62 us (2%)
    ppermute x15, starting transfers between devices, along_z(): lax.ppermute(value, 'mp', [(i, (i + step) % parts) for i in range(parts)])  23.5 us
    ppermute x15, waiting for transfers between devices, along_z(): lax.ppermute(value, 'mp', [(i, (i + step) % parts) for i in range(parts)])  12.1 us
    pallas_call x1, Pallas kernels, raw_products(): pl.pallas_call(functools.partial(raw_kernel, len(lines), tiles), in_specs...  9.76 us
    ppermute x5, starting transfers between devices, along_y(): lax.ppermute(value, 'y', [(i, (i + step) % chips) for i in range(chips)])  5.78 us
    ppermute x5, waiting for transfers between devices, other_core(): return lax.ppermute(value, 'core', [(0, 1), (1, 0)])  3.2 us
    ppermute x5, waiting for transfers between devices, along_y(): lax.ppermute(value, 'y', [(i, (i + step) % chips) for i in range(chips)])  2.25 us
    pallas_call x1, Pallas kernels, cut(): pl.pallas_call(functools.partial(cut_kernel, parts), out_shape=[jax.Shape...  2.23 us
    pallas_call x1, Pallas kernels, spread(): pl.pallas_call(functools.partial(spread_kernel, parts, exp_dev), out_shap...  2.06 us
  transfers between devices with their start and end apart: 25, of which 12 were waited for; matrix products, arithmetic and copies ran while one was open for 1% of the time, Pallas kernels for 24%

profile of v8, /device:TPU:0, one launch (start us, length us, event | category | flops | bytes accessed | tf_op | source)
XLA Modules:
  0.0 70.7 jit_solution(1715567886562117968)
XLA Ops:
  0.0 1.6 %attach.1 = bf16[8,4224]{1,0:T(8,128)(2,1)} custom-call(bf16[8,4096]{1,0:T(8,128)(2,1)} %tokens_ref.1, s32[8,8]{1,0:T(8,128)} %routes_ref.1, f32[8,8]{1,0:T(8,128)} %probs_ref.1), custom_call_target="tpu_custom_call" | custom-call | flops 1 | bytes 1 | tf_op jit(solution)/shard_map/attach/pallas_call | solution.py:61
  1.6 5.0 %collective-permute-start.2 = (bf16[8,4224]{1,0:T(8,128)(2,1)}, bf16[8,4224]{1,0:T(8,128)(2,1)S(1)}, u32[]{:S(2)}, u32[]{:S(2)}) collective-permute-start(bf16[8,4224]{1,0:T(8,128)(2,1)} %attach.1), channel_id=1, source_target_pairs={{0,3},{1,0},{2,1},{3,2},{4,7},{5,4},{6,5},{7,6},{8,11},{9,8},{10,9... | collective-permute-start | bytes 202760 | tf_op jit(solution)/shard_map/ppermute | solution.py:380
  6.6 1.0 %collective-permute-start = (bf16[8,4224]{1,0:T(8,128)(2,1)}, bf16[8,4224]{1,0:T(8,128)(2,1)S(1)}, u32[]{:S(2)}, u32[]{:S(2)}) collective-permute-start(bf16[8,4224]{1,0:T(8,128)(2,1)} %attach.1), channel_id=1, source_target_pairs={{0,1},{1,2},{2,3},{3,0},{4,5},{5,6},{6,7},{7,4},{8,9},{9,10},{10,1... | collective-permute-start | bytes 202760 | tf_op jit(solution)/shard_map/ppermute | solution.py:380
  7.6 1.5 %collective-permute-start.3 = (bf16[8,4224]{1,0:T(8,128)(2,1)}, bf16[8,4224]{1,0:T(8,128)(2,1)S(1)}, u32[]{:S(2)}, u32[]{:S(2)}) collective-permute-start(bf16[8,4224]{1,0:T(8,128)(2,1)} %attach.1), channel_id=1, source_target_pairs={{0,8},{8,0},{1,9},{9,1},{2,10},{10,2},{3,11},{11,3},{4,12},{12,4},... | collective-permute-start | bytes 202760 | tf_op jit(solution)/shard_map/ppermute | solution.py:383
  9.2 2.2 %cut.1 = (bf16[256,1024]{1,0:T(8,128)(2,1)}, bf16[3,32,192]{2,1,0:T(8,128)(2,1)}, bf16[3,32,192]{2,1,0:T(8,128)(2,1)}, bf16[3,32,192]{2,1,0:T(8,128)(2,1)}, bf16[3,32,192]{2,1,0:T(8,128)(2,1)}) custom-call(bf16[4,8,768]{2,1,0:T(8,128)(2,1)} %refs_0_.1, bf16[4,8,768]{2,1,0:T(8,128)(2,1)} %refs_1_.1, bf16[4,8,768]{2,1,0:T(8,128)(2,1)} %refs_2_.1, ...), custom_call_target="tpu_custom_call" | custom-call | flops 1 | bytes 1 | tf_op jit(solution)/shard_map/cut/pallas_call | solution.py:91
  11.4 2.1 %collective-permute-done.1 = bf16[8,4224]{1,0:T(8,128)(2,1)S(1)} collective-permute-done((bf16[8,4224]{1,0:T(8,128)(2,1)}, bf16[8,4224]{1,0:T(8,128)(2,1)S(1)}, u32[]{:S(2)}, u32[]{:S(2)}) %collective-permute-start.1) | collective-permute-done | bytes 67616 | tf_op jit(solution)/shard_map/ppermute | solution.py:380
  13.5 1.6 %collective-permute-start.4 = (bf16[24,4224]{1,0:T(8,128)(2,1)S(1)}, bf16[24,4224]{1,0:T(8,128)(2,1)S(1)}, u32[]{:S(2)}, u32[]{:S(2)}) collective-permute-start(bf16[24,4224]{1,0:T(8,128)(2,1)S(1)} %pad_maximum_fusion.2), channel_id=1, source_target_pairs={{0,8},{8,0},{1,9},{9,1},{2,10},{10,2},{3,11},{11,3},{4,12},{12,4},... | collective-permute-start | bytes 608264 | tf_op jit(solution)/shard_map/ppermute | solution.py:383
  15.1 0.9 %pad_maximum_fusion.refs_0_ = bf16[32,4224]{1,0:T(8,128)(2,1)S(1)} fusion(bf16[24,4224]{1,0:T(8,128)(2,1)S(1)} %pad_maximum_fusion.2, bf16[8,4224]{1,0:T(8,128)(2,1)} %attach.1), kind=kLoop, calls=%fused_computation | loop fusion | flops 540672 | bytes 540672 | tf_op jit(solution)/shard_map/concatenate | solution.py:394
  16.2 2.3 %collective-permute-start.6 = (bf16[3,32,192]{2,1,0:T(8,128)(2,1)}, bf16[3,32,192]{2,1,0:T(8,128)(2,1)S(1)}, u32[]{:S(2)}, u32[]{:S(2)}) collective-permute-start(bf16[3,32,192]{2,1,0:T(8,128)(2,1)} %get-tuple-element.51), channel_id=1, source_target_pairs={{0,2},{1,3},{2,0},{3,1},{4,6},{5,7},{6,4},{7,5},{8,10},{9,11},{10,... | collective-permute-start | bytes 110600 | tf_op jit(solution)/shard_map/ppermute | solution.py:380
  18.5 2.3 %collective-permute-start.7 = (bf16[3,32,192]{2,1,0:T(8,128)(2,1)}, bf16[3,32,192]{2,1,0:T(8,128)(2,1)S(1)}, u32[]{:S(2)}, u32[]{:S(2)}) collective-permute-start(bf16[3,32,192]{2,1,0:T(8,128)(2,1)} %get-tuple-element.52), channel_id=1, source_target_pairs={{0,3},{1,0},{2,1},{3,2},{4,7},{5,4},{6,5},{7,6},{8,11},{9,8},{10,9... | collective-permute-start | bytes 110600 | tf_op jit(solution)/shard_map/ppermute | solution.py:380
  21.3 1.1 %collective-permute-done.5.refs_1_ = bf16[3,32,192]{2,1,0:T(8,128)(2,1)S(1)} collective-permute-done((bf16[3,32,192]{2,1,0:T(8,128)(2,1)}, bf16[3,32,192]{2,1,0:T(8,128)(2,1)S(1)}, u32[]{:S(2)}, u32[]{:S(2)}) %collective-permute-start.5) | collective-permute-done | bytes 36896 | tf_op jit(solution)/shard_map/ppermute | solution.py:380
  22.4 0.7 collective-permute-done.6.refs_2_
  23.2 1.5 %collective-permute-done.10.refs_3_ = bf16[32,4224]{1,0:T(8,128)(2,1)S(1)} collective-permute-done((bf16[32,4224]{1,0:T(8,128)(2,1)S(1)}, bf16[32,4224]{1,0:T(8,128)(2,1)S(1)}, u32[]{:S(2)}, u32[]{:S(2)}) %collective-permute-start.10) | collective-permute-done | bytes 270368 | tf_op jit(solution)/shard_map/ppermute | solution.py:386
  24.7 1.0 %copy-done.1 = bf16[256,1024]{1,0:T(8,128)(2,1)S(1)} copy-done((bf16[256,1024]{1,0:T(8,128)(2,1)S(1)}, bf16[256,1024]{1,0:T(8,128)(2,1)}, u32[]{:S(2)}) %copy-start.1) | copy-done | bytes 524312
  26.1 1.6 %collective-permute-start.11 = (bf16[128,256]{1,0:T(8,128)(2,1)S(1)}, bf16[128,256]{1,0:T(8,128)(2,1)S(1)}, u32[]{:S(2)}, u32[]{:S(2)}) collective-permute-start(bf16[128,256]{1,0:T(8,128)(2,1)S(1)} %get-tuple-element.56), channel_id=1, source_target_pairs={{0,1},{1,2},{2,3},{3,0},{4,5},{5,6},{6,7},{7,4},{8,9},{9,10},{10,1... | collective-permute-start | bytes 196616 | tf_op jit(solution)/shard_map/ppermute | solution.py:380
  27.7 2.6 %collective-permute-start.12 = (bf16[128,256]{1,0:T(8,128)(2,1)S(1)}, bf16[128,256]{1,0:T(8,128)(2,1)S(1)}, u32[]{:S(2)}, u32[]{:S(2)}) collective-permute-start(bf16[128,256]{1,0:T(8,128)(2,1)S(1)} %get-tuple-element.57), channel_id=1, source_target_pairs={{0,2},{1,3},{2,0},{3,1},{4,6},{5,7},{6,4},{7,5},{8,10},{9,11},{10,... | collective-permute-start | bytes 196616 | tf_op jit(solution)/shard_map/ppermute | solution.py:380
  30.4 2.1 %spread.1.refs_10_ = bf16[3,128,768]{2,1,0:T(8,128)(2,1)} custom-call(bf16[3,32,192]{2,1,0:T(8,128)(2,1)} %get-tuple-element.49.refs_0_, bf16[3,32,192]{2,1,0:T(8,128)(2,1)} %copy-done.5, bf16[3,32,192]{2,1,0:T(8,128)(2,1)} %copy-done.6, bf16[3,32,192]{2,1,0:T(8,128)(2,1)} %copy-done.7), custom_call_target="tpu_custom_call" | custom-call | flops 1 | bytes 1 | tf_op jit(solution)/shard_map/spread/pallas_call | solution.py:123
  32.4 9.8 %raw.1 = (f32[128,768]{1,0:T(8,128)S(1)}, f32[128,768]{1,0:T(8,128)S(1)}) custom-call(bf16[32,4224]{1,0:T(8,128)(2,1)S(1)} %pad_maximum_fusion.refs_0_, bf16[32,4224]{1,0:T(8,128)(2,1)S(1)} %pad_maximum_fusion.1.refs_1_, bf16[32,4224]{1,0:T(8,128)(2,1)S(1)} %collective-permute-done.9.refs_2_, bf16[32,4224]{1,0:T(8,128)(2,1)S(1)} %collective-permute-done.10.refs_3_, ...), custom_call_target="tpu_custom_call" | custom-call | flops 1 | bytes 1 | tf_op jit(solution)/shard_map/raw/pallas_call | solution.py:180
  42.9 1.0 %down.1 = (f32[64,4096]{1,0:T(8,128)S(1)}, bf16[64,4096]{1,0:T(8,128)(2,1)S(1)}) custom-call(bf16[128,768]{1,0:T(8,128)(2,1)S(1)} %get-tuple-element.61.hidden_ref, bf16[768,4096]{1,0:T(8,128)(2,1)S(1)} %bitcast.11), custom_call_target="tpu_custom_call" | custom-call | flops 1 | bytes 1 | tf_op jit(solution)/shard_map/down/pallas_call | solution.py:245
  44.5 1.5 %collective-permute-done.15.far_ref = bf16[64,4096]{1,0:T(8,128)(2,1)S(1)} collective-permute-done((bf16[64,4096]{1,0:T(8,128)(2,1)S(1)}, bf16[64,4096]{1,0:T(8,128)(2,1)S(1)}, u32[]{:S(2)}, u32[]{:S(2)}) %collective-permute-start.15) | collective-permute-done | bytes 524320 | tf_op jit(solution)/shard_map/ppermute | solution.py:386
  46.7 1.4 %turn.1 = (bf16[64,256]{1,0:T(8,128)(2,1)}, bf16[64,256]{1,0:T(8,128)(2,1)}, bf16[64,256]{1,0:T(8,128)(2,1)}, bf16[64,256]{1,0:T(8,128)(2,1)}) custom-call(bf16[64,128]{1,0:T(8,128)(2,1)} %copy-done.4, bf16[64,128]{1,0:T(8,128)(2,1)} %copy-done.8), custom_call_target="tpu_custom_call" | custom-call | flops 1 | bytes 1 | tf_op jit(solution)/shard_map/turn/pallas_call | solution.py:265
  48.1 2.0 %collective-permute-start.16 = (bf16[64,256]{1,0:T(8,128)(2,1)}, bf16[64,256]{1,0:T(8,128)(2,1)S(1)}, u32[]{:S(2)}, u32[]{:S(2)}) collective-permute-start(bf16[64,256]{1,0:T(8,128)(2,1)} %get-tuple-element.69), channel_id=1, source_target_pairs={{0,1},{1,2},{2,3},{3,0},{4,5},{5,6},{6,7},{7,4},{8,9},{9,10},{10,1... | collective-permute-start | bytes 98312 | tf_op jit(solution)/shard_map/ppermute | solution.py:380
  50.4 2.3 %collective-permute-start.18 = (bf16[64,256]{1,0:T(8,128)(2,1)}, bf16[64,256]{1,0:T(8,128)(2,1)S(1)}, u32[]{:S(2)}, u32[]{:S(2)}) collective-permute-start(bf16[64,256]{1,0:T(8,128)(2,1)} %get-tuple-element.71), channel_id=1, source_target_pairs={{0,3},{1,0},{2,1},{3,2},{4,7},{5,4},{6,5},{7,6},{8,11},{9,8},{10,9... | collective-permute-start | bytes 98312 | tf_op jit(solution)/shard_map/ppermute | solution.py:380
  52.6 1.4 %collective-permute-done.16.refs_1_ = bf16[64,256]{1,0:T(8,128)(2,1)S(1)} collective-permute-done((bf16[64,256]{1,0:T(8,128)(2,1)}, bf16[64,256]{1,0:T(8,128)(2,1)S(1)}, u32[]{:S(2)}, u32[]{:S(2)}) %collective-permute-start.16) | collective-permute-done | bytes 32800 | tf_op jit(solution)/shard_map/ppermute | solution.py:380
  54.0 1.4 %collective-permute-done.17.refs_2_ = bf16[64,256]{1,0:T(8,128)(2,1)S(1)} collective-permute-done((bf16[64,256]{1,0:T(8,128)(2,1)}, bf16[64,256]{1,0:T(8,128)(2,1)S(1)}, u32[]{:S(2)}, u32[]{:S(2)}) %collective-permute-start.17) | collective-permute-done | bytes 32800 | tf_op jit(solution)/shard_map/ppermute | solution.py:380
  55.4 0.8 %copy-done.3 = bf16[64,256]{1,0:T(8,128)(2,1)S(1)} copy-done((bf16[64,256]{1,0:T(8,128)(2,1)S(1)}, bf16[64,256]{1,0:T(8,128)(2,1)}, u32[]{:S(2)}) %copy-start.3) | copy-done | bytes 32792
  56.4 1.6 %collective-permute-start.20 = (bf16[32,1024]{1,0:T(8,128)(2,1)S(1)}, bf16[32,1024]{1,0:T(8,128)(2,1)S(1)}, u32[]{:S(2)}, u32[]{:S(2)}) collective-permute-start(bf16[32,1024]{1,0:T(8,128)(2,1)S(1)} %get-tuple-element.74), channel_id=1, source_target_pairs={{0,8},{8,0},{1,9},{9,1},{2,10},{10,2},{3,11},{11,3},{4,12},{12,4},... | collective-permute-start | bytes 196616 | tf_op jit(solution)/shard_map/ppermute | solution.py:383
  58.5 2.2 %collective-permute-done.20.refs_1_ = bf16[32,1024]{1,0:T(8,128)(2,1)S(1)} collective-permute-done((bf16[32,1024]{1,0:T(8,128)(2,1)S(1)}, bf16[32,1024]{1,0:T(8,128)(2,1)S(1)}, u32[]{:S(2)}, u32[]{:S(2)}) %collective-permute-start.20) | collective-permute-done | bytes 65568 | tf_op jit(solution)/shard_map/ppermute | solution.py:383
  60.8 3.2 %collective-permute-start.22 = (bf16[8,4096]{1,0:T(8,128)(2,1)S(1)}, bf16[8,4096]{1,0:T(8,128)(2,1)S(1)}, u32[]{:S(2)}, u32[]{:S(2)}) collective-permute-start(bf16[8,4096]{1,0:T(8,128)(2,1)S(1)} %get-tuple-element.78), channel_id=1, source_target_pairs={{0,3},{1,0},{2,1},{3,2},{4,7},{5,4},{6,5},{7,6},{8,11},{9,8},{10,9... | collective-permute-start | bytes 196616 | tf_op jit(solution)/shard_map/ppermute | solution.py:380
  64.7 1.5 %collective-permute-done.22 = bf16[8,4096]{1,0:T(8,128)(2,1)S(1)} collective-permute-done((bf16[8,4096]{1,0:T(8,128)(2,1)S(1)}, bf16[8,4096]{1,0:T(8,128)(2,1)S(1)}, u32[]{:S(2)}, u32[]{:S(2)}) %collective-permute-start.22) | collective-permute-done | bytes 65568 | tf_op jit(solution)/shard_map/ppermute | solution.py:380
  66.2 3.0 %collective-permute-done.23 = bf16[8,4096]{1,0:T(8,128)(2,1)S(1)} collective-permute-done((bf16[8,4096]{1,0:T(8,128)(2,1)S(1)}, bf16[8,4096]{1,0:T(8,128)(2,1)S(1)}, u32[]{:S(2)}, u32[]{:S(2)}) %collective-permute-start.23) | collective-permute-done | bytes 65568 | tf_op jit(solution)/shard_map/ppermute | solution.py:380
  69.2 0.9 %collective-permute-done.24 = bf16[8,4096]{1,0:T(8,128)(2,1)S(1)} collective-permute-done((bf16[8,4096]{1,0:T(8,128)(2,1)S(1)}, bf16[8,4096]{1,0:T(8,128)(2,1)S(1)}, u32[]{:S(2)}, u32[]{:S(2)}) %collective-permute-start.24) | collective-permute-done | bytes 65568 | tf_op jit(solution)/shard_map/ppermute | solution.py:380
  (56 shorter events, 5.4 us)
Async XLA Ops:
  1.6 9.8 %collective-permute-start.2 = (bf16[8,4224]{1,0:T(8,128)(2,1)}, bf16[8,4224]{1,0:T(8,128)(2,1)S(1)}, u32[]{:S(2)}, u32[]{:S(2)}) collective-permute-start(bf16[8,4224]{1,0:T(8,128)(2,1)} %attach.1), channel_id=1, source_target_pairs={{0,3},{1,0},{2,1},{3,2},{4,7},{5,4},{6,5},{7,6},{8,11},{9,8},{10,9... | collective-permute-start | bytes 202760 | tf_op jit(solution)/shard_map/ppermute | solution.py:380
  6.6 6.9 %collective-permute-start.1 = (bf16[8,4224]{1,0:T(8,128)(2,1)}, bf16[8,4224]{1,0:T(8,128)(2,1)S(1)}, u32[]{:S(2)}, u32[]{:S(2)}) collective-permute-start(bf16[8,4224]{1,0:T(8,128)(2,1)} %attach.1), channel_id=1, source_target_pairs={{0,2},{1,3},{2,0},{3,1},{4,6},{5,7},{6,4},{7,5},{8,10},{9,11},{10,... | collective-permute-start | bytes 202760 | tf_op jit(solution)/shard_map/ppermute | solution.py:380
  6.6 6.9 %collective-permute-start = (bf16[8,4224]{1,0:T(8,128)(2,1)}, bf16[8,4224]{1,0:T(8,128)(2,1)S(1)}, u32[]{:S(2)}, u32[]{:S(2)}) collective-permute-start(bf16[8,4224]{1,0:T(8,128)(2,1)} %attach.1), channel_id=1, source_target_pairs={{0,1},{1,2},{2,3},{3,0},{4,5},{5,6},{6,7},{7,4},{8,9},{9,10},{10,1... | collective-permute-start | bytes 202760 | tf_op jit(solution)/shard_map/ppermute | solution.py:380
  7.6 13.1 %collective-permute-start.3 = (bf16[8,4224]{1,0:T(8,128)(2,1)}, bf16[8,4224]{1,0:T(8,128)(2,1)S(1)}, u32[]{:S(2)}, u32[]{:S(2)}) collective-permute-start(bf16[8,4224]{1,0:T(8,128)(2,1)} %attach.1), channel_id=1, source_target_pairs={{0,8},{8,0},{1,9},{9,1},{2,10},{10,2},{3,11},{11,3},{4,12},{12,4},... | collective-permute-start | bytes 202760 | tf_op jit(solution)/shard_map/ppermute | solution.py:383
  13.5 7.2 %collective-permute-start.4 = (bf16[24,4224]{1,0:T(8,128)(2,1)S(1)}, bf16[24,4224]{1,0:T(8,128)(2,1)S(1)}, u32[]{:S(2)}, u32[]{:S(2)}) collective-permute-start(bf16[24,4224]{1,0:T(8,128)(2,1)S(1)} %pad_maximum_fusion.2), channel_id=1, source_target_pairs={{0,8},{8,0},{1,9},{9,1},{2,10},{10,2},{3,11},{11,3},{4,12},{12,4},... | collective-permute-start | bytes 608264 | tf_op jit(solution)/shard_map/ppermute | solution.py:383
  16.0 6.4 %collective-permute-start.5 = (bf16[3,32,192]{2,1,0:T(8,128)(2,1)}, bf16[3,32,192]{2,1,0:T(8,128)(2,1)S(1)}, u32[]{:S(2)}, u32[]{:S(2)}) collective-permute-start(bf16[3,32,192]{2,1,0:T(8,128)(2,1)} %get-tuple-element.50), channel_id=1, source_target_pairs={{0,1},{1,2},{2,3},{3,0},{4,5},{5,6},{6,7},{7,4},{8,9},{9,10},{10,1... | collective-permute-start | bytes 110600 | tf_op jit(solution)/shard_map/ppermute | solution.py:380
  16.2 6.9 %collective-permute-start.6 = (bf16[3,32,192]{2,1,0:T(8,128)(2,1)}, bf16[3,32,192]{2,1,0:T(8,128)(2,1)S(1)}, u32[]{:S(2)}, u32[]{:S(2)}) collective-permute-start(bf16[3,32,192]{2,1,0:T(8,128)(2,1)} %get-tuple-element.51), channel_id=1, source_target_pairs={{0,2},{1,3},{2,0},{3,1},{4,6},{5,7},{6,4},{7,5},{8,10},{9,11},{10,... | collective-permute-start | bytes 110600 | tf_op jit(solution)/shard_map/ppermute | solution.py:380
  18.5 4.6 %collective-permute-start.7 = (bf16[3,32,192]{2,1,0:T(8,128)(2,1)}, bf16[3,32,192]{2,1,0:T(8,128)(2,1)S(1)}, u32[]{:S(2)}, u32[]{:S(2)}) collective-permute-start(bf16[3,32,192]{2,1,0:T(8,128)(2,1)} %get-tuple-element.52), channel_id=1, source_target_pairs={{0,3},{1,0},{2,1},{3,2},{4,7},{5,4},{6,5},{7,6},{8,11},{9,8},{10,9... | collective-permute-start | bytes 110600 | tf_op jit(solution)/shard_map/ppermute | solution.py:380
  20.7 2.4 %collective-permute-start.8 = (bf16[128,1024]{1,0:T(8,128)(2,1)}, bf16[128,1024]{1,0:T(8,128)(2,1)S(1)}, u32[]{:S(2)}, u32[]{:S(2)}) collective-permute-start(bf16[128,1024]{1,0:T(8,128)(2,1)} %bitcast.12), channel_id=1, source_target_pairs={{0,4},{4,0},{1,5},{5,1},{2,6},{6,2},{3,7},{7,3},{8,12},{12,8},{9,1... | collective-permute-start | bytes 786440 | tf_op jit(solution)/shard_map/ppermute | solution.py:386
  20.7 2.4 %collective-permute-start.9 = (bf16[32,4224]{1,0:T(8,128)(2,1)S(1)}, bf16[32,4224]{1,0:T(8,128)(2,1)S(1)}, u32[]{:S(2)}, u32[]{:S(2)}) collective-permute-start(bf16[32,4224]{1,0:T(8,128)(2,1)S(1)} %pad_maximum_fusion.refs_0_), channel_id=1, source_target_pairs={{0,4},{4,0},{1,5},{5,1},{2,6},{6,2},{3,7},{7,3},{8,12},{12,8},{9,1... | collective-permute-start | bytes 811016 | tf_op jit(solution)/shard_map/ppermute | solution.py:386
  22.4 7.9 %copy-start.5 = (bf16[3,32,192]{2,1,0:T(8,128)(2,1)}, bf16[3,32,192]{2,1,0:T(8,128)(2,1)S(1)}, u32[]{:S(2)}) copy-start(bf16[3,32,192]{2,1,0:T(8,128)(2,1)S(1)} %collective-permute-done.5.refs_1_) | copy-start | bytes 110596
  23.1 7.3 %copy-start.6 = (bf16[3,32,192]{2,1,0:T(8,128)(2,1)}, bf16[3,32,192]{2,1,0:T(8,128)(2,1)S(1)}, u32[]{:S(2)}) copy-start(bf16[3,32,192]{2,1,0:T(8,128)(2,1)S(1)} %collective-permute-done.6.refs_2_) | copy-start | bytes 110596
  23.1 7.3 %copy-start.7 = (bf16[3,32,192]{2,1,0:T(8,128)(2,1)}, bf16[3,32,192]{2,1,0:T(8,128)(2,1)S(1)}, u32[]{:S(2)}) copy-start(bf16[3,32,192]{2,1,0:T(8,128)(2,1)S(1)} %collective-permute-done.7.refs_3_) | copy-start | bytes 110596
  23.1 1.6 %collective-permute-start.10 = (bf16[32,4224]{1,0:T(8,128)(2,1)S(1)}, bf16[32,4224]{1,0:T(8,128)(2,1)S(1)}, u32[]{:S(2)}, u32[]{:S(2)}) collective-permute-start(bf16[32,4224]{1,0:T(8,128)(2,1)S(1)} %pad_maximum_fusion.1.refs_1_), channel_id=1, source_target_pairs={{0,4},{4,0},{1,5},{5,1},{2,6},{6,2},{3,7},{7,3},{8,12},{12,8},{9,1... | collective-permute-start | bytes 811016 | tf_op jit(solution)/shard_map/ppermute | solution.py:386
  26.1 16.1 %collective-permute-start.11 = (bf16[128,256]{1,0:T(8,128)(2,1)S(1)}, bf16[128,256]{1,0:T(8,128)(2,1)S(1)}, u32[]{:S(2)}, u32[]{:S(2)}) collective-permute-start(bf16[128,256]{1,0:T(8,128)(2,1)S(1)} %get-tuple-element.56), channel_id=1, source_target_pairs={{0,1},{1,2},{2,3},{3,0},{4,5},{5,6},{6,7},{7,4},{8,9},{9,10},{10,1... | collective-permute-start | bytes 196616 | tf_op jit(solution)/shard_map/ppermute | solution.py:380
  27.7 14.5 %collective-permute-start.12 = (bf16[128,256]{1,0:T(8,128)(2,1)S(1)}, bf16[128,256]{1,0:T(8,128)(2,1)S(1)}, u32[]{:S(2)}, u32[]{:S(2)}) collective-permute-start(bf16[128,256]{1,0:T(8,128)(2,1)S(1)} %get-tuple-element.57), channel_id=1, source_target_pairs={{0,2},{1,3},{2,0},{3,1},{4,6},{5,7},{6,4},{7,5},{8,10},{9,11},{10,... | collective-permute-start | bytes 196616 | tf_op jit(solution)/shard_map/ppermute | solution.py:380
  30.3 11.9 %collective-permute-start.13 = (bf16[128,256]{1,0:T(8,128)(2,1)S(1)}, bf16[128,256]{1,0:T(8,128)(2,1)S(1)}, u32[]{:S(2)}, u32[]{:S(2)}) collective-permute-start(bf16[128,256]{1,0:T(8,128)(2,1)S(1)} %get-tuple-element.58), channel_id=1, source_target_pairs={{0,3},{1,0},{2,1},{3,2},{4,7},{5,4},{6,5},{7,6},{8,11},{9,8},{10,9... | collective-permute-start | bytes 196616 | tf_op jit(solution)/shard_map/ppermute | solution.py:380
  32.4 10.4 %slice-start = ((s8[6291456]{0:T(1024)(128)(4,1)}), s8[4194304]{0:T(1024)(128)(4,1)S(1)}, s32[]{:S(2)}) async-start(s8[6291456]{0:T(1024)(128)(4,1)} %bitcast.9), calls=%async_computation | async-start | bytes 8388608
  32.4 9.8 %copy-start = (bf16[3,128,768]{2,1,0:T(8,128)(2,1)S(1)}, bf16[3,128,768]{2,1,0:T(8,128)(2,1)}, u32[]{:S(2)}) copy-start(bf16[3,128,768]{2,1,0:T(8,128)(2,1)} %spread.1.refs_10_) | copy-start | bytes 1769476
  32.4 10.5 %slice-start.1 = ((s8[6291456]{0:T(1024)(128)(4,1)}), s8[2097152]{0:T(1024)(128)(4,1)S(1)}, s32[]{:S(2)}) async-start(s8[6291456]{0:T(1024)(128)(4,1)} %bitcast.9), calls=%async_computation.1 | async-start | bytes 4194304
  42.2 13.2 %copy-start.2 = (bf16[4,32,1024]{2,1,0:T(8,128)(2,1)S(1)}, bf16[4,32,1024]{2,1,0:T(8,128)(2,1)}, u32[]{:S(2)}) copy-start(bf16[4,32,1024]{2,1,0:T(8,128)(2,1)} %param.23) | copy-start | bytes 786436
  42.8 1.2 %collective-permute-start.14 = (bf16[64,128]{1,0:T(8,128)(2,1)S(1)}, bf16[64,128]{1,0:T(8,128)(2,1)S(1)}, u32[]{:S(2)}, u32[]{:S(2)}) collective-permute-start(bf16[64,128]{1,0:T(8,128)(2,1)S(1)} %get-tuple-element.64), channel_id=1, source_target_pairs={{0,4},{4,0},{1,5},{5,1},{2,6},{6,2},{3,7},{7,3},{8,12},{12,8},{9,1... | collective-permute-start | bytes 49160 | tf_op jit(solution)/shard_map/ppermute | solution.py:386
  44.0 2.0 %collective-permute-start.15 = (bf16[64,4096]{1,0:T(8,128)(2,1)S(1)}, bf16[64,4096]{1,0:T(8,128)(2,1)S(1)}, u32[]{:S(2)}, u32[]{:S(2)}) collective-permute-start(bf16[64,4096]{1,0:T(8,128)(2,1)S(1)} %get-tuple-element.65), channel_id=1, source_target_pairs={{0,4},{4,0},{1,5},{5,1},{2,6},{6,2},{3,7},{7,3},{8,12},{12,8},{9,1... | collective-permute-start | bytes 1572872 | tf_op jit(solution)/shard_map/ppermute | solution.py:386
  46.1 11.9 %collective-permute-start.19 = (bf16[24,4096]{1,0:T(8,128)(2,1)S(1)}, bf16[24,4096]{1,0:T(8,128)(2,1)S(1)}, u32[]{:S(2)}, u32[]{:S(2)}) collective-permute-start(bf16[24,4096]{1,0:T(8,128)(2,1)S(1)} %get-tuple-element.73), channel_id=1, source_target_pairs={{0,8},{8,0},{1,9},{9,1},{2,10},{10,2},{3,11},{11,3},{4,12},{12,4},... | collective-permute-start | bytes 589832 | tf_op jit(solution)/shard_map/ppermute | solution.py:383
  48.1 6.0 %collective-permute-start.16 = (bf16[64,256]{1,0:T(8,128)(2,1)}, bf16[64,256]{1,0:T(8,128)(2,1)S(1)}, u32[]{:S(2)}, u32[]{:S(2)}) collective-permute-start(bf16[64,256]{1,0:T(8,128)(2,1)} %get-tuple-element.69), channel_id=1, source_target_pairs={{0,1},{1,2},{2,3},{3,0},{4,5},{5,6},{6,7},{7,4},{8,9},{9,10},{10,1... | collective-permute-start | bytes 98312 | tf_op jit(solution)/shard_map/ppermute | solution.py:380
  50.1 5.3 %collective-permute-start.17 = (bf16[64,256]{1,0:T(8,128)(2,1)}, bf16[64,256]{1,0:T(8,128)(2,1)S(1)}, u32[]{:S(2)}, u32[]{:S(2)}) collective-permute-start(bf16[64,256]{1,0:T(8,128)(2,1)} %get-tuple-element.70), channel_id=1, source_target_pairs={{0,2},{1,3},{2,0},{3,1},{4,6},{5,7},{6,4},{7,5},{8,10},{9,11},{10,... | collective-permute-start | bytes 98312 | tf_op jit(solution)/shard_map/ppermute | solution.py:380
  50.4 5.0 %collective-permute-start.18 = (bf16[64,256]{1,0:T(8,128)(2,1)}, bf16[64,256]{1,0:T(8,128)(2,1)S(1)}, u32[]{:S(2)}, u32[]{:S(2)}) collective-permute-start(bf16[64,256]{1,0:T(8,128)(2,1)} %get-tuple-element.71), channel_id=1, source_target_pairs={{0,3},{1,0},{2,1},{3,2},{4,7},{5,4},{6,5},{7,6},{8,11},{9,8},{10,9... | collective-permute-start | bytes 98312 | tf_op jit(solution)/shard_map/ppermute | solution.py:380
  56.4 4.3 %collective-permute-start.20 = (bf16[32,1024]{1,0:T(8,128)(2,1)S(1)}, bf16[32,1024]{1,0:T(8,128)(2,1)S(1)}, u32[]{:S(2)}, u32[]{:S(2)}) collective-permute-start(bf16[32,1024]{1,0:T(8,128)(2,1)S(1)} %get-tuple-element.74), channel_id=1, source_target_pairs={{0,8},{8,0},{1,9},{9,1},{2,10},{10,2},{3,11},{11,3},{4,12},{12,4},... | collective-permute-start | bytes 196616 | tf_op jit(solution)/shard_map/ppermute | solution.py:383
  58.0 6.7 %collective-permute-start.21 = (bf16[8,4096]{1,0:T(8,128)(2,1)S(1)}, bf16[8,4096]{1,0:T(8,128)(2,1)S(1)}, u32[]{:S(2)}, u32[]{:S(2)}) collective-permute-start(bf16[8,4096]{1,0:T(8,128)(2,1)S(1)} %get-tuple-element.77), channel_id=1, source_target_pairs={{0,8},{8,0},{1,9},{9,1},{2,10},{10,2},{3,11},{11,3},{4,12},{12,4},... | collective-permute-start | bytes 196616 | tf_op jit(solution)/shard_map/ppermute | solution.py:383
  60.8 5.4 %collective-permute-start.22 = (bf16[8,4096]{1,0:T(8,128)(2,1)S(1)}, bf16[8,4096]{1,0:T(8,128)(2,1)S(1)}, u32[]{:S(2)}, u32[]{:S(2)}) collective-permute-start(bf16[8,4096]{1,0:T(8,128)(2,1)S(1)} %get-tuple-element.78), channel_id=1, source_target_pairs={{0,3},{1,0},{2,1},{3,2},{4,7},{5,4},{6,5},{7,6},{8,11},{9,8},{10,9... | collective-permute-start | bytes 196616 | tf_op jit(solution)/shard_map/ppermute | solution.py:380
  64.0 5.2 %collective-permute-start.23 = (bf16[8,4096]{1,0:T(8,128)(2,1)S(1)}, bf16[8,4096]{1,0:T(8,128)(2,1)S(1)}, u32[]{:S(2)}, u32[]{:S(2)}) collective-permute-start(bf16[8,4096]{1,0:T(8,128)(2,1)S(1)} %get-tuple-element.79), channel_id=1, source_target_pairs={{0,2},{1,3},{2,0},{3,1},{4,6},{5,7},{6,4},{7,5},{8,10},{9,11},{10,... | collective-permute-start | bytes 196616 | tf_op jit(solution)/shard_map/ppermute | solution.py:380
  64.0 6.1 %collective-permute-start.24 = (bf16[8,4096]{1,0:T(8,128)(2,1)S(1)}, bf16[8,4096]{1,0:T(8,128)(2,1)S(1)}, u32[]{:S(2)}, u32[]{:S(2)}) collective-permute-start(bf16[8,4096]{1,0:T(8,128)(2,1)S(1)} %get-tuple-element.80), channel_id=1, source_target_pairs={{0,1},{1,2},{2,3},{3,0},{4,5},{5,6},{6,7},{7,4},{8,9},{9,10},{10,1... | collective-permute-start | bytes 196616 | tf_op jit(solution)/shard_map/ppermute | solution.py:380
  (4 other events, 7.8 us)

commit v9 on v8

--- a/solution.py
+++ b/solution.py
@@ -9,8 +9,10 @@
 
 BF = jnp.bfloat16
 F32 = jnp.float32
-VMEM_LIMIT = 16 * 1024 * 1024
-STREAM_LIMIT = 24 * 1024 * 1024
+SMALL_LIMIT = 4 * 1024 * 1024
+VMEM_LIMIT = 12 * 1024 * 1024
+STREAM_LIMIT = 16 * 1024 * 1024
+PIECES = 4
 BRIEF = pl.CostEstimate(flops=1, bytes_accessed=1, transcendentals=0)
 
 
@@ -61,6 +63,7 @@
     return pl.pallas_call(
         attach_kernel,
         out_shape=jax.ShapeDtypeStruct((rows, width + pair), BF),
+        compiler_params=pltpu.CompilerParams(vmem_limit_bytes=SMALL_LIMIT),
         cost_estimate=BRIEF,
         name="attach",
     )(*in_hbm(tokens, routes, probs))
@@ -92,6 +95,7 @@
         functools.partial(cut_kernel, parts),
         out_shape=[jax.ShapeDtypeStruct((2 * exp_dev * rank, block), BF)]
         + [jax.ShapeDtypeStruct((3, exp_dev * piece, hid // parts), BF)] * parts,
+        compiler_params=pltpu.CompilerParams(vmem_limit_bytes=SMALL_LIMIT),
         cost_estimate=BRIEF,
         name="cut",
     )(*in_hbm(*factors, *lefts))
@@ -123,6 +127,7 @@
     return pl.pallas_call(
         functools.partial(spread_kernel, parts, exp_dev),
         out_shape=jax.ShapeDtypeStruct((3, span * parts, cols * exp_dev), BF),
+        compiler_params=pltpu.CompilerParams(vmem_limit_bytes=SMALL_LIMIT),
         cost_estimate=BRIEF,
         name="spread",
     )(*pieces)
@@ -150,44 +155,64 @@
     )(*lines, left)
 
 
-def raw_kernel(count, tiles, *refs):
-    lines, weights, outs = refs[:count], refs[count : count + 2], refs[count + 2 : count + 4]
-    scratch, sems = refs[count + 4 : count + 6], refs[count + 6]
-    hid, width = weights[0].shape
-    tile = hid // tiles
+def load_kernel(source, target, sems):
+    step = source.shape[0] // PIECES
     copies = []
-    for i in range(tiles):
-        for n in range(2):
-            span = pl.ds(i * tile, tile)
-            copy = pltpu.make_async_copy(
-                weights[n].at[span], scratch[n].at[span], sems.at[2 * i + n]
-            )
-            copy.start()
-            copies.append(copy)
+    for i in range(PIECES):
+        span = pl.ds(i * step, step)
+        copies.append(pltpu.make_async_copy(source.at[span], target.at[span], sems.at[i]))
+    for copy in copies:
+        copy.start()
+    for copy in copies:
+        copy.wait()
+
+
+def load(weights):
+    return pl.pallas_call(
+        load_kernel,
+        in_specs=[pl.BlockSpec(memory_space=pltpu.HBM)],
+        out_specs=pl.BlockSpec(memory_space=pltpu.VMEM),
+        out_shape=pltpu.VMEM(weights.shape, weights.dtype),
+        scratch_shapes=[pltpu.SemaphoreType.DMA((PIECES,))],
+        compiler_params=pltpu.CompilerParams(vmem_limit_bytes=SMALL_LIMIT),
+        cost_estimate=BRIEF,
+        name="load",
+    )(*in_hbm(weights))
+
+
+def raw_kernel(count, tile, *refs):
+    lines, (gate_w, up_w, gate_ref, up_ref, scratch, sems) = refs[:count], refs[count:]
+    hid, width = gate_w.shape
+    spans = [pl.ds(i * tile, tile) for i in range(hid // tile)]
+    copies = [
+        pltpu.make_async_copy(up_w.at[span], scratch.at[span], sems.at[i])
+        for i, span in enumerate(spans)
+    ]
+    for copy in copies:
+        copy.start()
     x = jnp.concatenate([line[:, :width] for line in lines])
-    for i in range(tiles):
-        span = slice(i * tile, (i + 1) * tile)
-        for n in range(2):
-            copies[2 * i + n].wait()
-            outs[n][:, span] = dot_nt(x, scratch[n][span])
+    for span in spans:
+        gate_ref[:, span] = dot_nt(x, gate_w[span])
+    for span, copy in zip(spans, copies):
+        copy.wait()
+        up_ref[:, span] = dot_nt(x, scratch[span])
 
 
 def raw_products(lines, gate_w, up_w):
     hid = gate_w.shape[0]
     total = sum(line.shape[0] for line in lines)
-    tiles = hid // 128
+    tile = 256 if hid % 256 == 0 else 128
     vmem = pl.BlockSpec(memory_space=pltpu.VMEM)
     return pl.pallas_call(
-        functools.partial(raw_kernel, len(lines), tiles),
-        in_specs=[vmem] * len(lines) + [pl.BlockSpec(memory_space=pltpu.HBM)] * 2,
+        functools.partial(raw_kernel, len(lines), tile),
+        in_specs=[vmem] * (len(lines) + 1) + [pl.BlockSpec(memory_space=pltpu.HBM)],
         out_specs=[vmem] * 2,
         out_shape=[jax.ShapeDtypeStruct((total, hid), F32)] * 2,
-        scratch_shapes=[pltpu.VMEM(gate_w.shape, BF)] * 2
-        + [pltpu.SemaphoreType.DMA((2 * tiles,))],
+        scratch_shapes=[pltpu.VMEM(up_w.shape, BF), pltpu.SemaphoreType.DMA((hid // tile,))],
         compiler_params=pltpu.CompilerParams(vmem_limit_bytes=STREAM_LIMIT),
         cost_estimate=BRIEF,
         name="raw",
-    )(*lines, *in_hbm(gate_w, up_w))
+    )(*lines, gate_w, *in_hbm(up_w))
 
 
 def hidden_kernel(parts, count, exp_dev, pair, place_ref, *refs):
@@ -265,6 +290,7 @@
     return pl.pallas_call(
         functools.partial(turn_kernel, rows),
         out_shape=[jax.ShapeDtypeStruct((total, 2 * ranks), BF)] * parts,
+        compiler_params=pltpu.CompilerParams(vmem_limit_bytes=SMALL_LIMIT),
         cost_estimate=BRIEF,
         name="turn",
     )(near, far)
@@ -390,7 +416,8 @@
     arrived = [along_z(sent, k) for k in range(1, parts)]
     first = [along_y(sent, s) for s in range(1, chips)]
     left, *small = cut((gate_right, up_right, down_left), (gate_left, up_left), parts)
-    rest = after(jnp.concatenate(arrived), (left, small))
+    gate_w = load(jnp.swapaxes(w_gate, 1, 2).reshape(hid, width))
+    rest = after(jnp.concatenate(arrived), (left, small, gate_w))
     lines = [jnp.concatenate([sent, rest])]
     partner = [other_core(lines[0])]
     small = after(tuple(small), rest)
@@ -405,9 +432,9 @@
     lines += partner
     diag = spread(small, parts, exp_dev)
 
+    lines = after(tuple(lines), diag)
     inner = inner_products(lines, left, parts, rows)
     inner = [inner[0]] + [along_z(inner[k], k) for k in range(1, parts)]
-    gate_w = jnp.swapaxes(w_gate, 1, 2).reshape(hid, width)
     up_w = jnp.swapaxes(w_up, 1, 2).reshape(hid, width)
     raw = raw_products(lines, gate_w, up_w)
     first_expert = (me_g * exp_dev)[None]

time: 71.2 us -> 69.9 us (0.982)
  local copies, waits for them, and re-layouts: 1.83 us -> 6.96 us
  waiting for transfers between devices: 17.5 us -> 14.5 us
  Pallas kernels: 19.2 us -> 17.5 us
  other arithmetic: 1.62 us -> 0.74 us
    unnamed x22 -> x18, local copies, waits for them, and re-layouts: 1.83 us -> 6.96 us
    ppermute x15, waiting for transfers between devices: 12.1 us -> 8.36 us  [along_z(): lax.ppermute(value, 'mp', [(i, (i + step) % parts) for i in range(parts)])]
    ppermute x5, waiting for transfers between devices: 2.25 us -> 4.1 us  [along_y(): lax.ppermute(value, 'y', [(i, (i + step) % chips) for i in range(chips)])]
    pallas_call x1, Pallas kernels: 2.06 us -> 0.36 us  [spread(): pl.pallas_call(functools.partial(spread_kernel, parts, exp_dev), out_shap...]
    pallas_call x1, Pallas kernels: 1.39 us -> 0.01 us  [turn(): pl.pallas_call(functools.partial(turn_kernel, rows), out_shape=[jax.Shape...]
    ppermute x5, waiting for transfers between devices: 3.2 us -> 2.04 us  [other_core(): return lax.ppermute(value, 'core', [(0, 1), (1, 0)])]
    pallas_call x1 -> x2, Pallas kernels: 9.76 us -> 10.8 us  [the longest x1 7.86 us: raw_products(): pl.pallas_call(functools.partial(raw_kernel, len(lines), tile), in_specs=...]
    ppermute x5, starting transfers between devices: 5.78 us -> 4.78 us  [along_y(): lax.ppermute(value, 'y', [(i, (i + step) % chips) for i in range(chips)])]
  transfers between devices with their start and end apart: 25 -> 25, of which waited for: 12 -> 14; matrix products, arithmetic and copies ran while one was open for 1% -> 0% of each run, Pallas kernels for 24% -> 20%
where the time goes in v9:
time: 69.9 us; the launch traced here: 69.7 us
  starting transfers between devices  29.7 us (42%)
  Pallas kernels  17.5 us (25%)
  waiting for transfers between devices  14.5 us (21%)
  local copies, waits for them, and re-layouts  6.96 us (10%)
  other arithmetic  0.74 us (1%)
    ppermute x15, starting transfers between devices, along_z(): lax.ppermute(value, 'mp', [(i, (i + step) % parts) for i in range(parts)])  24.2 us
    ppermute x15, waiting for transfers between devices, along_z(): lax.ppermute(value, 'mp', [(i, (i + step) % parts) for i in range(parts)])  8.36 us
    pallas_call x1, Pallas kernels, raw_products(): pl.pallas_call(functools.partial(raw_kernel, len(lines), tile), in_specs=...  7.86 us
    unnamed x18, local copies, waits for them, and re-layouts  6.96 us
    ppermute x5, starting transfers between devices, along_y(): lax.ppermute(value, 'y', [(i, (i + step) % chips) for i in range(chips)])  4.78 us
    ppermute x5, waiting for transfers between devices, along_y(): lax.ppermute(value, 'y', [(i, (i + step) % chips) for i in range(chips)])  4.1 us
    pallas_call x1, Pallas kernels, load(): pl.pallas_call(load_kernel, in_specs=[pl.BlockSpec(memory_space=pltpu.HBM...  2.9 us
    ppermute x5, waiting for transfers between devices, other_core(): return lax.ppermute(value, 'core', [(0, 1), (1, 0)])  2.04 us
  transfers between devices with their start and end apart: 25, of which 14 were waited for; matrix products, arithmetic and copies ran while one was open for 0% of the time, Pallas kernels for 20%

profile of v9, /device:TPU:0, one launch (start us, length us, event | category | flops | bytes accessed | tf_op | source)
XLA Modules:
  0.0 69.7 jit_solution(18086750483937036566)
XLA Ops:
  0.0 0.9 %attach.1 = bf16[8,4224]{1,0:T(8,128)(2,1)S(1)} custom-call(bf16[8,4096]{1,0:T(8,128)(2,1)} %tokens_ref.1, s32[8,8]{1,0:T(8,128)} %routes_ref.1, f32[8,8]{1,0:T(8,128)} %probs_ref.1), custom_call_target="tpu_custom_call" | custom-call | flops 1 | bytes 1 | tf_op jit(solution)/shard_map/attach/pallas_call | solution.py:63
  1.0 5.1 %collective-permute-start.2 = (bf16[8,4224]{1,0:T(8,128)(2,1)S(1)}, bf16[8,4224]{1,0:T(8,128)(2,1)S(1)}, u32[]{:S(2)}, u32[]{:S(2)}) collective-permute-start(bf16[8,4224]{1,0:T(8,128)(2,1)S(1)} %attach.1), channel_id=1, source_target_pairs={{0,3},{1,0},{2,1},{3,2},{4,7},{5,4},{6,5},{7,6},{8,11},{9,8},{10,9... | collective-permute-start | bytes 202760 | tf_op jit(solution)/shard_map/ppermute | solution.py:406
  6.1 1.0 %collective-permute-start = (bf16[8,4224]{1,0:T(8,128)(2,1)S(1)}, bf16[8,4224]{1,0:T(8,128)(2,1)S(1)}, u32[]{:S(2)}, u32[]{:S(2)}) collective-permute-start(bf16[8,4224]{1,0:T(8,128)(2,1)S(1)} %attach.1), channel_id=1, source_target_pairs={{0,1},{1,2},{2,3},{3,0},{4,5},{5,6},{6,7},{7,4},{8,9},{9,10},{10,1... | collective-permute-start | bytes 202760 | tf_op jit(solution)/shard_map/ppermute | solution.py:406
  7.1 1.5 %collective-permute-start.3 = (bf16[8,4224]{1,0:T(8,128)(2,1)S(1)}, bf16[8,4224]{1,0:T(8,128)(2,1)S(1)}, u32[]{:S(2)}, u32[]{:S(2)}) collective-permute-start(bf16[8,4224]{1,0:T(8,128)(2,1)S(1)} %attach.1), channel_id=1, source_target_pairs={{0,8},{8,0},{1,9},{9,1},{2,10},{10,2},{3,11},{11,3},{4,12},{12,4},... | collective-permute-start | bytes 202760 | tf_op jit(solution)/shard_map/ppermute | solution.py:409
  8.6 2.9 %load.1.refs_4_ = bf16[768,4096]{1,0:T(8,128)(2,1)S(1)} custom-call(bf16[768,4096]{1,0:T(8,128)(2,1)} %bitcast.14), custom_call_target="tpu_custom_call" | custom-call | flops 1 | bytes 1 | tf_op jit(solution)/shard_map/load/pallas_call | solution.py:171
  11.5 2.7 %copy-done = bf16[768,4096]{1,0:T(8,128)(2,1)} copy-done((bf16[768,4096]{1,0:T(8,128)(2,1)}, bf16[768,4096]{1,0:T(8,128)(2,1)S(1)}, u32[]{:S(2)}) %copy-start) | copy-done | bytes 6291480
  14.2 1.6 %cut.1 = (bf16[256,1024]{1,0:T(8,128)(2,1)S(1)}, bf16[3,32,192]{2,1,0:T(8,128)(2,1)S(1)}, bf16[3,32,192]{2,1,0:T(8,128)(2,1)S(1)}, bf16[3,32,192]{2,1,0:T(8,128)(2,1)S(1)}, bf16[3,32,192]{2,1,0:T(8,128)(2,1)S(1)}) custom-call(bf16[4,8,768]{2,1,0:T(8,128)(2,1)} %refs_0_.1, bf16[4,8,768]{2,1,0:T(8,128)(2,1)} %refs_1_.1, bf16[4,8,768]{2,1,0:T(8,128)(2,1)} %refs_2_.1, ...), custom_call_target="tpu_custom_call" | custom-call | flops 1 | bytes 1 | tf_op jit(solution)/shard_map/cut/pallas_call | solution.py:94
  16.5 2.5 %collective-permute-start.5 = (bf16[3,32,192]{2,1,0:T(8,128)(2,1)S(1)}, bf16[3,32,192]{2,1,0:T(8,128)(2,1)S(1)}, u32[]{:S(2)}, u32[]{:S(2)}) collective-permute-start(bf16[3,32,192]{2,1,0:T(8,128)(2,1)S(1)} %get-tuple-element.54), channel_id=1, source_target_pairs={{0,1},{1,2},{2,3},{3,0},{4,5},{5,6},{6,7},{7,4},{8,9},{9,10},{10,1... | collective-permute-start | bytes 110600 | tf_op jit(solution)/shard_map/ppermute | solution.py:406
  19.0 0.9 %collective-permute-start.6 = (bf16[3,32,192]{2,1,0:T(8,128)(2,1)S(1)}, bf16[3,32,192]{2,1,0:T(8,128)(2,1)S(1)}, u32[]{:S(2)}, u32[]{:S(2)}) collective-permute-start(bf16[3,32,192]{2,1,0:T(8,128)(2,1)S(1)} %get-tuple-element.55), channel_id=1, source_target_pairs={{0,2},{1,3},{2,0},{3,1},{4,6},{5,7},{6,4},{7,5},{8,10},{9,11},{10,... | collective-permute-start | bytes 110600 | tf_op jit(solution)/shard_map/ppermute | solution.py:406
  19.9 1.5 %collective-permute-start.7 = (bf16[3,32,192]{2,1,0:T(8,128)(2,1)S(1)}, bf16[3,32,192]{2,1,0:T(8,128)(2,1)S(1)}, u32[]{:S(2)}, u32[]{:S(2)}) collective-permute-start(bf16[3,32,192]{2,1,0:T(8,128)(2,1)S(1)} %get-tuple-element.56), channel_id=1, source_target_pairs={{0,3},{1,0},{2,1},{3,2},{4,7},{5,4},{6,5},{7,6},{8,11},{9,8},{10,9... | collective-permute-start | bytes 110600 | tf_op jit(solution)/shard_map/ppermute | solution.py:406
  22.0 0.9 %collective-permute-done.5.refs_1_ = bf16[3,32,192]{2,1,0:T(8,128)(2,1)S(1)} collective-permute-done((bf16[3,32,192]{2,1,0:T(8,128)(2,1)S(1)}, bf16[3,32,192]{2,1,0:T(8,128)(2,1)S(1)}, u32[]{:S(2)}, u32[]{:S(2)}) %collective-permute-start.5) | collective-permute-done | bytes 36896 | tf_op jit(solution)/shard_map/ppermute | solution.py:406
  22.9 1.3 %collective-permute-done.6.refs_2_ = bf16[3,32,192]{2,1,0:T(8,128)(2,1)S(1)} collective-permute-done((bf16[3,32,192]{2,1,0:T(8,128)(2,1)S(1)}, bf16[3,32,192]{2,1,0:T(8,128)(2,1)S(1)}, u32[]{:S(2)}, u32[]{:S(2)}) %collective-permute-start.6) | collective-permute-done | bytes 36896 | tf_op jit(solution)/shard_map/ppermute | solution.py:406
  24.5 0.7 copy-done.5
  25.6 0.8 %copy-done.2 = bf16[3,128,768]{2,1,0:T(8,128)(2,1)} copy-done((bf16[3,128,768]{2,1,0:T(8,128)(2,1)}, bf16[3,128,768]{2,1,0:T(8,128)(2,1)S(1)}, u32[]{:S(2)}) %copy-start.2) | copy-done | bytes 589848
  26.8 1.0 %inner.1 = (bf16[128,256]{1,0:T(8,128)(2,1)S(1)}, bf16[128,256]{1,0:T(8,128)(2,1)}, bf16[128,256]{1,0:T(8,128)(2,1)}, bf16[128,256]{1,0:T(8,128)(2,1)}) custom-call(bf16[32,4224]{1,0:T(8,128)(2,1)S(1)} %pad_maximum_fusion.refs_0_, bf16[32,4224]{1,0:T(8,128)(2,1)S(1)} %pad_maximum_fusion.1.refs_1_, bf16[32,4224]{1,0:T(8,128)(2,1)S(1)} %collective-permute-done.9.refs_2_, ...), custom_call_target="tpu_custom_call" | custom-call | flops 1 | bytes 1 | tf_op jit(solution)/shard_map/inner/pallas_call | solution.py:149
  28.3 2.8 %collective-permute-start.12 = (bf16[128,256]{1,0:T(8,128)(2,1)}, bf16[128,256]{1,0:T(8,128)(2,1)}, u32[]{:S(2)}, u32[]{:S(2)}) collective-permute-start(bf16[128,256]{1,0:T(8,128)(2,1)} %get-tuple-element.65), channel_id=1, source_target_pairs={{0,2},{1,3},{2,0},{3,1},{4,6},{5,7},{6,4},{7,5},{8,10},{9,11},{10,... | collective-permute-start | bytes 196616 | tf_op jit(solution)/shard_map/ppermute | solution.py:406
  31.1 1.0 %collective-permute-start.13 = (bf16[128,256]{1,0:T(8,128)(2,1)}, bf16[128,256]{1,0:T(8,128)(2,1)}, u32[]{:S(2)}, u32[]{:S(2)}) collective-permute-start(bf16[128,256]{1,0:T(8,128)(2,1)} %get-tuple-element.66), channel_id=1, source_target_pairs={{0,3},{1,0},{2,1},{3,2},{4,7},{5,4},{6,5},{7,6},{8,11},{9,8},{10,9... | collective-permute-start | bytes 196616 | tf_op jit(solution)/shard_map/ppermute | solution.py:406
  32.2 2.8 %copy-done.1 = bf16[768,4096]{1,0:T(8,128)(2,1)S(1)} copy-done((bf16[768,4096]{1,0:T(8,128)(2,1)S(1)}, bf16[768,4096]{1,0:T(8,128)(2,1)}, u32[]{:S(2)}) %copy-start.1) | copy-done | bytes 6291480
  34.9 7.9 %raw.1 = (f32[128,768]{1,0:T(8,128)S(1)}, f32[128,768]{1,0:T(8,128)S(1)}) custom-call(bf16[32,4224]{1,0:T(8,128)(2,1)S(1)} %pad_maximum_fusion.refs_0_, bf16[32,4224]{1,0:T(8,128)(2,1)S(1)} %pad_maximum_fusion.1.refs_1_, bf16[32,4224]{1,0:T(8,128)(2,1)S(1)} %collective-permute-done.9.refs_2_, bf16[32,4224]{1,0:T(8,128)(2,1)S(1)} %collective-permute-done.10.refs_3_, ...), custom_call_target="tpu_custom_call" | custom-call | flops 1 | bytes 1 | tf_op jit(solution)/shard_map/raw/pallas_call | solution.py:206
  42.9 1.5 %hidden.1 = (bf16[128,768]{1,0:T(8,128)(2,1)S(1)}, bf16[64,128]{1,0:T(8,128)(2,1)S(1)}, bf16[64,128]{1,0:T(8,128)(2,1)S(1)}) custom-call(s32[1]{0:T(128)} %bitcast.place_ref, bf16[32,4224]{1,0:T(8,128)(2,1)S(1)} %pad_maximum_fusion.refs_0_, bf16[32,4224]{1,0:T(8,128)(2,1)S(1)} %pad_maximum_fusion.1.refs_1_, ...), custom_call_target="tpu_custom_call" | custom-call | flops 1 | bytes 1 | tf_op jit(solution)/shard_map/hidden/pallas_call | solution.py:245
  44.4 1.0 %down.1 = (f32[64,4096]{1,0:T(8,128)S(1)}, bf16[64,4096]{1,0:T(8,128)(2,1)S(1)}) custom-call(bf16[128,768]{1,0:T(8,128)(2,1)S(1)} %get-tuple-element.69.hidden_ref, bf16[768,4096]{1,0:T(8,128)(2,1)S(1)} %bitcast.11), custom_call_target="tpu_custom_call" | custom-call | flops 1 | bytes 1 | tf_op jit(solution)/shard_map/down/pallas_call | solution.py:270
  46.0 1.5 %collective-permute-done.15.far_ref = bf16[64,4096]{1,0:T(8,128)(2,1)S(1)} collective-permute-done((bf16[64,4096]{1,0:T(8,128)(2,1)S(1)}, bf16[64,4096]{1,0:T(8,128)(2,1)S(1)}, u32[]{:S(2)}, u32[]{:S(2)}) %collective-permute-start.15) | collective-permute-done | bytes 524320 | tf_op jit(solution)/shard_map/ppermute | solution.py:412
  47.6 1.6 %collective-permute-start.19 = (bf16[24,4096]{1,0:T(8,128)(2,1)S(1)}, bf16[24,4096]{1,0:T(8,128)(2,1)S(1)}, u32[]{:S(2)}, u32[]{:S(2)}) collective-permute-start(bf16[24,4096]{1,0:T(8,128)(2,1)S(1)} %get-tuple-element.81), channel_id=1, source_target_pairs={{0,8},{8,0},{1,9},{9,1},{2,10},{10,2},{3,11},{11,3},{4,12},{12,4},... | collective-permute-start | bytes 589832 | tf_op jit(solution)/shard_map/ppermute | solution.py:409
  49.2 1.0 %collective-permute-start.16 = (bf16[64,256]{1,0:T(8,128)(2,1)S(1)}, bf16[64,256]{1,0:T(8,128)(2,1)S(1)}, u32[]{:S(2)}, u32[]{:S(2)}) collective-permute-start(bf16[64,256]{1,0:T(8,128)(2,1)S(1)} %get-tuple-element.77), channel_id=1, source_target_pairs={{0,1},{1,2},{2,3},{3,0},{4,5},{5,6},{6,7},{7,4},{8,9},{9,10},{10,1... | collective-permute-start | bytes 98312 | tf_op jit(solution)/shard_map/ppermute | solution.py:406
  50.8 2.8 %collective-permute-start.18 = (bf16[64,256]{1,0:T(8,128)(2,1)S(1)}, bf16[64,256]{1,0:T(8,128)(2,1)S(1)}, u32[]{:S(2)}, u32[]{:S(2)}) collective-permute-start(bf16[64,256]{1,0:T(8,128)(2,1)S(1)} %get-tuple-element.79), channel_id=1, source_target_pairs={{0,3},{1,0},{2,1},{3,2},{4,7},{5,4},{6,5},{7,6},{8,11},{9,8},{10,9... | collective-permute-start | bytes 98312 | tf_op jit(solution)/shard_map/ppermute | solution.py:406
  53.7 1.6 %collective-permute-done.16.refs_1_ = bf16[64,256]{1,0:T(8,128)(2,1)S(1)} collective-permute-done((bf16[64,256]{1,0:T(8,128)(2,1)S(1)}, bf16[64,256]{1,0:T(8,128)(2,1)S(1)}, u32[]{:S(2)}, u32[]{:S(2)}) %collective-permute-start.16) | collective-permute-done | bytes 32800 | tf_op jit(solution)/shard_map/ppermute | solution.py:406
  56.6 3.8 %collective-permute-done.20.refs_1_ = bf16[32,1024]{1,0:T(8,128)(2,1)S(1)} collective-permute-done((bf16[32,1024]{1,0:T(8,128)(2,1)S(1)}, bf16[32,1024]{1,0:T(8,128)(2,1)S(1)}, u32[]{:S(2)}, u32[]{:S(2)}) %collective-permute-start.20) | collective-permute-done | bytes 65568 | tf_op jit(solution)/shard_map/ppermute | solution.py:409
  60.4 1.8 %collective-permute-start.24 = (bf16[8,4096]{1,0:T(8,128)(2,1)S(1)}, bf16[8,4096]{1,0:T(8,128)(2,1)S(1)}, u32[]{:S(2)}, u32[]{:S(2)}) collective-permute-start(bf16[8,4096]{1,0:T(8,128)(2,1)S(1)} %get-tuple-element.88), channel_id=1, source_target_pairs={{0,1},{1,2},{2,3},{3,0},{4,5},{5,6},{6,7},{7,4},{8,9},{9,10},{10,1... | collective-permute-start | bytes 196616 | tf_op jit(solution)/shard_map/ppermute | solution.py:406
  62.3 2.3 %collective-permute-start.23 = (bf16[8,4096]{1,0:T(8,128)(2,1)S(1)}, bf16[8,4096]{1,0:T(8,128)(2,1)S(1)}, u32[]{:S(2)}, u32[]{:S(2)}) collective-permute-start(bf16[8,4096]{1,0:T(8,128)(2,1)S(1)} %get-tuple-element.87), channel_id=1, source_target_pairs={{0,2},{1,3},{2,0},{3,1},{4,6},{5,7},{6,4},{7,5},{8,10},{9,11},{10,... | collective-permute-start | bytes 196616 | tf_op jit(solution)/shard_map/ppermute | solution.py:406
  65.2 1.3 %collective-permute-done.24 = bf16[8,4096]{1,0:T(8,128)(2,1)S(1)} collective-permute-done((bf16[8,4096]{1,0:T(8,128)(2,1)S(1)}, bf16[8,4096]{1,0:T(8,128)(2,1)S(1)}, u32[]{:S(2)}, u32[]{:S(2)}) %collective-permute-start.24) | collective-permute-done | bytes 65568 | tf_op jit(solution)/shard_map/ppermute | solution.py:406
  66.6 1.4 %collective-permute-done.23 = bf16[8,4096]{1,0:T(8,128)(2,1)S(1)} collective-permute-done((bf16[8,4096]{1,0:T(8,128)(2,1)S(1)}, bf16[8,4096]{1,0:T(8,128)(2,1)S(1)}, u32[]{:S(2)}, u32[]{:S(2)}) %collective-permute-start.23) | collective-permute-done | bytes 65568 | tf_op jit(solution)/shard_map/ppermute | solution.py:406
  68.0 0.9 %collective-permute-done.22 = bf16[8,4096]{1,0:T(8,128)(2,1)S(1)} collective-permute-done((bf16[8,4096]{1,0:T(8,128)(2,1)S(1)}, bf16[8,4096]{1,0:T(8,128)(2,1)S(1)}, u32[]{:S(2)}, u32[]{:S(2)}) %collective-permute-start.22) | collective-permute-done | bytes 65568 | tf_op jit(solution)/shard_map/ppermute | solution.py:406
  (53 shorter events, 7.0 us)
Async XLA Ops:
  1.0 14.9 %collective-permute-start.2 = (bf16[8,4224]{1,0:T(8,128)(2,1)S(1)}, bf16[8,4224]{1,0:T(8,128)(2,1)S(1)}, u32[]{:S(2)}, u32[]{:S(2)}) collective-permute-start(bf16[8,4224]{1,0:T(8,128)(2,1)S(1)} %attach.1), channel_id=1, source_target_pairs={{0,3},{1,0},{2,1},{3,2},{4,7},{5,4},{6,5},{7,6},{8,11},{9,8},{10,9... | collective-permute-start | bytes 202760 | tf_op jit(solution)/shard_map/ppermute | solution.py:406
  6.1 9.8 %collective-permute-start.1 = (bf16[8,4224]{1,0:T(8,128)(2,1)S(1)}, bf16[8,4224]{1,0:T(8,128)(2,1)S(1)}, u32[]{:S(2)}, u32[]{:S(2)}) collective-permute-start(bf16[8,4224]{1,0:T(8,128)(2,1)S(1)} %attach.1), channel_id=1, source_target_pairs={{0,2},{1,3},{2,0},{3,1},{4,6},{5,7},{6,4},{7,5},{8,10},{9,11},{10,... | collective-permute-start | bytes 202760 | tf_op jit(solution)/shard_map/ppermute | solution.py:406
  6.1 9.8 %collective-permute-start = (bf16[8,4224]{1,0:T(8,128)(2,1)S(1)}, bf16[8,4224]{1,0:T(8,128)(2,1)S(1)}, u32[]{:S(2)}, u32[]{:S(2)}) collective-permute-start(bf16[8,4224]{1,0:T(8,128)(2,1)S(1)} %attach.1), channel_id=1, source_target_pairs={{0,1},{1,2},{2,3},{3,0},{4,5},{5,6},{6,7},{7,4},{8,9},{9,10},{10,1... | collective-permute-start | bytes 202760 | tf_op jit(solution)/shard_map/ppermute | solution.py:406
  7.1 14.4 %collective-permute-start.3 = (bf16[8,4224]{1,0:T(8,128)(2,1)S(1)}, bf16[8,4224]{1,0:T(8,128)(2,1)S(1)}, u32[]{:S(2)}, u32[]{:S(2)}) collective-permute-start(bf16[8,4224]{1,0:T(8,128)(2,1)S(1)} %attach.1), channel_id=1, source_target_pairs={{0,8},{8,0},{1,9},{9,1},{2,10},{10,2},{3,11},{11,3},{4,12},{12,4},... | collective-permute-start | bytes 202760 | tf_op jit(solution)/shard_map/ppermute | solution.py:409
  8.6 12.9 %copy-start.4 = (bf16[4,32,1024]{2,1,0:T(8,128)(2,1)S(1)}, bf16[4,32,1024]{2,1,0:T(8,128)(2,1)}, u32[]{:S(2)}) copy-start(bf16[4,32,1024]{2,1,0:T(8,128)(2,1)} %param.23) | copy-start | bytes 786436
  11.5 2.7 %copy-start = (bf16[768,4096]{1,0:T(8,128)(2,1)}, bf16[768,4096]{1,0:T(8,128)(2,1)S(1)}, u32[]{:S(2)}) copy-start(bf16[768,4096]{1,0:T(8,128)(2,1)S(1)} %load.1.refs_4_) | copy-start | bytes 18874372
  15.8 28.6 %slice-start = ((s8[6291456]{0:T(1024)(128)(4,1)}), s8[2097152]{0:T(1024)(128)(4,1)S(1)}, s32[]{:S(2)}) async-start(s8[6291456]{0:T(1024)(128)(4,1)} %bitcast.9), calls=%async_computation | async-start | bytes 4194304
  15.9 5.8 %collective-permute-start.4 = (bf16[24,4224]{1,0:T(8,128)(2,1)S(1)}, bf16[24,4224]{1,0:T(8,128)(2,1)S(1)}, u32[]{:S(2)}, u32[]{:S(2)}) collective-permute-start(bf16[24,4224]{1,0:T(8,128)(2,1)S(1)} %pad_maximum_fusion.2), channel_id=1, source_target_pairs={{0,8},{8,0},{1,9},{9,1},{2,10},{10,2},{3,11},{11,3},{4,12},{12,4},... | collective-permute-start | bytes 608264 | tf_op jit(solution)/shard_map/ppermute | solution.py:409
  16.5 6.4 %collective-permute-start.5 = (bf16[3,32,192]{2,1,0:T(8,128)(2,1)S(1)}, bf16[3,32,192]{2,1,0:T(8,128)(2,1)S(1)}, u32[]{:S(2)}, u32[]{:S(2)}) collective-permute-start(bf16[3,32,192]{2,1,0:T(8,128)(2,1)S(1)} %get-tuple-element.54), channel_id=1, source_target_pairs={{0,1},{1,2},{2,3},{3,0},{4,5},{5,6},{6,7},{7,4},{8,9},{9,10},{10,1... | collective-permute-start | bytes 110600 | tf_op jit(solution)/shard_map/ppermute | solution.py:406
  19.0 5.1 %collective-permute-start.6 = (bf16[3,32,192]{2,1,0:T(8,128)(2,1)S(1)}, bf16[3,32,192]{2,1,0:T(8,128)(2,1)S(1)}, u32[]{:S(2)}, u32[]{:S(2)}) collective-permute-start(bf16[3,32,192]{2,1,0:T(8,128)(2,1)S(1)} %get-tuple-element.55), channel_id=1, source_target_pairs={{0,2},{1,3},{2,0},{3,1},{4,6},{5,7},{6,4},{7,5},{8,10},{9,11},{10,... | collective-permute-start | bytes 110600 | tf_op jit(solution)/shard_map/ppermute | solution.py:406
  19.9 4.6 %collective-permute-start.7 = (bf16[3,32,192]{2,1,0:T(8,128)(2,1)S(1)}, bf16[3,32,192]{2,1,0:T(8,128)(2,1)S(1)}, u32[]{:S(2)}, u32[]{:S(2)}) collective-permute-start(bf16[3,32,192]{2,1,0:T(8,128)(2,1)S(1)} %get-tuple-element.56), channel_id=1, source_target_pairs={{0,3},{1,0},{2,1},{3,2},{4,7},{5,4},{6,5},{7,6},{8,11},{9,8},{10,9... | collective-permute-start | bytes 110600 | tf_op jit(solution)/shard_map/ppermute | solution.py:406
  21.5 3.1 %collective-permute-start.8 = (bf16[128,1024]{1,0:T(8,128)(2,1)S(1)}, bf16[128,1024]{1,0:T(8,128)(2,1)S(1)}, u32[]{:S(2)}, u32[]{:S(2)}) collective-permute-start(bf16[128,1024]{1,0:T(8,128)(2,1)S(1)} %bitcast.12), channel_id=1, source_target_pairs={{0,4},{4,0},{1,5},{5,1},{2,6},{6,2},{3,7},{7,3},{8,12},{12,8},{9,1... | collective-permute-start | bytes 786440 | tf_op jit(solution)/shard_map/ppermute | solution.py:412
  21.7 4.7 %collective-permute-start.9 = (bf16[32,4224]{1,0:T(8,128)(2,1)S(1)}, bf16[32,4224]{1,0:T(8,128)(2,1)S(1)}, u32[]{:S(2)}, u32[]{:S(2)}) collective-permute-start(bf16[32,4224]{1,0:T(8,128)(2,1)S(1)} %pad_maximum_fusion.refs_0_), channel_id=1, source_target_pairs={{0,4},{4,0},{1,5},{5,1},{2,6},{6,2},{3,7},{7,3},{8,12},{12,8},{9,1... | collective-permute-start | bytes 811016 | tf_op jit(solution)/shard_map/ppermute | solution.py:412
  25.2 1.5 %collective-permute-start.10 = (bf16[32,4224]{1,0:T(8,128)(2,1)S(1)}, bf16[32,4224]{1,0:T(8,128)(2,1)S(1)}, u32[]{:S(2)}, u32[]{:S(2)}) collective-permute-start(bf16[32,4224]{1,0:T(8,128)(2,1)S(1)} %pad_maximum_fusion.1.refs_1_), channel_id=1, source_target_pairs={{0,4},{4,0},{1,5},{5,1},{2,6},{6,2},{3,7},{7,3},{8,12},{12,8},{9,1... | collective-permute-start | bytes 811016 | tf_op jit(solution)/shard_map/ppermute | solution.py:412
  27.7 15.1 %collective-permute-start.11 = (bf16[128,256]{1,0:T(8,128)(2,1)}, bf16[128,256]{1,0:T(8,128)(2,1)}, u32[]{:S(2)}, u32[]{:S(2)}) collective-permute-start(bf16[128,256]{1,0:T(8,128)(2,1)} %get-tuple-element.64), channel_id=1, source_target_pairs={{0,1},{1,2},{2,3},{3,0},{4,5},{5,6},{6,7},{7,4},{8,9},{9,10},{10,1... | collective-permute-start | bytes 196616 | tf_op jit(solution)/shard_map/ppermute | solution.py:406
  28.3 14.5 %collective-permute-start.12 = (bf16[128,256]{1,0:T(8,128)(2,1)}, bf16[128,256]{1,0:T(8,128)(2,1)}, u32[]{:S(2)}, u32[]{:S(2)}) collective-permute-start(bf16[128,256]{1,0:T(8,128)(2,1)} %get-tuple-element.65), channel_id=1, source_target_pairs={{0,2},{1,3},{2,0},{3,1},{4,6},{5,7},{6,4},{7,5},{8,10},{9,11},{10,... | collective-permute-start | bytes 196616 | tf_op jit(solution)/shard_map/ppermute | solution.py:406
  31.1 11.7 %collective-permute-start.13 = (bf16[128,256]{1,0:T(8,128)(2,1)}, bf16[128,256]{1,0:T(8,128)(2,1)}, u32[]{:S(2)}, u32[]{:S(2)}) collective-permute-start(bf16[128,256]{1,0:T(8,128)(2,1)} %get-tuple-element.66), channel_id=1, source_target_pairs={{0,3},{1,0},{2,1},{3,2},{4,7},{5,4},{6,5},{7,6},{8,11},{9,8},{10,9... | collective-permute-start | bytes 196616 | tf_op jit(solution)/shard_map/ppermute | solution.py:406
  32.2 2.8 %copy-start.1 = (bf16[768,4096]{1,0:T(8,128)(2,1)S(1)}, bf16[768,4096]{1,0:T(8,128)(2,1)}, u32[]{:S(2)}) copy-start(bf16[768,4096]{1,0:T(8,128)(2,1)} %copy-done) | copy-start | bytes 18874372
  34.9 7.9 %copy-start.3 = (bf16[3,128,768]{2,1,0:T(8,128)(2,1)S(1)}, bf16[3,128,768]{2,1,0:T(8,128)(2,1)}, u32[]{:S(2)}) copy-start(bf16[3,128,768]{2,1,0:T(8,128)(2,1)} %copy-done.2) | copy-start | bytes 1769476
  34.9 9.5 %slice-start.1 = ((s8[6291456]{0:T(1024)(128)(4,1)}), s8[4194304]{0:T(1024)(128)(4,1)S(1)}, s32[]{:S(2)}) async-start(s8[6291456]{0:T(1024)(128)(4,1)} %bitcast.9), calls=%async_computation.1 | async-start | bytes 8388608
  42.8 13.0 %copy-start.6 = (bf16[128,1024]{1,0:T(8,128)(2,1)S(1)}, bf16[128,1024]{1,0:T(8,128)(2,1)}, u32[]{:S(2)}) copy-start(bf16[128,1024]{1,0:T(8,128)(2,1)} %copy-done.5) | copy-start | bytes 786436
  44.3 1.2 %collective-permute-start.14 = (bf16[64,128]{1,0:T(8,128)(2,1)S(1)}, bf16[64,128]{1,0:T(8,128)(2,1)S(1)}, u32[]{:S(2)}, u32[]{:S(2)}) collective-permute-start(bf16[64,128]{1,0:T(8,128)(2,1)S(1)} %get-tuple-element.72), channel_id=1, source_target_pairs={{0,4},{4,0},{1,5},{5,1},{2,6},{6,2},{3,7},{7,3},{8,12},{12,8},{9,1... | collective-permute-start | bytes 49160 | tf_op jit(solution)/shard_map/ppermute | solution.py:412
  45.6 1.9 %collective-permute-start.15 = (bf16[64,4096]{1,0:T(8,128)(2,1)S(1)}, bf16[64,4096]{1,0:T(8,128)(2,1)S(1)}, u32[]{:S(2)}, u32[]{:S(2)}) collective-permute-start(bf16[64,4096]{1,0:T(8,128)(2,1)S(1)} %get-tuple-element.73), channel_id=1, source_target_pairs={{0,4},{4,0},{1,5},{5,1},{2,6},{6,2},{3,7},{7,3},{8,12},{12,8},{9,1... | collective-permute-start | bytes 1572872 | tf_op jit(solution)/shard_map/ppermute | solution.py:412
  47.6 12.7 %collective-permute-start.19 = (bf16[24,4096]{1,0:T(8,128)(2,1)S(1)}, bf16[24,4096]{1,0:T(8,128)(2,1)S(1)}, u32[]{:S(2)}, u32[]{:S(2)}) collective-permute-start(bf16[24,4096]{1,0:T(8,128)(2,1)S(1)} %get-tuple-element.81), channel_id=1, source_target_pairs={{0,8},{8,0},{1,9},{9,1},{2,10},{10,2},{3,11},{11,3},{4,12},{12,4},... | collective-permute-start | bytes 589832 | tf_op jit(solution)/shard_map/ppermute | solution.py:409
  49.2 6.0 %collective-permute-start.16 = (bf16[64,256]{1,0:T(8,128)(2,1)S(1)}, bf16[64,256]{1,0:T(8,128)(2,1)S(1)}, u32[]{:S(2)}, u32[]{:S(2)}) collective-permute-start(bf16[64,256]{1,0:T(8,128)(2,1)S(1)} %get-tuple-element.77), channel_id=1, source_target_pairs={{0,1},{1,2},{2,3},{3,0},{4,5},{5,6},{6,7},{7,4},{8,9},{9,10},{10,1... | collective-permute-start | bytes 98312 | tf_op jit(solution)/shard_map/ppermute | solution.py:406
  50.3 5.5 %collective-permute-start.17 = (bf16[64,256]{1,0:T(8,128)(2,1)S(1)}, bf16[64,256]{1,0:T(8,128)(2,1)S(1)}, u32[]{:S(2)}, u32[]{:S(2)}) collective-permute-start(bf16[64,256]{1,0:T(8,128)(2,1)S(1)} %get-tuple-element.78), channel_id=1, source_target_pairs={{0,2},{1,3},{2,0},{3,1},{4,6},{5,7},{6,4},{7,5},{8,10},{9,11},{10,... | collective-permute-start | bytes 98312 | tf_op jit(solution)/shard_map/ppermute | solution.py:406
  50.8 5.0 %collective-permute-start.18 = (bf16[64,256]{1,0:T(8,128)(2,1)S(1)}, bf16[64,256]{1,0:T(8,128)(2,1)S(1)}, u32[]{:S(2)}, u32[]{:S(2)}) collective-permute-start(bf16[64,256]{1,0:T(8,128)(2,1)S(1)} %get-tuple-element.79), channel_id=1, source_target_pairs={{0,3},{1,0},{2,1},{3,2},{4,7},{5,4},{6,5},{7,6},{8,11},{9,8},{10,9... | collective-permute-start | bytes 98312 | tf_op jit(solution)/shard_map/ppermute | solution.py:406
  56.0 4.3 %collective-permute-start.20 = (bf16[32,1024]{1,0:T(8,128)(2,1)S(1)}, bf16[32,1024]{1,0:T(8,128)(2,1)S(1)}, u32[]{:S(2)}, u32[]{:S(2)}) collective-permute-start(bf16[32,1024]{1,0:T(8,128)(2,1)S(1)} %get-tuple-element.82), channel_id=1, source_target_pairs={{0,8},{8,0},{1,9},{9,1},{2,10},{10,2},{3,11},{11,3},{4,12},{12,4},... | collective-permute-start | bytes 196616 | tf_op jit(solution)/shard_map/ppermute | solution.py:409
  60.4 6.1 %collective-permute-start.24 = (bf16[8,4096]{1,0:T(8,128)(2,1)S(1)}, bf16[8,4096]{1,0:T(8,128)(2,1)S(1)}, u32[]{:S(2)}, u32[]{:S(2)}) collective-permute-start(bf16[8,4096]{1,0:T(8,128)(2,1)S(1)} %get-tuple-element.88), channel_id=1, source_target_pairs={{0,1},{1,2},{2,3},{3,0},{4,5},{5,6},{6,7},{7,4},{8,9},{9,10},{10,1... | collective-permute-start | bytes 196616 | tf_op jit(solution)/shard_map/ppermute | solution.py:406
  62.3 5.7 %collective-permute-start.23 = (bf16[8,4096]{1,0:T(8,128)(2,1)S(1)}, bf16[8,4096]{1,0:T(8,128)(2,1)S(1)}, u32[]{:S(2)}, u32[]{:S(2)}) collective-permute-start(bf16[8,4096]{1,0:T(8,128)(2,1)S(1)} %get-tuple-element.87), channel_id=1, source_target_pairs={{0,2},{1,3},{2,0},{3,1},{4,6},{5,7},{6,4},{7,5},{8,10},{9,11},{10,... | collective-permute-start | bytes 196616 | tf_op jit(solution)/shard_map/ppermute | solution.py:406
  64.6 4.3 %collective-permute-start.22 = (bf16[8,4096]{1,0:T(8,128)(2,1)S(1)}, bf16[8,4096]{1,0:T(8,128)(2,1)S(1)}, u32[]{:S(2)}, u32[]{:S(2)}) collective-permute-start(bf16[8,4096]{1,0:T(8,128)(2,1)S(1)} %get-tuple-element.86), channel_id=1, source_target_pairs={{0,3},{1,0},{2,1},{3,2},{4,7},{5,4},{6,5},{7,6},{8,11},{9,8},{10,9... | collective-permute-start | bytes 196616 | tf_op jit(solution)/shard_map/ppermute | solution.py:406
  64.7 4.3 %collective-permute-start.21 = (bf16[8,4096]{1,0:T(8,128)(2,1)S(1)}, bf16[8,4096]{1,0:T(8,128)(2,1)S(1)}, u32[]{:S(2)}, u32[]{:S(2)}) collective-permute-start(bf16[8,4096]{1,0:T(8,128)(2,1)S(1)} %get-tuple-element.85), channel_id=1, source_target_pairs={{0,8},{8,0},{1,9},{9,1},{2,10},{10,2},{3,11},{11,3},{4,12},{12,4},... | collective-permute-start | bytes 196616 | tf_op jit(solution)/shard_map/ppermute | solution.py:409
  (2 other events, 1.5 us)

commit v10 on v9

--- a/solution.py
+++ b/solution.py
@@ -11,8 +11,7 @@
 F32 = jnp.float32
 SMALL_LIMIT = 4 * 1024 * 1024
 VMEM_LIMIT = 12 * 1024 * 1024
-STREAM_LIMIT = 16 * 1024 * 1024
-PIECES = 4
+PIECES = 8
 BRIEF = pl.CostEstimate(flops=1, bytes_accessed=1, transcendentals=0)
 
 
@@ -69,12 +68,25 @@
     )(*in_hbm(tokens, routes, probs))
 
 
-def cut_kernel(parts, *refs):
-    ins, lefts, left_ref, outs = refs[:3], refs[3:5], refs[5], refs[6:]
-    exp_dev, piece, hid = ins[0].shape
+def prepare_kernel(parts, *refs):
+    ins, lefts, weights = refs[:3], refs[3:5], refs[5:7]
+    loaded, left_ref, outs, sems = refs[7:9], refs[9], refs[10:-1], refs[-1]
+    step = weights[0].shape[0] // PIECES
+    copies = []
+    for n in range(2):
+        for i in range(PIECES):
+            span = pl.ds(i * step, step)
+            copies.append(
+                pltpu.make_async_copy(
+                    weights[n].at[span], loaded[n].at[span], sems.at[n * PIECES + i]
+                )
+            )
+    for copy in copies:
+        copy.start()
     half = left_ref.shape[0] // 2
     for n, ref in enumerate(lefts):
         left_ref[n * half : (n + 1) * half] = ref[...].reshape(half, left_ref.shape[1])
+    exp_dev, piece, hid = ins[0].shape
     cols = hid // parts
     me = lax.axis_index("mp")
     for n, ref in enumerate(ins):
@@ -86,19 +98,26 @@
             for j in range(1, parts):
                 block = jnp.where(target == j, blocks[j], block)
             outs[k][n] = block.astype(BF)
-
-
-def cut(factors, lefts, parts):
+    for copy in copies:
+        copy.wait()
+
+
+def prepare(factors, lefts, weights, parts):
     exp_dev, piece, hid = factors[0].shape
     _, rank, block = lefts[0].shape
-    return pl.pallas_call(
-        functools.partial(cut_kernel, parts),
-        out_shape=[jax.ShapeDtypeStruct((2 * exp_dev * rank, block), BF)]
+    vmem = pl.BlockSpec(memory_space=pltpu.VMEM)
+    return pl.pallas_call(
+        functools.partial(prepare_kernel, parts),
+        in_specs=[vmem] * 5 + [pl.BlockSpec(memory_space=pltpu.HBM)] * 2,
+        out_specs=[vmem] * (3 + parts),
+        out_shape=[pltpu.VMEM(w.shape, w.dtype) for w in weights]
+        + [jax.ShapeDtypeStruct((2 * exp_dev * rank, block), BF)]
         + [jax.ShapeDtypeStruct((3, exp_dev * piece, hid // parts), BF)] * parts,
+        scratch_shapes=[pltpu.SemaphoreType.DMA((2 * PIECES,))],
         compiler_params=pltpu.CompilerParams(vmem_limit_bytes=SMALL_LIMIT),
         cost_estimate=BRIEF,
-        name="cut",
-    )(*in_hbm(*factors, *lefts))
+        name="prepare",
+    )(*in_hbm(*factors, *lefts, *weights))
 
 
 def spread_kernel(parts, exp_dev, *refs):
@@ -155,67 +174,30 @@
     )(*lines, left)
 
 
-def load_kernel(source, target, sems):
-    step = source.shape[0] // PIECES
-    copies = []
-    for i in range(PIECES):
-        span = pl.ds(i * step, step)
-        copies.append(pltpu.make_async_copy(source.at[span], target.at[span], sems.at[i]))
-    for copy in copies:
-        copy.start()
-    for copy in copies:
-        copy.wait()
-
-
-def load(weights):
-    return pl.pallas_call(
-        load_kernel,
-        in_specs=[pl.BlockSpec(memory_space=pltpu.HBM)],
-        out_specs=pl.BlockSpec(memory_space=pltpu.VMEM),
-        out_shape=pltpu.VMEM(weights.shape, weights.dtype),
-        scratch_shapes=[pltpu.SemaphoreType.DMA((PIECES,))],
-        compiler_params=pltpu.CompilerParams(vmem_limit_bytes=SMALL_LIMIT),
-        cost_estimate=BRIEF,
-        name="load",
-    )(*in_hbm(weights))
-
-
 def raw_kernel(count, tile, *refs):
-    lines, (gate_w, up_w, gate_ref, up_ref, scratch, sems) = refs[:count], refs[count:]
+    lines, (gate_w, up_w, gate_ref, up_ref) = refs[:count], refs[count:]
     hid, width = gate_w.shape
-    spans = [pl.ds(i * tile, tile) for i in range(hid // tile)]
-    copies = [
-        pltpu.make_async_copy(up_w.at[span], scratch.at[span], sems.at[i])
-        for i, span in enumerate(spans)
-    ]
-    for copy in copies:
-        copy.start()
     x = jnp.concatenate([line[:, :width] for line in lines])
-    for span in spans:
+    for i in range(hid // tile):
+        span = pl.ds(i * tile, tile)
         gate_ref[:, span] = dot_nt(x, gate_w[span])
-    for span, copy in zip(spans, copies):
-        copy.wait()
-        up_ref[:, span] = dot_nt(x, scratch[span])
+        up_ref[:, span] = dot_nt(x, up_w[span])
 
 
 def raw_products(lines, gate_w, up_w):
     hid = gate_w.shape[0]
     total = sum(line.shape[0] for line in lines)
     tile = 256 if hid % 256 == 0 else 128
-    vmem = pl.BlockSpec(memory_space=pltpu.VMEM)
     return pl.pallas_call(
         functools.partial(raw_kernel, len(lines), tile),
-        in_specs=[vmem] * (len(lines) + 1) + [pl.BlockSpec(memory_space=pltpu.HBM)],
-        out_specs=[vmem] * 2,
         out_shape=[jax.ShapeDtypeStruct((total, hid), F32)] * 2,
-        scratch_shapes=[pltpu.VMEM(up_w.shape, BF), pltpu.SemaphoreType.DMA((hid // tile,))],
-        compiler_params=pltpu.CompilerParams(vmem_limit_bytes=STREAM_LIMIT),
+        compiler_params=pltpu.CompilerParams(vmem_limit_bytes=VMEM_LIMIT),
         cost_estimate=BRIEF,
         name="raw",
-    )(*lines, gate_w, *in_hbm(up_w))
-
-
-def hidden_kernel(parts, count, exp_dev, pair, place_ref, *refs):
+    )(*lines, gate_w, up_w)
+
+
+def hidden_kernel(parts, count, exp_dev, pair, *refs):
     lines, inner, rest = refs[:count], refs[count : count + parts], refs[count + parts :]
     gate_ref, up_ref, diag_ref, hidden_ref, near_ref, far_ref = rest
     hid = gate_ref.shape[1]
@@ -227,7 +209,8 @@
     lane = lax.broadcasted_iota(jnp.int32, (pair, hid), 0)
     lane = jnp.where(lane < pair // 2, lane, lane - pair // 2)
     cols = hid // exp_dev
-    place = lax.broadcasted_iota(jnp.int32, (pair, hid), 1) - (lane - place_ref[0]) * cols
+    first = (lax.axis_index("y") * 2 + lax.axis_index("core")) * exp_dev
+    place = lax.broadcasted_iota(jnp.int32, (pair, hid), 1) - (lane - first) * cols
     pick = ((place >= 0) & (place < cols)).astype(F32).astype(BF)
     scale = dot_nn(jnp.concatenate([line[:, wide:] for line in lines]), pick)
     hidden = (gate / (1.0 + jnp.exp(-gate)) * up * scale).astype(BF)
@@ -238,20 +221,17 @@
     far_ref[...] = value[near:].astype(BF)
 
 
-def hidden_units(place, lines, inner, raw, diag, parts, exp_dev, pair):
+def hidden_units(lines, inner, raw, diag, parts, exp_dev, pair):
     total, hid = raw[0].shape
     ranks = diag.shape[1]
-    vmem = pl.BlockSpec(memory_space=pltpu.VMEM)
     return pl.pallas_call(
         functools.partial(hidden_kernel, parts, len(lines), exp_dev, pair),
-        in_specs=[pl.BlockSpec(memory_space=pltpu.SMEM)]
-        + [vmem] * (len(lines) + len(inner) + 3),
         out_shape=[jax.ShapeDtypeStruct((total, hid), BF)]
         + [jax.ShapeDtypeStruct((total // 2, ranks), BF)] * 2,
         compiler_params=pltpu.CompilerParams(vmem_limit_bytes=VMEM_LIMIT),
         cost_estimate=BRIEF,
         name="hidden",
-    )(place, *lines, *inner, *raw, diag)
+    )(*lines, *inner, *raw, diag)
 
 
 def down_kernel(hidden_ref, down_ref, near_ref, far_ref):
@@ -398,7 +378,6 @@
     parts = lax.axis_size("mp")
     chips = lax.axis_size("y")
     experts = exp_dev * chips * 2
-    me_g = lax.axis_index("y") * 2 + lax.axis_index("core")
     ranks = exp_dev * rank
     hid = exp_dev * cols
 
@@ -415,9 +394,11 @@
     sent = attach(tokens, routes, probs, pair)
     arrived = [along_z(sent, k) for k in range(1, parts)]
     first = [along_y(sent, s) for s in range(1, chips)]
-    left, *small = cut((gate_right, up_right, down_left), (gate_left, up_left), parts)
-    gate_w = load(jnp.swapaxes(w_gate, 1, 2).reshape(hid, width))
-    rest = after(jnp.concatenate(arrived), (left, small, gate_w))
+    weights = [jnp.swapaxes(w, 1, 2).reshape(hid, width) for w in (w_gate, w_up)]
+    gate_w, up_w, left, *small = prepare(
+        (gate_right, up_right, down_left), (gate_left, up_left), weights, parts
+    )
+    rest = after(jnp.concatenate(arrived), (left, small, gate_w, up_w))
     lines = [jnp.concatenate([sent, rest])]
     partner = [other_core(lines[0])]
     small = after(tuple(small), rest)
@@ -435,11 +416,9 @@
     lines = after(tuple(lines), diag)
     inner = inner_products(lines, left, parts, rows)
     inner = [inner[0]] + [along_z(inner[k], k) for k in range(1, parts)]
-    up_w = jnp.swapaxes(w_up, 1, 2).reshape(hid, width)
     raw = raw_products(lines, gate_w, up_w)
-    first_expert = (me_g * exp_dev)[None]
     hidden, near, far = hidden_units(
-        first_expert, lines, inner, raw, diag, parts, exp_dev, pair
+        lines, inner, raw, diag, parts, exp_dev, pair
     )
     swapped = other_core(far)
     bottom = turn(near, swapped, parts, rows)

time: 69.9 us -> 60.6 us (0.87)
  local copies, waits for them, and re-layouts: 6.96 us -> 0.01 us
  Pallas kernels: 17.5 us -> 13.8 us
  waiting for transfers between devices: 14.5 us -> 16.2 us
    unnamed x18 -> x6, local copies, waits for them, and re-layouts: 6.96 us -> 0.01 us
    pallas_call x3 -> x2, Pallas kernels: 12.4 us -> 10.2 us  [the longest x1 6 us: prepare(): pl.pallas_call(functools.partial(prepare_kernel, parts), in_specs=[vmem]...]
    pallas_call x1, Pallas kernels: 1.46 us -> 0.52 us  [hidden_units(): pl.pallas_call(functools.partial(hidden_kernel, parts, len(lines), exp_de...]
    ppermute x15, waiting for transfers between devices: 8.36 us -> 9.2 us  [along_z(): lax.ppermute(value, 'mp', [(i, (i + step) % parts) for i in range(parts)])]
    ppermute x5, waiting for transfers between devices: 2.04 us -> 2.77 us  [other_core(): return lax.ppermute(value, 'core', [(0, 1), (1, 0)])]
  transfers between devices with their start and end apart: 25 -> 25, of which waited for: 14 -> 16; matrix products, arithmetic and copies ran while one was open for 0% -> 0% of each run, Pallas kernels for 20% -> 20%
where the time goes in v10:
time: 60.6 us; the launch traced here: 60.4 us
  starting transfers between devices  29.6 us (49%)
  waiting for transfers between devices  16.2 us (27%)
  Pallas kernels  13.8 us (23%)
  other arithmetic  0.73 us (1%)
    ppermute x15, starting transfers between devices, along_z(): lax.ppermute(value, 'mp', [(i, (i + step) % parts) for i in range(parts)])  24 us
    ppermute x15, waiting for transfers between devices, along_z(): lax.ppermute(value, 'mp', [(i, (i + step) % parts) for i in range(parts)])  9.2 us
    pallas_call x1, Pallas kernels, prepare(): pl.pallas_call(functools.partial(prepare_kernel, parts), in_specs=[vmem]...  6 us
    ppermute x5, starting transfers between devices, along_y(): lax.ppermute(value, 'y', [(i, (i + step) % chips) for i in range(chips)])  4.77 us
    ppermute x5, waiting for transfers between devices, along_y(): lax.ppermute(value, 'y', [(i, (i + step) % chips) for i in range(chips)])  4.2 us
    pallas_call x1, Pallas kernels, raw_products(): pl.pallas_call(functools.partial(raw_kernel, len(lines), tile), out_shape...  4.18 us
    ppermute x5, waiting for transfers between devices, other_core(): return lax.ppermute(value, 'core', [(0, 1), (1, 0)])  2.77 us
  transfers between devices with their start and end apart: 25, of which 16 were waited for; matrix products, arithmetic and copies ran while one was open for 0% of the time, Pallas kernels for 20%

profile of v10, /device:TPU:0, one launch (start us, length us, event | category | flops | bytes accessed | tf_op | source)
XLA Modules:
  0.0 60.4 jit_solution(6064971364390485784)
XLA Ops:
  0.0 0.9 %attach.1 = bf16[8,4224]{1,0:T(8,128)(2,1)S(1)} custom-call(bf16[8,4096]{1,0:T(8,128)(2,1)} %tokens_ref.1, s32[8,8]{1,0:T(8,128)} %routes_ref.1, f32[8,8]{1,0:T(8,128)} %probs_ref.1), custom_call_target="tpu_custom_call" | custom-call | flops 1 | bytes 1 | tf_op jit(solution)/shard_map/attach/pallas_call | solution.py:62
  1.0 5.1 %collective-permute-start.2 = (bf16[8,4224]{1,0:T(8,128)(2,1)S(1)}, bf16[8,4224]{1,0:T(8,128)(2,1)S(1)}, u32[]{:S(2)}, u32[]{:S(2)}) collective-permute-start(bf16[8,4224]{1,0:T(8,128)(2,1)S(1)} %attach.1), channel_id=1, source_target_pairs={{0,3},{1,0},{2,1},{3,2},{4,7},{5,4},{6,5},{7,6},{8,11},{9,8},{10,9... | collective-permute-start | bytes 202760 | tf_op jit(solution)/shard_map/ppermute | solution.py:385
  6.1 1.0 %collective-permute-start = (bf16[8,4224]{1,0:T(8,128)(2,1)S(1)}, bf16[8,4224]{1,0:T(8,128)(2,1)S(1)}, u32[]{:S(2)}, u32[]{:S(2)}) collective-permute-start(bf16[8,4224]{1,0:T(8,128)(2,1)S(1)} %attach.1), channel_id=1, source_target_pairs={{0,1},{1,2},{2,3},{3,0},{4,5},{5,6},{6,7},{7,4},{8,9},{9,10},{10,1... | collective-permute-start | bytes 202760 | tf_op jit(solution)/shard_map/ppermute | solution.py:385
  7.1 1.5 %collective-permute-start.3 = (bf16[8,4224]{1,0:T(8,128)(2,1)S(1)}, bf16[8,4224]{1,0:T(8,128)(2,1)S(1)}, u32[]{:S(2)}, u32[]{:S(2)}) collective-permute-start(bf16[8,4224]{1,0:T(8,128)(2,1)S(1)} %attach.1), channel_id=1, source_target_pairs={{0,8},{8,0},{1,9},{9,1},{2,10},{10,2},{3,11},{11,3},{4,12},{12,4},... | collective-permute-start | bytes 202760 | tf_op jit(solution)/shard_map/ppermute | solution.py:388
  8.6 6.0 %prepare.1 = (bf16[768,4096]{1,0:T(8,128)(2,1)S(1)}, bf16[768,4096]{1,0:T(8,128)(2,1)S(1)}, bf16[256,1024]{1,0:T(8,128)(2,1)S(1)}, bf16[3,32,192]{2,1,0:T(8,128)...) custom-call(bf16[4,8,768]{2,1,0:T(8,128)(2,1)} %refs_0_.1, ...), custom_call_target="tpu_custom_call" | custom-call | flops 1 | bytes 1 | tf_op jit(solution)/shard_map/prepare/pallas_call | solution.py:109
  15.3 2.5 %collective-permute-start.5 = (bf16[3,32,192]{2,1,0:T(8,128)(2,1)S(1)}, bf16[3,32,192]{2,1,0:T(8,128)(2,1)S(1)}, u32[]{:S(2)}, u32[]{:S(2)}) collective-permute-start(bf16[3,32,192]{2,1,0:T(8,128)(2,1)S(1)} %get-tuple-element.58), channel_id=1, source_target_pairs={{0,1},{1,2},{2,3},{3,0},{4,5},{5,6},{6,7},{7,4},{8,9},{9,10},{10,1... | collective-permute-start | bytes 110600 | tf_op jit(solution)/shard_map/ppermute | solution.py:385
  17.8 0.9 %collective-permute-start.6 = (bf16[3,32,192]{2,1,0:T(8,128)(2,1)S(1)}, bf16[3,32,192]{2,1,0:T(8,128)(2,1)S(1)}, u32[]{:S(2)}, u32[]{:S(2)}) collective-permute-start(bf16[3,32,192]{2,1,0:T(8,128)(2,1)S(1)} %get-tuple-element.59), channel_id=1, source_target_pairs={{0,2},{1,3},{2,0},{3,1},{4,6},{5,7},{6,4},{7,5},{8,10},{9,11},{10,... | collective-permute-start | bytes 110600 | tf_op jit(solution)/shard_map/ppermute | solution.py:385
  18.7 1.5 %collective-permute-start.7 = (bf16[3,32,192]{2,1,0:T(8,128)(2,1)S(1)}, bf16[3,32,192]{2,1,0:T(8,128)(2,1)S(1)}, u32[]{:S(2)}, u32[]{:S(2)}) collective-permute-start(bf16[3,32,192]{2,1,0:T(8,128)(2,1)S(1)} %get-tuple-element.60), channel_id=1, source_target_pairs={{0,3},{1,0},{2,1},{3,2},{4,7},{5,4},{6,5},{7,6},{8,11},{9,8},{10,9... | collective-permute-start | bytes 110600 | tf_op jit(solution)/shard_map/ppermute | solution.py:385
  20.8 0.9 %collective-permute-done.5.refs_1_ = bf16[3,32,192]{2,1,0:T(8,128)(2,1)S(1)} collective-permute-done((bf16[3,32,192]{2,1,0:T(8,128)(2,1)S(1)}, bf16[3,32,192]{2,1,0:T(8,128)(2,1)S(1)}, u32[]{:S(2)}, u32[]{:S(2)}) %collective-permute-start.5) | collective-permute-done | bytes 36896 | tf_op jit(solution)/shard_map/ppermute | solution.py:385
  21.7 1.3 %collective-permute-done.6.refs_2_ = bf16[3,32,192]{2,1,0:T(8,128)(2,1)S(1)} collective-permute-done((bf16[3,32,192]{2,1,0:T(8,128)(2,1)S(1)}, bf16[3,32,192]{2,1,0:T(8,128)(2,1)S(1)}, u32[]{:S(2)}, u32[]{:S(2)}) %collective-permute-start.6) | collective-permute-done | bytes 36896 | tf_op jit(solution)/shard_map/ppermute | solution.py:385
  23.7 1.2 %collective-permute-done.10.refs_3_ = bf16[32,4224]{1,0:T(8,128)(2,1)S(1)} collective-permute-done((bf16[32,4224]{1,0:T(8,128)(2,1)S(1)}, bf16[32,4224]{1,0:T(8,128)(2,1)S(1)}, u32[]{:S(2)}, u32[]{:S(2)}) %collective-permute-start.10) | collective-permute-done | bytes 270368 | tf_op jit(solution)/shard_map/ppermute | solution.py:391
  25.2 0.7 %collective-permute-start.11 = (bf16[128,256]{1,0:T(8,128)(2,1)S(1)}, bf16[128,256]{1,0:T(8,128)(2,1)S(1)}, u32[]{:S(2)}, u32[]{:S(2)}) collective-permute-start(bf16[128,256]{1,0:T(8,128)(2,1)S(1)} %get-tuple-element.68), channel_id=1, source_target_pairs={{0,1},{1,2},{2,3},{3,0},{4,5},{5,6},{6,7},{7,4},{8,9},{9,10},{10,1... | collective-permute-start | bytes 196616 | tf_op jit(solution)/shard_map/ppermute | solution.py:385
  25.8 2.8 %collective-permute-start.12 = (bf16[128,256]{1,0:T(8,128)(2,1)S(1)}, bf16[128,256]{1,0:T(8,128)(2,1)S(1)}, u32[]{:S(2)}, u32[]{:S(2)}) collective-permute-start(bf16[128,256]{1,0:T(8,128)(2,1)S(1)} %get-tuple-element.69), channel_id=1, source_target_pairs={{0,2},{1,3},{2,0},{3,1},{4,6},{5,7},{6,4},{7,5},{8,10},{9,11},{10,... | collective-permute-start | bytes 196616 | tf_op jit(solution)/shard_map/ppermute | solution.py:385
  28.6 1.1 %collective-permute-start.13 = (bf16[128,256]{1,0:T(8,128)(2,1)S(1)}, bf16[128,256]{1,0:T(8,128)(2,1)S(1)}, u32[]{:S(2)}, u32[]{:S(2)}) collective-permute-start(bf16[128,256]{1,0:T(8,128)(2,1)S(1)} %get-tuple-element.70), channel_id=1, source_target_pairs={{0,3},{1,0},{2,1},{3,2},{4,7},{5,4},{6,5},{7,6},{8,11},{9,8},{10,9... | collective-permute-start | bytes 196616 | tf_op jit(solution)/shard_map/ppermute | solution.py:385
  29.6 4.2 %raw.1 = (f32[128,768]{1,0:T(8,128)S(1)}, f32[128,768]{1,0:T(8,128)S(1)}) custom-call(bf16[32,4224]{1,0:T(8,128)(2,1)S(1)} %pad_maximum_fusion.refs_0_, bf16[32,4224]{1,0:T(8,128)(2,1)S(1)} %pad_maximum_fusion.1.refs_1_, bf16[32,4224]{1,0:T(8,128)(2,1)S(1)} %collective-permute-done.9.refs_2_, bf16[32,4224]{1,0:T(8,128)(2,1)S(1)} %collective-permute-done.10.refs_3_, ...), custom_call_target="tpu_custom_call" | custom-call | flops 1 | bytes 1 | tf_op jit(solution)/shard_map/raw/pallas_call | solution.py:191
  34.7 1.1 %down.1 = (f32[64,4096]{1,0:T(8,128)S(1)}, bf16[64,4096]{1,0:T(8,128)(2,1)S(1)}) custom-call(bf16[128,768]{1,0:T(8,128)(2,1)S(1)} %get-tuple-element.73.hidden_ref, bf16[768,4096]{1,0:T(8,128)(2,1)S(1)} %bitcast.10), custom_call_target="tpu_custom_call" | custom-call | flops 1 | bytes 1 | tf_op jit(solution)/shard_map/down/pallas_call | solution.py:250
  36.3 1.5 %collective-permute-done.15.far_ref = bf16[64,4096]{1,0:T(8,128)(2,1)S(1)} collective-permute-done((bf16[64,4096]{1,0:T(8,128)(2,1)S(1)}, bf16[64,4096]{1,0:T(8,128)(2,1)S(1)}, u32[]{:S(2)}, u32[]{:S(2)}) %collective-permute-start.15) | collective-permute-done | bytes 524320 | tf_op jit(solution)/shard_map/ppermute | solution.py:391
  37.9 1.6 %collective-permute-start.19 = (bf16[24,4096]{1,0:T(8,128)(2,1)S(1)}, bf16[24,4096]{1,0:T(8,128)(2,1)S(1)}, u32[]{:S(2)}, u32[]{:S(2)}) collective-permute-start(bf16[24,4096]{1,0:T(8,128)(2,1)S(1)} %get-tuple-element.85), channel_id=1, source_target_pairs={{0,8},{8,0},{1,9},{9,1},{2,10},{10,2},{3,11},{11,3},{4,12},{12,4},... | collective-permute-start | bytes 589832 | tf_op jit(solution)/shard_map/ppermute | solution.py:388
  39.5 1.5 %collective-permute-start.16 = (bf16[64,256]{1,0:T(8,128)(2,1)S(1)}, bf16[64,256]{1,0:T(8,128)(2,1)S(1)}, u32[]{:S(2)}, u32[]{:S(2)}) collective-permute-start(bf16[64,256]{1,0:T(8,128)(2,1)S(1)} %get-tuple-element.81), channel_id=1, source_target_pairs={{0,1},{1,2},{2,3},{3,0},{4,5},{5,6},{6,7},{7,4},{8,9},{9,10},{10,1... | collective-permute-start | bytes 98312 | tf_op jit(solution)/shard_map/ppermute | solution.py:385
  41.0 1.7 %collective-permute-start.17 = (bf16[64,256]{1,0:T(8,128)(2,1)S(1)}, bf16[64,256]{1,0:T(8,128)(2,1)S(1)}, u32[]{:S(2)}, u32[]{:S(2)}) collective-permute-start(bf16[64,256]{1,0:T(8,128)(2,1)S(1)} %get-tuple-element.82), channel_id=1, source_target_pairs={{0,2},{1,3},{2,0},{3,1},{4,6},{5,7},{6,4},{7,5},{8,10},{9,11},{10,... | collective-permute-start | bytes 98312 | tf_op jit(solution)/shard_map/ppermute | solution.py:385
  42.7 1.0 %collective-permute-start.18 = (bf16[64,256]{1,0:T(8,128)(2,1)S(1)}, bf16[64,256]{1,0:T(8,128)(2,1)S(1)}, u32[]{:S(2)}, u32[]{:S(2)}) collective-permute-start(bf16[64,256]{1,0:T(8,128)(2,1)S(1)} %get-tuple-element.83), channel_id=1, source_target_pairs={{0,3},{1,0},{2,1},{3,2},{4,7},{5,4},{6,5},{7,6},{8,11},{9,8},{10,9... | collective-permute-start | bytes 98312 | tf_op jit(solution)/shard_map/ppermute | solution.py:385
  43.8 1.6 %collective-permute-done.16.refs_1_ = bf16[64,256]{1,0:T(8,128)(2,1)S(1)} collective-permute-done((bf16[64,256]{1,0:T(8,128)(2,1)S(1)}, bf16[64,256]{1,0:T(8,128)(2,1)S(1)}, u32[]{:S(2)}, u32[]{:S(2)}) %collective-permute-start.16) | collective-permute-done | bytes 32800 | tf_op jit(solution)/shard_map/ppermute | solution.py:385
  45.4 1.0 %collective-permute-done.17.refs_2_ = bf16[64,256]{1,0:T(8,128)(2,1)S(1)} collective-permute-done((bf16[64,256]{1,0:T(8,128)(2,1)S(1)}, bf16[64,256]{1,0:T(8,128)(2,1)S(1)}, u32[]{:S(2)}, u32[]{:S(2)}) %collective-permute-start.17) | collective-permute-done | bytes 32800 | tf_op jit(solution)/shard_map/ppermute | solution.py:385
  46.9 0.6 collective-permute-start.20
  47.5 3.8 %collective-permute-done.20.refs_1_ = bf16[32,1024]{1,0:T(8,128)(2,1)S(1)} collective-permute-done((bf16[32,1024]{1,0:T(8,128)(2,1)S(1)}, bf16[32,1024]{1,0:T(8,128)(2,1)S(1)}, u32[]{:S(2)}, u32[]{:S(2)}) %collective-permute-start.20) | collective-permute-done | bytes 65568 | tf_op jit(solution)/shard_map/ppermute | solution.py:388
  51.3 1.3 %collective-permute-start.24 = (bf16[8,4096]{1,0:T(8,128)(2,1)S(1)}, bf16[8,4096]{1,0:T(8,128)(2,1)S(1)}, u32[]{:S(2)}, u32[]{:S(2)}) collective-permute-start(bf16[8,4096]{1,0:T(8,128)(2,1)S(1)} %get-tuple-element.92), channel_id=1, source_target_pairs={{0,1},{1,2},{2,3},{3,0},{4,5},{5,6},{6,7},{7,4},{8,9},{9,10},{10,1... | collective-permute-start | bytes 196616 | tf_op jit(solution)/shard_map/ppermute | solution.py:385
  52.6 2.1 %collective-permute-start.23 = (bf16[8,4096]{1,0:T(8,128)(2,1)S(1)}, bf16[8,4096]{1,0:T(8,128)(2,1)S(1)}, u32[]{:S(2)}, u32[]{:S(2)}) collective-permute-start(bf16[8,4096]{1,0:T(8,128)(2,1)S(1)} %get-tuple-element.91), channel_id=1, source_target_pairs={{0,2},{1,3},{2,0},{3,1},{4,6},{5,7},{6,4},{7,5},{8,10},{9,11},{10,... | collective-permute-start | bytes 196616 | tf_op jit(solution)/shard_map/ppermute | solution.py:385
  54.7 0.8 %collective-permute-start.22 = (bf16[8,4096]{1,0:T(8,128)(2,1)S(1)}, bf16[8,4096]{1,0:T(8,128)(2,1)S(1)}, u32[]{:S(2)}, u32[]{:S(2)}) collective-permute-start(bf16[8,4096]{1,0:T(8,128)(2,1)S(1)} %get-tuple-element.90), channel_id=1, source_target_pairs={{0,3},{1,0},{2,1},{3,2},{4,7},{5,4},{6,5},{7,6},{8,11},{9,8},{10,9... | collective-permute-start | bytes 196616 | tf_op jit(solution)/shard_map/ppermute | solution.py:385
  56.0 1.5 %collective-permute-done.24 = bf16[8,4096]{1,0:T(8,128)(2,1)S(1)} collective-permute-done((bf16[8,4096]{1,0:T(8,128)(2,1)S(1)}, bf16[8,4096]{1,0:T(8,128)(2,1)S(1)}, u32[]{:S(2)}, u32[]{:S(2)}) %collective-permute-start.24) | collective-permute-done | bytes 65568 | tf_op jit(solution)/shard_map/ppermute | solution.py:385
  57.5 1.4 %collective-permute-done.23 = bf16[8,4096]{1,0:T(8,128)(2,1)S(1)} collective-permute-done((bf16[8,4096]{1,0:T(8,128)(2,1)S(1)}, bf16[8,4096]{1,0:T(8,128)(2,1)S(1)}, u32[]{:S(2)}, u32[]{:S(2)}) %collective-permute-start.23) | collective-permute-done | bytes 65568 | tf_op jit(solution)/shard_map/ppermute | solution.py:385
  58.9 0.6 %collective-permute-done.22 = bf16[8,4096]{1,0:T(8,128)(2,1)S(1)} collective-permute-done((bf16[8,4096]{1,0:T(8,128)(2,1)S(1)}, bf16[8,4096]{1,0:T(8,128)(2,1)S(1)}, u32[]{:S(2)}, u32[]{:S(2)}) %collective-permute-start.22) | collective-permute-done | bytes 65568 | tf_op jit(solution)/shard_map/ppermute | solution.py:385
  59.7 0.7 %add_convert_fusion = bf16[8,4096]{1,0:T(8,128)(2,1)} fusion(bf16[8,4096]{1,0:T(8,128)(2,1)S(1)} %collective-permute-done.24, bf16[8,4096]{1,0:T(8,128)(2,1)S(1)} %collective-permute-done.23, bf16[8,4096]{1,0:T(8,128)(2,1)S(1)} %collective-permute-done.22, f32[8,4096]{1,0:T(8,128)S(1)} %get-tuple-element.87, bf16[8,4096]{1,0:T(8,128)(2,1)S(1)} %collective-permute-done.21), kind=kLoop, calls=%fused_computation.3 | loop fusion | flops 294912 | bytes 458752 | tf_op jit(solution)/shard_map/convert_element_type | solution.py:440
  (40 shorter events, 5.0 us)
Async XLA Ops:
  1.0 13.6 %collective-permute-start.2 = (bf16[8,4224]{1,0:T(8,128)(2,1)S(1)}, bf16[8,4224]{1,0:T(8,128)(2,1)S(1)}, u32[]{:S(2)}, u32[]{:S(2)}) collective-permute-start(bf16[8,4224]{1,0:T(8,128)(2,1)S(1)} %attach.1), channel_id=1, source_target_pairs={{0,3},{1,0},{2,1},{3,2},{4,7},{5,4},{6,5},{7,6},{8,11},{9,8},{10,9... | collective-permute-start | bytes 202760 | tf_op jit(solution)/shard_map/ppermute | solution.py:385
  6.1 8.6 %collective-permute-start.1 = (bf16[8,4224]{1,0:T(8,128)(2,1)S(1)}, bf16[8,4224]{1,0:T(8,128)(2,1)S(1)}, u32[]{:S(2)}, u32[]{:S(2)}) collective-permute-start(bf16[8,4224]{1,0:T(8,128)(2,1)S(1)} %attach.1), channel_id=1, source_target_pairs={{0,2},{1,3},{2,0},{3,1},{4,6},{5,7},{6,4},{7,5},{8,10},{9,11},{10,... | collective-permute-start | bytes 202760 | tf_op jit(solution)/shard_map/ppermute | solution.py:385
  6.1 8.6 %collective-permute-start = (bf16[8,4224]{1,0:T(8,128)(2,1)S(1)}, bf16[8,4224]{1,0:T(8,128)(2,1)S(1)}, u32[]{:S(2)}, u32[]{:S(2)}) collective-permute-start(bf16[8,4224]{1,0:T(8,128)(2,1)S(1)} %attach.1), channel_id=1, source_target_pairs={{0,1},{1,2},{2,3},{3,0},{4,5},{5,6},{6,7},{7,4},{8,9},{9,10},{10,1... | collective-permute-start | bytes 202760 | tf_op jit(solution)/shard_map/ppermute | solution.py:385
  7.1 13.2 %collective-permute-start.3 = (bf16[8,4224]{1,0:T(8,128)(2,1)S(1)}, bf16[8,4224]{1,0:T(8,128)(2,1)S(1)}, u32[]{:S(2)}, u32[]{:S(2)}) collective-permute-start(bf16[8,4224]{1,0:T(8,128)(2,1)S(1)} %attach.1), channel_id=1, source_target_pairs={{0,8},{8,0},{1,9},{9,1},{2,10},{10,2},{3,11},{11,3},{4,12},{12,4},... | collective-permute-start | bytes 202760 | tf_op jit(solution)/shard_map/ppermute | solution.py:388
  8.6 11.6 %copy-start = (bf16[4,32,1024]{2,1,0:T(8,128)(2,1)S(1)}, bf16[4,32,1024]{2,1,0:T(8,128)(2,1)}, u32[]{:S(2)}) copy-start(bf16[4,32,1024]{2,1,0:T(8,128)(2,1)} %param.23) | copy-start | bytes 786436
  14.7 5.8 %collective-permute-start.4 = (bf16[24,4224]{1,0:T(8,128)(2,1)S(1)}, bf16[24,4224]{1,0:T(8,128)(2,1)S(1)}, u32[]{:S(2)}, u32[]{:S(2)}) collective-permute-start(bf16[24,4224]{1,0:T(8,128)(2,1)S(1)} %pad_maximum_fusion.2), channel_id=1, source_target_pairs={{0,8},{8,0},{1,9},{9,1},{2,10},{10,2},{3,11},{11,3},{4,12},{12,4},... | collective-permute-start | bytes 608264 | tf_op jit(solution)/shard_map/ppermute | solution.py:388
  15.3 6.4 %collective-permute-start.5 = (bf16[3,32,192]{2,1,0:T(8,128)(2,1)S(1)}, bf16[3,32,192]{2,1,0:T(8,128)(2,1)S(1)}, u32[]{:S(2)}, u32[]{:S(2)}) collective-permute-start(bf16[3,32,192]{2,1,0:T(8,128)(2,1)S(1)} %get-tuple-element.58), channel_id=1, source_target_pairs={{0,1},{1,2},{2,3},{3,0},{4,5},{5,6},{6,7},{7,4},{8,9},{9,10},{10,1... | collective-permute-start | bytes 110600 | tf_op jit(solution)/shard_map/ppermute | solution.py:385
  17.8 5.1 %collective-permute-start.6 = (bf16[3,32,192]{2,1,0:T(8,128)(2,1)S(1)}, bf16[3,32,192]{2,1,0:T(8,128)(2,1)S(1)}, u32[]{:S(2)}, u32[]{:S(2)}) collective-permute-start(bf16[3,32,192]{2,1,0:T(8,128)(2,1)S(1)} %get-tuple-element.59), channel_id=1, source_target_pairs={{0,2},{1,3},{2,0},{3,1},{4,6},{5,7},{6,4},{7,5},{8,10},{9,11},{10,... | collective-permute-start | bytes 110600 | tf_op jit(solution)/shard_map/ppermute | solution.py:385
  18.7 4.6 %collective-permute-start.7 = (bf16[3,32,192]{2,1,0:T(8,128)(2,1)S(1)}, bf16[3,32,192]{2,1,0:T(8,128)(2,1)S(1)}, u32[]{:S(2)}, u32[]{:S(2)}) collective-permute-start(bf16[3,32,192]{2,1,0:T(8,128)(2,1)S(1)} %get-tuple-element.60), channel_id=1, source_target_pairs={{0,3},{1,0},{2,1},{3,2},{4,7},{5,4},{6,5},{7,6},{8,11},{9,8},{10,9... | collective-permute-start | bytes 110600 | tf_op jit(solution)/shard_map/ppermute | solution.py:385
  20.2 3.1 %collective-permute-start.8 = (bf16[128,1024]{1,0:T(8,128)(2,1)S(1)}, bf16[128,1024]{1,0:T(8,128)(2,1)S(1)}, u32[]{:S(2)}, u32[]{:S(2)}) collective-permute-start(bf16[128,1024]{1,0:T(8,128)(2,1)S(1)} %bitcast.11), channel_id=1, source_target_pairs={{0,4},{4,0},{1,5},{5,1},{2,6},{6,2},{3,7},{7,3},{8,12},{12,8},{9,1... | collective-permute-start | bytes 786440 | tf_op jit(solution)/shard_map/ppermute | solution.py:391
  20.5 3.2 %collective-permute-start.9 = (bf16[32,4224]{1,0:T(8,128)(2,1)S(1)}, bf16[32,4224]{1,0:T(8,128)(2,1)S(1)}, u32[]{:S(2)}, u32[]{:S(2)}) collective-permute-start(bf16[32,4224]{1,0:T(8,128)(2,1)S(1)} %pad_maximum_fusion.refs_0_), channel_id=1, source_target_pairs={{0,4},{4,0},{1,5},{5,1},{2,6},{6,2},{3,7},{7,3},{8,12},{12,8},{9,1... | collective-permute-start | bytes 811016 | tf_op jit(solution)/shard_map/ppermute | solution.py:391
  23.3 1.5 %collective-permute-start.10 = (bf16[32,4224]{1,0:T(8,128)(2,1)S(1)}, bf16[32,4224]{1,0:T(8,128)(2,1)S(1)}, u32[]{:S(2)}, u32[]{:S(2)}) collective-permute-start(bf16[32,4224]{1,0:T(8,128)(2,1)S(1)} %pad_maximum_fusion.1.refs_1_), channel_id=1, source_target_pairs={{0,4},{4,0},{1,5},{5,1},{2,6},{6,2},{3,7},{7,3},{8,12},{12,8},{9,1... | collective-permute-start | bytes 811016 | tf_op jit(solution)/shard_map/ppermute | solution.py:391
  25.2 8.7 %collective-permute-start.11 = (bf16[128,256]{1,0:T(8,128)(2,1)S(1)}, bf16[128,256]{1,0:T(8,128)(2,1)S(1)}, u32[]{:S(2)}, u32[]{:S(2)}) collective-permute-start(bf16[128,256]{1,0:T(8,128)(2,1)S(1)} %get-tuple-element.68), channel_id=1, source_target_pairs={{0,1},{1,2},{2,3},{3,0},{4,5},{5,6},{6,7},{7,4},{8,9},{9,10},{10,1... | collective-permute-start | bytes 196616 | tf_op jit(solution)/shard_map/ppermute | solution.py:385
  25.8 8.2 %collective-permute-start.12 = (bf16[128,256]{1,0:T(8,128)(2,1)S(1)}, bf16[128,256]{1,0:T(8,128)(2,1)S(1)}, u32[]{:S(2)}, u32[]{:S(2)}) collective-permute-start(bf16[128,256]{1,0:T(8,128)(2,1)S(1)} %get-tuple-element.69), channel_id=1, source_target_pairs={{0,2},{1,3},{2,0},{3,1},{4,6},{5,7},{6,4},{7,5},{8,10},{9,11},{10,... | collective-permute-start | bytes 196616 | tf_op jit(solution)/shard_map/ppermute | solution.py:385
  28.6 6.1 %slice-start = ((s8[6291456]{0:T(1024)(128)(4,1)}), s8[4194304]{0:T(1024)(128)(4,1)S(1)}, s32[]{:S(2)}) async-start(s8[6291456]{0:T(1024)(128)(4,1)} %bitcast.8), calls=%async_computation | async-start | bytes 8388608
  28.6 6.1 %slice-start.1 = ((s8[6291456]{0:T(1024)(128)(4,1)}), s8[2097152]{0:T(1024)(128)(4,1)S(1)}, s32[]{:S(2)}) async-start(s8[6291456]{0:T(1024)(128)(4,1)} %bitcast.8), calls=%async_computation.1 | async-start | bytes 4194304
  28.6 5.5 %collective-permute-start.13 = (bf16[128,256]{1,0:T(8,128)(2,1)S(1)}, bf16[128,256]{1,0:T(8,128)(2,1)S(1)}, u32[]{:S(2)}, u32[]{:S(2)}) collective-permute-start(bf16[128,256]{1,0:T(8,128)(2,1)S(1)} %get-tuple-element.70), channel_id=1, source_target_pairs={{0,3},{1,0},{2,1},{3,2},{4,7},{5,4},{6,5},{7,6},{8,11},{9,8},{10,9... | collective-permute-start | bytes 196616 | tf_op jit(solution)/shard_map/ppermute | solution.py:385
  34.6 1.2 %collective-permute-start.14 = (bf16[64,128]{1,0:T(8,128)(2,1)S(1)}, bf16[64,128]{1,0:T(8,128)(2,1)S(1)}, u32[]{:S(2)}, u32[]{:S(2)}) collective-permute-start(bf16[64,128]{1,0:T(8,128)(2,1)S(1)} %get-tuple-element.76), channel_id=1, source_target_pairs={{0,4},{4,0},{1,5},{5,1},{2,6},{6,2},{3,7},{7,3},{8,12},{12,8},{9,1... | collective-permute-start | bytes 49160 | tf_op jit(solution)/shard_map/ppermute | solution.py:391
  35.8 2.0 %collective-permute-start.15 = (bf16[64,4096]{1,0:T(8,128)(2,1)S(1)}, bf16[64,4096]{1,0:T(8,128)(2,1)S(1)}, u32[]{:S(2)}, u32[]{:S(2)}) collective-permute-start(bf16[64,4096]{1,0:T(8,128)(2,1)S(1)} %get-tuple-element.77), channel_id=1, source_target_pairs={{0,4},{4,0},{1,5},{5,1},{2,6},{6,2},{3,7},{7,3},{8,12},{12,8},{9,1... | collective-permute-start | bytes 1572872 | tf_op jit(solution)/shard_map/ppermute | solution.py:391
  37.9 13.3 %collective-permute-start.19 = (bf16[24,4096]{1,0:T(8,128)(2,1)S(1)}, bf16[24,4096]{1,0:T(8,128)(2,1)S(1)}, u32[]{:S(2)}, u32[]{:S(2)}) collective-permute-start(bf16[24,4096]{1,0:T(8,128)(2,1)S(1)} %get-tuple-element.85), channel_id=1, source_target_pairs={{0,8},{8,0},{1,9},{9,1},{2,10},{10,2},{3,11},{11,3},{4,12},{12,4},... | collective-permute-start | bytes 589832 | tf_op jit(solution)/shard_map/ppermute | solution.py:388
  39.5 5.8 %collective-permute-start.16 = (bf16[64,256]{1,0:T(8,128)(2,1)S(1)}, bf16[64,256]{1,0:T(8,128)(2,1)S(1)}, u32[]{:S(2)}, u32[]{:S(2)}) collective-permute-start(bf16[64,256]{1,0:T(8,128)(2,1)S(1)} %get-tuple-element.81), channel_id=1, source_target_pairs={{0,1},{1,2},{2,3},{3,0},{4,5},{5,6},{6,7},{7,4},{8,9},{9,10},{10,1... | collective-permute-start | bytes 98312 | tf_op jit(solution)/shard_map/ppermute | solution.py:385
  41.0 5.3 %collective-permute-start.17 = (bf16[64,256]{1,0:T(8,128)(2,1)S(1)}, bf16[64,256]{1,0:T(8,128)(2,1)S(1)}, u32[]{:S(2)}, u32[]{:S(2)}) collective-permute-start(bf16[64,256]{1,0:T(8,128)(2,1)S(1)} %get-tuple-element.82), channel_id=1, source_target_pairs={{0,2},{1,3},{2,0},{3,1},{4,6},{5,7},{6,4},{7,5},{8,10},{9,11},{10,... | collective-permute-start | bytes 98312 | tf_op jit(solution)/shard_map/ppermute | solution.py:385
  42.7 4.0 %collective-permute-start.18 = (bf16[64,256]{1,0:T(8,128)(2,1)S(1)}, bf16[64,256]{1,0:T(8,128)(2,1)S(1)}, u32[]{:S(2)}, u32[]{:S(2)}) collective-permute-start(bf16[64,256]{1,0:T(8,128)(2,1)S(1)} %get-tuple-element.83), channel_id=1, source_target_pairs={{0,3},{1,0},{2,1},{3,2},{4,7},{5,4},{6,5},{7,6},{8,11},{9,8},{10,9... | collective-permute-start | bytes 98312 | tf_op jit(solution)/shard_map/ppermute | solution.py:385
  46.9 4.3 %collective-permute-start.20 = (bf16[32,1024]{1,0:T(8,128)(2,1)S(1)}, bf16[32,1024]{1,0:T(8,128)(2,1)S(1)}, u32[]{:S(2)}, u32[]{:S(2)}) collective-permute-start(bf16[32,1024]{1,0:T(8,128)(2,1)S(1)} %get-tuple-element.86), channel_id=1, source_target_pairs={{0,8},{8,0},{1,9},{9,1},{2,10},{10,2},{3,11},{11,3},{4,12},{12,4},... | collective-permute-start | bytes 196616 | tf_op jit(solution)/shard_map/ppermute | solution.py:388
  51.3 6.2 %collective-permute-start.24 = (bf16[8,4096]{1,0:T(8,128)(2,1)S(1)}, bf16[8,4096]{1,0:T(8,128)(2,1)S(1)}, u32[]{:S(2)}, u32[]{:S(2)}) collective-permute-start(bf16[8,4096]{1,0:T(8,128)(2,1)S(1)} %get-tuple-element.92), channel_id=1, source_target_pairs={{0,1},{1,2},{2,3},{3,0},{4,5},{5,6},{6,7},{7,4},{8,9},{9,10},{10,1... | collective-permute-start | bytes 196616 | tf_op jit(solution)/shard_map/ppermute | solution.py:385
  52.6 6.3 %collective-permute-start.23 = (bf16[8,4096]{1,0:T(8,128)(2,1)S(1)}, bf16[8,4096]{1,0:T(8,128)(2,1)S(1)}, u32[]{:S(2)}, u32[]{:S(2)}) collective-permute-start(bf16[8,4096]{1,0:T(8,128)(2,1)S(1)} %get-tuple-element.91), channel_id=1, source_target_pairs={{0,2},{1,3},{2,0},{3,1},{4,6},{5,7},{6,4},{7,5},{8,10},{9,11},{10,... | collective-permute-start | bytes 196616 | tf_op jit(solution)/shard_map/ppermute | solution.py:385
  54.7 4.8 %collective-permute-start.22 = (bf16[8,4096]{1,0:T(8,128)(2,1)S(1)}, bf16[8,4096]{1,0:T(8,128)(2,1)S(1)}, u32[]{:S(2)}, u32[]{:S(2)}) collective-permute-start(bf16[8,4096]{1,0:T(8,128)(2,1)S(1)} %get-tuple-element.90), channel_id=1, source_target_pairs={{0,3},{1,0},{2,1},{3,2},{4,7},{5,4},{6,5},{7,6},{8,11},{9,8},{10,9... | collective-permute-start | bytes 196616 | tf_op jit(solution)/shard_map/ppermute | solution.py:385
  55.5 4.3 %collective-permute-start.21 = (bf16[8,4096]{1,0:T(8,128)(2,1)S(1)}, bf16[8,4096]{1,0:T(8,128)(2,1)S(1)}, u32[]{:S(2)}, u32[]{:S(2)}) collective-permute-start(bf16[8,4096]{1,0:T(8,128)(2,1)S(1)} %get-tuple-element.89), channel_id=1, source_target_pairs={{0,8},{8,0},{1,9},{9,1},{2,10},{10,2},{3,11},{11,3},{4,12},{12,4},... | collective-permute-start | bytes 196616 | tf_op jit(solution)/shard_map/ppermute | solution.py:388

commit v11 on v10

--- a/solution.py
+++ b/solution.py
@@ -34,12 +34,12 @@
 def rotated(value, rows, parts, step):
     if step == 0:
         return value
-    span = rows * parts
-    lines = []
-    for start in range(0, value.shape[0], span):
-        cut = start + span - step * rows
-        lines += [value[cut : start + span], value[start:cut]]
-    return jnp.concatenate(lines)
+    blocks = []
+    for start in range(0, value.shape[0], rows * parts):
+        for k in range(parts):
+            at = start + (k ^ step) * rows
+            blocks.append(value[at : at + rows])
+    return jnp.concatenate(blocks)
 
 
 def attach_kernel(tokens_ref, routes_ref, probs_ref, out_ref):
@@ -93,7 +93,7 @@
         value = ref[...].reshape(exp_dev * piece, hid).astype(F32)
         blocks = [value[:, j * cols : (j + 1) * cols] for j in range(parts)]
         for k in range(parts):
-            target = lax.rem(me + k, parts)
+            target = me ^ k
             block = blocks[0]
             for j in range(1, parts):
                 block = jnp.where(target == j, blocks[j], block)
@@ -128,7 +128,7 @@
     me = lax.axis_index("mp")
     row = lax.broadcasted_iota(jnp.int32, (ranks, ranks), 0)
     col = lax.broadcasted_iota(jnp.int32, (ranks, ranks), 1)
-    step = lax.rem(me - row % rank // piece + parts, parts)
+    step = me ^ (row % rank // piece)
     source = (step * exp_dev + row // rank) * piece + row % piece
     order = (col == source).astype(F32).astype(BF)
     cols = hid // exp_dev
@@ -259,44 +259,40 @@
     )(hidden, down_w)
 
 
-def turn_kernel(rows, near_ref, far_ref, *out_refs):
+def pair_kernel(near_ref, far_ref, *out_refs):
     value = jnp.concatenate([near_ref[...].astype(F32), far_ref[...].astype(F32)], axis=1)
-    for k, out_ref in enumerate(out_refs):
-        out_ref[...] = rotated(value, rows, len(out_refs), k).astype(BF)
-
-
-def turn(near, far, parts, rows):
+    span = out_refs[0].shape[0]
+    for n, out_ref in enumerate(out_refs):
+        out_ref[...] = value[n * span : (n + 1) * span].astype(BF)
+
+
+def side_by_side(near, far, chips):
     total, ranks = near.shape
     return pl.pallas_call(
-        functools.partial(turn_kernel, rows),
-        out_shape=[jax.ShapeDtypeStruct((total, 2 * ranks), BF)] * parts,
+        pair_kernel,
+        out_shape=[jax.ShapeDtypeStruct((total // chips, 2 * ranks), BF)] * chips,
         compiler_params=pltpu.CompilerParams(vmem_limit_bytes=SMALL_LIMIT),
         cost_estimate=BRIEF,
+        name="pair",
+    )(near, far)
+
+
+def turn_kernel(rows, chips, *refs):
+    ins, outs = refs[:chips], refs[chips:]
+    value = jnp.concatenate([ref[...].astype(F32) for ref in ins], axis=1)
+    for k, out_ref in enumerate(outs):
+        out_ref[...] = rotated(value, rows, len(outs), k).astype(BF)
+
+
+def turn(lines, parts, rows):
+    span, ranks = lines[0].shape
+    return pl.pallas_call(
+        functools.partial(turn_kernel, rows, len(lines)),
+        out_shape=[jax.ShapeDtypeStruct((span, len(lines) * ranks), BF)] * parts,
+        compiler_params=pltpu.CompilerParams(vmem_limit_bytes=SMALL_LIMIT),
+        cost_estimate=BRIEF,
         name="turn",
-    )(near, far)
-
-
-def extra_kernel(chips, near_ref, far_ref, *refs):
-    bottom, own_ref, outs = refs[: -chips], refs[-chips], refs[len(refs) - chips + 1 :]
-    ranks, span = near_ref.shape[0], own_ref.shape[0]
-    low = sum(ref[...].astype(F32) for ref in bottom).astype(BF)
-    value = dot_nn(low[:, :ranks], near_ref[...]) + dot_nn(low[:, ranks:], far_ref[...])
-    own_ref[...] = value[:span]
-    for n, out_ref in enumerate(outs):
-        out_ref[...] = value[(n + 1) * span : (n + 2) * span].astype(BF)
-
-
-def extra_products(near, far, bottom, chips):
-    span = bottom[0].shape[0] // chips
-    block = near.shape[1]
-    return pl.pallas_call(
-        functools.partial(extra_kernel, chips),
-        out_shape=[jax.ShapeDtypeStruct((span, block), F32)]
-        + [jax.ShapeDtypeStruct((span, block), BF)] * (chips - 1),
-        compiler_params=pltpu.CompilerParams(vmem_limit_bytes=VMEM_LIMIT),
-        cost_estimate=BRIEF,
-        name="extra",
-    )(near, far, *bottom)
+    )(*lines)
 
 
 def fold_kernel(head, near_ref, far_ref, own_ref, *out_refs):
@@ -323,38 +319,42 @@
     )(near, far)
 
 
-def merge_kernel(count, own_ref, low_ref, *refs):
-    backs, lows, outs = refs[:count], refs[count : 2 * count], refs[2 * count :]
+def merge_kernel(chips, parts, *refs):
+    own_ref, rights, refs = refs[0], refs[1 : 1 + 2 * chips], refs[1 + 2 * chips :]
+    bottom, backs, outs = refs[:parts], refs[parts:-parts], refs[-parts:]
     rows = outs[0].shape[0]
-    block = low_ref.shape[1]
+    ranks, block = rights[0].shape
     offset = pl.multiple_of(lax.axis_index("mp") * block, 128)
-    low = low_ref[...]
-    for ref in lows:
-        low += ref[...].astype(F32)
+    low = sum(ref[...].astype(F32) for ref in bottom).astype(BF)
+    value = jnp.zeros((low.shape[0], block), F32)
+    for n, ref in enumerate(rights):
+        at = (2 * n if n < chips else 2 * (n - chips) + 1) * ranks
+        value += dot_nn(low[:, at : at + ranks], ref[...])
     total = own_ref[rows:]
-    part = own_ref[:, pl.ds(offset, block)] + low
-    after_own = part[rows:]
+    value += own_ref[:, pl.ds(offset, block)]
+    rest = value[rows:]
     for ref in backs:
         total += ref[...].astype(F32)
-        after_own += ref[:, pl.ds(offset, block)].astype(F32)
+        rest += ref[:, pl.ds(offset, block)].astype(F32)
     outs[0][...] = own_ref[:rows]
-    outs[0][:, pl.ds(offset, block)] = part[:rows]
-    for k in range(1, len(outs)):
+    outs[0][:, pl.ds(offset, block)] = value[:rows]
+    for k in range(1, parts):
         span = slice((k - 1) * rows, k * rows)
         outs[k][...] = total[span].astype(BF)
-        outs[k][:, pl.ds(offset, block)] = after_own[span].astype(BF)
-
-
-def merge(own, low, backs, lows, rows):
+        outs[k][:, pl.ds(offset, block)] = rest[span].astype(BF)
+
+
+def merge(own, rights, bottom, backs, rows):
     total, width = own.shape
-    return pl.pallas_call(
-        functools.partial(merge_kernel, len(backs)),
+    parts = total // rows
+    return pl.pallas_call(
+        functools.partial(merge_kernel, len(backs) + 1, parts),
         out_shape=[jax.ShapeDtypeStruct((rows, width), F32)]
-        + [jax.ShapeDtypeStruct((rows, width), BF)] * (total // rows - 1),
+        + [jax.ShapeDtypeStruct((rows, width), BF)] * (parts - 1),
         compiler_params=pltpu.CompilerParams(vmem_limit_bytes=VMEM_LIMIT),
         cost_estimate=BRIEF,
         name="merge",
-    )(own, low, *backs, *lows)
+    )(own, *rights, *bottom, *backs)
 
 
 def local(
@@ -382,7 +382,7 @@
     hid = exp_dev * cols
 
     def along_z(value, step):
-        return lax.ppermute(value, "mp", [(i, (i + step) % parts) for i in range(parts)])
+        return lax.ppermute(value, "mp", [(i, i ^ step) for i in range(parts)])
 
     def along_y(value, step):
         return lax.ppermute(value, "y", [(i, (i + step) % chips) for i in range(chips)])
@@ -398,16 +398,15 @@
     gate_w, up_w, left, *small = prepare(
         (gate_right, up_right, down_left), (gate_left, up_left), weights, parts
     )
+    right = down_right.reshape(ranks, block)
     rest = after(jnp.concatenate(arrived), (left, small, gate_w, up_w))
     lines = [jnp.concatenate([sent, rest])]
     partner = [other_core(lines[0])]
     small = after(tuple(small), rest)
     small = [small[0]] + [along_z(small[k], k) for k in range(1, parts)]
-    right = after(down_right.reshape(ranks, block), rest)
-    partner_right = other_core(right)
     for s in range(1, chips):
         line = jnp.concatenate([first[s - 1], along_y(rest, s)])
-        line = after(line, (tuple(small), partner_right))
+        line = after(line, tuple(small))
         lines.append(line)
         partner.append(other_core(line))
     lines += partner
@@ -415,29 +414,33 @@
 
     lines = after(tuple(lines), diag)
     inner = inner_products(lines, left, parts, rows)
-    inner = [inner[0]] + [along_z(inner[k], k) for k in range(1, parts)]
+    inner = [along_z(inner[k], k) for k in range(parts - 1, 0, -1)] + [inner[0]]
     raw = raw_products(lines, gate_w, up_w)
+    right = after(right, lines[chips - 1])
+    rights = [right] + [along_y(right, -s) for s in range(1, chips)]
+    raw = after(tuple(raw), rights[1:])
+    rights += [other_core(right) for right in rights]
     hidden, near, far = hidden_units(
         lines, inner, raw, diag, parts, exp_dev, pair
     )
     swapped = other_core(far)
-    bottom = turn(near, swapped, parts, rows)
-    bottom = [bottom[0]] + [along_z(bottom[k], k) for k in range(1, parts)]
+    low, *lows = side_by_side(near, swapped, chips)
+    lows = [along_y(lows[s - 1], -s) for s in range(1, chips)]
+    bottom = turn([low] + lows, parts, rows)
+    bottom = [along_z(bottom[k], k) for k in range(parts - 1, 0, -1)] + [bottom[0]]
 
     near, far = down_products(hidden, w_down.reshape(hid, width))
-    out, *others = fold(near, other_core(after(far, swapped)), chips, rows)
+    far = after(other_core(after(far, swapped)), lows)
+    out, *others = fold(near, far, chips, rows)
     backs = [along_y(others[2 * s - 1], -s) for s in range(1, chips)]
-
-    low, *lows = extra_products(right, partner_right, bottom, chips)
-    lows = [along_y(lows[s - 1], -s) for s in range(1, chips)]
-
-    heads = [along_y(after(others[2 * s - 2], backs[s - 1]), -s) for s in range(1, chips)]
-    result, *pieces = merge(out, low, backs, lows, rows)
+    heads = [along_y(after(others[2 * s - 2], bottom[0]), -s) for s in range(1, chips)]
+    own, *pieces = merge(out, rights, bottom, backs, rows)
+    result = along_z(pieces[-1], parts - 1).astype(F32)
+    for k in range(parts - 2, 0, -1):
+        result += along_z(pieces[k - 1], k).astype(F32)
     for piece in heads:
         result += piece.astype(F32)
-    for k in range(1, parts):
-        result += along_z(pieces[k - 1], -k).astype(F32)
-    return result.astype(BF)
+    return (result + own).astype(BF)
 
 
 def solution(mesh):

time: 60.6 us -> 63.1 us (1.041)
  waiting for transfers between devices: 16.2 us -> 20.3 us
  starting transfers between devices: 29.6 us -> 27.9 us
    ppermute x15, waiting for transfers between devices: 9.2 us -> 14.9 us  [along_z(): return lax.ppermute(value, 'mp', [(i, i ^ step) for i in range(parts)])]
    ppermute x15, starting transfers between devices: 24 us -> 20.7 us  [along_z(): return lax.ppermute(value, 'mp', [(i, i ^ step) for i in range(parts)])]
    ppermute x5 -> x6, waiting for transfers between devices: 2.77 us -> 1.24 us  [other_core(): return lax.ppermute(value, 'core', [(0, 1), (1, 0)])]
    ppermute x5 -> x6, starting transfers between devices: 4.77 us -> 6.21 us  [along_y(): lax.ppermute(value, 'y', [(i, (i + step) % chips) for i in range(chips)])]
    ppermute x5 -> x6, waiting for transfers between devices: 4.2 us -> 4.18 us  [along_y(): lax.ppermute(value, 'y', [(i, (i + step) % chips) for i in range(chips)])]
  transfers between devices with their start and end apart: 25 -> 27, of which waited for: 16 -> 10; matrix products, arithmetic and copies ran while one was open for 0% -> 0% of each run, Pallas kernels for 20% -> 20%
where the time goes in v11:
time: 63.1 us; the launch traced here: 62.9 us
  starting transfers between devices  27.9 us (44%)
  waiting for transfers between devices  20.3 us (32%)
  Pallas kernels  13.8 us (22%)
  other arithmetic  0.73 us (1%)
    ppermute x15, starting transfers between devices, along_z(): return lax.ppermute(value, 'mp', [(i, i ^ step) for i in range(parts)])  20.7 us
    ppermute x15, waiting for transfers between devices, along_z(): return lax.ppermute(value, 'mp', [(i, i ^ step) for i in range(parts)])  14.9 us
    ppermute x6, starting transfers between devices, along_y(): lax.ppermute(value, 'y', [(i, (i + step) % chips) for i in range(chips)])  6.21 us
    pallas_call x1, Pallas kernels, prepare(): pl.pallas_call(functools.partial(prepare_kernel, parts), in_specs=[vmem]...  5.99 us
    ppermute x6, waiting for transfers between devices, along_y(): lax.ppermute(value, 'y', [(i, (i + step) % chips) for i in range(chips)])  4.18 us
    pallas_call x1, Pallas kernels, raw_products(): pl.pallas_call(functools.partial(raw_kernel, len(lines), tile), out_shape...  4.18 us
  transfers between devices with their start and end apart: 27, of which 10 were waited for; matrix products, arithmetic and copies ran while one was open for 0% of the time, Pallas kernels for 20%

profile of v11, /device:TPU:0, one launch (start us, length us, event | category | flops | bytes accessed | tf_op | source)
XLA Modules:
  0.0 62.9 jit_solution(2167609954453828287)
XLA Ops:
  0.0 0.9 %attach.1 = bf16[8,4224]{1,0:T(8,128)(2,1)S(1)} custom-call(bf16[8,4096]{1,0:T(8,128)(2,1)} %tokens_ref.1, s32[8,8]{1,0:T(8,128)} %routes_ref.1, f32[8,8]{1,0:T(8,128)} %probs_ref.1), custom_call_target="tpu_custom_call" | custom-call | flops 1 | bytes 1 | tf_op jit(solution)/shard_map/attach/pallas_call | solution.py:62
  1.0 5.1 %collective-permute-start.2 = (bf16[8,4224]{1,0:T(8,128)(2,1)S(1)}, bf16[8,4224]{1,0:T(8,128)(2,1)S(1)}, u32[]{:S(2)}, u32[]{:S(2)}) collective-permute-start(bf16[8,4224]{1,0:T(8,128)(2,1)S(1)} %attach.1), channel_id=1, source_target_pairs={{0,3},{1,2},{2,1},{3,0},{4,7},{5,6},{6,5},{7,4},{8,11},{9,10},{10,... | collective-permute-start | bytes 202760 | tf_op jit(solution)/shard_map/ppermute | solution.py:385
  6.1 0.6 %collective-permute-start = (bf16[8,4224]{1,0:T(8,128)(2,1)S(1)}, bf16[8,4224]{1,0:T(8,128)(2,1)S(1)}, u32[]{:S(2)}, u32[]{:S(2)}) collective-permute-start(bf16[8,4224]{1,0:T(8,128)(2,1)S(1)} %attach.1), channel_id=1, source_target_pairs={{0,1},{1,0},{2,3},{3,2},{4,5},{5,4},{6,7},{7,6},{8,9},{9,8},{10,11... | collective-permute-start | bytes 202760 | tf_op jit(solution)/shard_map/ppermute | solution.py:385
  6.7 1.7 %collective-permute-start.3 = (bf16[8,4224]{1,0:T(8,128)(2,1)S(1)}, bf16[8,4224]{1,0:T(8,128)(2,1)S(1)}, u32[]{:S(2)}, u32[]{:S(2)}) collective-permute-start(bf16[8,4224]{1,0:T(8,128)(2,1)S(1)} %attach.1), channel_id=1, source_target_pairs={{0,8},{8,0},{1,9},{9,1},{2,10},{10,2},{3,11},{11,3},{4,12},{12,4},... | collective-permute-start | bytes 202760 | tf_op jit(solution)/shard_map/ppermute | solution.py:388
  8.4 6.0 %prepare.1 = (bf16[768,4096]{1,0:T(8,128)(2,1)S(1)}, bf16[768,4096]{1,0:T(8,128)(2,1)S(1)}, bf16[256,1024]{1,0:T(8,128)(2,1)S(1)}, bf16[3,32,192]{2,1,0:T(8,128)...) custom-call(bf16[4,8,768]{2,1,0:T(8,128)(2,1)} %refs_0_.1, ...), custom_call_target="tpu_custom_call" | custom-call | flops 1 | bytes 1 | tf_op jit(solution)/shard_map/prepare/pallas_call | solution.py:109
  14.9 1.5 %collective-permute-start.5 = (bf16[3,32,192]{2,1,0:T(8,128)(2,1)S(1)}, bf16[3,32,192]{2,1,0:T(8,128)(2,1)S(1)}, u32[]{:S(2)}, u32[]{:S(2)}) collective-permute-start(bf16[3,32,192]{2,1,0:T(8,128)(2,1)S(1)} %get-tuple-element.61), channel_id=1, source_target_pairs={{0,1},{1,0},{2,3},{3,2},{4,5},{5,4},{6,7},{7,6},{8,9},{9,8},{10,11... | collective-permute-start | bytes 110600 | tf_op jit(solution)/shard_map/ppermute | solution.py:385
  16.3 2.9 %collective-permute-start.6 = (bf16[3,32,192]{2,1,0:T(8,128)(2,1)S(1)}, bf16[3,32,192]{2,1,0:T(8,128)(2,1)S(1)}, u32[]{:S(2)}, u32[]{:S(2)}) collective-permute-start(bf16[3,32,192]{2,1,0:T(8,128)(2,1)S(1)} %get-tuple-element.62), channel_id=1, source_target_pairs={{0,2},{1,3},{2,0},{3,1},{4,6},{5,7},{6,4},{7,5},{8,10},{9,11},{10,... | collective-permute-start | bytes 110600 | tf_op jit(solution)/shard_map/ppermute | solution.py:385
  19.4 0.9 %collective-permute-done.4 = bf16[24,4224]{1,0:T(8,128)(2,1)S(1)} collective-permute-done((bf16[24,4224]{1,0:T(8,128)(2,1)S(1)}, bf16[24,4224]{1,0:T(8,128)(2,1)S(1)}, u32[]{:S(2)}, u32[]{:S(2)}) %collective-permute-start.4) | collective-permute-done | bytes 202784 | tf_op jit(solution)/shard_map/ppermute | solution.py:388
  20.3 2.1 %collective-permute-done.6.refs_2_ = bf16[3,32,192]{2,1,0:T(8,128)(2,1)S(1)} collective-permute-done((bf16[3,32,192]{2,1,0:T(8,128)(2,1)S(1)}, bf16[3,32,192]{2,1,0:T(8,128)(2,1)S(1)}, u32[]{:S(2)}, u32[]{:S(2)}) %collective-permute-start.6) | collective-permute-done | bytes 36896 | tf_op jit(solution)/shard_map/ppermute | solution.py:385
  22.4 2.8 %collective-permute-done.7.refs_3_ = bf16[3,32,192]{2,1,0:T(8,128)(2,1)S(1)} collective-permute-done((bf16[3,32,192]{2,1,0:T(8,128)(2,1)S(1)}, bf16[3,32,192]{2,1,0:T(8,128)(2,1)S(1)}, u32[]{:S(2)}, u32[]{:S(2)}) %collective-permute-start.7) | collective-permute-done | bytes 36896 | tf_op jit(solution)/shard_map/ppermute | solution.py:385
  25.5 1.2 %collective-permute-done.9.refs_3_ = bf16[32,4224]{1,0:T(8,128)(2,1)S(1)} collective-permute-done((bf16[32,4224]{1,0:T(8,128)(2,1)S(1)}, bf16[32,4224]{1,0:T(8,128)(2,1)S(1)}, u32[]{:S(2)}, u32[]{:S(2)}) %collective-permute-start.9) | collective-permute-done | bytes 270368 | tf_op jit(solution)/shard_map/ppermute | solution.py:391
  26.7 1.5 %collective-permute-start.13 = (bf16[128,1024]{1,0:T(8,128)(2,1)S(1)}, bf16[128,1024]{1,0:T(8,128)(2,1)S(1)}, u32[]{:S(2)}, u32[]{:S(2)}) collective-permute-start(bf16[128,1024]{1,0:T(8,128)(2,1)S(1)} %bitcast.11), channel_id=1, source_target_pairs={{0,8},{8,0},{1,9},{9,1},{2,10},{10,2},{3,11},{11,3},{4,12},{12,4},... | collective-permute-start | bytes 786440 | tf_op jit(solution)/shard_map/ppermute | solution.py:388
  28.5 0.6 collective-permute-start.10
  29.1 3.9 %collective-permute-start.12 = (bf16[128,256]{1,0:T(8,128)(2,1)S(1)}, bf16[128,256]{1,0:T(8,128)(2,1)S(1)}, u32[]{:S(2)}, u32[]{:S(2)}) collective-permute-start(bf16[128,256]{1,0:T(8,128)(2,1)S(1)} %get-tuple-element.71), channel_id=1, source_target_pairs={{0,1},{1,0},{2,3},{3,2},{4,5},{5,4},{6,7},{7,6},{8,9},{9,8},{10,11... | collective-permute-start | bytes 196616 | tf_op jit(solution)/shard_map/ppermute | solution.py:385
  33.0 4.2 %raw.1 = (f32[128,768]{1,0:T(8,128)S(1)}, f32[128,768]{1,0:T(8,128)S(1)}) custom-call(bf16[32,4224]{1,0:T(8,128)(2,1)S(1)} %pad_maximum_fusion.refs_0_, bf16[32,4224]{1,0:T(8,128)(2,1)S(1)} %pad_maximum_fusion.1.refs_1_, bf16[32,4224]{1,0:T(8,128)(2,1)S(1)} %collective-permute-done.8.refs_2_, bf16[32,4224]{1,0:T(8,128)(2,1)S(1)} %collective-permute-done.9.refs_3_, ...), custom_call_target="tpu_custom_call" | custom-call | flops 1 | bytes 1 | tf_op jit(solution)/shard_map/raw/pallas_call | solution.py:191
  37.2 0.5 hidden.1
  37.9 1.1 %down.1 = (f32[64,4096]{1,0:T(8,128)S(1)}, bf16[64,4096]{1,0:T(8,128)(2,1)S(1)}) custom-call(bf16[128,768]{1,0:T(8,128)(2,1)S(1)} %get-tuple-element.78.hidden_ref, bf16[768,4096]{1,0:T(8,128)(2,1)S(1)} %bitcast.10), custom_call_target="tpu_custom_call" | custom-call | flops 1 | bytes 1 | tf_op jit(solution)/shard_map/down/pallas_call | solution.py:250
  39.0 0.5 collective-permute-start.15
  39.6 0.4 collective-permute-start.18
  40.0 0.5 collective-permute-start.16
  40.5 3.2 %collective-permute-done.16.refs_1_ = bf16[32,256]{1,0:T(8,128)(2,1)S(1)} collective-permute-done((bf16[32,256]{1,0:T(8,128)(2,1)S(1)}, bf16[32,256]{1,0:T(8,128)(2,1)S(1)}, u32[]{:S(2)}, u32[]{:S(2)}) %collective-permute-start.16) | collective-permute-done | bytes 16416 | tf_op jit(solution)/shard_map/ppermute | solution.py:388
  43.8 0.6 collective-permute-start.22
  44.4 0.9 %collective-permute-start.19 = (bf16[32,512]{1,0:T(8,128)(2,1)S(1)}, bf16[32,512]{1,0:T(8,128)(2,1)S(1)}, u32[]{:S(2)}, u32[]{:S(2)}) collective-permute-start(bf16[32,512]{1,0:T(8,128)(2,1)S(1)} %get-tuple-element.88), channel_id=1, source_target_pairs={{0,3},{1,2},{2,1},{3,0},{4,7},{5,6},{6,5},{7,4},{8,11},{9,10},{10,... | collective-permute-start | bytes 98312 | tf_op jit(solution)/shard_map/ppermute | solution.py:385
  45.3 0.7 %collective-permute-start.20 = (bf16[32,512]{1,0:T(8,128)(2,1)S(1)}, bf16[32,512]{1,0:T(8,128)(2,1)S(1)}, u32[]{:S(2)}, u32[]{:S(2)}) collective-permute-start(bf16[32,512]{1,0:T(8,128)(2,1)S(1)} %get-tuple-element.89), channel_id=1, source_target_pairs={{0,2},{1,3},{2,0},{3,1},{4,6},{5,7},{6,4},{7,5},{8,10},{9,11},{10,... | collective-permute-start | bytes 98312 | tf_op jit(solution)/shard_map/ppermute | solution.py:385
  46.0 4.3 %collective-permute-done.19.refs_5_ = bf16[32,512]{1,0:T(8,128)(2,1)S(1)} collective-permute-done((bf16[32,512]{1,0:T(8,128)(2,1)S(1)}, bf16[32,512]{1,0:T(8,128)(2,1)S(1)}, u32[]{:S(2)}, u32[]{:S(2)}) %collective-permute-start.19) | collective-permute-done | bytes 32800 | tf_op jit(solution)/shard_map/ppermute | solution.py:385
  50.3 1.5 %collective-permute-start.26 = (bf16[8,4096]{1,0:T(8,128)(2,1)S(1)}, bf16[8,4096]{1,0:T(8,128)(2,1)S(1)}, u32[]{:S(2)}, u32[]{:S(2)}) collective-permute-start(bf16[8,4096]{1,0:T(8,128)(2,1)S(1)} %get-tuple-element.97), channel_id=1, source_target_pairs={{0,8},{8,0},{1,9},{9,1},{2,10},{10,2},{3,11},{11,3},{4,12},{12,4},... | collective-permute-start | bytes 196616 | tf_op jit(solution)/shard_map/ppermute | solution.py:388
  51.8 2.7 %collective-permute-done.21.refs_7_ = bf16[32,512]{1,0:T(8,128)(2,1)S(1)} collective-permute-done((bf16[32,512]{1,0:T(8,128)(2,1)S(1)}, bf16[32,512]{1,0:T(8,128)(2,1)S(1)}, u32[]{:S(2)}, u32[]{:S(2)}) %collective-permute-start.21) | collective-permute-done | bytes 32800 | tf_op jit(solution)/shard_map/ppermute | solution.py:385
  54.9 1.2 %collective-permute-start.24 = (bf16[8,4096]{1,0:T(8,128)(2,1)S(1)}, bf16[8,4096]{1,0:T(8,128)(2,1)S(1)}, u32[]{:S(2)}, u32[]{:S(2)}) collective-permute-start(bf16[8,4096]{1,0:T(8,128)(2,1)S(1)} %get-tuple-element.94), channel_id=1, source_target_pairs={{0,2},{1,3},{2,0},{3,1},{4,6},{5,7},{6,4},{7,5},{8,10},{9,11},{10,... | collective-permute-start | bytes 196616 | tf_op jit(solution)/shard_map/ppermute | solution.py:385
  56.1 3.2 %collective-permute-start.23 = (bf16[8,4096]{1,0:T(8,128)(2,1)S(1)}, bf16[8,4096]{1,0:T(8,128)(2,1)S(1)}, u32[]{:S(2)}, u32[]{:S(2)}) collective-permute-start(bf16[8,4096]{1,0:T(8,128)(2,1)S(1)} %get-tuple-element.93), channel_id=1, source_target_pairs={{0,3},{1,2},{2,1},{3,0},{4,7},{5,6},{6,5},{7,4},{8,11},{9,10},{10,... | collective-permute-start | bytes 196616 | tf_op jit(solution)/shard_map/ppermute | solution.py:385
  59.3 0.8 %collective-permute-done.24 = bf16[8,4096]{1,0:T(8,128)(2,1)S(1)} collective-permute-done((bf16[8,4096]{1,0:T(8,128)(2,1)S(1)}, bf16[8,4096]{1,0:T(8,128)(2,1)S(1)}, u32[]{:S(2)}, u32[]{:S(2)}) %collective-permute-start.24) | collective-permute-done | bytes 65568 | tf_op jit(solution)/shard_map/ppermute | solution.py:385
  60.2 2.1 %collective-permute-done.23 = bf16[8,4096]{1,0:T(8,128)(2,1)S(1)} collective-permute-done((bf16[8,4096]{1,0:T(8,128)(2,1)S(1)}, bf16[8,4096]{1,0:T(8,128)(2,1)S(1)}, u32[]{:S(2)}, u32[]{:S(2)}) %collective-permute-start.23) | collective-permute-done | bytes 65568 | tf_op jit(solution)/shard_map/ppermute | solution.py:385
  62.3 0.7 %add_convert_fusion = bf16[8,4096]{1,0:T(8,128)(2,1)} fusion(f32[8,4096]{1,0:T(8,128)S(1)} %get-tuple-element.98, bf16[8,4096]{1,0:T(8,128)(2,1)S(1)} %collective-permute-done.26, bf16[8,4096]{1,0:T(8,128)(2,1)S(1)} %collective-permute-done.25, bf16[8,4096]{1,0:T(8,128)(2,1)S(1)} %collective-permute-done.24, bf16[8,4096]{1,0:T(8,128)(2,1)S(1)} %collective-permute-done.23), kind=kLoop, calls=%fused_computation.3 | loop fusion | flops 294912 | bytes 458752 | tf_op jit(solution)/shard_map/convert_element_type | solution.py:443
  (44 shorter events, 2.0 us)
Async XLA Ops:
  1.0 13.4 %collective-permute-start.2 = (bf16[8,4224]{1,0:T(8,128)(2,1)S(1)}, bf16[8,4224]{1,0:T(8,128)(2,1)S(1)}, u32[]{:S(2)}, u32[]{:S(2)}) collective-permute-start(bf16[8,4224]{1,0:T(8,128)(2,1)S(1)} %attach.1), channel_id=1, source_target_pairs={{0,3},{1,2},{2,1},{3,0},{4,7},{5,6},{6,5},{7,4},{8,11},{9,10},{10,... | collective-permute-start | bytes 202760 | tf_op jit(solution)/shard_map/ppermute | solution.py:385
  6.1 8.3 %collective-permute-start.1 = (bf16[8,4224]{1,0:T(8,128)(2,1)S(1)}, bf16[8,4224]{1,0:T(8,128)(2,1)S(1)}, u32[]{:S(2)}, u32[]{:S(2)}) collective-permute-start(bf16[8,4224]{1,0:T(8,128)(2,1)S(1)} %attach.1), channel_id=1, source_target_pairs={{0,2},{1,3},{2,0},{3,1},{4,6},{5,7},{6,4},{7,5},{8,10},{9,11},{10,... | collective-permute-start | bytes 202760 | tf_op jit(solution)/shard_map/ppermute | solution.py:385
  6.1 8.3 %collective-permute-start = (bf16[8,4224]{1,0:T(8,128)(2,1)S(1)}, bf16[8,4224]{1,0:T(8,128)(2,1)S(1)}, u32[]{:S(2)}, u32[]{:S(2)}) collective-permute-start(bf16[8,4224]{1,0:T(8,128)(2,1)S(1)} %attach.1), channel_id=1, source_target_pairs={{0,1},{1,0},{2,3},{3,2},{4,5},{5,4},{6,7},{7,6},{8,9},{9,8},{10,11... | collective-permute-start | bytes 202760 | tf_op jit(solution)/shard_map/ppermute | solution.py:385
  6.7 12.6 %collective-permute-start.3 = (bf16[8,4224]{1,0:T(8,128)(2,1)S(1)}, bf16[8,4224]{1,0:T(8,128)(2,1)S(1)}, u32[]{:S(2)}, u32[]{:S(2)}) collective-permute-start(bf16[8,4224]{1,0:T(8,128)(2,1)S(1)} %attach.1), channel_id=1, source_target_pairs={{0,8},{8,0},{1,9},{9,1},{2,10},{10,2},{3,11},{11,3},{4,12},{12,4},... | collective-permute-start | bytes 202760 | tf_op jit(solution)/shard_map/ppermute | solution.py:388
  8.4 18.3 %copy-start = (bf16[4,32,1024]{2,1,0:T(8,128)(2,1)S(1)}, bf16[4,32,1024]{2,1,0:T(8,128)(2,1)}, u32[]{:S(2)}) copy-start(bf16[4,32,1024]{2,1,0:T(8,128)(2,1)} %param.23) | copy-start | bytes 786436
  14.4 5.9 %collective-permute-start.4 = (bf16[24,4224]{1,0:T(8,128)(2,1)S(1)}, bf16[24,4224]{1,0:T(8,128)(2,1)S(1)}, u32[]{:S(2)}, u32[]{:S(2)}) collective-permute-start(bf16[24,4224]{1,0:T(8,128)(2,1)S(1)} %pad_maximum_fusion.2), channel_id=1, source_target_pairs={{0,8},{8,0},{1,9},{9,1},{2,10},{10,2},{3,11},{11,3},{4,12},{12,4},... | collective-permute-start | bytes 608264 | tf_op jit(solution)/shard_map/ppermute | solution.py:388
  14.9 5.4 %collective-permute-start.5 = (bf16[3,32,192]{2,1,0:T(8,128)(2,1)S(1)}, bf16[3,32,192]{2,1,0:T(8,128)(2,1)S(1)}, u32[]{:S(2)}, u32[]{:S(2)}) collective-permute-start(bf16[3,32,192]{2,1,0:T(8,128)(2,1)S(1)} %get-tuple-element.61), channel_id=1, source_target_pairs={{0,1},{1,0},{2,3},{3,2},{4,5},{5,4},{6,7},{7,6},{8,9},{9,8},{10,11... | collective-permute-start | bytes 110600 | tf_op jit(solution)/shard_map/ppermute | solution.py:385
  16.3 6.0 %collective-permute-start.6 = (bf16[3,32,192]{2,1,0:T(8,128)(2,1)S(1)}, bf16[3,32,192]{2,1,0:T(8,128)(2,1)S(1)}, u32[]{:S(2)}, u32[]{:S(2)}) collective-permute-start(bf16[3,32,192]{2,1,0:T(8,128)(2,1)S(1)} %get-tuple-element.62), channel_id=1, source_target_pairs={{0,2},{1,3},{2,0},{3,1},{4,6},{5,7},{6,4},{7,5},{8,10},{9,11},{10,... | collective-permute-start | bytes 110600 | tf_op jit(solution)/shard_map/ppermute | solution.py:385
  19.3 5.9 %collective-permute-start.7 = (bf16[3,32,192]{2,1,0:T(8,128)(2,1)S(1)}, bf16[3,32,192]{2,1,0:T(8,128)(2,1)S(1)}, u32[]{:S(2)}, u32[]{:S(2)}) collective-permute-start(bf16[3,32,192]{2,1,0:T(8,128)(2,1)S(1)} %get-tuple-element.63), channel_id=1, source_target_pairs={{0,3},{1,2},{2,1},{3,0},{4,7},{5,6},{6,5},{7,4},{8,11},{9,10},{10,... | collective-permute-start | bytes 110600 | tf_op jit(solution)/shard_map/ppermute | solution.py:385
  19.3 6.2 %collective-permute-start.8 = (bf16[32,4224]{1,0:T(8,128)(2,1)S(1)}, bf16[32,4224]{1,0:T(8,128)(2,1)S(1)}, u32[]{:S(2)}, u32[]{:S(2)}) collective-permute-start(bf16[32,4224]{1,0:T(8,128)(2,1)S(1)} %pad_maximum_fusion.refs_0_), channel_id=1, source_target_pairs={{0,4},{4,0},{1,5},{5,1},{2,6},{6,2},{3,7},{7,3},{8,12},{12,8},{9,1... | collective-permute-start | bytes 811016 | tf_op jit(solution)/shard_map/ppermute | solution.py:391
  25.2 1.5 %collective-permute-start.9 = (bf16[32,4224]{1,0:T(8,128)(2,1)S(1)}, bf16[32,4224]{1,0:T(8,128)(2,1)S(1)}, u32[]{:S(2)}, u32[]{:S(2)}) collective-permute-start(bf16[32,4224]{1,0:T(8,128)(2,1)S(1)} %pad_maximum_fusion.1.refs_1_), channel_id=1, source_target_pairs={{0,4},{4,0},{1,5},{5,1},{2,6},{6,2},{3,7},{7,3},{8,12},{12,8},{9,1... | collective-permute-start | bytes 811016 | tf_op jit(solution)/shard_map/ppermute | solution.py:391
  26.7 10.5 %collective-permute-start.13 = (bf16[128,1024]{1,0:T(8,128)(2,1)S(1)}, bf16[128,1024]{1,0:T(8,128)(2,1)S(1)}, u32[]{:S(2)}, u32[]{:S(2)}) collective-permute-start(bf16[128,1024]{1,0:T(8,128)(2,1)S(1)} %bitcast.11), channel_id=1, source_target_pairs={{0,8},{8,0},{1,9},{9,1},{2,10},{10,2},{3,11},{11,3},{4,12},{12,4},... | collective-permute-start | bytes 786440 | tf_op jit(solution)/shard_map/ppermute | solution.py:388
  28.5 8.7 %collective-permute-start.10 = (bf16[128,256]{1,0:T(8,128)(2,1)S(1)}, bf16[128,256]{1,0:T(8,128)(2,1)S(1)}, u32[]{:S(2)}, u32[]{:S(2)}) collective-permute-start(bf16[128,256]{1,0:T(8,128)(2,1)S(1)} %get-tuple-element.69), channel_id=1, source_target_pairs={{0,3},{1,2},{2,1},{3,0},{4,7},{5,6},{6,5},{7,4},{8,11},{9,10},{10,... | collective-permute-start | bytes 196616 | tf_op jit(solution)/shard_map/ppermute | solution.py:385
  29.1 8.1 %collective-permute-start.11 = (bf16[128,256]{1,0:T(8,128)(2,1)S(1)}, bf16[128,256]{1,0:T(8,128)(2,1)S(1)}, u32[]{:S(2)}, u32[]{:S(2)}) collective-permute-start(bf16[128,256]{1,0:T(8,128)(2,1)S(1)} %get-tuple-element.70), channel_id=1, source_target_pairs={{0,2},{1,3},{2,0},{3,1},{4,6},{5,7},{6,4},{7,5},{8,10},{9,11},{10,... | collective-permute-start | bytes 196616 | tf_op jit(solution)/shard_map/ppermute | solution.py:385
  29.1 8.7 %slice-start = ((s8[6291456]{0:T(1024)(128)(4,1)}), s8[4194304]{0:T(1024)(128)(4,1)S(1)}, s32[]{:S(2)}) async-start(s8[6291456]{0:T(1024)(128)(4,1)} %bitcast.8), calls=%async_computation | async-start | bytes 8388608
  29.1 8.7 %slice-start.1 = ((s8[6291456]{0:T(1024)(128)(4,1)}), s8[2097152]{0:T(1024)(128)(4,1)S(1)}, s32[]{:S(2)}) async-start(s8[6291456]{0:T(1024)(128)(4,1)} %bitcast.8), calls=%async_computation.1 | async-start | bytes 4194304
  29.1 8.1 %collective-permute-start.12 = (bf16[128,256]{1,0:T(8,128)(2,1)S(1)}, bf16[128,256]{1,0:T(8,128)(2,1)S(1)}, u32[]{:S(2)}, u32[]{:S(2)}) collective-permute-start(bf16[128,256]{1,0:T(8,128)(2,1)S(1)} %get-tuple-element.71), channel_id=1, source_target_pairs={{0,1},{1,0},{2,3},{3,2},{4,5},{5,4},{6,7},{7,6},{8,9},{9,8},{10,11... | collective-permute-start | bytes 196616 | tf_op jit(solution)/shard_map/ppermute | solution.py:385
  37.8 1.2 %collective-permute-start.14 = (bf16[64,128]{1,0:T(8,128)(2,1)S(1)}, bf16[64,128]{1,0:T(8,128)(2,1)S(1)}, u32[]{:S(2)}, u32[]{:S(2)}) collective-permute-start(bf16[64,128]{1,0:T(8,128)(2,1)S(1)} %get-tuple-element.81), channel_id=1, source_target_pairs={{0,4},{4,0},{1,5},{5,1},{2,6},{6,2},{3,7},{7,3},{8,12},{12,8},{9,1... | collective-permute-start | bytes 49160 | tf_op jit(solution)/shard_map/ppermute | solution.py:391
  39.0 4.7 %collective-permute-start.15 = (bf16[64,4096]{1,0:T(8,128)(2,1)S(1)}, bf16[64,4096]{1,0:T(8,128)(2,1)S(1)}, u32[]{:S(2)}, u32[]{:S(2)}) collective-permute-start(bf16[64,4096]{1,0:T(8,128)(2,1)S(1)} %get-tuple-element.82), channel_id=1, source_target_pairs={{0,4},{4,0},{1,5},{5,1},{2,6},{6,2},{3,7},{7,3},{8,12},{12,8},{9,1... | collective-permute-start | bytes 1572872 | tf_op jit(solution)/shard_map/ppermute | solution.py:391
  39.5 10.8 %collective-permute-start.17 = (bf16[128,1024]{1,0:T(8,128)(2,1)S(1)}, bf16[128,1024]{1,0:T(8,128)(2,1)S(1)}, u32[]{:S(2)}, u32[]{:S(2)}) collective-permute-start(bf16[128,1024]{1,0:T(8,128)(2,1)S(1)} %bitcast.12), channel_id=1, source_target_pairs={{0,4},{4,0},{1,5},{5,1},{2,6},{6,2},{3,7},{7,3},{8,12},{12,8},{9,1... | collective-permute-start | bytes 786440 | tf_op jit(solution)/shard_map/ppermute | solution.py:391
  39.6 15.0 %collective-permute-start.18 = (bf16[128,1024]{1,0:T(8,128)(2,1)S(1)}, bf16[128,1024]{1,0:T(8,128)(2,1)S(1)}, u32[]{:S(2)}, u32[]{:S(2)}) collective-permute-start(bf16[128,1024]{1,0:T(8,128)(2,1)S(1)} %collective-permute-done.13.refs_2_), channel_id=1, source_target_pairs={{0,4},{4,0},{1,5},{5,1},{2,6},{6,2},{3,7},{7,3},{8,12},{12,8},{9,1... | collective-permute-start | bytes 786440 | tf_op jit(solution)/shard_map/ppermute | solution.py:391
  40.0 3.7 %collective-permute-start.16 = (bf16[32,256]{1,0:T(8,128)(2,1)S(1)}, bf16[32,256]{1,0:T(8,128)(2,1)S(1)}, u32[]{:S(2)}, u32[]{:S(2)}) collective-permute-start(bf16[32,256]{1,0:T(8,128)(2,1)S(1)} %get-tuple-element.84), channel_id=1, source_target_pairs={{0,8},{8,0},{1,9},{9,1},{2,10},{10,2},{3,11},{11,3},{4,12},{12,4},... | collective-permute-start | bytes 49160 | tf_op jit(solution)/shard_map/ppermute | solution.py:388
  43.8 10.7 %collective-permute-start.22 = (bf16[24,4096]{1,0:T(8,128)(2,1)S(1)}, bf16[24,4096]{1,0:T(8,128)(2,1)S(1)}, u32[]{:S(2)}, u32[]{:S(2)}) collective-permute-start(bf16[24,4096]{1,0:T(8,128)(2,1)S(1)} %get-tuple-element.92), channel_id=1, source_target_pairs={{0,8},{8,0},{1,9},{9,1},{2,10},{10,2},{3,11},{11,3},{4,12},{12,4},... | collective-permute-start | bytes 589832 | tf_op jit(solution)/shard_map/ppermute | solution.py:388
  44.4 5.9 %collective-permute-start.19 = (bf16[32,512]{1,0:T(8,128)(2,1)S(1)}, bf16[32,512]{1,0:T(8,128)(2,1)S(1)}, u32[]{:S(2)}, u32[]{:S(2)}) collective-permute-start(bf16[32,512]{1,0:T(8,128)(2,1)S(1)} %get-tuple-element.88), channel_id=1, source_target_pairs={{0,3},{1,2},{2,1},{3,0},{4,7},{5,6},{6,5},{7,4},{8,11},{9,10},{10,... | collective-permute-start | bytes 98312 | tf_op jit(solution)/shard_map/ppermute | solution.py:385
  45.3 6.5 %collective-permute-start.20 = (bf16[32,512]{1,0:T(8,128)(2,1)S(1)}, bf16[32,512]{1,0:T(8,128)(2,1)S(1)}, u32[]{:S(2)}, u32[]{:S(2)}) collective-permute-start(bf16[32,512]{1,0:T(8,128)(2,1)S(1)} %get-tuple-element.89), channel_id=1, source_target_pairs={{0,2},{1,3},{2,0},{3,1},{4,6},{5,7},{6,4},{7,5},{8,10},{9,11},{10,... | collective-permute-start | bytes 98312 | tf_op jit(solution)/shard_map/ppermute | solution.py:385
  50.3 4.3 %collective-permute-start.21 = (bf16[32,512]{1,0:T(8,128)(2,1)S(1)}, bf16[32,512]{1,0:T(8,128)(2,1)S(1)}, u32[]{:S(2)}, u32[]{:S(2)}) collective-permute-start(bf16[32,512]{1,0:T(8,128)(2,1)S(1)} %get-tuple-element.90), channel_id=1, source_target_pairs={{0,1},{1,0},{2,3},{3,2},{4,5},{5,4},{6,7},{7,6},{8,9},{9,8},{10,11... | collective-permute-start | bytes 98312 | tf_op jit(solution)/shard_map/ppermute | solution.py:385
  50.3 9.0 %collective-permute-start.26 = (bf16[8,4096]{1,0:T(8,128)(2,1)S(1)}, bf16[8,4096]{1,0:T(8,128)(2,1)S(1)}, u32[]{:S(2)}, u32[]{:S(2)}) collective-permute-start(bf16[8,4096]{1,0:T(8,128)(2,1)S(1)} %get-tuple-element.97), channel_id=1, source_target_pairs={{0,8},{8,0},{1,9},{9,1},{2,10},{10,2},{3,11},{11,3},{4,12},{12,4},... | collective-permute-start | bytes 196616 | tf_op jit(solution)/shard_map/ppermute | solution.py:388
  54.8 4.5 %collective-permute-start.25 = (bf16[8,4096]{1,0:T(8,128)(2,1)S(1)}, bf16[8,4096]{1,0:T(8,128)(2,1)S(1)}, u32[]{:S(2)}, u32[]{:S(2)}) collective-permute-start(bf16[8,4096]{1,0:T(8,128)(2,1)S(1)} %get-tuple-element.95), channel_id=1, source_target_pairs={{0,1},{1,0},{2,3},{3,2},{4,5},{5,4},{6,7},{7,6},{8,9},{9,8},{10,11... | collective-permute-start | bytes 196616 | tf_op jit(solution)/shard_map/ppermute | solution.py:385
  54.9 5.2 %collective-permute-start.24 = (bf16[8,4096]{1,0:T(8,128)(2,1)S(1)}, bf16[8,4096]{1,0:T(8,128)(2,1)S(1)}, u32[]{:S(2)}, u32[]{:S(2)}) collective-permute-start(bf16[8,4096]{1,0:T(8,128)(2,1)S(1)} %get-tuple-element.94), channel_id=1, source_target_pairs={{0,2},{1,3},{2,0},{3,1},{4,6},{5,7},{6,4},{7,5},{8,10},{9,11},{10,... | collective-permute-start | bytes 196616 | tf_op jit(solution)/shard_map/ppermute | solution.py:385
  56.1 6.1 %collective-permute-start.23 = (bf16[8,4096]{1,0:T(8,128)(2,1)S(1)}, bf16[8,4096]{1,0:T(8,128)(2,1)S(1)}, u32[]{:S(2)}, u32[]{:S(2)}) collective-permute-start(bf16[8,4096]{1,0:T(8,128)(2,1)S(1)} %get-tuple-element.93), channel_id=1, source_target_pairs={{0,3},{1,2},{2,1},{3,0},{4,7},{5,6},{6,5},{7,4},{8,11},{9,10},{10,... | collective-permute-start | bytes 196616 | tf_op jit(solution)/shard_map/ppermute | solution.py:385

commit v12 on v10

--- a/solution.py
+++ b/solution.py
@@ -12,6 +12,7 @@
 SMALL_LIMIT = 4 * 1024 * 1024
 VMEM_LIMIT = 12 * 1024 * 1024
 PIECES = 8
+LONG = pl.CostEstimate(flops=100_000_000_000, bytes_accessed=12_000_000, transcendentals=0)
 BRIEF = pl.CostEstimate(flops=1, bytes_accessed=1, transcendentals=0)
 
 
@@ -68,19 +69,40 @@
     )(*in_hbm(tokens, routes, probs))
 
 
+def piece_copies(source, target, sems):
+    step = source.shape[0] // PIECES
+    spans = [pl.ds(i * step, step) for i in range(PIECES)]
+    return [
+        pltpu.make_async_copy(source.at[span], target.at[span], sems.at[i])
+        for i, span in enumerate(spans)
+    ]
+
+
+def load_kernel(source, target, sems):
+    copies = piece_copies(source, target, sems)
+    for copy in copies:
+        copy.start()
+    for copy in copies:
+        copy.wait()
+
+
+def load(weights):
+    return pl.pallas_call(
+        load_kernel,
+        in_specs=[pl.BlockSpec(memory_space=pltpu.HBM)],
+        out_specs=pl.BlockSpec(memory_space=pltpu.VMEM),
+        out_shape=pltpu.VMEM(weights.shape, weights.dtype),
+        scratch_shapes=[pltpu.SemaphoreType.DMA((PIECES,))],
+        compiler_params=pltpu.CompilerParams(vmem_limit_bytes=SMALL_LIMIT),
+        cost_estimate=BRIEF,
+        name="load",
+    )(*in_hbm(weights))
+
+
 def prepare_kernel(parts, *refs):
-    ins, lefts, weights = refs[:3], refs[3:5], refs[5:7]
-    loaded, left_ref, outs, sems = refs[7:9], refs[9], refs[10:-1], refs[-1]
-    step = weights[0].shape[0] // PIECES
-    copies = []
-    for n in range(2):
-        for i in range(PIECES):
-            span = pl.ds(i * step, step)
-            copies.append(
-                pltpu.make_async_copy(
-                    weights[n].at[span], loaded[n].at[span], sems.at[n * PIECES + i]
-                )
-            )
+    ins, lefts, source = refs[:3], refs[3:5], refs[5]
+    target, left_ref, outs, sems = refs[6], refs[7], refs[8:-1], refs[-1]
+    copies = piece_copies(source, target, sems)
     for copy in copies:
         copy.start()
     half = left_ref.shape[0] // 2
@@ -93,10 +115,10 @@
         value = ref[...].reshape(exp_dev * piece, hid).astype(F32)
         blocks = [value[:, j * cols : (j + 1) * cols] for j in range(parts)]
         for k in range(parts):
-            target = lax.rem(me + k, parts)
+            device = lax.rem(me + k, parts)
             block = blocks[0]
             for j in range(1, parts):
-                block = jnp.where(target == j, blocks[j], block)
+                block = jnp.where(device == j, blocks[j], block)
             outs[k][n] = block.astype(BF)
     for copy in copies:
         copy.wait()
@@ -108,16 +130,16 @@
     vmem = pl.BlockSpec(memory_space=pltpu.VMEM)
     return pl.pallas_call(
         functools.partial(prepare_kernel, parts),
-        in_specs=[vmem] * 5 + [pl.BlockSpec(memory_space=pltpu.HBM)] * 2,
-        out_specs=[vmem] * (3 + parts),
-        out_shape=[pltpu.VMEM(w.shape, w.dtype) for w in weights]
+        in_specs=[vmem] * 5 + [pl.BlockSpec(memory_space=pltpu.HBM)],
+        out_specs=[vmem] * (2 + parts),
+        out_shape=[pltpu.VMEM(weights.shape, weights.dtype)]
         + [jax.ShapeDtypeStruct((2 * exp_dev * rank, block), BF)]
         + [jax.ShapeDtypeStruct((3, exp_dev * piece, hid // parts), BF)] * parts,
-        scratch_shapes=[pltpu.SemaphoreType.DMA((2 * PIECES,))],
+        scratch_shapes=[pltpu.SemaphoreType.DMA((PIECES,))],
         compiler_params=pltpu.CompilerParams(vmem_limit_bytes=SMALL_LIMIT),
         cost_estimate=BRIEF,
         name="prepare",
-    )(*in_hbm(*factors, *lefts, *weights))
+    )(*in_hbm(*factors, *lefts, weights))
 
 
 def spread_kernel(parts, exp_dev, *refs):
@@ -294,7 +316,7 @@
         out_shape=[jax.ShapeDtypeStruct((span, block), F32)]
         + [jax.ShapeDtypeStruct((span, block), BF)] * (chips - 1),
         compiler_params=pltpu.CompilerParams(vmem_limit_bytes=VMEM_LIMIT),
-        cost_estimate=BRIEF,
+        cost_estimate=LONG,
         name="extra",
     )(near, far, *bottom)
 
@@ -394,11 +416,12 @@
     sent = attach(tokens, routes, probs, pair)
     arrived = [along_z(sent, k) for k in range(1, parts)]
     first = [along_y(sent, s) for s in range(1, chips)]
-    weights = [jnp.swapaxes(w, 1, 2).reshape(hid, width) for w in (w_gate, w_up)]
-    gate_w, up_w, left, *small = prepare(
-        (gate_right, up_right, down_left), (gate_left, up_left), weights, parts
+    gate_w, up_w = (jnp.swapaxes(w, 1, 2).reshape(hid, width) for w in (w_gate, w_up))
+    gate_w, left, *small = prepare(
+        (gate_right, up_right, down_left), (gate_left, up_left), gate_w, parts
     )
-    rest = after(jnp.concatenate(arrived), (left, small, gate_w, up_w))
+    rest = after(jnp.concatenate(arrived), (left, small, gate_w))
+    up_w = load(after(up_w, rest))
     lines = [jnp.concatenate([sent, rest])]
     partner = [other_core(lines[0])]
     small = after(tuple(small), rest)
@@ -407,7 +430,7 @@
     partner_right = other_core(right)
     for s in range(1, chips):
         line = jnp.concatenate([first[s - 1], along_y(rest, s)])
-        line = after(line, (tuple(small), partner_right))
+        line = after(line, (tuple(small), partner_right, up_w))
         lines.append(line)
         partner.append(other_core(line))
     lines += partner
@@ -431,7 +454,7 @@
     low, *lows = extra_products(right, partner_right, bottom, chips)
     lows = [along_y(lows[s - 1], -s) for s in range(1, chips)]
 
-    heads = [along_y(after(others[2 * s - 2], backs[s - 1]), -s) for s in range(1, chips)]
+    heads = [along_y(after(others[2 * s - 2], low), -s) for s in range(1, chips)]
     result, *pieces = merge(out, low, backs, lows, rows)
     for piece in heads:
         result += piece.astype(F32)

time: 60.6 us -> 57.1 us (0.942)
  waiting for transfers between devices: 16.2 us -> 10.1 us
  starting transfers between devices: 29.6 us -> 31.1 us
  Pallas kernels: 13.8 us -> 14.7 us
    ppermute x15, waiting for transfers between devices: 9.2 us -> 4.55 us  [along_z(): lax.ppermute(value, 'mp', [(i, (i + step) % parts) for i in range(parts)])]
    pallas_call x0 -> x1, Pallas kernels: none -> 2.9 us  [load(): pl.pallas_call(load_kernel, in_specs=[pl.BlockSpec(memory_space=pltpu.HBM...]
    pallas_call x1, Pallas kernels: 6 us -> 4.06 us  [prepare(): pl.pallas_call(functools.partial(prepare_kernel, parts), in_specs=[vmem]...]
    ppermute x5, starting transfers between devices: 4.77 us -> 6 us  [along_y(): lax.ppermute(value, 'y', [(i, (i + step) % chips) for i in range(chips)])]
    ppermute x5, waiting for transfers between devices: 4.2 us -> 3.49 us  [along_y(): lax.ppermute(value, 'y', [(i, (i + step) % chips) for i in range(chips)])]
    ppermute x5, waiting for transfers between devices: 2.77 us -> 2.07 us  [other_core(): return lax.ppermute(value, 'core', [(0, 1), (1, 0)])]
  transfers between devices with their start and end apart: 25 -> 25, of which waited for: 16 -> 9; matrix products, arithmetic and copies ran while one was open for 0% -> 0% of each run, Pallas kernels for 20% -> 23%
where the time goes in v12:
time: 57.1 us; the launch traced here: 56.9 us
  starting transfers between devices  31.1 us (54%)
  Pallas kernels  14.7 us (26%)
  waiting for transfers between devices  10.1 us (18%)
  other arithmetic  0.73 us (1%)
    ppermute x15, starting transfers between devices, along_z(): lax.ppermute(value, 'mp', [(i, (i + step) % parts) for i in range(parts)])  23.9 us
    ppermute x5, starting transfers between devices, along_y(): lax.ppermute(value, 'y', [(i, (i + step) % chips) for i in range(chips)])  6 us
    ppermute x15, waiting for transfers between devices, along_z(): lax.ppermute(value, 'mp', [(i, (i + step) % parts) for i in range(parts)])  4.55 us
    pallas_call x1, Pallas kernels, raw_products(): pl.pallas_call(functools.partial(raw_kernel, len(lines), tile), out_shape...  4.17 us
    pallas_call x1, Pallas kernels, prepare(): pl.pallas_call(functools.partial(prepare_kernel, parts), in_specs=[vmem]...  4.06 us
    ppermute x5, waiting for transfers between devices, along_y(): lax.ppermute(value, 'y', [(i, (i + step) % chips) for i in range(chips)])  3.49 us
    pallas_call x1, Pallas kernels, load(): pl.pallas_call(load_kernel, in_specs=[pl.BlockSpec(memory_space=pltpu.HBM...  2.9 us
    ppermute x5, waiting for transfers between devices, other_core(): return lax.ppermute(value, 'core', [(0, 1), (1, 0)])  2.07 us
  transfers between devices with their start and end apart: 25, of which 9 were waited for; matrix products, arithmetic and copies ran while one was open for 0% of the time, Pallas kernels for 23%

profile of v12, /device:TPU:0, one launch (start us, length us, event | category | flops | bytes accessed | tf_op | source)
XLA Modules:
  0.0 56.9 jit_solution(13551644201883043542)
XLA Ops:
  0.0 0.9 %attach.1 = bf16[8,4224]{1,0:T(8,128)(2,1)S(1)} custom-call(bf16[8,4096]{1,0:T(8,128)(2,1)} %tokens_ref.1, s32[8,8]{1,0:T(8,128)} %routes_ref.1, f32[8,8]{1,0:T(8,128)} %probs_ref.1), custom_call_target="tpu_custom_call" | custom-call | flops 1 | bytes 1 | tf_op jit(solution)/shard_map/attach/pallas_call | solution.py:63
  1.0 5.1 %collective-permute-start.2 = (bf16[8,4224]{1,0:T(8,128)(2,1)S(1)}, bf16[8,4224]{1,0:T(8,128)(2,1)S(1)}, u32[]{:S(2)}, u32[]{:S(2)}) collective-permute-start(bf16[8,4224]{1,0:T(8,128)(2,1)S(1)} %attach.1), channel_id=1, source_target_pairs={{0,3},{1,0},{2,1},{3,2},{4,7},{5,4},{6,5},{7,6},{8,11},{9,8},{10,9... | collective-permute-start | bytes 202760 | tf_op jit(solution)/shard_map/ppermute | solution.py:407
  6.1 1.0 %collective-permute-start = (bf16[8,4224]{1,0:T(8,128)(2,1)S(1)}, bf16[8,4224]{1,0:T(8,128)(2,1)S(1)}, u32[]{:S(2)}, u32[]{:S(2)}) collective-permute-start(bf16[8,4224]{1,0:T(8,128)(2,1)S(1)} %attach.1), channel_id=1, source_target_pairs={{0,1},{1,2},{2,3},{3,0},{4,5},{5,6},{6,7},{7,4},{8,9},{9,10},{10,1... | collective-permute-start | bytes 202760 | tf_op jit(solution)/shard_map/ppermute | solution.py:407
  7.1 1.5 %collective-permute-start.3 = (bf16[8,4224]{1,0:T(8,128)(2,1)S(1)}, bf16[8,4224]{1,0:T(8,128)(2,1)S(1)}, u32[]{:S(2)}, u32[]{:S(2)}) collective-permute-start(bf16[8,4224]{1,0:T(8,128)(2,1)S(1)} %attach.1), channel_id=1, source_target_pairs={{0,8},{8,0},{1,9},{9,1},{2,10},{10,2},{3,11},{11,3},{4,12},{12,4},... | collective-permute-start | bytes 202760 | tf_op jit(solution)/shard_map/ppermute | solution.py:410
  8.6 4.1 %prepare.1 = (bf16[768,4096]{1,0:T(8,128)(2,1)S(1)}, bf16[256,1024]{1,0:T(8,128)(2,1)S(1)}, bf16[3,32,192]{2,1,0:T(8,128)(2,1)S(1)}, bf16[3,32,192]{2,1,0:T(8,12...) custom-call(bf16[4,8,768]{2,1,0:T(8,128)(2,1)} %refs_0_.1, bf16[4,8,768]{2,1,0:T(8,128)(2,1)} %refs_1_.1, ...), custom_call_target="tpu_custom_call" | custom-call | flops 1 | bytes 1 | tf_op jit(solution)/shard_map/prepare/pallas_call | solution.py:131
  12.7 1.6 %collective-permute-start.4 = (bf16[24,4224]{1,0:T(8,128)(2,1)S(1)}, bf16[24,4224]{1,0:T(8,128)(2,1)S(1)}, u32[]{:S(2)}, u32[]{:S(2)}) collective-permute-start(bf16[24,4224]{1,0:T(8,128)(2,1)S(1)} %pad_maximum_fusion.2), channel_id=1, source_target_pairs={{0,8},{8,0},{1,9},{9,1},{2,10},{10,2},{3,11},{11,3},{4,12},{12,4},... | collective-permute-start | bytes 608264 | tf_op jit(solution)/shard_map/ppermute | solution.py:410
  14.3 1.5 %collective-permute-start.5 = (bf16[3,32,192]{2,1,0:T(8,128)(2,1)S(1)}, bf16[3,32,192]{2,1,0:T(8,128)(2,1)S(1)}, u32[]{:S(2)}, u32[]{:S(2)}) collective-permute-start(bf16[3,32,192]{2,1,0:T(8,128)(2,1)S(1)} %get-tuple-element.57), channel_id=1, source_target_pairs={{0,1},{1,2},{2,3},{3,0},{4,5},{5,6},{6,7},{7,4},{8,9},{9,10},{10,1... | collective-permute-start | bytes 110600 | tf_op jit(solution)/shard_map/ppermute | solution.py:407
  15.8 1.0 %collective-permute-start.6 = (bf16[3,32,192]{2,1,0:T(8,128)(2,1)S(1)}, bf16[3,32,192]{2,1,0:T(8,128)(2,1)S(1)}, u32[]{:S(2)}, u32[]{:S(2)}) collective-permute-start(bf16[3,32,192]{2,1,0:T(8,128)(2,1)S(1)} %get-tuple-element.58), channel_id=1, source_target_pairs={{0,2},{1,3},{2,0},{3,1},{4,6},{5,7},{6,4},{7,5},{8,10},{9,11},{10,... | collective-permute-start | bytes 110600 | tf_op jit(solution)/shard_map/ppermute | solution.py:407
  16.8 2.3 %collective-permute-start.7 = (bf16[3,32,192]{2,1,0:T(8,128)(2,1)S(1)}, bf16[3,32,192]{2,1,0:T(8,128)(2,1)S(1)}, u32[]{:S(2)}, u32[]{:S(2)}) collective-permute-start(bf16[3,32,192]{2,1,0:T(8,128)(2,1)S(1)} %get-tuple-element.59), channel_id=1, source_target_pairs={{0,3},{1,0},{2,1},{3,2},{4,7},{5,4},{6,5},{7,6},{8,11},{9,8},{10,9... | collective-permute-start | bytes 110600 | tf_op jit(solution)/shard_map/ppermute | solution.py:407
  19.1 2.9 %load.1.refs_5_ = bf16[768,4096]{1,0:T(8,128)(2,1)S(1)} custom-call(bf16[768,4096]{1,0:T(8,128)(2,1)} %bitcast.13), custom_call_target="tpu_custom_call" | custom-call | flops 1 | bytes 1 | tf_op jit(solution)/shard_map/load/pallas_call | solution.py:90
  22.1 0.5 collective-permute-start.9
  22.6 1.0 %collective-permute-done.8.far_ref = bf16[128,1024]{1,0:T(8,128)(2,1)S(1)} collective-permute-done((bf16[128,1024]{1,0:T(8,128)(2,1)S(1)}, bf16[128,1024]{1,0:T(8,128)(2,1)S(1)}, u32[]{:S(2)}, u32[]{:S(2)}) %collective-permute-start.8) | collective-permute-done | bytes 262176 | tf_op jit(solution)/shard_map/ppermute | solution.py:413
  24.1 1.0 %collective-permute-done.10.refs_3_ = bf16[32,4224]{1,0:T(8,128)(2,1)S(1)} collective-permute-done((bf16[32,4224]{1,0:T(8,128)(2,1)S(1)}, bf16[32,4224]{1,0:T(8,128)(2,1)S(1)}, u32[]{:S(2)}, u32[]{:S(2)}) %collective-permute-start.10) | collective-permute-done | bytes 270368 | tf_op jit(solution)/shard_map/ppermute | solution.py:413
  25.5 1.9 %collective-permute-start.12 = (bf16[128,256]{1,0:T(8,128)(2,1)S(1)}, bf16[128,256]{1,0:T(8,128)(2,1)S(1)}, u32[]{:S(2)}, u32[]{:S(2)}) collective-permute-start(bf16[128,256]{1,0:T(8,128)(2,1)S(1)} %get-tuple-element.69), channel_id=1, source_target_pairs={{0,2},{1,3},{2,0},{3,1},{4,6},{5,7},{6,4},{7,5},{8,10},{9,11},{10,... | collective-permute-start | bytes 196616 | tf_op jit(solution)/shard_map/ppermute | solution.py:407
  27.4 2.2 %collective-permute-start.13 = (bf16[128,256]{1,0:T(8,128)(2,1)S(1)}, bf16[128,256]{1,0:T(8,128)(2,1)S(1)}, u32[]{:S(2)}, u32[]{:S(2)}) collective-permute-start(bf16[128,256]{1,0:T(8,128)(2,1)S(1)} %get-tuple-element.70), channel_id=1, source_target_pairs={{0,3},{1,0},{2,1},{3,2},{4,7},{5,4},{6,5},{7,6},{8,11},{9,8},{10,9... | collective-permute-start | bytes 196616 | tf_op jit(solution)/shard_map/ppermute | solution.py:407
  29.6 4.2 %raw.1 = (f32[128,768]{1,0:T(8,128)S(1)}, f32[128,768]{1,0:T(8,128)S(1)}) custom-call(bf16[32,4224]{1,0:T(8,128)(2,1)S(1)} %pad_maximum_fusion.refs_0_, bf16[32,4224]{1,0:T(8,128)(2,1)S(1)} %pad_maximum_fusion.1.refs_1_, bf16[32,4224]{1,0:T(8,128)(2,1)S(1)} %collective-permute-done.9.refs_2_, bf16[32,4224]{1,0:T(8,128)(2,1)S(1)} %collective-permute-done.10.refs_3_, ...), custom_call_target="tpu_custom_call" | custom-call | flops 1 | bytes 1 | tf_op jit(solution)/shard_map/raw/pallas_call | solution.py:213
  34.1 0.5 hidden.1
  34.8 1.1 %down.1 = (f32[64,4096]{1,0:T(8,128)S(1)}, bf16[64,4096]{1,0:T(8,128)(2,1)S(1)}) custom-call(bf16[128,768]{1,0:T(8,128)(2,1)S(1)} %get-tuple-element.73.hidden_ref, bf16[768,4096]{1,0:T(8,128)(2,1)S(1)} %bitcast.10), custom_call_target="tpu_custom_call" | custom-call | flops 1 | bytes 1 | tf_op jit(solution)/shard_map/down/pallas_call | solution.py:272
  35.9 0.5 collective-permute-start.15
  36.4 1.4 %collective-permute-start.16 = (bf16[64,256]{1,0:T(8,128)(2,1)S(1)}, bf16[64,256]{1,0:T(8,128)(2,1)S(1)}, u32[]{:S(2)}, u32[]{:S(2)}) collective-permute-start(bf16[64,256]{1,0:T(8,128)(2,1)S(1)} %get-tuple-element.81), channel_id=1, source_target_pairs={{0,1},{1,2},{2,3},{3,0},{4,5},{5,6},{6,7},{7,4},{8,9},{9,10},{10,1... | collective-permute-start | bytes 98312 | tf_op jit(solution)/shard_map/ppermute | solution.py:407
  37.8 1.2 %collective-permute-start.17 = (bf16[64,256]{1,0:T(8,128)(2,1)S(1)}, bf16[64,256]{1,0:T(8,128)(2,1)S(1)}, u32[]{:S(2)}, u32[]{:S(2)}) collective-permute-start(bf16[64,256]{1,0:T(8,128)(2,1)S(1)} %get-tuple-element.82), channel_id=1, source_target_pairs={{0,2},{1,3},{2,0},{3,1},{4,6},{5,7},{6,4},{7,5},{8,10},{9,11},{10,... | collective-permute-start | bytes 98312 | tf_op jit(solution)/shard_map/ppermute | solution.py:407
  39.1 1.8 %collective-permute-start.18 = (bf16[64,256]{1,0:T(8,128)(2,1)S(1)}, bf16[64,256]{1,0:T(8,128)(2,1)S(1)}, u32[]{:S(2)}, u32[]{:S(2)}) collective-permute-start(bf16[64,256]{1,0:T(8,128)(2,1)S(1)} %get-tuple-element.83), channel_id=1, source_target_pairs={{0,3},{1,0},{2,1},{3,2},{4,7},{5,4},{6,5},{7,6},{8,11},{9,8},{10,9... | collective-permute-start | bytes 98312 | tf_op jit(solution)/shard_map/ppermute | solution.py:407
  40.9 0.8 %collective-permute-start.19 = (bf16[24,4096]{1,0:T(8,128)(2,1)S(1)}, bf16[24,4096]{1,0:T(8,128)(2,1)S(1)}, u32[]{:S(2)}, u32[]{:S(2)}) collective-permute-start(bf16[24,4096]{1,0:T(8,128)(2,1)S(1)} %get-tuple-element.85), channel_id=1, source_target_pairs={{0,8},{8,0},{1,9},{9,1},{2,10},{10,2},{3,11},{11,3},{4,12},{12,4},... | collective-permute-start | bytes 589832 | tf_op jit(solution)/shard_map/ppermute | solution.py:410
  42.2 1.1 %collective-permute-done.17.refs_2_ = bf16[64,256]{1,0:T(8,128)(2,1)S(1)} collective-permute-done((bf16[64,256]{1,0:T(8,128)(2,1)S(1)}, bf16[64,256]{1,0:T(8,128)(2,1)S(1)}, u32[]{:S(2)}, u32[]{:S(2)}) %collective-permute-start.17) | collective-permute-done | bytes 32800 | tf_op jit(solution)/shard_map/ppermute | solution.py:407
  43.5 1.0 %collective-permute-start.20 = (bf16[32,1024]{1,0:T(8,128)(2,1)S(1)}, bf16[32,1024]{1,0:T(8,128)(2,1)S(1)}, u32[]{:S(2)}, u32[]{:S(2)}) collective-permute-start(bf16[32,1024]{1,0:T(8,128)(2,1)S(1)} %get-tuple-element.86), channel_id=1, source_target_pairs={{0,8},{8,0},{1,9},{9,1},{2,10},{10,2},{3,11},{11,3},{4,12},{12,4},... | collective-permute-start | bytes 196616 | tf_op jit(solution)/shard_map/ppermute | solution.py:410
  44.5 1.1 %collective-permute-start.21 = (bf16[8,4096]{1,0:T(8,128)(2,1)S(1)}, bf16[8,4096]{1,0:T(8,128)(2,1)S(1)}, u32[]{:S(2)}, u32[]{:S(2)}) collective-permute-start(bf16[8,4096]{1,0:T(8,128)(2,1)S(1)} %get-tuple-element.89), channel_id=1, source_target_pairs={{0,8},{8,0},{1,9},{9,1},{2,10},{10,2},{3,11},{11,3},{4,12},{12,4},... | collective-permute-start | bytes 196616 | tf_op jit(solution)/shard_map/ppermute | solution.py:410
  45.6 3.5 %collective-permute-done.20.refs_1_ = bf16[32,1024]{1,0:T(8,128)(2,1)S(1)} collective-permute-done((bf16[32,1024]{1,0:T(8,128)(2,1)S(1)}, bf16[32,1024]{1,0:T(8,128)(2,1)S(1)}, u32[]{:S(2)}, u32[]{:S(2)}) %collective-permute-start.20) | collective-permute-done | bytes 65568 | tf_op jit(solution)/shard_map/ppermute | solution.py:410
  49.5 2.2 %collective-permute-start.23 = (bf16[8,4096]{1,0:T(8,128)(2,1)S(1)}, bf16[8,4096]{1,0:T(8,128)(2,1)S(1)}, u32[]{:S(2)}, u32[]{:S(2)}) collective-permute-start(bf16[8,4096]{1,0:T(8,128)(2,1)S(1)} %get-tuple-element.91), channel_id=1, source_target_pairs={{0,2},{1,3},{2,0},{3,1},{4,6},{5,7},{6,4},{7,5},{8,10},{9,11},{10,... | collective-permute-start | bytes 196616 | tf_op jit(solution)/shard_map/ppermute | solution.py:407
  51.8 1.9 %collective-permute-start.22 = (bf16[8,4096]{1,0:T(8,128)(2,1)S(1)}, bf16[8,4096]{1,0:T(8,128)(2,1)S(1)}, u32[]{:S(2)}, u32[]{:S(2)}) collective-permute-start(bf16[8,4096]{1,0:T(8,128)(2,1)S(1)} %get-tuple-element.90), channel_id=1, source_target_pairs={{0,3},{1,0},{2,1},{3,2},{4,7},{5,4},{6,5},{7,6},{8,11},{9,8},{10,9... | collective-permute-start | bytes 196616 | tf_op jit(solution)/shard_map/ppermute | solution.py:407
  53.7 1.7 %collective-permute-done.24 = bf16[8,4096]{1,0:T(8,128)(2,1)S(1)} collective-permute-done((bf16[8,4096]{1,0:T(8,128)(2,1)S(1)}, bf16[8,4096]{1,0:T(8,128)(2,1)S(1)}, u32[]{:S(2)}, u32[]{:S(2)}) %collective-permute-start.24) | collective-permute-done | bytes 65568 | tf_op jit(solution)/shard_map/ppermute | solution.py:407
  55.4 0.8 %collective-permute-done.23 = bf16[8,4096]{1,0:T(8,128)(2,1)S(1)} collective-permute-done((bf16[8,4096]{1,0:T(8,128)(2,1)S(1)}, bf16[8,4096]{1,0:T(8,128)(2,1)S(1)}, u32[]{:S(2)}, u32[]{:S(2)}) %collective-permute-start.23) | collective-permute-done | bytes 65568 | tf_op jit(solution)/shard_map/ppermute | solution.py:407
  56.2 0.7 %add_convert_fusion = bf16[8,4096]{1,0:T(8,128)(2,1)} fusion(bf16[8,4096]{1,0:T(8,128)(2,1)S(1)} %collective-permute-done.24, bf16[8,4096]{1,0:T(8,128)(2,1)S(1)} %collective-permute-done.23, bf16[8,4096]{1,0:T(8,128)(2,1)S(1)} %collective-permute-done.22, f32[8,4096]{1,0:T(8,128)S(1)} %get-tuple-element.87, bf16[8,4096]{1,0:T(8,128)(2,1)S(1)} %collective-permute-done.21), kind=kLoop, calls=%fused_computation.3 | loop fusion | flops 294912 | bytes 458752 | tf_op jit(solution)/shard_map/convert_element_type | solution.py:463
  (41 shorter events, 2.8 us)
Async XLA Ops:
  1.0 11.7 %collective-permute-start.2 = (bf16[8,4224]{1,0:T(8,128)(2,1)S(1)}, bf16[8,4224]{1,0:T(8,128)(2,1)S(1)}, u32[]{:S(2)}, u32[]{:S(2)}) collective-permute-start(bf16[8,4224]{1,0:T(8,128)(2,1)S(1)} %attach.1), channel_id=1, source_target_pairs={{0,3},{1,0},{2,1},{3,2},{4,7},{5,4},{6,5},{7,6},{8,11},{9,8},{10,9... | collective-permute-start | bytes 202760 | tf_op jit(solution)/shard_map/ppermute | solution.py:407
  6.1 6.6 %collective-permute-start.1 = (bf16[8,4224]{1,0:T(8,128)(2,1)S(1)}, bf16[8,4224]{1,0:T(8,128)(2,1)S(1)}, u32[]{:S(2)}, u32[]{:S(2)}) collective-permute-start(bf16[8,4224]{1,0:T(8,128)(2,1)S(1)} %attach.1), channel_id=1, source_target_pairs={{0,2},{1,3},{2,0},{3,1},{4,6},{5,7},{6,4},{7,5},{8,10},{9,11},{10,... | collective-permute-start | bytes 202760 | tf_op jit(solution)/shard_map/ppermute | solution.py:407
  6.1 6.6 %collective-permute-start = (bf16[8,4224]{1,0:T(8,128)(2,1)S(1)}, bf16[8,4224]{1,0:T(8,128)(2,1)S(1)}, u32[]{:S(2)}, u32[]{:S(2)}) collective-permute-start(bf16[8,4224]{1,0:T(8,128)(2,1)S(1)} %attach.1), channel_id=1, source_target_pairs={{0,1},{1,2},{2,3},{3,0},{4,5},{5,6},{6,7},{7,4},{8,9},{9,10},{10,1... | collective-permute-start | bytes 202760 | tf_op jit(solution)/shard_map/ppermute | solution.py:407
  7.1 14.9 %collective-permute-start.3 = (bf16[8,4224]{1,0:T(8,128)(2,1)S(1)}, bf16[8,4224]{1,0:T(8,128)(2,1)S(1)}, u32[]{:S(2)}, u32[]{:S(2)}) collective-permute-start(bf16[8,4224]{1,0:T(8,128)(2,1)S(1)} %attach.1), channel_id=1, source_target_pairs={{0,8},{8,0},{1,9},{9,1},{2,10},{10,2},{3,11},{11,3},{4,12},{12,4},... | collective-permute-start | bytes 202760 | tf_op jit(solution)/shard_map/ppermute | solution.py:410
  12.7 9.3 %collective-permute-start.4 = (bf16[24,4224]{1,0:T(8,128)(2,1)S(1)}, bf16[24,4224]{1,0:T(8,128)(2,1)S(1)}, u32[]{:S(2)}, u32[]{:S(2)}) collective-permute-start(bf16[24,4224]{1,0:T(8,128)(2,1)S(1)} %pad_maximum_fusion.2), channel_id=1, source_target_pairs={{0,8},{8,0},{1,9},{9,1},{2,10},{10,2},{3,11},{11,3},{4,12},{12,4},... | collective-permute-start | bytes 608264 | tf_op jit(solution)/shard_map/ppermute | solution.py:410
  14.3 8.3 %collective-permute-start.5 = (bf16[3,32,192]{2,1,0:T(8,128)(2,1)S(1)}, bf16[3,32,192]{2,1,0:T(8,128)(2,1)S(1)}, u32[]{:S(2)}, u32[]{:S(2)}) collective-permute-start(bf16[3,32,192]{2,1,0:T(8,128)(2,1)S(1)} %get-tuple-element.57), channel_id=1, source_target_pairs={{0,1},{1,2},{2,3},{3,0},{4,5},{5,6},{6,7},{7,4},{8,9},{9,10},{10,1... | collective-permute-start | bytes 110600 | tf_op jit(solution)/shard_map/ppermute | solution.py:407
  15.8 6.8 %collective-permute-start.6 = (bf16[3,32,192]{2,1,0:T(8,128)(2,1)S(1)}, bf16[3,32,192]{2,1,0:T(8,128)(2,1)S(1)}, u32[]{:S(2)}, u32[]{:S(2)}) collective-permute-start(bf16[3,32,192]{2,1,0:T(8,128)(2,1)S(1)} %get-tuple-element.58), channel_id=1, source_target_pairs={{0,2},{1,3},{2,0},{3,1},{4,6},{5,7},{6,4},{7,5},{8,10},{9,11},{10,... | collective-permute-start | bytes 110600 | tf_op jit(solution)/shard_map/ppermute | solution.py:407
  16.8 5.8 %collective-permute-start.7 = (bf16[3,32,192]{2,1,0:T(8,128)(2,1)S(1)}, bf16[3,32,192]{2,1,0:T(8,128)(2,1)S(1)}, u32[]{:S(2)}, u32[]{:S(2)}) collective-permute-start(bf16[3,32,192]{2,1,0:T(8,128)(2,1)S(1)} %get-tuple-element.59), channel_id=1, source_target_pairs={{0,3},{1,0},{2,1},{3,2},{4,7},{5,4},{6,5},{7,6},{8,11},{9,8},{10,9... | collective-permute-start | bytes 110600 | tf_op jit(solution)/shard_map/ppermute | solution.py:407
  19.1 2.9 %copy-start = (bf16[4,32,1024]{2,1,0:T(8,128)(2,1)S(1)}, bf16[4,32,1024]{2,1,0:T(8,128)(2,1)}, u32[]{:S(2)}) copy-start(bf16[4,32,1024]{2,1,0:T(8,128)(2,1)} %param.23) | copy-start | bytes 786436
  22.0 1.6 %collective-permute-start.8 = (bf16[128,1024]{1,0:T(8,128)(2,1)S(1)}, bf16[128,1024]{1,0:T(8,128)(2,1)S(1)}, u32[]{:S(2)}, u32[]{:S(2)}) collective-permute-start(bf16[128,1024]{1,0:T(8,128)(2,1)S(1)} %bitcast.11), channel_id=1, source_target_pairs={{0,4},{4,0},{1,5},{5,1},{2,6},{6,2},{3,7},{7,3},{8,12},{12,8},{9,1... | collective-permute-start | bytes 786440 | tf_op jit(solution)/shard_map/ppermute | solution.py:413
  22.1 2.0 %collective-permute-start.9 = (bf16[32,4224]{1,0:T(8,128)(2,1)S(1)}, bf16[32,4224]{1,0:T(8,128)(2,1)S(1)}, u32[]{:S(2)}, u32[]{:S(2)}) collective-permute-start(bf16[32,4224]{1,0:T(8,128)(2,1)S(1)} %pad_maximum_fusion.refs_0_), channel_id=1, source_target_pairs={{0,4},{4,0},{1,5},{5,1},{2,6},{6,2},{3,7},{7,3},{8,12},{12,8},{9,1... | collective-permute-start | bytes 811016 | tf_op jit(solution)/shard_map/ppermute | solution.py:413
  23.6 1.5 %collective-permute-start.10 = (bf16[32,4224]{1,0:T(8,128)(2,1)S(1)}, bf16[32,4224]{1,0:T(8,128)(2,1)S(1)}, u32[]{:S(2)}, u32[]{:S(2)}) collective-permute-start(bf16[32,4224]{1,0:T(8,128)(2,1)S(1)} %pad_maximum_fusion.1.refs_1_), channel_id=1, source_target_pairs={{0,4},{4,0},{1,5},{5,1},{2,6},{6,2},{3,7},{7,3},{8,12},{12,8},{9,1... | collective-permute-start | bytes 811016 | tf_op jit(solution)/shard_map/ppermute | solution.py:413
  25.5 8.3 %collective-permute-start.11 = (bf16[128,256]{1,0:T(8,128)(2,1)S(1)}, bf16[128,256]{1,0:T(8,128)(2,1)S(1)}, u32[]{:S(2)}, u32[]{:S(2)}) collective-permute-start(bf16[128,256]{1,0:T(8,128)(2,1)S(1)} %get-tuple-element.68), channel_id=1, source_target_pairs={{0,1},{1,2},{2,3},{3,0},{4,5},{5,6},{6,7},{7,4},{8,9},{9,10},{10,1... | collective-permute-start | bytes 196616 | tf_op jit(solution)/shard_map/ppermute | solution.py:407
  25.5 8.6 %collective-permute-start.12 = (bf16[128,256]{1,0:T(8,128)(2,1)S(1)}, bf16[128,256]{1,0:T(8,128)(2,1)S(1)}, u32[]{:S(2)}, u32[]{:S(2)}) collective-permute-start(bf16[128,256]{1,0:T(8,128)(2,1)S(1)} %get-tuple-element.69), channel_id=1, source_target_pairs={{0,2},{1,3},{2,0},{3,1},{4,6},{5,7},{6,4},{7,5},{8,10},{9,11},{10,... | collective-permute-start | bytes 196616 | tf_op jit(solution)/shard_map/ppermute | solution.py:407
  27.4 7.3 %slice-start = ((s8[6291456]{0:T(1024)(128)(4,1)}), s8[4194304]{0:T(1024)(128)(4,1)S(1)}, s32[]{:S(2)}) async-start(s8[6291456]{0:T(1024)(128)(4,1)} %bitcast.8), calls=%async_computation | async-start | bytes 8388608
  27.4 7.3 %slice-start.1 = ((s8[6291456]{0:T(1024)(128)(4,1)}), s8[2097152]{0:T(1024)(128)(4,1)S(1)}, s32[]{:S(2)}) async-start(s8[6291456]{0:T(1024)(128)(4,1)} %bitcast.8), calls=%async_computation.1 | async-start | bytes 4194304
  27.4 6.7 %collective-permute-start.13 = (bf16[128,256]{1,0:T(8,128)(2,1)S(1)}, bf16[128,256]{1,0:T(8,128)(2,1)S(1)}, u32[]{:S(2)}, u32[]{:S(2)}) collective-permute-start(bf16[128,256]{1,0:T(8,128)(2,1)S(1)} %get-tuple-element.70), channel_id=1, source_target_pairs={{0,3},{1,0},{2,1},{3,2},{4,7},{5,4},{6,5},{7,6},{8,11},{9,8},{10,9... | collective-permute-start | bytes 196616 | tf_op jit(solution)/shard_map/ppermute | solution.py:407
  34.7 1.2 %collective-permute-start.14 = (bf16[64,128]{1,0:T(8,128)(2,1)S(1)}, bf16[64,128]{1,0:T(8,128)(2,1)S(1)}, u32[]{:S(2)}, u32[]{:S(2)}) collective-permute-start(bf16[64,128]{1,0:T(8,128)(2,1)S(1)} %get-tuple-element.76), channel_id=1, source_target_pairs={{0,4},{4,0},{1,5},{5,1},{2,6},{6,2},{3,7},{7,3},{8,12},{12,8},{9,1... | collective-permute-start | bytes 49160 | tf_op jit(solution)/shard_map/ppermute | solution.py:413
  35.9 4.9 %collective-permute-start.15 = (bf16[64,4096]{1,0:T(8,128)(2,1)S(1)}, bf16[64,4096]{1,0:T(8,128)(2,1)S(1)}, u32[]{:S(2)}, u32[]{:S(2)}) collective-permute-start(bf16[64,4096]{1,0:T(8,128)(2,1)S(1)} %get-tuple-element.77), channel_id=1, source_target_pairs={{0,4},{4,0},{1,5},{5,1},{2,6},{6,2},{3,7},{7,3},{8,12},{12,8},{9,1... | collective-permute-start | bytes 1572872 | tf_op jit(solution)/shard_map/ppermute | solution.py:413
  36.4 5.8 %collective-permute-start.16 = (bf16[64,256]{1,0:T(8,128)(2,1)S(1)}, bf16[64,256]{1,0:T(8,128)(2,1)S(1)}, u32[]{:S(2)}, u32[]{:S(2)}) collective-permute-start(bf16[64,256]{1,0:T(8,128)(2,1)S(1)} %get-tuple-element.81), channel_id=1, source_target_pairs={{0,1},{1,2},{2,3},{3,0},{4,5},{5,6},{6,7},{7,4},{8,9},{9,10},{10,1... | collective-permute-start | bytes 98312 | tf_op jit(solution)/shard_map/ppermute | solution.py:407
  37.8 5.5 %collective-permute-start.17 = (bf16[64,256]{1,0:T(8,128)(2,1)S(1)}, bf16[64,256]{1,0:T(8,128)(2,1)S(1)}, u32[]{:S(2)}, u32[]{:S(2)}) collective-permute-start(bf16[64,256]{1,0:T(8,128)(2,1)S(1)} %get-tuple-element.82), channel_id=1, source_target_pairs={{0,2},{1,3},{2,0},{3,1},{4,6},{5,7},{6,4},{7,5},{8,10},{9,11},{10,... | collective-permute-start | bytes 98312 | tf_op jit(solution)/shard_map/ppermute | solution.py:407
  39.1 4.2 %collective-permute-start.18 = (bf16[64,256]{1,0:T(8,128)(2,1)S(1)}, bf16[64,256]{1,0:T(8,128)(2,1)S(1)}, u32[]{:S(2)}, u32[]{:S(2)}) collective-permute-start(bf16[64,256]{1,0:T(8,128)(2,1)S(1)} %get-tuple-element.83), channel_id=1, source_target_pairs={{0,3},{1,0},{2,1},{3,2},{4,7},{5,4},{6,5},{7,6},{8,11},{9,8},{10,9... | collective-permute-start | bytes 98312 | tf_op jit(solution)/shard_map/ppermute | solution.py:407
  40.9 8.2 %collective-permute-start.19 = (bf16[24,4096]{1,0:T(8,128)(2,1)S(1)}, bf16[24,4096]{1,0:T(8,128)(2,1)S(1)}, u32[]{:S(2)}, u32[]{:S(2)}) collective-permute-start(bf16[24,4096]{1,0:T(8,128)(2,1)S(1)} %get-tuple-element.85), channel_id=1, source_target_pairs={{0,8},{8,0},{1,9},{9,1},{2,10},{10,2},{3,11},{11,3},{4,12},{12,4},... | collective-permute-start | bytes 589832 | tf_op jit(solution)/shard_map/ppermute | solution.py:410
  43.5 5.6 %collective-permute-start.20 = (bf16[32,1024]{1,0:T(8,128)(2,1)S(1)}, bf16[32,1024]{1,0:T(8,128)(2,1)S(1)}, u32[]{:S(2)}, u32[]{:S(2)}) collective-permute-start(bf16[32,1024]{1,0:T(8,128)(2,1)S(1)} %get-tuple-element.86), channel_id=1, source_target_pairs={{0,8},{8,0},{1,9},{9,1},{2,10},{10,2},{3,11},{11,3},{4,12},{12,4},... | collective-permute-start | bytes 196616 | tf_op jit(solution)/shard_map/ppermute | solution.py:410
  44.5 9.2 %collective-permute-start.21 = (bf16[8,4096]{1,0:T(8,128)(2,1)S(1)}, bf16[8,4096]{1,0:T(8,128)(2,1)S(1)}, u32[]{:S(2)}, u32[]{:S(2)}) collective-permute-start(bf16[8,4096]{1,0:T(8,128)(2,1)S(1)} %get-tuple-element.89), channel_id=1, source_target_pairs={{0,8},{8,0},{1,9},{9,1},{2,10},{10,2},{3,11},{11,3},{4,12},{12,4},... | collective-permute-start | bytes 196616 | tf_op jit(solution)/shard_map/ppermute | solution.py:410
  49.2 6.2 %collective-permute-start.24 = (bf16[8,4096]{1,0:T(8,128)(2,1)S(1)}, bf16[8,4096]{1,0:T(8,128)(2,1)S(1)}, u32[]{:S(2)}, u32[]{:S(2)}) collective-permute-start(bf16[8,4096]{1,0:T(8,128)(2,1)S(1)} %get-tuple-element.92), channel_id=1, source_target_pairs={{0,1},{1,2},{2,3},{3,0},{4,5},{5,6},{6,7},{7,4},{8,9},{9,10},{10,1... | collective-permute-start | bytes 196616 | tf_op jit(solution)/shard_map/ppermute | solution.py:407
  49.5 6.7 %collective-permute-start.23 = (bf16[8,4096]{1,0:T(8,128)(2,1)S(1)}, bf16[8,4096]{1,0:T(8,128)(2,1)S(1)}, u32[]{:S(2)}, u32[]{:S(2)}) collective-permute-start(bf16[8,4096]{1,0:T(8,128)(2,1)S(1)} %get-tuple-element.91), channel_id=1, source_target_pairs={{0,2},{1,3},{2,0},{3,1},{4,6},{5,7},{6,4},{7,5},{8,10},{9,11},{10,... | collective-permute-start | bytes 196616 | tf_op jit(solution)/shard_map/ppermute | solution.py:407
  51.8 4.5 %collective-permute-start.22 = (bf16[8,4096]{1,0:T(8,128)(2,1)S(1)}, bf16[8,4096]{1,0:T(8,128)(2,1)S(1)}, u32[]{:S(2)}, u32[]{:S(2)}) collective-permute-start(bf16[8,4096]{1,0:T(8,128)(2,1)S(1)} %get-tuple-element.90), channel_id=1, source_target_pairs={{0,3},{1,0},{2,1},{3,2},{4,7},{5,4},{6,5},{7,6},{8,11},{9,8},{10,9... | collective-permute-start | bytes 196616 | tf_op jit(solution)/shard_map/ppermute | solution.py:407

commit v13 on v12

--- a/solution.py
+++ b/solution.py
@@ -12,7 +12,6 @@
 SMALL_LIMIT = 4 * 1024 * 1024
 VMEM_LIMIT = 12 * 1024 * 1024
 PIECES = 8
-LONG = pl.CostEstimate(flops=100_000_000_000, bytes_accessed=12_000_000, transcendentals=0)
 BRIEF = pl.CostEstimate(flops=1, bytes_accessed=1, transcendentals=0)
 
 
@@ -281,44 +280,54 @@
     )(hidden, down_w)
 
 
-def turn_kernel(rows, near_ref, far_ref, *out_refs):
+def pair_kernel(near_ref, far_ref, *out_refs):
     value = jnp.concatenate([near_ref[...].astype(F32), far_ref[...].astype(F32)], axis=1)
-    for k, out_ref in enumerate(out_refs):
-        out_ref[...] = rotated(value, rows, len(out_refs), k).astype(BF)
-
-
-def turn(near, far, parts, rows):
+    span = out_refs[0].shape[0]
+    for n, out_ref in enumerate(out_refs):
+        out_ref[...] = value[n * span : (n + 1) * span].astype(BF)
+
+
+def side_by_side(near, far, chips):
     total, ranks = near.shape
     return pl.pallas_call(
-        functools.partial(turn_kernel, rows),
-        out_shape=[jax.ShapeDtypeStruct((total, 2 * ranks), BF)] * parts,
+        pair_kernel,
+        out_shape=[jax.ShapeDtypeStruct((total // chips, 2 * ranks), BF)] * chips,
+        compiler_params=pltpu.CompilerParams(vmem_limit_bytes=SMALL_LIMIT),
+        cost_estimate=BRIEF,
+        name="pair",
+    )(near, far)
+
+
+def turn_kernel(rows, chips, *refs):
+    ins, outs = refs[:chips], refs[chips:]
+    value = jnp.concatenate([ref[...].astype(F32) for ref in ins], axis=1)
+    for k, out_ref in enumerate(outs):
+        out_ref[...] = rotated(value, rows, len(outs), k).astype(BF)
+
+
+def turn(lines, parts, rows):
+    span, ranks = lines[0].shape
+    return pl.pallas_call(
+        functools.partial(turn_kernel, rows, len(lines)),
+        out_shape=[jax.ShapeDtypeStruct((span, len(lines) * ranks), BF)] * parts,
         compiler_params=pltpu.CompilerParams(vmem_limit_bytes=SMALL_LIMIT),
         cost_estimate=BRIEF,
         name="turn",
-    )(near, far)
-
-
-def extra_kernel(chips, near_ref, far_ref, *refs):
-    bottom, own_ref, outs = refs[: -chips], refs[-chips], refs[len(refs) - chips + 1 :]
-    ranks, span = near_ref.shape[0], own_ref.shape[0]
-    low = sum(ref[...].astype(F32) for ref in bottom).astype(BF)
-    value = dot_nn(low[:, :ranks], near_ref[...]) + dot_nn(low[:, ranks:], far_ref[...])
-    own_ref[...] = value[:span]
-    for n, out_ref in enumerate(outs):
-        out_ref[...] = value[(n + 1) * span : (n + 2) * span].astype(BF)
-
-
-def extra_products(near, far, bottom, chips):
-    span = bottom[0].shape[0] // chips
-    block = near.shape[1]
-    return pl.pallas_call(
-        functools.partial(extra_kernel, chips),
-        out_shape=[jax.ShapeDtypeStruct((span, block), F32)]
-        + [jax.ShapeDtypeStruct((span, block), BF)] * (chips - 1),
-        compiler_params=pltpu.CompilerParams(vmem_limit_bytes=VMEM_LIMIT),
-        cost_estimate=LONG,
-        name="extra",
-    )(near, far, *bottom)
+    )(*lines)
+
+
+def add_up_kernel(*refs):
+    refs[-1][...] = sum(ref[...].astype(F32) for ref in refs[:-1]).astype(BF)
+
+
+def add_up(pieces):
+    return pl.pallas_call(
+        add_up_kernel,
+        out_shape=jax.ShapeDtypeStruct(pieces[0].shape, BF),
+        compiler_params=pltpu.CompilerParams(vmem_limit_bytes=SMALL_LIMIT),
+        cost_estimate=BRIEF,
+        name="add_up",
+    )(*pieces)
 
 
 def fold_kernel(head, near_ref, far_ref, own_ref, *out_refs):
@@ -345,38 +354,41 @@
     )(near, far)
 
 
-def merge_kernel(count, own_ref, low_ref, *refs):
-    backs, lows, outs = refs[:count], refs[count : 2 * count], refs[2 * count :]
+def merge_kernel(chips, parts, *refs):
+    own_ref, rights, refs = refs[0], refs[1 : 1 + 2 * chips], refs[1 + 2 * chips :]
+    low, backs, outs = refs[0][...], refs[1:-parts], refs[-parts:]
     rows = outs[0].shape[0]
-    block = low_ref.shape[1]
+    ranks, block = rights[0].shape
     offset = pl.multiple_of(lax.axis_index("mp") * block, 128)
-    low = low_ref[...]
-    for ref in lows:
-        low += ref[...].astype(F32)
+    value = jnp.zeros((low.shape[0], block), F32)
+    for n, ref in enumerate(rights):
+        at = (2 * n if n < chips else 2 * (n - chips) + 1) * ranks
+        value += dot_nn(low[:, at : at + ranks], ref[...])
     total = own_ref[rows:]
-    part = own_ref[:, pl.ds(offset, block)] + low
-    after_own = part[rows:]
+    value += own_ref[:, pl.ds(offset, block)]
+    rest = value[rows:]
     for ref in backs:
         total += ref[...].astype(F32)
-        after_own += ref[:, pl.ds(offset, block)].astype(F32)
+        rest += ref[:, pl.ds(offset, block)].astype(F32)
     outs[0][...] = own_ref[:rows]
-    outs[0][:, pl.ds(offset, block)] = part[:rows]
-    for k in range(1, len(outs)):
+    outs[0][:, pl.ds(offset, block)] = value[:rows]
+    for k in range(1, parts):
         span = slice((k - 1) * rows, k * rows)
         outs[k][...] = total[span].astype(BF)
-        outs[k][:, pl.ds(offset, block)] = after_own[span].astype(BF)
-
-
-def merge(own, low, backs, lows, rows):
+        outs[k][:, pl.ds(offset, block)] = rest[span].astype(BF)
+
+
+def merge(own, rights, low, backs, rows):
     total, width = own.shape
-    return pl.pallas_call(
-        functools.partial(merge_kernel, len(backs)),
+    parts = total // rows
+    return pl.pallas_call(
+        functools.partial(merge_kernel, len(backs) + 1, parts),
         out_shape=[jax.ShapeDtypeStruct((rows, width), F32)]
-        + [jax.ShapeDtypeStruct((rows, width), BF)] * (total // rows - 1),
+        + [jax.ShapeDtypeStruct((rows, width), BF)] * (parts - 1),
         compiler_params=pltpu.CompilerParams(vmem_limit_bytes=VMEM_LIMIT),
         cost_estimate=BRIEF,
         name="merge",
-    )(own, low, *backs, *lows)
+    )(own, *rights, low, *backs)
 
 
 def local(
@@ -420,17 +432,18 @@
     gate_w, left, *small = prepare(
         (gate_right, up_right, down_left), (gate_left, up_left), gate_w, parts
     )
-    rest = after(jnp.concatenate(arrived), (left, small, gate_w))
+    right = down_right.reshape(ranks, block)
+    partner_right = other_core(right)
+    rest = after(jnp.concatenate(arrived), (left, small, gate_w, partner_right))
     up_w = load(after(up_w, rest))
     lines = [jnp.concatenate([sent, rest])]
     partner = [other_core(lines[0])]
     small = after(tuple(small), rest)
     small = [small[0]] + [along_z(small[k], k) for k in range(1, parts)]
-    right = after(down_right.reshape(ranks, block), rest)
-    partner_right = other_core(right)
     for s in range(1, chips):
         line = jnp.concatenate([first[s - 1], along_y(rest, s)])
-        line = after(line, (tuple(small), partner_right, up_w))
+        arrival = line
+        line = after(line, (tuple(small), up_w))
         lines.append(line)
         partner.append(other_core(line))
     lines += partner
@@ -440,22 +453,26 @@
     inner = inner_products(lines, left, parts, rows)
     inner = [inner[0]] + [along_z(inner[k], k) for k in range(1, parts)]
     raw = raw_products(lines, gate_w, up_w)
+    right = after(right, arrival)
+    rights = [right] + [along_y(right, -s) for s in range(1, chips)]
+    raw = after(tuple(raw), rights[1:])
     hidden, near, far = hidden_units(
         lines, inner, raw, diag, parts, exp_dev, pair
     )
     swapped = other_core(far)
-    bottom = turn(near, swapped, parts, rows)
+    low, *lows = side_by_side(near, swapped, chips)
+    lows = [along_y(lows[s - 1], -s) for s in range(1, chips)]
+    bottom = turn([low] + lows, parts, rows)
     bottom = [bottom[0]] + [along_z(bottom[k], k) for k in range(1, parts)]
 
     near, far = down_products(hidden, w_down.reshape(hid, width))
-    out, *others = fold(near, other_core(after(far, swapped)), chips, rows)
+    far = after(other_core(after(far, swapped)), lows)
+    out, *others = fold(near, far, chips, rows)
     backs = [along_y(others[2 * s - 1], -s) for s in range(1, chips)]
-
-    low, *lows = extra_products(right, partner_right, bottom, chips)
-    lows = [along_y(lows[s - 1], -s) for s in range(1, chips)]
-
-    heads = [along_y(after(others[2 * s - 2], low), -s) for s in range(1, chips)]
-    result, *pieces = merge(out, low, backs, lows, rows)
+    rights += [partner_right] + [other_core(after(right, bottom[0])) for right in rights[1:]]
+    own, *pieces = merge(out, rights, add_up(bottom[1:] + bottom[:1]), backs, rows)
+    heads = [along_y(after(others[2 * s - 2], own), -s) for s in range(1, chips)]
+    result = own
     for piece in heads:
         result += piece.astype(F32)
     for k in range(1, parts):

time: 57.1 us -> 57.5 us (level)
    ppermute x15, waiting for transfers between devices: 4.55 us -> 6.5 us  [along_z(): lax.ppermute(value, 'mp', [(i, (i + step) % parts) for i in range(parts)])]
    ppermute x5 -> x6, waiting for transfers between devices: 2.07 us -> 0.26 us  [other_core(): return lax.ppermute(value, 'core', [(0, 1), (1, 0)])]
    ppermute x5 -> x6, starting transfers between devices: 6 us -> 6.46 us  [along_y(): lax.ppermute(value, 'y', [(i, (i + step) % chips) for i in range(chips)])]
    ppermute x5 -> x6, waiting for transfers between devices: 3.49 us -> 3.22 us  [along_y(): lax.ppermute(value, 'y', [(i, (i + step) % chips) for i in range(chips)])]
    ppermute x5 -> x6, starting transfers between devices: 1.25 us -> 1.24 us  [other_core(): return lax.ppermute(value, 'core', [(0, 1), (1, 0)])]
  transfers between devices with their start and end apart: 25 -> 27, of which waited for: 9 -> 11; matrix products, arithmetic and copies ran while one was open for 0% -> 0% of each run, Pallas kernels for 23% -> 23%
where the time goes in v13:
time: 57.5 us; the launch traced here: 57.3 us
  starting transfers between devices  31.6 us (55%)
  Pallas kernels  14.7 us (26%)
  waiting for transfers between devices  9.98 us (17%)
  other arithmetic  0.71 us (1%)
    ppermute x15, starting transfers between devices, along_z(): lax.ppermute(value, 'mp', [(i, (i + step) % parts) for i in range(parts)])  23.9 us
    ppermute x15, waiting for transfers between devices, along_z(): lax.ppermute(value, 'mp', [(i, (i + step) % parts) for i in range(parts)])  6.5 us
    ppermute x6, starting transfers between devices, along_y(): lax.ppermute(value, 'y', [(i, (i + step) % chips) for i in range(chips)])  6.46 us
    pallas_call x1, Pallas kernels, raw_products(): pl.pallas_call(functools.partial(raw_kernel, len(lines), tile), out_shape...  4.17 us
    pallas_call x1, Pallas kernels, prepare(): pl.pallas_call(functools.partial(prepare_kernel, parts), in_specs=[vmem]...  4.06 us
    ppermute x6, waiting for transfers between devices, along_y(): lax.ppermute(value, 'y', [(i, (i + step) % chips) for i in range(chips)])  3.22 us
    pallas_call x1, Pallas kernels, load(): pl.pallas_call(load_kernel, in_specs=[pl.BlockSpec(memory_space=pltpu.HBM...  2.9 us
    ppermute x6, starting transfers between devices, other_core(): return lax.ppermute(value, 'core', [(0, 1), (1, 0)])  1.24 us
  transfers between devices with their start and end apart: 27, of which 11 were waited for; matrix products, arithmetic and copies ran while one was open for 0% of the time, Pallas kernels for 23%

profile of v13, /device:TPU:0, one launch (start us, length us, event | category | flops | bytes accessed | tf_op | source)
XLA Modules:
  0.0 57.3 jit_solution(15525244880676175141)
XLA Ops:
  0.0 0.9 %attach.1 = bf16[8,4224]{1,0:T(8,128)(2,1)S(1)} custom-call(bf16[8,4096]{1,0:T(8,128)(2,1)} %tokens_ref.1, s32[8,8]{1,0:T(8,128)} %routes_ref.1, f32[8,8]{1,0:T(8,128)} %probs_ref.1), custom_call_target="tpu_custom_call" | custom-call | flops 1 | bytes 1 | tf_op jit(solution)/shard_map/attach/pallas_call | solution.py:62
  1.0 5.1 %collective-permute-start.2 = (bf16[8,4224]{1,0:T(8,128)(2,1)S(1)}, bf16[8,4224]{1,0:T(8,128)(2,1)S(1)}, u32[]{:S(2)}, u32[]{:S(2)}) collective-permute-start(bf16[8,4224]{1,0:T(8,128)(2,1)S(1)} %attach.1), channel_id=1, source_target_pairs={{0,3},{1,0},{2,1},{3,2},{4,7},{5,4},{6,5},{7,6},{8,11},{9,8},{10,9... | collective-permute-start | bytes 202760 | tf_op jit(solution)/shard_map/ppermute | solution.py:419
  6.1 1.0 %collective-permute-start = (bf16[8,4224]{1,0:T(8,128)(2,1)S(1)}, bf16[8,4224]{1,0:T(8,128)(2,1)S(1)}, u32[]{:S(2)}, u32[]{:S(2)}) collective-permute-start(bf16[8,4224]{1,0:T(8,128)(2,1)S(1)} %attach.1), channel_id=1, source_target_pairs={{0,1},{1,2},{2,3},{3,0},{4,5},{5,6},{6,7},{7,4},{8,9},{9,10},{10,1... | collective-permute-start | bytes 202760 | tf_op jit(solution)/shard_map/ppermute | solution.py:419
  7.1 1.5 %collective-permute-start.4 = (bf16[8,4224]{1,0:T(8,128)(2,1)S(1)}, bf16[8,4224]{1,0:T(8,128)(2,1)S(1)}, u32[]{:S(2)}, u32[]{:S(2)}) collective-permute-start(bf16[8,4224]{1,0:T(8,128)(2,1)S(1)} %attach.1), channel_id=1, source_target_pairs={{0,8},{8,0},{1,9},{9,1},{2,10},{10,2},{3,11},{11,3},{4,12},{12,4},... | collective-permute-start | bytes 202760 | tf_op jit(solution)/shard_map/ppermute | solution.py:422
  8.6 4.1 %prepare.1 = (bf16[768,4096]{1,0:T(8,128)(2,1)S(1)}, bf16[256,1024]{1,0:T(8,128)(2,1)S(1)}, bf16[3,32,192]{2,1,0:T(8,128)(2,1)S(1)}, bf16[3,32,192]{2,1,0:T(8,12...) custom-call(bf16[4,8,768]{2,1,0:T(8,128)(2,1)} %refs_0_.1, bf16[4,8,768]{2,1,0:T(8,128)(2,1)} %refs_1_.1, ...), custom_call_target="tpu_custom_call" | custom-call | flops 1 | bytes 1 | tf_op jit(solution)/shard_map/prepare/pallas_call | solution.py:130
  12.8 1.6 %collective-permute-start.5 = (bf16[24,4224]{1,0:T(8,128)(2,1)S(1)}, bf16[24,4224]{1,0:T(8,128)(2,1)S(1)}, u32[]{:S(2)}, u32[]{:S(2)}) collective-permute-start(bf16[24,4224]{1,0:T(8,128)(2,1)S(1)} %pad_maximum_fusion.1), channel_id=1, source_target_pairs={{0,8},{8,0},{1,9},{9,1},{2,10},{10,2},{3,11},{11,3},{4,12},{12,4},... | collective-permute-start | bytes 608264 | tf_op jit(solution)/shard_map/ppermute | solution.py:422
  14.4 1.5 %collective-permute-start.6 = (bf16[3,32,192]{2,1,0:T(8,128)(2,1)S(1)}, bf16[3,32,192]{2,1,0:T(8,128)(2,1)S(1)}, u32[]{:S(2)}, u32[]{:S(2)}) collective-permute-start(bf16[3,32,192]{2,1,0:T(8,128)(2,1)S(1)} %get-tuple-element.61), channel_id=1, source_target_pairs={{0,1},{1,2},{2,3},{3,0},{4,5},{5,6},{6,7},{7,4},{8,9},{9,10},{10,1... | collective-permute-start | bytes 110600 | tf_op jit(solution)/shard_map/ppermute | solution.py:419
  15.9 1.0 %collective-permute-start.7 = (bf16[3,32,192]{2,1,0:T(8,128)(2,1)S(1)}, bf16[3,32,192]{2,1,0:T(8,128)(2,1)S(1)}, u32[]{:S(2)}, u32[]{:S(2)}) collective-permute-start(bf16[3,32,192]{2,1,0:T(8,128)(2,1)S(1)} %get-tuple-element.62), channel_id=1, source_target_pairs={{0,2},{1,3},{2,0},{3,1},{4,6},{5,7},{6,4},{7,5},{8,10},{9,11},{10,... | collective-permute-start | bytes 110600 | tf_op jit(solution)/shard_map/ppermute | solution.py:419
  16.8 2.3 %collective-permute-start.8 = (bf16[3,32,192]{2,1,0:T(8,128)(2,1)S(1)}, bf16[3,32,192]{2,1,0:T(8,128)(2,1)S(1)}, u32[]{:S(2)}, u32[]{:S(2)}) collective-permute-start(bf16[3,32,192]{2,1,0:T(8,128)(2,1)S(1)} %get-tuple-element.63), channel_id=1, source_target_pairs={{0,3},{1,0},{2,1},{3,2},{4,7},{5,4},{6,5},{7,6},{8,11},{9,8},{10,9... | collective-permute-start | bytes 110600 | tf_op jit(solution)/shard_map/ppermute | solution.py:419
  19.1 2.9 %load.1.refs_5_ = bf16[768,4096]{1,0:T(8,128)(2,1)S(1)} custom-call(bf16[768,4096]{1,0:T(8,128)(2,1)} %bitcast.14), custom_call_target="tpu_custom_call" | custom-call | flops 1 | bytes 1 | tf_op jit(solution)/shard_map/load/pallas_call | solution.py:89
  22.7 0.7 %collective-permute-start.14 = (bf16[128,1024]{1,0:T(8,128)(2,1)S(1)}, bf16[128,1024]{1,0:T(8,128)(2,1)S(1)}, u32[]{:S(2)}, u32[]{:S(2)}) collective-permute-start(bf16[128,1024]{1,0:T(8,128)(2,1)S(1)} %bitcast.12), channel_id=1, source_target_pairs={{0,8},{8,0},{1,9},{9,1},{2,10},{10,2},{3,11},{11,3},{4,12},{12,4},... | collective-permute-start | bytes 786440 | tf_op jit(solution)/shard_map/ppermute | solution.py:422
  24.3 1.0 %collective-permute-start.11 = (bf16[128,256]{1,0:T(8,128)(2,1)S(1)}, bf16[128,256]{1,0:T(8,128)(2,1)S(1)}, u32[]{:S(2)}, u32[]{:S(2)}) collective-permute-start(bf16[128,256]{1,0:T(8,128)(2,1)S(1)} %get-tuple-element.71), channel_id=1, source_target_pairs={{0,1},{1,2},{2,3},{3,0},{4,5},{5,6},{6,7},{7,4},{8,9},{9,10},{10,1... | collective-permute-start | bytes 196616 | tf_op jit(solution)/shard_map/ppermute | solution.py:419
  25.3 2.1 %collective-permute-start.12 = (bf16[128,256]{1,0:T(8,128)(2,1)S(1)}, bf16[128,256]{1,0:T(8,128)(2,1)S(1)}, u32[]{:S(2)}, u32[]{:S(2)}) collective-permute-start(bf16[128,256]{1,0:T(8,128)(2,1)S(1)} %get-tuple-element.72), channel_id=1, source_target_pairs={{0,2},{1,3},{2,0},{3,1},{4,6},{5,7},{6,4},{7,5},{8,10},{9,11},{10,... | collective-permute-start | bytes 196616 | tf_op jit(solution)/shard_map/ppermute | solution.py:419
  27.5 1.0 %collective-permute-start.13 = (bf16[128,256]{1,0:T(8,128)(2,1)S(1)}, bf16[128,256]{1,0:T(8,128)(2,1)S(1)}, u32[]{:S(2)}, u32[]{:S(2)}) collective-permute-start(bf16[128,256]{1,0:T(8,128)(2,1)S(1)} %get-tuple-element.73), channel_id=1, source_target_pairs={{0,3},{1,0},{2,1},{3,2},{4,7},{5,4},{6,5},{7,6},{8,11},{9,8},{10,9... | collective-permute-start | bytes 196616 | tf_op jit(solution)/shard_map/ppermute | solution.py:419
  28.5 4.2 %raw.1 = (f32[128,768]{1,0:T(8,128)S(1)}, f32[128,768]{1,0:T(8,128)S(1)}) custom-call(bf16[32,4224]{1,0:T(8,128)(2,1)S(1)} %pad_maximum_fusion.refs_0_, bf16[32,4224]{1,0:T(8,128)(2,1)S(1)} %constant_dynamic-update-slice_fusion.refs_1_, bf16[32,4224]{1,0:T(8,128)(2,1)S(1)} %collective-permute-done.9.refs_2_, ...), custom_call_target="tpu_custom_call" | custom-call | flops 1 | bytes 1 | tf_op jit(solution)/shard_map/raw/pallas_call | solution.py:212
  32.7 0.6 %collective-permute-done.12.refs_6_ = bf16[128,256]{1,0:T(8,128)(2,1)S(1)} collective-permute-done((bf16[128,256]{1,0:T(8,128)(2,1)S(1)}, bf16[128,256]{1,0:T(8,128)(2,1)S(1)}, u32[]{:S(2)}, u32[]{:S(2)}) %collective-permute-start.12) | collective-permute-done | bytes 65568 | tf_op jit(solution)/shard_map/ppermute | solution.py:419
  33.9 1.1 %down.1 = (f32[64,4096]{1,0:T(8,128)S(1)}, bf16[64,4096]{1,0:T(8,128)(2,1)S(1)}) custom-call(bf16[128,768]{1,0:T(8,128)(2,1)S(1)} %get-tuple-element.79.hidden_ref, bf16[768,4096]{1,0:T(8,128)(2,1)S(1)} %bitcast.10), custom_call_target="tpu_custom_call" | custom-call | flops 1 | bytes 1 | tf_op jit(solution)/shard_map/down/pallas_call | solution.py:271
  35.6 0.8 %collective-permute-start.17 = (bf16[32,256]{1,0:T(8,128)(2,1)S(1)}, bf16[32,256]{1,0:T(8,128)(2,1)S(1)}, u32[]{:S(2)}, u32[]{:S(2)}) collective-permute-start(bf16[32,256]{1,0:T(8,128)(2,1)S(1)} %get-tuple-element.85), channel_id=1, source_target_pairs={{0,8},{8,0},{1,9},{9,1},{2,10},{10,2},{3,11},{11,3},{4,12},{12,4},... | collective-permute-start | bytes 49160 | tf_op jit(solution)/shard_map/ppermute | solution.py:422
  36.4 3.0 %collective-permute-done.17.refs_1_ = bf16[32,256]{1,0:T(8,128)(2,1)S(1)} collective-permute-done((bf16[32,256]{1,0:T(8,128)(2,1)S(1)}, bf16[32,256]{1,0:T(8,128)(2,1)S(1)}, u32[]{:S(2)}, u32[]{:S(2)}) %collective-permute-start.17) | collective-permute-done | bytes 16416 | tf_op jit(solution)/shard_map/ppermute | solution.py:422
  39.5 0.8 %collective-permute-start.22 = (bf16[24,4096]{1,0:T(8,128)(2,1)S(1)}, bf16[24,4096]{1,0:T(8,128)(2,1)S(1)}, u32[]{:S(2)}, u32[]{:S(2)}) collective-permute-start(bf16[24,4096]{1,0:T(8,128)(2,1)S(1)} %get-tuple-element.94), channel_id=1, source_target_pairs={{0,8},{8,0},{1,9},{9,1},{2,10},{10,2},{3,11},{11,3},{4,12},{12,4},... | collective-permute-start | bytes 589832 | tf_op jit(solution)/shard_map/ppermute | solution.py:422
  40.4 1.9 %collective-permute-start.19 = (bf16[32,512]{1,0:T(8,128)(2,1)S(1)}, bf16[32,512]{1,0:T(8,128)(2,1)S(1)}, u32[]{:S(2)}, u32[]{:S(2)}) collective-permute-start(bf16[32,512]{1,0:T(8,128)(2,1)S(1)} %get-tuple-element.91), channel_id=1, source_target_pairs={{0,1},{1,2},{2,3},{3,0},{4,5},{5,6},{6,7},{7,4},{8,9},{9,10},{10,1... | collective-permute-start | bytes 98312 | tf_op jit(solution)/shard_map/ppermute | solution.py:419
  42.2 1.2 %collective-permute-start.20 = (bf16[32,512]{1,0:T(8,128)(2,1)S(1)}, bf16[32,512]{1,0:T(8,128)(2,1)S(1)}, u32[]{:S(2)}, u32[]{:S(2)}) collective-permute-start(bf16[32,512]{1,0:T(8,128)(2,1)S(1)} %get-tuple-element.92), channel_id=1, source_target_pairs={{0,2},{1,3},{2,0},{3,1},{4,6},{5,7},{6,4},{7,5},{8,10},{9,11},{10,... | collective-permute-start | bytes 98312 | tf_op jit(solution)/shard_map/ppermute | solution.py:419
  43.5 1.3 %collective-permute-start.21 = (bf16[32,512]{1,0:T(8,128)(2,1)S(1)}, bf16[32,512]{1,0:T(8,128)(2,1)S(1)}, u32[]{:S(2)}, u32[]{:S(2)}) collective-permute-start(bf16[32,512]{1,0:T(8,128)(2,1)S(1)} %get-tuple-element.93), channel_id=1, source_target_pairs={{0,3},{1,0},{2,1},{3,2},{4,7},{5,4},{6,5},{7,6},{8,11},{9,8},{10,9... | collective-permute-start | bytes 98312 | tf_op jit(solution)/shard_map/ppermute | solution.py:419
  44.8 1.4 %collective-permute-done.19.refs_0_ = bf16[32,512]{1,0:T(8,128)(2,1)S(1)} collective-permute-done((bf16[32,512]{1,0:T(8,128)(2,1)S(1)}, bf16[32,512]{1,0:T(8,128)(2,1)S(1)}, u32[]{:S(2)}, u32[]{:S(2)}) %collective-permute-start.19) | collective-permute-done | bytes 32800 | tf_op jit(solution)/shard_map/ppermute | solution.py:419
  46.2 1.2 %collective-permute-done.20.refs_1_ = bf16[32,512]{1,0:T(8,128)(2,1)S(1)} collective-permute-done((bf16[32,512]{1,0:T(8,128)(2,1)S(1)}, bf16[32,512]{1,0:T(8,128)(2,1)S(1)}, u32[]{:S(2)}, u32[]{:S(2)}) %collective-permute-start.20) | collective-permute-done | bytes 32800 | tf_op jit(solution)/shard_map/ppermute | solution.py:419
  47.9 1.1 %collective-permute-start.26 = (bf16[8,4096]{1,0:T(8,128)(2,1)S(1)}, bf16[8,4096]{1,0:T(8,128)(2,1)S(1)}, u32[]{:S(2)}, u32[]{:S(2)}) collective-permute-start(bf16[8,4096]{1,0:T(8,128)(2,1)S(1)} %get-tuple-element.100), channel_id=1, source_target_pairs={{0,1},{1,2},{2,3},{3,0},{4,5},{5,6},{6,7},{7,4},{8,9},{9,10},{10,1... | collective-permute-start | bytes 196616 | tf_op jit(solution)/shard_map/ppermute | solution.py:419
  49.0 2.4 %collective-permute-start.25 = (bf16[8,4096]{1,0:T(8,128)(2,1)S(1)}, bf16[8,4096]{1,0:T(8,128)(2,1)S(1)}, u32[]{:S(2)}, u32[]{:S(2)}) collective-permute-start(bf16[8,4096]{1,0:T(8,128)(2,1)S(1)} %get-tuple-element.99), channel_id=1, source_target_pairs={{0,2},{1,3},{2,0},{3,1},{4,6},{5,7},{6,4},{7,5},{8,10},{9,11},{10,... | collective-permute-start | bytes 196616 | tf_op jit(solution)/shard_map/ppermute | solution.py:419
  51.4 1.0 %collective-permute-start.24 = (bf16[8,4096]{1,0:T(8,128)(2,1)S(1)}, bf16[8,4096]{1,0:T(8,128)(2,1)S(1)}, u32[]{:S(2)}, u32[]{:S(2)}) collective-permute-start(bf16[8,4096]{1,0:T(8,128)(2,1)S(1)} %get-tuple-element.98), channel_id=1, source_target_pairs={{0,3},{1,0},{2,1},{3,2},{4,7},{5,4},{6,5},{7,6},{8,11},{9,8},{10,9... | collective-permute-start | bytes 196616 | tf_op jit(solution)/shard_map/ppermute | solution.py:419
  52.4 1.0 %collective-permute-start.23 = (bf16[8,4096]{1,0:T(8,128)(2,1)S(1)}, bf16[8,4096]{1,0:T(8,128)(2,1)S(1)}, u32[]{:S(2)}, u32[]{:S(2)}) collective-permute-start(bf16[8,4096]{1,0:T(8,128)(2,1)S(1)} %get-tuple-element.97), channel_id=1, source_target_pairs={{0,8},{8,0},{1,9},{9,1},{2,10},{10,2},{3,11},{11,3},{4,12},{12,4},... | collective-permute-start | bytes 196616 | tf_op jit(solution)/shard_map/ppermute | solution.py:422
  53.4 1.2 %collective-permute-done.26 = bf16[8,4096]{1,0:T(8,128)(2,1)S(1)} collective-permute-done((bf16[8,4096]{1,0:T(8,128)(2,1)S(1)}, bf16[8,4096]{1,0:T(8,128)(2,1)S(1)}, u32[]{:S(2)}, u32[]{:S(2)}) %collective-permute-start.26) | collective-permute-done | bytes 65568 | tf_op jit(solution)/shard_map/ppermute | solution.py:419
  54.5 1.7 %collective-permute-done.25 = bf16[8,4096]{1,0:T(8,128)(2,1)S(1)} collective-permute-done((bf16[8,4096]{1,0:T(8,128)(2,1)S(1)}, bf16[8,4096]{1,0:T(8,128)(2,1)S(1)}, u32[]{:S(2)}, u32[]{:S(2)}) %collective-permute-start.25) | collective-permute-done | bytes 65568 | tf_op jit(solution)/shard_map/ppermute | solution.py:419
  56.6 0.7 %add_convert_fusion = bf16[8,4096]{1,0:T(8,128)(2,1)} fusion(bf16[8,4096]{1,0:T(8,128)(2,1)S(1)} %collective-permute-done.26, bf16[8,4096]{1,0:T(8,128)(2,1)S(1)} %collective-permute-done.25, bf16[8,4096]{1,0:T(8,128)(2,1)S(1)} %collective-permute-done.24, f32[8,4096]{1,0:T(8,128)S(1)} %get-tuple-element.95, bf16[8,4096]{1,0:T(8,128)(2,1)S(1)} %collective-permute-done.23), kind=kLoop, calls=%fused_computation.2 | loop fusion | flops 294912 | bytes 458752 | tf_op jit(solution)/shard_map/convert_element_type | solution.py:480
  (47 shorter events, 3.8 us)
Async XLA Ops:
  1.0 11.7 %collective-permute-start.2 = (bf16[8,4224]{1,0:T(8,128)(2,1)S(1)}, bf16[8,4224]{1,0:T(8,128)(2,1)S(1)}, u32[]{:S(2)}, u32[]{:S(2)}) collective-permute-start(bf16[8,4224]{1,0:T(8,128)(2,1)S(1)} %attach.1), channel_id=1, source_target_pairs={{0,3},{1,0},{2,1},{3,2},{4,7},{5,4},{6,5},{7,6},{8,11},{9,8},{10,9... | collective-permute-start | bytes 202760 | tf_op jit(solution)/shard_map/ppermute | solution.py:419
  6.1 6.6 %collective-permute-start.1 = (bf16[8,4224]{1,0:T(8,128)(2,1)S(1)}, bf16[8,4224]{1,0:T(8,128)(2,1)S(1)}, u32[]{:S(2)}, u32[]{:S(2)}) collective-permute-start(bf16[8,4224]{1,0:T(8,128)(2,1)S(1)} %attach.1), channel_id=1, source_target_pairs={{0,2},{1,3},{2,0},{3,1},{4,6},{5,7},{6,4},{7,5},{8,10},{9,11},{10,... | collective-permute-start | bytes 202760 | tf_op jit(solution)/shard_map/ppermute | solution.py:419
  6.1 6.6 %collective-permute-start = (bf16[8,4224]{1,0:T(8,128)(2,1)S(1)}, bf16[8,4224]{1,0:T(8,128)(2,1)S(1)}, u32[]{:S(2)}, u32[]{:S(2)}) collective-permute-start(bf16[8,4224]{1,0:T(8,128)(2,1)S(1)} %attach.1), channel_id=1, source_target_pairs={{0,1},{1,2},{2,3},{3,0},{4,5},{5,6},{6,7},{7,4},{8,9},{9,10},{10,1... | collective-permute-start | bytes 202760 | tf_op jit(solution)/shard_map/ppermute | solution.py:419
  7.1 5.7 %collective-permute-start.4 = (bf16[8,4224]{1,0:T(8,128)(2,1)S(1)}, bf16[8,4224]{1,0:T(8,128)(2,1)S(1)}, u32[]{:S(2)}, u32[]{:S(2)}) collective-permute-start(bf16[8,4224]{1,0:T(8,128)(2,1)S(1)} %attach.1), channel_id=1, source_target_pairs={{0,8},{8,0},{1,9},{9,1},{2,10},{10,2},{3,11},{11,3},{4,12},{12,4},... | collective-permute-start | bytes 202760 | tf_op jit(solution)/shard_map/ppermute | solution.py:422
  8.6 4.2 %collective-permute-start.3 = (bf16[128,1024]{1,0:T(8,128)(2,1)}, bf16[128,1024]{1,0:T(8,128)(2,1)S(1)}, u32[]{:S(2)}, u32[]{:S(2)}) collective-permute-start(bf16[128,1024]{1,0:T(8,128)(2,1)} %bitcast.11), channel_id=1, source_target_pairs={{0,4},{4,0},{1,5},{5,1},{2,6},{6,2},{3,7},{7,3},{8,12},{12,8},{9,1... | collective-permute-start | bytes 786440 | tf_op jit(solution)/shard_map/ppermute | solution.py:425
  12.8 9.3 %collective-permute-start.5 = (bf16[24,4224]{1,0:T(8,128)(2,1)S(1)}, bf16[24,4224]{1,0:T(8,128)(2,1)S(1)}, u32[]{:S(2)}, u32[]{:S(2)}) collective-permute-start(bf16[24,4224]{1,0:T(8,128)(2,1)S(1)} %pad_maximum_fusion.1), channel_id=1, source_target_pairs={{0,8},{8,0},{1,9},{9,1},{2,10},{10,2},{3,11},{11,3},{4,12},{12,4},... | collective-permute-start | bytes 608264 | tf_op jit(solution)/shard_map/ppermute | solution.py:422
  14.4 7.8 %collective-permute-start.6 = (bf16[3,32,192]{2,1,0:T(8,128)(2,1)S(1)}, bf16[3,32,192]{2,1,0:T(8,128)(2,1)S(1)}, u32[]{:S(2)}, u32[]{:S(2)}) collective-permute-start(bf16[3,32,192]{2,1,0:T(8,128)(2,1)S(1)} %get-tuple-element.61), channel_id=1, source_target_pairs={{0,1},{1,2},{2,3},{3,0},{4,5},{5,6},{6,7},{7,4},{8,9},{9,10},{10,1... | collective-permute-start | bytes 110600 | tf_op jit(solution)/shard_map/ppermute | solution.py:419
  15.9 6.3 %collective-permute-start.7 = (bf16[3,32,192]{2,1,0:T(8,128)(2,1)S(1)}, bf16[3,32,192]{2,1,0:T(8,128)(2,1)S(1)}, u32[]{:S(2)}, u32[]{:S(2)}) collective-permute-start(bf16[3,32,192]{2,1,0:T(8,128)(2,1)S(1)} %get-tuple-element.62), channel_id=1, source_target_pairs={{0,2},{1,3},{2,0},{3,1},{4,6},{5,7},{6,4},{7,5},{8,10},{9,11},{10,... | collective-permute-start | bytes 110600 | tf_op jit(solution)/shard_map/ppermute | solution.py:419
  16.8 5.3 %collective-permute-start.8 = (bf16[3,32,192]{2,1,0:T(8,128)(2,1)S(1)}, bf16[3,32,192]{2,1,0:T(8,128)(2,1)S(1)}, u32[]{:S(2)}, u32[]{:S(2)}) collective-permute-start(bf16[3,32,192]{2,1,0:T(8,128)(2,1)S(1)} %get-tuple-element.63), channel_id=1, source_target_pairs={{0,3},{1,0},{2,1},{3,2},{4,7},{5,4},{6,5},{7,6},{8,11},{9,8},{10,9... | collective-permute-start | bytes 110600 | tf_op jit(solution)/shard_map/ppermute | solution.py:419
  19.1 3.6 %copy-start = (bf16[4,32,1024]{2,1,0:T(8,128)(2,1)S(1)}, bf16[4,32,1024]{2,1,0:T(8,128)(2,1)}, u32[]{:S(2)}) copy-start(bf16[4,32,1024]{2,1,0:T(8,128)(2,1)} %param.23) | copy-start | bytes 786436
  22.0 1.8 %collective-permute-start.9 = (bf16[32,4224]{1,0:T(8,128)(2,1)S(1)}, bf16[32,4224]{1,0:T(8,128)(2,1)S(1)}, u32[]{:S(2)}, u32[]{:S(2)}) collective-permute-start(bf16[32,4224]{1,0:T(8,128)(2,1)S(1)} %pad_maximum_fusion.refs_0_), channel_id=1, source_target_pairs={{0,4},{4,0},{1,5},{5,1},{2,6},{6,2},{3,7},{7,3},{8,12},{12,8},{9,1... | collective-permute-start | bytes 811016 | tf_op jit(solution)/shard_map/ppermute | solution.py:425
  22.2 1.9 %collective-permute-start.10 = (bf16[32,4224]{1,0:T(8,128)(2,1)S(1)}, bf16[32,4224]{1,0:T(8,128)(2,1)S(1)}, u32[]{:S(2)}, u32[]{:S(2)}) collective-permute-start(bf16[32,4224]{1,0:T(8,128)(2,1)S(1)} %constant_dynamic-update-slice_fusion.refs_1_), channel_id=1, source_target_pairs={{0,4},{4,0},{1,5},{5,1},{2,6},{6,2},{3,7},{7,3},{8,12},{12,8},{9,1... | collective-permute-start | bytes 811016 | tf_op jit(solution)/shard_map/ppermute | solution.py:425
  22.7 10.0 %collective-permute-start.14 = (bf16[128,1024]{1,0:T(8,128)(2,1)S(1)}, bf16[128,1024]{1,0:T(8,128)(2,1)S(1)}, u32[]{:S(2)}, u32[]{:S(2)}) collective-permute-start(bf16[128,1024]{1,0:T(8,128)(2,1)S(1)} %bitcast.12), channel_id=1, source_target_pairs={{0,8},{8,0},{1,9},{9,1},{2,10},{10,2},{3,11},{11,3},{4,12},{12,4},... | collective-permute-start | bytes 786440 | tf_op jit(solution)/shard_map/ppermute | solution.py:422
  24.3 8.4 %collective-permute-start.11 = (bf16[128,256]{1,0:T(8,128)(2,1)S(1)}, bf16[128,256]{1,0:T(8,128)(2,1)S(1)}, u32[]{:S(2)}, u32[]{:S(2)}) collective-permute-start(bf16[128,256]{1,0:T(8,128)(2,1)S(1)} %get-tuple-element.71), channel_id=1, source_target_pairs={{0,1},{1,2},{2,3},{3,0},{4,5},{5,6},{6,7},{7,4},{8,9},{9,10},{10,1... | collective-permute-start | bytes 196616 | tf_op jit(solution)/shard_map/ppermute | solution.py:419
  25.3 8.0 %collective-permute-start.12 = (bf16[128,256]{1,0:T(8,128)(2,1)S(1)}, bf16[128,256]{1,0:T(8,128)(2,1)S(1)}, u32[]{:S(2)}, u32[]{:S(2)}) collective-permute-start(bf16[128,256]{1,0:T(8,128)(2,1)S(1)} %get-tuple-element.72), channel_id=1, source_target_pairs={{0,2},{1,3},{2,0},{3,1},{4,6},{5,7},{6,4},{7,5},{8,10},{9,11},{10,... | collective-permute-start | bytes 196616 | tf_op jit(solution)/shard_map/ppermute | solution.py:419
  27.5 6.5 %slice-start = ((s8[6291456]{0:T(1024)(128)(4,1)}), s8[4194304]{0:T(1024)(128)(4,1)S(1)}, s32[]{:S(2)}) async-start(s8[6291456]{0:T(1024)(128)(4,1)} %bitcast.8), calls=%async_computation | async-start | bytes 8388608
  27.5 6.5 %slice-start.1 = ((s8[6291456]{0:T(1024)(128)(4,1)}), s8[2097152]{0:T(1024)(128)(4,1)S(1)}, s32[]{:S(2)}) async-start(s8[6291456]{0:T(1024)(128)(4,1)} %bitcast.8), calls=%async_computation.1 | async-start | bytes 4194304
  27.5 5.8 %collective-permute-start.13 = (bf16[128,256]{1,0:T(8,128)(2,1)S(1)}, bf16[128,256]{1,0:T(8,128)(2,1)S(1)}, u32[]{:S(2)}, u32[]{:S(2)}) collective-permute-start(bf16[128,256]{1,0:T(8,128)(2,1)S(1)} %get-tuple-element.73), channel_id=1, source_target_pairs={{0,3},{1,0},{2,1},{3,2},{4,7},{5,4},{6,5},{7,6},{8,11},{9,8},{10,9... | collective-permute-start | bytes 196616 | tf_op jit(solution)/shard_map/ppermute | solution.py:419
  33.8 1.2 %collective-permute-start.15 = (bf16[64,128]{1,0:T(8,128)(2,1)S(1)}, bf16[64,128]{1,0:T(8,128)(2,1)S(1)}, u32[]{:S(2)}, u32[]{:S(2)}) collective-permute-start(bf16[64,128]{1,0:T(8,128)(2,1)S(1)} %get-tuple-element.82), channel_id=1, source_target_pairs={{0,4},{4,0},{1,5},{5,1},{2,6},{6,2},{3,7},{7,3},{8,12},{12,8},{9,1... | collective-permute-start | bytes 49160 | tf_op jit(solution)/shard_map/ppermute | solution.py:425
  35.1 4.3 %collective-permute-start.16 = (bf16[64,4096]{1,0:T(8,128)(2,1)S(1)}, bf16[64,4096]{1,0:T(8,128)(2,1)S(1)}, u32[]{:S(2)}, u32[]{:S(2)}) collective-permute-start(bf16[64,4096]{1,0:T(8,128)(2,1)S(1)} %get-tuple-element.83), channel_id=1, source_target_pairs={{0,4},{4,0},{1,5},{5,1},{2,6},{6,2},{3,7},{7,3},{8,12},{12,8},{9,1... | collective-permute-start | bytes 1572872 | tf_op jit(solution)/shard_map/ppermute | solution.py:425
  35.6 3.7 %collective-permute-start.17 = (bf16[32,256]{1,0:T(8,128)(2,1)S(1)}, bf16[32,256]{1,0:T(8,128)(2,1)S(1)}, u32[]{:S(2)}, u32[]{:S(2)}) collective-permute-start(bf16[32,256]{1,0:T(8,128)(2,1)S(1)} %get-tuple-element.85), channel_id=1, source_target_pairs={{0,8},{8,0},{1,9},{9,1},{2,10},{10,2},{3,11},{11,3},{4,12},{12,4},... | collective-permute-start | bytes 49160 | tf_op jit(solution)/shard_map/ppermute | solution.py:422
  39.3 8.3 %collective-permute-start.18 = (bf16[128,1024]{1,0:T(8,128)(2,1)S(1)}, bf16[128,1024]{1,0:T(8,128)(2,1)S(1)}, u32[]{:S(2)}, u32[]{:S(2)}) collective-permute-start(bf16[128,1024]{1,0:T(8,128)(2,1)S(1)} %collective-permute-done.14.refs_2_), channel_id=1, source_target_pairs={{0,4},{4,0},{1,5},{5,1},{2,6},{6,2},{3,7},{7,3},{8,12},{12,8},{9,1... | collective-permute-start | bytes 786440 | tf_op jit(solution)/shard_map/ppermute | solution.py:425
  39.5 8.1 %collective-permute-start.22 = (bf16[24,4096]{1,0:T(8,128)(2,1)S(1)}, bf16[24,4096]{1,0:T(8,128)(2,1)S(1)}, u32[]{:S(2)}, u32[]{:S(2)}) collective-permute-start(bf16[24,4096]{1,0:T(8,128)(2,1)S(1)} %get-tuple-element.94), channel_id=1, source_target_pairs={{0,8},{8,0},{1,9},{9,1},{2,10},{10,2},{3,11},{11,3},{4,12},{12,4},... | collective-permute-start | bytes 589832 | tf_op jit(solution)/shard_map/ppermute | solution.py:422
  40.4 5.9 %collective-permute-start.19 = (bf16[32,512]{1,0:T(8,128)(2,1)S(1)}, bf16[32,512]{1,0:T(8,128)(2,1)S(1)}, u32[]{:S(2)}, u32[]{:S(2)}) collective-permute-start(bf16[32,512]{1,0:T(8,128)(2,1)S(1)} %get-tuple-element.91), channel_id=1, source_target_pairs={{0,1},{1,2},{2,3},{3,0},{4,5},{5,6},{6,7},{7,4},{8,9},{9,10},{10,1... | collective-permute-start | bytes 98312 | tf_op jit(solution)/shard_map/ppermute | solution.py:419
  42.2 5.2 %collective-permute-start.20 = (bf16[32,512]{1,0:T(8,128)(2,1)S(1)}, bf16[32,512]{1,0:T(8,128)(2,1)S(1)}, u32[]{:S(2)}, u32[]{:S(2)}) collective-permute-start(bf16[32,512]{1,0:T(8,128)(2,1)S(1)} %get-tuple-element.92), channel_id=1, source_target_pairs={{0,2},{1,3},{2,0},{3,1},{4,6},{5,7},{6,4},{7,5},{8,10},{9,11},{10,... | collective-permute-start | bytes 98312 | tf_op jit(solution)/shard_map/ppermute | solution.py:419
  43.5 4.1 %collective-permute-start.21 = (bf16[32,512]{1,0:T(8,128)(2,1)S(1)}, bf16[32,512]{1,0:T(8,128)(2,1)S(1)}, u32[]{:S(2)}, u32[]{:S(2)}) collective-permute-start(bf16[32,512]{1,0:T(8,128)(2,1)S(1)} %get-tuple-element.93), channel_id=1, source_target_pairs={{0,3},{1,0},{2,1},{3,2},{4,7},{5,4},{6,5},{7,6},{8,11},{9,8},{10,9... | collective-permute-start | bytes 98312 | tf_op jit(solution)/shard_map/ppermute | solution.py:419
  47.9 6.6 %collective-permute-start.26 = (bf16[8,4096]{1,0:T(8,128)(2,1)S(1)}, bf16[8,4096]{1,0:T(8,128)(2,1)S(1)}, u32[]{:S(2)}, u32[]{:S(2)}) collective-permute-start(bf16[8,4096]{1,0:T(8,128)(2,1)S(1)} %get-tuple-element.100), channel_id=1, source_target_pairs={{0,1},{1,2},{2,3},{3,0},{4,5},{5,6},{6,7},{7,4},{8,9},{9,10},{10,1... | collective-permute-start | bytes 196616 | tf_op jit(solution)/shard_map/ppermute | solution.py:419
  49.0 7.2 %collective-permute-start.25 = (bf16[8,4096]{1,0:T(8,128)(2,1)S(1)}, bf16[8,4096]{1,0:T(8,128)(2,1)S(1)}, u32[]{:S(2)}, u32[]{:S(2)}) collective-permute-start(bf16[8,4096]{1,0:T(8,128)(2,1)S(1)} %get-tuple-element.99), channel_id=1, source_target_pairs={{0,2},{1,3},{2,0},{3,1},{4,6},{5,7},{6,4},{7,5},{8,10},{9,11},{10,... | collective-permute-start | bytes 196616 | tf_op jit(solution)/shard_map/ppermute | solution.py:419
  51.4 5.0 %collective-permute-start.24 = (bf16[8,4096]{1,0:T(8,128)(2,1)S(1)}, bf16[8,4096]{1,0:T(8,128)(2,1)S(1)}, u32[]{:S(2)}, u32[]{:S(2)}) collective-permute-start(bf16[8,4096]{1,0:T(8,128)(2,1)S(1)} %get-tuple-element.98), channel_id=1, source_target_pairs={{0,3},{1,0},{2,1},{3,2},{4,7},{5,4},{6,5},{7,6},{8,11},{9,8},{10,9... | collective-permute-start | bytes 196616 | tf_op jit(solution)/shard_map/ppermute | solution.py:419
  52.4 4.3 %collective-permute-start.23 = (bf16[8,4096]{1,0:T(8,128)(2,1)S(1)}, bf16[8,4096]{1,0:T(8,128)(2,1)S(1)}, u32[]{:S(2)}, u32[]{:S(2)}) collective-permute-start(bf16[8,4096]{1,0:T(8,128)(2,1)S(1)} %get-tuple-element.97), channel_id=1, source_target_pairs={{0,8},{8,0},{1,9},{9,1},{2,10},{10,2},{3,11},{11,3},{4,12},{12,4},... | collective-permute-start | bytes 196616 | tf_op jit(solution)/shard_map/ppermute | solution.py:422

commit v14 on v13

--- a/solution.py
+++ b/solution.py
@@ -201,14 +201,14 @@
     x = jnp.concatenate([line[:, :width] for line in lines])
     for i in range(hid // tile):
         span = pl.ds(i * tile, tile)
-        gate_ref[:, span] = dot_nt(x, gate_w[span])
-        up_ref[:, span] = dot_nt(x, up_w[span])
+        gate_ref[:, span] = dot_nt(gate_w[span], x).T
+        up_ref[:, span] = dot_nt(up_w[span], x).T
 
 
 def raw_products(lines, gate_w, up_w):
     hid = gate_w.shape[0]
     total = sum(line.shape[0] for line in lines)
-    tile = 256 if hid % 256 == 0 else 128
+    tile = 384
     return pl.pallas_call(
         functools.partial(raw_kernel, len(lines), tile),
         out_shape=[jax.ShapeDtypeStruct((total, hid), F32)] * 2,
@@ -330,24 +330,21 @@
     )(*pieces)
 
 
-def fold_kernel(head, near_ref, far_ref, own_ref, *out_refs):
+def fold_kernel(near_ref, far_ref, own_ref, *out_refs):
     span = own_ref.shape[0]
     total = near_ref[...] + far_ref[...].astype(F32)
     own_ref[...] = total[:span]
-    for n in range(len(out_refs) // 2):
-        line = total[(n + 1) * span : (n + 2) * span]
-        out_refs[2 * n][...] = line[:head].astype(BF)
-        out_refs[2 * n + 1][...] = line[head:].astype(BF)
-
-
-def fold(near, far, chips, head):
+    for n, out_ref in enumerate(out_refs):
+        out_ref[...] = total[(n + 1) * span : (n + 2) * span].astype(BF)
+
+
+def fold(near, far, chips):
     total, width = near.shape
     span = total // chips
-    cuts = [head, span - head]
-    return pl.pallas_call(
-        functools.partial(fold_kernel, head),
+    return pl.pallas_call(
+        fold_kernel,
         out_shape=[jax.ShapeDtypeStruct((span, width), F32)]
-        + [jax.ShapeDtypeStruct((rows, width), BF) for rows in cuts] * (chips - 1),
+        + [jax.ShapeDtypeStruct((span, width), BF)] * (chips - 1),
         compiler_params=pltpu.CompilerParams(vmem_limit_bytes=VMEM_LIMIT),
         cost_estimate=BRIEF,
         name="fold",
@@ -364,18 +361,15 @@
     for n, ref in enumerate(rights):
         at = (2 * n if n < chips else 2 * (n - chips) + 1) * ranks
         value += dot_nn(low[:, at : at + ranks], ref[...])
-    total = own_ref[rows:]
+    total = own_ref[...]
     value += own_ref[:, pl.ds(offset, block)]
-    rest = value[rows:]
     for ref in backs:
         total += ref[...].astype(F32)
-        rest += ref[:, pl.ds(offset, block)].astype(F32)
-    outs[0][...] = own_ref[:rows]
-    outs[0][:, pl.ds(offset, block)] = value[:rows]
-    for k in range(1, parts):
-        span = slice((k - 1) * rows, k * rows)
-        outs[k][...] = total[span].astype(BF)
-        outs[k][:, pl.ds(offset, block)] = rest[span].astype(BF)
+        value += ref[:, pl.ds(offset, block)].astype(F32)
+    for k, out_ref in enumerate(outs):
+        span = slice(k * rows, (k + 1) * rows)
+        out_ref[...] = total[span].astype(out_ref.dtype)
+        out_ref[:, pl.ds(offset, block)] = value[span].astype(out_ref.dtype)
 
 
 def merge(own, rights, low, backs, rows):
@@ -467,14 +461,11 @@
 
     near, far = down_products(hidden, w_down.reshape(hid, width))
     far = after(other_core(after(far, swapped)), lows)
-    out, *others = fold(near, far, chips, rows)
-    backs = [along_y(others[2 * s - 1], -s) for s in range(1, chips)]
+    out, *others = fold(near, far, chips)
+    backs = [along_y(others[s - 1], -s) for s in range(1, chips)]
     rights += [partner_right] + [other_core(after(right, bottom[0])) for right in rights[1:]]
     own, *pieces = merge(out, rights, add_up(bottom[1:] + bottom[:1]), backs, rows)
-    heads = [along_y(after(others[2 * s - 2], own), -s) for s in range(1, chips)]
     result = own
-    for piece in heads:
-        result += piece.astype(F32)
     for k in range(1, parts):
         result += along_z(pieces[k - 1], -k).astype(F32)
     return result.astype(BF)

time: 57.5 us -> 57.9 us (level)
  waiting for transfers between devices: 9.98 us -> 12.6 us
  starting transfers between devices: 31.6 us -> 30.1 us
  Pallas kernels: 14.7 us -> 14.1 us
    ppermute x15, waiting for transfers between devices: 6.5 us -> 8.75 us  [along_z(): lax.ppermute(value, 'mp', [(i, (i + step) % parts) for i in range(parts)])]
    ppermute x6 -> x5, starting transfers between devices: 6.46 us -> 5.47 us  [along_y(): lax.ppermute(value, 'y', [(i, (i + step) % chips) for i in range(chips)])]
    pallas_call x1, Pallas kernels: 4.17 us -> 3.51 us  [raw_products(): pl.pallas_call(functools.partial(raw_kernel, len(lines), tile), out_shape...]
    ppermute x6 -> x5, waiting for transfers between devices: 3.22 us -> 3.63 us  [along_y(): lax.ppermute(value, 'y', [(i, (i + step) % chips) for i in range(chips)])]
  transfers between devices with their start and end apart: 27 -> 26, of which waited for: 11 -> 10; matrix products, arithmetic and copies ran while one was open for 0% -> 0% of each run, Pallas kernels for 23% -> 21%
where the time goes in v14:
time: 57.9 us; the launch traced here: 57.8 us
  starting transfers between devices  30.1 us (52%)
  Pallas kernels  14.1 us (24%)
  waiting for transfers between devices  12.6 us (22%)
  other arithmetic  0.71 us (1%)
    ppermute x15, starting transfers between devices, along_z(): lax.ppermute(value, 'mp', [(i, (i + step) % parts) for i in range(parts)])  23.3 us
    ppermute x15, waiting for transfers between devices, along_z(): lax.ppermute(value, 'mp', [(i, (i + step) % parts) for i in range(parts)])  8.75 us
    ppermute x5, starting transfers between devices, along_y(): lax.ppermute(value, 'y', [(i, (i + step) % chips) for i in range(chips)])  5.47 us
    pallas_call x1, Pallas kernels, prepare(): pl.pallas_call(functools.partial(prepare_kernel, parts), in_specs=[vmem]...  4.06 us
    ppermute x5, waiting for transfers between devices, along_y(): lax.ppermute(value, 'y', [(i, (i + step) % chips) for i in range(chips)])  3.63 us
    pallas_call x1, Pallas kernels, raw_products(): pl.pallas_call(functools.partial(raw_kernel, len(lines), tile), out_shape...  3.51 us
    pallas_call x1, Pallas kernels, load(): pl.pallas_call(load_kernel, in_specs=[pl.BlockSpec(memory_space=pltpu.HBM...  2.9 us
    ppermute x6, starting transfers between devices, other_core(): return lax.ppermute(value, 'core', [(0, 1), (1, 0)])  1.24 us
  transfers between devices with their start and end apart: 26, of which 10 were waited for; matrix products, arithmetic and copies ran while one was open for 0% of the time, Pallas kernels for 21%

profile of v14, /device:TPU:0, one launch (start us, length us, event | category | flops | bytes accessed | tf_op | source)
XLA Modules:
  0.0 57.8 jit_solution(15844004336608821776)
XLA Ops:
  0.0 0.9 %attach.1 = bf16[8,4224]{1,0:T(8,128)(2,1)S(1)} custom-call(bf16[8,4096]{1,0:T(8,128)(2,1)} %tokens_ref.1, s32[8,8]{1,0:T(8,128)} %routes_ref.1, f32[8,8]{1,0:T(8,128)} %probs_ref.1), custom_call_target="tpu_custom_call" | custom-call | flops 1 | bytes 1 | tf_op jit(solution)/shard_map/attach/pallas_call | solution.py:62
  1.0 5.1 %collective-permute-start.2 = (bf16[8,4224]{1,0:T(8,128)(2,1)S(1)}, bf16[8,4224]{1,0:T(8,128)(2,1)S(1)}, u32[]{:S(2)}, u32[]{:S(2)}) collective-permute-start(bf16[8,4224]{1,0:T(8,128)(2,1)S(1)} %attach.1), channel_id=1, source_target_pairs={{0,3},{1,0},{2,1},{3,2},{4,7},{5,4},{6,5},{7,6},{8,11},{9,8},{10,9... | collective-permute-start | bytes 202760 | tf_op jit(solution)/shard_map/ppermute | solution.py:413
  6.1 1.0 %collective-permute-start = (bf16[8,4224]{1,0:T(8,128)(2,1)S(1)}, bf16[8,4224]{1,0:T(8,128)(2,1)S(1)}, u32[]{:S(2)}, u32[]{:S(2)}) collective-permute-start(bf16[8,4224]{1,0:T(8,128)(2,1)S(1)} %attach.1), channel_id=1, source_target_pairs={{0,1},{1,2},{2,3},{3,0},{4,5},{5,6},{6,7},{7,4},{8,9},{9,10},{10,1... | collective-permute-start | bytes 202760 | tf_op jit(solution)/shard_map/ppermute | solution.py:413
  7.1 1.5 %collective-permute-start.4 = (bf16[8,4224]{1,0:T(8,128)(2,1)S(1)}, bf16[8,4224]{1,0:T(8,128)(2,1)S(1)}, u32[]{:S(2)}, u32[]{:S(2)}) collective-permute-start(bf16[8,4224]{1,0:T(8,128)(2,1)S(1)} %attach.1), channel_id=1, source_target_pairs={{0,8},{8,0},{1,9},{9,1},{2,10},{10,2},{3,11},{11,3},{4,12},{12,4},... | collective-permute-start | bytes 202760 | tf_op jit(solution)/shard_map/ppermute | solution.py:416
  8.6 4.1 %prepare.1 = (bf16[768,4096]{1,0:T(8,128)(2,1)S(1)}, bf16[256,1024]{1,0:T(8,128)(2,1)S(1)}, bf16[3,32,192]{2,1,0:T(8,128)(2,1)S(1)}, bf16[3,32,192]{2,1,0:T(8,12...) custom-call(bf16[4,8,768]{2,1,0:T(8,128)(2,1)} %refs_0_.1, bf16[4,8,768]{2,1,0:T(8,128)(2,1)} %refs_1_.1, ...), custom_call_target="tpu_custom_call" | custom-call | flops 1 | bytes 1 | tf_op jit(solution)/shard_map/prepare/pallas_call | solution.py:130
  12.8 1.6 %collective-permute-start.5 = (bf16[24,4224]{1,0:T(8,128)(2,1)S(1)}, bf16[24,4224]{1,0:T(8,128)(2,1)S(1)}, u32[]{:S(2)}, u32[]{:S(2)}) collective-permute-start(bf16[24,4224]{1,0:T(8,128)(2,1)S(1)} %pad_maximum_fusion.1), channel_id=1, source_target_pairs={{0,8},{8,0},{1,9},{9,1},{2,10},{10,2},{3,11},{11,3},{4,12},{12,4},... | collective-permute-start | bytes 608264 | tf_op jit(solution)/shard_map/ppermute | solution.py:416
  14.4 1.5 %collective-permute-start.6 = (bf16[3,32,192]{2,1,0:T(8,128)(2,1)S(1)}, bf16[3,32,192]{2,1,0:T(8,128)(2,1)S(1)}, u32[]{:S(2)}, u32[]{:S(2)}) collective-permute-start(bf16[3,32,192]{2,1,0:T(8,128)(2,1)S(1)} %get-tuple-element.59), channel_id=1, source_target_pairs={{0,1},{1,2},{2,3},{3,0},{4,5},{5,6},{6,7},{7,4},{8,9},{9,10},{10,1... | collective-permute-start | bytes 110600 | tf_op jit(solution)/shard_map/ppermute | solution.py:413
  15.9 1.0 %collective-permute-start.7 = (bf16[3,32,192]{2,1,0:T(8,128)(2,1)S(1)}, bf16[3,32,192]{2,1,0:T(8,128)(2,1)S(1)}, u32[]{:S(2)}, u32[]{:S(2)}) collective-permute-start(bf16[3,32,192]{2,1,0:T(8,128)(2,1)S(1)} %get-tuple-element.60), channel_id=1, source_target_pairs={{0,2},{1,3},{2,0},{3,1},{4,6},{5,7},{6,4},{7,5},{8,10},{9,11},{10,... | collective-permute-start | bytes 110600 | tf_op jit(solution)/shard_map/ppermute | solution.py:413
  16.8 2.3 %collective-permute-start.8 = (bf16[3,32,192]{2,1,0:T(8,128)(2,1)S(1)}, bf16[3,32,192]{2,1,0:T(8,128)(2,1)S(1)}, u32[]{:S(2)}, u32[]{:S(2)}) collective-permute-start(bf16[3,32,192]{2,1,0:T(8,128)(2,1)S(1)} %get-tuple-element.61), channel_id=1, source_target_pairs={{0,3},{1,0},{2,1},{3,2},{4,7},{5,4},{6,5},{7,6},{8,11},{9,8},{10,9... | collective-permute-start | bytes 110600 | tf_op jit(solution)/shard_map/ppermute | solution.py:413
  19.1 2.9 %load.1.refs_5_ = bf16[768,4096]{1,0:T(8,128)(2,1)S(1)} custom-call(bf16[768,4096]{1,0:T(8,128)(2,1)} %bitcast.14), custom_call_target="tpu_custom_call" | custom-call | flops 1 | bytes 1 | tf_op jit(solution)/shard_map/load/pallas_call | solution.py:89
  22.7 0.7 %collective-permute-start.14 = (bf16[128,1024]{1,0:T(8,128)(2,1)S(1)}, bf16[128,1024]{1,0:T(8,128)(2,1)S(1)}, u32[]{:S(2)}, u32[]{:S(2)}) collective-permute-start(bf16[128,1024]{1,0:T(8,128)(2,1)S(1)} %bitcast.12), channel_id=1, source_target_pairs={{0,8},{8,0},{1,9},{9,1},{2,10},{10,2},{3,11},{11,3},{4,12},{12,4},... | collective-permute-start | bytes 786440 | tf_op jit(solution)/shard_map/ppermute | solution.py:416
  24.3 1.0 %collective-permute-start.11 = (bf16[128,256]{1,0:T(8,128)(2,1)S(1)}, bf16[128,256]{1,0:T(8,128)(2,1)S(1)}, u32[]{:S(2)}, u32[]{:S(2)}) collective-permute-start(bf16[128,256]{1,0:T(8,128)(2,1)S(1)} %get-tuple-element.69), channel_id=1, source_target_pairs={{0,1},{1,2},{2,3},{3,0},{4,5},{5,6},{6,7},{7,4},{8,9},{9,10},{10,1... | collective-permute-start | bytes 196616 | tf_op jit(solution)/shard_map/ppermute | solution.py:413
  25.3 2.1 %collective-permute-start.12 = (bf16[128,256]{1,0:T(8,128)(2,1)S(1)}, bf16[128,256]{1,0:T(8,128)(2,1)S(1)}, u32[]{:S(2)}, u32[]{:S(2)}) collective-permute-start(bf16[128,256]{1,0:T(8,128)(2,1)S(1)} %get-tuple-element.70), channel_id=1, source_target_pairs={{0,2},{1,3},{2,0},{3,1},{4,6},{5,7},{6,4},{7,5},{8,10},{9,11},{10,... | collective-permute-start | bytes 196616 | tf_op jit(solution)/shard_map/ppermute | solution.py:413
  27.5 1.0 %collective-permute-start.13 = (bf16[128,256]{1,0:T(8,128)(2,1)S(1)}, bf16[128,256]{1,0:T(8,128)(2,1)S(1)}, u32[]{:S(2)}, u32[]{:S(2)}) collective-permute-start(bf16[128,256]{1,0:T(8,128)(2,1)S(1)} %get-tuple-element.71), channel_id=1, source_target_pairs={{0,3},{1,0},{2,1},{3,2},{4,7},{5,4},{6,5},{7,6},{8,11},{9,8},{10,9... | collective-permute-start | bytes 196616 | tf_op jit(solution)/shard_map/ppermute | solution.py:413
  28.5 3.5 %raw.1 = (f32[128,768]{1,0:T(8,128)S(1)}, f32[128,768]{1,0:T(8,128)S(1)}) custom-call(bf16[32,4224]{1,0:T(8,128)(2,1)S(1)} %pad_maximum_fusion.refs_0_, bf16[32,4224]{1,0:T(8,128)(2,1)S(1)} %constant_dynamic-update-slice_fusion.refs_1_, bf16[32,4224]{1,0:T(8,128)(2,1)S(1)} %collective-permute-done.9.refs_2_, ...), custom_call_target="tpu_custom_call" | custom-call | flops 1 | bytes 1 | tf_op jit(solution)/shard_map/raw/pallas_call | solution.py:212
  32.0 1.3 %collective-permute-done.12.refs_6_ = bf16[128,256]{1,0:T(8,128)(2,1)S(1)} collective-permute-done((bf16[128,256]{1,0:T(8,128)(2,1)S(1)}, bf16[128,256]{1,0:T(8,128)(2,1)S(1)}, u32[]{:S(2)}, u32[]{:S(2)}) %collective-permute-start.12) | collective-permute-done | bytes 65568 | tf_op jit(solution)/shard_map/ppermute | solution.py:413
  33.9 1.1 %down.1 = (f32[64,4096]{1,0:T(8,128)S(1)}, bf16[64,4096]{1,0:T(8,128)(2,1)S(1)}) custom-call(bf16[128,768]{1,0:T(8,128)(2,1)S(1)} %get-tuple-element.77.hidden_ref, bf16[768,4096]{1,0:T(8,128)(2,1)S(1)} %bitcast.10), custom_call_target="tpu_custom_call" | custom-call | flops 1 | bytes 1 | tf_op jit(solution)/shard_map/down/pallas_call | solution.py:271
  35.6 0.8 %collective-permute-start.17 = (bf16[32,256]{1,0:T(8,128)(2,1)S(1)}, bf16[32,256]{1,0:T(8,128)(2,1)S(1)}, u32[]{:S(2)}, u32[]{:S(2)}) collective-permute-start(bf16[32,256]{1,0:T(8,128)(2,1)S(1)} %get-tuple-element.83), channel_id=1, source_target_pairs={{0,8},{8,0},{1,9},{9,1},{2,10},{10,2},{3,11},{11,3},{4,12},{12,4},... | collective-permute-start | bytes 49160 | tf_op jit(solution)/shard_map/ppermute | solution.py:416
  36.4 3.0 %collective-permute-done.17.refs_1_ = bf16[32,256]{1,0:T(8,128)(2,1)S(1)} collective-permute-done((bf16[32,256]{1,0:T(8,128)(2,1)S(1)}, bf16[32,256]{1,0:T(8,128)(2,1)S(1)}, u32[]{:S(2)}, u32[]{:S(2)}) %collective-permute-start.17) | collective-permute-done | bytes 16416 | tf_op jit(solution)/shard_map/ppermute | solution.py:416
  39.5 0.8 %collective-permute-start.22 = (bf16[32,4096]{1,0:T(8,128)(2,1)S(1)}, bf16[32,4096]{1,0:T(8,128)(2,1)S(1)}, u32[]{:S(2)}, u32[]{:S(2)}) collective-permute-start(bf16[32,4096]{1,0:T(8,128)(2,1)S(1)} %get-tuple-element.92), channel_id=1, source_target_pairs={{0,8},{8,0},{1,9},{9,1},{2,10},{10,2},{3,11},{11,3},{4,12},{12,4},... | collective-permute-start | bytes 786440 | tf_op jit(solution)/shard_map/ppermute | solution.py:416
  40.4 1.9 %collective-permute-start.19 = (bf16[32,512]{1,0:T(8,128)(2,1)S(1)}, bf16[32,512]{1,0:T(8,128)(2,1)S(1)}, u32[]{:S(2)}, u32[]{:S(2)}) collective-permute-start(bf16[32,512]{1,0:T(8,128)(2,1)S(1)} %get-tuple-element.89), channel_id=1, source_target_pairs={{0,1},{1,2},{2,3},{3,0},{4,5},{5,6},{6,7},{7,4},{8,9},{9,10},{10,1... | collective-permute-start | bytes 98312 | tf_op jit(solution)/shard_map/ppermute | solution.py:413
  42.2 1.2 %collective-permute-start.20 = (bf16[32,512]{1,0:T(8,128)(2,1)S(1)}, bf16[32,512]{1,0:T(8,128)(2,1)S(1)}, u32[]{:S(2)}, u32[]{:S(2)}) collective-permute-start(bf16[32,512]{1,0:T(8,128)(2,1)S(1)} %get-tuple-element.90), channel_id=1, source_target_pairs={{0,2},{1,3},{2,0},{3,1},{4,6},{5,7},{6,4},{7,5},{8,10},{9,11},{10,... | collective-permute-start | bytes 98312 | tf_op jit(solution)/shard_map/ppermute | solution.py:413
  43.5 1.1 %collective-permute-start.21 = (bf16[32,512]{1,0:T(8,128)(2,1)S(1)}, bf16[32,512]{1,0:T(8,128)(2,1)S(1)}, u32[]{:S(2)}, u32[]{:S(2)}) collective-permute-start(bf16[32,512]{1,0:T(8,128)(2,1)S(1)} %get-tuple-element.91), channel_id=1, source_target_pairs={{0,3},{1,0},{2,1},{3,2},{4,7},{5,4},{6,5},{7,6},{8,11},{9,8},{10,9... | collective-permute-start | bytes 98312 | tf_op jit(solution)/shard_map/ppermute | solution.py:413
  44.6 1.6 %collective-permute-done.19.refs_0_ = bf16[32,512]{1,0:T(8,128)(2,1)S(1)} collective-permute-done((bf16[32,512]{1,0:T(8,128)(2,1)S(1)}, bf16[32,512]{1,0:T(8,128)(2,1)S(1)}, u32[]{:S(2)}, u32[]{:S(2)}) %collective-permute-start.19) | collective-permute-done | bytes 32800 | tf_op jit(solution)/shard_map/ppermute | solution.py:413
  46.2 1.2 %collective-permute-done.20.refs_1_ = bf16[32,512]{1,0:T(8,128)(2,1)S(1)} collective-permute-done((bf16[32,512]{1,0:T(8,128)(2,1)S(1)}, bf16[32,512]{1,0:T(8,128)(2,1)S(1)}, u32[]{:S(2)}, u32[]{:S(2)}) %collective-permute-start.20) | collective-permute-done | bytes 32800 | tf_op jit(solution)/shard_map/ppermute | solution.py:413
  47.6 0.7 %collective-permute-done.22.refs_6_ = bf16[32,4096]{1,0:T(8,128)(2,1)S(1)} collective-permute-done((bf16[32,4096]{1,0:T(8,128)(2,1)S(1)}, bf16[32,4096]{1,0:T(8,128)(2,1)S(1)}, u32[]{:S(2)}, u32[]{:S(2)}) %collective-permute-start.22) | collective-permute-done | bytes 262176 | tf_op jit(solution)/shard_map/ppermute | solution.py:416
  48.6 1.7 %collective-permute-start.25 = (bf16[8,4096]{1,0:T(8,128)(2,1)S(1)}, bf16[8,4096]{1,0:T(8,128)(2,1)S(1)}, u32[]{:S(2)}, u32[]{:S(2)}) collective-permute-start(bf16[8,4096]{1,0:T(8,128)(2,1)S(1)} %get-tuple-element.96), channel_id=1, source_target_pairs={{0,1},{1,2},{2,3},{3,0},{4,5},{5,6},{6,7},{7,4},{8,9},{9,10},{10,1... | collective-permute-start | bytes 196616 | tf_op jit(solution)/shard_map/ppermute | solution.py:413
  50.2 1.5 %collective-permute-start.24 = (bf16[8,4096]{1,0:T(8,128)(2,1)S(1)}, bf16[8,4096]{1,0:T(8,128)(2,1)S(1)}, u32[]{:S(2)}, u32[]{:S(2)}) collective-permute-start(bf16[8,4096]{1,0:T(8,128)(2,1)S(1)} %get-tuple-element.95), channel_id=1, source_target_pairs={{0,2},{1,3},{2,0},{3,1},{4,6},{5,7},{6,4},{7,5},{8,10},{9,11},{10,... | collective-permute-start | bytes 196616 | tf_op jit(solution)/shard_map/ppermute | solution.py:413
  51.7 0.9 %collective-permute-start.23 = (bf16[8,4096]{1,0:T(8,128)(2,1)S(1)}, bf16[8,4096]{1,0:T(8,128)(2,1)S(1)}, u32[]{:S(2)}, u32[]{:S(2)}) collective-permute-start(bf16[8,4096]{1,0:T(8,128)(2,1)S(1)} %get-tuple-element.94), channel_id=1, source_target_pairs={{0,3},{1,0},{2,1},{3,2},{4,7},{5,4},{6,5},{7,6},{8,11},{9,8},{10,9... | collective-permute-start | bytes 196616 | tf_op jit(solution)/shard_map/ppermute | solution.py:413
  52.7 2.7 %collective-permute-done.25 = bf16[8,4096]{1,0:T(8,128)(2,1)S(1)} collective-permute-done((bf16[8,4096]{1,0:T(8,128)(2,1)S(1)}, bf16[8,4096]{1,0:T(8,128)(2,1)S(1)}, u32[]{:S(2)}, u32[]{:S(2)}) %collective-permute-start.25) | collective-permute-done | bytes 65568 | tf_op jit(solution)/shard_map/ppermute | solution.py:413
  55.3 1.8 %collective-permute-done.24 = bf16[8,4096]{1,0:T(8,128)(2,1)S(1)} collective-permute-done((bf16[8,4096]{1,0:T(8,128)(2,1)S(1)}, bf16[8,4096]{1,0:T(8,128)(2,1)S(1)}, u32[]{:S(2)}, u32[]{:S(2)}) %collective-permute-start.24) | collective-permute-done | bytes 65568 | tf_op jit(solution)/shard_map/ppermute | solution.py:413
  57.1 0.7 %add_convert_fusion = bf16[8,4096]{1,0:T(8,128)(2,1)} fusion(bf16[8,4096]{1,0:T(8,128)(2,1)S(1)} %collective-permute-done.25, bf16[8,4096]{1,0:T(8,128)(2,1)S(1)} %collective-permute-done.24, f32[8,4096]{1,0:T(8,128)S(1)} %get-tuple-element.93, bf16[8,4096]{1,0:T(8,128)(2,1)S(1)} %collective-permute-done.23), kind=kLoop, calls=%fused_computation.2 | loop fusion | flops 229376 | bytes 393216 | tf_op jit(solution)/shard_map/convert_element_type | solution.py:471
  (45 shorter events, 3.4 us)
Async XLA Ops:
  1.0 11.7 %collective-permute-start.2 = (bf16[8,4224]{1,0:T(8,128)(2,1)S(1)}, bf16[8,4224]{1,0:T(8,128)(2,1)S(1)}, u32[]{:S(2)}, u32[]{:S(2)}) collective-permute-start(bf16[8,4224]{1,0:T(8,128)(2,1)S(1)} %attach.1), channel_id=1, source_target_pairs={{0,3},{1,0},{2,1},{3,2},{4,7},{5,4},{6,5},{7,6},{8,11},{9,8},{10,9... | collective-permute-start | bytes 202760 | tf_op jit(solution)/shard_map/ppermute | solution.py:413
  6.1 6.6 %collective-permute-start.1 = (bf16[8,4224]{1,0:T(8,128)(2,1)S(1)}, bf16[8,4224]{1,0:T(8,128)(2,1)S(1)}, u32[]{:S(2)}, u32[]{:S(2)}) collective-permute-start(bf16[8,4224]{1,0:T(8,128)(2,1)S(1)} %attach.1), channel_id=1, source_target_pairs={{0,2},{1,3},{2,0},{3,1},{4,6},{5,7},{6,4},{7,5},{8,10},{9,11},{10,... | collective-permute-start | bytes 202760 | tf_op jit(solution)/shard_map/ppermute | solution.py:413
  6.1 6.6 %collective-permute-start = (bf16[8,4224]{1,0:T(8,128)(2,1)S(1)}, bf16[8,4224]{1,0:T(8,128)(2,1)S(1)}, u32[]{:S(2)}, u32[]{:S(2)}) collective-permute-start(bf16[8,4224]{1,0:T(8,128)(2,1)S(1)} %attach.1), channel_id=1, source_target_pairs={{0,1},{1,2},{2,3},{3,0},{4,5},{5,6},{6,7},{7,4},{8,9},{9,10},{10,1... | collective-permute-start | bytes 202760 | tf_op jit(solution)/shard_map/ppermute | solution.py:413
  7.1 5.7 %collective-permute-start.4 = (bf16[8,4224]{1,0:T(8,128)(2,1)S(1)}, bf16[8,4224]{1,0:T(8,128)(2,1)S(1)}, u32[]{:S(2)}, u32[]{:S(2)}) collective-permute-start(bf16[8,4224]{1,0:T(8,128)(2,1)S(1)} %attach.1), channel_id=1, source_target_pairs={{0,8},{8,0},{1,9},{9,1},{2,10},{10,2},{3,11},{11,3},{4,12},{12,4},... | collective-permute-start | bytes 202760 | tf_op jit(solution)/shard_map/ppermute | solution.py:416
  8.6 4.2 %collective-permute-start.3 = (bf16[128,1024]{1,0:T(8,128)(2,1)}, bf16[128,1024]{1,0:T(8,128)(2,1)S(1)}, u32[]{:S(2)}, u32[]{:S(2)}) collective-permute-start(bf16[128,1024]{1,0:T(8,128)(2,1)} %bitcast.11), channel_id=1, source_target_pairs={{0,4},{4,0},{1,5},{5,1},{2,6},{6,2},{3,7},{7,3},{8,12},{12,8},{9,1... | collective-permute-start | bytes 786440 | tf_op jit(solution)/shard_map/ppermute | solution.py:419
  12.8 9.3 %collective-permute-start.5 = (bf16[24,4224]{1,0:T(8,128)(2,1)S(1)}, bf16[24,4224]{1,0:T(8,128)(2,1)S(1)}, u32[]{:S(2)}, u32[]{:S(2)}) collective-permute-start(bf16[24,4224]{1,0:T(8,128)(2,1)S(1)} %pad_maximum_fusion.1), channel_id=1, source_target_pairs={{0,8},{8,0},{1,9},{9,1},{2,10},{10,2},{3,11},{11,3},{4,12},{12,4},... | collective-permute-start | bytes 608264 | tf_op jit(solution)/shard_map/ppermute | solution.py:416
  14.4 7.8 %collective-permute-start.6 = (bf16[3,32,192]{2,1,0:T(8,128)(2,1)S(1)}, bf16[3,32,192]{2,1,0:T(8,128)(2,1)S(1)}, u32[]{:S(2)}, u32[]{:S(2)}) collective-permute-start(bf16[3,32,192]{2,1,0:T(8,128)(2,1)S(1)} %get-tuple-element.59), channel_id=1, source_target_pairs={{0,1},{1,2},{2,3},{3,0},{4,5},{5,6},{6,7},{7,4},{8,9},{9,10},{10,1... | collective-permute-start | bytes 110600 | tf_op jit(solution)/shard_map/ppermute | solution.py:413
  15.9 6.3 %collective-permute-start.7 = (bf16[3,32,192]{2,1,0:T(8,128)(2,1)S(1)}, bf16[3,32,192]{2,1,0:T(8,128)(2,1)S(1)}, u32[]{:S(2)}, u32[]{:S(2)}) collective-permute-start(bf16[3,32,192]{2,1,0:T(8,128)(2,1)S(1)} %get-tuple-element.60), channel_id=1, source_target_pairs={{0,2},{1,3},{2,0},{3,1},{4,6},{5,7},{6,4},{7,5},{8,10},{9,11},{10,... | collective-permute-start | bytes 110600 | tf_op jit(solution)/shard_map/ppermute | solution.py:413
  16.8 5.3 %collective-permute-start.8 = (bf16[3,32,192]{2,1,0:T(8,128)(2,1)S(1)}, bf16[3,32,192]{2,1,0:T(8,128)(2,1)S(1)}, u32[]{:S(2)}, u32[]{:S(2)}) collective-permute-start(bf16[3,32,192]{2,1,0:T(8,128)(2,1)S(1)} %get-tuple-element.61), channel_id=1, source_target_pairs={{0,3},{1,0},{2,1},{3,2},{4,7},{5,4},{6,5},{7,6},{8,11},{9,8},{10,9... | collective-permute-start | bytes 110600 | tf_op jit(solution)/shard_map/ppermute | solution.py:413
  19.1 3.6 %copy-start = (bf16[4,32,1024]{2,1,0:T(8,128)(2,1)S(1)}, bf16[4,32,1024]{2,1,0:T(8,128)(2,1)}, u32[]{:S(2)}) copy-start(bf16[4,32,1024]{2,1,0:T(8,128)(2,1)} %param.23) | copy-start | bytes 786436
  22.0 1.8 %collective-permute-start.9 = (bf16[32,4224]{1,0:T(8,128)(2,1)S(1)}, bf16[32,4224]{1,0:T(8,128)(2,1)S(1)}, u32[]{:S(2)}, u32[]{:S(2)}) collective-permute-start(bf16[32,4224]{1,0:T(8,128)(2,1)S(1)} %pad_maximum_fusion.refs_0_), channel_id=1, source_target_pairs={{0,4},{4,0},{1,5},{5,1},{2,6},{6,2},{3,7},{7,3},{8,12},{12,8},{9,1... | collective-permute-start | bytes 811016 | tf_op jit(solution)/shard_map/ppermute | solution.py:419
  22.2 1.9 %collective-permute-start.10 = (bf16[32,4224]{1,0:T(8,128)(2,1)S(1)}, bf16[32,4224]{1,0:T(8,128)(2,1)S(1)}, u32[]{:S(2)}, u32[]{:S(2)}) collective-permute-start(bf16[32,4224]{1,0:T(8,128)(2,1)S(1)} %constant_dynamic-update-slice_fusion.refs_1_), channel_id=1, source_target_pairs={{0,4},{4,0},{1,5},{5,1},{2,6},{6,2},{3,7},{7,3},{8,12},{12,8},{9,1... | collective-permute-start | bytes 811016 | tf_op jit(solution)/shard_map/ppermute | solution.py:419
  22.7 9.3 %collective-permute-start.14 = (bf16[128,1024]{1,0:T(8,128)(2,1)S(1)}, bf16[128,1024]{1,0:T(8,128)(2,1)S(1)}, u32[]{:S(2)}, u32[]{:S(2)}) collective-permute-start(bf16[128,1024]{1,0:T(8,128)(2,1)S(1)} %bitcast.12), channel_id=1, source_target_pairs={{0,8},{8,0},{1,9},{9,1},{2,10},{10,2},{3,11},{11,3},{4,12},{12,4},... | collective-permute-start | bytes 786440 | tf_op jit(solution)/shard_map/ppermute | solution.py:416
  24.3 7.7 %collective-permute-start.11 = (bf16[128,256]{1,0:T(8,128)(2,1)S(1)}, bf16[128,256]{1,0:T(8,128)(2,1)S(1)}, u32[]{:S(2)}, u32[]{:S(2)}) collective-permute-start(bf16[128,256]{1,0:T(8,128)(2,1)S(1)} %get-tuple-element.69), channel_id=1, source_target_pairs={{0,1},{1,2},{2,3},{3,0},{4,5},{5,6},{6,7},{7,4},{8,9},{9,10},{10,1... | collective-permute-start | bytes 196616 | tf_op jit(solution)/shard_map/ppermute | solution.py:413
  25.3 8.0 %collective-permute-start.12 = (bf16[128,256]{1,0:T(8,128)(2,1)S(1)}, bf16[128,256]{1,0:T(8,128)(2,1)S(1)}, u32[]{:S(2)}, u32[]{:S(2)}) collective-permute-start(bf16[128,256]{1,0:T(8,128)(2,1)S(1)} %get-tuple-element.70), channel_id=1, source_target_pairs={{0,2},{1,3},{2,0},{3,1},{4,6},{5,7},{6,4},{7,5},{8,10},{9,11},{10,... | collective-permute-start | bytes 196616 | tf_op jit(solution)/shard_map/ppermute | solution.py:413
  27.5 6.5 %slice-start = ((s8[6291456]{0:T(1024)(128)(4,1)}), s8[4194304]{0:T(1024)(128)(4,1)S(1)}, s32[]{:S(2)}) async-start(s8[6291456]{0:T(1024)(128)(4,1)} %bitcast.8), calls=%async_computation | async-start | bytes 8388608
  27.5 6.5 %slice-start.1 = ((s8[6291456]{0:T(1024)(128)(4,1)}), s8[2097152]{0:T(1024)(128)(4,1)S(1)}, s32[]{:S(2)}) async-start(s8[6291456]{0:T(1024)(128)(4,1)} %bitcast.8), calls=%async_computation.1 | async-start | bytes 4194304
  27.5 5.8 %collective-permute-start.13 = (bf16[128,256]{1,0:T(8,128)(2,1)S(1)}, bf16[128,256]{1,0:T(8,128)(2,1)S(1)}, u32[]{:S(2)}, u32[]{:S(2)}) collective-permute-start(bf16[128,256]{1,0:T(8,128)(2,1)S(1)} %get-tuple-element.71), channel_id=1, source_target_pairs={{0,3},{1,0},{2,1},{3,2},{4,7},{5,4},{6,5},{7,6},{8,11},{9,8},{10,9... | collective-permute-start | bytes 196616 | tf_op jit(solution)/shard_map/ppermute | solution.py:413
  33.8 1.2 %collective-permute-start.15 = (bf16[64,128]{1,0:T(8,128)(2,1)S(1)}, bf16[64,128]{1,0:T(8,128)(2,1)S(1)}, u32[]{:S(2)}, u32[]{:S(2)}) collective-permute-start(bf16[64,128]{1,0:T(8,128)(2,1)S(1)} %get-tuple-element.80), channel_id=1, source_target_pairs={{0,4},{4,0},{1,5},{5,1},{2,6},{6,2},{3,7},{7,3},{8,12},{12,8},{9,1... | collective-permute-start | bytes 49160 | tf_op jit(solution)/shard_map/ppermute | solution.py:419
  35.1 4.3 %collective-permute-start.16 = (bf16[64,4096]{1,0:T(8,128)(2,1)S(1)}, bf16[64,4096]{1,0:T(8,128)(2,1)S(1)}, u32[]{:S(2)}, u32[]{:S(2)}) collective-permute-start(bf16[64,4096]{1,0:T(8,128)(2,1)S(1)} %get-tuple-element.81), channel_id=1, source_target_pairs={{0,4},{4,0},{1,5},{5,1},{2,6},{6,2},{3,7},{7,3},{8,12},{12,8},{9,1... | collective-permute-start | bytes 1572872 | tf_op jit(solution)/shard_map/ppermute | solution.py:419
  35.6 3.7 %collective-permute-start.17 = (bf16[32,256]{1,0:T(8,128)(2,1)S(1)}, bf16[32,256]{1,0:T(8,128)(2,1)S(1)}, u32[]{:S(2)}, u32[]{:S(2)}) collective-permute-start(bf16[32,256]{1,0:T(8,128)(2,1)S(1)} %get-tuple-element.83), channel_id=1, source_target_pairs={{0,8},{8,0},{1,9},{9,1},{2,10},{10,2},{3,11},{11,3},{4,12},{12,4},... | collective-permute-start | bytes 49160 | tf_op jit(solution)/shard_map/ppermute | solution.py:416
  39.3 8.3 %collective-permute-start.18 = (bf16[128,1024]{1,0:T(8,128)(2,1)S(1)}, bf16[128,1024]{1,0:T(8,128)(2,1)S(1)}, u32[]{:S(2)}, u32[]{:S(2)}) collective-permute-start(bf16[128,1024]{1,0:T(8,128)(2,1)S(1)} %collective-permute-done.14.refs_2_), channel_id=1, source_target_pairs={{0,4},{4,0},{1,5},{5,1},{2,6},{6,2},{3,7},{7,3},{8,12},{12,8},{9,1... | collective-permute-start | bytes 786440 | tf_op jit(solution)/shard_map/ppermute | solution.py:419
  39.5 8.8 %collective-permute-start.22 = (bf16[32,4096]{1,0:T(8,128)(2,1)S(1)}, bf16[32,4096]{1,0:T(8,128)(2,1)S(1)}, u32[]{:S(2)}, u32[]{:S(2)}) collective-permute-start(bf16[32,4096]{1,0:T(8,128)(2,1)S(1)} %get-tuple-element.92), channel_id=1, source_target_pairs={{0,8},{8,0},{1,9},{9,1},{2,10},{10,2},{3,11},{11,3},{4,12},{12,4},... | collective-permute-start | bytes 786440 | tf_op jit(solution)/shard_map/ppermute | solution.py:416
  40.4 5.9 %collective-permute-start.19 = (bf16[32,512]{1,0:T(8,128)(2,1)S(1)}, bf16[32,512]{1,0:T(8,128)(2,1)S(1)}, u32[]{:S(2)}, u32[]{:S(2)}) collective-permute-start(bf16[32,512]{1,0:T(8,128)(2,1)S(1)} %get-tuple-element.89), channel_id=1, source_target_pairs={{0,1},{1,2},{2,3},{3,0},{4,5},{5,6},{6,7},{7,4},{8,9},{9,10},{10,1... | collective-permute-start | bytes 98312 | tf_op jit(solution)/shard_map/ppermute | solution.py:413
  42.2 5.2 %collective-permute-start.20 = (bf16[32,512]{1,0:T(8,128)(2,1)S(1)}, bf16[32,512]{1,0:T(8,128)(2,1)S(1)}, u32[]{:S(2)}, u32[]{:S(2)}) collective-permute-start(bf16[32,512]{1,0:T(8,128)(2,1)S(1)} %get-tuple-element.90), channel_id=1, source_target_pairs={{0,2},{1,3},{2,0},{3,1},{4,6},{5,7},{6,4},{7,5},{8,10},{9,11},{10,... | collective-permute-start | bytes 98312 | tf_op jit(solution)/shard_map/ppermute | solution.py:413
  43.5 4.1 %collective-permute-start.21 = (bf16[32,512]{1,0:T(8,128)(2,1)S(1)}, bf16[32,512]{1,0:T(8,128)(2,1)S(1)}, u32[]{:S(2)}, u32[]{:S(2)}) collective-permute-start(bf16[32,512]{1,0:T(8,128)(2,1)S(1)} %get-tuple-element.91), channel_id=1, source_target_pairs={{0,3},{1,0},{2,1},{3,2},{4,7},{5,4},{6,5},{7,6},{8,11},{9,8},{10,9... | collective-permute-start | bytes 98312 | tf_op jit(solution)/shard_map/ppermute | solution.py:413
  48.6 6.8 %collective-permute-start.25 = (bf16[8,4096]{1,0:T(8,128)(2,1)S(1)}, bf16[8,4096]{1,0:T(8,128)(2,1)S(1)}, u32[]{:S(2)}, u32[]{:S(2)}) collective-permute-start(bf16[8,4096]{1,0:T(8,128)(2,1)S(1)} %get-tuple-element.96), channel_id=1, source_target_pairs={{0,1},{1,2},{2,3},{3,0},{4,5},{5,6},{6,7},{7,4},{8,9},{9,10},{10,1... | collective-permute-start | bytes 196616 | tf_op jit(solution)/shard_map/ppermute | solution.py:413
  50.2 6.9 %collective-permute-start.24 = (bf16[8,4096]{1,0:T(8,128)(2,1)S(1)}, bf16[8,4096]{1,0:T(8,128)(2,1)S(1)}, u32[]{:S(2)}, u32[]{:S(2)}) collective-permute-start(bf16[8,4096]{1,0:T(8,128)(2,1)S(1)} %get-tuple-element.95), channel_id=1, source_target_pairs={{0,2},{1,3},{2,0},{3,1},{4,6},{5,7},{6,4},{7,5},{8,10},{9,11},{10,... | collective-permute-start | bytes 196616 | tf_op jit(solution)/shard_map/ppermute | solution.py:413
  51.7 5.4 %collective-permute-start.23 = (bf16[8,4096]{1,0:T(8,128)(2,1)S(1)}, bf16[8,4096]{1,0:T(8,128)(2,1)S(1)}, u32[]{:S(2)}, u32[]{:S(2)}) collective-permute-start(bf16[8,4096]{1,0:T(8,128)(2,1)S(1)} %get-tuple-element.94), channel_id=1, source_target_pairs={{0,3},{1,0},{2,1},{3,2},{4,7},{5,4},{6,5},{7,6},{8,11},{9,8},{10,9... | collective-permute-start | bytes 196616 | tf_op jit(solution)/shard_map/ppermute | solution.py:413

commit v15 on v14

--- a/solution.py
+++ b/solution.py
@@ -12,6 +12,8 @@
 SMALL_LIMIT = 4 * 1024 * 1024
 VMEM_LIMIT = 12 * 1024 * 1024
 PIECES = 8
+LONG = pl.CostEstimate(flops=1_000_000_000, bytes_accessed=1, transcendentals=0)
+LONGER = pl.CostEstimate(flops=10_000_000_000, bytes_accessed=1, transcendentals=0)
 BRIEF = pl.CostEstimate(flops=1, bytes_accessed=1, transcendentals=0)
 
 
@@ -220,7 +222,8 @@
 
 def hidden_kernel(parts, count, exp_dev, pair, *refs):
     lines, inner, rest = refs[:count], refs[count : count + parts], refs[count + parts :]
-    gate_ref, up_ref, diag_ref, hidden_ref, near_ref, far_ref = rest
+    gate_ref, up_ref, diag_ref, hidden_ref = rest[:4]
+    outs = rest[4:]
     hid = gate_ref.shape[1]
     ranks = diag_ref.shape[1]
     wide = lines[0].shape[1] - pair
@@ -237,18 +240,20 @@
     hidden = (gate / (1.0 + jnp.exp(-gate)) * up * scale).astype(BF)
     hidden_ref[...] = hidden
     value = dot_nt(hidden, diag_ref[2])
-    near = near_ref.shape[0]
-    near_ref[...] = value[:near].astype(BF)
-    far_ref[...] = value[near:].astype(BF)
-
-
-def hidden_units(lines, inner, raw, diag, parts, exp_dev, pair):
+    chips = len(outs)
+    span = value.shape[0] // (2 * chips)
+    for n, out_ref in enumerate(outs):
+        rows = [value[i * span : (i + 1) * span] for i in (n, n + chips)]
+        out_ref[...] = jnp.concatenate(rows).astype(BF)
+
+
+def hidden_units(lines, inner, raw, diag, parts, exp_dev, pair, chips):
     total, hid = raw[0].shape
     ranks = diag.shape[1]
     return pl.pallas_call(
         functools.partial(hidden_kernel, parts, len(lines), exp_dev, pair),
         out_shape=[jax.ShapeDtypeStruct((total, hid), BF)]
-        + [jax.ShapeDtypeStruct((total // 2, ranks), BF)] * 2,
+        + [jax.ShapeDtypeStruct((total // chips, ranks), BF)] * chips,
         compiler_params=pltpu.CompilerParams(vmem_limit_bytes=VMEM_LIMIT),
         cost_estimate=BRIEF,
         name="hidden",
@@ -280,40 +285,40 @@
     )(hidden, down_w)
 
 
-def pair_kernel(near_ref, far_ref, *out_refs):
+def pair_kernel(*refs):
+    ins, (near_ref, far_ref) = refs[:-2], refs[-2:]
+    value = jnp.concatenate([ref[...].astype(F32) for ref in ins], axis=1)
+    span = near_ref.shape[0]
+    near_ref[...] = value[:span].astype(BF)
+    far_ref[...] = value[span:].astype(BF)
+
+
+def side_by_side(lines):
+    total, ranks = lines[0].shape
+    return pl.pallas_call(
+        pair_kernel,
+        out_shape=[jax.ShapeDtypeStruct((total // 2, len(lines) * ranks), BF)] * 2,
+        compiler_params=pltpu.CompilerParams(vmem_limit_bytes=SMALL_LIMIT),
+        cost_estimate=LONGER,
+        name="pair",
+    )(*lines)
+
+
+def turn_kernel(rows, near_ref, far_ref, *outs):
     value = jnp.concatenate([near_ref[...].astype(F32), far_ref[...].astype(F32)], axis=1)
-    span = out_refs[0].shape[0]
-    for n, out_ref in enumerate(out_refs):
-        out_ref[...] = value[n * span : (n + 1) * span].astype(BF)
-
-
-def side_by_side(near, far, chips):
-    total, ranks = near.shape
-    return pl.pallas_call(
-        pair_kernel,
-        out_shape=[jax.ShapeDtypeStruct((total // chips, 2 * ranks), BF)] * chips,
-        compiler_params=pltpu.CompilerParams(vmem_limit_bytes=SMALL_LIMIT),
-        cost_estimate=BRIEF,
-        name="pair",
-    )(near, far)
-
-
-def turn_kernel(rows, chips, *refs):
-    ins, outs = refs[:chips], refs[chips:]
-    value = jnp.concatenate([ref[...].astype(F32) for ref in ins], axis=1)
     for k, out_ref in enumerate(outs):
         out_ref[...] = rotated(value, rows, len(outs), k).astype(BF)
 
 
-def turn(lines, parts, rows):
-    span, ranks = lines[0].shape
-    return pl.pallas_call(
-        functools.partial(turn_kernel, rows, len(lines)),
-        out_shape=[jax.ShapeDtypeStruct((span, len(lines) * ranks), BF)] * parts,
+def turn(near, far, parts, rows):
+    span, ranks = near.shape
+    return pl.pallas_call(
+        functools.partial(turn_kernel, rows),
+        out_shape=[jax.ShapeDtypeStruct((span, 2 * ranks), BF)] * parts,
         compiler_params=pltpu.CompilerParams(vmem_limit_bytes=SMALL_LIMIT),
         cost_estimate=BRIEF,
         name="turn",
-    )(*lines)
+    )(near, far)
 
 
 def add_up_kernel(*refs):
@@ -325,26 +330,29 @@
         add_up_kernel,
         out_shape=jax.ShapeDtypeStruct(pieces[0].shape, BF),
         compiler_params=pltpu.CompilerParams(vmem_limit_bytes=SMALL_LIMIT),
-        cost_estimate=BRIEF,
+        cost_estimate=LONG,
         name="add_up",
     )(*pieces)
 
 
-def fold_kernel(near_ref, far_ref, own_ref, *out_refs):
+def fold_kernel(head, near_ref, far_ref, own_ref, *out_refs):
     span = own_ref.shape[0]
     total = near_ref[...] + far_ref[...].astype(F32)
     own_ref[...] = total[:span]
-    for n, out_ref in enumerate(out_refs):
-        out_ref[...] = total[(n + 1) * span : (n + 2) * span].astype(BF)
-
-
-def fold(near, far, chips):
+    for n in range(len(out_refs) // 2):
+        line = total[(n + 1) * span : (n + 2) * span]
+        out_refs[2 * n][...] = line[:head].astype(BF)
+        out_refs[2 * n + 1][...] = line[head:].astype(BF)
+
+
+def fold(near, far, chips, head):
     total, width = near.shape
     span = total // chips
     return pl.pallas_call(
-        fold_kernel,
+        functools.partial(fold_kernel, head),
         out_shape=[jax.ShapeDtypeStruct((span, width), F32)]
-        + [jax.ShapeDtypeStruct((span, width), BF)] * (chips - 1),
+        + [jax.ShapeDtypeStruct((rows, width), BF) for rows in (head, span - head)]
+        * (chips - 1),
         compiler_params=pltpu.CompilerParams(vmem_limit_bytes=VMEM_LIMIT),
         cost_estimate=BRIEF,
         name="fold",
@@ -359,13 +367,14 @@
     offset = pl.multiple_of(lax.axis_index("mp") * block, 128)
     value = jnp.zeros((low.shape[0], block), F32)
     for n, ref in enumerate(rights):
-        at = (2 * n if n < chips else 2 * (n - chips) + 1) * ranks
-        value += dot_nn(low[:, at : at + ranks], ref[...])
+        value += dot_nn(low[:, n * ranks : (n + 1) * ranks], ref[...])
     total = own_ref[...]
     value += own_ref[:, pl.ds(offset, block)]
-    for ref in backs:
-        total += ref[...].astype(F32)
-        value += ref[:, pl.ds(offset, block)].astype(F32)
+    for n in range(0, len(backs), 2):
+        total += jnp.concatenate([ref[...].astype(F32) for ref in backs[n : n + 2]])
+        value += jnp.concatenate(
+            [ref[:, pl.ds(offset, block)].astype(F32) for ref in backs[n : n + 2]]
+        )
     for k, out_ref in enumerate(outs):
         span = slice(k * rows, (k + 1) * rows)
         out_ref[...] = total[span].astype(out_ref.dtype)
@@ -376,7 +385,7 @@
     total, width = own.shape
     parts = total // rows
     return pl.pallas_call(
-        functools.partial(merge_kernel, len(backs) + 1, parts),
+        functools.partial(merge_kernel, len(rights) // 2, parts),
         out_shape=[jax.ShapeDtypeStruct((rows, width), F32)]
         + [jax.ShapeDtypeStruct((rows, width), BF)] * (parts - 1),
         compiler_params=pltpu.CompilerParams(vmem_limit_bytes=VMEM_LIMIT),
@@ -450,19 +459,17 @@
     right = after(right, arrival)
     rights = [right] + [along_y(right, -s) for s in range(1, chips)]
     raw = after(tuple(raw), rights[1:])
-    hidden, near, far = hidden_units(
-        lines, inner, raw, diag, parts, exp_dev, pair
+    hidden, low, *lows = hidden_units(
+        lines, inner, raw, diag, parts, exp_dev, pair, chips
     )
-    swapped = other_core(far)
-    low, *lows = side_by_side(near, swapped, chips)
     lows = [along_y(lows[s - 1], -s) for s in range(1, chips)]
-    bottom = turn([low] + lows, parts, rows)
+    near, far = side_by_side([low] + lows)
+    bottom = turn(near, other_core(far), parts, rows)
     bottom = [bottom[0]] + [along_z(bottom[k], k) for k in range(1, parts)]
 
     near, far = down_products(hidden, w_down.reshape(hid, width))
-    far = after(other_core(after(far, swapped)), lows)
-    out, *others = fold(near, far, chips)
-    backs = [along_y(others[s - 1], -s) for s in range(1, chips)]
+    out, *others = fold(near, other_core(far), chips, rows)
+    backs = [along_y(others[n], -(n // 2 + 1)) for n in range(2 * chips - 2)]
     rights += [partner_right] + [other_core(after(right, bottom[0])) for right in rights[1:]]
     own, *pieces = merge(out, rights, add_up(bottom[1:] + bottom[:1]), backs, rows)
     result = own

time: 57.9 us -> 58.1 us (level)
  starting transfers between devices: 30.1 us -> 30.8 us
    ppermute x15, waiting for transfers between devices: 8.75 us -> 6.14 us  [along_z(): lax.ppermute(value, 'mp', [(i, (i + step) % parts) for i in range(parts)])]
    ppermute x5 -> x6, starting transfers between devices: 5.47 us -> 6.73 us  [along_y(): lax.ppermute(value, 'y', [(i, (i + step) % chips) for i in range(chips)])]
    ppermute x6, waiting for transfers between devices: 0.26 us -> 1.36 us  [other_core(): return lax.ppermute(value, 'core', [(0, 1), (1, 0)])]
    ppermute x5 -> x6, waiting for transfers between devices: 3.63 us -> 4.64 us  [along_y(): lax.ppermute(value, 'y', [(i, (i + step) % chips) for i in range(chips)])]
  transfers between devices with their start and end apart: 26 -> 27, of which waited for: 10 -> 9; matrix products, arithmetic and copies ran while one was open for 0% -> 0% of each run, Pallas kernels for 21% -> 21%
where the time goes in v15:
time: 58.1 us; the launch traced here: 57.9 us
  starting transfers between devices  30.8 us (53%)
  Pallas kernels  14.1 us (24%)
  waiting for transfers between devices  12.1 us (21%)
  other arithmetic  0.7 us (1%)
    ppermute x15, starting transfers between devices, along_z(): lax.ppermute(value, 'mp', [(i, (i + step) % parts) for i in range(parts)])  23.1 us
    ppermute x6, starting transfers between devices, along_y(): lax.ppermute(value, 'y', [(i, (i + step) % chips) for i in range(chips)])  6.73 us
    ppermute x15, waiting for transfers between devices, along_z(): lax.ppermute(value, 'mp', [(i, (i + step) % parts) for i in range(parts)])  6.14 us
    ppermute x6, waiting for transfers between devices, along_y(): lax.ppermute(value, 'y', [(i, (i + step) % chips) for i in range(chips)])  4.64 us
    pallas_call x1, Pallas kernels, prepare(): pl.pallas_call(functools.partial(prepare_kernel, parts), in_specs=[vmem]...  4.06 us
    pallas_call x1, Pallas kernels, raw_products(): pl.pallas_call(functools.partial(raw_kernel, len(lines), tile), out_shape...  3.51 us
    pallas_call x1, Pallas kernels, load(): pl.pallas_call(load_kernel, in_specs=[pl.BlockSpec(memory_space=pltpu.HBM...  2.9 us
    ppermute x6, waiting for transfers between devices, other_core(): return lax.ppermute(value, 'core', [(0, 1), (1, 0)])  1.36 us
  transfers between devices with their start and end apart: 27, of which 9 were waited for; matrix products, arithmetic and copies ran while one was open for 0% of the time, Pallas kernels for 21%

profile of v15, /device:TPU:0, one launch (start us, length us, event | category | flops | bytes accessed | tf_op | source)
XLA Modules:
  0.0 57.9 jit_solution(11009753623306238283)
XLA Ops:
  0.0 0.9 %attach.1 = bf16[8,4224]{1,0:T(8,128)(2,1)S(1)} custom-call(bf16[8,4096]{1,0:T(8,128)(2,1)} %tokens_ref.1, s32[8,8]{1,0:T(8,128)} %routes_ref.1, f32[8,8]{1,0:T(8,128)} %probs_ref.1), custom_call_target="tpu_custom_call" | custom-call | flops 1 | bytes 1 | tf_op jit(solution)/shard_map/attach/pallas_call | solution.py:64
  1.0 5.1 %collective-permute-start.2 = (bf16[8,4224]{1,0:T(8,128)(2,1)S(1)}, bf16[8,4224]{1,0:T(8,128)(2,1)S(1)}, u32[]{:S(2)}, u32[]{:S(2)}) collective-permute-start(bf16[8,4224]{1,0:T(8,128)(2,1)S(1)} %attach.1), channel_id=1, source_target_pairs={{0,3},{1,0},{2,1},{3,2},{4,7},{5,4},{6,5},{7,6},{8,11},{9,8},{10,9... | collective-permute-start | bytes 202760 | tf_op jit(solution)/shard_map/ppermute | solution.py:422
  6.1 1.0 %collective-permute-start = (bf16[8,4224]{1,0:T(8,128)(2,1)S(1)}, bf16[8,4224]{1,0:T(8,128)(2,1)S(1)}, u32[]{:S(2)}, u32[]{:S(2)}) collective-permute-start(bf16[8,4224]{1,0:T(8,128)(2,1)S(1)} %attach.1), channel_id=1, source_target_pairs={{0,1},{1,2},{2,3},{3,0},{4,5},{5,6},{6,7},{7,4},{8,9},{9,10},{10,1... | collective-permute-start | bytes 202760 | tf_op jit(solution)/shard_map/ppermute | solution.py:422
  7.1 1.5 %collective-permute-start.4 = (bf16[8,4224]{1,0:T(8,128)(2,1)S(1)}, bf16[8,4224]{1,0:T(8,128)(2,1)S(1)}, u32[]{:S(2)}, u32[]{:S(2)}) collective-permute-start(bf16[8,4224]{1,0:T(8,128)(2,1)S(1)} %attach.1), channel_id=1, source_target_pairs={{0,8},{8,0},{1,9},{9,1},{2,10},{10,2},{3,11},{11,3},{4,12},{12,4},... | collective-permute-start | bytes 202760 | tf_op jit(solution)/shard_map/ppermute | solution.py:425
  8.6 4.1 %prepare.1 = (bf16[768,4096]{1,0:T(8,128)(2,1)S(1)}, bf16[256,1024]{1,0:T(8,128)(2,1)S(1)}, bf16[3,32,192]{2,1,0:T(8,128)(2,1)S(1)}, bf16[3,32,192]{2,1,0:T(8,12...) custom-call(bf16[4,8,768]{2,1,0:T(8,128)(2,1)} %refs_0_.1, bf16[4,8,768]{2,1,0:T(8,128)(2,1)} %refs_1_.1, ...), custom_call_target="tpu_custom_call" | custom-call | flops 1 | bytes 1 | tf_op jit(solution)/shard_map/prepare/pallas_call | solution.py:132
  12.8 1.6 %collective-permute-start.5 = (bf16[24,4224]{1,0:T(8,128)(2,1)S(1)}, bf16[24,4224]{1,0:T(8,128)(2,1)S(1)}, u32[]{:S(2)}, u32[]{:S(2)}) collective-permute-start(bf16[24,4224]{1,0:T(8,128)(2,1)S(1)} %pad_maximum_fusion.1), channel_id=1, source_target_pairs={{0,8},{8,0},{1,9},{9,1},{2,10},{10,2},{3,11},{11,3},{4,12},{12,4},... | collective-permute-start | bytes 608264 | tf_op jit(solution)/shard_map/ppermute | solution.py:425
  14.4 1.5 %collective-permute-start.6 = (bf16[3,32,192]{2,1,0:T(8,128)(2,1)S(1)}, bf16[3,32,192]{2,1,0:T(8,128)(2,1)S(1)}, u32[]{:S(2)}, u32[]{:S(2)}) collective-permute-start(bf16[3,32,192]{2,1,0:T(8,128)(2,1)S(1)} %get-tuple-element.58), channel_id=1, source_target_pairs={{0,1},{1,2},{2,3},{3,0},{4,5},{5,6},{6,7},{7,4},{8,9},{9,10},{10,1... | collective-permute-start | bytes 110600 | tf_op jit(solution)/shard_map/ppermute | solution.py:422
  15.9 1.0 %collective-permute-start.7 = (bf16[3,32,192]{2,1,0:T(8,128)(2,1)S(1)}, bf16[3,32,192]{2,1,0:T(8,128)(2,1)S(1)}, u32[]{:S(2)}, u32[]{:S(2)}) collective-permute-start(bf16[3,32,192]{2,1,0:T(8,128)(2,1)S(1)} %get-tuple-element.59), channel_id=1, source_target_pairs={{0,2},{1,3},{2,0},{3,1},{4,6},{5,7},{6,4},{7,5},{8,10},{9,11},{10,... | collective-permute-start | bytes 110600 | tf_op jit(solution)/shard_map/ppermute | solution.py:422
  16.8 2.3 %collective-permute-start.8 = (bf16[3,32,192]{2,1,0:T(8,128)(2,1)S(1)}, bf16[3,32,192]{2,1,0:T(8,128)(2,1)S(1)}, u32[]{:S(2)}, u32[]{:S(2)}) collective-permute-start(bf16[3,32,192]{2,1,0:T(8,128)(2,1)S(1)} %get-tuple-element.60), channel_id=1, source_target_pairs={{0,3},{1,0},{2,1},{3,2},{4,7},{5,4},{6,5},{7,6},{8,11},{9,8},{10,9... | collective-permute-start | bytes 110600 | tf_op jit(solution)/shard_map/ppermute | solution.py:422
  19.1 2.9 %load.1.refs_5_ = bf16[768,4096]{1,0:T(8,128)(2,1)S(1)} custom-call(bf16[768,4096]{1,0:T(8,128)(2,1)} %bitcast.14), custom_call_target="tpu_custom_call" | custom-call | flops 1 | bytes 1 | tf_op jit(solution)/shard_map/load/pallas_call | solution.py:91
  22.7 0.7 %collective-permute-start.14 = (bf16[128,1024]{1,0:T(8,128)(2,1)S(1)}, bf16[128,1024]{1,0:T(8,128)(2,1)S(1)}, u32[]{:S(2)}, u32[]{:S(2)}) collective-permute-start(bf16[128,1024]{1,0:T(8,128)(2,1)S(1)} %bitcast.12), channel_id=1, source_target_pairs={{0,8},{8,0},{1,9},{9,1},{2,10},{10,2},{3,11},{11,3},{4,12},{12,4},... | collective-permute-start | bytes 786440 | tf_op jit(solution)/shard_map/ppermute | solution.py:425
  24.3 1.0 %collective-permute-start.11 = (bf16[128,256]{1,0:T(8,128)(2,1)S(1)}, bf16[128,256]{1,0:T(8,128)(2,1)S(1)}, u32[]{:S(2)}, u32[]{:S(2)}) collective-permute-start(bf16[128,256]{1,0:T(8,128)(2,1)S(1)} %get-tuple-element.68), channel_id=1, source_target_pairs={{0,1},{1,2},{2,3},{3,0},{4,5},{5,6},{6,7},{7,4},{8,9},{9,10},{10,1... | collective-permute-start | bytes 196616 | tf_op jit(solution)/shard_map/ppermute | solution.py:422
  25.3 2.1 %collective-permute-start.12 = (bf16[128,256]{1,0:T(8,128)(2,1)S(1)}, bf16[128,256]{1,0:T(8,128)(2,1)S(1)}, u32[]{:S(2)}, u32[]{:S(2)}) collective-permute-start(bf16[128,256]{1,0:T(8,128)(2,1)S(1)} %get-tuple-element.69), channel_id=1, source_target_pairs={{0,2},{1,3},{2,0},{3,1},{4,6},{5,7},{6,4},{7,5},{8,10},{9,11},{10,... | collective-permute-start | bytes 196616 | tf_op jit(solution)/shard_map/ppermute | solution.py:422
  27.5 1.0 %collective-permute-start.13 = (bf16[128,256]{1,0:T(8,128)(2,1)S(1)}, bf16[128,256]{1,0:T(8,128)(2,1)S(1)}, u32[]{:S(2)}, u32[]{:S(2)}) collective-permute-start(bf16[128,256]{1,0:T(8,128)(2,1)S(1)} %get-tuple-element.70), channel_id=1, source_target_pairs={{0,3},{1,0},{2,1},{3,2},{4,7},{5,4},{6,5},{7,6},{8,11},{9,8},{10,9... | collective-permute-start | bytes 196616 | tf_op jit(solution)/shard_map/ppermute | solution.py:422
  28.5 3.5 %raw.1 = (f32[128,768]{1,0:T(8,128)S(1)}, f32[128,768]{1,0:T(8,128)S(1)}) custom-call(bf16[32,4224]{1,0:T(8,128)(2,1)S(1)} %pad_maximum_fusion.refs_0_, bf16[32,4224]{1,0:T(8,128)(2,1)S(1)} %constant_dynamic-update-slice_fusion.refs_1_, bf16[32,4224]{1,0:T(8,128)(2,1)S(1)} %collective-permute-done.9.refs_2_, ...), custom_call_target="tpu_custom_call" | custom-call | flops 1 | bytes 1 | tf_op jit(solution)/shard_map/raw/pallas_call | solution.py:214
  32.0 1.3 %collective-permute-done.12.refs_6_ = bf16[128,256]{1,0:T(8,128)(2,1)S(1)} collective-permute-done((bf16[128,256]{1,0:T(8,128)(2,1)S(1)}, bf16[128,256]{1,0:T(8,128)(2,1)S(1)}, u32[]{:S(2)}, u32[]{:S(2)}) %collective-permute-start.12) | collective-permute-done | bytes 65568 | tf_op jit(solution)/shard_map/ppermute | solution.py:422
  33.8 0.8 %collective-permute-start.16 = (bf16[64,128]{1,0:T(8,128)(2,1)S(1)}, bf16[64,128]{1,0:T(8,128)(2,1)S(1)}, u32[]{:S(2)}, u32[]{:S(2)}) collective-permute-start(bf16[64,128]{1,0:T(8,128)(2,1)S(1)} %get-tuple-element.81), channel_id=1, source_target_pairs={{0,8},{8,0},{1,9},{9,1},{2,10},{10,2},{3,11},{11,3},{4,12},{12,4},... | collective-permute-start | bytes 49160 | tf_op jit(solution)/shard_map/ppermute | solution.py:425
  34.7 1.1 %down.1 = (f32[64,4096]{1,0:T(8,128)S(1)}, bf16[64,4096]{1,0:T(8,128)(2,1)S(1)}) custom-call(bf16[128,768]{1,0:T(8,128)(2,1)S(1)} %get-tuple-element.76.hidden_ref, bf16[768,4096]{1,0:T(8,128)(2,1)S(1)} %bitcast.10), custom_call_target="tpu_custom_call" | custom-call | flops 1 | bytes 1 | tf_op jit(solution)/shard_map/down/pallas_call | solution.py:276
  35.8 1.8 %collective-permute-done.16.refs_1_ = bf16[64,128]{1,0:T(8,128)(2,1)S(1)} collective-permute-done((bf16[64,128]{1,0:T(8,128)(2,1)S(1)}, bf16[64,128]{1,0:T(8,128)(2,1)S(1)}, u32[]{:S(2)}, u32[]{:S(2)}) %collective-permute-start.16) | collective-permute-done | bytes 16416 | tf_op jit(solution)/shard_map/ppermute | solution.py:425
  37.7 1.2 %collective-permute-done.17.far_ref = bf16[32,256]{1,0:T(8,128)(2,1)S(1)} collective-permute-done((bf16[32,256]{1,0:T(8,128)(2,1)S(1)}, bf16[32,256]{1,0:T(8,128)(2,1)S(1)}, u32[]{:S(2)}, u32[]{:S(2)}) %collective-permute-start.17) | collective-permute-done | bytes 16416 | tf_op jit(solution)/shard_map/ppermute | solution.py:428
  39.2 0.8 %collective-permute-start.23 = (bf16[24,4096]{1,0:T(8,128)(2,1)S(1)}, bf16[24,4096]{1,0:T(8,128)(2,1)S(1)}, u32[]{:S(2)}, u32[]{:S(2)}) collective-permute-start(bf16[24,4096]{1,0:T(8,128)(2,1)S(1)} %get-tuple-element.90), channel_id=1, source_target_pairs={{0,8},{8,0},{1,9},{9,1},{2,10},{10,2},{3,11},{11,3},{4,12},{12,4},... | collective-permute-start | bytes 589832 | tf_op jit(solution)/shard_map/ppermute | solution.py:425
  40.0 1.9 %collective-permute-start.19 = (bf16[32,512]{1,0:T(8,128)(2,1)S(1)}, bf16[32,512]{1,0:T(8,128)(2,1)S(1)}, u32[]{:S(2)}, u32[]{:S(2)}) collective-permute-start(bf16[32,512]{1,0:T(8,128)(2,1)S(1)} %get-tuple-element.86), channel_id=1, source_target_pairs={{0,1},{1,2},{2,3},{3,0},{4,5},{5,6},{6,7},{7,4},{8,9},{9,10},{10,1... | collective-permute-start | bytes 98312 | tf_op jit(solution)/shard_map/ppermute | solution.py:422
  41.9 1.2 %collective-permute-start.20 = (bf16[32,512]{1,0:T(8,128)(2,1)S(1)}, bf16[32,512]{1,0:T(8,128)(2,1)S(1)}, u32[]{:S(2)}, u32[]{:S(2)}) collective-permute-start(bf16[32,512]{1,0:T(8,128)(2,1)S(1)} %get-tuple-element.87), channel_id=1, source_target_pairs={{0,2},{1,3},{2,0},{3,1},{4,6},{5,7},{6,4},{7,5},{8,10},{9,11},{10,... | collective-permute-start | bytes 98312 | tf_op jit(solution)/shard_map/ppermute | solution.py:422
  43.1 1.1 %collective-permute-start.21 = (bf16[32,512]{1,0:T(8,128)(2,1)S(1)}, bf16[32,512]{1,0:T(8,128)(2,1)S(1)}, u32[]{:S(2)}, u32[]{:S(2)}) collective-permute-start(bf16[32,512]{1,0:T(8,128)(2,1)S(1)} %get-tuple-element.88), channel_id=1, source_target_pairs={{0,3},{1,0},{2,1},{3,2},{4,7},{5,4},{6,5},{7,6},{8,11},{9,8},{10,9... | collective-permute-start | bytes 98312 | tf_op jit(solution)/shard_map/ppermute | solution.py:422
  44.3 1.6 %collective-permute-done.19.refs_0_ = bf16[32,512]{1,0:T(8,128)(2,1)S(1)} collective-permute-done((bf16[32,512]{1,0:T(8,128)(2,1)S(1)}, bf16[32,512]{1,0:T(8,128)(2,1)S(1)}, u32[]{:S(2)}, u32[]{:S(2)}) %collective-permute-start.19) | collective-permute-done | bytes 32800 | tf_op jit(solution)/shard_map/ppermute | solution.py:422
  45.8 1.2 %collective-permute-start.22 = (bf16[8,4096]{1,0:T(8,128)(2,1)S(1)}, bf16[8,4096]{1,0:T(8,128)(2,1)S(1)}, u32[]{:S(2)}, u32[]{:S(2)}) collective-permute-start(bf16[8,4096]{1,0:T(8,128)(2,1)S(1)} %get-tuple-element.89), channel_id=1, source_target_pairs={{0,8},{8,0},{1,9},{9,1},{2,10},{10,2},{3,11},{11,3},{4,12},{12,4},... | collective-permute-start | bytes 196616 | tf_op jit(solution)/shard_map/ppermute | solution.py:425
  47.3 2.8 %collective-permute-done.22.refs_6_ = bf16[8,4096]{1,0:T(8,128)(2,1)S(1)} collective-permute-done((bf16[8,4096]{1,0:T(8,128)(2,1)S(1)}, bf16[8,4096]{1,0:T(8,128)(2,1)S(1)}, u32[]{:S(2)}, u32[]{:S(2)}) %collective-permute-start.22) | collective-permute-done | bytes 65568 | tf_op jit(solution)/shard_map/ppermute | solution.py:425
  50.7 1.0 %collective-permute-start.25 = (bf16[8,4096]{1,0:T(8,128)(2,1)S(1)}, bf16[8,4096]{1,0:T(8,128)(2,1)S(1)}, u32[]{:S(2)}, u32[]{:S(2)}) collective-permute-start(bf16[8,4096]{1,0:T(8,128)(2,1)S(1)} %get-tuple-element.93), channel_id=1, source_target_pairs={{0,2},{1,3},{2,0},{3,1},{4,6},{5,7},{6,4},{7,5},{8,10},{9,11},{10,... | collective-permute-start | bytes 196616 | tf_op jit(solution)/shard_map/ppermute | solution.py:422
  51.7 2.6 %collective-permute-start.24 = (bf16[8,4096]{1,0:T(8,128)(2,1)S(1)}, bf16[8,4096]{1,0:T(8,128)(2,1)S(1)}, u32[]{:S(2)}, u32[]{:S(2)}) collective-permute-start(bf16[8,4096]{1,0:T(8,128)(2,1)S(1)} %get-tuple-element.92), channel_id=1, source_target_pairs={{0,3},{1,0},{2,1},{3,2},{4,7},{5,4},{6,5},{7,6},{8,11},{9,8},{10,9... | collective-permute-start | bytes 196616 | tf_op jit(solution)/shard_map/ppermute | solution.py:422
  54.3 2.3 %collective-permute-done.26 = bf16[8,4096]{1,0:T(8,128)(2,1)S(1)} collective-permute-done((bf16[8,4096]{1,0:T(8,128)(2,1)S(1)}, bf16[8,4096]{1,0:T(8,128)(2,1)S(1)}, u32[]{:S(2)}, u32[]{:S(2)}) %collective-permute-start.26) | collective-permute-done | bytes 65568 | tf_op jit(solution)/shard_map/ppermute | solution.py:422
  56.6 0.7 %collective-permute-done.24 = bf16[8,4096]{1,0:T(8,128)(2,1)S(1)} collective-permute-done((bf16[8,4096]{1,0:T(8,128)(2,1)S(1)}, bf16[8,4096]{1,0:T(8,128)(2,1)S(1)}, u32[]{:S(2)}, u32[]{:S(2)}) %collective-permute-start.24) | collective-permute-done | bytes 65568 | tf_op jit(solution)/shard_map/ppermute | solution.py:422
  57.3 0.7 %add_convert_fusion = bf16[8,4096]{1,0:T(8,128)(2,1)} fusion(bf16[8,4096]{1,0:T(8,128)(2,1)S(1)} %collective-permute-done.26, bf16[8,4096]{1,0:T(8,128)(2,1)S(1)} %collective-permute-done.25, f32[8,4096]{1,0:T(8,128)S(1)} %get-tuple-element.91, bf16[8,4096]{1,0:T(8,128)(2,1)S(1)} %collective-permute-done.24), kind=kLoop, calls=%fused_computation.2 | loop fusion | flops 229376 | bytes 393216 | tf_op jit(solution)/shard_map/convert_element_type | solution.py:478
  (47 shorter events, 3.4 us)
Async XLA Ops:
  1.0 11.7 %collective-permute-start.2 = (bf16[8,4224]{1,0:T(8,128)(2,1)S(1)}, bf16[8,4224]{1,0:T(8,128)(2,1)S(1)}, u32[]{:S(2)}, u32[]{:S(2)}) collective-permute-start(bf16[8,4224]{1,0:T(8,128)(2,1)S(1)} %attach.1), channel_id=1, source_target_pairs={{0,3},{1,0},{2,1},{3,2},{4,7},{5,4},{6,5},{7,6},{8,11},{9,8},{10,9... | collective-permute-start | bytes 202760 | tf_op jit(solution)/shard_map/ppermute | solution.py:422
  6.1 6.6 %collective-permute-start.1 = (bf16[8,4224]{1,0:T(8,128)(2,1)S(1)}, bf16[8,4224]{1,0:T(8,128)(2,1)S(1)}, u32[]{:S(2)}, u32[]{:S(2)}) collective-permute-start(bf16[8,4224]{1,0:T(8,128)(2,1)S(1)} %attach.1), channel_id=1, source_target_pairs={{0,2},{1,3},{2,0},{3,1},{4,6},{5,7},{6,4},{7,5},{8,10},{9,11},{10,... | collective-permute-start | bytes 202760 | tf_op jit(solution)/shard_map/ppermute | solution.py:422
  6.1 6.6 %collective-permute-start = (bf16[8,4224]{1,0:T(8,128)(2,1)S(1)}, bf16[8,4224]{1,0:T(8,128)(2,1)S(1)}, u32[]{:S(2)}, u32[]{:S(2)}) collective-permute-start(bf16[8,4224]{1,0:T(8,128)(2,1)S(1)} %attach.1), channel_id=1, source_target_pairs={{0,1},{1,2},{2,3},{3,0},{4,5},{5,6},{6,7},{7,4},{8,9},{9,10},{10,1... | collective-permute-start | bytes 202760 | tf_op jit(solution)/shard_map/ppermute | solution.py:422
  7.1 5.7 %collective-permute-start.4 = (bf16[8,4224]{1,0:T(8,128)(2,1)S(1)}, bf16[8,4224]{1,0:T(8,128)(2,1)S(1)}, u32[]{:S(2)}, u32[]{:S(2)}) collective-permute-start(bf16[8,4224]{1,0:T(8,128)(2,1)S(1)} %attach.1), channel_id=1, source_target_pairs={{0,8},{8,0},{1,9},{9,1},{2,10},{10,2},{3,11},{11,3},{4,12},{12,4},... | collective-permute-start | bytes 202760 | tf_op jit(solution)/shard_map/ppermute | solution.py:425
  8.6 4.2 %collective-permute-start.3 = (bf16[128,1024]{1,0:T(8,128)(2,1)}, bf16[128,1024]{1,0:T(8,128)(2,1)S(1)}, u32[]{:S(2)}, u32[]{:S(2)}) collective-permute-start(bf16[128,1024]{1,0:T(8,128)(2,1)} %bitcast.11), channel_id=1, source_target_pairs={{0,4},{4,0},{1,5},{5,1},{2,6},{6,2},{3,7},{7,3},{8,12},{12,8},{9,1... | collective-permute-start | bytes 786440 | tf_op jit(solution)/shard_map/ppermute | solution.py:428
  12.8 9.3 %collective-permute-start.5 = (bf16[24,4224]{1,0:T(8,128)(2,1)S(1)}, bf16[24,4224]{1,0:T(8,128)(2,1)S(1)}, u32[]{:S(2)}, u32[]{:S(2)}) collective-permute-start(bf16[24,4224]{1,0:T(8,128)(2,1)S(1)} %pad_maximum_fusion.1), channel_id=1, source_target_pairs={{0,8},{8,0},{1,9},{9,1},{2,10},{10,2},{3,11},{11,3},{4,12},{12,4},... | collective-permute-start | bytes 608264 | tf_op jit(solution)/shard_map/ppermute | solution.py:425
  14.4 7.8 %collective-permute-start.6 = (bf16[3,32,192]{2,1,0:T(8,128)(2,1)S(1)}, bf16[3,32,192]{2,1,0:T(8,128)(2,1)S(1)}, u32[]{:S(2)}, u32[]{:S(2)}) collective-permute-start(bf16[3,32,192]{2,1,0:T(8,128)(2,1)S(1)} %get-tuple-element.58), channel_id=1, source_target_pairs={{0,1},{1,2},{2,3},{3,0},{4,5},{5,6},{6,7},{7,4},{8,9},{9,10},{10,1... | collective-permute-start | bytes 110600 | tf_op jit(solution)/shard_map/ppermute | solution.py:422
  15.9 6.3 %collective-permute-start.7 = (bf16[3,32,192]{2,1,0:T(8,128)(2,1)S(1)}, bf16[3,32,192]{2,1,0:T(8,128)(2,1)S(1)}, u32[]{:S(2)}, u32[]{:S(2)}) collective-permute-start(bf16[3,32,192]{2,1,0:T(8,128)(2,1)S(1)} %get-tuple-element.59), channel_id=1, source_target_pairs={{0,2},{1,3},{2,0},{3,1},{4,6},{5,7},{6,4},{7,5},{8,10},{9,11},{10,... | collective-permute-start | bytes 110600 | tf_op jit(solution)/shard_map/ppermute | solution.py:422
  16.8 5.3 %collective-permute-start.8 = (bf16[3,32,192]{2,1,0:T(8,128)(2,1)S(1)}, bf16[3,32,192]{2,1,0:T(8,128)(2,1)S(1)}, u32[]{:S(2)}, u32[]{:S(2)}) collective-permute-start(bf16[3,32,192]{2,1,0:T(8,128)(2,1)S(1)} %get-tuple-element.60), channel_id=1, source_target_pairs={{0,3},{1,0},{2,1},{3,2},{4,7},{5,4},{6,5},{7,6},{8,11},{9,8},{10,9... | collective-permute-start | bytes 110600 | tf_op jit(solution)/shard_map/ppermute | solution.py:422
  19.1 3.6 %copy-start = (bf16[4,32,1024]{2,1,0:T(8,128)(2,1)S(1)}, bf16[4,32,1024]{2,1,0:T(8,128)(2,1)}, u32[]{:S(2)}) copy-start(bf16[4,32,1024]{2,1,0:T(8,128)(2,1)} %param.23) | copy-start | bytes 786436
  22.0 1.8 %collective-permute-start.9 = (bf16[32,4224]{1,0:T(8,128)(2,1)S(1)}, bf16[32,4224]{1,0:T(8,128)(2,1)S(1)}, u32[]{:S(2)}, u32[]{:S(2)}) collective-permute-start(bf16[32,4224]{1,0:T(8,128)(2,1)S(1)} %pad_maximum_fusion.refs_0_), channel_id=1, source_target_pairs={{0,4},{4,0},{1,5},{5,1},{2,6},{6,2},{3,7},{7,3},{8,12},{12,8},{9,1... | collective-permute-start | bytes 811016 | tf_op jit(solution)/shard_map/ppermute | solution.py:428
  22.2 1.9 %collective-permute-start.10 = (bf16[32,4224]{1,0:T(8,128)(2,1)S(1)}, bf16[32,4224]{1,0:T(8,128)(2,1)S(1)}, u32[]{:S(2)}, u32[]{:S(2)}) collective-permute-start(bf16[32,4224]{1,0:T(8,128)(2,1)S(1)} %constant_dynamic-update-slice_fusion.refs_1_), channel_id=1, source_target_pairs={{0,4},{4,0},{1,5},{5,1},{2,6},{6,2},{3,7},{7,3},{8,12},{12,8},{9,1... | collective-permute-start | bytes 811016 | tf_op jit(solution)/shard_map/ppermute | solution.py:428
  22.7 9.3 %collective-permute-start.14 = (bf16[128,1024]{1,0:T(8,128)(2,1)S(1)}, bf16[128,1024]{1,0:T(8,128)(2,1)S(1)}, u32[]{:S(2)}, u32[]{:S(2)}) collective-permute-start(bf16[128,1024]{1,0:T(8,128)(2,1)S(1)} %bitcast.12), channel_id=1, source_target_pairs={{0,8},{8,0},{1,9},{9,1},{2,10},{10,2},{3,11},{11,3},{4,12},{12,4},... | collective-permute-start | bytes 786440 | tf_op jit(solution)/shard_map/ppermute | solution.py:425
  24.3 7.7 %collective-permute-start.11 = (bf16[128,256]{1,0:T(8,128)(2,1)S(1)}, bf16[128,256]{1,0:T(8,128)(2,1)S(1)}, u32[]{:S(2)}, u32[]{:S(2)}) collective-permute-start(bf16[128,256]{1,0:T(8,128)(2,1)S(1)} %get-tuple-element.68), channel_id=1, source_target_pairs={{0,1},{1,2},{2,3},{3,0},{4,5},{5,6},{6,7},{7,4},{8,9},{9,10},{10,1... | collective-permute-start | bytes 196616 | tf_op jit(solution)/shard_map/ppermute | solution.py:422
  25.3 8.0 %collective-permute-start.12 = (bf16[128,256]{1,0:T(8,128)(2,1)S(1)}, bf16[128,256]{1,0:T(8,128)(2,1)S(1)}, u32[]{:S(2)}, u32[]{:S(2)}) collective-permute-start(bf16[128,256]{1,0:T(8,128)(2,1)S(1)} %get-tuple-element.69), channel_id=1, source_target_pairs={{0,2},{1,3},{2,0},{3,1},{4,6},{5,7},{6,4},{7,5},{8,10},{9,11},{10,... | collective-permute-start | bytes 196616 | tf_op jit(solution)/shard_map/ppermute | solution.py:422
  27.5 7.2 %slice-start = ((s8[6291456]{0:T(1024)(128)(4,1)}), s8[4194304]{0:T(1024)(128)(4,1)S(1)}, s32[]{:S(2)}) async-start(s8[6291456]{0:T(1024)(128)(4,1)} %bitcast.8), calls=%async_computation | async-start | bytes 8388608
  27.5 7.2 %slice-start.1 = ((s8[6291456]{0:T(1024)(128)(4,1)}), s8[2097152]{0:T(1024)(128)(4,1)S(1)}, s32[]{:S(2)}) async-start(s8[6291456]{0:T(1024)(128)(4,1)} %bitcast.8), calls=%async_computation.1 | async-start | bytes 4194304
  27.5 5.8 %collective-permute-start.13 = (bf16[128,256]{1,0:T(8,128)(2,1)S(1)}, bf16[128,256]{1,0:T(8,128)(2,1)S(1)}, u32[]{:S(2)}, u32[]{:S(2)}) collective-permute-start(bf16[128,256]{1,0:T(8,128)(2,1)S(1)} %get-tuple-element.70), channel_id=1, source_target_pairs={{0,3},{1,0},{2,1},{3,2},{4,7},{5,4},{6,5},{7,6},{8,11},{9,8},{10,9... | collective-permute-start | bytes 196616 | tf_op jit(solution)/shard_map/ppermute | solution.py:422
  33.8 3.8 %collective-permute-start.16 = (bf16[64,128]{1,0:T(8,128)(2,1)S(1)}, bf16[64,128]{1,0:T(8,128)(2,1)S(1)}, u32[]{:S(2)}, u32[]{:S(2)}) collective-permute-start(bf16[64,128]{1,0:T(8,128)(2,1)S(1)} %get-tuple-element.81), channel_id=1, source_target_pairs={{0,8},{8,0},{1,9},{9,1},{2,10},{10,2},{3,11},{11,3},{4,12},{12,4},... | collective-permute-start | bytes 49160 | tf_op jit(solution)/shard_map/ppermute | solution.py:425
  35.8 3.3 %collective-permute-start.15 = (bf16[64,4096]{1,0:T(8,128)(2,1)S(1)}, bf16[64,4096]{1,0:T(8,128)(2,1)S(1)}, u32[]{:S(2)}, u32[]{:S(2)}) collective-permute-start(bf16[64,4096]{1,0:T(8,128)(2,1)S(1)} %get-tuple-element.78), channel_id=1, source_target_pairs={{0,4},{4,0},{1,5},{5,1},{2,6},{6,2},{3,7},{7,3},{8,12},{12,8},{9,1... | collective-permute-start | bytes 1572872 | tf_op jit(solution)/shard_map/ppermute | solution.py:428
  37.7 1.2 %collective-permute-start.17 = (bf16[32,256]{1,0:T(8,128)(2,1)S(1)}, bf16[32,256]{1,0:T(8,128)(2,1)S(1)}, u32[]{:S(2)}, u32[]{:S(2)}) collective-permute-start(bf16[32,256]{1,0:T(8,128)(2,1)S(1)} %get-tuple-element.83), channel_id=1, source_target_pairs={{0,4},{4,0},{1,5},{5,1},{2,6},{6,2},{3,7},{7,3},{8,12},{12,8},{9,1... | collective-permute-start | bytes 49160 | tf_op jit(solution)/shard_map/ppermute | solution.py:428
  38.8 8.4 %collective-permute-start.18 = (bf16[128,1024]{1,0:T(8,128)(2,1)S(1)}, bf16[128,1024]{1,0:T(8,128)(2,1)S(1)}, u32[]{:S(2)}, u32[]{:S(2)}) collective-permute-start(bf16[128,1024]{1,0:T(8,128)(2,1)S(1)} %collective-permute-done.14.refs_2_), channel_id=1, source_target_pairs={{0,4},{4,0},{1,5},{5,1},{2,6},{6,2},{3,7},{7,3},{8,12},{12,8},{9,1... | collective-permute-start | bytes 786440 | tf_op jit(solution)/shard_map/ppermute | solution.py:428
  39.2 10.9 %collective-permute-start.23 = (bf16[24,4096]{1,0:T(8,128)(2,1)S(1)}, bf16[24,4096]{1,0:T(8,128)(2,1)S(1)}, u32[]{:S(2)}, u32[]{:S(2)}) collective-permute-start(bf16[24,4096]{1,0:T(8,128)(2,1)S(1)} %get-tuple-element.90), channel_id=1, source_target_pairs={{0,8},{8,0},{1,9},{9,1},{2,10},{10,2},{3,11},{11,3},{4,12},{12,4},... | collective-permute-start | bytes 589832 | tf_op jit(solution)/shard_map/ppermute | solution.py:425
  40.0 5.8 %collective-permute-start.19 = (bf16[32,512]{1,0:T(8,128)(2,1)S(1)}, bf16[32,512]{1,0:T(8,128)(2,1)S(1)}, u32[]{:S(2)}, u32[]{:S(2)}) collective-permute-start(bf16[32,512]{1,0:T(8,128)(2,1)S(1)} %get-tuple-element.86), channel_id=1, source_target_pairs={{0,1},{1,2},{2,3},{3,0},{4,5},{5,6},{6,7},{7,4},{8,9},{9,10},{10,1... | collective-permute-start | bytes 98312 | tf_op jit(solution)/shard_map/ppermute | solution.py:422
  41.9 5.1 %collective-permute-start.20 = (bf16[32,512]{1,0:T(8,128)(2,1)S(1)}, bf16[32,512]{1,0:T(8,128)(2,1)S(1)}, u32[]{:S(2)}, u32[]{:S(2)}) collective-permute-start(bf16[32,512]{1,0:T(8,128)(2,1)S(1)} %get-tuple-element.87), channel_id=1, source_target_pairs={{0,2},{1,3},{2,0},{3,1},{4,6},{5,7},{6,4},{7,5},{8,10},{9,11},{10,... | collective-permute-start | bytes 98312 | tf_op jit(solution)/shard_map/ppermute | solution.py:422
  43.1 4.1 %collective-permute-start.21 = (bf16[32,512]{1,0:T(8,128)(2,1)S(1)}, bf16[32,512]{1,0:T(8,128)(2,1)S(1)}, u32[]{:S(2)}, u32[]{:S(2)}) collective-permute-start(bf16[32,512]{1,0:T(8,128)(2,1)S(1)} %get-tuple-element.88), channel_id=1, source_target_pairs={{0,3},{1,0},{2,1},{3,2},{4,7},{5,4},{6,5},{7,6},{8,11},{9,8},{10,9... | collective-permute-start | bytes 98312 | tf_op jit(solution)/shard_map/ppermute | solution.py:422
  45.8 4.3 %collective-permute-start.22 = (bf16[8,4096]{1,0:T(8,128)(2,1)S(1)}, bf16[8,4096]{1,0:T(8,128)(2,1)S(1)}, u32[]{:S(2)}, u32[]{:S(2)}) collective-permute-start(bf16[8,4096]{1,0:T(8,128)(2,1)S(1)} %get-tuple-element.89), channel_id=1, source_target_pairs={{0,8},{8,0},{1,9},{9,1},{2,10},{10,2},{3,11},{11,3},{4,12},{12,4},... | collective-permute-start | bytes 196616 | tf_op jit(solution)/shard_map/ppermute | solution.py:425
  50.4 6.2 %collective-permute-start.26 = (bf16[8,4096]{1,0:T(8,128)(2,1)S(1)}, bf16[8,4096]{1,0:T(8,128)(2,1)S(1)}, u32[]{:S(2)}, u32[]{:S(2)}) collective-permute-start(bf16[8,4096]{1,0:T(8,128)(2,1)S(1)} %get-tuple-element.94), channel_id=1, source_target_pairs={{0,1},{1,2},{2,3},{3,0},{4,5},{5,6},{6,7},{7,4},{8,9},{9,10},{10,1... | collective-permute-start | bytes 196616 | tf_op jit(solution)/shard_map/ppermute | solution.py:422
  50.7 5.9 %collective-permute-start.25 = (bf16[8,4096]{1,0:T(8,128)(2,1)S(1)}, bf16[8,4096]{1,0:T(8,128)(2,1)S(1)}, u32[]{:S(2)}, u32[]{:S(2)}) collective-permute-start(bf16[8,4096]{1,0:T(8,128)(2,1)S(1)} %get-tuple-element.93), channel_id=1, source_target_pairs={{0,2},{1,3},{2,0},{3,1},{4,6},{5,7},{6,4},{7,5},{8,10},{9,11},{10,... | collective-permute-start | bytes 196616 | tf_op jit(solution)/shard_map/ppermute | solution.py:422
  51.7 5.6 %collective-permute-start.24 = (bf16[8,4096]{1,0:T(8,128)(2,1)S(1)}, bf16[8,4096]{1,0:T(8,128)(2,1)S(1)}, u32[]{:S(2)}, u32[]{:S(2)}) collective-permute-start(bf16[8,4096]{1,0:T(8,128)(2,1)S(1)} %get-tuple-element.92), channel_id=1, source_target_pairs={{0,3},{1,0},{2,1},{3,2},{4,7},{5,4},{6,5},{7,6},{8,11},{9,8},{10,9... | collective-permute-start | bytes 196616 | tf_op jit(solution)/shard_map/ppermute | solution.py:422

commit v16 on v15

--- a/solution.py
+++ b/solution.py
@@ -14,6 +14,7 @@
 PIECES = 8
 LONG = pl.CostEstimate(flops=1_000_000_000, bytes_accessed=1, transcendentals=0)
 LONGER = pl.CostEstimate(flops=10_000_000_000, bytes_accessed=1, transcendentals=0)
+LAST = pl.CostEstimate(flops=1_000_000_000, bytes_accessed=1, transcendentals=0)
 BRIEF = pl.CostEstimate(flops=1, bytes_accessed=1, transcendentals=0)
 
 
@@ -370,15 +371,33 @@
         value += dot_nn(low[:, n * ranks : (n + 1) * ranks], ref[...])
     total = own_ref[...]
     value += own_ref[:, pl.ds(offset, block)]
-    for n in range(0, len(backs), 2):
-        total += jnp.concatenate([ref[...].astype(F32) for ref in backs[n : n + 2]])
-        value += jnp.concatenate(
-            [ref[:, pl.ds(offset, block)].astype(F32) for ref in backs[n : n + 2]]
-        )
-    for k, out_ref in enumerate(outs):
-        span = slice(k * rows, (k + 1) * rows)
-        out_ref[...] = total[span].astype(out_ref.dtype)
-        out_ref[:, pl.ds(offset, block)] = value[span].astype(out_ref.dtype)
+    rest, rest_value = total[rows:], value[rows:]
+    for ref in backs:
+        rest += ref[...].astype(F32)
+        rest_value += ref[:, pl.ds(offset, block)].astype(F32)
+    outs[0][...] = total[:rows]
+    outs[0][:, pl.ds(offset, block)] = value[:rows]
+    for k in range(1, parts):
+        span = slice((k - 1) * rows, k * rows)
+        outs[k][...] = rest[span].astype(BF)
+        outs[k][:, pl.ds(offset, block)] = rest_value[span].astype(BF)
+
+
+def plus_kernel(own_ref, *refs):
+    total = own_ref[...]
+    for ref in refs[:-1]:
+        total += ref[...].astype(F32)
+    refs[-1][...] = total
+
+
+def plus(own, pieces):
+    return pl.pallas_call(
+        plus_kernel,
+        out_shape=jax.ShapeDtypeStruct(own.shape, F32),
+        compiler_params=pltpu.CompilerParams(vmem_limit_bytes=SMALL_LIMIT),
+        cost_estimate=LAST,
+        name="plus",
+    )(own, *pieces)
 
 
 def merge(own, rights, low, backs, rows):
@@ -471,8 +490,8 @@
     out, *others = fold(near, other_core(far), chips, rows)
     backs = [along_y(others[n], -(n // 2 + 1)) for n in range(2 * chips - 2)]
     rights += [partner_right] + [other_core(after(right, bottom[0])) for right in rights[1:]]
-    own, *pieces = merge(out, rights, add_up(bottom[1:] + bottom[:1]), backs, rows)
-    result = own
+    own, *pieces = merge(out, rights, add_up(bottom[1:] + bottom[:1]), backs[1::2], rows)
+    result = plus(own, backs[::2])
     for k in range(1, parts):
         result += along_z(pieces[k - 1], -k).astype(F32)
     return result.astype(BF)

time: 58.1 us -> 56.8 us (0.978)
  waiting for transfers between devices: 12.1 us -> 10.2 us
    ppermute x6, waiting for transfers between devices: 4.64 us -> 1.81 us  [along_y(): lax.ppermute(value, 'y', [(i, (i + step) % chips) for i in range(chips)])]
    ppermute x15, waiting for transfers between devices: 6.14 us -> 7.04 us  [along_z(): lax.ppermute(value, 'mp', [(i, (i + step) % parts) for i in range(parts)])]
    ppermute x15, starting transfers between devices: 23.1 us -> 23.7 us  [along_z(): lax.ppermute(value, 'mp', [(i, (i + step) % parts) for i in range(parts)])]
  transfers between devices with their start and end apart: 27 -> 27, of which waited for: 9 -> 8; matrix products, arithmetic and copies ran while one was open for 0% -> 0% of each run, Pallas kernels for 21% -> 22%
where the time goes in v16:
time: 56.8 us; the launch traced here: 56.6 us
  starting transfers between devices  31.3 us (55%)
  Pallas kernels  14.1 us (25%)
  waiting for transfers between devices  10.2 us (18%)
  other arithmetic  0.71 us (1%)
    ppermute x15, starting transfers between devices, along_z(): lax.ppermute(value, 'mp', [(i, (i + step) % parts) for i in range(parts)])  23.7 us
    ppermute x15, waiting for transfers between devices, along_z(): lax.ppermute(value, 'mp', [(i, (i + step) % parts) for i in range(parts)])  7.04 us
    ppermute x6, starting transfers between devices, along_y(): lax.ppermute(value, 'y', [(i, (i + step) % chips) for i in range(chips)])  6.73 us
    pallas_call x1, Pallas kernels, prepare(): pl.pallas_call(functools.partial(prepare_kernel, parts), in_specs=[vmem]...  4.06 us
    pallas_call x1, Pallas kernels, raw_products(): pl.pallas_call(functools.partial(raw_kernel, len(lines), tile), out_shape...  3.51 us
    pallas_call x1, Pallas kernels, load(): pl.pallas_call(load_kernel, in_specs=[pl.BlockSpec(memory_space=pltpu.HBM...  2.9 us
    ppermute x6, waiting for transfers between devices, along_y(): lax.ppermute(value, 'y', [(i, (i + step) % chips) for i in range(chips)])  1.81 us
    ppermute x6, waiting for transfers between devices, other_core(): return lax.ppermute(value, 'core', [(0, 1), (1, 0)])  1.36 us
  transfers between devices with their start and end apart: 27, of which 8 were waited for; matrix products, arithmetic and copies ran while one was open for 0% of the time, Pallas kernels for 22%

profile of v16, /device:TPU:0, one launch (start us, length us, event | category | flops | bytes accessed | tf_op | source)
XLA Modules:
  0.0 56.6 jit_solution(14975158974596885200)
XLA Ops:
  0.0 0.9 %attach.1 = bf16[8,4224]{1,0:T(8,128)(2,1)S(1)} custom-call(bf16[8,4096]{1,0:T(8,128)(2,1)} %tokens_ref.1, s32[8,8]{1,0:T(8,128)} %routes_ref.1, f32[8,8]{1,0:T(8,128)} %probs_ref.1), custom_call_target="tpu_custom_call" | custom-call | flops 1 | bytes 1 | tf_op jit(solution)/shard_map/attach/pallas_call | solution.py:65
  1.0 5.1 %collective-permute-start.2 = (bf16[8,4224]{1,0:T(8,128)(2,1)S(1)}, bf16[8,4224]{1,0:T(8,128)(2,1)S(1)}, u32[]{:S(2)}, u32[]{:S(2)}) collective-permute-start(bf16[8,4224]{1,0:T(8,128)(2,1)S(1)} %attach.1), channel_id=1, source_target_pairs={{0,3},{1,0},{2,1},{3,2},{4,7},{5,4},{6,5},{7,6},{8,11},{9,8},{10,9... | collective-permute-start | bytes 202760 | tf_op jit(solution)/shard_map/ppermute | solution.py:441
  6.1 1.0 %collective-permute-start = (bf16[8,4224]{1,0:T(8,128)(2,1)S(1)}, bf16[8,4224]{1,0:T(8,128)(2,1)S(1)}, u32[]{:S(2)}, u32[]{:S(2)}) collective-permute-start(bf16[8,4224]{1,0:T(8,128)(2,1)S(1)} %attach.1), channel_id=1, source_target_pairs={{0,1},{1,2},{2,3},{3,0},{4,5},{5,6},{6,7},{7,4},{8,9},{9,10},{10,1... | collective-permute-start | bytes 202760 | tf_op jit(solution)/shard_map/ppermute | solution.py:441
  7.1 1.5 %collective-permute-start.4 = (bf16[8,4224]{1,0:T(8,128)(2,1)S(1)}, bf16[8,4224]{1,0:T(8,128)(2,1)S(1)}, u32[]{:S(2)}, u32[]{:S(2)}) collective-permute-start(bf16[8,4224]{1,0:T(8,128)(2,1)S(1)} %attach.1), channel_id=1, source_target_pairs={{0,8},{8,0},{1,9},{9,1},{2,10},{10,2},{3,11},{11,3},{4,12},{12,4},... | collective-permute-start | bytes 202760 | tf_op jit(solution)/shard_map/ppermute | solution.py:444
  8.6 4.1 %prepare.1 = (bf16[768,4096]{1,0:T(8,128)(2,1)S(1)}, bf16[256,1024]{1,0:T(8,128)(2,1)S(1)}, bf16[3,32,192]{2,1,0:T(8,128)(2,1)S(1)}, bf16[3,32,192]{2,1,0:T(8,12...) custom-call(bf16[4,8,768]{2,1,0:T(8,128)(2,1)} %refs_0_.1, bf16[4,8,768]{2,1,0:T(8,128)(2,1)} %refs_1_.1, ...), custom_call_target="tpu_custom_call" | custom-call | flops 1 | bytes 1 | tf_op jit(solution)/shard_map/prepare/pallas_call | solution.py:133
  12.8 1.6 %collective-permute-start.5 = (bf16[24,4224]{1,0:T(8,128)(2,1)S(1)}, bf16[24,4224]{1,0:T(8,128)(2,1)S(1)}, u32[]{:S(2)}, u32[]{:S(2)}) collective-permute-start(bf16[24,4224]{1,0:T(8,128)(2,1)S(1)} %pad_maximum_fusion.1), channel_id=1, source_target_pairs={{0,8},{8,0},{1,9},{9,1},{2,10},{10,2},{3,11},{11,3},{4,12},{12,4},... | collective-permute-start | bytes 608264 | tf_op jit(solution)/shard_map/ppermute | solution.py:444
  14.4 1.5 %collective-permute-start.6 = (bf16[3,32,192]{2,1,0:T(8,128)(2,1)S(1)}, bf16[3,32,192]{2,1,0:T(8,128)(2,1)S(1)}, u32[]{:S(2)}, u32[]{:S(2)}) collective-permute-start(bf16[3,32,192]{2,1,0:T(8,128)(2,1)S(1)} %get-tuple-element.58), channel_id=1, source_target_pairs={{0,1},{1,2},{2,3},{3,0},{4,5},{5,6},{6,7},{7,4},{8,9},{9,10},{10,1... | collective-permute-start | bytes 110600 | tf_op jit(solution)/shard_map/ppermute | solution.py:441
  15.9 1.0 %collective-permute-start.7 = (bf16[3,32,192]{2,1,0:T(8,128)(2,1)S(1)}, bf16[3,32,192]{2,1,0:T(8,128)(2,1)S(1)}, u32[]{:S(2)}, u32[]{:S(2)}) collective-permute-start(bf16[3,32,192]{2,1,0:T(8,128)(2,1)S(1)} %get-tuple-element.59), channel_id=1, source_target_pairs={{0,2},{1,3},{2,0},{3,1},{4,6},{5,7},{6,4},{7,5},{8,10},{9,11},{10,... | collective-permute-start | bytes 110600 | tf_op jit(solution)/shard_map/ppermute | solution.py:441
  16.8 2.3 %collective-permute-start.8 = (bf16[3,32,192]{2,1,0:T(8,128)(2,1)S(1)}, bf16[3,32,192]{2,1,0:T(8,128)(2,1)S(1)}, u32[]{:S(2)}, u32[]{:S(2)}) collective-permute-start(bf16[3,32,192]{2,1,0:T(8,128)(2,1)S(1)} %get-tuple-element.60), channel_id=1, source_target_pairs={{0,3},{1,0},{2,1},{3,2},{4,7},{5,4},{6,5},{7,6},{8,11},{9,8},{10,9... | collective-permute-start | bytes 110600 | tf_op jit(solution)/shard_map/ppermute | solution.py:441
  19.1 2.9 %load.1.refs_5_ = bf16[768,4096]{1,0:T(8,128)(2,1)S(1)} custom-call(bf16[768,4096]{1,0:T(8,128)(2,1)} %bitcast.14), custom_call_target="tpu_custom_call" | custom-call | flops 1 | bytes 1 | tf_op jit(solution)/shard_map/load/pallas_call | solution.py:92
  22.7 0.7 %collective-permute-start.14 = (bf16[128,1024]{1,0:T(8,128)(2,1)S(1)}, bf16[128,1024]{1,0:T(8,128)(2,1)S(1)}, u32[]{:S(2)}, u32[]{:S(2)}) collective-permute-start(bf16[128,1024]{1,0:T(8,128)(2,1)S(1)} %bitcast.12), channel_id=1, source_target_pairs={{0,8},{8,0},{1,9},{9,1},{2,10},{10,2},{3,11},{11,3},{4,12},{12,4},... | collective-permute-start | bytes 786440 | tf_op jit(solution)/shard_map/ppermute | solution.py:444
  24.3 1.0 %collective-permute-start.11 = (bf16[128,256]{1,0:T(8,128)(2,1)S(1)}, bf16[128,256]{1,0:T(8,128)(2,1)S(1)}, u32[]{:S(2)}, u32[]{:S(2)}) collective-permute-start(bf16[128,256]{1,0:T(8,128)(2,1)S(1)} %get-tuple-element.68), channel_id=1, source_target_pairs={{0,1},{1,2},{2,3},{3,0},{4,5},{5,6},{6,7},{7,4},{8,9},{9,10},{10,1... | collective-permute-start | bytes 196616 | tf_op jit(solution)/shard_map/ppermute | solution.py:441
  25.3 2.1 %collective-permute-start.12 = (bf16[128,256]{1,0:T(8,128)(2,1)S(1)}, bf16[128,256]{1,0:T(8,128)(2,1)S(1)}, u32[]{:S(2)}, u32[]{:S(2)}) collective-permute-start(bf16[128,256]{1,0:T(8,128)(2,1)S(1)} %get-tuple-element.69), channel_id=1, source_target_pairs={{0,2},{1,3},{2,0},{3,1},{4,6},{5,7},{6,4},{7,5},{8,10},{9,11},{10,... | collective-permute-start | bytes 196616 | tf_op jit(solution)/shard_map/ppermute | solution.py:441
  27.5 1.0 %collective-permute-start.13 = (bf16[128,256]{1,0:T(8,128)(2,1)S(1)}, bf16[128,256]{1,0:T(8,128)(2,1)S(1)}, u32[]{:S(2)}, u32[]{:S(2)}) collective-permute-start(bf16[128,256]{1,0:T(8,128)(2,1)S(1)} %get-tuple-element.70), channel_id=1, source_target_pairs={{0,3},{1,0},{2,1},{3,2},{4,7},{5,4},{6,5},{7,6},{8,11},{9,8},{10,9... | collective-permute-start | bytes 196616 | tf_op jit(solution)/shard_map/ppermute | solution.py:441
  28.5 3.5 %raw.1 = (f32[128,768]{1,0:T(8,128)S(1)}, f32[128,768]{1,0:T(8,128)S(1)}) custom-call(bf16[32,4224]{1,0:T(8,128)(2,1)S(1)} %pad_maximum_fusion.refs_0_, bf16[32,4224]{1,0:T(8,128)(2,1)S(1)} %constant_dynamic-update-slice_fusion.refs_1_, bf16[32,4224]{1,0:T(8,128)(2,1)S(1)} %collective-permute-done.9.refs_2_, ...), custom_call_target="tpu_custom_call" | custom-call | flops 1 | bytes 1 | tf_op jit(solution)/shard_map/raw/pallas_call | solution.py:215
  32.0 1.3 %collective-permute-done.12.refs_6_ = bf16[128,256]{1,0:T(8,128)(2,1)S(1)} collective-permute-done((bf16[128,256]{1,0:T(8,128)(2,1)S(1)}, bf16[128,256]{1,0:T(8,128)(2,1)S(1)}, u32[]{:S(2)}, u32[]{:S(2)}) %collective-permute-start.12) | collective-permute-done | bytes 65568 | tf_op jit(solution)/shard_map/ppermute | solution.py:441
  33.8 0.8 %collective-permute-start.16 = (bf16[64,128]{1,0:T(8,128)(2,1)S(1)}, bf16[64,128]{1,0:T(8,128)(2,1)S(1)}, u32[]{:S(2)}, u32[]{:S(2)}) collective-permute-start(bf16[64,128]{1,0:T(8,128)(2,1)S(1)} %get-tuple-element.81), channel_id=1, source_target_pairs={{0,8},{8,0},{1,9},{9,1},{2,10},{10,2},{3,11},{11,3},{4,12},{12,4},... | collective-permute-start | bytes 49160 | tf_op jit(solution)/shard_map/ppermute | solution.py:444
  34.7 1.1 %down.1 = (f32[64,4096]{1,0:T(8,128)S(1)}, bf16[64,4096]{1,0:T(8,128)(2,1)S(1)}) custom-call(bf16[128,768]{1,0:T(8,128)(2,1)S(1)} %get-tuple-element.76.hidden_ref, bf16[768,4096]{1,0:T(8,128)(2,1)S(1)} %bitcast.10), custom_call_target="tpu_custom_call" | custom-call | flops 1 | bytes 1 | tf_op jit(solution)/shard_map/down/pallas_call | solution.py:277
  35.8 1.8 %collective-permute-done.16.refs_1_ = bf16[64,128]{1,0:T(8,128)(2,1)S(1)} collective-permute-done((bf16[64,128]{1,0:T(8,128)(2,1)S(1)}, bf16[64,128]{1,0:T(8,128)(2,1)S(1)}, u32[]{:S(2)}, u32[]{:S(2)}) %collective-permute-start.16) | collective-permute-done | bytes 16416 | tf_op jit(solution)/shard_map/ppermute | solution.py:444
  37.7 1.2 %collective-permute-done.17.far_ref = bf16[32,256]{1,0:T(8,128)(2,1)S(1)} collective-permute-done((bf16[32,256]{1,0:T(8,128)(2,1)S(1)}, bf16[32,256]{1,0:T(8,128)(2,1)S(1)}, u32[]{:S(2)}, u32[]{:S(2)}) %collective-permute-start.17) | collective-permute-done | bytes 16416 | tf_op jit(solution)/shard_map/ppermute | solution.py:447
  39.2 0.8 %collective-permute-start.22 = (bf16[24,4096]{1,0:T(8,128)(2,1)S(1)}, bf16[24,4096]{1,0:T(8,128)(2,1)S(1)}, u32[]{:S(2)}, u32[]{:S(2)}) collective-permute-start(bf16[24,4096]{1,0:T(8,128)(2,1)S(1)} %get-tuple-element.89), channel_id=1, source_target_pairs={{0,8},{8,0},{1,9},{9,1},{2,10},{10,2},{3,11},{11,3},{4,12},{12,4},... | collective-permute-start | bytes 589832 | tf_op jit(solution)/shard_map/ppermute | solution.py:444
  40.0 1.9 %collective-permute-start.19 = (bf16[32,512]{1,0:T(8,128)(2,1)S(1)}, bf16[32,512]{1,0:T(8,128)(2,1)S(1)}, u32[]{:S(2)}, u32[]{:S(2)}) collective-permute-start(bf16[32,512]{1,0:T(8,128)(2,1)S(1)} %get-tuple-element.86), channel_id=1, source_target_pairs={{0,1},{1,2},{2,3},{3,0},{4,5},{5,6},{6,7},{7,4},{8,9},{9,10},{10,1... | collective-permute-start | bytes 98312 | tf_op jit(solution)/shard_map/ppermute | solution.py:441
  41.9 1.2 %collective-permute-start.20 = (bf16[32,512]{1,0:T(8,128)(2,1)S(1)}, bf16[32,512]{1,0:T(8,128)(2,1)S(1)}, u32[]{:S(2)}, u32[]{:S(2)}) collective-permute-start(bf16[32,512]{1,0:T(8,128)(2,1)S(1)} %get-tuple-element.87), channel_id=1, source_target_pairs={{0,2},{1,3},{2,0},{3,1},{4,6},{5,7},{6,4},{7,5},{8,10},{9,11},{10,... | collective-permute-start | bytes 98312 | tf_op jit(solution)/shard_map/ppermute | solution.py:441
  43.1 1.1 %collective-permute-start.21 = (bf16[32,512]{1,0:T(8,128)(2,1)S(1)}, bf16[32,512]{1,0:T(8,128)(2,1)S(1)}, u32[]{:S(2)}, u32[]{:S(2)}) collective-permute-start(bf16[32,512]{1,0:T(8,128)(2,1)S(1)} %get-tuple-element.88), channel_id=1, source_target_pairs={{0,3},{1,0},{2,1},{3,2},{4,7},{5,4},{6,5},{7,6},{8,11},{9,8},{10,9... | collective-permute-start | bytes 98312 | tf_op jit(solution)/shard_map/ppermute | solution.py:441
  44.3 1.6 %collective-permute-done.19.refs_0_ = bf16[32,512]{1,0:T(8,128)(2,1)S(1)} collective-permute-done((bf16[32,512]{1,0:T(8,128)(2,1)S(1)}, bf16[32,512]{1,0:T(8,128)(2,1)S(1)}, u32[]{:S(2)}, u32[]{:S(2)}) %collective-permute-start.19) | collective-permute-done | bytes 32800 | tf_op jit(solution)/shard_map/ppermute | solution.py:441
  45.8 1.2 %collective-permute-start.23 = (bf16[8,4096]{1,0:T(8,128)(2,1)S(1)}, bf16[8,4096]{1,0:T(8,128)(2,1)S(1)}, u32[]{:S(2)}, u32[]{:S(2)}) collective-permute-start(bf16[8,4096]{1,0:T(8,128)(2,1)S(1)} %get-tuple-element.91), channel_id=1, source_target_pairs={{0,8},{8,0},{1,9},{9,1},{2,10},{10,2},{3,11},{11,3},{4,12},{12,4},... | collective-permute-start | bytes 196616 | tf_op jit(solution)/shard_map/ppermute | solution.py:444
  47.6 1.1 %collective-permute-start.26 = (bf16[8,4096]{1,0:T(8,128)(2,1)S(1)}, bf16[8,4096]{1,0:T(8,128)(2,1)S(1)}, u32[]{:S(2)}, u32[]{:S(2)}) collective-permute-start(bf16[8,4096]{1,0:T(8,128)(2,1)S(1)} %get-tuple-element.94), channel_id=1, source_target_pairs={{0,1},{1,2},{2,3},{3,0},{4,5},{5,6},{6,7},{7,4},{8,9},{9,10},{10,1... | collective-permute-start | bytes 196616 | tf_op jit(solution)/shard_map/ppermute | solution.py:441
  48.7 2.2 %collective-permute-start.25 = (bf16[8,4096]{1,0:T(8,128)(2,1)S(1)}, bf16[8,4096]{1,0:T(8,128)(2,1)S(1)}, u32[]{:S(2)}, u32[]{:S(2)}) collective-permute-start(bf16[8,4096]{1,0:T(8,128)(2,1)S(1)} %get-tuple-element.93), channel_id=1, source_target_pairs={{0,2},{1,3},{2,0},{3,1},{4,6},{5,7},{6,4},{7,5},{8,10},{9,11},{10,... | collective-permute-start | bytes 196616 | tf_op jit(solution)/shard_map/ppermute | solution.py:441
  50.9 1.1 %collective-permute-start.24 = (bf16[8,4096]{1,0:T(8,128)(2,1)S(1)}, bf16[8,4096]{1,0:T(8,128)(2,1)S(1)}, u32[]{:S(2)}, u32[]{:S(2)}) collective-permute-start(bf16[8,4096]{1,0:T(8,128)(2,1)S(1)} %get-tuple-element.92), channel_id=1, source_target_pairs={{0,3},{1,0},{2,1},{3,2},{4,7},{5,4},{6,5},{7,6},{8,11},{9,8},{10,9... | collective-permute-start | bytes 196616 | tf_op jit(solution)/shard_map/ppermute | solution.py:441
  52.1 1.9 %collective-permute-done.26 = bf16[8,4096]{1,0:T(8,128)(2,1)S(1)} collective-permute-done((bf16[8,4096]{1,0:T(8,128)(2,1)S(1)}, bf16[8,4096]{1,0:T(8,128)(2,1)S(1)}, u32[]{:S(2)}, u32[]{:S(2)}) %collective-permute-start.26) | collective-permute-done | bytes 65568 | tf_op jit(solution)/shard_map/ppermute | solution.py:441
  54.0 1.9 %collective-permute-done.25 = bf16[8,4096]{1,0:T(8,128)(2,1)S(1)} collective-permute-done((bf16[8,4096]{1,0:T(8,128)(2,1)S(1)}, bf16[8,4096]{1,0:T(8,128)(2,1)S(1)}, u32[]{:S(2)}, u32[]{:S(2)}) %collective-permute-start.25) | collective-permute-done | bytes 65568 | tf_op jit(solution)/shard_map/ppermute | solution.py:441
  55.9 0.7 %add_convert_fusion = bf16[8,4096]{1,0:T(8,128)(2,1)} fusion(bf16[8,4096]{1,0:T(8,128)(2,1)S(1)} %collective-permute-done.26, bf16[8,4096]{1,0:T(8,128)(2,1)S(1)} %collective-permute-done.25, f32[8,4096]{1,0:T(8,128)S(1)} %plus.1, bf16[8,4096]{1,0:T(8,128)(2,1)S(1)} %collective-permute-done.24), kind=kLoop, calls=%fused_computation.2 | loop fusion | flops 229376 | bytes 393216 | tf_op jit(solution)/shard_map/convert_element_type | solution.py:497
  (48 shorter events, 3.1 us)
Async XLA Ops:
  1.0 11.7 %collective-permute-start.2 = (bf16[8,4224]{1,0:T(8,128)(2,1)S(1)}, bf16[8,4224]{1,0:T(8,128)(2,1)S(1)}, u32[]{:S(2)}, u32[]{:S(2)}) collective-permute-start(bf16[8,4224]{1,0:T(8,128)(2,1)S(1)} %attach.1), channel_id=1, source_target_pairs={{0,3},{1,0},{2,1},{3,2},{4,7},{5,4},{6,5},{7,6},{8,11},{9,8},{10,9... | collective-permute-start | bytes 202760 | tf_op jit(solution)/shard_map/ppermute | solution.py:441
  6.1 6.6 %collective-permute-start.1 = (bf16[8,4224]{1,0:T(8,128)(2,1)S(1)}, bf16[8,4224]{1,0:T(8,128)(2,1)S(1)}, u32[]{:S(2)}, u32[]{:S(2)}) collective-permute-start(bf16[8,4224]{1,0:T(8,128)(2,1)S(1)} %attach.1), channel_id=1, source_target_pairs={{0,2},{1,3},{2,0},{3,1},{4,6},{5,7},{6,4},{7,5},{8,10},{9,11},{10,... | collective-permute-start | bytes 202760 | tf_op jit(solution)/shard_map/ppermute | solution.py:441
  6.1 6.6 %collective-permute-start = (bf16[8,4224]{1,0:T(8,128)(2,1)S(1)}, bf16[8,4224]{1,0:T(8,128)(2,1)S(1)}, u32[]{:S(2)}, u32[]{:S(2)}) collective-permute-start(bf16[8,4224]{1,0:T(8,128)(2,1)S(1)} %attach.1), channel_id=1, source_target_pairs={{0,1},{1,2},{2,3},{3,0},{4,5},{5,6},{6,7},{7,4},{8,9},{9,10},{10,1... | collective-permute-start | bytes 202760 | tf_op jit(solution)/shard_map/ppermute | solution.py:441
  7.1 5.7 %collective-permute-start.4 = (bf16[8,4224]{1,0:T(8,128)(2,1)S(1)}, bf16[8,4224]{1,0:T(8,128)(2,1)S(1)}, u32[]{:S(2)}, u32[]{:S(2)}) collective-permute-start(bf16[8,4224]{1,0:T(8,128)(2,1)S(1)} %attach.1), channel_id=1, source_target_pairs={{0,8},{8,0},{1,9},{9,1},{2,10},{10,2},{3,11},{11,3},{4,12},{12,4},... | collective-permute-start | bytes 202760 | tf_op jit(solution)/shard_map/ppermute | solution.py:444
  8.6 4.2 %collective-permute-start.3 = (bf16[128,1024]{1,0:T(8,128)(2,1)}, bf16[128,1024]{1,0:T(8,128)(2,1)S(1)}, u32[]{:S(2)}, u32[]{:S(2)}) collective-permute-start(bf16[128,1024]{1,0:T(8,128)(2,1)} %bitcast.11), channel_id=1, source_target_pairs={{0,4},{4,0},{1,5},{5,1},{2,6},{6,2},{3,7},{7,3},{8,12},{12,8},{9,1... | collective-permute-start | bytes 786440 | tf_op jit(solution)/shard_map/ppermute | solution.py:447
  12.8 9.3 %collective-permute-start.5 = (bf16[24,4224]{1,0:T(8,128)(2,1)S(1)}, bf16[24,4224]{1,0:T(8,128)(2,1)S(1)}, u32[]{:S(2)}, u32[]{:S(2)}) collective-permute-start(bf16[24,4224]{1,0:T(8,128)(2,1)S(1)} %pad_maximum_fusion.1), channel_id=1, source_target_pairs={{0,8},{8,0},{1,9},{9,1},{2,10},{10,2},{3,11},{11,3},{4,12},{12,4},... | collective-permute-start | bytes 608264 | tf_op jit(solution)/shard_map/ppermute | solution.py:444
  14.4 7.8 %collective-permute-start.6 = (bf16[3,32,192]{2,1,0:T(8,128)(2,1)S(1)}, bf16[3,32,192]{2,1,0:T(8,128)(2,1)S(1)}, u32[]{:S(2)}, u32[]{:S(2)}) collective-permute-start(bf16[3,32,192]{2,1,0:T(8,128)(2,1)S(1)} %get-tuple-element.58), channel_id=1, source_target_pairs={{0,1},{1,2},{2,3},{3,0},{4,5},{5,6},{6,7},{7,4},{8,9},{9,10},{10,1... | collective-permute-start | bytes 110600 | tf_op jit(solution)/shard_map/ppermute | solution.py:441
  15.9 6.3 %collective-permute-start.7 = (bf16[3,32,192]{2,1,0:T(8,128)(2,1)S(1)}, bf16[3,32,192]{2,1,0:T(8,128)(2,1)S(1)}, u32[]{:S(2)}, u32[]{:S(2)}) collective-permute-start(bf16[3,32,192]{2,1,0:T(8,128)(2,1)S(1)} %get-tuple-element.59), channel_id=1, source_target_pairs={{0,2},{1,3},{2,0},{3,1},{4,6},{5,7},{6,4},{7,5},{8,10},{9,11},{10,... | collective-permute-start | bytes 110600 | tf_op jit(solution)/shard_map/ppermute | solution.py:441
  16.8 5.3 %collective-permute-start.8 = (bf16[3,32,192]{2,1,0:T(8,128)(2,1)S(1)}, bf16[3,32,192]{2,1,0:T(8,128)(2,1)S(1)}, u32[]{:S(2)}, u32[]{:S(2)}) collective-permute-start(bf16[3,32,192]{2,1,0:T(8,128)(2,1)S(1)} %get-tuple-element.60), channel_id=1, source_target_pairs={{0,3},{1,0},{2,1},{3,2},{4,7},{5,4},{6,5},{7,6},{8,11},{9,8},{10,9... | collective-permute-start | bytes 110600 | tf_op jit(solution)/shard_map/ppermute | solution.py:441
  19.1 3.6 %copy-start = (bf16[4,32,1024]{2,1,0:T(8,128)(2,1)S(1)}, bf16[4,32,1024]{2,1,0:T(8,128)(2,1)}, u32[]{:S(2)}) copy-start(bf16[4,32,1024]{2,1,0:T(8,128)(2,1)} %param.23) | copy-start | bytes 786436
  22.0 1.8 %collective-permute-start.9 = (bf16[32,4224]{1,0:T(8,128)(2,1)S(1)}, bf16[32,4224]{1,0:T(8,128)(2,1)S(1)}, u32[]{:S(2)}, u32[]{:S(2)}) collective-permute-start(bf16[32,4224]{1,0:T(8,128)(2,1)S(1)} %pad_maximum_fusion.refs_0_), channel_id=1, source_target_pairs={{0,4},{4,0},{1,5},{5,1},{2,6},{6,2},{3,7},{7,3},{8,12},{12,8},{9,1... | collective-permute-start | bytes 811016 | tf_op jit(solution)/shard_map/ppermute | solution.py:447
  22.2 1.9 %collective-permute-start.10 = (bf16[32,4224]{1,0:T(8,128)(2,1)S(1)}, bf16[32,4224]{1,0:T(8,128)(2,1)S(1)}, u32[]{:S(2)}, u32[]{:S(2)}) collective-permute-start(bf16[32,4224]{1,0:T(8,128)(2,1)S(1)} %constant_dynamic-update-slice_fusion.refs_1_), channel_id=1, source_target_pairs={{0,4},{4,0},{1,5},{5,1},{2,6},{6,2},{3,7},{7,3},{8,12},{12,8},{9,1... | collective-permute-start | bytes 811016 | tf_op jit(solution)/shard_map/ppermute | solution.py:447
  22.7 9.3 %collective-permute-start.14 = (bf16[128,1024]{1,0:T(8,128)(2,1)S(1)}, bf16[128,1024]{1,0:T(8,128)(2,1)S(1)}, u32[]{:S(2)}, u32[]{:S(2)}) collective-permute-start(bf16[128,1024]{1,0:T(8,128)(2,1)S(1)} %bitcast.12), channel_id=1, source_target_pairs={{0,8},{8,0},{1,9},{9,1},{2,10},{10,2},{3,11},{11,3},{4,12},{12,4},... | collective-permute-start | bytes 786440 | tf_op jit(solution)/shard_map/ppermute | solution.py:444
  24.3 7.7 %collective-permute-start.11 = (bf16[128,256]{1,0:T(8,128)(2,1)S(1)}, bf16[128,256]{1,0:T(8,128)(2,1)S(1)}, u32[]{:S(2)}, u32[]{:S(2)}) collective-permute-start(bf16[128,256]{1,0:T(8,128)(2,1)S(1)} %get-tuple-element.68), channel_id=1, source_target_pairs={{0,1},{1,2},{2,3},{3,0},{4,5},{5,6},{6,7},{7,4},{8,9},{9,10},{10,1... | collective-permute-start | bytes 196616 | tf_op jit(solution)/shard_map/ppermute | solution.py:441
  25.3 8.0 %collective-permute-start.12 = (bf16[128,256]{1,0:T(8,128)(2,1)S(1)}, bf16[128,256]{1,0:T(8,128)(2,1)S(1)}, u32[]{:S(2)}, u32[]{:S(2)}) collective-permute-start(bf16[128,256]{1,0:T(8,128)(2,1)S(1)} %get-tuple-element.69), channel_id=1, source_target_pairs={{0,2},{1,3},{2,0},{3,1},{4,6},{5,7},{6,4},{7,5},{8,10},{9,11},{10,... | collective-permute-start | bytes 196616 | tf_op jit(solution)/shard_map/ppermute | solution.py:441
  27.5 7.2 %slice-start = ((s8[6291456]{0:T(1024)(128)(4,1)}), s8[4194304]{0:T(1024)(128)(4,1)S(1)}, s32[]{:S(2)}) async-start(s8[6291456]{0:T(1024)(128)(4,1)} %bitcast.8), calls=%async_computation | async-start | bytes 8388608
  27.5 7.2 %slice-start.1 = ((s8[6291456]{0:T(1024)(128)(4,1)}), s8[2097152]{0:T(1024)(128)(4,1)S(1)}, s32[]{:S(2)}) async-start(s8[6291456]{0:T(1024)(128)(4,1)} %bitcast.8), calls=%async_computation.1 | async-start | bytes 4194304
  27.5 5.8 %collective-permute-start.13 = (bf16[128,256]{1,0:T(8,128)(2,1)S(1)}, bf16[128,256]{1,0:T(8,128)(2,1)S(1)}, u32[]{:S(2)}, u32[]{:S(2)}) collective-permute-start(bf16[128,256]{1,0:T(8,128)(2,1)S(1)} %get-tuple-element.70), channel_id=1, source_target_pairs={{0,3},{1,0},{2,1},{3,2},{4,7},{5,4},{6,5},{7,6},{8,11},{9,8},{10,9... | collective-permute-start | bytes 196616 | tf_op jit(solution)/shard_map/ppermute | solution.py:441
  33.8 3.8 %collective-permute-start.16 = (bf16[64,128]{1,0:T(8,128)(2,1)S(1)}, bf16[64,128]{1,0:T(8,128)(2,1)S(1)}, u32[]{:S(2)}, u32[]{:S(2)}) collective-permute-start(bf16[64,128]{1,0:T(8,128)(2,1)S(1)} %get-tuple-element.81), channel_id=1, source_target_pairs={{0,8},{8,0},{1,9},{9,1},{2,10},{10,2},{3,11},{11,3},{4,12},{12,4},... | collective-permute-start | bytes 49160 | tf_op jit(solution)/shard_map/ppermute | solution.py:444
  35.8 3.3 %collective-permute-start.15 = (bf16[64,4096]{1,0:T(8,128)(2,1)S(1)}, bf16[64,4096]{1,0:T(8,128)(2,1)S(1)}, u32[]{:S(2)}, u32[]{:S(2)}) collective-permute-start(bf16[64,4096]{1,0:T(8,128)(2,1)S(1)} %get-tuple-element.78), channel_id=1, source_target_pairs={{0,4},{4,0},{1,5},{5,1},{2,6},{6,2},{3,7},{7,3},{8,12},{12,8},{9,1... | collective-permute-start | bytes 1572872 | tf_op jit(solution)/shard_map/ppermute | solution.py:447
  37.7 1.2 %collective-permute-start.17 = (bf16[32,256]{1,0:T(8,128)(2,1)S(1)}, bf16[32,256]{1,0:T(8,128)(2,1)S(1)}, u32[]{:S(2)}, u32[]{:S(2)}) collective-permute-start(bf16[32,256]{1,0:T(8,128)(2,1)S(1)} %get-tuple-element.83), channel_id=1, source_target_pairs={{0,4},{4,0},{1,5},{5,1},{2,6},{6,2},{3,7},{7,3},{8,12},{12,8},{9,1... | collective-permute-start | bytes 49160 | tf_op jit(solution)/shard_map/ppermute | solution.py:447
  38.8 8.4 %collective-permute-start.18 = (bf16[128,1024]{1,0:T(8,128)(2,1)S(1)}, bf16[128,1024]{1,0:T(8,128)(2,1)S(1)}, u32[]{:S(2)}, u32[]{:S(2)}) collective-permute-start(bf16[128,1024]{1,0:T(8,128)(2,1)S(1)} %collective-permute-done.14.refs_2_), channel_id=1, source_target_pairs={{0,4},{4,0},{1,5},{5,1},{2,6},{6,2},{3,7},{7,3},{8,12},{12,8},{9,1... | collective-permute-start | bytes 786440 | tf_op jit(solution)/shard_map/ppermute | solution.py:447
  39.2 8.1 %collective-permute-start.22 = (bf16[24,4096]{1,0:T(8,128)(2,1)S(1)}, bf16[24,4096]{1,0:T(8,128)(2,1)S(1)}, u32[]{:S(2)}, u32[]{:S(2)}) collective-permute-start(bf16[24,4096]{1,0:T(8,128)(2,1)S(1)} %get-tuple-element.89), channel_id=1, source_target_pairs={{0,8},{8,0},{1,9},{9,1},{2,10},{10,2},{3,11},{11,3},{4,12},{12,4},... | collective-permute-start | bytes 589832 | tf_op jit(solution)/shard_map/ppermute | solution.py:444
  40.0 5.8 %collective-permute-start.19 = (bf16[32,512]{1,0:T(8,128)(2,1)S(1)}, bf16[32,512]{1,0:T(8,128)(2,1)S(1)}, u32[]{:S(2)}, u32[]{:S(2)}) collective-permute-start(bf16[32,512]{1,0:T(8,128)(2,1)S(1)} %get-tuple-element.86), channel_id=1, source_target_pairs={{0,1},{1,2},{2,3},{3,0},{4,5},{5,6},{6,7},{7,4},{8,9},{9,10},{10,1... | collective-permute-start | bytes 98312 | tf_op jit(solution)/shard_map/ppermute | solution.py:441
  41.9 5.1 %collective-permute-start.20 = (bf16[32,512]{1,0:T(8,128)(2,1)S(1)}, bf16[32,512]{1,0:T(8,128)(2,1)S(1)}, u32[]{:S(2)}, u32[]{:S(2)}) collective-permute-start(bf16[32,512]{1,0:T(8,128)(2,1)S(1)} %get-tuple-element.87), channel_id=1, source_target_pairs={{0,2},{1,3},{2,0},{3,1},{4,6},{5,7},{6,4},{7,5},{8,10},{9,11},{10,... | collective-permute-start | bytes 98312 | tf_op jit(solution)/shard_map/ppermute | solution.py:441
  43.1 4.1 %collective-permute-start.21 = (bf16[32,512]{1,0:T(8,128)(2,1)S(1)}, bf16[32,512]{1,0:T(8,128)(2,1)S(1)}, u32[]{:S(2)}, u32[]{:S(2)}) collective-permute-start(bf16[32,512]{1,0:T(8,128)(2,1)S(1)} %get-tuple-element.88), channel_id=1, source_target_pairs={{0,3},{1,0},{2,1},{3,2},{4,7},{5,4},{6,5},{7,6},{8,11},{9,8},{10,9... | collective-permute-start | bytes 98312 | tf_op jit(solution)/shard_map/ppermute | solution.py:441
  45.8 6.2 %collective-permute-start.23 = (bf16[8,4096]{1,0:T(8,128)(2,1)S(1)}, bf16[8,4096]{1,0:T(8,128)(2,1)S(1)}, u32[]{:S(2)}, u32[]{:S(2)}) collective-permute-start(bf16[8,4096]{1,0:T(8,128)(2,1)S(1)} %get-tuple-element.91), channel_id=1, source_target_pairs={{0,8},{8,0},{1,9},{9,1},{2,10},{10,2},{3,11},{11,3},{4,12},{12,4},... | collective-permute-start | bytes 196616 | tf_op jit(solution)/shard_map/ppermute | solution.py:444
  47.6 6.4 %collective-permute-start.26 = (bf16[8,4096]{1,0:T(8,128)(2,1)S(1)}, bf16[8,4096]{1,0:T(8,128)(2,1)S(1)}, u32[]{:S(2)}, u32[]{:S(2)}) collective-permute-start(bf16[8,4096]{1,0:T(8,128)(2,1)S(1)} %get-tuple-element.94), channel_id=1, source_target_pairs={{0,1},{1,2},{2,3},{3,0},{4,5},{5,6},{6,7},{7,4},{8,9},{9,10},{10,1... | collective-permute-start | bytes 196616 | tf_op jit(solution)/shard_map/ppermute | solution.py:441
  48.7 7.2 %collective-permute-start.25 = (bf16[8,4096]{1,0:T(8,128)(2,1)S(1)}, bf16[8,4096]{1,0:T(8,128)(2,1)S(1)}, u32[]{:S(2)}, u32[]{:S(2)}) collective-permute-start(bf16[8,4096]{1,0:T(8,128)(2,1)S(1)} %get-tuple-element.93), channel_id=1, source_target_pairs={{0,2},{1,3},{2,0},{3,1},{4,6},{5,7},{6,4},{7,5},{8,10},{9,11},{10,... | collective-permute-start | bytes 196616 | tf_op jit(solution)/shard_map/ppermute | solution.py:441
  50.9 5.0 %collective-permute-start.24 = (bf16[8,4096]{1,0:T(8,128)(2,1)S(1)}, bf16[8,4096]{1,0:T(8,128)(2,1)S(1)}, u32[]{:S(2)}, u32[]{:S(2)}) collective-permute-start(bf16[8,4096]{1,0:T(8,128)(2,1)S(1)} %get-tuple-element.92), channel_id=1, source_target_pairs={{0,3},{1,0},{2,1},{3,2},{4,7},{5,4},{6,5},{7,6},{8,11},{9,8},{10,9... | collective-permute-start | bytes 196616 | tf_op jit(solution)/shard_map/ppermute | solution.py:441

commit v17 on v16

--- a/solution.py
+++ b/solution.py
@@ -11,10 +11,12 @@
 F32 = jnp.float32
 SMALL_LIMIT = 4 * 1024 * 1024
 VMEM_LIMIT = 12 * 1024 * 1024
+STREAM_LIMIT = 14 * 1024 * 1024
 PIECES = 8
 LONG = pl.CostEstimate(flops=1_000_000_000, bytes_accessed=1, transcendentals=0)
 LONGER = pl.CostEstimate(flops=10_000_000_000, bytes_accessed=1, transcendentals=0)
 LAST = pl.CostEstimate(flops=1_000_000_000, bytes_accessed=1, transcendentals=0)
+SOME = pl.CostEstimate(flops=3_000_000_000, bytes_accessed=1, transcendentals=0)
 BRIEF = pl.CostEstimate(flops=1, bytes_accessed=1, transcendentals=0)
 
 
@@ -78,27 +80,6 @@
         pltpu.make_async_copy(source.at[span], target.at[span], sems.at[i])
         for i, span in enumerate(spans)
     ]
-
-
-def load_kernel(source, target, sems):
-    copies = piece_copies(source, target, sems)
-    for copy in copies:
-        copy.start()
-    for copy in copies:
-        copy.wait()
-
-
-def load(weights):
-    return pl.pallas_call(
-        load_kernel,
-        in_specs=[pl.BlockSpec(memory_space=pltpu.HBM)],
-        out_specs=pl.BlockSpec(memory_space=pltpu.VMEM),
-        out_shape=pltpu.VMEM(weights.shape, weights.dtype),
-        scratch_shapes=[pltpu.SemaphoreType.DMA((PIECES,))],
-        compiler_params=pltpu.CompilerParams(vmem_limit_bytes=SMALL_LIMIT),
-        cost_estimate=BRIEF,
-        name="load",
-    )(*in_hbm(weights))
 
 
 def prepare_kernel(parts, *refs):
@@ -171,7 +152,7 @@
         functools.partial(spread_kernel, parts, exp_dev),
         out_shape=jax.ShapeDtypeStruct((3, span * parts, cols * exp_dev), BF),
         compiler_params=pltpu.CompilerParams(vmem_limit_bytes=SMALL_LIMIT),
-        cost_estimate=BRIEF,
+        cost_estimate=SOME,
         name="spread",
     )(*pieces)
 
@@ -199,26 +180,36 @@
 
 
 def raw_kernel(count, tile, *refs):
-    lines, (gate_w, up_w, gate_ref, up_ref) = refs[:count], refs[count:]
+    lines, (gate_w, up_w, gate_ref, up_ref, scratch, sems) = refs[:count], refs[count:]
     hid, width = gate_w.shape
+    copies = piece_copies(up_w, scratch, sems)
+    for copy in copies:
+        copy.start()
     x = jnp.concatenate([line[:, :width] for line in lines])
-    for i in range(hid // tile):
-        span = pl.ds(i * tile, tile)
+    spans = [pl.ds(i * tile, tile) for i in range(hid // tile)]
+    for span in spans:
         gate_ref[:, span] = dot_nt(gate_w[span], x).T
-        up_ref[:, span] = dot_nt(up_w[span], x).T
+    per = PIECES // len(spans)
+    for i, span in enumerate(spans):
+        for copy in copies[i * per : (i + 1) * per]:
+            copy.wait()
+        up_ref[:, span] = dot_nt(scratch[span], x).T
 
 
 def raw_products(lines, gate_w, up_w):
     hid = gate_w.shape[0]
     total = sum(line.shape[0] for line in lines)
-    tile = 384
-    return pl.pallas_call(
-        functools.partial(raw_kernel, len(lines), tile),
+    vmem = pl.BlockSpec(memory_space=pltpu.VMEM)
+    return pl.pallas_call(
+        functools.partial(raw_kernel, len(lines), 384),
+        in_specs=[vmem] * (len(lines) + 1) + [pl.BlockSpec(memory_space=pltpu.HBM)],
+        out_specs=[vmem] * 2,
         out_shape=[jax.ShapeDtypeStruct((total, hid), F32)] * 2,
-        compiler_params=pltpu.CompilerParams(vmem_limit_bytes=VMEM_LIMIT),
+        scratch_shapes=[pltpu.VMEM(up_w.shape, BF), pltpu.SemaphoreType.DMA((PIECES,))],
+        compiler_params=pltpu.CompilerParams(vmem_limit_bytes=STREAM_LIMIT),
         cost_estimate=BRIEF,
         name="raw",
-    )(*lines, gate_w, up_w)
+    )(*lines, gate_w, *in_hbm(up_w))
 
 
 def hidden_kernel(parts, count, exp_dev, pair, *refs):
@@ -457,7 +448,6 @@
     right = down_right.reshape(ranks, block)
     partner_right = other_core(right)
     rest = after(jnp.concatenate(arrived), (left, small, gate_w, partner_right))
-    up_w = load(after(up_w, rest))
     lines = [jnp.concatenate([sent, rest])]
     partner = [other_core(lines[0])]
     small = after(tuple(small), rest)
@@ -465,7 +455,6 @@
     for s in range(1, chips):
         line = jnp.concatenate([first[s - 1], along_y(rest, s)])
         arrival = line
-        line = after(line, (tuple(small), up_w))
         lines.append(line)
         partner.append(other_core(line))
     lines += partner

time: 56.8 us -> 58.7 us (1.033)
  waiting for transfers between devices: 10.2 us -> 11.6 us
  Pallas kernels: 14.1 us -> 15.1 us
    pallas_call x2 -> x1, Pallas kernels: 6.41 us -> 7.44 us  [raw_products(): pl.pallas_call(functools.partial(raw_kernel, len(lines), 384), in_specs=[...]
    ppermute x6, waiting for transfers between devices: 1.81 us -> 2.72 us  [along_y(): lax.ppermute(value, 'y', [(i, (i + step) % chips) for i in range(chips)])]
    ppermute x15, waiting for transfers between devices: 7.04 us -> 7.67 us  [along_z(): lax.ppermute(value, 'mp', [(i, (i + step) % parts) for i in range(parts)])]
  transfers between devices with their start and end apart: 27 -> 27, of which waited for: 8 -> 9; matrix products, arithmetic and copies ran while one was open for 0% -> 0% of each run, Pallas kernels for 22% -> 23%
where the time goes in v17:
time: 58.7 us; the launch traced here: 58.5 us
  starting transfers between devices  30.9 us (53%)
  Pallas kernels  15.1 us (26%)
  waiting for transfers between devices  11.6 us (20%)
  other arithmetic  0.71 us (1%)
    ppermute x15, starting transfers between devices, along_z(): lax.ppermute(value, 'mp', [(i, (i + step) % parts) for i in range(parts)])  23.8 us
    ppermute x15, waiting for transfers between devices, along_z(): lax.ppermute(value, 'mp', [(i, (i + step) % parts) for i in range(parts)])  7.67 us
    pallas_call x1, Pallas kernels, raw_products(): pl.pallas_call(functools.partial(raw_kernel, len(lines), 384), in_specs=[...  7.44 us
    ppermute x6, starting transfers between devices, along_y(): lax.ppermute(value, 'y', [(i, (i + step) % chips) for i in range(chips)])  6.62 us
    pallas_call x1, Pallas kernels, prepare(): pl.pallas_call(functools.partial(prepare_kernel, parts), in_specs=[vmem]...  4.06 us
    ppermute x6, waiting for transfers between devices, along_y(): lax.ppermute(value, 'y', [(i, (i + step) % chips) for i in range(chips)])  2.72 us
    ppermute x6, waiting for transfers between devices, other_core(): return lax.ppermute(value, 'core', [(0, 1), (1, 0)])  1.19 us
  transfers between devices with their start and end apart: 27, of which 9 were waited for; matrix products, arithmetic and copies ran while one was open for 0% of the time, Pallas kernels for 23%

profile of v17, /device:TPU:0, one launch (start us, length us, event | category | flops | bytes accessed | tf_op | source)
XLA Modules:
  0.0 58.5 jit_solution(4968149205333674790)
XLA Ops:
  0.0 1.0 %attach.1 = bf16[8,4224]{1,0:T(8,128)(2,1)S(1)} custom-call(bf16[8,4096]{1,0:T(8,128)(2,1)} %tokens_ref.1, s32[8,8]{1,0:T(8,128)} %routes_ref.1, f32[8,8]{1,0:T(8,128)} %probs_ref.1), custom_call_target="tpu_custom_call" | custom-call | flops 1 | bytes 1 | tf_op jit(solution)/shard_map/attach/pallas_call | solution.py:67
  1.0 5.1 %collective-permute-start.2 = (bf16[8,4224]{1,0:T(8,128)(2,1)S(1)}, bf16[8,4224]{1,0:T(8,128)(2,1)S(1)}, u32[]{:S(2)}, u32[]{:S(2)}) collective-permute-start(bf16[8,4224]{1,0:T(8,128)(2,1)S(1)} %attach.1), channel_id=1, source_target_pairs={{0,3},{1,0},{2,1},{3,2},{4,7},{5,4},{6,5},{7,6},{8,11},{9,8},{10,9... | collective-permute-start | bytes 202760 | tf_op jit(solution)/shard_map/ppermute | solution.py:432
  6.1 1.0 %collective-permute-start = (bf16[8,4224]{1,0:T(8,128)(2,1)S(1)}, bf16[8,4224]{1,0:T(8,128)(2,1)S(1)}, u32[]{:S(2)}, u32[]{:S(2)}) collective-permute-start(bf16[8,4224]{1,0:T(8,128)(2,1)S(1)} %attach.1), channel_id=1, source_target_pairs={{0,1},{1,2},{2,3},{3,0},{4,5},{5,6},{6,7},{7,4},{8,9},{9,10},{10,1... | collective-permute-start | bytes 202760 | tf_op jit(solution)/shard_map/ppermute | solution.py:432
  7.1 1.5 %collective-permute-start.4 = (bf16[8,4224]{1,0:T(8,128)(2,1)S(1)}, bf16[8,4224]{1,0:T(8,128)(2,1)S(1)}, u32[]{:S(2)}, u32[]{:S(2)}) collective-permute-start(bf16[8,4224]{1,0:T(8,128)(2,1)S(1)} %attach.1), channel_id=1, source_target_pairs={{0,8},{8,0},{1,9},{9,1},{2,10},{10,2},{3,11},{11,3},{4,12},{12,4},... | collective-permute-start | bytes 202760 | tf_op jit(solution)/shard_map/ppermute | solution.py:435
  8.6 4.1 %prepare.1 = (bf16[768,4096]{1,0:T(8,128)(2,1)S(1)}, bf16[256,1024]{1,0:T(8,128)(2,1)S(1)}, bf16[3,32,192]{2,1,0:T(8,128)(2,1)S(1)}, bf16[3,32,192]{2,1,0:T(8,12...) custom-call(bf16[4,8,768]{2,1,0:T(8,128)(2,1)} %refs_0_.1, bf16[4,8,768]{2,1,0:T(8,128)(2,1)} %refs_1_.1, ...), custom_call_target="tpu_custom_call" | custom-call | flops 1 | bytes 1 | tf_op jit(solution)/shard_map/prepare/pallas_call | solution.py:114
  12.8 1.6 %collective-permute-start.5 = (bf16[24,4224]{1,0:T(8,128)(2,1)S(1)}, bf16[24,4224]{1,0:T(8,128)(2,1)S(1)}, u32[]{:S(2)}, u32[]{:S(2)}) collective-permute-start(bf16[24,4224]{1,0:T(8,128)(2,1)S(1)} %pad_maximum_fusion.1), channel_id=1, source_target_pairs={{0,8},{8,0},{1,9},{9,1},{2,10},{10,2},{3,11},{11,3},{4,12},{12,4},... | collective-permute-start | bytes 608264 | tf_op jit(solution)/shard_map/ppermute | solution.py:435
  14.5 1.7 %collective-permute-start.8 = (bf16[3,32,192]{2,1,0:T(8,128)(2,1)S(1)}, bf16[3,32,192]{2,1,0:T(8,128)(2,1)S(1)}, u32[]{:S(2)}, u32[]{:S(2)}) collective-permute-start(bf16[3,32,192]{2,1,0:T(8,128)(2,1)S(1)} %get-tuple-element.56), channel_id=1, source_target_pairs={{0,1},{1,2},{2,3},{3,0},{4,5},{5,6},{6,7},{7,4},{8,9},{9,10},{10,1... | collective-permute-start | bytes 110600 | tf_op jit(solution)/shard_map/ppermute | solution.py:432
  16.2 0.9 %collective-permute-start.9 = (bf16[3,32,192]{2,1,0:T(8,128)(2,1)S(1)}, bf16[3,32,192]{2,1,0:T(8,128)(2,1)S(1)}, u32[]{:S(2)}, u32[]{:S(2)}) collective-permute-start(bf16[3,32,192]{2,1,0:T(8,128)(2,1)S(1)} %get-tuple-element.57), channel_id=1, source_target_pairs={{0,2},{1,3},{2,0},{3,1},{4,6},{5,7},{6,4},{7,5},{8,10},{9,11},{10,... | collective-permute-start | bytes 110600 | tf_op jit(solution)/shard_map/ppermute | solution.py:432
  17.1 2.2 %collective-permute-start.10 = (bf16[3,32,192]{2,1,0:T(8,128)(2,1)S(1)}, bf16[3,32,192]{2,1,0:T(8,128)(2,1)S(1)}, u32[]{:S(2)}, u32[]{:S(2)}) collective-permute-start(bf16[3,32,192]{2,1,0:T(8,128)(2,1)S(1)} %get-tuple-element.58), channel_id=1, source_target_pairs={{0,3},{1,0},{2,1},{3,2},{4,7},{5,4},{6,5},{7,6},{8,11},{9,8},{10,9... | collective-permute-start | bytes 110600 | tf_op jit(solution)/shard_map/ppermute | solution.py:432
  19.2 1.1 %collective-permute-done.5 = bf16[24,4224]{1,0:T(8,128)(2,1)S(1)} collective-permute-done((bf16[24,4224]{1,0:T(8,128)(2,1)S(1)}, bf16[24,4224]{1,0:T(8,128)(2,1)S(1)}, u32[]{:S(2)}, u32[]{:S(2)}) %collective-permute-start.5) | collective-permute-done | bytes 202784 | tf_op jit(solution)/shard_map/ppermute | solution.py:435
  20.4 0.6 %collective-permute-done.8.refs_1_ = bf16[3,32,192]{2,1,0:T(8,128)(2,1)S(1)} collective-permute-done((bf16[3,32,192]{2,1,0:T(8,128)(2,1)S(1)}, bf16[3,32,192]{2,1,0:T(8,128)(2,1)S(1)}, u32[]{:S(2)}, u32[]{:S(2)}) %collective-permute-start.8) | collective-permute-done | bytes 36896 | tf_op jit(solution)/shard_map/ppermute | solution.py:432
  21.4 1.2 %collective-permute-done.9.refs_2_ = bf16[3,32,192]{2,1,0:T(8,128)(2,1)S(1)} collective-permute-done((bf16[3,32,192]{2,1,0:T(8,128)(2,1)S(1)}, bf16[3,32,192]{2,1,0:T(8,128)(2,1)S(1)}, u32[]{:S(2)}, u32[]{:S(2)}) %collective-permute-start.9) | collective-permute-done | bytes 36896 | tf_op jit(solution)/shard_map/ppermute | solution.py:432
  23.3 1.6 %collective-permute-start.11 = (bf16[128,256]{1,0:T(8,128)(2,1)S(1)}, bf16[128,256]{1,0:T(8,128)(2,1)S(1)}, u32[]{:S(2)}, u32[]{:S(2)}) collective-permute-start(bf16[128,256]{1,0:T(8,128)(2,1)S(1)} %get-tuple-element.64), channel_id=1, source_target_pairs={{0,1},{1,2},{2,3},{3,0},{4,5},{5,6},{6,7},{7,4},{8,9},{9,10},{10,1... | collective-permute-start | bytes 196616 | tf_op jit(solution)/shard_map/ppermute | solution.py:432
  24.9 1.5 %collective-permute-start.12 = (bf16[128,256]{1,0:T(8,128)(2,1)S(1)}, bf16[128,256]{1,0:T(8,128)(2,1)S(1)}, u32[]{:S(2)}, u32[]{:S(2)}) collective-permute-start(bf16[128,256]{1,0:T(8,128)(2,1)S(1)} %get-tuple-element.65), channel_id=1, source_target_pairs={{0,2},{1,3},{2,0},{3,1},{4,6},{5,7},{6,4},{7,5},{8,10},{9,11},{10,... | collective-permute-start | bytes 196616 | tf_op jit(solution)/shard_map/ppermute | solution.py:432
  26.4 0.9 %collective-permute-start.13 = (bf16[128,256]{1,0:T(8,128)(2,1)S(1)}, bf16[128,256]{1,0:T(8,128)(2,1)S(1)}, u32[]{:S(2)}, u32[]{:S(2)}) collective-permute-start(bf16[128,256]{1,0:T(8,128)(2,1)S(1)} %get-tuple-element.66), channel_id=1, source_target_pairs={{0,3},{1,0},{2,1},{3,2},{4,7},{5,4},{6,5},{7,6},{8,11},{9,8},{10,9... | collective-permute-start | bytes 196616 | tf_op jit(solution)/shard_map/ppermute | solution.py:432
  27.4 7.4 %raw.1 = (f32[128,768]{1,0:T(8,128)S(1)}, f32[128,768]{1,0:T(8,128)S(1)}) custom-call(bf16[32,4224]{1,0:T(8,128)(2,1)S(1)} %pad_maximum_fusion.refs_0_, bf16[32,4224]{1,0:T(8,128)(2,1)S(1)} %constant_dynamic-update-slice_fusion.refs_1_, bf16[32,4224]{1,0:T(8,128)(2,1)S(1)} %collective-permute-done.6.refs_2_, ...), custom_call_target="tpu_custom_call" | custom-call | flops 1 | bytes 1 | tf_op jit(solution)/shard_map/raw/pallas_call | solution.py:203
  35.4 1.1 %collective-permute-start.16 = (bf16[64,128]{1,0:T(8,128)(2,1)S(1)}, bf16[64,128]{1,0:T(8,128)(2,1)S(1)}, u32[]{:S(2)}, u32[]{:S(2)}) collective-permute-start(bf16[64,128]{1,0:T(8,128)(2,1)S(1)} %get-tuple-element.77), channel_id=1, source_target_pairs={{0,8},{8,0},{1,9},{9,1},{2,10},{10,2},{3,11},{11,3},{4,12},{12,4},... | collective-permute-start | bytes 49160 | tf_op jit(solution)/shard_map/ppermute | solution.py:435
  36.5 1.0 %down.1 = (f32[64,4096]{1,0:T(8,128)S(1)}, bf16[64,4096]{1,0:T(8,128)(2,1)S(1)}) custom-call(bf16[128,768]{1,0:T(8,128)(2,1)S(1)} %get-tuple-element.72.hidden_ref, bf16[768,4096]{1,0:T(8,128)(2,1)S(1)} %bitcast.10), custom_call_target="tpu_custom_call" | custom-call | flops 1 | bytes 1 | tf_op jit(solution)/shard_map/down/pallas_call | solution.py:268
  37.6 1.6 %collective-permute-done.16.refs_1_ = bf16[64,128]{1,0:T(8,128)(2,1)S(1)} collective-permute-done((bf16[64,128]{1,0:T(8,128)(2,1)S(1)}, bf16[64,128]{1,0:T(8,128)(2,1)S(1)}, u32[]{:S(2)}, u32[]{:S(2)}) %collective-permute-start.16) | collective-permute-done | bytes 16416 | tf_op jit(solution)/shard_map/ppermute | solution.py:435
  39.2 1.2 %collective-permute-done.17.far_ref = bf16[32,256]{1,0:T(8,128)(2,1)S(1)} collective-permute-done((bf16[32,256]{1,0:T(8,128)(2,1)S(1)}, bf16[32,256]{1,0:T(8,128)(2,1)S(1)}, u32[]{:S(2)}, u32[]{:S(2)}) %collective-permute-start.17) | collective-permute-done | bytes 16416 | tf_op jit(solution)/shard_map/ppermute | solution.py:438
  40.7 1.1 %collective-permute-start.22 = (bf16[24,4096]{1,0:T(8,128)(2,1)S(1)}, bf16[24,4096]{1,0:T(8,128)(2,1)S(1)}, u32[]{:S(2)}, u32[]{:S(2)}) collective-permute-start(bf16[24,4096]{1,0:T(8,128)(2,1)S(1)} %get-tuple-element.85), channel_id=1, source_target_pairs={{0,8},{8,0},{1,9},{9,1},{2,10},{10,2},{3,11},{11,3},{4,12},{12,4},... | collective-permute-start | bytes 589832 | tf_op jit(solution)/shard_map/ppermute | solution.py:435
  41.8 0.9 %collective-permute-start.19 = (bf16[32,512]{1,0:T(8,128)(2,1)S(1)}, bf16[32,512]{1,0:T(8,128)(2,1)S(1)}, u32[]{:S(2)}, u32[]{:S(2)}) collective-permute-start(bf16[32,512]{1,0:T(8,128)(2,1)S(1)} %get-tuple-element.82), channel_id=1, source_target_pairs={{0,1},{1,2},{2,3},{3,0},{4,5},{5,6},{6,7},{7,4},{8,9},{9,10},{10,1... | collective-permute-start | bytes 98312 | tf_op jit(solution)/shard_map/ppermute | solution.py:432
  42.7 1.4 %collective-permute-start.20 = (bf16[32,512]{1,0:T(8,128)(2,1)S(1)}, bf16[32,512]{1,0:T(8,128)(2,1)S(1)}, u32[]{:S(2)}, u32[]{:S(2)}) collective-permute-start(bf16[32,512]{1,0:T(8,128)(2,1)S(1)} %get-tuple-element.83), channel_id=1, source_target_pairs={{0,2},{1,3},{2,0},{3,1},{4,6},{5,7},{6,4},{7,5},{8,10},{9,11},{10,... | collective-permute-start | bytes 98312 | tf_op jit(solution)/shard_map/ppermute | solution.py:432
  44.2 2.5 %collective-permute-start.21 = (bf16[32,512]{1,0:T(8,128)(2,1)S(1)}, bf16[32,512]{1,0:T(8,128)(2,1)S(1)}, u32[]{:S(2)}, u32[]{:S(2)}) collective-permute-start(bf16[32,512]{1,0:T(8,128)(2,1)S(1)} %get-tuple-element.84), channel_id=1, source_target_pairs={{0,3},{1,0},{2,1},{3,2},{4,7},{5,4},{6,5},{7,6},{8,11},{9,8},{10,9... | collective-permute-start | bytes 98312 | tf_op jit(solution)/shard_map/ppermute | solution.py:432
  46.6 1.3 %collective-permute-done.19.refs_0_ = bf16[32,512]{1,0:T(8,128)(2,1)S(1)} collective-permute-done((bf16[32,512]{1,0:T(8,128)(2,1)S(1)}, bf16[32,512]{1,0:T(8,128)(2,1)S(1)}, u32[]{:S(2)}, u32[]{:S(2)}) %collective-permute-start.19) | collective-permute-done | bytes 32800 | tf_op jit(solution)/shard_map/ppermute | solution.py:432
  48.0 0.9 %collective-permute-start.23 = (bf16[8,4096]{1,0:T(8,128)(2,1)S(1)}, bf16[8,4096]{1,0:T(8,128)(2,1)S(1)}, u32[]{:S(2)}, u32[]{:S(2)}) collective-permute-start(bf16[8,4096]{1,0:T(8,128)(2,1)S(1)} %get-tuple-element.87), channel_id=1, source_target_pairs={{0,8},{8,0},{1,9},{9,1},{2,10},{10,2},{3,11},{11,3},{4,12},{12,4},... | collective-permute-start | bytes 196616 | tf_op jit(solution)/shard_map/ppermute | solution.py:435
  49.2 1.3 %collective-permute-start.26 = (bf16[8,4096]{1,0:T(8,128)(2,1)S(1)}, bf16[8,4096]{1,0:T(8,128)(2,1)S(1)}, u32[]{:S(2)}, u32[]{:S(2)}) collective-permute-start(bf16[8,4096]{1,0:T(8,128)(2,1)S(1)} %get-tuple-element.90), channel_id=1, source_target_pairs={{0,1},{1,2},{2,3},{3,0},{4,5},{5,6},{6,7},{7,4},{8,9},{9,10},{10,1... | collective-permute-start | bytes 196616 | tf_op jit(solution)/shard_map/ppermute | solution.py:432
  50.5 2.8 %collective-permute-start.25 = (bf16[8,4096]{1,0:T(8,128)(2,1)S(1)}, bf16[8,4096]{1,0:T(8,128)(2,1)S(1)}, u32[]{:S(2)}, u32[]{:S(2)}) collective-permute-start(bf16[8,4096]{1,0:T(8,128)(2,1)S(1)} %get-tuple-element.89), channel_id=1, source_target_pairs={{0,2},{1,3},{2,0},{3,1},{4,6},{5,7},{6,4},{7,5},{8,10},{9,11},{10,... | collective-permute-start | bytes 196616 | tf_op jit(solution)/shard_map/ppermute | solution.py:432
  53.4 2.2 %collective-permute-done.26 = bf16[8,4096]{1,0:T(8,128)(2,1)S(1)} collective-permute-done((bf16[8,4096]{1,0:T(8,128)(2,1)S(1)}, bf16[8,4096]{1,0:T(8,128)(2,1)S(1)}, u32[]{:S(2)}, u32[]{:S(2)}) %collective-permute-start.26) | collective-permute-done | bytes 65568 | tf_op jit(solution)/shard_map/ppermute | solution.py:432
  55.6 1.6 %collective-permute-done.25 = bf16[8,4096]{1,0:T(8,128)(2,1)S(1)} collective-permute-done((bf16[8,4096]{1,0:T(8,128)(2,1)S(1)}, bf16[8,4096]{1,0:T(8,128)(2,1)S(1)}, u32[]{:S(2)}, u32[]{:S(2)}) %collective-permute-start.25) | collective-permute-done | bytes 65568 | tf_op jit(solution)/shard_map/ppermute | solution.py:432
  57.2 0.7 %collective-permute-done.24 = bf16[8,4096]{1,0:T(8,128)(2,1)S(1)} collective-permute-done((bf16[8,4096]{1,0:T(8,128)(2,1)S(1)}, bf16[8,4096]{1,0:T(8,128)(2,1)S(1)}, u32[]{:S(2)}, u32[]{:S(2)}) %collective-permute-start.24) | collective-permute-done | bytes 65568 | tf_op jit(solution)/shard_map/ppermute | solution.py:432
  57.8 0.7 %add_convert_fusion = bf16[8,4096]{1,0:T(8,128)(2,1)} fusion(bf16[8,4096]{1,0:T(8,128)(2,1)S(1)} %collective-permute-done.26, bf16[8,4096]{1,0:T(8,128)(2,1)S(1)} %collective-permute-done.25, f32[8,4096]{1,0:T(8,128)S(1)} %plus.1, bf16[8,4096]{1,0:T(8,128)(2,1)S(1)} %collective-permute-done.24), kind=kLoop, calls=%fused_computation.2 | loop fusion | flops 229376 | bytes 393216 | tf_op jit(solution)/shard_map/convert_element_type | solution.py:486
  (47 shorter events, 2.7 us)
Async XLA Ops:
  0.0 21.0 %copy-start = (bf16[4,32,1024]{2,1,0:T(8,128)(2,1)S(1)}, bf16[4,32,1024]{2,1,0:T(8,128)(2,1)}, u32[]{:S(2)}) copy-start(bf16[4,32,1024]{2,1,0:T(8,128)(2,1)} %param.23) | copy-start | bytes 786436
  1.0 11.7 %collective-permute-start.2 = (bf16[8,4224]{1,0:T(8,128)(2,1)S(1)}, bf16[8,4224]{1,0:T(8,128)(2,1)S(1)}, u32[]{:S(2)}, u32[]{:S(2)}) collective-permute-start(bf16[8,4224]{1,0:T(8,128)(2,1)S(1)} %attach.1), channel_id=1, source_target_pairs={{0,3},{1,0},{2,1},{3,2},{4,7},{5,4},{6,5},{7,6},{8,11},{9,8},{10,9... | collective-permute-start | bytes 202760 | tf_op jit(solution)/shard_map/ppermute | solution.py:432
  6.1 6.6 %collective-permute-start.1 = (bf16[8,4224]{1,0:T(8,128)(2,1)S(1)}, bf16[8,4224]{1,0:T(8,128)(2,1)S(1)}, u32[]{:S(2)}, u32[]{:S(2)}) collective-permute-start(bf16[8,4224]{1,0:T(8,128)(2,1)S(1)} %attach.1), channel_id=1, source_target_pairs={{0,2},{1,3},{2,0},{3,1},{4,6},{5,7},{6,4},{7,5},{8,10},{9,11},{10,... | collective-permute-start | bytes 202760 | tf_op jit(solution)/shard_map/ppermute | solution.py:432
  6.1 6.6 %collective-permute-start = (bf16[8,4224]{1,0:T(8,128)(2,1)S(1)}, bf16[8,4224]{1,0:T(8,128)(2,1)S(1)}, u32[]{:S(2)}, u32[]{:S(2)}) collective-permute-start(bf16[8,4224]{1,0:T(8,128)(2,1)S(1)} %attach.1), channel_id=1, source_target_pairs={{0,1},{1,2},{2,3},{3,0},{4,5},{5,6},{6,7},{7,4},{8,9},{9,10},{10,1... | collective-permute-start | bytes 202760 | tf_op jit(solution)/shard_map/ppermute | solution.py:432
  7.1 5.7 %collective-permute-start.4 = (bf16[8,4224]{1,0:T(8,128)(2,1)S(1)}, bf16[8,4224]{1,0:T(8,128)(2,1)S(1)}, u32[]{:S(2)}, u32[]{:S(2)}) collective-permute-start(bf16[8,4224]{1,0:T(8,128)(2,1)S(1)} %attach.1), channel_id=1, source_target_pairs={{0,8},{8,0},{1,9},{9,1},{2,10},{10,2},{3,11},{11,3},{4,12},{12,4},... | collective-permute-start | bytes 202760 | tf_op jit(solution)/shard_map/ppermute | solution.py:435
  8.6 4.2 %collective-permute-start.3 = (bf16[128,1024]{1,0:T(8,128)(2,1)}, bf16[128,1024]{1,0:T(8,128)(2,1)S(1)}, u32[]{:S(2)}, u32[]{:S(2)}) collective-permute-start(bf16[128,1024]{1,0:T(8,128)(2,1)} %bitcast.11), channel_id=1, source_target_pairs={{0,4},{4,0},{1,5},{5,1},{2,6},{6,2},{3,7},{7,3},{8,12},{12,8},{9,1... | collective-permute-start | bytes 786440 | tf_op jit(solution)/shard_map/ppermute | solution.py:438
  12.8 7.5 %collective-permute-start.5 = (bf16[24,4224]{1,0:T(8,128)(2,1)S(1)}, bf16[24,4224]{1,0:T(8,128)(2,1)S(1)}, u32[]{:S(2)}, u32[]{:S(2)}) collective-permute-start(bf16[24,4224]{1,0:T(8,128)(2,1)S(1)} %pad_maximum_fusion.1), channel_id=1, source_target_pairs={{0,8},{8,0},{1,9},{9,1},{2,10},{10,2},{3,11},{11,3},{4,12},{12,4},... | collective-permute-start | bytes 608264 | tf_op jit(solution)/shard_map/ppermute | solution.py:435
  14.4 8.6 %collective-permute-start.6 = (bf16[32,4224]{1,0:T(8,128)(2,1)S(1)}, bf16[32,4224]{1,0:T(8,128)(2,1)S(1)}, u32[]{:S(2)}, u32[]{:S(2)}) collective-permute-start(bf16[32,4224]{1,0:T(8,128)(2,1)S(1)} %pad_maximum_fusion.refs_0_), channel_id=1, source_target_pairs={{0,4},{4,0},{1,5},{5,1},{2,6},{6,2},{3,7},{7,3},{8,12},{12,8},{9,1... | collective-permute-start | bytes 811016 | tf_op jit(solution)/shard_map/ppermute | solution.py:438
  14.5 6.5 %collective-permute-start.8 = (bf16[3,32,192]{2,1,0:T(8,128)(2,1)S(1)}, bf16[3,32,192]{2,1,0:T(8,128)(2,1)S(1)}, u32[]{:S(2)}, u32[]{:S(2)}) collective-permute-start(bf16[3,32,192]{2,1,0:T(8,128)(2,1)S(1)} %get-tuple-element.56), channel_id=1, source_target_pairs={{0,1},{1,2},{2,3},{3,0},{4,5},{5,6},{6,7},{7,4},{8,9},{9,10},{10,1... | collective-permute-start | bytes 110600 | tf_op jit(solution)/shard_map/ppermute | solution.py:432
  16.2 6.5 %collective-permute-start.9 = (bf16[3,32,192]{2,1,0:T(8,128)(2,1)S(1)}, bf16[3,32,192]{2,1,0:T(8,128)(2,1)S(1)}, u32[]{:S(2)}, u32[]{:S(2)}) collective-permute-start(bf16[3,32,192]{2,1,0:T(8,128)(2,1)S(1)} %get-tuple-element.57), channel_id=1, source_target_pairs={{0,2},{1,3},{2,0},{3,1},{4,6},{5,7},{6,4},{7,5},{8,10},{9,11},{10,... | collective-permute-start | bytes 110600 | tf_op jit(solution)/shard_map/ppermute | solution.py:432
  17.1 5.6 %collective-permute-start.10 = (bf16[3,32,192]{2,1,0:T(8,128)(2,1)S(1)}, bf16[3,32,192]{2,1,0:T(8,128)(2,1)S(1)}, u32[]{:S(2)}, u32[]{:S(2)}) collective-permute-start(bf16[3,32,192]{2,1,0:T(8,128)(2,1)S(1)} %get-tuple-element.58), channel_id=1, source_target_pairs={{0,3},{1,0},{2,1},{3,2},{4,7},{5,4},{6,5},{7,6},{8,11},{9,8},{10,9... | collective-permute-start | bytes 110600 | tf_op jit(solution)/shard_map/ppermute | solution.py:432
  20.3 2.7 %collective-permute-start.7 = (bf16[32,4224]{1,0:T(8,128)(2,1)S(1)}, bf16[32,4224]{1,0:T(8,128)(2,1)S(1)}, u32[]{:S(2)}, u32[]{:S(2)}) collective-permute-start(bf16[32,4224]{1,0:T(8,128)(2,1)S(1)} %constant_dynamic-update-slice_fusion.refs_1_), channel_id=1, source_target_pairs={{0,4},{4,0},{1,5},{5,1},{2,6},{6,2},{3,7},{7,3},{8,12},{12,8},{9,1... | collective-permute-start | bytes 811016 | tf_op jit(solution)/shard_map/ppermute | solution.py:438
  21.0 13.8 %collective-permute-start.14 = (bf16[128,1024]{1,0:T(8,128)(2,1)S(1)}, bf16[128,1024]{1,0:T(8,128)(2,1)S(1)}, u32[]{:S(2)}, u32[]{:S(2)}) collective-permute-start(bf16[128,1024]{1,0:T(8,128)(2,1)S(1)} %bitcast.12), channel_id=1, source_target_pairs={{0,8},{8,0},{1,9},{9,1},{2,10},{10,2},{3,11},{11,3},{4,12},{12,4},... | collective-permute-start | bytes 786440 | tf_op jit(solution)/shard_map/ppermute | solution.py:435
  23.3 11.5 %collective-permute-start.11 = (bf16[128,256]{1,0:T(8,128)(2,1)S(1)}, bf16[128,256]{1,0:T(8,128)(2,1)S(1)}, u32[]{:S(2)}, u32[]{:S(2)}) collective-permute-start(bf16[128,256]{1,0:T(8,128)(2,1)S(1)} %get-tuple-element.64), channel_id=1, source_target_pairs={{0,1},{1,2},{2,3},{3,0},{4,5},{5,6},{6,7},{7,4},{8,9},{9,10},{10,1... | collective-permute-start | bytes 196616 | tf_op jit(solution)/shard_map/ppermute | solution.py:432
  24.9 9.9 %collective-permute-start.12 = (bf16[128,256]{1,0:T(8,128)(2,1)S(1)}, bf16[128,256]{1,0:T(8,128)(2,1)S(1)}, u32[]{:S(2)}, u32[]{:S(2)}) collective-permute-start(bf16[128,256]{1,0:T(8,128)(2,1)S(1)} %get-tuple-element.65), channel_id=1, source_target_pairs={{0,2},{1,3},{2,0},{3,1},{4,6},{5,7},{6,4},{7,5},{8,10},{9,11},{10,... | collective-permute-start | bytes 196616 | tf_op jit(solution)/shard_map/ppermute | solution.py:432
  26.4 8.4 %collective-permute-start.13 = (bf16[128,256]{1,0:T(8,128)(2,1)S(1)}, bf16[128,256]{1,0:T(8,128)(2,1)S(1)}, u32[]{:S(2)}, u32[]{:S(2)}) collective-permute-start(bf16[128,256]{1,0:T(8,128)(2,1)S(1)} %get-tuple-element.66), channel_id=1, source_target_pairs={{0,3},{1,0},{2,1},{3,2},{4,7},{5,4},{6,5},{7,6},{8,11},{9,8},{10,9... | collective-permute-start | bytes 196616 | tf_op jit(solution)/shard_map/ppermute | solution.py:432
  27.4 9.1 %slice-start = ((s8[6291456]{0:T(1024)(128)(4,1)}), s8[4194304]{0:T(1024)(128)(4,1)S(1)}, s32[]{:S(2)}) async-start(s8[6291456]{0:T(1024)(128)(4,1)} %bitcast.8), calls=%async_computation | async-start | bytes 8388608
  27.4 9.1 %slice-start.1 = ((s8[6291456]{0:T(1024)(128)(4,1)}), s8[2097152]{0:T(1024)(128)(4,1)S(1)}, s32[]{:S(2)}) async-start(s8[6291456]{0:T(1024)(128)(4,1)} %bitcast.8), calls=%async_computation.1 | async-start | bytes 4194304
  35.4 3.8 %collective-permute-start.16 = (bf16[64,128]{1,0:T(8,128)(2,1)S(1)}, bf16[64,128]{1,0:T(8,128)(2,1)S(1)}, u32[]{:S(2)}, u32[]{:S(2)}) collective-permute-start(bf16[64,128]{1,0:T(8,128)(2,1)S(1)} %get-tuple-element.77), channel_id=1, source_target_pairs={{0,8},{8,0},{1,9},{9,1},{2,10},{10,2},{3,11},{11,3},{4,12},{12,4},... | collective-permute-start | bytes 49160 | tf_op jit(solution)/shard_map/ppermute | solution.py:435
  37.5 3.1 %collective-permute-start.15 = (bf16[64,4096]{1,0:T(8,128)(2,1)S(1)}, bf16[64,4096]{1,0:T(8,128)(2,1)S(1)}, u32[]{:S(2)}, u32[]{:S(2)}) collective-permute-start(bf16[64,4096]{1,0:T(8,128)(2,1)S(1)} %get-tuple-element.74), channel_id=1, source_target_pairs={{0,4},{4,0},{1,5},{5,1},{2,6},{6,2},{3,7},{7,3},{8,12},{12,8},{9,1... | collective-permute-start | bytes 1572872 | tf_op jit(solution)/shard_map/ppermute | solution.py:438
  39.2 1.2 %collective-permute-start.17 = (bf16[32,256]{1,0:T(8,128)(2,1)S(1)}, bf16[32,256]{1,0:T(8,128)(2,1)S(1)}, u32[]{:S(2)}, u32[]{:S(2)}) collective-permute-start(bf16[32,256]{1,0:T(8,128)(2,1)S(1)} %get-tuple-element.79), channel_id=1, source_target_pairs={{0,4},{4,0},{1,5},{5,1},{2,6},{6,2},{3,7},{7,3},{8,12},{12,8},{9,1... | collective-permute-start | bytes 49160 | tf_op jit(solution)/shard_map/ppermute | solution.py:438
  40.4 8.5 %collective-permute-start.18 = (bf16[128,1024]{1,0:T(8,128)(2,1)S(1)}, bf16[128,1024]{1,0:T(8,128)(2,1)S(1)}, u32[]{:S(2)}, u32[]{:S(2)}) collective-permute-start(bf16[128,1024]{1,0:T(8,128)(2,1)S(1)} %collective-permute-done.14.refs_2_), channel_id=1, source_target_pairs={{0,4},{4,0},{1,5},{5,1},{2,6},{6,2},{3,7},{7,3},{8,12},{12,8},{9,1... | collective-permute-start | bytes 786440 | tf_op jit(solution)/shard_map/ppermute | solution.py:438
  40.7 8.2 %collective-permute-start.22 = (bf16[24,4096]{1,0:T(8,128)(2,1)S(1)}, bf16[24,4096]{1,0:T(8,128)(2,1)S(1)}, u32[]{:S(2)}, u32[]{:S(2)}) collective-permute-start(bf16[24,4096]{1,0:T(8,128)(2,1)S(1)} %get-tuple-element.85), channel_id=1, source_target_pairs={{0,8},{8,0},{1,9},{9,1},{2,10},{10,2},{3,11},{11,3},{4,12},{12,4},... | collective-permute-start | bytes 589832 | tf_op jit(solution)/shard_map/ppermute | solution.py:435
  41.8 6.1 %collective-permute-start.19 = (bf16[32,512]{1,0:T(8,128)(2,1)S(1)}, bf16[32,512]{1,0:T(8,128)(2,1)S(1)}, u32[]{:S(2)}, u32[]{:S(2)}) collective-permute-start(bf16[32,512]{1,0:T(8,128)(2,1)S(1)} %get-tuple-element.82), channel_id=1, source_target_pairs={{0,1},{1,2},{2,3},{3,0},{4,5},{5,6},{6,7},{7,4},{8,9},{9,10},{10,1... | collective-permute-start | bytes 98312 | tf_op jit(solution)/shard_map/ppermute | solution.py:432
  42.7 6.2 %collective-permute-start.20 = (bf16[32,512]{1,0:T(8,128)(2,1)S(1)}, bf16[32,512]{1,0:T(8,128)(2,1)S(1)}, u32[]{:S(2)}, u32[]{:S(2)}) collective-permute-start(bf16[32,512]{1,0:T(8,128)(2,1)S(1)} %get-tuple-element.83), channel_id=1, source_target_pairs={{0,2},{1,3},{2,0},{3,1},{4,6},{5,7},{6,4},{7,5},{8,10},{9,11},{10,... | collective-permute-start | bytes 98312 | tf_op jit(solution)/shard_map/ppermute | solution.py:432
  44.2 4.7 %collective-permute-start.21 = (bf16[32,512]{1,0:T(8,128)(2,1)S(1)}, bf16[32,512]{1,0:T(8,128)(2,1)S(1)}, u32[]{:S(2)}, u32[]{:S(2)}) collective-permute-start(bf16[32,512]{1,0:T(8,128)(2,1)S(1)} %get-tuple-element.84), channel_id=1, source_target_pairs={{0,3},{1,0},{2,1},{3,2},{4,7},{5,4},{6,5},{7,6},{8,11},{9,8},{10,9... | collective-permute-start | bytes 98312 | tf_op jit(solution)/shard_map/ppermute | solution.py:432
  48.0 5.4 %collective-permute-start.23 = (bf16[8,4096]{1,0:T(8,128)(2,1)S(1)}, bf16[8,4096]{1,0:T(8,128)(2,1)S(1)}, u32[]{:S(2)}, u32[]{:S(2)}) collective-permute-start(bf16[8,4096]{1,0:T(8,128)(2,1)S(1)} %get-tuple-element.87), channel_id=1, source_target_pairs={{0,8},{8,0},{1,9},{9,1},{2,10},{10,2},{3,11},{11,3},{4,12},{12,4},... | collective-permute-start | bytes 196616 | tf_op jit(solution)/shard_map/ppermute | solution.py:435
  49.2 6.4 %collective-permute-start.26 = (bf16[8,4096]{1,0:T(8,128)(2,1)S(1)}, bf16[8,4096]{1,0:T(8,128)(2,1)S(1)}, u32[]{:S(2)}, u32[]{:S(2)}) collective-permute-start(bf16[8,4096]{1,0:T(8,128)(2,1)S(1)} %get-tuple-element.90), channel_id=1, source_target_pairs={{0,1},{1,2},{2,3},{3,0},{4,5},{5,6},{6,7},{7,4},{8,9},{9,10},{10,1... | collective-permute-start | bytes 196616 | tf_op jit(solution)/shard_map/ppermute | solution.py:432
  50.5 6.7 %collective-permute-start.25 = (bf16[8,4096]{1,0:T(8,128)(2,1)S(1)}, bf16[8,4096]{1,0:T(8,128)(2,1)S(1)}, u32[]{:S(2)}, u32[]{:S(2)}) collective-permute-start(bf16[8,4096]{1,0:T(8,128)(2,1)S(1)} %get-tuple-element.89), channel_id=1, source_target_pairs={{0,2},{1,3},{2,0},{3,1},{4,6},{5,7},{6,4},{7,5},{8,10},{9,11},{10,... | collective-permute-start | bytes 196616 | tf_op jit(solution)/shard_map/ppermute | solution.py:432
  53.3 4.6 %collective-permute-start.24 = (bf16[8,4096]{1,0:T(8,128)(2,1)S(1)}, bf16[8,4096]{1,0:T(8,128)(2,1)S(1)}, u32[]{:S(2)}, u32[]{:S(2)}) collective-permute-start(bf16[8,4096]{1,0:T(8,128)(2,1)S(1)} %get-tuple-element.88), channel_id=1, source_target_pairs={{0,3},{1,0},{2,1},{3,2},{4,7},{5,4},{6,5},{7,6},{8,11},{9,8},{10,9... | collective-permute-start | bytes 196616 | tf_op jit(solution)/shard_map/ppermute | solution.py:432

commit v18 on v16

--- a/solution.py
+++ b/solution.py
@@ -15,6 +15,7 @@
 LONG = pl.CostEstimate(flops=1_000_000_000, bytes_accessed=1, transcendentals=0)
 LONGER = pl.CostEstimate(flops=10_000_000_000, bytes_accessed=1, transcendentals=0)
 LAST = pl.CostEstimate(flops=1_000_000_000, bytes_accessed=1, transcendentals=0)
+SOME = pl.CostEstimate(flops=3_000_000_000, bytes_accessed=1, transcendentals=0)
 BRIEF = pl.CostEstimate(flops=1, bytes_accessed=1, transcendentals=0)
 
 
@@ -96,7 +97,7 @@
         out_shape=pltpu.VMEM(weights.shape, weights.dtype),
         scratch_shapes=[pltpu.SemaphoreType.DMA((PIECES,))],
         compiler_params=pltpu.CompilerParams(vmem_limit_bytes=SMALL_LIMIT),
-        cost_estimate=BRIEF,
+        cost_estimate=SOME,
         name="load",
     )(*in_hbm(weights))
 
@@ -171,7 +172,7 @@
         functools.partial(spread_kernel, parts, exp_dev),
         out_shape=jax.ShapeDtypeStruct((3, span * parts, cols * exp_dev), BF),
         compiler_params=pltpu.CompilerParams(vmem_limit_bytes=SMALL_LIMIT),
-        cost_estimate=BRIEF,
+        cost_estimate=SOME,
         name="spread",
     )(*pieces)
 
@@ -465,7 +466,7 @@
     for s in range(1, chips):
         line = jnp.concatenate([first[s - 1], along_y(rest, s)])
         arrival = line
-        line = after(line, (tuple(small), up_w))
+        line = after(line, up_w)
         lines.append(line)
         partner.append(other_core(line))
     lines += partner

time: 56.8 us -> 56.3 us (level)
  no operation moved by 1% of the time
where the time goes in v18:
time: 56.3 us; the launch traced here: 56.1 us
  starting transfers between devices  30.8 us (55%)
  Pallas kernels  14 us (25%)
  waiting for transfers between devices  10.3 us (18%)
  other arithmetic  0.71 us (1%)
    ppermute x15, starting transfers between devices, along_z(): lax.ppermute(value, 'mp', [(i, (i + step) % parts) for i in range(parts)])  23.2 us
    ppermute x15, waiting for transfers between devices, along_z(): lax.ppermute(value, 'mp', [(i, (i + step) % parts) for i in range(parts)])  7.33 us
    ppermute x6, starting transfers between devices, along_y(): lax.ppermute(value, 'y', [(i, (i + step) % chips) for i in range(chips)])  7.2 us
    pallas_call x1, Pallas kernels, prepare(): pl.pallas_call(functools.partial(prepare_kernel, parts), in_specs=[vmem]...  4.06 us
    pallas_call x1, Pallas kernels, raw_products(): pl.pallas_call(functools.partial(raw_kernel, len(lines), tile), out_shape...  3.51 us
    pallas_call x1, Pallas kernels, load(): pl.pallas_call(load_kernel, in_specs=[pl.BlockSpec(memory_space=pltpu.HBM...  2.86 us
    ppermute x6, waiting for transfers between devices, along_y(): lax.ppermute(value, 'y', [(i, (i + step) % chips) for i in range(chips)])  1.61 us
    ppermute x6, waiting for transfers between devices, other_core(): return lax.ppermute(value, 'core', [(0, 1), (1, 0)])  1.35 us
  transfers between devices with their start and end apart: 27, of which 8 were waited for; matrix products, arithmetic and copies ran while one was open for 0% of the time, Pallas kernels for 22%

profile of v18, /device:TPU:0, one launch (start us, length us, event | category | flops | bytes accessed | tf_op | source)
XLA Modules:
  0.0 56.1 jit_solution(9302329904630479629)
XLA Ops:
  0.0 0.9 %attach.1 = bf16[8,4224]{1,0:T(8,128)(2,1)S(1)} custom-call(bf16[8,4096]{1,0:T(8,128)(2,1)} %tokens_ref.1, s32[8,8]{1,0:T(8,128)} %routes_ref.1, f32[8,8]{1,0:T(8,128)} %probs_ref.1), custom_call_target="tpu_custom_call" | custom-call | flops 1 | bytes 1 | tf_op jit(solution)/shard_map/attach/pallas_call | solution.py:66
  1.0 5.1 %collective-permute-start.2 = (bf16[8,4224]{1,0:T(8,128)(2,1)S(1)}, bf16[8,4224]{1,0:T(8,128)(2,1)S(1)}, u32[]{:S(2)}, u32[]{:S(2)}) collective-permute-start(bf16[8,4224]{1,0:T(8,128)(2,1)S(1)} %attach.1), channel_id=1, source_target_pairs={{0,3},{1,0},{2,1},{3,2},{4,7},{5,4},{6,5},{7,6},{8,11},{9,8},{10,9... | collective-permute-start | bytes 202760 | tf_op jit(solution)/shard_map/ppermute | solution.py:442
  6.1 1.0 %collective-permute-start = (bf16[8,4224]{1,0:T(8,128)(2,1)S(1)}, bf16[8,4224]{1,0:T(8,128)(2,1)S(1)}, u32[]{:S(2)}, u32[]{:S(2)}) collective-permute-start(bf16[8,4224]{1,0:T(8,128)(2,1)S(1)} %attach.1), channel_id=1, source_target_pairs={{0,1},{1,2},{2,3},{3,0},{4,5},{5,6},{6,7},{7,4},{8,9},{9,10},{10,1... | collective-permute-start | bytes 202760 | tf_op jit(solution)/shard_map/ppermute | solution.py:442
  7.1 1.5 %collective-permute-start.4 = (bf16[8,4224]{1,0:T(8,128)(2,1)S(1)}, bf16[8,4224]{1,0:T(8,128)(2,1)S(1)}, u32[]{:S(2)}, u32[]{:S(2)}) collective-permute-start(bf16[8,4224]{1,0:T(8,128)(2,1)S(1)} %attach.1), channel_id=1, source_target_pairs={{0,8},{8,0},{1,9},{9,1},{2,10},{10,2},{3,11},{11,3},{4,12},{12,4},... | collective-permute-start | bytes 202760 | tf_op jit(solution)/shard_map/ppermute | solution.py:445
  8.6 4.1 %prepare.1 = (bf16[768,4096]{1,0:T(8,128)(2,1)S(1)}, bf16[256,1024]{1,0:T(8,128)(2,1)S(1)}, bf16[3,32,192]{2,1,0:T(8,128)(2,1)S(1)}, bf16[3,32,192]{2,1,0:T(8,12...) custom-call(bf16[4,8,768]{2,1,0:T(8,128)(2,1)} %refs_0_.1, bf16[4,8,768]{2,1,0:T(8,128)(2,1)} %refs_1_.1, ...), custom_call_target="tpu_custom_call" | custom-call | flops 1 | bytes 1 | tf_op jit(solution)/shard_map/prepare/pallas_call | solution.py:134
  12.8 1.6 %collective-permute-start.5 = (bf16[24,4224]{1,0:T(8,128)(2,1)S(1)}, bf16[24,4224]{1,0:T(8,128)(2,1)S(1)}, u32[]{:S(2)}, u32[]{:S(2)}) collective-permute-start(bf16[24,4224]{1,0:T(8,128)(2,1)S(1)} %pad_maximum_fusion.1), channel_id=1, source_target_pairs={{0,8},{8,0},{1,9},{9,1},{2,10},{10,2},{3,11},{11,3},{4,12},{12,4},... | collective-permute-start | bytes 608264 | tf_op jit(solution)/shard_map/ppermute | solution.py:445
  14.4 1.7 %collective-permute-start.8 = (bf16[3,32,192]{2,1,0:T(8,128)(2,1)S(1)}, bf16[3,32,192]{2,1,0:T(8,128)(2,1)S(1)}, u32[]{:S(2)}, u32[]{:S(2)}) collective-permute-start(bf16[3,32,192]{2,1,0:T(8,128)(2,1)S(1)} %get-tuple-element.60), channel_id=1, source_target_pairs={{0,1},{1,2},{2,3},{3,0},{4,5},{5,6},{6,7},{7,4},{8,9},{9,10},{10,1... | collective-permute-start | bytes 110600 | tf_op jit(solution)/shard_map/ppermute | solution.py:442
  16.1 0.9 %collective-permute-start.9 = (bf16[3,32,192]{2,1,0:T(8,128)(2,1)S(1)}, bf16[3,32,192]{2,1,0:T(8,128)(2,1)S(1)}, u32[]{:S(2)}, u32[]{:S(2)}) collective-permute-start(bf16[3,32,192]{2,1,0:T(8,128)(2,1)S(1)} %get-tuple-element.61), channel_id=1, source_target_pairs={{0,2},{1,3},{2,0},{3,1},{4,6},{5,7},{6,4},{7,5},{8,10},{9,11},{10,... | collective-permute-start | bytes 110600 | tf_op jit(solution)/shard_map/ppermute | solution.py:442
  17.0 2.1 %collective-permute-start.10 = (bf16[3,32,192]{2,1,0:T(8,128)(2,1)S(1)}, bf16[3,32,192]{2,1,0:T(8,128)(2,1)S(1)}, u32[]{:S(2)}, u32[]{:S(2)}) collective-permute-start(bf16[3,32,192]{2,1,0:T(8,128)(2,1)S(1)} %get-tuple-element.62), channel_id=1, source_target_pairs={{0,3},{1,0},{2,1},{3,2},{4,7},{5,4},{6,5},{7,6},{8,11},{9,8},{10,9... | collective-permute-start | bytes 110600 | tf_op jit(solution)/shard_map/ppermute | solution.py:442
  19.1 2.9 %load.1.refs_5_ = bf16[768,4096]{1,0:T(8,128)(2,1)S(1)} custom-call(bf16[768,4096]{1,0:T(8,128)(2,1)} %bitcast.14), custom_call_target="tpu_custom_call" | custom-call | flops 3000000000 | bytes 1 | tf_op jit(solution)/shard_map/load/pallas_call | solution.py:93
  22.1 1.0 %collective-permute-start.14 = (bf16[128,1024]{1,0:T(8,128)(2,1)S(1)}, bf16[128,1024]{1,0:T(8,128)(2,1)S(1)}, u32[]{:S(2)}, u32[]{:S(2)}) collective-permute-start(bf16[128,1024]{1,0:T(8,128)(2,1)S(1)} %bitcast.12), channel_id=1, source_target_pairs={{0,8},{8,0},{1,9},{9,1},{2,10},{10,2},{3,11},{11,3},{4,12},{12,4},... | collective-permute-start | bytes 786440 | tf_op jit(solution)/shard_map/ppermute | solution.py:445
  23.9 0.9 %collective-permute-start.11 = (bf16[128,256]{1,0:T(8,128)(2,1)S(1)}, bf16[128,256]{1,0:T(8,128)(2,1)S(1)}, u32[]{:S(2)}, u32[]{:S(2)}) collective-permute-start(bf16[128,256]{1,0:T(8,128)(2,1)S(1)} %get-tuple-element.68), channel_id=1, source_target_pairs={{0,1},{1,2},{2,3},{3,0},{4,5},{5,6},{6,7},{7,4},{8,9},{9,10},{10,1... | collective-permute-start | bytes 196616 | tf_op jit(solution)/shard_map/ppermute | solution.py:442
  24.8 1.5 %collective-permute-start.12 = (bf16[128,256]{1,0:T(8,128)(2,1)S(1)}, bf16[128,256]{1,0:T(8,128)(2,1)S(1)}, u32[]{:S(2)}, u32[]{:S(2)}) collective-permute-start(bf16[128,256]{1,0:T(8,128)(2,1)S(1)} %get-tuple-element.69), channel_id=1, source_target_pairs={{0,2},{1,3},{2,0},{3,1},{4,6},{5,7},{6,4},{7,5},{8,10},{9,11},{10,... | collective-permute-start | bytes 196616 | tf_op jit(solution)/shard_map/ppermute | solution.py:442
  26.4 1.7 %collective-permute-start.13 = (bf16[128,256]{1,0:T(8,128)(2,1)S(1)}, bf16[128,256]{1,0:T(8,128)(2,1)S(1)}, u32[]{:S(2)}, u32[]{:S(2)}) collective-permute-start(bf16[128,256]{1,0:T(8,128)(2,1)S(1)} %get-tuple-element.70), channel_id=1, source_target_pairs={{0,3},{1,0},{2,1},{3,2},{4,7},{5,4},{6,5},{7,6},{8,11},{9,8},{10,9... | collective-permute-start | bytes 196616 | tf_op jit(solution)/shard_map/ppermute | solution.py:442
  28.0 3.5 %raw.1 = (f32[128,768]{1,0:T(8,128)S(1)}, f32[128,768]{1,0:T(8,128)S(1)}) custom-call(bf16[32,4224]{1,0:T(8,128)(2,1)S(1)} %pad_maximum_fusion.refs_0_, bf16[32,4224]{1,0:T(8,128)(2,1)S(1)} %constant_dynamic-update-slice_fusion.refs_1_, bf16[32,4224]{1,0:T(8,128)(2,1)S(1)} %collective-permute-done.6.refs_2_, ...), custom_call_target="tpu_custom_call" | custom-call | flops 1 | bytes 1 | tf_op jit(solution)/shard_map/raw/pallas_call | solution.py:216
  31.6 1.2 %collective-permute-done.12.refs_6_ = bf16[128,256]{1,0:T(8,128)(2,1)S(1)} collective-permute-done((bf16[128,256]{1,0:T(8,128)(2,1)S(1)}, bf16[128,256]{1,0:T(8,128)(2,1)S(1)}, u32[]{:S(2)}, u32[]{:S(2)}) %collective-permute-start.12) | collective-permute-done | bytes 65568 | tf_op jit(solution)/shard_map/ppermute | solution.py:442
  33.3 1.1 %collective-permute-start.16 = (bf16[64,128]{1,0:T(8,128)(2,1)S(1)}, bf16[64,128]{1,0:T(8,128)(2,1)S(1)}, u32[]{:S(2)}, u32[]{:S(2)}) collective-permute-start(bf16[64,128]{1,0:T(8,128)(2,1)S(1)} %get-tuple-element.81), channel_id=1, source_target_pairs={{0,8},{8,0},{1,9},{9,1},{2,10},{10,2},{3,11},{11,3},{4,12},{12,4},... | collective-permute-start | bytes 49160 | tf_op jit(solution)/shard_map/ppermute | solution.py:445
  34.4 1.1 %down.1 = (f32[64,4096]{1,0:T(8,128)S(1)}, bf16[64,4096]{1,0:T(8,128)(2,1)S(1)}) custom-call(bf16[128,768]{1,0:T(8,128)(2,1)S(1)} %get-tuple-element.76.hidden_ref, bf16[768,4096]{1,0:T(8,128)(2,1)S(1)} %bitcast.10), custom_call_target="tpu_custom_call" | custom-call | flops 1 | bytes 1 | tf_op jit(solution)/shard_map/down/pallas_call | solution.py:278
  35.5 1.6 %collective-permute-done.16.refs_1_ = bf16[64,128]{1,0:T(8,128)(2,1)S(1)} collective-permute-done((bf16[64,128]{1,0:T(8,128)(2,1)S(1)}, bf16[64,128]{1,0:T(8,128)(2,1)S(1)}, u32[]{:S(2)}, u32[]{:S(2)}) %collective-permute-start.16) | collective-permute-done | bytes 16416 | tf_op jit(solution)/shard_map/ppermute | solution.py:445
  37.1 1.2 %collective-permute-done.17.far_ref = bf16[32,256]{1,0:T(8,128)(2,1)S(1)} collective-permute-done((bf16[32,256]{1,0:T(8,128)(2,1)S(1)}, bf16[32,256]{1,0:T(8,128)(2,1)S(1)}, u32[]{:S(2)}, u32[]{:S(2)}) %collective-permute-start.17) | collective-permute-done | bytes 16416 | tf_op jit(solution)/shard_map/ppermute | solution.py:448
  38.7 1.1 %collective-permute-start.22 = (bf16[24,4096]{1,0:T(8,128)(2,1)S(1)}, bf16[24,4096]{1,0:T(8,128)(2,1)S(1)}, u32[]{:S(2)}, u32[]{:S(2)}) collective-permute-start(bf16[24,4096]{1,0:T(8,128)(2,1)S(1)} %get-tuple-element.89), channel_id=1, source_target_pairs={{0,8},{8,0},{1,9},{9,1},{2,10},{10,2},{3,11},{11,3},{4,12},{12,4},... | collective-permute-start | bytes 589832 | tf_op jit(solution)/shard_map/ppermute | solution.py:445
  39.7 1.5 %collective-permute-start.19 = (bf16[32,512]{1,0:T(8,128)(2,1)S(1)}, bf16[32,512]{1,0:T(8,128)(2,1)S(1)}, u32[]{:S(2)}, u32[]{:S(2)}) collective-permute-start(bf16[32,512]{1,0:T(8,128)(2,1)S(1)} %get-tuple-element.86), channel_id=1, source_target_pairs={{0,1},{1,2},{2,3},{3,0},{4,5},{5,6},{6,7},{7,4},{8,9},{9,10},{10,1... | collective-permute-start | bytes 98312 | tf_op jit(solution)/shard_map/ppermute | solution.py:442
  41.2 1.3 %collective-permute-start.20 = (bf16[32,512]{1,0:T(8,128)(2,1)S(1)}, bf16[32,512]{1,0:T(8,128)(2,1)S(1)}, u32[]{:S(2)}, u32[]{:S(2)}) collective-permute-start(bf16[32,512]{1,0:T(8,128)(2,1)S(1)} %get-tuple-element.87), channel_id=1, source_target_pairs={{0,2},{1,3},{2,0},{3,1},{4,6},{5,7},{6,4},{7,5},{8,10},{9,11},{10,... | collective-permute-start | bytes 98312 | tf_op jit(solution)/shard_map/ppermute | solution.py:442
  42.5 1.1 %collective-permute-start.21 = (bf16[32,512]{1,0:T(8,128)(2,1)S(1)}, bf16[32,512]{1,0:T(8,128)(2,1)S(1)}, u32[]{:S(2)}, u32[]{:S(2)}) collective-permute-start(bf16[32,512]{1,0:T(8,128)(2,1)S(1)} %get-tuple-element.88), channel_id=1, source_target_pairs={{0,3},{1,0},{2,1},{3,2},{4,7},{5,4},{6,5},{7,6},{8,11},{9,8},{10,9... | collective-permute-start | bytes 98312 | tf_op jit(solution)/shard_map/ppermute | solution.py:442
  43.6 1.9 %collective-permute-done.19.refs_0_ = bf16[32,512]{1,0:T(8,128)(2,1)S(1)} collective-permute-done((bf16[32,512]{1,0:T(8,128)(2,1)S(1)}, bf16[32,512]{1,0:T(8,128)(2,1)S(1)}, u32[]{:S(2)}, u32[]{:S(2)}) %collective-permute-start.19) | collective-permute-done | bytes 32800 | tf_op jit(solution)/shard_map/ppermute | solution.py:442
  45.5 1.0 %collective-permute-start.23 = (bf16[8,4096]{1,0:T(8,128)(2,1)S(1)}, bf16[8,4096]{1,0:T(8,128)(2,1)S(1)}, u32[]{:S(2)}, u32[]{:S(2)}) collective-permute-start(bf16[8,4096]{1,0:T(8,128)(2,1)S(1)} %get-tuple-element.91), channel_id=1, source_target_pairs={{0,8},{8,0},{1,9},{9,1},{2,10},{10,2},{3,11},{11,3},{4,12},{12,4},... | collective-permute-start | bytes 196616 | tf_op jit(solution)/shard_map/ppermute | solution.py:445
  47.0 1.4 %collective-permute-start.26 = (bf16[8,4096]{1,0:T(8,128)(2,1)S(1)}, bf16[8,4096]{1,0:T(8,128)(2,1)S(1)}, u32[]{:S(2)}, u32[]{:S(2)}) collective-permute-start(bf16[8,4096]{1,0:T(8,128)(2,1)S(1)} %get-tuple-element.94), channel_id=1, source_target_pairs={{0,1},{1,2},{2,3},{3,0},{4,5},{5,6},{6,7},{7,4},{8,9},{9,10},{10,1... | collective-permute-start | bytes 196616 | tf_op jit(solution)/shard_map/ppermute | solution.py:442
  48.4 1.9 %collective-permute-start.25 = (bf16[8,4096]{1,0:T(8,128)(2,1)S(1)}, bf16[8,4096]{1,0:T(8,128)(2,1)S(1)}, u32[]{:S(2)}, u32[]{:S(2)}) collective-permute-start(bf16[8,4096]{1,0:T(8,128)(2,1)S(1)} %get-tuple-element.93), channel_id=1, source_target_pairs={{0,2},{1,3},{2,0},{3,1},{4,6},{5,7},{6,4},{7,5},{8,10},{9,11},{10,... | collective-permute-start | bytes 196616 | tf_op jit(solution)/shard_map/ppermute | solution.py:442
  50.2 1.1 %collective-permute-start.24 = (bf16[8,4096]{1,0:T(8,128)(2,1)S(1)}, bf16[8,4096]{1,0:T(8,128)(2,1)S(1)}, u32[]{:S(2)}, u32[]{:S(2)}) collective-permute-start(bf16[8,4096]{1,0:T(8,128)(2,1)S(1)} %get-tuple-element.92), channel_id=1, source_target_pairs={{0,3},{1,0},{2,1},{3,2},{4,7},{5,4},{6,5},{7,6},{8,11},{9,8},{10,9... | collective-permute-start | bytes 196616 | tf_op jit(solution)/shard_map/ppermute | solution.py:442
  51.4 2.4 %collective-permute-done.26 = bf16[8,4096]{1,0:T(8,128)(2,1)S(1)} collective-permute-done((bf16[8,4096]{1,0:T(8,128)(2,1)S(1)}, bf16[8,4096]{1,0:T(8,128)(2,1)S(1)}, u32[]{:S(2)}, u32[]{:S(2)}) %collective-permute-start.26) | collective-permute-done | bytes 65568 | tf_op jit(solution)/shard_map/ppermute | solution.py:442
  53.8 1.6 %collective-permute-done.25 = bf16[8,4096]{1,0:T(8,128)(2,1)S(1)} collective-permute-done((bf16[8,4096]{1,0:T(8,128)(2,1)S(1)}, bf16[8,4096]{1,0:T(8,128)(2,1)S(1)}, u32[]{:S(2)}, u32[]{:S(2)}) %collective-permute-start.25) | collective-permute-done | bytes 65568 | tf_op jit(solution)/shard_map/ppermute | solution.py:442
  55.4 0.7 %add_convert_fusion = bf16[8,4096]{1,0:T(8,128)(2,1)} fusion(bf16[8,4096]{1,0:T(8,128)(2,1)S(1)} %collective-permute-done.26, bf16[8,4096]{1,0:T(8,128)(2,1)S(1)} %collective-permute-done.25, f32[8,4096]{1,0:T(8,128)S(1)} %plus.1, bf16[8,4096]{1,0:T(8,128)(2,1)S(1)} %collective-permute-done.24), kind=kLoop, calls=%fused_computation.2 | loop fusion | flops 229376 | bytes 393216 | tf_op jit(solution)/shard_map/convert_element_type | solution.py:498
  (48 shorter events, 2.4 us)
Async XLA Ops:
  1.0 11.7 %collective-permute-start.2 = (bf16[8,4224]{1,0:T(8,128)(2,1)S(1)}, bf16[8,4224]{1,0:T(8,128)(2,1)S(1)}, u32[]{:S(2)}, u32[]{:S(2)}) collective-permute-start(bf16[8,4224]{1,0:T(8,128)(2,1)S(1)} %attach.1), channel_id=1, source_target_pairs={{0,3},{1,0},{2,1},{3,2},{4,7},{5,4},{6,5},{7,6},{8,11},{9,8},{10,9... | collective-permute-start | bytes 202760 | tf_op jit(solution)/shard_map/ppermute | solution.py:442
  6.1 6.6 %collective-permute-start.1 = (bf16[8,4224]{1,0:T(8,128)(2,1)S(1)}, bf16[8,4224]{1,0:T(8,128)(2,1)S(1)}, u32[]{:S(2)}, u32[]{:S(2)}) collective-permute-start(bf16[8,4224]{1,0:T(8,128)(2,1)S(1)} %attach.1), channel_id=1, source_target_pairs={{0,2},{1,3},{2,0},{3,1},{4,6},{5,7},{6,4},{7,5},{8,10},{9,11},{10,... | collective-permute-start | bytes 202760 | tf_op jit(solution)/shard_map/ppermute | solution.py:442
  6.1 6.6 %collective-permute-start = (bf16[8,4224]{1,0:T(8,128)(2,1)S(1)}, bf16[8,4224]{1,0:T(8,128)(2,1)S(1)}, u32[]{:S(2)}, u32[]{:S(2)}) collective-permute-start(bf16[8,4224]{1,0:T(8,128)(2,1)S(1)} %attach.1), channel_id=1, source_target_pairs={{0,1},{1,2},{2,3},{3,0},{4,5},{5,6},{6,7},{7,4},{8,9},{9,10},{10,1... | collective-permute-start | bytes 202760 | tf_op jit(solution)/shard_map/ppermute | solution.py:442
  7.1 5.7 %collective-permute-start.4 = (bf16[8,4224]{1,0:T(8,128)(2,1)S(1)}, bf16[8,4224]{1,0:T(8,128)(2,1)S(1)}, u32[]{:S(2)}, u32[]{:S(2)}) collective-permute-start(bf16[8,4224]{1,0:T(8,128)(2,1)S(1)} %attach.1), channel_id=1, source_target_pairs={{0,8},{8,0},{1,9},{9,1},{2,10},{10,2},{3,11},{11,3},{4,12},{12,4},... | collective-permute-start | bytes 202760 | tf_op jit(solution)/shard_map/ppermute | solution.py:445
  8.6 4.2 %collective-permute-start.3 = (bf16[128,1024]{1,0:T(8,128)(2,1)}, bf16[128,1024]{1,0:T(8,128)(2,1)S(1)}, u32[]{:S(2)}, u32[]{:S(2)}) collective-permute-start(bf16[128,1024]{1,0:T(8,128)(2,1)} %bitcast.11), channel_id=1, source_target_pairs={{0,4},{4,0},{1,5},{5,1},{2,6},{6,2},{3,7},{7,3},{8,12},{12,8},{9,1... | collective-permute-start | bytes 786440 | tf_op jit(solution)/shard_map/ppermute | solution.py:448
  12.8 9.1 %collective-permute-start.5 = (bf16[24,4224]{1,0:T(8,128)(2,1)S(1)}, bf16[24,4224]{1,0:T(8,128)(2,1)S(1)}, u32[]{:S(2)}, u32[]{:S(2)}) collective-permute-start(bf16[24,4224]{1,0:T(8,128)(2,1)S(1)} %pad_maximum_fusion.1), channel_id=1, source_target_pairs={{0,8},{8,0},{1,9},{9,1},{2,10},{10,2},{3,11},{11,3},{4,12},{12,4},... | collective-permute-start | bytes 608264 | tf_op jit(solution)/shard_map/ppermute | solution.py:445
  14.4 7.7 %copy-start = (bf16[4,32,1024]{2,1,0:T(8,128)(2,1)S(1)}, bf16[4,32,1024]{2,1,0:T(8,128)(2,1)}, u32[]{:S(2)}) copy-start(bf16[4,32,1024]{2,1,0:T(8,128)(2,1)} %param.23) | copy-start | bytes 786436
  14.4 9.0 %collective-permute-start.6 = (bf16[32,4224]{1,0:T(8,128)(2,1)S(1)}, bf16[32,4224]{1,0:T(8,128)(2,1)S(1)}, u32[]{:S(2)}, u32[]{:S(2)}) collective-permute-start(bf16[32,4224]{1,0:T(8,128)(2,1)S(1)} %pad_maximum_fusion.refs_0_), channel_id=1, source_target_pairs={{0,4},{4,0},{1,5},{5,1},{2,6},{6,2},{3,7},{7,3},{8,12},{12,8},{9,1... | collective-permute-start | bytes 811016 | tf_op jit(solution)/shard_map/ppermute | solution.py:448
  14.4 7.7 %collective-permute-start.8 = (bf16[3,32,192]{2,1,0:T(8,128)(2,1)S(1)}, bf16[3,32,192]{2,1,0:T(8,128)(2,1)S(1)}, u32[]{:S(2)}, u32[]{:S(2)}) collective-permute-start(bf16[3,32,192]{2,1,0:T(8,128)(2,1)S(1)} %get-tuple-element.60), channel_id=1, source_target_pairs={{0,1},{1,2},{2,3},{3,0},{4,5},{5,6},{6,7},{7,4},{8,9},{9,10},{10,1... | collective-permute-start | bytes 110600 | tf_op jit(solution)/shard_map/ppermute | solution.py:442
  16.1 7.0 %collective-permute-start.9 = (bf16[3,32,192]{2,1,0:T(8,128)(2,1)S(1)}, bf16[3,32,192]{2,1,0:T(8,128)(2,1)S(1)}, u32[]{:S(2)}, u32[]{:S(2)}) collective-permute-start(bf16[3,32,192]{2,1,0:T(8,128)(2,1)S(1)} %get-tuple-element.61), channel_id=1, source_target_pairs={{0,2},{1,3},{2,0},{3,1},{4,6},{5,7},{6,4},{7,5},{8,10},{9,11},{10,... | collective-permute-start | bytes 110600 | tf_op jit(solution)/shard_map/ppermute | solution.py:442
  17.0 6.1 %collective-permute-start.10 = (bf16[3,32,192]{2,1,0:T(8,128)(2,1)S(1)}, bf16[3,32,192]{2,1,0:T(8,128)(2,1)S(1)}, u32[]{:S(2)}, u32[]{:S(2)}) collective-permute-start(bf16[3,32,192]{2,1,0:T(8,128)(2,1)S(1)} %get-tuple-element.62), channel_id=1, source_target_pairs={{0,3},{1,0},{2,1},{3,2},{4,7},{5,4},{6,5},{7,6},{8,11},{9,8},{10,9... | collective-permute-start | bytes 110600 | tf_op jit(solution)/shard_map/ppermute | solution.py:442
  22.0 1.6 %collective-permute-start.7 = (bf16[32,4224]{1,0:T(8,128)(2,1)S(1)}, bf16[32,4224]{1,0:T(8,128)(2,1)S(1)}, u32[]{:S(2)}, u32[]{:S(2)}) collective-permute-start(bf16[32,4224]{1,0:T(8,128)(2,1)S(1)} %constant_dynamic-update-slice_fusion.refs_1_), channel_id=1, source_target_pairs={{0,4},{4,0},{1,5},{5,1},{2,6},{6,2},{3,7},{7,3},{8,12},{12,8},{9,1... | collective-permute-start | bytes 811016 | tf_op jit(solution)/shard_map/ppermute | solution.py:448
  22.1 9.5 %collective-permute-start.14 = (bf16[128,1024]{1,0:T(8,128)(2,1)S(1)}, bf16[128,1024]{1,0:T(8,128)(2,1)S(1)}, u32[]{:S(2)}, u32[]{:S(2)}) collective-permute-start(bf16[128,1024]{1,0:T(8,128)(2,1)S(1)} %bitcast.12), channel_id=1, source_target_pairs={{0,8},{8,0},{1,9},{9,1},{2,10},{10,2},{3,11},{11,3},{4,12},{12,4},... | collective-permute-start | bytes 786440 | tf_op jit(solution)/shard_map/ppermute | solution.py:445
  23.9 7.7 %collective-permute-start.11 = (bf16[128,256]{1,0:T(8,128)(2,1)S(1)}, bf16[128,256]{1,0:T(8,128)(2,1)S(1)}, u32[]{:S(2)}, u32[]{:S(2)}) collective-permute-start(bf16[128,256]{1,0:T(8,128)(2,1)S(1)} %get-tuple-element.68), channel_id=1, source_target_pairs={{0,1},{1,2},{2,3},{3,0},{4,5},{5,6},{6,7},{7,4},{8,9},{9,10},{10,1... | collective-permute-start | bytes 196616 | tf_op jit(solution)/shard_map/ppermute | solution.py:442
  24.8 8.0 %collective-permute-start.12 = (bf16[128,256]{1,0:T(8,128)(2,1)S(1)}, bf16[128,256]{1,0:T(8,128)(2,1)S(1)}, u32[]{:S(2)}, u32[]{:S(2)}) collective-permute-start(bf16[128,256]{1,0:T(8,128)(2,1)S(1)} %get-tuple-element.69), channel_id=1, source_target_pairs={{0,2},{1,3},{2,0},{3,1},{4,6},{5,7},{6,4},{7,5},{8,10},{9,11},{10,... | collective-permute-start | bytes 196616 | tf_op jit(solution)/shard_map/ppermute | solution.py:442
  26.4 8.0 %slice-start = ((s8[6291456]{0:T(1024)(128)(4,1)}), s8[4194304]{0:T(1024)(128)(4,1)S(1)}, s32[]{:S(2)}) async-start(s8[6291456]{0:T(1024)(128)(4,1)} %bitcast.8), calls=%async_computation | async-start | bytes 8388608
  26.4 8.0 %slice-start.1 = ((s8[6291456]{0:T(1024)(128)(4,1)}), s8[2097152]{0:T(1024)(128)(4,1)S(1)}, s32[]{:S(2)}) async-start(s8[6291456]{0:T(1024)(128)(4,1)} %bitcast.8), calls=%async_computation.1 | async-start | bytes 4194304
  26.4 6.4 %collective-permute-start.13 = (bf16[128,256]{1,0:T(8,128)(2,1)S(1)}, bf16[128,256]{1,0:T(8,128)(2,1)S(1)}, u32[]{:S(2)}, u32[]{:S(2)}) collective-permute-start(bf16[128,256]{1,0:T(8,128)(2,1)S(1)} %get-tuple-element.70), channel_id=1, source_target_pairs={{0,3},{1,0},{2,1},{3,2},{4,7},{5,4},{6,5},{7,6},{8,11},{9,8},{10,9... | collective-permute-start | bytes 196616 | tf_op jit(solution)/shard_map/ppermute | solution.py:442
  33.3 3.8 %collective-permute-start.16 = (bf16[64,128]{1,0:T(8,128)(2,1)S(1)}, bf16[64,128]{1,0:T(8,128)(2,1)S(1)}, u32[]{:S(2)}, u32[]{:S(2)}) collective-permute-start(bf16[64,128]{1,0:T(8,128)(2,1)S(1)} %get-tuple-element.81), channel_id=1, source_target_pairs={{0,8},{8,0},{1,9},{9,1},{2,10},{10,2},{3,11},{11,3},{4,12},{12,4},... | collective-permute-start | bytes 49160 | tf_op jit(solution)/shard_map/ppermute | solution.py:445
  35.4 3.1 %collective-permute-start.15 = (bf16[64,4096]{1,0:T(8,128)(2,1)S(1)}, bf16[64,4096]{1,0:T(8,128)(2,1)S(1)}, u32[]{:S(2)}, u32[]{:S(2)}) collective-permute-start(bf16[64,4096]{1,0:T(8,128)(2,1)S(1)} %get-tuple-element.78), channel_id=1, source_target_pairs={{0,4},{4,0},{1,5},{5,1},{2,6},{6,2},{3,7},{7,3},{8,12},{12,8},{9,1... | collective-permute-start | bytes 1572872 | tf_op jit(solution)/shard_map/ppermute | solution.py:448
  37.1 1.2 %collective-permute-start.17 = (bf16[32,256]{1,0:T(8,128)(2,1)S(1)}, bf16[32,256]{1,0:T(8,128)(2,1)S(1)}, u32[]{:S(2)}, u32[]{:S(2)}) collective-permute-start(bf16[32,256]{1,0:T(8,128)(2,1)S(1)} %get-tuple-element.83), channel_id=1, source_target_pairs={{0,4},{4,0},{1,5},{5,1},{2,6},{6,2},{3,7},{7,3},{8,12},{12,8},{9,1... | collective-permute-start | bytes 49160 | tf_op jit(solution)/shard_map/ppermute | solution.py:448
  38.3 8.3 %collective-permute-start.18 = (bf16[128,1024]{1,0:T(8,128)(2,1)S(1)}, bf16[128,1024]{1,0:T(8,128)(2,1)S(1)}, u32[]{:S(2)}, u32[]{:S(2)}) collective-permute-start(bf16[128,1024]{1,0:T(8,128)(2,1)S(1)} %collective-permute-done.14.refs_2_), channel_id=1, source_target_pairs={{0,4},{4,0},{1,5},{5,1},{2,6},{6,2},{3,7},{7,3},{8,12},{12,8},{9,1... | collective-permute-start | bytes 786440 | tf_op jit(solution)/shard_map/ppermute | solution.py:448
  38.7 8.0 %collective-permute-start.22 = (bf16[24,4096]{1,0:T(8,128)(2,1)S(1)}, bf16[24,4096]{1,0:T(8,128)(2,1)S(1)}, u32[]{:S(2)}, u32[]{:S(2)}) collective-permute-start(bf16[24,4096]{1,0:T(8,128)(2,1)S(1)} %get-tuple-element.89), channel_id=1, source_target_pairs={{0,8},{8,0},{1,9},{9,1},{2,10},{10,2},{3,11},{11,3},{4,12},{12,4},... | collective-permute-start | bytes 589832 | tf_op jit(solution)/shard_map/ppermute | solution.py:445
  39.7 5.8 %collective-permute-start.19 = (bf16[32,512]{1,0:T(8,128)(2,1)S(1)}, bf16[32,512]{1,0:T(8,128)(2,1)S(1)}, u32[]{:S(2)}, u32[]{:S(2)}) collective-permute-start(bf16[32,512]{1,0:T(8,128)(2,1)S(1)} %get-tuple-element.86), channel_id=1, source_target_pairs={{0,1},{1,2},{2,3},{3,0},{4,5},{5,6},{6,7},{7,4},{8,9},{9,10},{10,1... | collective-permute-start | bytes 98312 | tf_op jit(solution)/shard_map/ppermute | solution.py:442
  41.2 5.3 %collective-permute-start.20 = (bf16[32,512]{1,0:T(8,128)(2,1)S(1)}, bf16[32,512]{1,0:T(8,128)(2,1)S(1)}, u32[]{:S(2)}, u32[]{:S(2)}) collective-permute-start(bf16[32,512]{1,0:T(8,128)(2,1)S(1)} %get-tuple-element.87), channel_id=1, source_target_pairs={{0,2},{1,3},{2,0},{3,1},{4,6},{5,7},{6,4},{7,5},{8,10},{9,11},{10,... | collective-permute-start | bytes 98312 | tf_op jit(solution)/shard_map/ppermute | solution.py:442
  42.5 4.1 %collective-permute-start.21 = (bf16[32,512]{1,0:T(8,128)(2,1)S(1)}, bf16[32,512]{1,0:T(8,128)(2,1)S(1)}, u32[]{:S(2)}, u32[]{:S(2)}) collective-permute-start(bf16[32,512]{1,0:T(8,128)(2,1)S(1)} %get-tuple-element.88), channel_id=1, source_target_pairs={{0,3},{1,0},{2,1},{3,2},{4,7},{5,4},{6,5},{7,6},{8,11},{9,8},{10,9... | collective-permute-start | bytes 98312 | tf_op jit(solution)/shard_map/ppermute | solution.py:442
  45.5 5.9 %collective-permute-start.23 = (bf16[8,4096]{1,0:T(8,128)(2,1)S(1)}, bf16[8,4096]{1,0:T(8,128)(2,1)S(1)}, u32[]{:S(2)}, u32[]{:S(2)}) collective-permute-start(bf16[8,4096]{1,0:T(8,128)(2,1)S(1)} %get-tuple-element.91), channel_id=1, source_target_pairs={{0,8},{8,0},{1,9},{9,1},{2,10},{10,2},{3,11},{11,3},{4,12},{12,4},... | collective-permute-start | bytes 196616 | tf_op jit(solution)/shard_map/ppermute | solution.py:445
  47.0 6.9 %collective-permute-start.26 = (bf16[8,4096]{1,0:T(8,128)(2,1)S(1)}, bf16[8,4096]{1,0:T(8,128)(2,1)S(1)}, u32[]{:S(2)}, u32[]{:S(2)}) collective-permute-start(bf16[8,4096]{1,0:T(8,128)(2,1)S(1)} %get-tuple-element.94), channel_id=1, source_target_pairs={{0,1},{1,2},{2,3},{3,0},{4,5},{5,6},{6,7},{7,4},{8,9},{9,10},{10,1... | collective-permute-start | bytes 196616 | tf_op jit(solution)/shard_map/ppermute | solution.py:442
  48.4 7.1 %collective-permute-start.25 = (bf16[8,4096]{1,0:T(8,128)(2,1)S(1)}, bf16[8,4096]{1,0:T(8,128)(2,1)S(1)}, u32[]{:S(2)}, u32[]{:S(2)}) collective-permute-start(bf16[8,4096]{1,0:T(8,128)(2,1)S(1)} %get-tuple-element.93), channel_id=1, source_target_pairs={{0,2},{1,3},{2,0},{3,1},{4,6},{5,7},{6,4},{7,5},{8,10},{9,11},{10,... | collective-permute-start | bytes 196616 | tf_op jit(solution)/shard_map/ppermute | solution.py:442
  50.2 5.2 %collective-permute-start.24 = (bf16[8,4096]{1,0:T(8,128)(2,1)S(1)}, bf16[8,4096]{1,0:T(8,128)(2,1)S(1)}, u32[]{:S(2)}, u32[]{:S(2)}) collective-permute-start(bf16[8,4096]{1,0:T(8,128)(2,1)S(1)} %get-tuple-element.92), channel_id=1, source_target_pairs={{0,3},{1,0},{2,1},{3,2},{4,7},{5,4},{6,5},{7,6},{8,11},{9,8},{10,9... | collective-permute-start | bytes 196616 | tf_op jit(solution)/shard_map/ppermute | solution.py:442

commit v19 on v18

--- a/solution.py
+++ b/solution.py
@@ -16,6 +16,7 @@
 LONGER = pl.CostEstimate(flops=10_000_000_000, bytes_accessed=1, transcendentals=0)
 LAST = pl.CostEstimate(flops=1_000_000_000, bytes_accessed=1, transcendentals=0)
 SOME = pl.CostEstimate(flops=3_000_000_000, bytes_accessed=1, transcendentals=0)
+TURN = pl.CostEstimate(flops=3_000_000_000, bytes_accessed=1, transcendentals=0)
 BRIEF = pl.CostEstimate(flops=1, bytes_accessed=1, transcendentals=0)
 
 
@@ -318,7 +319,7 @@
         functools.partial(turn_kernel, rows),
         out_shape=[jax.ShapeDtypeStruct((span, 2 * ranks), BF)] * parts,
         compiler_params=pltpu.CompilerParams(vmem_limit_bytes=SMALL_LIMIT),
-        cost_estimate=BRIEF,
+        cost_estimate=TURN,
         name="turn",
     )(near, far)
 
@@ -490,7 +491,7 @@
     near, far = down_products(hidden, w_down.reshape(hid, width))
     out, *others = fold(near, other_core(far), chips, rows)
     backs = [along_y(others[n], -(n // 2 + 1)) for n in range(2 * chips - 2)]
-    rights += [partner_right] + [other_core(after(right, bottom[0])) for right in rights[1:]]
+    rights += [partner_right] + [other_core(after(right, out)) for right in rights[1:]]
     own, *pieces = merge(out, rights, add_up(bottom[1:] + bottom[:1]), backs[1::2], rows)
     result = plus(own, backs[::2])
     for k in range(1, parts):

time: 56.3 us -> 55.5 us (0.986)
  waiting for transfers between devices: 10.3 us -> 9.4 us
    ppermute x6, waiting for transfers between devices: 1.35 us -> 0.46 us  [other_core(): return lax.ppermute(value, 'core', [(0, 1), (1, 0)])]
  transfers between devices with their start and end apart: 27 -> 27, of which waited for: 8 -> 8; matrix products, arithmetic and copies ran while one was open for 0% -> 0% of each run, Pallas kernels for 22% -> 23%
where the time goes in v19:
time: 55.5 us; the launch traced here: 55.3 us
  starting transfers between devices  30.9 us (56%)
  Pallas kernels  14 us (25%)
  waiting for transfers between devices  9.4 us (17%)
  other arithmetic  0.71 us (1%)
    ppermute x15, starting transfers between devices, along_z(): lax.ppermute(value, 'mp', [(i, (i + step) % parts) for i in range(parts)])  23.3 us
    ppermute x15, waiting for transfers between devices, along_z(): lax.ppermute(value, 'mp', [(i, (i + step) % parts) for i in range(parts)])  7.33 us
    ppermute x6, starting transfers between devices, along_y(): lax.ppermute(value, 'y', [(i, (i + step) % chips) for i in range(chips)])  7.14 us
    pallas_call x1, Pallas kernels, prepare(): pl.pallas_call(functools.partial(prepare_kernel, parts), in_specs=[vmem]...  4.06 us
    pallas_call x1, Pallas kernels, raw_products(): pl.pallas_call(functools.partial(raw_kernel, len(lines), tile), out_shape...  3.51 us
    pallas_call x1, Pallas kernels, load(): pl.pallas_call(load_kernel, in_specs=[pl.BlockSpec(memory_space=pltpu.HBM...  2.86 us
    ppermute x6, waiting for transfers between devices, along_y(): lax.ppermute(value, 'y', [(i, (i + step) % chips) for i in range(chips)])  1.61 us
  transfers between devices with their start and end apart: 27, of which 8 were waited for; matrix products, arithmetic and copies ran while one was open for 0% of the time, Pallas kernels for 23%

profile of v19, /device:TPU:0, one launch (start us, length us, event | category | flops | bytes accessed | tf_op | source)
XLA Modules:
  0.0 55.3 jit_solution(7133786188439092525)
XLA Ops:
  0.0 0.9 %attach.1 = bf16[8,4224]{1,0:T(8,128)(2,1)S(1)} custom-call(bf16[8,4096]{1,0:T(8,128)(2,1)} %tokens_ref.1, s32[8,8]{1,0:T(8,128)} %routes_ref.1, f32[8,8]{1,0:T(8,128)} %probs_ref.1), custom_call_target="tpu_custom_call" | custom-call | flops 1 | bytes 1 | tf_op jit(solution)/shard_map/attach/pallas_call | solution.py:67
  1.0 5.1 %collective-permute-start.2 = (bf16[8,4224]{1,0:T(8,128)(2,1)S(1)}, bf16[8,4224]{1,0:T(8,128)(2,1)S(1)}, u32[]{:S(2)}, u32[]{:S(2)}) collective-permute-start(bf16[8,4224]{1,0:T(8,128)(2,1)S(1)} %attach.1), channel_id=1, source_target_pairs={{0,3},{1,0},{2,1},{3,2},{4,7},{5,4},{6,5},{7,6},{8,11},{9,8},{10,9... | collective-permute-start | bytes 202760 | tf_op jit(solution)/shard_map/ppermute | solution.py:443
  6.1 1.0 %collective-permute-start = (bf16[8,4224]{1,0:T(8,128)(2,1)S(1)}, bf16[8,4224]{1,0:T(8,128)(2,1)S(1)}, u32[]{:S(2)}, u32[]{:S(2)}) collective-permute-start(bf16[8,4224]{1,0:T(8,128)(2,1)S(1)} %attach.1), channel_id=1, source_target_pairs={{0,1},{1,2},{2,3},{3,0},{4,5},{5,6},{6,7},{7,4},{8,9},{9,10},{10,1... | collective-permute-start | bytes 202760 | tf_op jit(solution)/shard_map/ppermute | solution.py:443
  7.1 1.5 %collective-permute-start.4 = (bf16[8,4224]{1,0:T(8,128)(2,1)S(1)}, bf16[8,4224]{1,0:T(8,128)(2,1)S(1)}, u32[]{:S(2)}, u32[]{:S(2)}) collective-permute-start(bf16[8,4224]{1,0:T(8,128)(2,1)S(1)} %attach.1), channel_id=1, source_target_pairs={{0,8},{8,0},{1,9},{9,1},{2,10},{10,2},{3,11},{11,3},{4,12},{12,4},... | collective-permute-start | bytes 202760 | tf_op jit(solution)/shard_map/ppermute | solution.py:446
  8.6 4.1 %prepare.1 = (bf16[768,4096]{1,0:T(8,128)(2,1)S(1)}, bf16[256,1024]{1,0:T(8,128)(2,1)S(1)}, bf16[3,32,192]{2,1,0:T(8,128)(2,1)S(1)}, bf16[3,32,192]{2,1,0:T(8,12...) custom-call(bf16[4,8,768]{2,1,0:T(8,128)(2,1)} %refs_0_.1, bf16[4,8,768]{2,1,0:T(8,128)(2,1)} %refs_1_.1, ...), custom_call_target="tpu_custom_call" | custom-call | flops 1 | bytes 1 | tf_op jit(solution)/shard_map/prepare/pallas_call | solution.py:135
  12.8 1.6 %collective-permute-start.5 = (bf16[24,4224]{1,0:T(8,128)(2,1)S(1)}, bf16[24,4224]{1,0:T(8,128)(2,1)S(1)}, u32[]{:S(2)}, u32[]{:S(2)}) collective-permute-start(bf16[24,4224]{1,0:T(8,128)(2,1)S(1)} %pad_maximum_fusion.1), channel_id=1, source_target_pairs={{0,8},{8,0},{1,9},{9,1},{2,10},{10,2},{3,11},{11,3},{4,12},{12,4},... | collective-permute-start | bytes 608264 | tf_op jit(solution)/shard_map/ppermute | solution.py:446
  14.4 1.7 %collective-permute-start.8 = (bf16[3,32,192]{2,1,0:T(8,128)(2,1)S(1)}, bf16[3,32,192]{2,1,0:T(8,128)(2,1)S(1)}, u32[]{:S(2)}, u32[]{:S(2)}) collective-permute-start(bf16[3,32,192]{2,1,0:T(8,128)(2,1)S(1)} %get-tuple-element.60), channel_id=1, source_target_pairs={{0,1},{1,2},{2,3},{3,0},{4,5},{5,6},{6,7},{7,4},{8,9},{9,10},{10,1... | collective-permute-start | bytes 110600 | tf_op jit(solution)/shard_map/ppermute | solution.py:443
  16.1 0.9 %collective-permute-start.9 = (bf16[3,32,192]{2,1,0:T(8,128)(2,1)S(1)}, bf16[3,32,192]{2,1,0:T(8,128)(2,1)S(1)}, u32[]{:S(2)}, u32[]{:S(2)}) collective-permute-start(bf16[3,32,192]{2,1,0:T(8,128)(2,1)S(1)} %get-tuple-element.61), channel_id=1, source_target_pairs={{0,2},{1,3},{2,0},{3,1},{4,6},{5,7},{6,4},{7,5},{8,10},{9,11},{10,... | collective-permute-start | bytes 110600 | tf_op jit(solution)/shard_map/ppermute | solution.py:443
  17.0 2.1 %collective-permute-start.10 = (bf16[3,32,192]{2,1,0:T(8,128)(2,1)S(1)}, bf16[3,32,192]{2,1,0:T(8,128)(2,1)S(1)}, u32[]{:S(2)}, u32[]{:S(2)}) collective-permute-start(bf16[3,32,192]{2,1,0:T(8,128)(2,1)S(1)} %get-tuple-element.62), channel_id=1, source_target_pairs={{0,3},{1,0},{2,1},{3,2},{4,7},{5,4},{6,5},{7,6},{8,11},{9,8},{10,9... | collective-permute-start | bytes 110600 | tf_op jit(solution)/shard_map/ppermute | solution.py:443
  19.1 2.9 %load.1.refs_5_ = bf16[768,4096]{1,0:T(8,128)(2,1)S(1)} custom-call(bf16[768,4096]{1,0:T(8,128)(2,1)} %bitcast.14), custom_call_target="tpu_custom_call" | custom-call | flops 3000000000 | bytes 1 | tf_op jit(solution)/shard_map/load/pallas_call | solution.py:94
  22.1 1.0 %collective-permute-start.14 = (bf16[128,1024]{1,0:T(8,128)(2,1)S(1)}, bf16[128,1024]{1,0:T(8,128)(2,1)S(1)}, u32[]{:S(2)}, u32[]{:S(2)}) collective-permute-start(bf16[128,1024]{1,0:T(8,128)(2,1)S(1)} %bitcast.12), channel_id=1, source_target_pairs={{0,8},{8,0},{1,9},{9,1},{2,10},{10,2},{3,11},{11,3},{4,12},{12,4},... | collective-permute-start | bytes 786440 | tf_op jit(solution)/shard_map/ppermute | solution.py:446
  23.9 0.9 %collective-permute-start.11 = (bf16[128,256]{1,0:T(8,128)(2,1)S(1)}, bf16[128,256]{1,0:T(8,128)(2,1)S(1)}, u32[]{:S(2)}, u32[]{:S(2)}) collective-permute-start(bf16[128,256]{1,0:T(8,128)(2,1)S(1)} %get-tuple-element.68), channel_id=1, source_target_pairs={{0,1},{1,2},{2,3},{3,0},{4,5},{5,6},{6,7},{7,4},{8,9},{9,10},{10,1... | collective-permute-start | bytes 196616 | tf_op jit(solution)/shard_map/ppermute | solution.py:443
  24.8 1.5 %collective-permute-start.12 = (bf16[128,256]{1,0:T(8,128)(2,1)S(1)}, bf16[128,256]{1,0:T(8,128)(2,1)S(1)}, u32[]{:S(2)}, u32[]{:S(2)}) collective-permute-start(bf16[128,256]{1,0:T(8,128)(2,1)S(1)} %get-tuple-element.69), channel_id=1, source_target_pairs={{0,2},{1,3},{2,0},{3,1},{4,6},{5,7},{6,4},{7,5},{8,10},{9,11},{10,... | collective-permute-start | bytes 196616 | tf_op jit(solution)/shard_map/ppermute | solution.py:443
  26.4 1.7 %collective-permute-start.13 = (bf16[128,256]{1,0:T(8,128)(2,1)S(1)}, bf16[128,256]{1,0:T(8,128)(2,1)S(1)}, u32[]{:S(2)}, u32[]{:S(2)}) collective-permute-start(bf16[128,256]{1,0:T(8,128)(2,1)S(1)} %get-tuple-element.70), channel_id=1, source_target_pairs={{0,3},{1,0},{2,1},{3,2},{4,7},{5,4},{6,5},{7,6},{8,11},{9,8},{10,9... | collective-permute-start | bytes 196616 | tf_op jit(solution)/shard_map/ppermute | solution.py:443
  28.0 3.5 %raw.1 = (f32[128,768]{1,0:T(8,128)S(1)}, f32[128,768]{1,0:T(8,128)S(1)}) custom-call(bf16[32,4224]{1,0:T(8,128)(2,1)S(1)} %pad_maximum_fusion.refs_0_, bf16[32,4224]{1,0:T(8,128)(2,1)S(1)} %constant_dynamic-update-slice_fusion.refs_1_, bf16[32,4224]{1,0:T(8,128)(2,1)S(1)} %collective-permute-done.6.refs_2_, ...), custom_call_target="tpu_custom_call" | custom-call | flops 1 | bytes 1 | tf_op jit(solution)/shard_map/raw/pallas_call | solution.py:217
  31.6 1.2 %collective-permute-done.12.refs_6_ = bf16[128,256]{1,0:T(8,128)(2,1)S(1)} collective-permute-done((bf16[128,256]{1,0:T(8,128)(2,1)S(1)}, bf16[128,256]{1,0:T(8,128)(2,1)S(1)}, u32[]{:S(2)}, u32[]{:S(2)}) %collective-permute-start.12) | collective-permute-done | bytes 65568 | tf_op jit(solution)/shard_map/ppermute | solution.py:443
  32.8 0.5 hidden.1
  33.3 1.1 %collective-permute-start.17 = (bf16[64,128]{1,0:T(8,128)(2,1)S(1)}, bf16[64,128]{1,0:T(8,128)(2,1)S(1)}, u32[]{:S(2)}, u32[]{:S(2)}) collective-permute-start(bf16[64,128]{1,0:T(8,128)(2,1)S(1)} %get-tuple-element.82), channel_id=1, source_target_pairs={{0,8},{8,0},{1,9},{9,1},{2,10},{10,2},{3,11},{11,3},{4,12},{12,4},... | collective-permute-start | bytes 49160 | tf_op jit(solution)/shard_map/ppermute | solution.py:446
  34.4 1.1 %down.1 = (f32[64,4096]{1,0:T(8,128)S(1)}, bf16[64,4096]{1,0:T(8,128)(2,1)S(1)}) custom-call(bf16[128,768]{1,0:T(8,128)(2,1)S(1)} %get-tuple-element.76.hidden_ref, bf16[768,4096]{1,0:T(8,128)(2,1)S(1)} %bitcast.10), custom_call_target="tpu_custom_call" | custom-call | flops 1 | bytes 1 | tf_op jit(solution)/shard_map/down/pallas_call | solution.py:279
  35.5 1.6 %collective-permute-done.17.refs_1_ = bf16[64,128]{1,0:T(8,128)(2,1)S(1)} collective-permute-done((bf16[64,128]{1,0:T(8,128)(2,1)S(1)}, bf16[64,128]{1,0:T(8,128)(2,1)S(1)}, u32[]{:S(2)}, u32[]{:S(2)}) %collective-permute-start.17) | collective-permute-done | bytes 16416 | tf_op jit(solution)/shard_map/ppermute | solution.py:446
  37.8 1.0 %collective-permute-start.22 = (bf16[24,4096]{1,0:T(8,128)(2,1)S(1)}, bf16[24,4096]{1,0:T(8,128)(2,1)S(1)}, u32[]{:S(2)}, u32[]{:S(2)}) collective-permute-start(bf16[24,4096]{1,0:T(8,128)(2,1)S(1)} %get-tuple-element.89), channel_id=1, source_target_pairs={{0,8},{8,0},{1,9},{9,1},{2,10},{10,2},{3,11},{11,3},{4,12},{12,4},... | collective-permute-start | bytes 589832 | tf_op jit(solution)/shard_map/ppermute | solution.py:446
  38.8 1.6 %collective-permute-start.19 = (bf16[32,512]{1,0:T(8,128)(2,1)S(1)}, bf16[32,512]{1,0:T(8,128)(2,1)S(1)}, u32[]{:S(2)}, u32[]{:S(2)}) collective-permute-start(bf16[32,512]{1,0:T(8,128)(2,1)S(1)} %get-tuple-element.85), channel_id=1, source_target_pairs={{0,1},{1,2},{2,3},{3,0},{4,5},{5,6},{6,7},{7,4},{8,9},{9,10},{10,1... | collective-permute-start | bytes 98312 | tf_op jit(solution)/shard_map/ppermute | solution.py:443
  40.4 1.3 %collective-permute-start.20 = (bf16[32,512]{1,0:T(8,128)(2,1)S(1)}, bf16[32,512]{1,0:T(8,128)(2,1)S(1)}, u32[]{:S(2)}, u32[]{:S(2)}) collective-permute-start(bf16[32,512]{1,0:T(8,128)(2,1)S(1)} %get-tuple-element.86), channel_id=1, source_target_pairs={{0,2},{1,3},{2,0},{3,1},{4,6},{5,7},{6,4},{7,5},{8,10},{9,11},{10,... | collective-permute-start | bytes 98312 | tf_op jit(solution)/shard_map/ppermute | solution.py:443
  41.7 1.1 %collective-permute-start.21 = (bf16[32,512]{1,0:T(8,128)(2,1)S(1)}, bf16[32,512]{1,0:T(8,128)(2,1)S(1)}, u32[]{:S(2)}, u32[]{:S(2)}) collective-permute-start(bf16[32,512]{1,0:T(8,128)(2,1)S(1)} %get-tuple-element.87), channel_id=1, source_target_pairs={{0,3},{1,0},{2,1},{3,2},{4,7},{5,4},{6,5},{7,6},{8,11},{9,8},{10,9... | collective-permute-start | bytes 98312 | tf_op jit(solution)/shard_map/ppermute | solution.py:443
  42.8 1.9 %collective-permute-done.19.refs_0_ = bf16[32,512]{1,0:T(8,128)(2,1)S(1)} collective-permute-done((bf16[32,512]{1,0:T(8,128)(2,1)S(1)}, bf16[32,512]{1,0:T(8,128)(2,1)S(1)}, u32[]{:S(2)}, u32[]{:S(2)}) %collective-permute-start.19) | collective-permute-done | bytes 32800 | tf_op jit(solution)/shard_map/ppermute | solution.py:443
  44.7 1.0 %collective-permute-start.23 = (bf16[8,4096]{1,0:T(8,128)(2,1)S(1)}, bf16[8,4096]{1,0:T(8,128)(2,1)S(1)}, u32[]{:S(2)}, u32[]{:S(2)}) collective-permute-start(bf16[8,4096]{1,0:T(8,128)(2,1)S(1)} %get-tuple-element.91), channel_id=1, source_target_pairs={{0,8},{8,0},{1,9},{9,1},{2,10},{10,2},{3,11},{11,3},{4,12},{12,4},... | collective-permute-start | bytes 196616 | tf_op jit(solution)/shard_map/ppermute | solution.py:446
  46.1 1.4 %collective-permute-start.26 = (bf16[8,4096]{1,0:T(8,128)(2,1)S(1)}, bf16[8,4096]{1,0:T(8,128)(2,1)S(1)}, u32[]{:S(2)}, u32[]{:S(2)}) collective-permute-start(bf16[8,4096]{1,0:T(8,128)(2,1)S(1)} %get-tuple-element.94), channel_id=1, source_target_pairs={{0,1},{1,2},{2,3},{3,0},{4,5},{5,6},{6,7},{7,4},{8,9},{9,10},{10,1... | collective-permute-start | bytes 196616 | tf_op jit(solution)/shard_map/ppermute | solution.py:443
  47.5 1.9 %collective-permute-start.25 = (bf16[8,4096]{1,0:T(8,128)(2,1)S(1)}, bf16[8,4096]{1,0:T(8,128)(2,1)S(1)}, u32[]{:S(2)}, u32[]{:S(2)}) collective-permute-start(bf16[8,4096]{1,0:T(8,128)(2,1)S(1)} %get-tuple-element.93), channel_id=1, source_target_pairs={{0,2},{1,3},{2,0},{3,1},{4,6},{5,7},{6,4},{7,5},{8,10},{9,11},{10,... | collective-permute-start | bytes 196616 | tf_op jit(solution)/shard_map/ppermute | solution.py:443
  49.5 1.0 %collective-permute-start.24 = (bf16[8,4096]{1,0:T(8,128)(2,1)S(1)}, bf16[8,4096]{1,0:T(8,128)(2,1)S(1)}, u32[]{:S(2)}, u32[]{:S(2)}) collective-permute-start(bf16[8,4096]{1,0:T(8,128)(2,1)S(1)} %get-tuple-element.92), channel_id=1, source_target_pairs={{0,3},{1,0},{2,1},{3,2},{4,7},{5,4},{6,5},{7,6},{8,11},{9,8},{10,9... | collective-permute-start | bytes 196616 | tf_op jit(solution)/shard_map/ppermute | solution.py:443
  50.5 2.4 %collective-permute-done.26 = bf16[8,4096]{1,0:T(8,128)(2,1)S(1)} collective-permute-done((bf16[8,4096]{1,0:T(8,128)(2,1)S(1)}, bf16[8,4096]{1,0:T(8,128)(2,1)S(1)}, u32[]{:S(2)}, u32[]{:S(2)}) %collective-permute-start.26) | collective-permute-done | bytes 65568 | tf_op jit(solution)/shard_map/ppermute | solution.py:443
  52.9 1.7 %collective-permute-done.25 = bf16[8,4096]{1,0:T(8,128)(2,1)S(1)} collective-permute-done((bf16[8,4096]{1,0:T(8,128)(2,1)S(1)}, bf16[8,4096]{1,0:T(8,128)(2,1)S(1)}, u32[]{:S(2)}, u32[]{:S(2)}) %collective-permute-start.25) | collective-permute-done | bytes 65568 | tf_op jit(solution)/shard_map/ppermute | solution.py:443
  54.7 0.7 %add_convert_fusion = bf16[8,4096]{1,0:T(8,128)(2,1)} fusion(bf16[8,4096]{1,0:T(8,128)(2,1)S(1)} %collective-permute-done.26, bf16[8,4096]{1,0:T(8,128)(2,1)S(1)} %collective-permute-done.25, f32[8,4096]{1,0:T(8,128)S(1)} %plus.1, bf16[8,4096]{1,0:T(8,128)(2,1)S(1)} %collective-permute-done.24), kind=kLoop, calls=%fused_computation.2 | loop fusion | flops 229376 | bytes 393216 | tf_op jit(solution)/shard_map/convert_element_type | solution.py:499
  (48 shorter events, 2.2 us)
Async XLA Ops:
  1.0 11.7 %collective-permute-start.2 = (bf16[8,4224]{1,0:T(8,128)(2,1)S(1)}, bf16[8,4224]{1,0:T(8,128)(2,1)S(1)}, u32[]{:S(2)}, u32[]{:S(2)}) collective-permute-start(bf16[8,4224]{1,0:T(8,128)(2,1)S(1)} %attach.1), channel_id=1, source_target_pairs={{0,3},{1,0},{2,1},{3,2},{4,7},{5,4},{6,5},{7,6},{8,11},{9,8},{10,9... | collective-permute-start | bytes 202760 | tf_op jit(solution)/shard_map/ppermute | solution.py:443
  6.1 6.6 %collective-permute-start.1 = (bf16[8,4224]{1,0:T(8,128)(2,1)S(1)}, bf16[8,4224]{1,0:T(8,128)(2,1)S(1)}, u32[]{:S(2)}, u32[]{:S(2)}) collective-permute-start(bf16[8,4224]{1,0:T(8,128)(2,1)S(1)} %attach.1), channel_id=1, source_target_pairs={{0,2},{1,3},{2,0},{3,1},{4,6},{5,7},{6,4},{7,5},{8,10},{9,11},{10,... | collective-permute-start | bytes 202760 | tf_op jit(solution)/shard_map/ppermute | solution.py:443
  6.1 6.6 %collective-permute-start = (bf16[8,4224]{1,0:T(8,128)(2,1)S(1)}, bf16[8,4224]{1,0:T(8,128)(2,1)S(1)}, u32[]{:S(2)}, u32[]{:S(2)}) collective-permute-start(bf16[8,4224]{1,0:T(8,128)(2,1)S(1)} %attach.1), channel_id=1, source_target_pairs={{0,1},{1,2},{2,3},{3,0},{4,5},{5,6},{6,7},{7,4},{8,9},{9,10},{10,1... | collective-permute-start | bytes 202760 | tf_op jit(solution)/shard_map/ppermute | solution.py:443
  7.1 5.7 %collective-permute-start.4 = (bf16[8,4224]{1,0:T(8,128)(2,1)S(1)}, bf16[8,4224]{1,0:T(8,128)(2,1)S(1)}, u32[]{:S(2)}, u32[]{:S(2)}) collective-permute-start(bf16[8,4224]{1,0:T(8,128)(2,1)S(1)} %attach.1), channel_id=1, source_target_pairs={{0,8},{8,0},{1,9},{9,1},{2,10},{10,2},{3,11},{11,3},{4,12},{12,4},... | collective-permute-start | bytes 202760 | tf_op jit(solution)/shard_map/ppermute | solution.py:446
  8.6 4.2 %collective-permute-start.3 = (bf16[128,1024]{1,0:T(8,128)(2,1)}, bf16[128,1024]{1,0:T(8,128)(2,1)S(1)}, u32[]{:S(2)}, u32[]{:S(2)}) collective-permute-start(bf16[128,1024]{1,0:T(8,128)(2,1)} %bitcast.11), channel_id=1, source_target_pairs={{0,4},{4,0},{1,5},{5,1},{2,6},{6,2},{3,7},{7,3},{8,12},{12,8},{9,1... | collective-permute-start | bytes 786440 | tf_op jit(solution)/shard_map/ppermute | solution.py:449
  12.8 9.1 %collective-permute-start.5 = (bf16[24,4224]{1,0:T(8,128)(2,1)S(1)}, bf16[24,4224]{1,0:T(8,128)(2,1)S(1)}, u32[]{:S(2)}, u32[]{:S(2)}) collective-permute-start(bf16[24,4224]{1,0:T(8,128)(2,1)S(1)} %pad_maximum_fusion.1), channel_id=1, source_target_pairs={{0,8},{8,0},{1,9},{9,1},{2,10},{10,2},{3,11},{11,3},{4,12},{12,4},... | collective-permute-start | bytes 608264 | tf_op jit(solution)/shard_map/ppermute | solution.py:446
  14.4 7.7 %copy-start = (bf16[4,32,1024]{2,1,0:T(8,128)(2,1)S(1)}, bf16[4,32,1024]{2,1,0:T(8,128)(2,1)}, u32[]{:S(2)}) copy-start(bf16[4,32,1024]{2,1,0:T(8,128)(2,1)} %param.23) | copy-start | bytes 786436
  14.4 9.0 %collective-permute-start.6 = (bf16[32,4224]{1,0:T(8,128)(2,1)S(1)}, bf16[32,4224]{1,0:T(8,128)(2,1)S(1)}, u32[]{:S(2)}, u32[]{:S(2)}) collective-permute-start(bf16[32,4224]{1,0:T(8,128)(2,1)S(1)} %pad_maximum_fusion.refs_0_), channel_id=1, source_target_pairs={{0,4},{4,0},{1,5},{5,1},{2,6},{6,2},{3,7},{7,3},{8,12},{12,8},{9,1... | collective-permute-start | bytes 811016 | tf_op jit(solution)/shard_map/ppermute | solution.py:449
  14.4 7.7 %collective-permute-start.8 = (bf16[3,32,192]{2,1,0:T(8,128)(2,1)S(1)}, bf16[3,32,192]{2,1,0:T(8,128)(2,1)S(1)}, u32[]{:S(2)}, u32[]{:S(2)}) collective-permute-start(bf16[3,32,192]{2,1,0:T(8,128)(2,1)S(1)} %get-tuple-element.60), channel_id=1, source_target_pairs={{0,1},{1,2},{2,3},{3,0},{4,5},{5,6},{6,7},{7,4},{8,9},{9,10},{10,1... | collective-permute-start | bytes 110600 | tf_op jit(solution)/shard_map/ppermute | solution.py:443
  16.1 7.0 %collective-permute-start.9 = (bf16[3,32,192]{2,1,0:T(8,128)(2,1)S(1)}, bf16[3,32,192]{2,1,0:T(8,128)(2,1)S(1)}, u32[]{:S(2)}, u32[]{:S(2)}) collective-permute-start(bf16[3,32,192]{2,1,0:T(8,128)(2,1)S(1)} %get-tuple-element.61), channel_id=1, source_target_pairs={{0,2},{1,3},{2,0},{3,1},{4,6},{5,7},{6,4},{7,5},{8,10},{9,11},{10,... | collective-permute-start | bytes 110600 | tf_op jit(solution)/shard_map/ppermute | solution.py:443
  17.0 6.1 %collective-permute-start.10 = (bf16[3,32,192]{2,1,0:T(8,128)(2,1)S(1)}, bf16[3,32,192]{2,1,0:T(8,128)(2,1)S(1)}, u32[]{:S(2)}, u32[]{:S(2)}) collective-permute-start(bf16[3,32,192]{2,1,0:T(8,128)(2,1)S(1)} %get-tuple-element.62), channel_id=1, source_target_pairs={{0,3},{1,0},{2,1},{3,2},{4,7},{5,4},{6,5},{7,6},{8,11},{9,8},{10,9... | collective-permute-start | bytes 110600 | tf_op jit(solution)/shard_map/ppermute | solution.py:443
  22.0 1.6 %collective-permute-start.7 = (bf16[32,4224]{1,0:T(8,128)(2,1)S(1)}, bf16[32,4224]{1,0:T(8,128)(2,1)S(1)}, u32[]{:S(2)}, u32[]{:S(2)}) collective-permute-start(bf16[32,4224]{1,0:T(8,128)(2,1)S(1)} %constant_dynamic-update-slice_fusion.refs_1_), channel_id=1, source_target_pairs={{0,4},{4,0},{1,5},{5,1},{2,6},{6,2},{3,7},{7,3},{8,12},{12,8},{9,1... | collective-permute-start | bytes 811016 | tf_op jit(solution)/shard_map/ppermute | solution.py:449
  22.1 9.5 %collective-permute-start.14 = (bf16[128,1024]{1,0:T(8,128)(2,1)S(1)}, bf16[128,1024]{1,0:T(8,128)(2,1)S(1)}, u32[]{:S(2)}, u32[]{:S(2)}) collective-permute-start(bf16[128,1024]{1,0:T(8,128)(2,1)S(1)} %bitcast.12), channel_id=1, source_target_pairs={{0,8},{8,0},{1,9},{9,1},{2,10},{10,2},{3,11},{11,3},{4,12},{12,4},... | collective-permute-start | bytes 786440 | tf_op jit(solution)/shard_map/ppermute | solution.py:446
  23.9 7.7 %collective-permute-start.11 = (bf16[128,256]{1,0:T(8,128)(2,1)S(1)}, bf16[128,256]{1,0:T(8,128)(2,1)S(1)}, u32[]{:S(2)}, u32[]{:S(2)}) collective-permute-start(bf16[128,256]{1,0:T(8,128)(2,1)S(1)} %get-tuple-element.68), channel_id=1, source_target_pairs={{0,1},{1,2},{2,3},{3,0},{4,5},{5,6},{6,7},{7,4},{8,9},{9,10},{10,1... | collective-permute-start | bytes 196616 | tf_op jit(solution)/shard_map/ppermute | solution.py:443
  24.8 8.0 %collective-permute-start.12 = (bf16[128,256]{1,0:T(8,128)(2,1)S(1)}, bf16[128,256]{1,0:T(8,128)(2,1)S(1)}, u32[]{:S(2)}, u32[]{:S(2)}) collective-permute-start(bf16[128,256]{1,0:T(8,128)(2,1)S(1)} %get-tuple-element.69), channel_id=1, source_target_pairs={{0,2},{1,3},{2,0},{3,1},{4,6},{5,7},{6,4},{7,5},{8,10},{9,11},{10,... | collective-permute-start | bytes 196616 | tf_op jit(solution)/shard_map/ppermute | solution.py:443
  26.4 8.0 %slice-start = ((s8[6291456]{0:T(1024)(128)(4,1)}), s8[4194304]{0:T(1024)(128)(4,1)S(1)}, s32[]{:S(2)}) async-start(s8[6291456]{0:T(1024)(128)(4,1)} %bitcast.8), calls=%async_computation | async-start | bytes 8388608
  26.4 8.0 %slice-start.1 = ((s8[6291456]{0:T(1024)(128)(4,1)}), s8[2097152]{0:T(1024)(128)(4,1)S(1)}, s32[]{:S(2)}) async-start(s8[6291456]{0:T(1024)(128)(4,1)} %bitcast.8), calls=%async_computation.1 | async-start | bytes 4194304
  26.4 6.4 %collective-permute-start.13 = (bf16[128,256]{1,0:T(8,128)(2,1)S(1)}, bf16[128,256]{1,0:T(8,128)(2,1)S(1)}, u32[]{:S(2)}, u32[]{:S(2)}) collective-permute-start(bf16[128,256]{1,0:T(8,128)(2,1)S(1)} %get-tuple-element.70), channel_id=1, source_target_pairs={{0,3},{1,0},{2,1},{3,2},{4,7},{5,4},{6,5},{7,6},{8,11},{9,8},{10,9... | collective-permute-start | bytes 196616 | tf_op jit(solution)/shard_map/ppermute | solution.py:443
  33.3 3.8 %collective-permute-start.17 = (bf16[64,128]{1,0:T(8,128)(2,1)S(1)}, bf16[64,128]{1,0:T(8,128)(2,1)S(1)}, u32[]{:S(2)}, u32[]{:S(2)}) collective-permute-start(bf16[64,128]{1,0:T(8,128)(2,1)S(1)} %get-tuple-element.82), channel_id=1, source_target_pairs={{0,8},{8,0},{1,9},{9,1},{2,10},{10,2},{3,11},{11,3},{4,12},{12,4},... | collective-permute-start | bytes 49160 | tf_op jit(solution)/shard_map/ppermute | solution.py:446
  35.4 2.0 %collective-permute-start.15 = (bf16[64,4096]{1,0:T(8,128)(2,1)S(1)}, bf16[64,4096]{1,0:T(8,128)(2,1)S(1)}, u32[]{:S(2)}, u32[]{:S(2)}) collective-permute-start(bf16[64,4096]{1,0:T(8,128)(2,1)S(1)} %get-tuple-element.78), channel_id=1, source_target_pairs={{0,4},{4,0},{1,5},{5,1},{2,6},{6,2},{3,7},{7,3},{8,12},{12,8},{9,1... | collective-permute-start | bytes 1572872 | tf_op jit(solution)/shard_map/ppermute | solution.py:449
  37.1 1.7 %collective-permute-start.18 = (bf16[32,256]{1,0:T(8,128)(2,1)S(1)}, bf16[32,256]{1,0:T(8,128)(2,1)S(1)}, u32[]{:S(2)}, u32[]{:S(2)}) collective-permute-start(bf16[32,256]{1,0:T(8,128)(2,1)S(1)} %get-tuple-element.84), channel_id=1, source_target_pairs={{0,4},{4,0},{1,5},{5,1},{2,6},{6,2},{3,7},{7,3},{8,12},{12,8},{9,1... | collective-permute-start | bytes 49160 | tf_op jit(solution)/shard_map/ppermute | solution.py:449
  37.5 8.3 %collective-permute-start.16 = (bf16[128,1024]{1,0:T(8,128)(2,1)S(1)}, bf16[128,1024]{1,0:T(8,128)(2,1)S(1)}, u32[]{:S(2)}, u32[]{:S(2)}) collective-permute-start(bf16[128,1024]{1,0:T(8,128)(2,1)S(1)} %collective-permute-done.14.refs_2_), channel_id=1, source_target_pairs={{0,4},{4,0},{1,5},{5,1},{2,6},{6,2},{3,7},{7,3},{8,12},{12,8},{9,1... | collective-permute-start | bytes 786440 | tf_op jit(solution)/shard_map/ppermute | solution.py:449
  37.8 8.0 %collective-permute-start.22 = (bf16[24,4096]{1,0:T(8,128)(2,1)S(1)}, bf16[24,4096]{1,0:T(8,128)(2,1)S(1)}, u32[]{:S(2)}, u32[]{:S(2)}) collective-permute-start(bf16[24,4096]{1,0:T(8,128)(2,1)S(1)} %get-tuple-element.89), channel_id=1, source_target_pairs={{0,8},{8,0},{1,9},{9,1},{2,10},{10,2},{3,11},{11,3},{4,12},{12,4},... | collective-permute-start | bytes 589832 | tf_op jit(solution)/shard_map/ppermute | solution.py:446
  38.8 5.9 %collective-permute-start.19 = (bf16[32,512]{1,0:T(8,128)(2,1)S(1)}, bf16[32,512]{1,0:T(8,128)(2,1)S(1)}, u32[]{:S(2)}, u32[]{:S(2)}) collective-permute-start(bf16[32,512]{1,0:T(8,128)(2,1)S(1)} %get-tuple-element.85), channel_id=1, source_target_pairs={{0,1},{1,2},{2,3},{3,0},{4,5},{5,6},{6,7},{7,4},{8,9},{9,10},{10,1... | collective-permute-start | bytes 98312 | tf_op jit(solution)/shard_map/ppermute | solution.py:443
  40.4 5.3 %collective-permute-start.20 = (bf16[32,512]{1,0:T(8,128)(2,1)S(1)}, bf16[32,512]{1,0:T(8,128)(2,1)S(1)}, u32[]{:S(2)}, u32[]{:S(2)}) collective-permute-start(bf16[32,512]{1,0:T(8,128)(2,1)S(1)} %get-tuple-element.86), channel_id=1, source_target_pairs={{0,2},{1,3},{2,0},{3,1},{4,6},{5,7},{6,4},{7,5},{8,10},{9,11},{10,... | collective-permute-start | bytes 98312 | tf_op jit(solution)/shard_map/ppermute | solution.py:443
  41.7 4.1 %collective-permute-start.21 = (bf16[32,512]{1,0:T(8,128)(2,1)S(1)}, bf16[32,512]{1,0:T(8,128)(2,1)S(1)}, u32[]{:S(2)}, u32[]{:S(2)}) collective-permute-start(bf16[32,512]{1,0:T(8,128)(2,1)S(1)} %get-tuple-element.87), channel_id=1, source_target_pairs={{0,3},{1,0},{2,1},{3,2},{4,7},{5,4},{6,5},{7,6},{8,11},{9,8},{10,9... | collective-permute-start | bytes 98312 | tf_op jit(solution)/shard_map/ppermute | solution.py:443
  44.7 5.8 %collective-permute-start.23 = (bf16[8,4096]{1,0:T(8,128)(2,1)S(1)}, bf16[8,4096]{1,0:T(8,128)(2,1)S(1)}, u32[]{:S(2)}, u32[]{:S(2)}) collective-permute-start(bf16[8,4096]{1,0:T(8,128)(2,1)S(1)} %get-tuple-element.91), channel_id=1, source_target_pairs={{0,8},{8,0},{1,9},{9,1},{2,10},{10,2},{3,11},{11,3},{4,12},{12,4},... | collective-permute-start | bytes 196616 | tf_op jit(solution)/shard_map/ppermute | solution.py:446
  46.1 6.8 %collective-permute-start.26 = (bf16[8,4096]{1,0:T(8,128)(2,1)S(1)}, bf16[8,4096]{1,0:T(8,128)(2,1)S(1)}, u32[]{:S(2)}, u32[]{:S(2)}) collective-permute-start(bf16[8,4096]{1,0:T(8,128)(2,1)S(1)} %get-tuple-element.94), channel_id=1, source_target_pairs={{0,1},{1,2},{2,3},{3,0},{4,5},{5,6},{6,7},{7,4},{8,9},{9,10},{10,1... | collective-permute-start | bytes 196616 | tf_op jit(solution)/shard_map/ppermute | solution.py:443
  47.5 7.1 %collective-permute-start.25 = (bf16[8,4096]{1,0:T(8,128)(2,1)S(1)}, bf16[8,4096]{1,0:T(8,128)(2,1)S(1)}, u32[]{:S(2)}, u32[]{:S(2)}) collective-permute-start(bf16[8,4096]{1,0:T(8,128)(2,1)S(1)} %get-tuple-element.93), channel_id=1, source_target_pairs={{0,2},{1,3},{2,0},{3,1},{4,6},{5,7},{6,4},{7,5},{8,10},{9,11},{10,... | collective-permute-start | bytes 196616 | tf_op jit(solution)/shard_map/ppermute | solution.py:443
  49.5 5.2 %collective-permute-start.24 = (bf16[8,4096]{1,0:T(8,128)(2,1)S(1)}, bf16[8,4096]{1,0:T(8,128)(2,1)S(1)}, u32[]{:S(2)}, u32[]{:S(2)}) collective-permute-start(bf16[8,4096]{1,0:T(8,128)(2,1)S(1)} %get-tuple-element.92), channel_id=1, source_target_pairs={{0,3},{1,0},{2,1},{3,2},{4,7},{5,4},{6,5},{7,6},{8,11},{9,8},{10,9... | collective-permute-start | bytes 196616 | tf_op jit(solution)/shard_map/ppermute | solution.py:443

commit v20 on v19

--- a/solution.py
+++ b/solution.py
@@ -12,6 +12,7 @@
 SMALL_LIMIT = 4 * 1024 * 1024
 VMEM_LIMIT = 12 * 1024 * 1024
 PIECES = 8
+FIRST = 128
 LONG = pl.CostEstimate(flops=1_000_000_000, bytes_accessed=1, transcendentals=0)
 LONGER = pl.CostEstimate(flops=10_000_000_000, bytes_accessed=1, transcendentals=0)
 LAST = pl.CostEstimate(flops=1_000_000_000, bytes_accessed=1, transcendentals=0)
@@ -73,17 +74,20 @@
     )(*in_hbm(tokens, routes, probs))
 
 
-def piece_copies(source, target, sems):
-    step = source.shape[0] // PIECES
-    spans = [pl.ds(i * step, step) for i in range(PIECES)]
+def piece_copies(source, target, sems, skip=0):
+    step = target.shape[0] // PIECES
     return [
-        pltpu.make_async_copy(source.at[span], target.at[span], sems.at[i])
-        for i, span in enumerate(spans)
+        pltpu.make_async_copy(
+            source.at[pl.ds(skip + i * step, step)],
+            target.at[pl.ds(i * step, step)],
+            sems.at[i],
+        )
+        for i in range(PIECES)
     ]
 
 
 def load_kernel(source, target, sems):
-    copies = piece_copies(source, target, sems)
+    copies = piece_copies(source, target, sems, source.shape[0] - target.shape[0])
     for copy in copies:
         copy.start()
     for copy in copies:
@@ -95,7 +99,7 @@
         load_kernel,
         in_specs=[pl.BlockSpec(memory_space=pltpu.HBM)],
         out_specs=pl.BlockSpec(memory_space=pltpu.VMEM),
-        out_shape=pltpu.VMEM(weights.shape, weights.dtype),
+        out_shape=pltpu.VMEM((weights.shape[0] - FIRST, weights.shape[1]), weights.dtype),
         scratch_shapes=[pltpu.SemaphoreType.DMA((PIECES,))],
         compiler_params=pltpu.CompilerParams(vmem_limit_bytes=SMALL_LIMIT),
         cost_estimate=SOME,
@@ -104,9 +108,12 @@
 
 
 def prepare_kernel(parts, *refs):
-    ins, lefts, source = refs[:3], refs[3:5], refs[5]
-    target, left_ref, outs, sems = refs[6], refs[7], refs[8:-1], refs[-1]
-    copies = piece_copies(source, target, sems)
+    ins, lefts, sources = refs[:3], refs[3:5], refs[5:7]
+    targets, left_ref, outs, sems = refs[7:9], refs[9], refs[10:-1], refs[-1]
+    copies = piece_copies(sources[0], targets[0], sems)
+    copies.append(
+        pltpu.make_async_copy(sources[1].at[pl.ds(0, FIRST)], targets[1], sems.at[PIECES])
+    )
     for copy in copies:
         copy.start()
     half = left_ref.shape[0] // 2
@@ -134,16 +141,19 @@
     vmem = pl.BlockSpec(memory_space=pltpu.VMEM)
     return pl.pallas_call(
         functools.partial(prepare_kernel, parts),
-        in_specs=[vmem] * 5 + [pl.BlockSpec(memory_space=pltpu.HBM)],
-        out_specs=[vmem] * (2 + parts),
-        out_shape=[pltpu.VMEM(weights.shape, weights.dtype)]
+        in_specs=[vmem] * 5 + [pl.BlockSpec(memory_space=pltpu.HBM)] * 2,
+        out_specs=[vmem] * (3 + parts),
+        out_shape=[
+            pltpu.VMEM(weights[0].shape, BF),
+            pltpu.VMEM((FIRST, weights[1].shape[1]), BF),
+        ]
         + [jax.ShapeDtypeStruct((2 * exp_dev * rank, block), BF)]
         + [jax.ShapeDtypeStruct((3, exp_dev * piece, hid // parts), BF)] * parts,
-        scratch_shapes=[pltpu.SemaphoreType.DMA((PIECES,))],
+        scratch_shapes=[pltpu.SemaphoreType.DMA((PIECES + 1,))],
         compiler_params=pltpu.CompilerParams(vmem_limit_bytes=SMALL_LIMIT),
         cost_estimate=BRIEF,
         name="prepare",
-    )(*in_hbm(*factors, *lefts, weights))
+    )(*in_hbm(*factors, *lefts, *weights))
 
 
 def spread_kernel(parts, exp_dev, *refs):
@@ -201,16 +211,17 @@
 
 
 def raw_kernel(count, tile, *refs):
-    lines, (gate_w, up_w, gate_ref, up_ref) = refs[:count], refs[count:]
+    lines, (gate_w, up_first, up_w, gate_ref, up_ref) = refs[:count], refs[count:]
     hid, width = gate_w.shape
     x = jnp.concatenate([line[:, :width] for line in lines])
     for i in range(hid // tile):
         span = pl.ds(i * tile, tile)
         gate_ref[:, span] = dot_nt(gate_w[span], x).T
-        up_ref[:, span] = dot_nt(up_w[span], x).T
-
-
-def raw_products(lines, gate_w, up_w):
+    up_ref[:, :FIRST] = dot_nt(up_first[...], x).T
+    up_ref[:, FIRST:] = dot_nt(up_w[...], x).T
+
+
+def raw_products(lines, gate_w, up_first, up_w):
     hid = gate_w.shape[0]
     total = sum(line.shape[0] for line in lines)
     tile = 384
@@ -220,7 +231,7 @@
         compiler_params=pltpu.CompilerParams(vmem_limit_bytes=VMEM_LIMIT),
         cost_estimate=BRIEF,
         name="raw",
-    )(*lines, gate_w, up_w)
+    )(*lines, gate_w, up_first, up_w)
 
 
 def hidden_kernel(parts, count, exp_dev, pair, *refs):
@@ -453,12 +464,12 @@
     arrived = [along_z(sent, k) for k in range(1, parts)]
     first = [along_y(sent, s) for s in range(1, chips)]
     gate_w, up_w = (jnp.swapaxes(w, 1, 2).reshape(hid, width) for w in (w_gate, w_up))
-    gate_w, left, *small = prepare(
-        (gate_right, up_right, down_left), (gate_left, up_left), gate_w, parts
+    gate_w, up_first, left, *small = prepare(
+        (gate_right, up_right, down_left), (gate_left, up_left), (gate_w, up_w), parts
     )
     right = down_right.reshape(ranks, block)
     partner_right = other_core(right)
-    rest = after(jnp.concatenate(arrived), (left, small, gate_w, partner_right))
+    rest = after(jnp.concatenate(arrived), (left, small, gate_w, up_first, partner_right))
     up_w = load(after(up_w, rest))
     lines = [jnp.concatenate([sent, rest])]
     partner = [other_core(lines[0])]
@@ -476,7 +487,7 @@
     lines = after(tuple(lines), diag)
     inner = inner_products(lines, left, parts, rows)
     inner = [inner[0]] + [along_z(inner[k], k) for k in range(1, parts)]
-    raw = raw_products(lines, gate_w, up_w)
+    raw = raw_products(lines, gate_w, up_first, up_w)
     right = after(right, arrival)
     rights = [right] + [along_y(right, -s) for s in range(1, chips)]
     raw = after(tuple(raw), rights[1:])

time: 55.5 us -> 55.5 us (level)
  no operation moved by 1% of the time
where the time goes in v20:
time: 55.5 us; the launch traced here: 55.3 us
  starting transfers between devices  31.3 us (56%)
  Pallas kernels  14 us (25%)
  waiting for transfers between devices  9.02 us (16%)
  other arithmetic  0.71 us (1%)
    ppermute x15, starting transfers between devices, along_z(): lax.ppermute(value, 'mp', [(i, (i + step) % parts) for i in range(parts)])  23.7 us
    ppermute x6, starting transfers between devices, along_y(): lax.ppermute(value, 'y', [(i, (i + step) % chips) for i in range(chips)])  7.18 us
    ppermute x15, waiting for transfers between devices, along_z(): lax.ppermute(value, 'mp', [(i, (i + step) % parts) for i in range(parts)])  7.11 us
    pallas_call x1, Pallas kernels, prepare(): pl.pallas_call(functools.partial(prepare_kernel, parts), in_specs=[vmem]...  4.41 us
    pallas_call x1, Pallas kernels, raw_products(): pl.pallas_call(functools.partial(raw_kernel, len(lines), tile), out_shape...  3.49 us
    pallas_call x1, Pallas kernels, load(): pl.pallas_call(load_kernel, in_specs=[pl.BlockSpec(memory_space=pltpu.HBM...  2.54 us
    ppermute x6, waiting for transfers between devices, along_y(): lax.ppermute(value, 'y', [(i, (i + step) % chips) for i in range(chips)])  1.64 us
  transfers between devices with their start and end apart: 27, of which 8 were waited for; matrix products, arithmetic and copies ran while one was open for 0% of the time, Pallas kernels for 23%

profile of v20, /device:TPU:0, one launch (start us, length us, event | category | flops | bytes accessed | tf_op | source)
XLA Modules:
  0.0 55.3 jit_solution(16266922723768843011)
XLA Ops:
  0.0 0.9 %attach.1 = bf16[8,4224]{1,0:T(8,128)(2,1)S(1)} custom-call(bf16[8,4096]{1,0:T(8,128)(2,1)} %tokens_ref.1, s32[8,8]{1,0:T(8,128)} %routes_ref.1, f32[8,8]{1,0:T(8,128)} %probs_ref.1), custom_call_target="tpu_custom_call" | custom-call | flops 1 | bytes 1 | tf_op jit(solution)/shard_map/attach/pallas_call | solution.py:68
  1.0 5.1 %collective-permute-start.2 = (bf16[8,4224]{1,0:T(8,128)(2,1)S(1)}, bf16[8,4224]{1,0:T(8,128)(2,1)S(1)}, u32[]{:S(2)}, u32[]{:S(2)}) collective-permute-start(bf16[8,4224]{1,0:T(8,128)(2,1)S(1)} %attach.1), channel_id=1, source_target_pairs={{0,3},{1,0},{2,1},{3,2},{4,7},{5,4},{6,5},{7,6},{8,11},{9,8},{10,9... | collective-permute-start | bytes 202760 | tf_op jit(solution)/shard_map/ppermute | solution.py:454
  6.1 1.0 %collective-permute-start = (bf16[8,4224]{1,0:T(8,128)(2,1)S(1)}, bf16[8,4224]{1,0:T(8,128)(2,1)S(1)}, u32[]{:S(2)}, u32[]{:S(2)}) collective-permute-start(bf16[8,4224]{1,0:T(8,128)(2,1)S(1)} %attach.1), channel_id=1, source_target_pairs={{0,1},{1,2},{2,3},{3,0},{4,5},{5,6},{6,7},{7,4},{8,9},{9,10},{10,1... | collective-permute-start | bytes 202760 | tf_op jit(solution)/shard_map/ppermute | solution.py:454
  7.1 1.5 %collective-permute-start.4 = (bf16[8,4224]{1,0:T(8,128)(2,1)S(1)}, bf16[8,4224]{1,0:T(8,128)(2,1)S(1)}, u32[]{:S(2)}, u32[]{:S(2)}) collective-permute-start(bf16[8,4224]{1,0:T(8,128)(2,1)S(1)} %attach.1), channel_id=1, source_target_pairs={{0,8},{8,0},{1,9},{9,1},{2,10},{10,2},{3,11},{11,3},{4,12},{12,4},... | collective-permute-start | bytes 202760 | tf_op jit(solution)/shard_map/ppermute | solution.py:457
  8.6 4.4 %prepare.1 = (bf16[768,4096]{1,0:T(8,128)(2,1)S(1)}, bf16[128,4096]{1,0:T(8,128)(2,1)S(1)}, bf16[256,1024]{1,0:T(8,128)(2,1)S(1)}, bf16[3,32,192]{2,1,0:T(8,128)...) custom-call(bf16[4,8,768]{2,1,0:T(8,128)(2,1)} %refs_0_.1, ...), custom_call_target="tpu_custom_call" | custom-call | flops 1 | bytes 1 | tf_op jit(solution)/shard_map/prepare/pallas_call | solution.py:142
  13.1 1.2 %collective-permute-start.5 = (bf16[24,4224]{1,0:T(8,128)(2,1)S(1)}, bf16[24,4224]{1,0:T(8,128)(2,1)S(1)}, u32[]{:S(2)}, u32[]{:S(2)}) collective-permute-start(bf16[24,4224]{1,0:T(8,128)(2,1)S(1)} %pad_maximum_fusion.1), channel_id=1, source_target_pairs={{0,8},{8,0},{1,9},{9,1},{2,10},{10,2},{3,11},{11,3},{4,12},{12,4},... | collective-permute-start | bytes 608264 | tf_op jit(solution)/shard_map/ppermute | solution.py:457
  14.4 2.0 %collective-permute-start.8 = (bf16[3,32,192]{2,1,0:T(8,128)(2,1)S(1)}, bf16[3,32,192]{2,1,0:T(8,128)(2,1)S(1)}, u32[]{:S(2)}, u32[]{:S(2)}) collective-permute-start(bf16[3,32,192]{2,1,0:T(8,128)(2,1)S(1)} %get-tuple-element.62), channel_id=1, source_target_pairs={{0,1},{1,2},{2,3},{3,0},{4,5},{5,6},{6,7},{7,4},{8,9},{9,10},{10,1... | collective-permute-start | bytes 110600 | tf_op jit(solution)/shard_map/ppermute | solution.py:454
  16.4 0.9 %collective-permute-start.9 = (bf16[3,32,192]{2,1,0:T(8,128)(2,1)S(1)}, bf16[3,32,192]{2,1,0:T(8,128)(2,1)S(1)}, u32[]{:S(2)}, u32[]{:S(2)}) collective-permute-start(bf16[3,32,192]{2,1,0:T(8,128)(2,1)S(1)} %get-tuple-element.63), channel_id=1, source_target_pairs={{0,2},{1,3},{2,0},{3,1},{4,6},{5,7},{6,4},{7,5},{8,10},{9,11},{10,... | collective-permute-start | bytes 110600 | tf_op jit(solution)/shard_map/ppermute | solution.py:454
  17.3 1.7 %collective-permute-start.10 = (bf16[3,32,192]{2,1,0:T(8,128)(2,1)S(1)}, bf16[3,32,192]{2,1,0:T(8,128)(2,1)S(1)}, u32[]{:S(2)}, u32[]{:S(2)}) collective-permute-start(bf16[3,32,192]{2,1,0:T(8,128)(2,1)S(1)} %get-tuple-element.64), channel_id=1, source_target_pairs={{0,3},{1,0},{2,1},{3,2},{4,7},{5,4},{6,5},{7,6},{8,11},{9,8},{10,9... | collective-permute-start | bytes 110600 | tf_op jit(solution)/shard_map/ppermute | solution.py:454
  19.1 2.5 %load.1.refs_6_ = bf16[640,4096]{1,0:T(8,128)(2,1)S(1)} custom-call(bf16[768,4096]{1,0:T(8,128)(2,1)} %bitcast.15), custom_call_target="tpu_custom_call" | custom-call | flops 3000000000 | bytes 1 | tf_op jit(solution)/shard_map/load/pallas_call | solution.py:98
  21.7 1.3 %collective-permute-start.14 = (bf16[128,1024]{1,0:T(8,128)(2,1)S(1)}, bf16[128,1024]{1,0:T(8,128)(2,1)S(1)}, u32[]{:S(2)}, u32[]{:S(2)}) collective-permute-start(bf16[128,1024]{1,0:T(8,128)(2,1)S(1)} %bitcast.12), channel_id=1, source_target_pairs={{0,8},{8,0},{1,9},{9,1},{2,10},{10,2},{3,11},{11,3},{4,12},{12,4},... | collective-permute-start | bytes 786440 | tf_op jit(solution)/shard_map/ppermute | solution.py:457
  23.8 1.4 %collective-permute-start.11 = (bf16[128,256]{1,0:T(8,128)(2,1)S(1)}, bf16[128,256]{1,0:T(8,128)(2,1)S(1)}, u32[]{:S(2)}, u32[]{:S(2)}) collective-permute-start(bf16[128,256]{1,0:T(8,128)(2,1)S(1)} %get-tuple-element.70), channel_id=1, source_target_pairs={{0,1},{1,2},{2,3},{3,0},{4,5},{5,6},{6,7},{7,4},{8,9},{9,10},{10,1... | collective-permute-start | bytes 196616 | tf_op jit(solution)/shard_map/ppermute | solution.py:454
  25.1 1.3 %collective-permute-start.12 = (bf16[128,256]{1,0:T(8,128)(2,1)S(1)}, bf16[128,256]{1,0:T(8,128)(2,1)S(1)}, u32[]{:S(2)}, u32[]{:S(2)}) collective-permute-start(bf16[128,256]{1,0:T(8,128)(2,1)S(1)} %get-tuple-element.71), channel_id=1, source_target_pairs={{0,2},{1,3},{2,0},{3,1},{4,6},{5,7},{6,4},{7,5},{8,10},{9,11},{10,... | collective-permute-start | bytes 196616 | tf_op jit(solution)/shard_map/ppermute | solution.py:454
  26.4 1.4 %collective-permute-start.13 = (bf16[128,256]{1,0:T(8,128)(2,1)S(1)}, bf16[128,256]{1,0:T(8,128)(2,1)S(1)}, u32[]{:S(2)}, u32[]{:S(2)}) collective-permute-start(bf16[128,256]{1,0:T(8,128)(2,1)S(1)} %get-tuple-element.72), channel_id=1, source_target_pairs={{0,3},{1,0},{2,1},{3,2},{4,7},{5,4},{6,5},{7,6},{8,11},{9,8},{10,9... | collective-permute-start | bytes 196616 | tf_op jit(solution)/shard_map/ppermute | solution.py:454
  27.8 3.5 %raw.1 = (f32[128,768]{1,0:T(8,128)S(1)}, f32[128,768]{1,0:T(8,128)S(1)}) custom-call(bf16[32,4224]{1,0:T(8,128)(2,1)S(1)} %pad_maximum_fusion.refs_0_, bf16[32,4224]{1,0:T(8,128)(2,1)S(1)} %constant_dynamic-update-slice_fusion.refs_1_, bf16[32,4224]{1,0:T(8,128)(2,1)S(1)} %collective-permute-done.6.refs_2_, ...), custom_call_target="tpu_custom_call" | custom-call | flops 1 | bytes 1 | tf_op jit(solution)/shard_map/raw/pallas_call | solution.py:228
  31.3 1.4 %collective-permute-done.12.refs_6_ = bf16[128,256]{1,0:T(8,128)(2,1)S(1)} collective-permute-done((bf16[128,256]{1,0:T(8,128)(2,1)S(1)}, bf16[128,256]{1,0:T(8,128)(2,1)S(1)}, u32[]{:S(2)}, u32[]{:S(2)}) %collective-permute-start.12) | collective-permute-done | bytes 65568 | tf_op jit(solution)/shard_map/ppermute | solution.py:454
  32.7 0.5 hidden.1
  33.2 1.1 %collective-permute-start.17 = (bf16[64,128]{1,0:T(8,128)(2,1)S(1)}, bf16[64,128]{1,0:T(8,128)(2,1)S(1)}, u32[]{:S(2)}, u32[]{:S(2)}) collective-permute-start(bf16[64,128]{1,0:T(8,128)(2,1)S(1)} %get-tuple-element.84), channel_id=1, source_target_pairs={{0,8},{8,0},{1,9},{9,1},{2,10},{10,2},{3,11},{11,3},{4,12},{12,4},... | collective-permute-start | bytes 49160 | tf_op jit(solution)/shard_map/ppermute | solution.py:457
  34.3 1.0 %down.1 = (f32[64,4096]{1,0:T(8,128)S(1)}, bf16[64,4096]{1,0:T(8,128)(2,1)S(1)}) custom-call(bf16[128,768]{1,0:T(8,128)(2,1)S(1)} %get-tuple-element.78.hidden_ref, bf16[768,4096]{1,0:T(8,128)(2,1)S(1)} %bitcast.10), custom_call_target="tpu_custom_call" | custom-call | flops 1 | bytes 1 | tf_op jit(solution)/shard_map/down/pallas_call | solution.py:290
  35.4 1.6 %collective-permute-done.17.refs_1_ = bf16[64,128]{1,0:T(8,128)(2,1)S(1)} collective-permute-done((bf16[64,128]{1,0:T(8,128)(2,1)S(1)}, bf16[64,128]{1,0:T(8,128)(2,1)S(1)}, u32[]{:S(2)}, u32[]{:S(2)}) %collective-permute-start.17) | collective-permute-done | bytes 16416 | tf_op jit(solution)/shard_map/ppermute | solution.py:457
  37.7 1.0 %collective-permute-start.22 = (bf16[24,4096]{1,0:T(8,128)(2,1)S(1)}, bf16[24,4096]{1,0:T(8,128)(2,1)S(1)}, u32[]{:S(2)}, u32[]{:S(2)}) collective-permute-start(bf16[24,4096]{1,0:T(8,128)(2,1)S(1)} %get-tuple-element.91), channel_id=1, source_target_pairs={{0,8},{8,0},{1,9},{9,1},{2,10},{10,2},{3,11},{11,3},{4,12},{12,4},... | collective-permute-start | bytes 589832 | tf_op jit(solution)/shard_map/ppermute | solution.py:457
  38.7 1.9 %collective-permute-start.19 = (bf16[32,512]{1,0:T(8,128)(2,1)S(1)}, bf16[32,512]{1,0:T(8,128)(2,1)S(1)}, u32[]{:S(2)}, u32[]{:S(2)}) collective-permute-start(bf16[32,512]{1,0:T(8,128)(2,1)S(1)} %get-tuple-element.87), channel_id=1, source_target_pairs={{0,1},{1,2},{2,3},{3,0},{4,5},{5,6},{6,7},{7,4},{8,9},{9,10},{10,1... | collective-permute-start | bytes 98312 | tf_op jit(solution)/shard_map/ppermute | solution.py:454
  40.7 1.1 %collective-permute-start.20 = (bf16[32,512]{1,0:T(8,128)(2,1)S(1)}, bf16[32,512]{1,0:T(8,128)(2,1)S(1)}, u32[]{:S(2)}, u32[]{:S(2)}) collective-permute-start(bf16[32,512]{1,0:T(8,128)(2,1)S(1)} %get-tuple-element.88), channel_id=1, source_target_pairs={{0,2},{1,3},{2,0},{3,1},{4,6},{5,7},{6,4},{7,5},{8,10},{9,11},{10,... | collective-permute-start | bytes 98312 | tf_op jit(solution)/shard_map/ppermute | solution.py:454
  41.7 1.4 %collective-permute-start.21 = (bf16[32,512]{1,0:T(8,128)(2,1)S(1)}, bf16[32,512]{1,0:T(8,128)(2,1)S(1)}, u32[]{:S(2)}, u32[]{:S(2)}) collective-permute-start(bf16[32,512]{1,0:T(8,128)(2,1)S(1)} %get-tuple-element.89), channel_id=1, source_target_pairs={{0,3},{1,0},{2,1},{3,2},{4,7},{5,4},{6,5},{7,6},{8,11},{9,8},{10,9... | collective-permute-start | bytes 98312 | tf_op jit(solution)/shard_map/ppermute | solution.py:454
  43.1 1.5 %collective-permute-done.19.refs_0_ = bf16[32,512]{1,0:T(8,128)(2,1)S(1)} collective-permute-done((bf16[32,512]{1,0:T(8,128)(2,1)S(1)}, bf16[32,512]{1,0:T(8,128)(2,1)S(1)}, u32[]{:S(2)}, u32[]{:S(2)}) %collective-permute-start.19) | collective-permute-done | bytes 32800 | tf_op jit(solution)/shard_map/ppermute | solution.py:454
  44.6 1.0 %collective-permute-start.23 = (bf16[8,4096]{1,0:T(8,128)(2,1)S(1)}, bf16[8,4096]{1,0:T(8,128)(2,1)S(1)}, u32[]{:S(2)}, u32[]{:S(2)}) collective-permute-start(bf16[8,4096]{1,0:T(8,128)(2,1)S(1)} %get-tuple-element.93), channel_id=1, source_target_pairs={{0,8},{8,0},{1,9},{9,1},{2,10},{10,2},{3,11},{11,3},{4,12},{12,4},... | collective-permute-start | bytes 196616 | tf_op jit(solution)/shard_map/ppermute | solution.py:457
  46.2 1.2 %collective-permute-start.26 = (bf16[8,4096]{1,0:T(8,128)(2,1)S(1)}, bf16[8,4096]{1,0:T(8,128)(2,1)S(1)}, u32[]{:S(2)}, u32[]{:S(2)}) collective-permute-start(bf16[8,4096]{1,0:T(8,128)(2,1)S(1)} %get-tuple-element.96), channel_id=1, source_target_pairs={{0,1},{1,2},{2,3},{3,0},{4,5},{5,6},{6,7},{7,4},{8,9},{9,10},{10,1... | collective-permute-start | bytes 196616 | tf_op jit(solution)/shard_map/ppermute | solution.py:454
  47.5 2.3 %collective-permute-start.25 = (bf16[8,4096]{1,0:T(8,128)(2,1)S(1)}, bf16[8,4096]{1,0:T(8,128)(2,1)S(1)}, u32[]{:S(2)}, u32[]{:S(2)}) collective-permute-start(bf16[8,4096]{1,0:T(8,128)(2,1)S(1)} %get-tuple-element.95), channel_id=1, source_target_pairs={{0,2},{1,3},{2,0},{3,1},{4,6},{5,7},{6,4},{7,5},{8,10},{9,11},{10,... | collective-permute-start | bytes 196616 | tf_op jit(solution)/shard_map/ppermute | solution.py:454
  49.7 1.1 %collective-permute-start.24 = (bf16[8,4096]{1,0:T(8,128)(2,1)S(1)}, bf16[8,4096]{1,0:T(8,128)(2,1)S(1)}, u32[]{:S(2)}, u32[]{:S(2)}) collective-permute-start(bf16[8,4096]{1,0:T(8,128)(2,1)S(1)} %get-tuple-element.94), channel_id=1, source_target_pairs={{0,3},{1,0},{2,1},{3,2},{4,7},{5,4},{6,5},{7,6},{8,11},{9,8},{10,9... | collective-permute-start | bytes 196616 | tf_op jit(solution)/shard_map/ppermute | solution.py:454
  50.8 1.7 %collective-permute-done.26 = bf16[8,4096]{1,0:T(8,128)(2,1)S(1)} collective-permute-done((bf16[8,4096]{1,0:T(8,128)(2,1)S(1)}, bf16[8,4096]{1,0:T(8,128)(2,1)S(1)}, u32[]{:S(2)}, u32[]{:S(2)}) %collective-permute-start.26) | collective-permute-done | bytes 65568 | tf_op jit(solution)/shard_map/ppermute | solution.py:454
  52.5 2.1 %collective-permute-done.25 = bf16[8,4096]{1,0:T(8,128)(2,1)S(1)} collective-permute-done((bf16[8,4096]{1,0:T(8,128)(2,1)S(1)}, bf16[8,4096]{1,0:T(8,128)(2,1)S(1)}, u32[]{:S(2)}, u32[]{:S(2)}) %collective-permute-start.25) | collective-permute-done | bytes 65568 | tf_op jit(solution)/shard_map/ppermute | solution.py:454
  54.7 0.7 %add_convert_fusion = bf16[8,4096]{1,0:T(8,128)(2,1)} fusion(bf16[8,4096]{1,0:T(8,128)(2,1)S(1)} %collective-permute-done.26, bf16[8,4096]{1,0:T(8,128)(2,1)S(1)} %collective-permute-done.25, f32[8,4096]{1,0:T(8,128)S(1)} %plus.1, bf16[8,4096]{1,0:T(8,128)(2,1)S(1)} %collective-permute-done.24), kind=kLoop, calls=%fused_computation.2 | loop fusion | flops 229376 | bytes 393216 | tf_op jit(solution)/shard_map/convert_element_type | solution.py:510
  (48 shorter events, 2.3 us)
Async XLA Ops:
  1.0 12.1 %collective-permute-start.2 = (bf16[8,4224]{1,0:T(8,128)(2,1)S(1)}, bf16[8,4224]{1,0:T(8,128)(2,1)S(1)}, u32[]{:S(2)}, u32[]{:S(2)}) collective-permute-start(bf16[8,4224]{1,0:T(8,128)(2,1)S(1)} %attach.1), channel_id=1, source_target_pairs={{0,3},{1,0},{2,1},{3,2},{4,7},{5,4},{6,5},{7,6},{8,11},{9,8},{10,9... | collective-permute-start | bytes 202760 | tf_op jit(solution)/shard_map/ppermute | solution.py:454
  6.1 7.0 %collective-permute-start.1 = (bf16[8,4224]{1,0:T(8,128)(2,1)S(1)}, bf16[8,4224]{1,0:T(8,128)(2,1)S(1)}, u32[]{:S(2)}, u32[]{:S(2)}) collective-permute-start(bf16[8,4224]{1,0:T(8,128)(2,1)S(1)} %attach.1), channel_id=1, source_target_pairs={{0,2},{1,3},{2,0},{3,1},{4,6},{5,7},{6,4},{7,5},{8,10},{9,11},{10,... | collective-permute-start | bytes 202760 | tf_op jit(solution)/shard_map/ppermute | solution.py:454
  6.1 7.0 %collective-permute-start = (bf16[8,4224]{1,0:T(8,128)(2,1)S(1)}, bf16[8,4224]{1,0:T(8,128)(2,1)S(1)}, u32[]{:S(2)}, u32[]{:S(2)}) collective-permute-start(bf16[8,4224]{1,0:T(8,128)(2,1)S(1)} %attach.1), channel_id=1, source_target_pairs={{0,1},{1,2},{2,3},{3,0},{4,5},{5,6},{6,7},{7,4},{8,9},{9,10},{10,1... | collective-permute-start | bytes 202760 | tf_op jit(solution)/shard_map/ppermute | solution.py:454
  7.1 6.0 %collective-permute-start.4 = (bf16[8,4224]{1,0:T(8,128)(2,1)S(1)}, bf16[8,4224]{1,0:T(8,128)(2,1)S(1)}, u32[]{:S(2)}, u32[]{:S(2)}) collective-permute-start(bf16[8,4224]{1,0:T(8,128)(2,1)S(1)} %attach.1), channel_id=1, source_target_pairs={{0,8},{8,0},{1,9},{9,1},{2,10},{10,2},{3,11},{11,3},{4,12},{12,4},... | collective-permute-start | bytes 202760 | tf_op jit(solution)/shard_map/ppermute | solution.py:457
  8.6 4.5 %collective-permute-start.3 = (bf16[128,1024]{1,0:T(8,128)(2,1)}, bf16[128,1024]{1,0:T(8,128)(2,1)S(1)}, u32[]{:S(2)}, u32[]{:S(2)}) collective-permute-start(bf16[128,1024]{1,0:T(8,128)(2,1)} %bitcast.11), channel_id=1, source_target_pairs={{0,4},{4,0},{1,5},{5,1},{2,6},{6,2},{3,7},{7,3},{8,12},{12,8},{9,1... | collective-permute-start | bytes 786440 | tf_op jit(solution)/shard_map/ppermute | solution.py:460
  13.1 8.7 %copy-start = (bf16[4,32,1024]{2,1,0:T(8,128)(2,1)S(1)}, bf16[4,32,1024]{2,1,0:T(8,128)(2,1)}, u32[]{:S(2)}) copy-start(bf16[4,32,1024]{2,1,0:T(8,128)(2,1)} %param.23) | copy-start | bytes 786436
  13.1 8.5 %collective-permute-start.5 = (bf16[24,4224]{1,0:T(8,128)(2,1)S(1)}, bf16[24,4224]{1,0:T(8,128)(2,1)S(1)}, u32[]{:S(2)}, u32[]{:S(2)}) collective-permute-start(bf16[24,4224]{1,0:T(8,128)(2,1)S(1)} %pad_maximum_fusion.1), channel_id=1, source_target_pairs={{0,8},{8,0},{1,9},{9,1},{2,10},{10,2},{3,11},{11,3},{4,12},{12,4},... | collective-permute-start | bytes 608264 | tf_op jit(solution)/shard_map/ppermute | solution.py:457
  14.4 9.0 %collective-permute-start.6 = (bf16[32,4224]{1,0:T(8,128)(2,1)S(1)}, bf16[32,4224]{1,0:T(8,128)(2,1)S(1)}, u32[]{:S(2)}, u32[]{:S(2)}) collective-permute-start(bf16[32,4224]{1,0:T(8,128)(2,1)S(1)} %pad_maximum_fusion.refs_0_), channel_id=1, source_target_pairs={{0,4},{4,0},{1,5},{5,1},{2,6},{6,2},{3,7},{7,3},{8,12},{12,8},{9,1... | collective-permute-start | bytes 811016 | tf_op jit(solution)/shard_map/ppermute | solution.py:460
  14.4 7.3 %collective-permute-start.8 = (bf16[3,32,192]{2,1,0:T(8,128)(2,1)S(1)}, bf16[3,32,192]{2,1,0:T(8,128)(2,1)S(1)}, u32[]{:S(2)}, u32[]{:S(2)}) collective-permute-start(bf16[3,32,192]{2,1,0:T(8,128)(2,1)S(1)} %get-tuple-element.62), channel_id=1, source_target_pairs={{0,1},{1,2},{2,3},{3,0},{4,5},{5,6},{6,7},{7,4},{8,9},{9,10},{10,1... | collective-permute-start | bytes 110600 | tf_op jit(solution)/shard_map/ppermute | solution.py:454
  16.4 6.6 %collective-permute-start.9 = (bf16[3,32,192]{2,1,0:T(8,128)(2,1)S(1)}, bf16[3,32,192]{2,1,0:T(8,128)(2,1)S(1)}, u32[]{:S(2)}, u32[]{:S(2)}) collective-permute-start(bf16[3,32,192]{2,1,0:T(8,128)(2,1)S(1)} %get-tuple-element.63), channel_id=1, source_target_pairs={{0,2},{1,3},{2,0},{3,1},{4,6},{5,7},{6,4},{7,5},{8,10},{9,11},{10,... | collective-permute-start | bytes 110600 | tf_op jit(solution)/shard_map/ppermute | solution.py:454
  17.3 5.7 %collective-permute-start.10 = (bf16[3,32,192]{2,1,0:T(8,128)(2,1)S(1)}, bf16[3,32,192]{2,1,0:T(8,128)(2,1)S(1)}, u32[]{:S(2)}, u32[]{:S(2)}) collective-permute-start(bf16[3,32,192]{2,1,0:T(8,128)(2,1)S(1)} %get-tuple-element.64), channel_id=1, source_target_pairs={{0,3},{1,0},{2,1},{3,2},{4,7},{5,4},{6,5},{7,6},{8,11},{9,8},{10,9... | collective-permute-start | bytes 110600 | tf_op jit(solution)/shard_map/ppermute | solution.py:454
  21.6 1.8 %collective-permute-start.7 = (bf16[32,4224]{1,0:T(8,128)(2,1)S(1)}, bf16[32,4224]{1,0:T(8,128)(2,1)S(1)}, u32[]{:S(2)}, u32[]{:S(2)}) collective-permute-start(bf16[32,4224]{1,0:T(8,128)(2,1)S(1)} %constant_dynamic-update-slice_fusion.refs_1_), channel_id=1, source_target_pairs={{0,4},{4,0},{1,5},{5,1},{2,6},{6,2},{3,7},{7,3},{8,12},{12,8},{9,1... | collective-permute-start | bytes 811016 | tf_op jit(solution)/shard_map/ppermute | solution.py:460
  21.7 9.5 %collective-permute-start.14 = (bf16[128,1024]{1,0:T(8,128)(2,1)S(1)}, bf16[128,1024]{1,0:T(8,128)(2,1)S(1)}, u32[]{:S(2)}, u32[]{:S(2)}) collective-permute-start(bf16[128,1024]{1,0:T(8,128)(2,1)S(1)} %bitcast.12), channel_id=1, source_target_pairs={{0,8},{8,0},{1,9},{9,1},{2,10},{10,2},{3,11},{11,3},{4,12},{12,4},... | collective-permute-start | bytes 786440 | tf_op jit(solution)/shard_map/ppermute | solution.py:457
  23.8 7.5 %collective-permute-start.11 = (bf16[128,256]{1,0:T(8,128)(2,1)S(1)}, bf16[128,256]{1,0:T(8,128)(2,1)S(1)}, u32[]{:S(2)}, u32[]{:S(2)}) collective-permute-start(bf16[128,256]{1,0:T(8,128)(2,1)S(1)} %get-tuple-element.70), channel_id=1, source_target_pairs={{0,1},{1,2},{2,3},{3,0},{4,5},{5,6},{6,7},{7,4},{8,9},{9,10},{10,1... | collective-permute-start | bytes 196616 | tf_op jit(solution)/shard_map/ppermute | solution.py:454
  25.1 7.5 %collective-permute-start.12 = (bf16[128,256]{1,0:T(8,128)(2,1)S(1)}, bf16[128,256]{1,0:T(8,128)(2,1)S(1)}, u32[]{:S(2)}, u32[]{:S(2)}) collective-permute-start(bf16[128,256]{1,0:T(8,128)(2,1)S(1)} %get-tuple-element.71), channel_id=1, source_target_pairs={{0,2},{1,3},{2,0},{3,1},{4,6},{5,7},{6,4},{7,5},{8,10},{9,11},{10,... | collective-permute-start | bytes 196616 | tf_op jit(solution)/shard_map/ppermute | solution.py:454
  26.4 7.9 %slice-start = ((s8[6291456]{0:T(1024)(128)(4,1)}), s8[4194304]{0:T(1024)(128)(4,1)S(1)}, s32[]{:S(2)}) async-start(s8[6291456]{0:T(1024)(128)(4,1)} %bitcast.8), calls=%async_computation | async-start | bytes 8388608
  26.4 7.9 %slice-start.1 = ((s8[6291456]{0:T(1024)(128)(4,1)}), s8[2097152]{0:T(1024)(128)(4,1)S(1)}, s32[]{:S(2)}) async-start(s8[6291456]{0:T(1024)(128)(4,1)} %bitcast.8), calls=%async_computation.1 | async-start | bytes 4194304
  26.4 6.3 %collective-permute-start.13 = (bf16[128,256]{1,0:T(8,128)(2,1)S(1)}, bf16[128,256]{1,0:T(8,128)(2,1)S(1)}, u32[]{:S(2)}, u32[]{:S(2)}) collective-permute-start(bf16[128,256]{1,0:T(8,128)(2,1)S(1)} %get-tuple-element.72), channel_id=1, source_target_pairs={{0,3},{1,0},{2,1},{3,2},{4,7},{5,4},{6,5},{7,6},{8,11},{9,8},{10,9... | collective-permute-start | bytes 196616 | tf_op jit(solution)/shard_map/ppermute | solution.py:454
  33.2 3.8 %collective-permute-start.17 = (bf16[64,128]{1,0:T(8,128)(2,1)S(1)}, bf16[64,128]{1,0:T(8,128)(2,1)S(1)}, u32[]{:S(2)}, u32[]{:S(2)}) collective-permute-start(bf16[64,128]{1,0:T(8,128)(2,1)S(1)} %get-tuple-element.84), channel_id=1, source_target_pairs={{0,8},{8,0},{1,9},{9,1},{2,10},{10,2},{3,11},{11,3},{4,12},{12,4},... | collective-permute-start | bytes 49160 | tf_op jit(solution)/shard_map/ppermute | solution.py:457
  35.3 2.0 %collective-permute-start.15 = (bf16[64,4096]{1,0:T(8,128)(2,1)S(1)}, bf16[64,4096]{1,0:T(8,128)(2,1)S(1)}, u32[]{:S(2)}, u32[]{:S(2)}) collective-permute-start(bf16[64,4096]{1,0:T(8,128)(2,1)S(1)} %get-tuple-element.80), channel_id=1, source_target_pairs={{0,4},{4,0},{1,5},{5,1},{2,6},{6,2},{3,7},{7,3},{8,12},{12,8},{9,1... | collective-permute-start | bytes 1572872 | tf_op jit(solution)/shard_map/ppermute | solution.py:460
  37.0 1.7 %collective-permute-start.18 = (bf16[32,256]{1,0:T(8,128)(2,1)S(1)}, bf16[32,256]{1,0:T(8,128)(2,1)S(1)}, u32[]{:S(2)}, u32[]{:S(2)}) collective-permute-start(bf16[32,256]{1,0:T(8,128)(2,1)S(1)} %get-tuple-element.86), channel_id=1, source_target_pairs={{0,4},{4,0},{1,5},{5,1},{2,6},{6,2},{3,7},{7,3},{8,12},{12,8},{9,1... | collective-permute-start | bytes 49160 | tf_op jit(solution)/shard_map/ppermute | solution.py:460
  37.4 8.6 %collective-permute-start.16 = (bf16[128,1024]{1,0:T(8,128)(2,1)S(1)}, bf16[128,1024]{1,0:T(8,128)(2,1)S(1)}, u32[]{:S(2)}, u32[]{:S(2)}) collective-permute-start(bf16[128,1024]{1,0:T(8,128)(2,1)S(1)} %collective-permute-done.14.refs_2_), channel_id=1, source_target_pairs={{0,4},{4,0},{1,5},{5,1},{2,6},{6,2},{3,7},{7,3},{8,12},{12,8},{9,1... | collective-permute-start | bytes 786440 | tf_op jit(solution)/shard_map/ppermute | solution.py:460
  37.7 8.3 %collective-permute-start.22 = (bf16[24,4096]{1,0:T(8,128)(2,1)S(1)}, bf16[24,4096]{1,0:T(8,128)(2,1)S(1)}, u32[]{:S(2)}, u32[]{:S(2)}) collective-permute-start(bf16[24,4096]{1,0:T(8,128)(2,1)S(1)} %get-tuple-element.91), channel_id=1, source_target_pairs={{0,8},{8,0},{1,9},{9,1},{2,10},{10,2},{3,11},{11,3},{4,12},{12,4},... | collective-permute-start | bytes 589832 | tf_op jit(solution)/shard_map/ppermute | solution.py:457
  38.7 5.9 %collective-permute-start.19 = (bf16[32,512]{1,0:T(8,128)(2,1)S(1)}, bf16[32,512]{1,0:T(8,128)(2,1)S(1)}, u32[]{:S(2)}, u32[]{:S(2)}) collective-permute-start(bf16[32,512]{1,0:T(8,128)(2,1)S(1)} %get-tuple-element.87), channel_id=1, source_target_pairs={{0,1},{1,2},{2,3},{3,0},{4,5},{5,6},{6,7},{7,4},{8,9},{9,10},{10,1... | collective-permute-start | bytes 98312 | tf_op jit(solution)/shard_map/ppermute | solution.py:454
  40.7 5.1 %collective-permute-start.20 = (bf16[32,512]{1,0:T(8,128)(2,1)S(1)}, bf16[32,512]{1,0:T(8,128)(2,1)S(1)}, u32[]{:S(2)}, u32[]{:S(2)}) collective-permute-start(bf16[32,512]{1,0:T(8,128)(2,1)S(1)} %get-tuple-element.88), channel_id=1, source_target_pairs={{0,2},{1,3},{2,0},{3,1},{4,6},{5,7},{6,4},{7,5},{8,10},{9,11},{10,... | collective-permute-start | bytes 98312 | tf_op jit(solution)/shard_map/ppermute | solution.py:454
  41.7 4.2 %collective-permute-start.21 = (bf16[32,512]{1,0:T(8,128)(2,1)S(1)}, bf16[32,512]{1,0:T(8,128)(2,1)S(1)}, u32[]{:S(2)}, u32[]{:S(2)}) collective-permute-start(bf16[32,512]{1,0:T(8,128)(2,1)S(1)} %get-tuple-element.89), channel_id=1, source_target_pairs={{0,3},{1,0},{2,1},{3,2},{4,7},{5,4},{6,5},{7,6},{8,11},{9,8},{10,9... | collective-permute-start | bytes 98312 | tf_op jit(solution)/shard_map/ppermute | solution.py:454
  44.6 6.2 %collective-permute-start.23 = (bf16[8,4096]{1,0:T(8,128)(2,1)S(1)}, bf16[8,4096]{1,0:T(8,128)(2,1)S(1)}, u32[]{:S(2)}, u32[]{:S(2)}) collective-permute-start(bf16[8,4096]{1,0:T(8,128)(2,1)S(1)} %get-tuple-element.93), channel_id=1, source_target_pairs={{0,8},{8,0},{1,9},{9,1},{2,10},{10,2},{3,11},{11,3},{4,12},{12,4},... | collective-permute-start | bytes 196616 | tf_op jit(solution)/shard_map/ppermute | solution.py:457
  46.2 6.3 %collective-permute-start.26 = (bf16[8,4096]{1,0:T(8,128)(2,1)S(1)}, bf16[8,4096]{1,0:T(8,128)(2,1)S(1)}, u32[]{:S(2)}, u32[]{:S(2)}) collective-permute-start(bf16[8,4096]{1,0:T(8,128)(2,1)S(1)} %get-tuple-element.96), channel_id=1, source_target_pairs={{0,1},{1,2},{2,3},{3,0},{4,5},{5,6},{6,7},{7,4},{8,9},{9,10},{10,1... | collective-permute-start | bytes 196616 | tf_op jit(solution)/shard_map/ppermute | solution.py:454
  47.5 7.2 %collective-permute-start.25 = (bf16[8,4096]{1,0:T(8,128)(2,1)S(1)}, bf16[8,4096]{1,0:T(8,128)(2,1)S(1)}, u32[]{:S(2)}, u32[]{:S(2)}) collective-permute-start(bf16[8,4096]{1,0:T(8,128)(2,1)S(1)} %get-tuple-element.95), channel_id=1, source_target_pairs={{0,2},{1,3},{2,0},{3,1},{4,6},{5,7},{6,4},{7,5},{8,10},{9,11},{10,... | collective-permute-start | bytes 196616 | tf_op jit(solution)/shard_map/ppermute | solution.py:454
  49.7 4.9 %collective-permute-start.24 = (bf16[8,4096]{1,0:T(8,128)(2,1)S(1)}, bf16[8,4096]{1,0:T(8,128)(2,1)S(1)}, u32[]{:S(2)}, u32[]{:S(2)}) collective-permute-start(bf16[8,4096]{1,0:T(8,128)(2,1)S(1)} %get-tuple-element.94), channel_id=1, source_target_pairs={{0,3},{1,0},{2,1},{3,2},{4,7},{5,4},{6,5},{7,6},{8,11},{9,8},{10,9... | collective-permute-start | bytes 196616 | tf_op jit(solution)/shard_map/ppermute | solution.py:454

commit v21 on v19

--- a/solution.py
+++ b/solution.py
@@ -494,7 +494,7 @@
     rights += [partner_right] + [other_core(after(right, out)) for right in rights[1:]]
     own, *pieces = merge(out, rights, add_up(bottom[1:] + bottom[:1]), backs[1::2], rows)
     result = plus(own, backs[::2])
-    for k in range(1, parts):
+    for k in sorted(range(1, parts), key=lambda k: -min(k, parts - k)):
         result += along_z(pieces[k - 1], -k).astype(F32)
     return result.astype(BF)
 

time: 55.5 us -> 56.2 us (1.013)
  waiting for transfers between devices: 9.4 us -> 10.6 us
    ppermute x15, waiting for transfers between devices: 7.33 us -> 8.56 us  [along_z(): lax.ppermute(value, 'mp', [(i, (i + step) % parts) for i in range(parts)])]
  transfers between devices with their start and end apart: 27 -> 27, of which waited for: 8 -> 8; matrix products, arithmetic and copies ran while one was open for 0% -> 0% of each run, Pallas kernels for 23% -> 22%
where the time goes in v21:
time: 56.2 us; the launch traced here: 56 us
  starting transfers between devices  30.4 us (54%)
  Pallas kernels  14 us (25%)
  waiting for transfers between devices  10.6 us (19%)
  other arithmetic  0.71 us (1%)
    ppermute x15, starting transfers between devices, along_z(): lax.ppermute(value, 'mp', [(i, (i + step) % parts) for i in range(parts)])  22.8 us
    ppermute x15, waiting for transfers between devices, along_z(): lax.ppermute(value, 'mp', [(i, (i + step) % parts) for i in range(parts)])  8.56 us
    ppermute x6, starting transfers between devices, along_y(): lax.ppermute(value, 'y', [(i, (i + step) % chips) for i in range(chips)])  7.14 us
    pallas_call x1, Pallas kernels, prepare(): pl.pallas_call(functools.partial(prepare_kernel, parts), in_specs=[vmem]...  4.06 us
    pallas_call x1, Pallas kernels, raw_products(): pl.pallas_call(functools.partial(raw_kernel, len(lines), tile), out_shape...  3.51 us
    pallas_call x1, Pallas kernels, load(): pl.pallas_call(load_kernel, in_specs=[pl.BlockSpec(memory_space=pltpu.HBM...  2.86 us
    ppermute x6, waiting for transfers between devices, along_y(): lax.ppermute(value, 'y', [(i, (i + step) % chips) for i in range(chips)])  1.61 us
  transfers between devices with their start and end apart: 27, of which 8 were waited for; matrix products, arithmetic and copies ran while one was open for 0% of the time, Pallas kernels for 22%

profile of v21, /device:TPU:0, one launch (start us, length us, event | category | flops | bytes accessed | tf_op | source)
XLA Modules:
  0.0 56.0 jit_solution(12850107600384498754)
XLA Ops:
  0.0 0.9 %attach.1 = bf16[8,4224]{1,0:T(8,128)(2,1)S(1)} custom-call(bf16[8,4096]{1,0:T(8,128)(2,1)} %tokens_ref.1, s32[8,8]{1,0:T(8,128)} %routes_ref.1, f32[8,8]{1,0:T(8,128)} %probs_ref.1), custom_call_target="tpu_custom_call" | custom-call | flops 1 | bytes 1 | tf_op jit(solution)/shard_map/attach/pallas_call | solution.py:67
  1.0 5.1 %collective-permute-start.2 = (bf16[8,4224]{1,0:T(8,128)(2,1)S(1)}, bf16[8,4224]{1,0:T(8,128)(2,1)S(1)}, u32[]{:S(2)}, u32[]{:S(2)}) collective-permute-start(bf16[8,4224]{1,0:T(8,128)(2,1)S(1)} %attach.1), channel_id=1, source_target_pairs={{0,3},{1,0},{2,1},{3,2},{4,7},{5,4},{6,5},{7,6},{8,11},{9,8},{10,9... | collective-permute-start | bytes 202760 | tf_op jit(solution)/shard_map/ppermute | solution.py:443
  6.1 1.0 %collective-permute-start = (bf16[8,4224]{1,0:T(8,128)(2,1)S(1)}, bf16[8,4224]{1,0:T(8,128)(2,1)S(1)}, u32[]{:S(2)}, u32[]{:S(2)}) collective-permute-start(bf16[8,4224]{1,0:T(8,128)(2,1)S(1)} %attach.1), channel_id=1, source_target_pairs={{0,1},{1,2},{2,3},{3,0},{4,5},{5,6},{6,7},{7,4},{8,9},{9,10},{10,1... | collective-permute-start | bytes 202760 | tf_op jit(solution)/shard_map/ppermute | solution.py:443
  7.1 1.5 %collective-permute-start.4 = (bf16[8,4224]{1,0:T(8,128)(2,1)S(1)}, bf16[8,4224]{1,0:T(8,128)(2,1)S(1)}, u32[]{:S(2)}, u32[]{:S(2)}) collective-permute-start(bf16[8,4224]{1,0:T(8,128)(2,1)S(1)} %attach.1), channel_id=1, source_target_pairs={{0,8},{8,0},{1,9},{9,1},{2,10},{10,2},{3,11},{11,3},{4,12},{12,4},... | collective-permute-start | bytes 202760 | tf_op jit(solution)/shard_map/ppermute | solution.py:446
  8.6 4.1 %prepare.1 = (bf16[768,4096]{1,0:T(8,128)(2,1)S(1)}, bf16[256,1024]{1,0:T(8,128)(2,1)S(1)}, bf16[3,32,192]{2,1,0:T(8,128)(2,1)S(1)}, bf16[3,32,192]{2,1,0:T(8,12...) custom-call(bf16[4,8,768]{2,1,0:T(8,128)(2,1)} %refs_0_.1, bf16[4,8,768]{2,1,0:T(8,128)(2,1)} %refs_1_.1, ...), custom_call_target="tpu_custom_call" | custom-call | flops 1 | bytes 1 | tf_op jit(solution)/shard_map/prepare/pallas_call | solution.py:135
  12.8 1.6 %collective-permute-start.5 = (bf16[24,4224]{1,0:T(8,128)(2,1)S(1)}, bf16[24,4224]{1,0:T(8,128)(2,1)S(1)}, u32[]{:S(2)}, u32[]{:S(2)}) collective-permute-start(bf16[24,4224]{1,0:T(8,128)(2,1)S(1)} %pad_maximum_fusion.1), channel_id=1, source_target_pairs={{0,8},{8,0},{1,9},{9,1},{2,10},{10,2},{3,11},{11,3},{4,12},{12,4},... | collective-permute-start | bytes 608264 | tf_op jit(solution)/shard_map/ppermute | solution.py:446
  14.4 1.7 %collective-permute-start.8 = (bf16[3,32,192]{2,1,0:T(8,128)(2,1)S(1)}, bf16[3,32,192]{2,1,0:T(8,128)(2,1)S(1)}, u32[]{:S(2)}, u32[]{:S(2)}) collective-permute-start(bf16[3,32,192]{2,1,0:T(8,128)(2,1)S(1)} %get-tuple-element.60), channel_id=1, source_target_pairs={{0,1},{1,2},{2,3},{3,0},{4,5},{5,6},{6,7},{7,4},{8,9},{9,10},{10,1... | collective-permute-start | bytes 110600 | tf_op jit(solution)/shard_map/ppermute | solution.py:443
  16.1 0.9 %collective-permute-start.9 = (bf16[3,32,192]{2,1,0:T(8,128)(2,1)S(1)}, bf16[3,32,192]{2,1,0:T(8,128)(2,1)S(1)}, u32[]{:S(2)}, u32[]{:S(2)}) collective-permute-start(bf16[3,32,192]{2,1,0:T(8,128)(2,1)S(1)} %get-tuple-element.61), channel_id=1, source_target_pairs={{0,2},{1,3},{2,0},{3,1},{4,6},{5,7},{6,4},{7,5},{8,10},{9,11},{10,... | collective-permute-start | bytes 110600 | tf_op jit(solution)/shard_map/ppermute | solution.py:443
  17.0 2.1 %collective-permute-start.10 = (bf16[3,32,192]{2,1,0:T(8,128)(2,1)S(1)}, bf16[3,32,192]{2,1,0:T(8,128)(2,1)S(1)}, u32[]{:S(2)}, u32[]{:S(2)}) collective-permute-start(bf16[3,32,192]{2,1,0:T(8,128)(2,1)S(1)} %get-tuple-element.62), channel_id=1, source_target_pairs={{0,3},{1,0},{2,1},{3,2},{4,7},{5,4},{6,5},{7,6},{8,11},{9,8},{10,9... | collective-permute-start | bytes 110600 | tf_op jit(solution)/shard_map/ppermute | solution.py:443
  19.1 2.9 %load.1.refs_5_ = bf16[768,4096]{1,0:T(8,128)(2,1)S(1)} custom-call(bf16[768,4096]{1,0:T(8,128)(2,1)} %bitcast.14), custom_call_target="tpu_custom_call" | custom-call | flops 3000000000 | bytes 1 | tf_op jit(solution)/shard_map/load/pallas_call | solution.py:94
  22.1 1.0 %collective-permute-start.14 = (bf16[128,1024]{1,0:T(8,128)(2,1)S(1)}, bf16[128,1024]{1,0:T(8,128)(2,1)S(1)}, u32[]{:S(2)}, u32[]{:S(2)}) collective-permute-start(bf16[128,1024]{1,0:T(8,128)(2,1)S(1)} %bitcast.12), channel_id=1, source_target_pairs={{0,8},{8,0},{1,9},{9,1},{2,10},{10,2},{3,11},{11,3},{4,12},{12,4},... | collective-permute-start | bytes 786440 | tf_op jit(solution)/shard_map/ppermute | solution.py:446
  23.0 0.4 spread.1.refs_10_
  23.9 0.9 %collective-permute-start.11 = (bf16[128,256]{1,0:T(8,128)(2,1)S(1)}, bf16[128,256]{1,0:T(8,128)(2,1)S(1)}, u32[]{:S(2)}, u32[]{:S(2)}) collective-permute-start(bf16[128,256]{1,0:T(8,128)(2,1)S(1)} %get-tuple-element.68), channel_id=1, source_target_pairs={{0,1},{1,2},{2,3},{3,0},{4,5},{5,6},{6,7},{7,4},{8,9},{9,10},{10,1... | collective-permute-start | bytes 196616 | tf_op jit(solution)/shard_map/ppermute | solution.py:443
  24.8 1.5 %collective-permute-start.12 = (bf16[128,256]{1,0:T(8,128)(2,1)S(1)}, bf16[128,256]{1,0:T(8,128)(2,1)S(1)}, u32[]{:S(2)}, u32[]{:S(2)}) collective-permute-start(bf16[128,256]{1,0:T(8,128)(2,1)S(1)} %get-tuple-element.69), channel_id=1, source_target_pairs={{0,2},{1,3},{2,0},{3,1},{4,6},{5,7},{6,4},{7,5},{8,10},{9,11},{10,... | collective-permute-start | bytes 196616 | tf_op jit(solution)/shard_map/ppermute | solution.py:443
  26.4 1.7 %collective-permute-start.13 = (bf16[128,256]{1,0:T(8,128)(2,1)S(1)}, bf16[128,256]{1,0:T(8,128)(2,1)S(1)}, u32[]{:S(2)}, u32[]{:S(2)}) collective-permute-start(bf16[128,256]{1,0:T(8,128)(2,1)S(1)} %get-tuple-element.70), channel_id=1, source_target_pairs={{0,3},{1,0},{2,1},{3,2},{4,7},{5,4},{6,5},{7,6},{8,11},{9,8},{10,9... | collective-permute-start | bytes 196616 | tf_op jit(solution)/shard_map/ppermute | solution.py:443
  28.0 3.5 %raw.1 = (f32[128,768]{1,0:T(8,128)S(1)}, f32[128,768]{1,0:T(8,128)S(1)}) custom-call(bf16[32,4224]{1,0:T(8,128)(2,1)S(1)} %pad_maximum_fusion.refs_0_, bf16[32,4224]{1,0:T(8,128)(2,1)S(1)} %constant_dynamic-update-slice_fusion.refs_1_, bf16[32,4224]{1,0:T(8,128)(2,1)S(1)} %collective-permute-done.6.refs_2_, ...), custom_call_target="tpu_custom_call" | custom-call | flops 1 | bytes 1 | tf_op jit(solution)/shard_map/raw/pallas_call | solution.py:217
  31.6 1.2 %collective-permute-done.12.refs_6_ = bf16[128,256]{1,0:T(8,128)(2,1)S(1)} collective-permute-done((bf16[128,256]{1,0:T(8,128)(2,1)S(1)}, bf16[128,256]{1,0:T(8,128)(2,1)S(1)}, u32[]{:S(2)}, u32[]{:S(2)}) %collective-permute-start.12) | collective-permute-done | bytes 65568 | tf_op jit(solution)/shard_map/ppermute | solution.py:443
  32.8 0.5 hidden.1
  33.3 1.1 %collective-permute-start.17 = (bf16[64,128]{1,0:T(8,128)(2,1)S(1)}, bf16[64,128]{1,0:T(8,128)(2,1)S(1)}, u32[]{:S(2)}, u32[]{:S(2)}) collective-permute-start(bf16[64,128]{1,0:T(8,128)(2,1)S(1)} %get-tuple-element.82), channel_id=1, source_target_pairs={{0,8},{8,0},{1,9},{9,1},{2,10},{10,2},{3,11},{11,3},{4,12},{12,4},... | collective-permute-start | bytes 49160 | tf_op jit(solution)/shard_map/ppermute | solution.py:446
  34.4 1.1 %down.1 = (f32[64,4096]{1,0:T(8,128)S(1)}, bf16[64,4096]{1,0:T(8,128)(2,1)S(1)}) custom-call(bf16[128,768]{1,0:T(8,128)(2,1)S(1)} %get-tuple-element.76.hidden_ref, bf16[768,4096]{1,0:T(8,128)(2,1)S(1)} %bitcast.10), custom_call_target="tpu_custom_call" | custom-call | flops 1 | bytes 1 | tf_op jit(solution)/shard_map/down/pallas_call | solution.py:279
  35.5 1.6 %collective-permute-done.17.refs_1_ = bf16[64,128]{1,0:T(8,128)(2,1)S(1)} collective-permute-done((bf16[64,128]{1,0:T(8,128)(2,1)S(1)}, bf16[64,128]{1,0:T(8,128)(2,1)S(1)}, u32[]{:S(2)}, u32[]{:S(2)}) %collective-permute-start.17) | collective-permute-done | bytes 16416 | tf_op jit(solution)/shard_map/ppermute | solution.py:446
  37.8 1.0 %collective-permute-start.22 = (bf16[24,4096]{1,0:T(8,128)(2,1)S(1)}, bf16[24,4096]{1,0:T(8,128)(2,1)S(1)}, u32[]{:S(2)}, u32[]{:S(2)}) collective-permute-start(bf16[24,4096]{1,0:T(8,128)(2,1)S(1)} %get-tuple-element.89), channel_id=1, source_target_pairs={{0,8},{8,0},{1,9},{9,1},{2,10},{10,2},{3,11},{11,3},{4,12},{12,4},... | collective-permute-start | bytes 589832 | tf_op jit(solution)/shard_map/ppermute | solution.py:446
  38.8 1.6 %collective-permute-start.19 = (bf16[32,512]{1,0:T(8,128)(2,1)S(1)}, bf16[32,512]{1,0:T(8,128)(2,1)S(1)}, u32[]{:S(2)}, u32[]{:S(2)}) collective-permute-start(bf16[32,512]{1,0:T(8,128)(2,1)S(1)} %get-tuple-element.85), channel_id=1, source_target_pairs={{0,1},{1,2},{2,3},{3,0},{4,5},{5,6},{6,7},{7,4},{8,9},{9,10},{10,1... | collective-permute-start | bytes 98312 | tf_op jit(solution)/shard_map/ppermute | solution.py:443
  40.4 1.3 %collective-permute-start.20 = (bf16[32,512]{1,0:T(8,128)(2,1)S(1)}, bf16[32,512]{1,0:T(8,128)(2,1)S(1)}, u32[]{:S(2)}, u32[]{:S(2)}) collective-permute-start(bf16[32,512]{1,0:T(8,128)(2,1)S(1)} %get-tuple-element.86), channel_id=1, source_target_pairs={{0,2},{1,3},{2,0},{3,1},{4,6},{5,7},{6,4},{7,5},{8,10},{9,11},{10,... | collective-permute-start | bytes 98312 | tf_op jit(solution)/shard_map/ppermute | solution.py:443
  41.7 1.1 %collective-permute-start.21 = (bf16[32,512]{1,0:T(8,128)(2,1)S(1)}, bf16[32,512]{1,0:T(8,128)(2,1)S(1)}, u32[]{:S(2)}, u32[]{:S(2)}) collective-permute-start(bf16[32,512]{1,0:T(8,128)(2,1)S(1)} %get-tuple-element.87), channel_id=1, source_target_pairs={{0,3},{1,0},{2,1},{3,2},{4,7},{5,4},{6,5},{7,6},{8,11},{9,8},{10,9... | collective-permute-start | bytes 98312 | tf_op jit(solution)/shard_map/ppermute | solution.py:443
  42.8 1.9 %collective-permute-done.19.refs_0_ = bf16[32,512]{1,0:T(8,128)(2,1)S(1)} collective-permute-done((bf16[32,512]{1,0:T(8,128)(2,1)S(1)}, bf16[32,512]{1,0:T(8,128)(2,1)S(1)}, u32[]{:S(2)}, u32[]{:S(2)}) %collective-permute-start.19) | collective-permute-done | bytes 32800 | tf_op jit(solution)/shard_map/ppermute | solution.py:443
  44.7 1.0 %collective-permute-start.23 = (bf16[8,4096]{1,0:T(8,128)(2,1)S(1)}, bf16[8,4096]{1,0:T(8,128)(2,1)S(1)}, u32[]{:S(2)}, u32[]{:S(2)}) collective-permute-start(bf16[8,4096]{1,0:T(8,128)(2,1)S(1)} %get-tuple-element.91), channel_id=1, source_target_pairs={{0,8},{8,0},{1,9},{9,1},{2,10},{10,2},{3,11},{11,3},{4,12},{12,4},... | collective-permute-start | bytes 196616 | tf_op jit(solution)/shard_map/ppermute | solution.py:446
  46.1 1.4 %collective-permute-start.26 = (bf16[8,4096]{1,0:T(8,128)(2,1)S(1)}, bf16[8,4096]{1,0:T(8,128)(2,1)S(1)}, u32[]{:S(2)}, u32[]{:S(2)}) collective-permute-start(bf16[8,4096]{1,0:T(8,128)(2,1)S(1)} %get-tuple-element.94), channel_id=1, source_target_pairs={{0,1},{1,2},{2,3},{3,0},{4,5},{5,6},{6,7},{7,4},{8,9},{9,10},{10,1... | collective-permute-start | bytes 196616 | tf_op jit(solution)/shard_map/ppermute | solution.py:443
  47.5 2.5 %collective-permute-start.25 = (bf16[8,4096]{1,0:T(8,128)(2,1)S(1)}, bf16[8,4096]{1,0:T(8,128)(2,1)S(1)}, u32[]{:S(2)}, u32[]{:S(2)}) collective-permute-start(bf16[8,4096]{1,0:T(8,128)(2,1)S(1)} %get-tuple-element.93), channel_id=1, source_target_pairs={{0,3},{1,0},{2,1},{3,2},{4,7},{5,4},{6,5},{7,6},{8,11},{9,8},{10,9... | collective-permute-start | bytes 196616 | tf_op jit(solution)/shard_map/ppermute | solution.py:443
  50.0 3.0 %collective-permute-done.26 = bf16[8,4096]{1,0:T(8,128)(2,1)S(1)} collective-permute-done((bf16[8,4096]{1,0:T(8,128)(2,1)S(1)}, bf16[8,4096]{1,0:T(8,128)(2,1)S(1)}, u32[]{:S(2)}, u32[]{:S(2)}) %collective-permute-start.26) | collective-permute-done | bytes 65568 | tf_op jit(solution)/shard_map/ppermute | solution.py:443
  53.0 2.4 %collective-permute-done.24 = bf16[8,4096]{1,0:T(8,128)(2,1)S(1)} collective-permute-done((bf16[8,4096]{1,0:T(8,128)(2,1)S(1)}, bf16[8,4096]{1,0:T(8,128)(2,1)S(1)}, u32[]{:S(2)}, u32[]{:S(2)}) %collective-permute-start.24) | collective-permute-done | bytes 65568 | tf_op jit(solution)/shard_map/ppermute | solution.py:443
  55.4 0.7 %add_convert_fusion = bf16[8,4096]{1,0:T(8,128)(2,1)} fusion(bf16[8,4096]{1,0:T(8,128)(2,1)S(1)} %collective-permute-done.26, bf16[8,4096]{1,0:T(8,128)(2,1)S(1)} %collective-permute-done.25, f32[8,4096]{1,0:T(8,128)S(1)} %plus.1, bf16[8,4096]{1,0:T(8,128)(2,1)S(1)} %collective-permute-done.24), kind=kLoop, calls=%fused_computation.2 | loop fusion | flops 229376 | bytes 393216 | tf_op jit(solution)/shard_map/convert_element_type | solution.py:499
  (48 shorter events, 1.8 us)
Async XLA Ops:
  1.0 11.7 %collective-permute-start.2 = (bf16[8,4224]{1,0:T(8,128)(2,1)S(1)}, bf16[8,4224]{1,0:T(8,128)(2,1)S(1)}, u32[]{:S(2)}, u32[]{:S(2)}) collective-permute-start(bf16[8,4224]{1,0:T(8,128)(2,1)S(1)} %attach.1), channel_id=1, source_target_pairs={{0,3},{1,0},{2,1},{3,2},{4,7},{5,4},{6,5},{7,6},{8,11},{9,8},{10,9... | collective-permute-start | bytes 202760 | tf_op jit(solution)/shard_map/ppermute | solution.py:443
  6.1 6.6 %collective-permute-start.1 = (bf16[8,4224]{1,0:T(8,128)(2,1)S(1)}, bf16[8,4224]{1,0:T(8,128)(2,1)S(1)}, u32[]{:S(2)}, u32[]{:S(2)}) collective-permute-start(bf16[8,4224]{1,0:T(8,128)(2,1)S(1)} %attach.1), channel_id=1, source_target_pairs={{0,2},{1,3},{2,0},{3,1},{4,6},{5,7},{6,4},{7,5},{8,10},{9,11},{10,... | collective-permute-start | bytes 202760 | tf_op jit(solution)/shard_map/ppermute | solution.py:443
  6.1 6.6 %collective-permute-start = (bf16[8,4224]{1,0:T(8,128)(2,1)S(1)}, bf16[8,4224]{1,0:T(8,128)(2,1)S(1)}, u32[]{:S(2)}, u32[]{:S(2)}) collective-permute-start(bf16[8,4224]{1,0:T(8,128)(2,1)S(1)} %attach.1), channel_id=1, source_target_pairs={{0,1},{1,2},{2,3},{3,0},{4,5},{5,6},{6,7},{7,4},{8,9},{9,10},{10,1... | collective-permute-start | bytes 202760 | tf_op jit(solution)/shard_map/ppermute | solution.py:443
  7.1 5.7 %collective-permute-start.4 = (bf16[8,4224]{1,0:T(8,128)(2,1)S(1)}, bf16[8,4224]{1,0:T(8,128)(2,1)S(1)}, u32[]{:S(2)}, u32[]{:S(2)}) collective-permute-start(bf16[8,4224]{1,0:T(8,128)(2,1)S(1)} %attach.1), channel_id=1, source_target_pairs={{0,8},{8,0},{1,9},{9,1},{2,10},{10,2},{3,11},{11,3},{4,12},{12,4},... | collective-permute-start | bytes 202760 | tf_op jit(solution)/shard_map/ppermute | solution.py:446
  8.6 4.2 %collective-permute-start.3 = (bf16[128,1024]{1,0:T(8,128)(2,1)}, bf16[128,1024]{1,0:T(8,128)(2,1)S(1)}, u32[]{:S(2)}, u32[]{:S(2)}) collective-permute-start(bf16[128,1024]{1,0:T(8,128)(2,1)} %bitcast.11), channel_id=1, source_target_pairs={{0,4},{4,0},{1,5},{5,1},{2,6},{6,2},{3,7},{7,3},{8,12},{12,8},{9,1... | collective-permute-start | bytes 786440 | tf_op jit(solution)/shard_map/ppermute | solution.py:449
  12.8 9.1 %collective-permute-start.5 = (bf16[24,4224]{1,0:T(8,128)(2,1)S(1)}, bf16[24,4224]{1,0:T(8,128)(2,1)S(1)}, u32[]{:S(2)}, u32[]{:S(2)}) collective-permute-start(bf16[24,4224]{1,0:T(8,128)(2,1)S(1)} %pad_maximum_fusion.1), channel_id=1, source_target_pairs={{0,8},{8,0},{1,9},{9,1},{2,10},{10,2},{3,11},{11,3},{4,12},{12,4},... | collective-permute-start | bytes 608264 | tf_op jit(solution)/shard_map/ppermute | solution.py:446
  14.4 7.7 %copy-start = (bf16[4,32,1024]{2,1,0:T(8,128)(2,1)S(1)}, bf16[4,32,1024]{2,1,0:T(8,128)(2,1)}, u32[]{:S(2)}) copy-start(bf16[4,32,1024]{2,1,0:T(8,128)(2,1)} %param.23) | copy-start | bytes 786436
  14.4 9.0 %collective-permute-start.6 = (bf16[32,4224]{1,0:T(8,128)(2,1)S(1)}, bf16[32,4224]{1,0:T(8,128)(2,1)S(1)}, u32[]{:S(2)}, u32[]{:S(2)}) collective-permute-start(bf16[32,4224]{1,0:T(8,128)(2,1)S(1)} %pad_maximum_fusion.refs_0_), channel_id=1, source_target_pairs={{0,4},{4,0},{1,5},{5,1},{2,6},{6,2},{3,7},{7,3},{8,12},{12,8},{9,1... | collective-permute-start | bytes 811016 | tf_op jit(solution)/shard_map/ppermute | solution.py:449
  14.4 7.7 %collective-permute-start.8 = (bf16[3,32,192]{2,1,0:T(8,128)(2,1)S(1)}, bf16[3,32,192]{2,1,0:T(8,128)(2,1)S(1)}, u32[]{:S(2)}, u32[]{:S(2)}) collective-permute-start(bf16[3,32,192]{2,1,0:T(8,128)(2,1)S(1)} %get-tuple-element.60), channel_id=1, source_target_pairs={{0,1},{1,2},{2,3},{3,0},{4,5},{5,6},{6,7},{7,4},{8,9},{9,10},{10,1... | collective-permute-start | bytes 110600 | tf_op jit(solution)/shard_map/ppermute | solution.py:443
  16.1 7.0 %collective-permute-start.9 = (bf16[3,32,192]{2,1,0:T(8,128)(2,1)S(1)}, bf16[3,32,192]{2,1,0:T(8,128)(2,1)S(1)}, u32[]{:S(2)}, u32[]{:S(2)}) collective-permute-start(bf16[3,32,192]{2,1,0:T(8,128)(2,1)S(1)} %get-tuple-element.61), channel_id=1, source_target_pairs={{0,2},{1,3},{2,0},{3,1},{4,6},{5,7},{6,4},{7,5},{8,10},{9,11},{10,... | collective-permute-start | bytes 110600 | tf_op jit(solution)/shard_map/ppermute | solution.py:443
  17.0 6.1 %collective-permute-start.10 = (bf16[3,32,192]{2,1,0:T(8,128)(2,1)S(1)}, bf16[3,32,192]{2,1,0:T(8,128)(2,1)S(1)}, u32[]{:S(2)}, u32[]{:S(2)}) collective-permute-start(bf16[3,32,192]{2,1,0:T(8,128)(2,1)S(1)} %get-tuple-element.62), channel_id=1, source_target_pairs={{0,3},{1,0},{2,1},{3,2},{4,7},{5,4},{6,5},{7,6},{8,11},{9,8},{10,9... | collective-permute-start | bytes 110600 | tf_op jit(solution)/shard_map/ppermute | solution.py:443
  22.0 1.6 %collective-permute-start.7 = (bf16[32,4224]{1,0:T(8,128)(2,1)S(1)}, bf16[32,4224]{1,0:T(8,128)(2,1)S(1)}, u32[]{:S(2)}, u32[]{:S(2)}) collective-permute-start(bf16[32,4224]{1,0:T(8,128)(2,1)S(1)} %constant_dynamic-update-slice_fusion.refs_1_), channel_id=1, source_target_pairs={{0,4},{4,0},{1,5},{5,1},{2,6},{6,2},{3,7},{7,3},{8,12},{12,8},{9,1... | collective-permute-start | bytes 811016 | tf_op jit(solution)/shard_map/ppermute | solution.py:449
  22.1 9.5 %collective-permute-start.14 = (bf16[128,1024]{1,0:T(8,128)(2,1)S(1)}, bf16[128,1024]{1,0:T(8,128)(2,1)S(1)}, u32[]{:S(2)}, u32[]{:S(2)}) collective-permute-start(bf16[128,1024]{1,0:T(8,128)(2,1)S(1)} %bitcast.12), channel_id=1, source_target_pairs={{0,8},{8,0},{1,9},{9,1},{2,10},{10,2},{3,11},{11,3},{4,12},{12,4},... | collective-permute-start | bytes 786440 | tf_op jit(solution)/shard_map/ppermute | solution.py:446
  23.9 7.7 %collective-permute-start.11 = (bf16[128,256]{1,0:T(8,128)(2,1)S(1)}, bf16[128,256]{1,0:T(8,128)(2,1)S(1)}, u32[]{:S(2)}, u32[]{:S(2)}) collective-permute-start(bf16[128,256]{1,0:T(8,128)(2,1)S(1)} %get-tuple-element.68), channel_id=1, source_target_pairs={{0,1},{1,2},{2,3},{3,0},{4,5},{5,6},{6,7},{7,4},{8,9},{9,10},{10,1... | collective-permute-start | bytes 196616 | tf_op jit(solution)/shard_map/ppermute | solution.py:443
  24.8 8.0 %collective-permute-start.12 = (bf16[128,256]{1,0:T(8,128)(2,1)S(1)}, bf16[128,256]{1,0:T(8,128)(2,1)S(1)}, u32[]{:S(2)}, u32[]{:S(2)}) collective-permute-start(bf16[128,256]{1,0:T(8,128)(2,1)S(1)} %get-tuple-element.69), channel_id=1, source_target_pairs={{0,2},{1,3},{2,0},{3,1},{4,6},{5,7},{6,4},{7,5},{8,10},{9,11},{10,... | collective-permute-start | bytes 196616 | tf_op jit(solution)/shard_map/ppermute | solution.py:443
  26.4 8.0 %slice-start = ((s8[6291456]{0:T(1024)(128)(4,1)}), s8[4194304]{0:T(1024)(128)(4,1)S(1)}, s32[]{:S(2)}) async-start(s8[6291456]{0:T(1024)(128)(4,1)} %bitcast.8), calls=%async_computation | async-start | bytes 8388608
  26.4 8.0 %slice-start.1 = ((s8[6291456]{0:T(1024)(128)(4,1)}), s8[2097152]{0:T(1024)(128)(4,1)S(1)}, s32[]{:S(2)}) async-start(s8[6291456]{0:T(1024)(128)(4,1)} %bitcast.8), calls=%async_computation.1 | async-start | bytes 4194304
  26.4 6.4 %collective-permute-start.13 = (bf16[128,256]{1,0:T(8,128)(2,1)S(1)}, bf16[128,256]{1,0:T(8,128)(2,1)S(1)}, u32[]{:S(2)}, u32[]{:S(2)}) collective-permute-start(bf16[128,256]{1,0:T(8,128)(2,1)S(1)} %get-tuple-element.70), channel_id=1, source_target_pairs={{0,3},{1,0},{2,1},{3,2},{4,7},{5,4},{6,5},{7,6},{8,11},{9,8},{10,9... | collective-permute-start | bytes 196616 | tf_op jit(solution)/shard_map/ppermute | solution.py:443
  33.3 3.8 %collective-permute-start.17 = (bf16[64,128]{1,0:T(8,128)(2,1)S(1)}, bf16[64,128]{1,0:T(8,128)(2,1)S(1)}, u32[]{:S(2)}, u32[]{:S(2)}) collective-permute-start(bf16[64,128]{1,0:T(8,128)(2,1)S(1)} %get-tuple-element.82), channel_id=1, source_target_pairs={{0,8},{8,0},{1,9},{9,1},{2,10},{10,2},{3,11},{11,3},{4,12},{12,4},... | collective-permute-start | bytes 49160 | tf_op jit(solution)/shard_map/ppermute | solution.py:446
  35.4 2.0 %collective-permute-start.15 = (bf16[64,4096]{1,0:T(8,128)(2,1)S(1)}, bf16[64,4096]{1,0:T(8,128)(2,1)S(1)}, u32[]{:S(2)}, u32[]{:S(2)}) collective-permute-start(bf16[64,4096]{1,0:T(8,128)(2,1)S(1)} %get-tuple-element.78), channel_id=1, source_target_pairs={{0,4},{4,0},{1,5},{5,1},{2,6},{6,2},{3,7},{7,3},{8,12},{12,8},{9,1... | collective-permute-start | bytes 1572872 | tf_op jit(solution)/shard_map/ppermute | solution.py:449
  37.1 1.7 %collective-permute-start.18 = (bf16[32,256]{1,0:T(8,128)(2,1)S(1)}, bf16[32,256]{1,0:T(8,128)(2,1)S(1)}, u32[]{:S(2)}, u32[]{:S(2)}) collective-permute-start(bf16[32,256]{1,0:T(8,128)(2,1)S(1)} %get-tuple-element.84), channel_id=1, source_target_pairs={{0,4},{4,0},{1,5},{5,1},{2,6},{6,2},{3,7},{7,3},{8,12},{12,8},{9,1... | collective-permute-start | bytes 49160 | tf_op jit(solution)/shard_map/ppermute | solution.py:449
  37.5 8.3 %collective-permute-start.16 = (bf16[128,1024]{1,0:T(8,128)(2,1)S(1)}, bf16[128,1024]{1,0:T(8,128)(2,1)S(1)}, u32[]{:S(2)}, u32[]{:S(2)}) collective-permute-start(bf16[128,1024]{1,0:T(8,128)(2,1)S(1)} %collective-permute-done.14.refs_2_), channel_id=1, source_target_pairs={{0,4},{4,0},{1,5},{5,1},{2,6},{6,2},{3,7},{7,3},{8,12},{12,8},{9,1... | collective-permute-start | bytes 786440 | tf_op jit(solution)/shard_map/ppermute | solution.py:449
  37.8 8.0 %collective-permute-start.22 = (bf16[24,4096]{1,0:T(8,128)(2,1)S(1)}, bf16[24,4096]{1,0:T(8,128)(2,1)S(1)}, u32[]{:S(2)}, u32[]{:S(2)}) collective-permute-start(bf16[24,4096]{1,0:T(8,128)(2,1)S(1)} %get-tuple-element.89), channel_id=1, source_target_pairs={{0,8},{8,0},{1,9},{9,1},{2,10},{10,2},{3,11},{11,3},{4,12},{12,4},... | collective-permute-start | bytes 589832 | tf_op jit(solution)/shard_map/ppermute | solution.py:446
  38.8 5.9 %collective-permute-start.19 = (bf16[32,512]{1,0:T(8,128)(2,1)S(1)}, bf16[32,512]{1,0:T(8,128)(2,1)S(1)}, u32[]{:S(2)}, u32[]{:S(2)}) collective-permute-start(bf16[32,512]{1,0:T(8,128)(2,1)S(1)} %get-tuple-element.85), channel_id=1, source_target_pairs={{0,1},{1,2},{2,3},{3,0},{4,5},{5,6},{6,7},{7,4},{8,9},{9,10},{10,1... | collective-permute-start | bytes 98312 | tf_op jit(solution)/shard_map/ppermute | solution.py:443
  40.4 5.3 %collective-permute-start.20 = (bf16[32,512]{1,0:T(8,128)(2,1)S(1)}, bf16[32,512]{1,0:T(8,128)(2,1)S(1)}, u32[]{:S(2)}, u32[]{:S(2)}) collective-permute-start(bf16[32,512]{1,0:T(8,128)(2,1)S(1)} %get-tuple-element.86), channel_id=1, source_target_pairs={{0,2},{1,3},{2,0},{3,1},{4,6},{5,7},{6,4},{7,5},{8,10},{9,11},{10,... | collective-permute-start | bytes 98312 | tf_op jit(solution)/shard_map/ppermute | solution.py:443
  41.7 4.1 %collective-permute-start.21 = (bf16[32,512]{1,0:T(8,128)(2,1)S(1)}, bf16[32,512]{1,0:T(8,128)(2,1)S(1)}, u32[]{:S(2)}, u32[]{:S(2)}) collective-permute-start(bf16[32,512]{1,0:T(8,128)(2,1)S(1)} %get-tuple-element.87), channel_id=1, source_target_pairs={{0,3},{1,0},{2,1},{3,2},{4,7},{5,4},{6,5},{7,6},{8,11},{9,8},{10,9... | collective-permute-start | bytes 98312 | tf_op jit(solution)/shard_map/ppermute | solution.py:443
  44.7 5.3 %collective-permute-start.23 = (bf16[8,4096]{1,0:T(8,128)(2,1)S(1)}, bf16[8,4096]{1,0:T(8,128)(2,1)S(1)}, u32[]{:S(2)}, u32[]{:S(2)}) collective-permute-start(bf16[8,4096]{1,0:T(8,128)(2,1)S(1)} %get-tuple-element.91), channel_id=1, source_target_pairs={{0,8},{8,0},{1,9},{9,1},{2,10},{10,2},{3,11},{11,3},{4,12},{12,4},... | collective-permute-start | bytes 196616 | tf_op jit(solution)/shard_map/ppermute | solution.py:446
  46.1 6.9 %collective-permute-start.26 = (bf16[8,4096]{1,0:T(8,128)(2,1)S(1)}, bf16[8,4096]{1,0:T(8,128)(2,1)S(1)}, u32[]{:S(2)}, u32[]{:S(2)}) collective-permute-start(bf16[8,4096]{1,0:T(8,128)(2,1)S(1)} %get-tuple-element.94), channel_id=1, source_target_pairs={{0,1},{1,2},{2,3},{3,0},{4,5},{5,6},{6,7},{7,4},{8,9},{9,10},{10,1... | collective-permute-start | bytes 196616 | tf_op jit(solution)/shard_map/ppermute | solution.py:443
  47.5 5.4 %collective-permute-start.25 = (bf16[8,4096]{1,0:T(8,128)(2,1)S(1)}, bf16[8,4096]{1,0:T(8,128)(2,1)S(1)}, u32[]{:S(2)}, u32[]{:S(2)}) collective-permute-start(bf16[8,4096]{1,0:T(8,128)(2,1)S(1)} %get-tuple-element.93), channel_id=1, source_target_pairs={{0,3},{1,0},{2,1},{3,2},{4,7},{5,4},{6,5},{7,6},{8,11},{9,8},{10,9... | collective-permute-start | bytes 196616 | tf_op jit(solution)/shard_map/ppermute | solution.py:443
  50.0 5.4 %collective-permute-start.24 = (bf16[8,4096]{1,0:T(8,128)(2,1)S(1)}, bf16[8,4096]{1,0:T(8,128)(2,1)S(1)}, u32[]{:S(2)}, u32[]{:S(2)}) collective-permute-start(bf16[8,4096]{1,0:T(8,128)(2,1)S(1)} %get-tuple-element.92), channel_id=1, source_target_pairs={{0,2},{1,3},{2,0},{3,1},{4,6},{5,7},{6,4},{7,5},{8,10},{9,11},{10,... | collective-permute-start | bytes 196616 | tf_op jit(solution)/shard_map/ppermute | solution.py:443
